TPU v7x, 32 devices: a whole 2x2x4 slice. The times are simulated.
32 devices in a mesh: index: 16 (over z, y, x), query: 2 (over core).
Axes of the slice: x: 2, y: 2, z: 4, core: 2. Of those that a mesh axis runs over, the one named last changes fastest.
Arguments:
- table: bfloat16 [8192, 768], P('index'), may hold values from -150 to 150, as said below
- ages: int32 [8192], P('index'), may hold values from 0 to 63
- refresh_ids: int32 [4096], P('index'), may hold values from 0 to 8191, as said below
- fresh_rows: bfloat16 [4096, 768], P('index'), may hold values from -150 to 150, as said below
- neg_ids: int32 [16, 2048], P('index'), may hold values from 0 to 8191, as said below
- queries: bfloat16 [8192, 768], P(('index', 'query')), may hold values from -150 to 150, as said below
- pos_ids: int32 [8192], P(('index', 'query')), may hold values from 0 to 8191, as said below
Outputs:
- new_table: bfloat16 [8192, 768], P('index')
- new_ages: int32 [8192], P('index')
- loss: float32 [8192], P(('index', 'query'))
Inputs may be any that keep to these rules, and one draw needn't show every extreme that they name: `refresh_ids`: all ids are distinct. Owner o holds rows o * 512 to (o + 1) * 512 - 1; at most 32 of the 256 ids of one refresher fall in one owner's rows, and in every draw some owner receives exactly 32 from every refresher. `neg_ids`: the 2048 ids of one list are distinct; at most 256 of them fall in one owner's block of 512 rows, and in every draw some owner receives exactly 256 from every list. `pos_ids`: the positive of query i is one of the ids of list i // 512. `table`: Real-valued embeddings. `fresh_rows`: Real-valued embeddings. `queries`: Real-valued embeddings.
All inputs are finite; a program needn't handle non-finite values.
Results may differ from a plain program's by a relative error of at most 0.001.
Values may be sent and summed in bfloat16 or wider, within the bound.
No kernel may reach another device: no remote copies, remote signals or barrier semaphores. Data moves between devices by JAX's collectives and lax.ppermute only.
A program may use at most 64 MiB of HBM per device.

v0:
```python
import jax
import jax.numpy as jnp
from jax import lax
from jax.sharding import PartitionSpec as P

NEG = 2048


score_scale = 20.0
age_scale = 16.0
epsilon = 1e-06


def bucket_slots(list_ids, owner_count, rows_dev):
    owner_of = list_ids // rows_dev
    local_row = list_ids - owner_of * rows_dev
    onehot = (owner_of[:, None] == jnp.arange(owner_count, dtype=jnp.int32)[None, :]).astype(
        jnp.int32
    )
    slot_rank = jnp.sum(jnp.cumsum(onehot, axis=0) * onehot, axis=1) - 1
    return (owner_of, slot_rank, local_row)


def inverse_norm(matrix):
    squares = jnp.einsum("md,md->m", matrix, matrix, preferred_element_type=jnp.float32)
    return lax.rsqrt(squares / matrix.shape[1] + epsilon)


def on_device(table, ages, refresh_ids, fresh_rows, neg_ids, queries, pos_ids):
    rows_dev, width = table.shape
    owners = lax.axis_size("index")
    replicas = lax.axis_size("query")
    refresher_rows = refresh_ids.shape[0]
    refresh_cap = max(2, (2 * refresher_rows + owners - 1) // owners)
    owner_of, slot_rank, local_row = bucket_slots(refresh_ids, owners, rows_dev)
    fresh_slots = (
        jnp.zeros((owners, refresh_cap, width), jnp.bfloat16)
        .at[owner_of, slot_rank]
        .set(fresh_rows)
    )
    fresh_index = (
        jnp.full((owners, refresh_cap), -1, jnp.int32).at[owner_of, slot_rank].set(local_row)
    )
    arrived_rows, arrived_index = (
        lax.all_to_all(fresh_slots, "index", split_axis=0, concat_axis=0, tiled=True),
        lax.all_to_all(fresh_index, "index", split_axis=0, concat_axis=0, tiled=True),
    )
    flat_index = arrived_index.reshape(-1)
    target = jnp.where(flat_index >= 0, flat_index, rows_dev)
    new_table = table.at[target].set(arrived_rows.reshape(-1, width), mode="drop")
    new_ages = ages.at[target].set(0, mode="drop")
    capacity = replicas * ((2 * NEG + owners * replicas - 1) // (owners * replicas))
    list_ids = neg_ids[0]
    neg_owner, neg_rank, neg_local = bucket_slots(list_ids, owners, rows_dev)
    wanted = jnp.full((owners, capacity), -1, jnp.int32).at[neg_owner, neg_rank].set(neg_local)
    owner_base = jnp.arange(owners, dtype=jnp.int32)[:, None] * rows_dev
    slot_global = jnp.where(wanted >= 0, wanted + owner_base, -1)
    share = capacity // replicas
    request = lax.dynamic_slice_in_dim(wanted, lax.axis_index("query") * share, share, 1)
    incoming = lax.all_to_all(request, "index", split_axis=0, concat_axis=0, tiled=True)
    is_valid = incoming >= 0
    picked = jnp.where(is_valid, incoming, 0)
    served_rows = new_table[picked]
    decay = jnp.exp(-new_ages[picked].astype(jnp.float32) / age_scale)
    served_weight = jnp.where(is_valid, decay, 0.0).astype(jnp.bfloat16)
    part_rows, part_weight = (
        lax.all_to_all(served_rows, "index", split_axis=0, concat_axis=0, tiled=True),
        lax.all_to_all(served_weight, "index", split_axis=0, concat_axis=0, tiled=True),
    )
    fetched_rows, fetched_weight = (
        lax.all_gather(part_rows, "query", axis=1, tiled=True),
        lax.all_gather(part_weight, "query", axis=1, tiled=True),
    )
    slot_count = owners * capacity
    flat_rows = fetched_rows.reshape(slot_count, width)
    weights = fetched_weight.reshape(slot_count).astype(jnp.float32)
    slot_ids = slot_global.reshape(slot_count)
    row_inverse = inverse_norm(flat_rows)
    query_inverse = inverse_norm(queries)
    query_count = queries.shape[0]
    block_size = min(512, query_count)
    block_count = query_count // block_size

    def score_block(inputs):
        query_block, inverse_block, positive_block = inputs
        raw_product = lax.dot_general(
            query_block, flat_rows, (((1,), (1,)), ((), ())), preferred_element_type=jnp.float32
        )
        scores = raw_product * (score_scale / width) * inverse_block[:, None] * row_inverse[None, :]
        weighted = jnp.sum(weights[None, :] * jnp.exp(scores), axis=1)
        is_positive = slot_ids[None, :] == positive_block[:, None]
        positive_score = jnp.sum(jnp.where(is_positive, scores, 0.0), axis=1)
        positive_weight = jnp.sum(jnp.where(is_positive, weights[None, :], 0.0), axis=1)
        return jnp.log(weighted) - positive_score - jnp.log(positive_weight)

    losses = lax.map(
        score_block,
        (
            queries.reshape(block_count, block_size, width),
            query_inverse.reshape(block_count, block_size),
            pos_ids.reshape(block_count, block_size),
        ),
    )
    return (new_table, new_ages, losses.reshape(query_count))


def solution(mesh):
    placed = (
        P("index", None),
        P("index"),
        P("index"),
        P("index", None),
        P("index", None),
        P(("index", "query"), None),
        P(("index", "query")),
    )
    return jax.shard_map(
        on_device,
        mesh=mesh,
        in_specs=placed,
        out_specs=(P("index", None), P("index"), P(("index", "query"))),
        check_vma=False,
    )
```

profile of v0, /device:TPU:0, one launch (start us, length us, event | category | flops | bytes accessed | tf_op | source)
XLA Modules:
  0.0 271.8 jit_solution(3669791024710519117)
XLA Ops:
  7.2 0.0 copy-start.9
  7.2 0.0 copy-start.8
  7.2 0.0 copy-start.6
  7.2 0.0 copy-start.7
  7.2 0.7 multiply_subtract_fusion.1
  8.0 0.6 reduce-window.14
  8.6 0.2 slice_reduce_fusion.1
  8.8 0.1 fusion.10
  8.9 0.6 broadcast_in_dim.35
  9.5 37.0 %scatter_fusion = s32[16,32]{1,0:T(8,128)} fusion(s32[16,32]{1,0:T(8,128)} %broadcast_in_dim.35, s32[256]{0:T(256)S(1)} %bitcast.71, s32[256]{0:T(256)S(1)} %get-tuple-element.24), kind=kCustom, calls=%fused_computation.2 | custom fusion | bytes 5120 | tf_op jit(solution)/shard_map/scatter | solution.py:42
  46.5 7.9 %all-to-all-start = ((s32[16,1,32]{2,1,0:T(1,128)}), s32[16,1,32]{2,1,0:T(1,128)S(1)}, u32[]{:S(2)}, u32[]{:S(2)}) async-start(s32[16,1,32]{2,1,0:T(1,128)} %bitcast.7), calls=%async_computation | async-start | bytes 16384 | tf_op jit(solution)/shard_map/all_to_all | solution.py:46
  54.4 0.7 add_select_fusion
  55.1 4.5 %reduce-window.16 = s32[16,16,128]{2,1,0:T(8,128)S(1)} reduce-window(s32[16,16,128]{2,1,0:T(8,128)S(1)} %fusion.8, s32[]{:T(128)} %constant.45.clone.1), window={size=1x1x128 pad=0_0x0_0x127_0}, to_apply=%region_7.8 | reduce-window | flops 4161536 | bytes 262148 | tf_op jit(solution)/shard_map/reduce-window.2
  59.6 0.4 slice_reduce_fusion
  60.1 0.2 reduce-window.19
  60.2 0.1 broadcast_add_fusion
  60.4 0.0 copy-done.7
  60.4 0.1 fusion.7
  60.5 0.1 compare_select_fusion.2
  60.5 0.0 copy-done.9
  60.5 0.1 multiply_reduce_fusion.1
  60.6 0.0 copy-done.8
  60.6 0.1 and_reduce_fusion
  60.8 8.1 %scatter_custom_fusion.4 = s32[4096]{0:T(1024)S(1)} fusion(s32[2048]{0:T(1024)S(1)} %broadcast_select_fusion, s32[2048]{0:T(1024)S(1)} %get-tuple-element.26, s32[]{:T(128)} %constant.40.clone.1), kind=kCustom, calls=%fused_computation.66 | custom fusion | bytes 16388
  68.8 0.6 constant_dynamic-slice_fusion
  69.4 0.0 all-to-all-done
  69.5 6.9 %all-to-all-start.2 = ((s32[16,1,128]{2,1,0:T(1,128)}), s32[16,1,128]{2,1,0:T(1,128)S(1)}, u32[]{:S(2)}, u32[]{:S(2)}) async-start(s32[16,1,128]{2,1,0:T(1,128)} %bitcast.16), calls=%async_computation.2 | async-start | bytes 16384 | tf_op jit(solution)/shard_map/all_to_all | solution.py:60
  76.4 1.0 broadcast_in_dim.42
  77.3 0.0 copy-done.6
  77.3 35.1 %scatter_fusion.1 = bf16[16,32,768]{2,1,0:T(8,128)(2,1)} fusion(bf16[16,32,768]{2,1,0:T(8,128)(2,1)} %broadcast_in_dim.42, s32[256]{0:T(256)S(1)} %bitcast.72, bf16[256,768]{1,0:T(8,128)(2,1)S(1)} %copy-done.6), kind=kCustom, calls=%fused_computation.3 | custom fusion | bytes 1181696 | tf_op jit(solution)/shard_map/scatter | solution.py:39
  112.4 0.0 all-to-all-done.2
  112.5 7.1 %all-to-all-start.1 = ((bf16[16,32,768]{2,1,0:T(8,128)(2,1)}), bf16[16,32,768]{2,1,0:T(8,128)(2,1)S(1)}, u32[]{:S(2)}, u32[]{:S(2)}) async-start(bf16[16,32,768]{2,1,0:T(8,128)(2,1)} %scatter_fusion.1), calls=%async_computation.1 | async-start | bytes 1572864 | tf_op jit(solution)/shard_map/all_to_all | solution.py:45
  119.5 0.0 all-gather.3.cloned.1.call-start
  119.6 0.5 broadcast.408
  120.1 0.7 reduce.15
  120.8 0.1 reshape.297
  120.9 17.3 %all-to-all-done.1 = bf16[16,32,768]{2,1,0:T(8,128)(2,1)S(1)} async-done(((bf16[16,32,768]{2,1,0:T(8,128)(2,1)}), bf16[16,32,768]{2,1,0:T(8,128)(2,1)S(1)}, u32[]{:S(2)}, u32[]{:S(2)}) %all-to-all-start.1) | async-done | bytes 786464 | tf_op jit(solution)/shard_map/all_to_all | solution.py:45
  138.2 0.0 copy-done.3
  138.2 3.0 %scatter_fusion.2 = bf16[512,768]{1,0:T(8,128)(2,1)S(1)} fusion(bf16[512,768]{1,0:T(8,128)(2,1)S(1)} %copy-done.3, s32[512]{0:T(512)S(1)} %bitcast.84, bf16[512,768]{1,0:T(8,128)(2,1)S(1)} %bitcast.75), kind=kCustom, calls=%fused_computation.4 | custom fusion | bytes 2361344 | tf_op jit(solution)/shard_map/scatter | solution.py:50
  141.2 0.0 copy-start.2
  141.2 9.4 %gather_fusion.1 = bf16[2048,768]{1,0:T(8,128)(2,1)} fusion(bf16[512,768]{1,0:T(8,128)(2,1)S(1)} %scatter_fusion.2, s32[2048]{0:T(1024)S(1)} %fusion.15), kind=kCustom, calls=%fused_computation.1 | custom fusion | bytes 6299648 | tf_op jit(solution)/shard_map/gather | solution.py:63
  150.6 0.0 copy-done.2
  150.6 75.3 %all_to_all.40 = bf16[16,128,768]{2,1,0:T(8,128)(2,1)} all-to-all(bf16[16,128,768]{2,1,0:T(8,128)(2,1)} %bitcast.73), channel_id=1, replica_groups=mesh['index'=16,'query'=2] {'index'}, dimensions={0} | all-to-all | bytes 6291456 | tf_op jit(solution)/shard_map/all_to_all | solution.py:67
  225.9 0.0 all-gather.3.cloned.1.call-update
  226.0 0.0 copy-done.5
  226.0 0.2 fusion.5
  226.2 0.1 select_bitcast_fusion
  226.2 0.0 copy-done.1
  226.2 2.4 scatter_fusion.3
  228.7 0.0 copy-start
  228.7 13.2 %gather_fusion = s32[2048]{0:T(1024)S(1)} fusion(s32[512]{0:T(512)S(1)} %scatter_fusion.3, s32[2048]{0:T(1024)S(1)} %fusion.15), kind=kCustom, calls=%fused_computation | custom fusion | bytes 24576 | tf_op jit(solution)/shard_map/gather | solution.py:64
  241.9 0.0 copy-done
  241.9 0.0 copy-start.10
  241.9 0.6 fusion.16
  242.5 4.0 %all-to-all-start.3 = ((bf16[16,1,128]{2,1,0:T(2,128)(2,1)}), bf16[16,1,128]{2,1,0:T(2,128)(2,1)S(1)}, u32[]{:S(2)}, u32[]{:S(2)}) async-start(bf16[16,1,128]{2,1,0:T(2,128)(2,1)} %fusion.16), calls=%async_computation.3 | async-start | bytes 16384 | tf_op jit(solution)/shard_map/all_to_all | solution.py:68
  246.6 7.2 %all-to-all-done.3 = bf16[16,1,128]{2,1,0:T(2,128)(2,1)S(1)} async-done(((bf16[16,1,128]{2,1,0:T(2,128)(2,1)}), bf16[16,1,128]{2,1,0:T(2,128)(2,1)S(1)}, u32[]{:S(2)}, u32[]{:S(2)}) %all-to-all-start.3) | async-done | bytes 4128 | tf_op jit(solution)/shard_map/all_to_all | solution.py:68
  253.8 1.8 all-gather
  255.6 0.0 all-gather.3.cloned.1.call-done
  255.7 0.0 copy-start.4
  255.7 4.2 %fusion = f32[4096]{0:T(1024)S(1)} fusion(bf16[16,256,768]{2,1,0:T(8,128)(2,1)} %all-gather.3.cloned.1.call-done), kind=kLoop, calls=%fused_computation.8 | loop fusion | flops 9433088 | bytes 6307840 | tf_op jit(solution)/shard_map/md,md->m/dot_general | solution.py:25
  259.9 0.0 copy-done.10
  259.9 0.3 copy-done.4
  260.3 4.1 %multiply_reduce_fusion = (f32[256]{0:T(256)S(1)}, f32[256]{0:T(256)S(1)}, f32[256]{0:T(256)S(1)}) fusion(f32[4096]{0:T(1024)S(1)} %bitcast.88, s32[256]{0:T(256)S(1)} %copy-done.10, s32[4096]{0:T(1024)S(1)} %bitcast.87, f32[4096]{0:T(1024)S(1)} %add_rsqrt_fusion, f32[256]{0:T(256)S(1)} %rsqrt_multiply_fusion, bf16[4096,768]{1,0:T(8,128)(2,1)S(1)} %bitcast.74, ...), kind=kOutput, calls=%fused_computation.16 | convolution fusion | flops 1620049152 | bytes 6738944 | tf_op jit(solution)/shard_map/while/body/eval_jaxpr/dot_general | solution.py:86
  264.4 0.6 log_subtract_fusion
  (23 shorter events, 0.2 us)
Async XLA Ops:
  7.2 53.4 %copy-start.9 = (s32[2]{0:T(128)S(1)}, s32[2]{0:T(128)}, u32[]{:S(2)}) copy-start(s32[2]{0:T(128)} %constant.103) | copy-start | bytes 28
  7.2 53.5 %copy-start.8 = (s32[2]{0:T(128)S(1)}, s32[2]{0:T(128)}, u32[]{:S(2)}) copy-start(s32[2]{0:T(128)} %constant.106) | copy-start | bytes 28
  7.2 70.1 %copy-start.6 = (bf16[256,768]{1,0:T(8,128)(2,1)S(1)}, bf16[256,768]{1,0:T(8,128)(2,1)}, u32[]{:S(2)}) copy-start(bf16[256,768]{1,0:T(8,128)(2,1)} %param.10) | copy-start | bytes 1179652
  7.2 53.2 %copy-start.7 = (s32[1,2048]{1,0:T(1,128)S(1)}, s32[1,2048]{1,0:T(1,128)}, u32[]{:S(2)}) copy-start(s32[1,2048]{1,0:T(1,128)} %param.11) | copy-start | bytes 24580
  46.5 23.0 %all-to-all-start = ((s32[16,1,32]{2,1,0:T(1,128)}), s32[16,1,32]{2,1,0:T(1,128)S(1)}, u32[]{:S(2)}, u32[]{:S(2)}) async-start(s32[16,1,32]{2,1,0:T(1,128)} %bitcast.7), calls=%async_computation | async-start | bytes 16384 | tf_op jit(solution)/shard_map/all_to_all | solution.py:46
  69.5 43.0 %all-to-all-start.2 = ((s32[16,1,128]{2,1,0:T(1,128)}), s32[16,1,128]{2,1,0:T(1,128)S(1)}, u32[]{:S(2)}, u32[]{:S(2)}) async-start(s32[16,1,128]{2,1,0:T(1,128)} %bitcast.16), calls=%async_computation.2 | async-start | bytes 16384 | tf_op jit(solution)/shard_map/all_to_all | solution.py:60
  77.3 60.8 %copy-start.3 = (bf16[512,768]{1,0:T(8,128)(2,1)S(1)}, bf16[512,768]{1,0:T(8,128)(2,1)}, u32[]{:S(2)}) copy-start(bf16[512,768]{1,0:T(8,128)(2,1)} %param.7) | copy-start | bytes 2359300
  112.5 25.7 %all-to-all-start.1 = ((bf16[16,32,768]{2,1,0:T(8,128)(2,1)}), bf16[16,32,768]{2,1,0:T(8,128)(2,1)S(1)}, u32[]{:S(2)}, u32[]{:S(2)}) async-start(bf16[16,32,768]{2,1,0:T(8,128)(2,1)} %scatter_fusion.1), calls=%async_computation.1 | async-start | bytes 1572864 | tf_op jit(solution)/shard_map/all_to_all | solution.py:45
  119.5 136.1 %all-gather.3.cloned.1.call-start = ((), (), s32[]{:S(2)}) async-start(), calls=%async_computation.5 | async-start | bytes 9437184 | tf_op jit(solution)/shard_map/all_gather | solution.py:71
  141.2 9.4 %copy-start.2 = (bf16[512,768]{1,0:T(8,128)(2,1)}, bf16[512,768]{1,0:T(8,128)(2,1)S(1)}, u32[]{:S(2)}) copy-start(bf16[512,768]{1,0:T(8,128)(2,1)S(1)} %scatter_fusion.2) | copy-start | bytes 2359300
  150.6 75.4 %copy-start.5 = (bf16[256,768]{1,0:T(8,128)(2,1)S(1)}, bf16[256,768]{1,0:T(8,128)(2,1)}, u32[]{:S(2)}) copy-start(bf16[256,768]{1,0:T(8,128)(2,1)} %param.12) | copy-start | bytes 1179652
  150.6 75.6 %copy-start.1 = (s32[512]{0:T(512)S(1)}, s32[512]{0:T(512)}, u32[]{:S(2)}) copy-start(s32[512]{0:T(512)} %param.8) | copy-start | bytes 6148
  228.7 13.2 %copy-start = (s32[512]{0:T(512)}, s32[512]{0:T(512)S(1)}, u32[]{:S(2)}) copy-start(s32[512]{0:T(512)S(1)} %scatter_fusion.3) | copy-start | bytes 6148
  241.9 18.0 %copy-start.10 = (s32[256]{0:T(256)S(1)}, s32[256]{0:T(256)}, u32[]{:S(2)}) copy-start(s32[256]{0:T(256)} %param.13) | copy-start | bytes 3076
  242.5 11.3 %all-to-all-start.3 = ((bf16[16,1,128]{2,1,0:T(2,128)(2,1)}), bf16[16,1,128]{2,1,0:T(2,128)(2,1)S(1)}, u32[]{:S(2)}, u32[]{:S(2)}) async-start(bf16[16,1,128]{2,1,0:T(2,128)(2,1)} %fusion.16), calls=%async_computation.3 | async-start | bytes 16384 | tf_op jit(solution)/shard_map/all_to_all | solution.py:68
  255.7 4.6 %copy-start.4 = (bf16[16,256,768]{2,1,0:T(8,128)(2,1)S(1)}, bf16[16,256,768]{2,1,0:T(8,128)(2,1)}, u32[]{:S(2)}) copy-start(bf16[16,256,768]{2,1,0:T(8,128)(2,1)} %all-gather.3.cloned.1.call-done) | copy-start | bytes 18874372
Sparse Core Ops, SparseCore 0:
  226.1 15.1 all-gather.2
where the time goes:
time: 274 us; the launch traced here: 272 us
  local copies, waits for them, and re-layouts  112 us (41%)
  blocking collectives  77.2 us (28%)
  starting transfers between devices  25.9 us (9%)
  waiting for transfers between devices  24.6 us (9%)
  between operations  14.4 us (5%)
  other arithmetic  13.7 us (5%)
  matrix products  4.14 us (2%)
    all_to_all x1, blocking collectives, on_device(): lax.all_to_all(served_rows, 'index', split_axis=0, concat_axis=0, tiled=T...  75.3 us
    scatter x1, local copies, waits for them, and re-layouts, on_device(): jnp.full((owners, refresh_cap), -1, jnp.int32).at[owner_of, slot_rank]  37 us
    scatter x1, local copies, waits for them, and re-layouts, on_device(): fresh_slots = jnp.zeros((owners, refresh_cap, width), jnp.bfloat16).at[ow...  35.1 us
    all_to_all x1, waiting for transfers between devices, on_device(): lax.all_to_all(fresh_slots, 'index', split_axis=0, concat_axis=0, tiled=T...  17.3 us
    gather x1, local copies, waits for them, and re-layouts, on_device(): decay = jnp.exp(-new_ages[picked].astype(jnp.float32) / age_scale)  13.2 us
    gather x1, local copies, waits for them, and re-layouts, on_device(): served_rows = new_table[picked]  9.38 us
    unnamed x24, local copies, waits for them, and re-layouts  8.45 us
    all_to_all x1, starting transfers between devices, on_device(): lax.all_to_all(fresh_index, 'index', split_axis=0, concat_axis=0, tiled=T...  7.88 us
  transfers between devices with their start and end apart: 5, of which 2 were waited for; matrix products, arithmetic and copies ran while one was open for 25% of the time, Pallas kernels for 0%

commit v1 on v0

v1 whole, which is shorter than its diff:
```python
import functools
import math

import jax
import jax.numpy as jnp
from jax import lax
from jax.experimental import pallas as pl
from jax.experimental.pallas import tpu as pltpu
from jax.sharding import Mesh, PartitionSpec as P

score_scale = 20.0
age_scale = 16.0
epsilon = 1e-06
LOG2E = math.log2(math.e)
MASKED = -1e30
LANES = 128
VMEM_LIMIT = 48 * 1024 * 1024

NT = (((1,), (1,)), ((), ()))
NN = (((1,), (0,)), ((), ()))


def one_hot(ids, count):
    rows = lax.broadcasted_iota(jnp.int32, (count, ids.shape[1]), 0)
    return jnp.where(rows == ids, 1.0, 0.0).astype(jnp.bfloat16)


def split_one_hot(ids, high_count):
    return one_hot(ids >> 7, high_count), one_hot(ids & 127, LANES)


def bitmap(ids, high_count):
    high, low = split_one_hot(ids, high_count)
    return lax.dot_general(low, high, NT, preferred_element_type=jnp.float32)


def meta_kernel(
    place, ref_ids, neg, log_weight, lw_out, row_out, pack_out, apply_out, own_out, *, rows_dev, cap, replicas
):
    outer, inner, core = place[0], place[1], place[2]
    planes, plane_refresh = ref_ids.shape
    plane_rows = log_weight.shape[1]
    owners_plane = plane_rows // rows_dev
    high_count = planes * plane_rows // LANES
    plane_ids = ref_ids[pl.ds(outer, 1), :]
    table_ids = outer * plane_rows + lax.broadcasted_iota(jnp.int32, (1, plane_rows), 1)

    refreshed_map = jnp.zeros((LANES, high_count), jnp.float32)
    for plane in range(planes):
        refreshed_map += bitmap(ref_ids[plane : plane + 1, :], high_count)
    refreshed_map = refreshed_map.astype(jnp.bfloat16)

    table_high, table_low = split_one_hot(table_ids, high_count)
    fresh_high, fresh_low = split_one_hot(plane_ids, high_count)

    def lookup(one_map, high, low):
        hit = lax.dot_general(one_map, high, NN, preferred_element_type=jnp.float32)
        return jnp.sum(hit * low.astype(jnp.float32), axis=0, keepdims=True)

    refreshed = lookup(refreshed_map, table_high, table_low) > 0.5
    row_out[:, :plane_rows] = jnp.where(refreshed, -1, table_ids).astype(jnp.float32)
    row_out[:, plane_rows:] = plane_ids.astype(jnp.float32)
    own_ids = (outer * owners_plane + inner) * rows_dev + lax.broadcasted_iota(jnp.int32, (1, rows_dev), 1)
    own_out[...] = (lookup(refreshed_map, *split_one_hot(own_ids, high_count)) > 0.5).astype(jnp.int32)

    for group in range(planes):
        one_map = bitmap(neg[group : group + 1, :], high_count).astype(jnp.bfloat16)
        in_list = lookup(one_map, table_high, table_low) > 0.5
        lw_out[group : group + 1, :plane_rows] = jnp.where(in_list & ~refreshed, log_weight[...], MASKED)
        in_list = lookup(one_map, fresh_high, fresh_low) > 0.5
        lw_out[group : group + 1, plane_rows:] = jnp.where(in_list, 0.0, MASKED)

    share = cap // replicas
    earlier = jnp.where(
        lax.broadcasted_iota(jnp.int32, (plane_refresh, plane_refresh), 0)
        < lax.broadcasted_iota(jnp.int32, (plane_refresh, plane_refresh), 1),
        1.0,
        0.0,
    ).astype(jnp.bfloat16)
    plane_owner = plane_ids // rows_dev
    target_plane = lax.broadcasted_iota(jnp.int32, (planes, plane_refresh), 0)
    send_match = plane_owner == target_plane * owners_plane + inner
    take_match = (ref_ids[...] // rows_dev) == outer * owners_plane + inner

    def ranked(match):
        ones = jnp.where(match, 1.0, 0.0)
        rank = lax.dot_general(ones.astype(jnp.bfloat16), earlier, NN, preferred_element_type=jnp.float32)
        return jnp.where(match, rank.astype(jnp.int32), -1)

    send_rank = ranked(send_match) - core * share
    send_rank = jnp.where(send_match, send_rank, -1)
    take_rank = ranked(take_match)
    take_row = ref_ids[...] - (outer * owners_plane + inner) * rows_dev
    for plane in range(planes):
        pack_out[plane * share : (plane + 1) * share, :] = one_hot(send_rank[plane : plane + 1, :], share)
        slot = one_hot(take_rank[plane : plane + 1, :], cap)
        row = one_hot(take_row[plane : plane + 1, :], rows_dev)
        where_to = lax.dot_general(row, slot, NT, preferred_element_type=jnp.float32)
        for replica in range(replicas):
            first = (replica * planes + plane) * share
            apply_out[:, first : first + share] = where_to[:, replica * share : (replica + 1) * share]


def pack_kernel(select, rows, out):
    out[...] = lax.dot_general(select[...], rows[...], NN, preferred_element_type=jnp.float32).astype(jnp.bfloat16)


def apply_kernel(select, arrived, table, out):
    chosen = select[...]
    fresh = lax.dot_general(chosen.astype(jnp.bfloat16), arrived[...], NN, preferred_element_type=jnp.float32)
    hit = jnp.sum(chosen, axis=1, keepdims=True) > 0.5
    out[...] = jnp.where(hit, fresh, table[...].astype(jnp.float32)).astype(jnp.bfloat16)


def to_lanes(row):
    return jnp.broadcast_to(row, (LANES, LANES)).T


def score_kernel(
    queries, table, fresh, log_weight, row_ids, scale, positive, out, q_scale, pos_b, total, pos_total, *, table_steps, groups
):
    step = pl.program_id(0)
    count, width = queries.shape
    per_group = count // groups

    @pl.when(step == 0)
    def _():
        for block in range(count // LANES):
            part = pl.ds(block * LANES, LANES)
            values = queries[part, :].astype(jnp.float32)
            squares = jnp.sum(values * values, axis=1, keepdims=True)
            q_scale[part, :] = jnp.broadcast_to(lax.rsqrt(squares / width + epsilon), (LANES, LANES))
            pos_b[part, :] = to_lanes(positive[block : block + 1, :])
        total[...] = jnp.zeros_like(total)
        pos_total[...] = jnp.zeros_like(pos_total)

    def add(rows):
        block = rows.shape[0]
        for group in range(groups):
            part = pl.ds(group * per_group, per_group)
            raw = lax.dot_general(queries[part, :], rows[...], NT, preferred_element_type=jnp.float32)
            sums = total[part, :]
            positives = pos_total[part, :]
            for chunk in range(block // LANES):
                cols = slice(chunk * LANES, (chunk + 1) * LANES)
                powers = raw[:, cols] * q_scale[part, :] * scale[:, cols] + log_weight[group : group + 1, cols]
                sums = sums + jnp.exp2(powers)
                positives = positives + jnp.where(pos_b[part, :] == row_ids[:, cols], powers, 0.0)
            total[part, :] = sums
            pos_total[part, :] = positives

    @pl.when(step < table_steps)
    def _():
        add(table)

    @pl.when(step >= table_steps)
    def _():
        add(fresh)

    @pl.when(step == pl.num_programs(0) - 1)
    def _():
        for block in range(count // LANES):
            part = pl.ds(block * LANES, LANES)
            out[0, block : block + 1, :] = jnp.sum(total[part, :].T, axis=0, keepdims=True)
            out[1, block : block + 1, :] = jnp.sum(pos_total[part, :].T, axis=0, keepdims=True)


def whole(memory=pltpu.VMEM):
    return pl.BlockSpec(memory_space=memory)


def params():
    return pltpu.CompilerParams(vmem_limit_bytes=VMEM_LIMIT)


def on_device(table, ages, refresh_ids, fresh_rows, neg_ids, queries, pos_ids):
    rows_dev, width = table.shape
    refresh_dev = refresh_ids.shape[0]
    planes = lax.axis_size("outer")
    owners_plane = lax.axis_size("inner")
    replicas = lax.axis_size("query")
    owners = planes * owners_plane
    query_count = queries.shape[0]
    list_size = neg_ids.shape[1]
    outer, inner, core = lax.axis_index("outer"), lax.axis_index("inner"), lax.axis_index("query")
    plane_rows = owners_plane * rows_dev
    plane_refresh = owners_plane * refresh_dev
    cap = owners_plane * max(2, (2 * refresh_dev + owners - 1) // owners)

    table_half = lax.dynamic_slice_in_dim(table, core * (rows_dev // replicas), rows_dev // replicas, 0)
    fresh_half = lax.dynamic_slice_in_dim(fresh_rows, core * (refresh_dev // replicas), refresh_dev // replicas, 0)
    fresh_plane = lax.all_gather(fresh_half, ("inner", "query"), axis=0, tiled=True)
    table_plane = lax.all_gather(table_half, ("inner", "query"), axis=0, tiled=True)
    queries_line = lax.all_gather(queries, "outer", axis=0, tiled=True)

    def row_scale(rows):
        values = rows.astype(jnp.float32)
        squares = jnp.sum(values * values, axis=1)
        return lax.rsqrt(squares / width + epsilon) * (score_scale / width * LOG2E)

    weight = jnp.exp(-ages.astype(jnp.float32) / age_scale).astype(jnp.bfloat16).astype(jnp.float32)
    meta = jnp.concatenate(
        [
            refresh_ids.astype(jnp.float32),
            neg_ids[0].astype(jnp.float32),
            pos_ids.astype(jnp.float32),
            jnp.log2(weight),
            row_scale(table),
            row_scale(fresh_rows),
        ]
    )
    meta_all = lax.all_gather(meta, ("outer", "inner"), axis=0).reshape(planes, owners_plane, -1)
    cuts = [refresh_dev, list_size, query_count, rows_dev, rows_dev, refresh_dev]
    ends = [sum(cuts[: i + 1]) for i in range(len(cuts))]

    def piece(values, i):
        return values[..., ends[i] - cuts[i] : ends[i]]

    line = lax.dynamic_index_in_dim(meta_all, inner, 1, keepdims=False)
    plane = lax.dynamic_index_in_dim(meta_all, outer, 0, keepdims=False)
    ref_all = piece(meta_all, 0).reshape(planes, plane_refresh).astype(jnp.int32)
    neg_line = piece(line, 1).astype(jnp.int32)
    positive = piece(line, 2).reshape(-1, LANES)
    log_weight_plane = piece(plane, 3).reshape(1, plane_rows)
    scale_plane = jnp.concatenate([piece(plane, 4).reshape(1, -1), piece(plane, 5).reshape(1, -1)], axis=1)

    share = cap // replicas
    all_rows = plane_rows + plane_refresh
    lw, row_ids, pack, apply_to, own = pl.pallas_call(
        functools.partial(meta_kernel, rows_dev=rows_dev, cap=cap, replicas=replicas),
        out_shape=(
            jax.ShapeDtypeStruct((planes, all_rows), jnp.float32),
            jax.ShapeDtypeStruct((1, all_rows), jnp.float32),
            jax.ShapeDtypeStruct((planes * share, plane_refresh), jnp.bfloat16),
            jax.ShapeDtypeStruct((rows_dev, planes * cap), jnp.float32),
            jax.ShapeDtypeStruct((1, rows_dev), jnp.int32),
        ),
        in_specs=[whole(pltpu.SMEM)] + [whole()] * 3,
        out_specs=[whole()] * 5,
        compiler_params=params(),
        name="meta",
    )(jnp.stack([outer, inner, core]).astype(jnp.int32), ref_all, neg_line, log_weight_plane)
    new_ages = jnp.where(own.reshape(rows_dev) > 0, 0, ages)

    packed = pl.pallas_call(
        pack_kernel,
        out_shape=jax.ShapeDtypeStruct((planes * share, width), jnp.bfloat16),
        in_specs=[whole()] * 2,
        out_specs=whole(),
        compiler_params=params(),
        name="pack",
    )(pack, fresh_plane)
    arrived = lax.all_to_all(packed.reshape(planes, share, width), "outer", split_axis=0, concat_axis=0, tiled=True)
    arrived = lax.all_gather(arrived.reshape(planes * share, width), "query", axis=0, tiled=True)
    new_table = pl.pallas_call(
        apply_kernel,
        out_shape=jax.ShapeDtypeStruct(table.shape, jnp.bfloat16),
        in_specs=[whole()] * 3,
        out_specs=whole(),
        compiler_params=params(),
        name="apply",
    )(apply_to, arrived, table)

    block = min(512, plane_refresh)
    table_steps, fresh_steps = plane_rows // block, plane_refresh // block
    all_queries = planes * query_count
    partial = pl.pallas_call(
        functools.partial(score_kernel, table_steps=table_steps, groups=planes),
        out_shape=jax.ShapeDtypeStruct((2, all_queries // LANES, LANES), jnp.float32),
        grid=(table_steps + fresh_steps,),
        in_specs=[
            pl.BlockSpec((all_queries, width), lambda i: (0, 0)),
            pl.BlockSpec((block, width), lambda i: (jnp.minimum(i, table_steps - 1), 0)),
            pl.BlockSpec((block, width), lambda i: (jnp.maximum(i - table_steps, 0), 0)),
            pl.BlockSpec((planes, block), lambda i: (0, i)),
            pl.BlockSpec((1, block), lambda i: (0, i)),
            pl.BlockSpec((1, block), lambda i: (0, i)),
            pl.BlockSpec((all_queries // LANES, LANES), lambda i: (0, 0)),
        ],
        out_specs=pl.BlockSpec((2, all_queries // LANES, LANES), lambda i: (0, 0, 0)),
        scratch_shapes=[pltpu.VMEM((all_queries, LANES), jnp.float32)] * 4,
        compiler_params=params(),
        name="score",
    )(queries_line, table_plane, fresh_plane, lw, row_ids, scale_plane, positive)

    partial = partial.reshape(2, planes, query_count)
    mine = lax.dynamic_index_in_dim(partial, outer, 1, keepdims=False)
    for shift in range(1, planes):
        target = lax.rem(outer + shift, planes)
        sent = lax.dynamic_index_in_dim(partial, target, 1, keepdims=False)
        mine = mine + lax.ppermute(sent, "outer", [(i, (i + shift) % planes) for i in range(planes)])
    loss = (jnp.log2(mine[0]) - mine[1]) * math.log(2.0)
    return new_table, new_ages, loss


def solution(mesh):
    owners, replicas = mesh.shape["index"], mesh.shape["query"]
    inner = 1 << (int(math.log2(owners)) // 2)
    split = Mesh(mesh.devices.reshape(owners // inner, inner, replicas), ("outer", "inner", "query"))
    index = ("outer", "inner")
    placed = (
        P(index, None),
        P(index),
        P(index),
        P(index, None),
        P(index, None),
        P(("outer", "inner", "query"), None),
        P(("outer", "inner", "query")),
    )
    return jax.shard_map(
        on_device,
        mesh=split,
        in_specs=placed,
        out_specs=(P(index, None), P(index), P(("outer", "inner", "query"))),
        check_vma=False,
    )
```

time: 274 us -> 147 us (0.54)
  local copies, waits for them, and re-layouts: 112 us -> 8.42 us
  blocking collectives: 77.2 us -> 46.8 us
  waiting for transfers between devices: 24.6 us -> 48.9 us
  Pallas kernels: 0 us -> 17.4 us
  starting transfers between devices: 25.9 us -> 8.71 us
  other arithmetic: 13.7 us -> 2.3 us
  matrix products: 4.14 us -> 0 us
    scatter x5 -> x0, local copies, waits for them, and re-layouts: 77.6 us -> none  [the longest x1 37 us: on_device(): jnp.full((owners, refresh_cap), -1, jnp.int32).at[owner_of, slot_rank]]
    all_to_all x1 -> x0, blocking collectives: 75.3 us -> none  [on_device(): lax.all_to_all(served_rows, 'index', split_axis=0, concat_axis=0, tiled=T...]
    all_gather x1 -> x3, waiting for transfers between devices: 0.02 us -> 47.9 us  [the longest x1 33.6 us: on_device(): lax.all_gather(table_half, ('inner', 'query'), axis=0, tiled=True)]
    all_gather x1 -> x2, blocking collectives: 1.81 us -> 46.8 us  [the longest x1 44.2 us: on_device(): lax.all_gather(meta, ('outer', 'inner'), axis=0)]
    all_to_all x4 -> x1, waiting for transfers between devices: 24.6 us -> 0.01 us  [on_device(): lax.all_to_all(packed.reshape(planes, share, width), 'outer', split_axis=...]
    gather x2 -> x0, local copies, waits for them, and re-layouts: 22.6 us -> none  [the longest x1 13.2 us: on_device(): decay = jnp.exp(-new_ages[picked].astype(jnp.float32) / age_scale)]
    all_to_all x4 -> x1, starting transfers between devices: 25.8 us -> 4.11 us  [on_device(): lax.all_to_all(packed.reshape(planes, share, width), 'outer', split_axis=...]
    pallas_call x0 -> x4, Pallas kernels: none -> 17.4 us  [the longest x1 9.16 us: on_device(): pl.pallas_call(functools.partial(score_kernel, table_steps=table_steps, g...]
  transfers between devices with their start and end apart: 5 -> 7, of which waited for: 2 -> 3; matrix products, arithmetic and copies ran while one was open for 25% -> 3% of each run, Pallas kernels for 0% -> 12%
where the time goes in v1:
time: 147 us
  waiting for transfers between devices  48.9 us (33%)
  blocking collectives  46.8 us (32%)
  Pallas kernels  17.4 us (12%)
  between operations  14.1 us (10%)
  starting transfers between devices  8.71 us (6%)
  local copies, waits for them, and re-layouts  8.42 us (6%)
  other arithmetic  2.3 us (2%)
    all_gather x1, blocking collectives, on_device(): lax.all_gather(meta, ('outer', 'inner'), axis=0)  44.2 us
    all_gather x1, waiting for transfers between devices, on_device(): lax.all_gather(table_half, ('inner', 'query'), axis=0, tiled=True)  33.6 us
    all_gather x1, waiting for transfers between devices, on_device(): queries_line = lax.all_gather(queries, 'outer', axis=0, tiled=True)  14.3 us
    pallas_call x1, Pallas kernels, on_device(): pl.pallas_call(functools.partial(score_kernel, table_steps=table_steps, g...  9.16 us
    pallas_call x1, Pallas kernels, on_device(): pl.pallas_call(functools.partial(meta_kernel, rows_dev=rows_dev, cap=cap,...  5.5 us
    unnamed x34, local copies, waits for them, and re-layouts  4.75 us
    ppermute x3, starting transfers between devices, on_device(): lax.ppermute(sent, 'outer', [(i, (i + shift) % planes) for i in range(pla...  4.48 us
    all_to_all x1, starting transfers between devices, on_device(): lax.all_to_all(packed.reshape(planes, share, width), 'outer', split_axis=...  4.11 us
  transfers between devices with their start and end apart: 7, of which 3 were waited for; matrix products, arithmetic and copies ran while one was open for 3% of the time, Pallas kernels for 12%

profile of v1, /device:TPU:0, one launch (start us, length us, event | category | flops | bytes accessed | tf_op | source)
XLA Modules:
  0.0 146.7 jit_solution(2692151350171518226)
XLA Ops:
  7.2 0.0 copy-start.6
  7.2 0.0 copy-start.2
  7.2 0.0 copy-start.7
  7.2 0.0 copy-start.9
  7.2 0.0 all-gather.6.cloned.1.call-start
  7.3 1.7 %constant_dynamic-slice_fusion.5 = bf16[128,768]{1,0:T(8,128)(2,1)} fusion(bf16[256,768]{1,0:T(8,128)(2,1)} %param.10, s32[]{:T(128)S(6)} %select_n.31), kind=kLoop, calls=%fused_computation.29 | loop fusion | bytes 393220 | tf_op jit(solution)/shard_map/dynamic_slice | solution.py:191
  9.0 0.0 copy-start.10
  9.0 0.0 copy-start.8
  9.0 0.0 all-gather.6.cloned.1.call-update
  9.0 0.0 all-gather.8.cloned.1.call-start
  9.0 0.7 all-gather.8.cloned.1.call-update
  9.7 0.0 all-gather.10.cloned.1.call-start
  9.8 1.8 %constant_dynamic-slice_fusion.4 = bf16[256,768]{1,0:T(8,128)(2,1)} fusion(bf16[512,768]{1,0:T(8,128)(2,1)} %table.1, s32[]{:T(128)S(6)} %select_n.33), kind=kLoop, calls=%fused_computation.28 | loop fusion | bytes 786436 | tf_op jit(solution)/shard_map/dynamic_slice | solution.py:190
  11.6 0.0 all-gather.10.cloned.1.call-update
  11.6 0.0 copy-done.7
  11.7 0.0 copy-done.9
  11.7 0.0 copy-done.6
  11.7 0.2 multiply_reduce_fusion.1
  11.9 0.0 copy-done.2
  11.9 0.2 multiply_reduce_fusion
  12.1 0.0 copy-done.10
  12.1 0.0 copy-done.8
  12.2 44.2 %all-gather.1 = f32[16,1,3840]{2,1,0:T(1,128)S(1)} all-gather(f32[1,1,3840]{2,1,0:T(1,128)S(1)} %reshape.52), channel_id=2, replica_groups=mesh['outer'=4,'inner'=4,'query'=2] {'outer','inner'}, dimensions={0}, use_global_device_ids=true | all-gather | bytes 261120 | tf_op jit(solution)/shard_map/all_gather | solution.py:212
  56.4 0.6 reduce
  57.0 0.1 reshape.42
  57.1 0.1 constant_dynamic-slice_fusion.6
  57.4 0.1 pad_add_fusion.place
  57.4 5.5 %meta.1 = (f32[4,3072]{1,0:T(4,128)S(1)}, f32[1,3072]{1,0:T(1,128)S(1)}, bf16[256,1024]{1,0:T(8,128)(2,1)S(1)}, f32[512,512]{1,0:T(8,128)S(1)}, s32[1,512]{1,0:T(1,128)S(1)}) custom-call(s32[3]{0:T(128)S(1)} %pad_add_fusion.place, s32[4,1024]{1,0:T(4,128)S(1)} %bitcast.42, s32[4,2048]{1,0:T(4,128)S(1)} %slice_convert_fusion.neg, f32[1,2048]{1,0:T(1,128)S(1)} %bitcast.43), custom_call_target="tpu_custom_call" | custom-call | tf_op jit(solution)/shard_map/meta/pallas_call | solution.py:229
  62.9 0.0 copy-start.4
  63.0 0.8 copy-done.4
  63.8 0.0 all-gather.6.cloned.1.call-done.rows.fresh
  63.8 0.0 copy-start
  63.8 1.4 copy-done
  65.2 0.0 copy-start.5
  65.2 1.0 copy-done.5
  66.2 0.0 copy-start.1
  66.2 1.3 pack.1
  67.6 4.1 %all-to-all-start = ((bf16[4,64,768]{2,1,0:T(8,128)(2,1)}), bf16[4,64,768]{2,1,0:T(8,128)(2,1)}, u32[]{:S(2)}, u32[]{:S(2)}) async-start(bf16[4,64,768]{2,1,0:T(8,128)(2,1)} %bitcast.5), calls=%async_computation | async-start | bytes 786432 | tf_op jit(solution)/shard_map/all_to_all | solution.py:253
  71.7 0.6 broadcast_select_fusion
  72.3 14.3 %all-gather.8.cloned.1.call-done.queries = bf16[1024,768]{1,0:T(8,128)(2,1)} async-done(((bf16[256,768]{1,0:T(8,128)(2,1)}), bf16[1024,768]{1,0:T(8,128)(2,1)}) %all-gather.8.cloned.1.call-update) | async-done | bytes 1572880 | tf_op jit(solution)/shard_map/all_gather | solution.py:194
  86.6 33.6 %all-gather.10.cloned.1.call-done.table = bf16[2048,768]{1,0:T(8,128)(2,1)} async-done(((bf16[256,768]{1,0:T(8,128)(2,1)}), bf16[2048,768]{1,0:T(8,128)(2,1)}) %all-gather.10.cloned.1.call-update) | async-done | bytes 3145744 | tf_op jit(solution)/shard_map/all_gather | solution.py:193
  120.2 0.0 copy-done.1
  120.2 0.0 copy-start.3
  120.2 1.4 copy-done.3
  121.6 9.2 %score.1 = f32[2,8,128]{2,1,0:T(8,128)S(1)} custom-call(bf16[1024,768]{1,0:T(8,128)(2,1)S(1)} %copy-done.3, bf16[2048,768]{1,0:T(8,128)(2,1)} %all-gather.10.cloned.1.call-done.table, bf16[1024,768]{1,0:T(8,128)(2,1)S(1)} %copy-done.1, f32[4,3072]{1,0:T(4,128)S(1)} %get-tuple-element.11.log_weight, f32[1,3072]{1,0:T(1,128)S(1)} %get-tuple-element.12.row_ids, ...), custom_call_target="tpu_custom_call" | custom-call | tf_op jit(solution)/shard_map/score/pallas_call | solution.py:267
  130.8 3.4 %collective-permute-start.2 = (f32[2,256]{1,0:T(2,128)S(1)}, f32[2,256]{1,0:T(2,128)S(1)}, u32[]{:S(2)}, u32[]{:S(2)}) collective-permute-start(f32[2,256]{1,0:T(2,128)S(1)} %bitcast.49), channel_id=1, source_target_pairs={{0,24},{8,0},{16,8},{24,16},{1,25},{9,1},{17,9},{25,17},{2,26},{10... | collective-permute-start | bytes 6152 | tf_op jit(solution)/shard_map/ppermute | solution.py:291
  134.2 0.0 collective-permute-start.1
  134.2 1.1 collective-permute-start
  135.3 0.0 all-to-all-done
  135.3 2.6 %all_gather.21.arrived = bf16[512,768]{1,0:T(8,128)(2,1)S(1)} all-gather(bf16[256,768]{1,0:T(8,128)(2,1)} %bitcast.6), channel_id=1, replica_groups=mesh['outer'=4,'inner'=4,'query'=2] {'query'}, dimensions={0}, use_global_device_ids=true | all-gather | bytes 1179648 | tf_op jit(solution)/shard_map/all_gather | solution.py:254
  137.9 1.5 apply.1
  139.3 0.0 collective-permute-done.2
  139.3 0.0 collective-permute-done.1
  139.3 0.2 collective-permute-done
  139.6 0.6 fusion.3
  (29 shorter events, 0.2 us)
Async XLA Ops:
  7.2 4.5 %copy-start.6 = (bf16[256,768]{1,0:T(8,128)(2,1)S(1)}, bf16[256,768]{1,0:T(8,128)(2,1)}, u32[]{:S(2)}) copy-start(bf16[256,768]{1,0:T(8,128)(2,1)} %param.10) | copy-start | bytes 1179652
  7.2 4.7 %copy-start.2 = (bf16[512,768]{1,0:T(8,128)(2,1)S(1)}, bf16[512,768]{1,0:T(8,128)(2,1)}, u32[]{:S(2)}) copy-start(bf16[512,768]{1,0:T(8,128)(2,1)} %table.1) | copy-start | bytes 2359300
  7.2 4.4 %copy-start.7 = (s32[1,2048]{1,0:T(1,128)S(1)}, s32[1,2048]{1,0:T(1,128)}, u32[]{:S(2)}) copy-start(s32[1,2048]{1,0:T(1,128)} %param.11) | copy-start | bytes 24580
  7.2 4.5 %copy-start.9 = (s32[256]{0:T(256)S(1)}, s32[256]{0:T(256)}, u32[]{:S(2)}) copy-start(s32[256]{0:T(256)} %param.9) | copy-start | bytes 3076
  7.2 56.6 %all-gather.6.cloned.1.call-start = ((), (), s32[]{:S(2)}) async-start(), calls=%async_computation.1 | async-start | bytes 1769472 | tf_op jit(solution)/shard_map/all_gather | solution.py:192
  9.0 3.1 %copy-start.10 = (s32[256]{0:T(256)S(1)}, s32[256]{0:T(256)}, u32[]{:S(2)}) copy-start(s32[256]{0:T(256)} %param.13) | copy-start | bytes 3076
  9.0 3.2 %copy-start.8 = (s32[512]{0:T(512)S(1)}, s32[512]{0:T(512)}, u32[]{:S(2)}) copy-start(s32[512]{0:T(512)} %param.8) | copy-start | bytes 6148
  9.0 77.6 %all-gather.8.cloned.1.call-start = ((), (), s32[]{:S(2)}) async-start(), calls=%async_computation.2 | async-start | bytes 1966080 | tf_op jit(solution)/shard_map/all_gather | solution.py:194
  9.7 110.4 %all-gather.10.cloned.1.call-start = ((), (), s32[]{:S(2)}) async-start(), calls=%async_computation.3 | async-start | bytes 3538944 | tf_op jit(solution)/shard_map/all_gather | solution.py:193
  62.9 0.8 copy-start.4
  63.8 1.4 copy-start
  65.2 1.0 copy-start.5
  66.2 54.0 %copy-start.1 = (bf16[1024,768]{1,0:T(8,128)(2,1)S(1)}, bf16[1024,768]{1,0:T(8,128)(2,1)}, u32[]{:S(2)}) copy-start(bf16[1024,768]{1,0:T(8,128)(2,1)} %all-gather.6.cloned.1.call-done.rows.fresh) | copy-start | bytes 4718596
  67.6 67.7 %all-to-all-start = ((bf16[4,64,768]{2,1,0:T(8,128)(2,1)}), bf16[4,64,768]{2,1,0:T(8,128)(2,1)}, u32[]{:S(2)}, u32[]{:S(2)}) async-start(bf16[4,64,768]{2,1,0:T(8,128)(2,1)} %bitcast.5), calls=%async_computation | async-start | bytes 786432 | tf_op jit(solution)/shard_map/all_to_all | solution.py:253
  120.2 1.4 copy-start.3
  130.8 8.5 %collective-permute-start.2 = (f32[2,256]{1,0:T(2,128)S(1)}, f32[2,256]{1,0:T(2,128)S(1)}, u32[]{:S(2)}, u32[]{:S(2)}) collective-permute-start(f32[2,256]{1,0:T(2,128)S(1)} %bitcast.49), channel_id=1, source_target_pairs={{0,24},{8,0},{16,8},{24,16},{1,25},{9,1},{17,9},{25,17},{2,26},{10... | collective-permute-start | bytes 6152 | tf_op jit(solution)/shard_map/ppermute | solution.py:291
  134.2 5.1 %collective-permute-start.1 = (f32[2,256]{1,0:T(2,128)S(1)}, f32[2,256]{1,0:T(2,128)S(1)}, u32[]{:S(2)}, u32[]{:S(2)}) collective-permute-start(f32[2,256]{1,0:T(2,128)S(1)} %bitcast.50), channel_id=1, source_target_pairs={{0,16},{8,24},{16,0},{24,8},{1,17},{9,25},{17,1},{25,9},{2,18},{10... | collective-permute-start | bytes 6152 | tf_op jit(solution)/shard_map/ppermute | solution.py:291
  134.2 5.4 %collective-permute-start = (f32[2,256]{1,0:T(2,128)S(1)}, f32[2,256]{1,0:T(2,128)S(1)}, u32[]{:S(2)}, u32[]{:S(2)}) collective-permute-start(f32[2,256]{1,0:T(2,128)S(1)} %bitcast.51), channel_id=1, source_target_pairs={{0,8},{8,16},{16,24},{24,0},{1,9},{9,17},{17,25},{25,1},{2,10},{10... | collective-permute-start | bytes 6152 | tf_op jit(solution)/shard_map/ppermute | solution.py:291
Sparse Core Ops, SparseCore 0:
  9.9 29.7 all-gather.5
  41.3 45.2 all-gather.7
  88.5 31.6 all-gather.9

commit v2 on v1

v2 whole, which is shorter than its diff:
```python
import functools
import math

import jax
import jax.numpy as jnp
from jax import lax
from jax.experimental import pallas as pl
from jax.experimental.pallas import tpu as pltpu
from jax.sharding import Mesh, PartitionSpec as P

score_scale = 20.0
age_scale = 16.0
epsilon = 1e-06
LOG2E = math.log2(math.e)
MASKED = -1e30
LANES = 128
VMEM_LIMIT = 48 * 1024 * 1024

NT = (((1,), (1,)), ((), ()))
NN = (((1,), (0,)), ((), ()))


def one_hot(ids, count):
    rows = lax.broadcasted_iota(jnp.int32, (count, ids.shape[1]), 0)
    return jnp.where(rows == ids, 1.0, 0.0).astype(jnp.bfloat16)


def split_one_hot(ids, high_count):
    return one_hot(ids >> 7, high_count), one_hot(ids & 127, LANES)


def bitmap(ids, high_count):
    high, low = split_one_hot(ids, high_count)
    return lax.dot_general(low, high, NT, preferred_element_type=jnp.float32)


def prep_kernel(place, table, fresh, ages, ref_ids, rows_out, meta_out, *, replicas):
    core = place[2]
    row = 0
    for source in (table, fresh):
        half = source.shape[0] // replicas
        rows_out[row : row + half, :] = source[pl.ds(pl.multiple_of(core * half, half), half), :]
        row += half
    width = table.shape[1]
    ref_rows, age_rows = ref_ids.shape[0], ages.shape[0]
    meta_out[:ref_rows, :] = ref_ids[...].astype(jnp.float32)
    weight = jnp.exp(-ages[...].astype(jnp.float32) / age_scale).astype(jnp.bfloat16).astype(jnp.float32)
    meta_out[ref_rows : ref_rows + age_rows, :] = jnp.log2(weight)
    line = ref_rows + age_rows
    for source in (table, fresh):
        for block in range(source.shape[0] // LANES):
            squares = jnp.zeros((LANES, LANES), jnp.float32)
            for chunk in range(width // LANES):
                values = source[block * LANES : (block + 1) * LANES, chunk * LANES : (chunk + 1) * LANES]
                values = values.astype(jnp.float32)
                squares += values * values
            mean = jnp.sum(squares.T, axis=0, keepdims=True) / width
            meta_out[line : line + 1, :] = lax.rsqrt(mean + epsilon) * (score_scale / width * LOG2E)
            line += 1


def meta_kernel(
    place, ref_ids, neg, log_weight, lw_out, row_out, pack_out, apply_out, own_out, *, rows_dev, refresh_dev, cap, replicas
):
    outer, inner, core = place[0], place[1], place[2]
    planes, plane_refresh = ref_ids.shape
    plane_rows = log_weight.shape[1]
    owners_plane = plane_rows // rows_dev
    high_count = planes * plane_rows // LANES
    own_owner = outer * owners_plane + inner
    plane_ids = ref_ids[0:1, :]
    column = lax.broadcasted_iota(jnp.int32, (1, plane_rows), 1)
    table_ids = (outer * owners_plane + (inner ^ (column // rows_dev))) * rows_dev + column % rows_dev

    refreshed_map = jnp.zeros((LANES, high_count), jnp.float32)
    for plane in range(planes):
        refreshed_map += bitmap(ref_ids[plane : plane + 1, :], high_count)
    refreshed_map = refreshed_map.astype(jnp.bfloat16)

    table_high, table_low = split_one_hot(table_ids, high_count)
    fresh_high, fresh_low = split_one_hot(plane_ids, high_count)

    def lookup(one_map, high, low):
        hit = lax.dot_general(one_map, high, NN, preferred_element_type=jnp.float32)
        return jnp.sum(hit * low.astype(jnp.float32), axis=0, keepdims=True)

    refreshed = lookup(refreshed_map, table_high, table_low) > 0.5
    row_out[:, :plane_rows] = jnp.where(refreshed, -1, table_ids).astype(jnp.float32)
    row_out[:, plane_rows:] = plane_ids.astype(jnp.float32)
    own_out[...] = refreshed[:, :rows_dev].astype(jnp.int32)

    for group in range(planes):
        one_map = bitmap(neg[group : group + 1, :], high_count).astype(jnp.bfloat16)
        in_list = lookup(one_map, table_high, table_low) > 0.5
        lw_out[group : group + 1, :plane_rows] = jnp.where(in_list & ~refreshed, log_weight[...], MASKED)
        in_list = lookup(one_map, fresh_high, fresh_low) > 0.5
        lw_out[group : group + 1, plane_rows:] = jnp.where(in_list, 0.0, MASKED)

    share = cap // replicas
    earlier = jnp.where(
        lax.broadcasted_iota(jnp.int32, (plane_refresh, plane_refresh), 0)
        < lax.broadcasted_iota(jnp.int32, (plane_refresh, plane_refresh), 1),
        1.0,
        0.0,
    ).astype(jnp.bfloat16)
    target_plane = outer ^ lax.broadcasted_iota(jnp.int32, (planes, plane_refresh), 0)
    send_match = plane_ids // rows_dev == target_plane * owners_plane + inner
    take_match = ref_ids[...] // rows_dev == own_owner

    def ranked(match):
        ones = jnp.where(match, 1.0, 0.0)
        rank = lax.dot_general(ones.astype(jnp.bfloat16), earlier, NN, preferred_element_type=jnp.float32)
        return jnp.where(match, rank.astype(jnp.int32), -cap)

    send_rank, take_rank = ranked(send_match), ranked(take_match)
    take_row = ref_ids[...] - own_owner * rows_dev
    pack_out[:cap, :] = one_hot(send_rank[0:1, :], cap)
    for plane in range(1, planes):
        first = cap + (plane - 1) * share
        pack_out[first : first + share, :] = one_hot(send_rank[plane : plane + 1, :] - core * share, share)
    for plane in range(planes):
        row = one_hot(take_row[plane : plane + 1, :], rows_dev)
        for part in range(1 if plane == 0 else replicas):
            size = cap if plane == 0 else share
            skip = 0 if plane == 0 else (core ^ part) * share
            slot = one_hot(take_rank[plane : plane + 1, :] - skip, size)
            first = plane * cap + part * share
            apply_out[:, first : first + size] = lax.dot_general(row, slot, NT, preferred_element_type=jnp.float32)


def piece_offset(place, piece):
    column, size, flip = piece
    if flip is None:
        return column
    return pl.multiple_of(column + (place[2] ^ flip) * size, size)


def pack_kernel(place, select, *refs, pieces):
    out = refs[-1]
    total = jnp.zeros(out.shape, jnp.float32)
    for source, start, size, column in pieces:
        columns = pl.ds(piece_offset(place, column), size)
        total += lax.dot_general(
            select[:, columns], refs[source][start : start + size, :], NN, preferred_element_type=jnp.float32
        )
    out[...] = total.astype(jnp.bfloat16)


def apply_kernel(select, table, *refs):
    out = refs[-1]
    fresh = jnp.zeros(out.shape, jnp.float32)
    first = 0
    for arrived in refs[:-1]:
        part = select[:, first : first + arrived.shape[0]].astype(jnp.bfloat16)
        fresh += lax.dot_general(part, arrived[...], NN, preferred_element_type=jnp.float32)
        first += arrived.shape[0]
    hit = jnp.sum(select[...], axis=1, keepdims=True) > 0.5
    out[...] = jnp.where(hit, fresh, table[...].astype(jnp.float32)).astype(jnp.bfloat16)


def to_lanes(row):
    return jnp.broadcast_to(row, (LANES, LANES)).T


def score_kernel(place, queries, positive, log_weight, row_ids, scale, *refs, pieces):
    out, total, pos_total, q_scale, pos_b = refs[-5:]
    count, width = queries.shape
    for block in range(count // LANES):
        part = slice(block * LANES, (block + 1) * LANES)
        values = queries[part, :].astype(jnp.float32)
        squares = jnp.sum(values * values, axis=1, keepdims=True)
        q_scale[part, :] = jnp.broadcast_to(lax.rsqrt(squares / width + epsilon), (LANES, LANES))
        pos_b[part, :] = to_lanes(positive[block : block + 1, :])
    total[...] = jnp.zeros_like(total)
    pos_total[...] = jnp.zeros_like(pos_total)
    for source, start, size, column in pieces:
        first = piece_offset(place, column)
        raw = lax.dot_general(
            queries[...], refs[source][start : start + size, :], NT, preferred_element_type=jnp.float32
        )
        sums = total[...]
        positives = pos_total[...]
        for chunk in range(size // LANES):
            cols = pl.ds(first + chunk * LANES, LANES)
            part = raw[:, chunk * LANES : (chunk + 1) * LANES]
            powers = part * q_scale[...] * scale[:, cols] + log_weight[:, cols]
            sums = sums + jnp.exp2(powers)
            positives = positives + jnp.where(pos_b[...] == row_ids[:, cols], powers, 0.0)
        total[...] = sums
        pos_total[...] = positives
    for block in range(count // LANES):
        part = slice(block * LANES, (block + 1) * LANES)
        out[0, block : block + 1, :] = jnp.sum(total[part, :].T, axis=0, keepdims=True)
        out[1, block : block + 1, :] = jnp.sum(pos_total[part, :].T, axis=0, keepdims=True)


def whole(memory=pltpu.VMEM):
    return pl.BlockSpec(memory_space=memory)


def call(kernel, name, outs, place, *operands, scratch=(), flops=0, **options):
    specs = [whole()] * len(operands)
    if place is not None:
        specs = [whole(pltpu.SMEM)] + specs
        operands = (place, *operands)
    moved = sum(math.prod(x.shape) * x.dtype.itemsize for x in (*operands, *outs))
    return pl.pallas_call(
        functools.partial(kernel, **options),
        out_shape=tuple(outs),
        in_specs=specs,
        out_specs=tuple(whole() for _ in outs),
        scratch_shapes=list(scratch),
        compiler_params=pltpu.CompilerParams(vmem_limit_bytes=VMEM_LIMIT),
        cost_estimate=pl.CostEstimate(flops=flops, bytes_accessed=moved, transcendentals=0),
        name=name,
    )(*operands)


def swap(values, axis, flip):
    return lax.ppermute(values, axis, [(i, i ^ flip) for i in range(lax.axis_size(axis))])


def on_device(table, ages, refresh_ids, fresh_rows, neg_ids, queries, pos_ids):
    rows_dev, width = table.shape
    refresh_dev = refresh_ids.shape[0]
    planes = lax.axis_size("outer")
    owners_plane = lax.axis_size("inner")
    replicas = lax.axis_size("query")
    owners = planes * owners_plane
    query_count = queries.shape[0]
    list_size = neg_ids.shape[1]
    place = jnp.stack([lax.axis_index(name) for name in ("outer", "inner", "query")]).astype(jnp.int32)
    plane_rows = owners_plane * rows_dev
    plane_refresh = owners_plane * refresh_dev
    all_rows = plane_rows + plane_refresh
    cap = owners_plane * max(2, (2 * refresh_dev + owners - 1) // owners)
    share = cap // replicas
    table_half, fresh_half = rows_dev // replicas, refresh_dev // replicas
    bf16, f32 = jnp.bfloat16, jnp.float32

    meta_lines = (2 * refresh_dev + 2 * rows_dev) // LANES
    rows_half, meta = call(
        prep_kernel,
        "prep",
        [jax.ShapeDtypeStruct((table_half + fresh_half, width), bf16), jax.ShapeDtypeStruct((meta_lines, LANES), f32)],
        place,
        table,
        fresh_rows,
        ages.reshape(-1, LANES),
        refresh_ids.reshape(-1, LANES),
        replicas=replicas,
    )
    metas = jnp.stack([meta] + [swap(meta, "inner", s) for s in range(1, owners_plane)])
    got_queries = [queries] + [swap(queries, "outer", s) for s in range(1, planes)]
    got_rows = [swap(rows_half, "inner", s) for s in range(1, owners_plane)]
    cuts = [refresh_dev, rows_dev, rows_dev, refresh_dev]
    ends = [sum(cuts[: i + 1]) // LANES for i in range(len(cuts))]

    def piece(i):
        return metas[:, ends[i] - cuts[i] // LANES : ends[i]].reshape(1, -1)

    ref_plane, log_weight_plane = piece(0), piece(1)
    scale_plane = jnp.concatenate([piece(2), piece(3)], axis=1)
    line = jnp.concatenate([ref_plane[0], neg_ids[0].astype(f32), pos_ids.astype(f32)])
    lines = jnp.stack([line] + [swap(line, "outer", s) for s in range(1, planes)])
    ref_all = lines[:, :plane_refresh].astype(jnp.int32)
    neg_line = lines[:, plane_refresh : plane_refresh + list_size].astype(jnp.int32)
    positive = lines[:, plane_refresh + list_size :].reshape(planes, -1, LANES)

    lw, row_ids, pack, apply_to, own = call(
        meta_kernel,
        "meta",
        [
            jax.ShapeDtypeStruct((planes, all_rows), f32),
            jax.ShapeDtypeStruct((1, all_rows), f32),
            jax.ShapeDtypeStruct((cap + (planes - 1) * share, plane_refresh), bf16),
            jax.ShapeDtypeStruct((rows_dev, planes * cap), f32),
            jax.ShapeDtypeStruct((1, rows_dev), jnp.int32),
        ],
        place,
        ref_all,
        neg_line,
        log_weight_plane,
        rows_dev=rows_dev,
        refresh_dev=refresh_dev,
        cap=cap,
        replicas=replicas,
    )
    new_ages = jnp.where(own.reshape(rows_dev) > 0, 0, ages)

    if replicas == 2:
        buffers = [table, fresh_rows]
        table_pieces = [(0, 0, rows_dev, (0, rows_dev, None))]
        fresh_pieces = [(1, 0, refresh_dev, (0, refresh_dev, None))]
        for s in range(1, owners_plane):
            for flip, rows in enumerate((got_rows[s - 1], swap(got_rows[s - 1], "query", 1))):
                table_pieces.append((len(buffers), 0, table_half, (s * rows_dev, table_half, flip)))
                fresh_pieces.append((len(buffers), table_half, fresh_half, (s * refresh_dev, fresh_half, flip)))
                buffers.append(rows)
    else:
        gathered = lax.all_gather(jnp.stack([rows_half] + got_rows), "query", axis=0)
        gathered = jnp.swapaxes(gathered, 0, 1)
        buffers = [
            gathered[:, :, :table_half].reshape(plane_rows, width),
            gathered[:, :, table_half:].reshape(plane_refresh, width),
        ]
        table_pieces = [(0, i * 512, 512, (i * 512, 512, None)) for i in range(plane_rows // 512)]
        fresh_pieces = [(1, i * 512, 512, (i * 512, 512, None)) for i in range(plane_refresh // 512)]

    def shift(pieces, columns):
        return [(a, b, c, (d[0] + columns, *d[1:])) for a, b, c, d in pieces]

    (packed,) = call(
        pack_kernel, "pack", [jax.ShapeDtypeStruct((pack.shape[0], width), bf16)], place, pack, *buffers, pieces=fresh_pieces
    )
    arrived = [packed[:cap]]
    for s in range(1, planes):
        first = cap + (s - 1) * share
        part = swap(packed[first : first + share], "outer", s)
        arrived += [part] + [swap(part, "query", flip) for flip in range(1, replicas)]

    pieces = table_pieces + shift(fresh_pieces, plane_rows)
    mine = None
    for s in [*range(1, planes), 0]:
        (partial,) = call(
            score_kernel,
            "score",
            [jax.ShapeDtypeStruct((2, query_count // LANES, LANES), f32)],
            place,
            got_queries[s],
            positive[s],
            lw[s : s + 1],
            row_ids,
            scale_plane,
            *buffers,
            scratch=[pltpu.VMEM((query_count, LANES), f32)] * 4,
            flops=2 * query_count * all_rows * width,
            pieces=pieces,
        )
        if s:
            partial = swap(partial, "outer", s)
        mine = partial if mine is None else mine + partial
    (new_table,) = call(
        apply_kernel, "apply", [jax.ShapeDtypeStruct(table.shape, bf16)], None, apply_to, table, *arrived
    )
    loss = (jnp.log2(mine[0]) - mine[1]) * math.log(2.0)
    return new_table, new_ages, loss.reshape(query_count)


def solution(mesh):
    owners, replicas = mesh.shape["index"], mesh.shape["query"]
    inner = 1 << (int(math.log2(owners)) // 2)
    split = Mesh(mesh.devices.reshape(owners // inner, inner, replicas), ("outer", "inner", "query"))
    index = ("outer", "inner")
    placed = (
        P(index, None),
        P(index),
        P(index),
        P(index, None),
        P(index, None),
        P(("outer", "inner", "query"), None),
        P(("outer", "inner", "query")),
    )
    return jax.shard_map(
        on_device,
        mesh=split,
        in_specs=placed,
        out_specs=(P(index, None), P(index), P(("outer", "inner", "query"))),
        check_vma=False,
    )
```

time: 147 us -> 77.4 us (0.53)
  blocking collectives: 46.8 us -> 0 us
  waiting for transfers between devices: 48.9 us -> 11.4 us
  starting transfers between devices: 8.71 us -> 39 us
  between operations: 14.1 us -> 0.89 us
  local copies, waits for them, and re-layouts: 8.42 us -> 2.93 us
  Pallas kernels: 17.4 us -> 21.6 us
    all_gather x3 -> x0, waiting for transfers between devices: 47.9 us -> none  [the longest x1 33.6 us: on_device(): lax.all_gather(table_half, ('inner', 'query'), axis=0, tiled=True)]
    all_gather x2 -> x0, blocking collectives: 46.8 us -> none  [the longest x1 44.2 us: on_device(): lax.all_gather(meta, ('outer', 'inner'), axis=0)]
    ppermute x3 -> x24, starting transfers between devices: 4.48 us -> 39 us  [swap(): lax.ppermute(values, axis, [(i, i ^ flip) for i in range(lax.axis_size(ax...]
    ppermute x3 -> x24, waiting for transfers between devices: 0.25 us -> 11.4 us  [swap(): lax.ppermute(values, axis, [(i, i ^ flip) for i in range(lax.axis_size(ax...]
    pallas_call x4 -> x8, Pallas kernels: 17.4 us -> 21.6 us  [call(): pl.pallas_call(functools.partial(kernel, **options), out_shape=tuple(outs...]
    all_to_all x1 -> x0, starting transfers between devices: 4.11 us -> none  [on_device(): lax.all_to_all(packed.reshape(planes, share, width), 'outer', split_axis=...]
    dynamic_slice x4 -> x0, local copies, waits for them, and re-layouts: 3.56 us -> none  [the longest x1 1.79 us: on_device(): lax.dynamic_slice_in_dim(table, core * (rows_dev // replicas), rows_dev /...]
    unnamed x34 -> x18, local copies, waits for them, and re-layouts: 4.75 us -> 2.84 us
  transfers between devices with their start and end apart: 7 -> 24, of which waited for: 3 -> 7; matrix products, arithmetic and copies ran while one was open for 3% -> 2% of each run, Pallas kernels for 12% -> 24%
where the time goes in v2:
time: 77.4 us; the launch traced here: 77.1 us
  starting transfers between devices  39 us (50%)
  Pallas kernels  21.6 us (28%)
  waiting for transfers between devices  11.4 us (15%)
  local copies, waits for them, and re-layouts  2.93 us (4%)
  other arithmetic  1.4 us (2%)
  between operations  0.89 us (1%)
    ppermute x24, starting transfers between devices, swap(): lax.ppermute(values, axis, [(i, i ^ flip) for i in range(lax.axis_size(ax...  39 us
    pallas_call x8, Pallas kernels, call(): pl.pallas_call(functools.partial(kernel, **options), out_shape=tuple(outs...  21.6 us
    ppermute x24, waiting for transfers between devices, swap(): lax.ppermute(values, axis, [(i, i ^ flip) for i in range(lax.axis_size(ax...  11.4 us
    unnamed x18, local copies, waits for them, and re-layouts  2.84 us
  transfers between devices with their start and end apart: 24, of which 7 were waited for; matrix products, arithmetic and copies ran while one was open for 2% of the time, Pallas kernels for 24%

profile of v2, /device:TPU:0, one launch (start us, length us, event | category | flops | bytes accessed | tf_op | source)
XLA Modules:
  0.0 77.1 jit_solution(9288608234966445893)
XLA Ops:
  0.6 0.0 copy-start.7
  0.6 0.1 pad_add_fusion.place
  0.7 0.7 copy-done.5
  1.4 0.0 copy-done.6
  1.4 1.1 %copy-done = bf16[512,768]{1,0:T(8,128)(2,1)S(1)} copy-done((bf16[512,768]{1,0:T(8,128)(2,1)S(1)}, bf16[512,768]{1,0:T(8,128)(2,1)}, u32[]{:S(2)}) %copy-start) | copy-done | bytes 786456
  2.6 1.0 %copy-done.2 = bf16[256,768]{1,0:T(8,128)(2,1)S(1)} copy-done((bf16[256,768]{1,0:T(8,128)(2,1)S(1)}, bf16[256,768]{1,0:T(8,128)(2,1)}, u32[]{:S(2)}) %copy-start.2) | copy-done | bytes 393240
  3.6 0.8 %prep.1 = (bf16[384,768]{1,0:T(8,128)(2,1)S(1)}, f32[12,128]{1,0:T(8,128)S(1)}) custom-call(s32[3]{0:T(128)S(1)} %pad_add_fusion.place, bf16[512,768]{1,0:T(8,128)(2,1)S(1)} %copy-done, bf16[256,768]{1,0:T(8,128)(2,1)S(1)} %copy-done.2, s32[4,128]{1,0:T(4,128)S(1)} %bitcast.23, s32[2,128]{1,0:T(2,128)S(1)} %bitcast.28), custom_call_target="tpu_custom_call" | custom-call | bytes 1778700 | tf_op jit(solution)/shard_map/prep/pallas_call | solution.py:207
  4.4 3.0 %collective-permute-start = (f32[12,128]{1,0:T(8,128)S(1)}, f32[12,128]{1,0:T(8,128)S(1)}, u32[]{:S(2)}, u32[]{:S(2)}) collective-permute-start(f32[12,128]{1,0:T(8,128)S(1)} %get-tuple-element.10), channel_id=1, source_target_pairs={{0,2},{2,0},{4,6},{6,4},{1,3},{3,1},{5,7},{7,5},{8,10},{10,8},{12,... | collective-permute-start | bytes 18440 | tf_op jit(solution)/shard_map/ppermute | solution.py:220
  7.4 1.5 %collective-permute-start.1 = (f32[12,128]{1,0:T(8,128)S(1)}, f32[12,128]{1,0:T(8,128)S(1)}, u32[]{:S(2)}, u32[]{:S(2)}) collective-permute-start(f32[12,128]{1,0:T(8,128)S(1)} %get-tuple-element.10), channel_id=1, source_target_pairs={{0,4},{2,6},{4,0},{6,2},{1,5},{3,7},{5,1},{7,3},{8,12},{10,14},{12... | collective-permute-start | bytes 18440 | tf_op jit(solution)/shard_map/ppermute | solution.py:220
  8.9 0.0 collective-permute-start.2
  9.0 2.9 %collective-permute-start.10 = (bf16[384,768]{1,0:T(8,128)(2,1)S(1)}, bf16[384,768]{1,0:T(8,128)(2,1)S(1)}, u32[]{:S(2)}, u32[]{:S(2)}) collective-permute-start(bf16[384,768]{1,0:T(8,128)(2,1)S(1)} %get-tuple-element.13), channel_id=1, source_target_pairs={{0,6},{2,4},{4,2},{6,0},{1,7},{3,5},{5,3},{7,1},{8,14},{10,12},{12... | collective-permute-start | bytes 1769480 | tf_op jit(solution)/shard_map/ppermute | solution.py:220
  11.9 0.5 collective-permute-start.6
  12.4 0.0 collective-permute-done
  12.4 0.1 collective-permute-start.8
  12.6 0.0 collective-permute-done.1
  12.6 1.1 %collective-permute-done.2 = f32[12,128]{1,0:T(8,128)S(1)} collective-permute-done((f32[12,128]{1,0:T(8,128)S(1)}, f32[12,128]{1,0:T(8,128)S(1)}, u32[]{:S(2)}, u32[]{:S(2)}) %collective-permute-start.2) | collective-permute-done | bytes 6176 | tf_op jit(solution)/shard_map/ppermute | solution.py:220
  13.7 1.6 %collective-permute-start.3 = (f32[3328]{0:T(1024)S(1)}, f32[3328]{0:T(1024)S(1)}, u32[]{:S(2)}, u32[]{:S(2)}) collective-permute-start(f32[3328]{0:T(1024)S(1)} %pad_maximum_fusion.3), channel_id=1, source_target_pairs={{0,8},{8,0},{16,24},{24,16},{1,9},{9,1},{17,25},{25,17},{2,10},{10... | collective-permute-start | bytes 39944 | tf_op jit(solution)/shard_map/ppermute | solution.py:220
  15.3 2.6 %collective-permute-start.4 = (f32[3328]{0:T(1024)S(1)}, f32[3328]{0:T(1024)S(1)}, u32[]{:S(2)}, u32[]{:S(2)}) collective-permute-start(f32[3328]{0:T(1024)S(1)} %pad_maximum_fusion.3), channel_id=1, source_target_pairs={{0,16},{8,24},{16,0},{24,8},{1,17},{9,25},{17,1},{25,9},{2,18},{10... | collective-permute-start | bytes 39944 | tf_op jit(solution)/shard_map/ppermute | solution.py:220
  17.9 0.0 collective-permute-done.3
  17.9 3.2 %collective-permute-start.5 = (f32[3328]{0:T(1024)S(1)}, f32[3328]{0:T(1024)S(1)}, u32[]{:S(2)}, u32[]{:S(2)}) collective-permute-start(f32[3328]{0:T(1024)S(1)} %pad_maximum_fusion.3), channel_id=1, source_target_pairs={{0,24},{8,16},{16,8},{24,0},{1,25},{9,17},{17,9},{25,1},{2,26},{10... | collective-permute-start | bytes 39944 | tf_op jit(solution)/shard_map/ppermute | solution.py:220
  21.1 0.0 collective-permute-done.4
  21.1 1.5 %collective-permute-start.20 = (bf16[256,768]{1,0:T(8,128)(2,1)S(1)}, bf16[256,768]{1,0:T(8,128)(2,1)S(1)}, u32[]{:S(2)}, u32[]{:S(2)}) collective-permute-start(bf16[256,768]{1,0:T(8,128)(2,1)S(1)} %copy-done.4), channel_id=1, source_target_pairs={{0,16},{8,24},{16,0},{24,8},{1,17},{9,25},{17,1},{25,9},{2,18},{10... | collective-permute-start | bytes 1179656 | tf_op jit(solution)/shard_map/ppermute | solution.py:220
  22.6 1.1 %collective-permute-done.5 = f32[3328]{0:T(1024)S(1)} collective-permute-done((f32[3328]{0:T(1024)S(1)}, f32[3328]{0:T(1024)S(1)}, u32[]{:S(2)}, u32[]{:S(2)}) %collective-permute-start.5) | collective-permute-done | bytes 13344 | tf_op jit(solution)/shard_map/ppermute | solution.py:220
  23.7 2.7 %collective-permute-start.18 = (bf16[256,768]{1,0:T(8,128)(2,1)S(1)}, bf16[256,768]{1,0:T(8,128)(2,1)S(1)}, u32[]{:S(2)}, u32[]{:S(2)}) collective-permute-start(bf16[256,768]{1,0:T(8,128)(2,1)S(1)} %copy-done.4), channel_id=1, source_target_pairs={{0,8},{8,0},{16,24},{24,16},{1,9},{9,1},{17,25},{25,17},{2,10},{10... | collective-permute-start | bytes 1179656 | tf_op jit(solution)/shard_map/ppermute | solution.py:220
  26.5 6.4 %meta.1 = (f32[4,3072]{1,0:T(4,128)S(1)}, f32[1,3072]{1,0:T(1,128)S(1)}, bf16[320,1024]{1,0:T(8,128)(2,1)S(1)}, f32[512,512]{1,0:T(8,128)S(1)}, s32[1,512]{1,0:T(1,128)S(1)}) custom-call(s32[3]{0:T(128)S(1)} %pad_add_fusion.place, s32[4,1024]{1,0:T(4,128)S(1)} %maximum_convert_fusion.ref_ids, s32[4,2048]{1,0:T(4,128)S(1)} %fusion.neg, f32[1,2048]{1,0:T(1,128)S(1)} %bitcast.22), custom_call_target="tpu_custom_call" | custom-call | bytes 1824780 | tf_op jit(solution)/shard_map/meta/pallas_call | solution.py:207
  32.9 0.0 collective-permute-done.10.refs_6_
  32.9 0.1 collective-permute-start.11
  33.0 4.4 %collective-permute-done.6.refs_2_ = bf16[384,768]{1,0:T(8,128)(2,1)S(1)} collective-permute-done((bf16[384,768]{1,0:T(8,128)(2,1)S(1)}, bf16[384,768]{1,0:T(8,128)(2,1)S(1)}, u32[]{:S(2)}, u32[]{:S(2)}) %collective-permute-start.6) | collective-permute-done | bytes 589856 | tf_op jit(solution)/shard_map/ppermute | solution.py:220
  37.4 0.0 collective-permute-start.7
  37.4 0.0 collective-permute-done.8.refs_4_
  37.4 0.5 collective-permute-start.9
  38.0 0.6 broadcast_select_fusion
  38.6 0.0 collective-permute-done.20.queries
  38.6 3.6 %collective-permute-start.22 = (bf16[256,768]{1,0:T(8,128)(2,1)S(1)}, bf16[256,768]{1,0:T(8,128)(2,1)S(1)}, u32[]{:S(2)}, u32[]{:S(2)}) collective-permute-start(bf16[256,768]{1,0:T(8,128)(2,1)S(1)} %copy-done.4), channel_id=1, source_target_pairs={{0,24},{8,16},{16,8},{24,0},{1,25},{9,17},{17,9},{25,1},{2,26},{10... | collective-permute-start | bytes 1179656 | tf_op jit(solution)/shard_map/ppermute | solution.py:220
  42.2 0.0 collective-permute-done.11.refs_7_
  42.2 0.0 collective-permute-done.7.refs_3_
  42.2 0.0 collective-permute-done.9.refs_5_
  42.2 2.5 %score.5 = f32[2,2,128]{2,1,0:T(2,128)S(1)} custom-call(s32[3]{0:T(128)S(1)} %pad_add_fusion.place, bf16[256,768]{1,0:T(8,128)(2,1)S(1)} %collective-permute-done.20.queries, f32[2,128]{1,0:T(2,128)S(1)} %bitcast.27, f32[1,3072]{1,0:T(1,128)S(1)} %get-tuple-element.20.log_weight, f32[1,3072]{1,0:T(1,128)S(1)} %get-tuple-element.16.row_ids, ...), custom_call_target="tpu_custom_call" | custom-call | flops 1207959552 | bytes 5151756 | tf_op jit(solution)/shard_map/score/pallas_call | solution.py:207
  44.7 0.7 collective-permute-start.21
  45.4 0.0 collective-permute-done.18.queries
  45.4 2.5 %score.4 = f32[2,2,128]{2,1,0:T(2,128)S(1)} custom-call(s32[3]{0:T(128)S(1)} %pad_add_fusion.place, bf16[256,768]{1,0:T(8,128)(2,1)S(1)} %collective-permute-done.18.queries, f32[2,128]{1,0:T(2,128)S(1)} %bitcast.26, f32[1,3072]{1,0:T(1,128)S(1)} %get-tuple-element.23.log_weight, f32[1,3072]{1,0:T(1,128)S(1)} %get-tuple-element.16.row_ids, ...), custom_call_target="tpu_custom_call" | custom-call | flops 1207959552 | bytes 5151756 | tf_op jit(solution)/shard_map/score/pallas_call | solution.py:207
  48.0 1.6 %collective-permute-start.19 = (f32[2,2,128]{2,1,0:T(2,128)S(1)}, f32[2,2,128]{2,1,0:T(2,128)S(1)}, u32[]{:S(2)}, u32[]{:S(2)}) collective-permute-start(f32[2,2,128]{2,1,0:T(2,128)S(1)} %score.4), channel_id=1, source_target_pairs={{0,8},{8,0},{16,24},{24,16},{1,9},{9,1},{17,25},{25,17},{2,10},{10... | collective-permute-start | bytes 6152 | tf_op jit(solution)/shard_map/ppermute | solution.py:220
  49.6 1.6 %pack.1 = bf16[320,768]{1,0:T(8,128)(2,1)S(1)} custom-call(s32[3]{0:T(128)S(1)} %pad_add_fusion.place, bf16[320,1024]{1,0:T(8,128)(2,1)S(1)} %get-tuple-element.12.select, bf16[512,768]{1,0:T(8,128)(2,1)S(1)} %copy-done.1, bf16[256,768]{1,0:T(8,128)(2,1)S(1)} %copy-done.3, bf16[384,768]{1,0:T(8,128)(2,1)S(1)} %collective-permute-done.6.refs_2_, ...), custom_call_target="tpu_custom_call" | custom-call | bytes 5865484 | tf_op jit(solution)/shard_map/pack/pallas_call | solution.py:207
  51.2 0.4 collective-permute-done.22.queries
  51.6 2.7 %score.6 = f32[2,2,128]{2,1,0:T(2,128)S(1)} custom-call(s32[3]{0:T(128)S(1)} %pad_add_fusion.place, bf16[256,768]{1,0:T(8,128)(2,1)S(1)} %collective-permute-done.22.queries, f32[2,128]{1,0:T(2,128)S(1)} %bitcast.25, f32[1,3072]{1,0:T(1,128)S(1)} %get-tuple-element.22.log_weight, f32[1,3072]{1,0:T(1,128)S(1)} %get-tuple-element.16.row_ids, ...), custom_call_target="tpu_custom_call" | custom-call | flops 1207959552 | bytes 5151756 | tf_op jit(solution)/shard_map/score/pallas_call | solution.py:207
  54.3 3.6 %collective-permute-start.23 = (f32[2,2,128]{2,1,0:T(2,128)S(1)}, f32[2,2,128]{2,1,0:T(2,128)S(1)}, u32[]{:S(2)}, u32[]{:S(2)}) collective-permute-start(f32[2,2,128]{2,1,0:T(2,128)S(1)} %score.6), channel_id=1, source_target_pairs={{0,24},{8,16},{16,8},{24,0},{1,25},{9,17},{17,9},{25,1},{2,26},{10... | collective-permute-start | bytes 6152 | tf_op jit(solution)/shard_map/ppermute | solution.py:220
  57.9 6.1 %collective-permute-start.12 = (bf16[64,768]{1,0:T(8,128)(2,1)S(1)}, bf16[64,768]{1,0:T(8,128)(2,1)S(1)}, u32[]{:S(2)}, u32[]{:S(2)}) collective-permute-start(bf16[64,768]{1,0:T(8,128)(2,1)S(1)} %get-tuple-element.19), channel_id=1, source_target_pairs={{0,8},{8,0},{16,24},{24,16},{1,9},{9,1},{17,25},{25,17},{2,10},{10... | collective-permute-start | bytes 294920 | tf_op jit(solution)/shard_map/ppermute | solution.py:220
  64.0 0.0 collective-permute-start.14
  64.0 2.5 %score.7 = f32[2,2,128]{2,1,0:T(2,128)S(1)} custom-call(s32[3]{0:T(128)S(1)} %pad_add_fusion.place, bf16[256,768]{1,0:T(8,128)(2,1)S(1)} %copy-done.4, f32[2,128]{1,0:T(2,128)S(1)} %bitcast.24, f32[1,3072]{1,0:T(1,128)S(1)} %get-tuple-element.21.log_weight, f32[1,3072]{1,0:T(1,128)S(1)} %get-tuple-element.16.row_ids, f32[1,3072]{1,0:T(1,128)S(1)} %get-tuple-element.28.scale, ...), custom_call_target="tpu_custom_call" | custom-call | flops 1207959552 | bytes 5151756 | tf_op jit(solution)/shard_map/score/pallas_call | solution.py:207
  66.6 0.0 collective-permute-done.21
  66.6 2.4 %collective-permute-start.16 = (bf16[64,768]{1,0:T(8,128)(2,1)S(1)}, bf16[64,768]{1,0:T(8,128)(2,1)S(1)}, u32[]{:S(2)}, u32[]{:S(2)}) collective-permute-start(bf16[64,768]{1,0:T(8,128)(2,1)S(1)} %get-tuple-element.17), channel_id=1, source_target_pairs={{0,24},{8,16},{16,8},{24,0},{1,25},{9,17},{17,9},{25,1},{2,26},{10... | collective-permute-start | bytes 294920 | tf_op jit(solution)/shard_map/ppermute | solution.py:220
  69.0 0.0 collective-permute-done.19
  69.0 0.0 collective-permute-done.23
  69.0 0.0 collective-permute-done.12.refs_1_
  69.0 0.1 collective-permute-start.13
  69.1 4.1 %collective-permute-done.14.refs_3_ = bf16[64,768]{1,0:T(8,128)(2,1)S(1)} collective-permute-done((bf16[64,768]{1,0:T(8,128)(2,1)S(1)}, bf16[64,768]{1,0:T(8,128)(2,1)S(1)}, u32[]{:S(2)}, u32[]{:S(2)}) %collective-permute-start.14) | collective-permute-done | bytes 98336 | tf_op jit(solution)/shard_map/ppermute | solution.py:220
  73.2 0.0 collective-permute-start.15
  73.2 0.0 collective-permute-done.16.refs_5_
  73.2 0.5 collective-permute-start.17
  73.7 0.6 fusion.2
  74.3 0.0 collective-permute-done.13.refs_2_
  74.3 0.2 collective-permute-done.15.refs_4_
  74.5 0.2 collective-permute-done.17.refs_6_
  74.7 2.5 %apply.1 = bf16[512,768]{1,0:T(8,128)(2,1)} custom-call(f32[512,512]{1,0:T(8,128)S(1)} %get-tuple-element.11.select, bf16[512,768]{1,0:T(8,128)(2,1)S(1)} %copy-done.1, bf16[128,768]{1,0:T(8,128)(2,1)S(1)} %slice.93.refs_0_, bf16[64,768]{1,0:T(8,128)(2,1)S(1)} %collective-permute-done.12.refs_1_, bf16[64,768]{1,0:T(8,128)(2,1)S(1)} %collective-permute-done.13.refs_2_, ...), custom_call_target="tpu_custom_call" | custom-call | bytes 3407872 | tf_op jit(solution)/shard_map/apply/pallas_call | solution.py:207
  (33 shorter events, 0.3 us)
Async XLA Ops:
  0.6 11.8 %copy-start.7 = (s32[1,2048]{1,0:T(1,128)S(1)}, s32[1,2048]{1,0:T(1,128)}, u32[]{:S(2)}) copy-start(s32[1,2048]{1,0:T(1,128)} %param.11) | copy-start | bytes 24580
  0.7 0.7 copy-start.5
  0.7 0.7 copy-start.6
  1.4 1.1 %copy-start = (bf16[512,768]{1,0:T(8,128)(2,1)S(1)}, bf16[512,768]{1,0:T(8,128)(2,1)}, u32[]{:S(2)}) copy-start(bf16[512,768]{1,0:T(8,128)(2,1)} %refs_0_.9) | copy-start | bytes 2359300
  2.6 1.0 %copy-start.2 = (bf16[256,768]{1,0:T(8,128)(2,1)S(1)}, bf16[256,768]{1,0:T(8,128)(2,1)}, u32[]{:S(2)}) copy-start(bf16[256,768]{1,0:T(8,128)(2,1)} %refs_1_.9) | copy-start | bytes 1179652
  3.5 8.9 %copy-start.8 = (s32[256]{0:T(256)S(1)}, s32[256]{0:T(256)}, u32[]{:S(2)}) copy-start(s32[256]{0:T(256)} %param.13) | copy-start | bytes 3076
  3.6 17.6 %copy-start.4 = (bf16[256,768]{1,0:T(8,128)(2,1)S(1)}, bf16[256,768]{1,0:T(8,128)(2,1)}, u32[]{:S(2)}) copy-start(bf16[256,768]{1,0:T(8,128)(2,1)} %queries.1) | copy-start | bytes 1179652
  3.6 38.6 %copy-start.1 = (bf16[512,768]{1,0:T(8,128)(2,1)S(1)}, bf16[512,768]{1,0:T(8,128)(2,1)}, u32[]{:S(2)}) copy-start(bf16[512,768]{1,0:T(8,128)(2,1)} %refs_0_.9) | copy-start | bytes 2359300
  4.4 37.8 %copy-start.3 = (bf16[256,768]{1,0:T(8,128)(2,1)S(1)}, bf16[256,768]{1,0:T(8,128)(2,1)}, u32[]{:S(2)}) copy-start(bf16[256,768]{1,0:T(8,128)(2,1)} %refs_1_.9) | copy-start | bytes 1179652
  4.4 8.0 %collective-permute-start = (f32[12,128]{1,0:T(8,128)S(1)}, f32[12,128]{1,0:T(8,128)S(1)}, u32[]{:S(2)}, u32[]{:S(2)}) collective-permute-start(f32[12,128]{1,0:T(8,128)S(1)} %get-tuple-element.10), channel_id=1, source_target_pairs={{0,2},{2,0},{4,6},{6,4},{1,3},{3,1},{5,7},{7,5},{8,10},{10,8},{12,... | collective-permute-start | bytes 18440 | tf_op jit(solution)/shard_map/ppermute | solution.py:220
  7.4 5.2 %collective-permute-start.1 = (f32[12,128]{1,0:T(8,128)S(1)}, f32[12,128]{1,0:T(8,128)S(1)}, u32[]{:S(2)}, u32[]{:S(2)}) collective-permute-start(f32[12,128]{1,0:T(8,128)S(1)} %get-tuple-element.10), channel_id=1, source_target_pairs={{0,4},{2,6},{4,0},{6,2},{1,5},{3,7},{5,1},{7,3},{8,12},{10,14},{12... | collective-permute-start | bytes 18440 | tf_op jit(solution)/shard_map/ppermute | solution.py:220
  8.9 4.7 %collective-permute-start.2 = (f32[12,128]{1,0:T(8,128)S(1)}, f32[12,128]{1,0:T(8,128)S(1)}, u32[]{:S(2)}, u32[]{:S(2)}) collective-permute-start(f32[12,128]{1,0:T(8,128)S(1)} %get-tuple-element.10), channel_id=1, source_target_pairs={{0,6},{2,4},{4,2},{6,0},{1,7},{3,5},{5,3},{7,1},{8,14},{10,12},{12... | collective-permute-start | bytes 18440 | tf_op jit(solution)/shard_map/ppermute | solution.py:220
  9.0 24.0 %collective-permute-start.10 = (bf16[384,768]{1,0:T(8,128)(2,1)S(1)}, bf16[384,768]{1,0:T(8,128)(2,1)S(1)}, u32[]{:S(2)}, u32[]{:S(2)}) collective-permute-start(bf16[384,768]{1,0:T(8,128)(2,1)S(1)} %get-tuple-element.13), channel_id=1, source_target_pairs={{0,6},{2,4},{4,2},{6,0},{1,7},{3,5},{5,3},{7,1},{8,14},{10,12},{12... | collective-permute-start | bytes 1769480 | tf_op jit(solution)/shard_map/ppermute | solution.py:220
  11.9 25.5 %collective-permute-start.6 = (bf16[384,768]{1,0:T(8,128)(2,1)S(1)}, bf16[384,768]{1,0:T(8,128)(2,1)S(1)}, u32[]{:S(2)}, u32[]{:S(2)}) collective-permute-start(bf16[384,768]{1,0:T(8,128)(2,1)S(1)} %get-tuple-element.13), channel_id=1, source_target_pairs={{0,2},{2,0},{4,6},{6,4},{1,3},{3,1},{5,7},{7,5},{8,10},{10,8},{12,... | collective-permute-start | bytes 1769480 | tf_op jit(solution)/shard_map/ppermute | solution.py:220
  12.4 24.9 %collective-permute-start.8 = (bf16[384,768]{1,0:T(8,128)(2,1)S(1)}, bf16[384,768]{1,0:T(8,128)(2,1)S(1)}, u32[]{:S(2)}, u32[]{:S(2)}) collective-permute-start(bf16[384,768]{1,0:T(8,128)(2,1)S(1)} %get-tuple-element.13), channel_id=1, source_target_pairs={{0,4},{2,6},{4,0},{6,2},{1,5},{3,7},{5,1},{7,3},{8,12},{10,14},{12... | collective-permute-start | bytes 1769480 | tf_op jit(solution)/shard_map/ppermute | solution.py:220
  13.7 4.2 %collective-permute-start.3 = (f32[3328]{0:T(1024)S(1)}, f32[3328]{0:T(1024)S(1)}, u32[]{:S(2)}, u32[]{:S(2)}) collective-permute-start(f32[3328]{0:T(1024)S(1)} %pad_maximum_fusion.3), channel_id=1, source_target_pairs={{0,8},{8,0},{16,24},{24,16},{1,9},{9,1},{17,25},{25,17},{2,10},{10... | collective-permute-start | bytes 39944 | tf_op jit(solution)/shard_map/ppermute | solution.py:220
  15.3 5.8 %collective-permute-start.4 = (f32[3328]{0:T(1024)S(1)}, f32[3328]{0:T(1024)S(1)}, u32[]{:S(2)}, u32[]{:S(2)}) collective-permute-start(f32[3328]{0:T(1024)S(1)} %pad_maximum_fusion.3), channel_id=1, source_target_pairs={{0,16},{8,24},{16,0},{24,8},{1,17},{9,25},{17,1},{25,9},{2,18},{10... | collective-permute-start | bytes 39944 | tf_op jit(solution)/shard_map/ppermute | solution.py:220
  17.9 5.9 %collective-permute-start.5 = (f32[3328]{0:T(1024)S(1)}, f32[3328]{0:T(1024)S(1)}, u32[]{:S(2)}, u32[]{:S(2)}) collective-permute-start(f32[3328]{0:T(1024)S(1)} %pad_maximum_fusion.3), channel_id=1, source_target_pairs={{0,24},{8,16},{16,8},{24,0},{1,25},{9,17},{17,9},{25,1},{2,26},{10... | collective-permute-start | bytes 39944 | tf_op jit(solution)/shard_map/ppermute | solution.py:220
  21.1 17.4 %collective-permute-start.20 = (bf16[256,768]{1,0:T(8,128)(2,1)S(1)}, bf16[256,768]{1,0:T(8,128)(2,1)S(1)}, u32[]{:S(2)}, u32[]{:S(2)}) collective-permute-start(bf16[256,768]{1,0:T(8,128)(2,1)S(1)} %copy-done.4), channel_id=1, source_target_pairs={{0,16},{8,24},{16,0},{24,8},{1,17},{9,25},{17,1},{25,9},{2,18},{10... | collective-permute-start | bytes 1179656 | tf_op jit(solution)/shard_map/ppermute | solution.py:220
  23.7 21.7 %collective-permute-start.18 = (bf16[256,768]{1,0:T(8,128)(2,1)S(1)}, bf16[256,768]{1,0:T(8,128)(2,1)S(1)}, u32[]{:S(2)}, u32[]{:S(2)}) collective-permute-start(bf16[256,768]{1,0:T(8,128)(2,1)S(1)} %copy-done.4), channel_id=1, source_target_pairs={{0,8},{8,0},{16,24},{24,16},{1,9},{9,1},{17,25},{25,17},{2,10},{10... | collective-permute-start | bytes 1179656 | tf_op jit(solution)/shard_map/ppermute | solution.py:220
  32.9 9.3 %collective-permute-start.11 = (bf16[384,768]{1,0:T(8,128)(2,1)S(1)}, bf16[384,768]{1,0:T(8,128)(2,1)S(1)}, u32[]{:S(2)}, u32[]{:S(2)}) collective-permute-start(bf16[384,768]{1,0:T(8,128)(2,1)S(1)} %collective-permute-done.10.refs_6_), channel_id=1, source_target_pairs={{0,1},{1,0},{2,3},{3,2},{4,5},{5,4},{6,7},{7,6},{8,9},{9,8},{10,11... | collective-permute-start | bytes 1769480 | tf_op jit(solution)/shard_map/ppermute | solution.py:220
  37.4 4.8 %collective-permute-start.7 = (bf16[384,768]{1,0:T(8,128)(2,1)S(1)}, bf16[384,768]{1,0:T(8,128)(2,1)S(1)}, u32[]{:S(2)}, u32[]{:S(2)}) collective-permute-start(bf16[384,768]{1,0:T(8,128)(2,1)S(1)} %collective-permute-done.6.refs_2_), channel_id=1, source_target_pairs={{0,1},{1,0},{2,3},{3,2},{4,5},{5,4},{6,7},{7,6},{8,9},{9,8},{10,11... | collective-permute-start | bytes 1769480 | tf_op jit(solution)/shard_map/ppermute | solution.py:220
  37.4 4.8 %collective-permute-start.9 = (bf16[384,768]{1,0:T(8,128)(2,1)S(1)}, bf16[384,768]{1,0:T(8,128)(2,1)S(1)}, u32[]{:S(2)}, u32[]{:S(2)}) collective-permute-start(bf16[384,768]{1,0:T(8,128)(2,1)S(1)} %collective-permute-done.8.refs_4_), channel_id=1, source_target_pairs={{0,1},{1,0},{2,3},{3,2},{4,5},{5,4},{6,7},{7,6},{8,9},{9,8},{10,11... | collective-permute-start | bytes 1769480 | tf_op jit(solution)/shard_map/ppermute | solution.py:220
  38.6 13.0 %collective-permute-start.22 = (bf16[256,768]{1,0:T(8,128)(2,1)S(1)}, bf16[256,768]{1,0:T(8,128)(2,1)S(1)}, u32[]{:S(2)}, u32[]{:S(2)}) collective-permute-start(bf16[256,768]{1,0:T(8,128)(2,1)S(1)} %copy-done.4), channel_id=1, source_target_pairs={{0,24},{8,16},{16,8},{24,0},{1,25},{9,17},{17,9},{25,1},{2,26},{10... | collective-permute-start | bytes 1179656 | tf_op jit(solution)/shard_map/ppermute | solution.py:220
  44.7 21.8 %collective-permute-start.21 = (f32[2,2,128]{2,1,0:T(2,128)S(1)}, f32[2,2,128]{2,1,0:T(2,128)S(1)}, u32[]{:S(2)}, u32[]{:S(2)}) collective-permute-start(f32[2,2,128]{2,1,0:T(2,128)S(1)} %score.5), channel_id=1, source_target_pairs={{0,16},{8,24},{16,0},{24,8},{1,17},{9,25},{17,1},{25,9},{2,18},{10... | collective-permute-start | bytes 6152 | tf_op jit(solution)/shard_map/ppermute | solution.py:220
  48.0 21.1 %collective-permute-start.19 = (f32[2,2,128]{2,1,0:T(2,128)S(1)}, f32[2,2,128]{2,1,0:T(2,128)S(1)}, u32[]{:S(2)}, u32[]{:S(2)}) collective-permute-start(f32[2,2,128]{2,1,0:T(2,128)S(1)} %score.4), channel_id=1, source_target_pairs={{0,8},{8,0},{16,24},{24,16},{1,9},{9,1},{17,25},{25,17},{2,10},{10... | collective-permute-start | bytes 6152 | tf_op jit(solution)/shard_map/ppermute | solution.py:220
  54.3 14.7 %collective-permute-start.23 = (f32[2,2,128]{2,1,0:T(2,128)S(1)}, f32[2,2,128]{2,1,0:T(2,128)S(1)}, u32[]{:S(2)}, u32[]{:S(2)}) collective-permute-start(f32[2,2,128]{2,1,0:T(2,128)S(1)} %score.6), channel_id=1, source_target_pairs={{0,24},{8,16},{16,8},{24,0},{1,25},{9,17},{17,9},{25,1},{2,26},{10... | collective-permute-start | bytes 6152 | tf_op jit(solution)/shard_map/ppermute | solution.py:220
  57.9 11.1 %collective-permute-start.12 = (bf16[64,768]{1,0:T(8,128)(2,1)S(1)}, bf16[64,768]{1,0:T(8,128)(2,1)S(1)}, u32[]{:S(2)}, u32[]{:S(2)}) collective-permute-start(bf16[64,768]{1,0:T(8,128)(2,1)S(1)} %get-tuple-element.19), channel_id=1, source_target_pairs={{0,8},{8,0},{16,24},{24,16},{1,9},{9,1},{17,25},{25,17},{2,10},{10... | collective-permute-start | bytes 294920 | tf_op jit(solution)/shard_map/ppermute | solution.py:220
  64.0 9.2 %collective-permute-start.14 = (bf16[64,768]{1,0:T(8,128)(2,1)S(1)}, bf16[64,768]{1,0:T(8,128)(2,1)S(1)}, u32[]{:S(2)}, u32[]{:S(2)}) collective-permute-start(bf16[64,768]{1,0:T(8,128)(2,1)S(1)} %get-tuple-element.18), channel_id=1, source_target_pairs={{0,16},{8,24},{16,0},{24,8},{1,17},{9,25},{17,1},{25,9},{2,18},{10... | collective-permute-start | bytes 294920 | tf_op jit(solution)/shard_map/ppermute | solution.py:220
  66.6 6.6 %collective-permute-start.16 = (bf16[64,768]{1,0:T(8,128)(2,1)S(1)}, bf16[64,768]{1,0:T(8,128)(2,1)S(1)}, u32[]{:S(2)}, u32[]{:S(2)}) collective-permute-start(bf16[64,768]{1,0:T(8,128)(2,1)S(1)} %get-tuple-element.17), channel_id=1, source_target_pairs={{0,24},{8,16},{16,8},{24,0},{1,25},{9,17},{17,9},{25,1},{2,26},{10... | collective-permute-start | bytes 294920 | tf_op jit(solution)/shard_map/ppermute | solution.py:220
  69.0 5.3 %collective-permute-start.13 = (bf16[64,768]{1,0:T(8,128)(2,1)S(1)}, bf16[64,768]{1,0:T(8,128)(2,1)S(1)}, u32[]{:S(2)}, u32[]{:S(2)}) collective-permute-start(bf16[64,768]{1,0:T(8,128)(2,1)S(1)} %collective-permute-done.12.refs_1_), channel_id=1, source_target_pairs={{0,1},{1,0},{2,3},{3,2},{4,5},{5,4},{6,7},{7,6},{8,9},{9,8},{10,11... | collective-permute-start | bytes 294920 | tf_op jit(solution)/shard_map/ppermute | solution.py:220
  73.2 1.3 %collective-permute-start.15 = (bf16[64,768]{1,0:T(8,128)(2,1)S(1)}, bf16[64,768]{1,0:T(8,128)(2,1)S(1)}, u32[]{:S(2)}, u32[]{:S(2)}) collective-permute-start(bf16[64,768]{1,0:T(8,128)(2,1)S(1)} %collective-permute-done.14.refs_3_), channel_id=1, source_target_pairs={{0,1},{1,0},{2,3},{3,2},{4,5},{5,4},{6,7},{7,6},{8,9},{9,8},{10,11... | collective-permute-start | bytes 294920 | tf_op jit(solution)/shard_map/ppermute | solution.py:220
  73.2 1.5 %collective-permute-start.17 = (bf16[64,768]{1,0:T(8,128)(2,1)S(1)}, bf16[64,768]{1,0:T(8,128)(2,1)S(1)}, u32[]{:S(2)}, u32[]{:S(2)}) collective-permute-start(bf16[64,768]{1,0:T(8,128)(2,1)S(1)} %collective-permute-done.16.refs_5_), channel_id=1, source_target_pairs={{0,1},{1,0},{2,3},{3,2},{4,5},{5,4},{6,7},{7,6},{8,9},{9,8},{10,11... | collective-permute-start | bytes 294920 | tf_op jit(solution)/shard_map/ppermute | solution.py:220

commit v3 on v2

--- a/solution.py
+++ b/solution.py
@@ -124,15 +124,18 @@
             size = cap if plane == 0 else share
             skip = 0 if plane == 0 else (core ^ part) * share
             slot = one_hot(take_rank[plane : plane + 1, :] - skip, size)
-            first = plane * cap + part * share
+            first = plane and cap + (part * (planes - 1) + plane - 1) * share
             apply_out[:, first : first + size] = lax.dot_general(row, slot, NT, preferred_element_type=jnp.float32)
 
 
 def piece_offset(place, piece):
-    column, size, flip = piece
+    column, size, flip, by_core = piece
     if flip is None:
         return column
-    return pl.multiple_of(column + (place[2] ^ flip) * size, size)
+    column += (place[2] ^ flip) * size
+    if by_core is not None:
+        column += (place[2] ^ by_core) * size * 2
+    return pl.multiple_of(column, size)
 
 
 def pack_kernel(place, select, *refs, pieces):
@@ -162,9 +165,15 @@
     return jnp.broadcast_to(row, (LANES, LANES)).T
 
 
-def score_kernel(place, queries, positive, log_weight, row_ids, scale, *refs, pieces):
-    out, total, pos_total, q_scale, pos_b = refs[-5:]
+def score_kernel(place, *refs, pieces, sources):
+    positive, log_weight, row_ids, scale = refs[sources : sources + 4]
+    out, total, pos_total, q_scale, pos_b, chosen = refs[-6:]
+    queries = refs[0]
     count, width = queries.shape
+    if sources == 2:
+        at_end = (place[0] == 0) | (place[0] == 3)
+        chosen[...] = jnp.where(at_end, refs[0][...], refs[1][...])
+        queries = chosen
     for block in range(count // LANES):
         part = slice(block * LANES, (block + 1) * LANES)
         values = queries[part, :].astype(jnp.float32)
@@ -176,7 +185,7 @@
     for source, start, size, column in pieces:
         first = piece_offset(place, column)
         raw = lax.dot_general(
-            queries[...], refs[source][start : start + size, :], NT, preferred_element_type=jnp.float32
+            queries[...], refs[sources + 4 + source][start : start + size, :], NT, preferred_element_type=jnp.float32
         )
         sums = total[...]
         positives = pos_total[...]
@@ -198,12 +207,11 @@
     return pl.BlockSpec(memory_space=memory)
 
 
-def call(kernel, name, outs, place, *operands, scratch=(), flops=0, **options):
+def call(kernel, name, outs, place, *operands, scratch=(), **options):
     specs = [whole()] * len(operands)
     if place is not None:
         specs = [whole(pltpu.SMEM)] + specs
         operands = (place, *operands)
-    moved = sum(math.prod(x.shape) * x.dtype.itemsize for x in (*operands, *outs))
     return pl.pallas_call(
         functools.partial(kernel, **options),
         out_shape=tuple(outs),
@@ -211,13 +219,27 @@
         out_specs=tuple(whole() for _ in outs),
         scratch_shapes=list(scratch),
         compiler_params=pltpu.CompilerParams(vmem_limit_bytes=VMEM_LIMIT),
-        cost_estimate=pl.CostEstimate(flops=flops, bytes_accessed=moved, transcendentals=0),
+        cost_estimate=pl.CostEstimate(flops=1, bytes_accessed=1, transcendentals=0),
         name=name,
     )(*operands)
 
 
 def swap(values, axis, flip):
     return lax.ppermute(values, axis, [(i, i ^ flip) for i in range(lax.axis_size(axis))])
+
+
+def gather_line(values, small):
+    planes = lax.axis_size("outer")
+    if planes != 4:
+        return [(swap(values, "outer", s),) for s in range(1, planes)], small
+    middle, outward = [(1, 2), (2, 1)], [(1, 0), (2, 3)]
+    beside = swap(values, "outer", 1)
+    across = lax.ppermute(values, "outer", middle)
+    beside, across, small = lax.optimization_barrier((beside, across, small))
+    from_end = lax.ppermute(beside, "outer", middle)
+    to_end = lax.ppermute(across, "outer", outward)
+    last = lax.ppermute(from_end, "outer", outward)
+    return [(beside,), (to_end, from_end), (last, across)], small
 
 
 def on_device(table, ages, refresh_ids, fresh_rows, neg_ids, queries, pos_ids):
@@ -251,8 +273,6 @@
         replicas=replicas,
     )
     metas = jnp.stack([meta] + [swap(meta, "inner", s) for s in range(1, owners_plane)])
-    got_queries = [queries] + [swap(queries, "outer", s) for s in range(1, planes)]
-    got_rows = [swap(rows_half, "inner", s) for s in range(1, owners_plane)]
     cuts = [refresh_dev, rows_dev, rows_dev, refresh_dev]
     ends = [sum(cuts[: i + 1]) // LANES for i in range(len(cuts))]
 
@@ -262,6 +282,8 @@
     ref_plane, log_weight_plane = piece(0), piece(1)
     scale_plane = jnp.concatenate([piece(2), piece(3)], axis=1)
     line = jnp.concatenate([ref_plane[0], neg_ids[0].astype(f32), pos_ids.astype(f32)])
+    got_queries, line = gather_line(queries, line)
+    got_queries = [(queries,)] + got_queries
     lines = jnp.stack([line] + [swap(line, "outer", s) for s in range(1, planes)])
     ref_all = lines[:, :plane_refresh].astype(jnp.int32)
     neg_line = lines[:, plane_refresh : plane_refresh + list_size].astype(jnp.int32)
@@ -288,24 +310,32 @@
     )
     new_ages = jnp.where(own.reshape(rows_dev) > 0, 0, ages)
 
-    if replicas == 2:
+    if replicas == 2 and owners_plane == 4:
+        axes = ("inner", "query")
+        first = [(2 * i + c, 2 * (i ^ (1 + c)) + c) for i in range(4) for c in range(2)]
+        second = [(2 * i + c, 2 * (i ^ (2 - c)) + c) for i in range(4) for c in range(2)]
+        near = lax.ppermute(rows_half, axes, first)
+        side = lax.ppermute(rows_half, axes, second)
+        far = lax.ppermute(near, axes, second)
         buffers = [table, fresh_rows]
-        table_pieces = [(0, 0, rows_dev, (0, rows_dev, None))]
-        fresh_pieces = [(1, 0, refresh_dev, (0, refresh_dev, None))]
-        for s in range(1, owners_plane):
-            for flip, rows in enumerate((got_rows[s - 1], swap(got_rows[s - 1], "query", 1))):
-                table_pieces.append((len(buffers), 0, table_half, (s * rows_dev, table_half, flip)))
-                fresh_pieces.append((len(buffers), table_half, fresh_half, (s * refresh_dev, fresh_half, flip)))
+        table_pieces = [(0, 0, rows_dev, (0, rows_dev, None, None))]
+        fresh_pieces = [(1, 0, refresh_dev, (0, refresh_dev, None, None))]
+        for slot, by_core, mine in ((1, 0, near), (1, 1, side), (3, None, far)):
+            for flip, rows in enumerate((mine, swap(mine, "query", 1))):
+                by = None if by_core is None else by_core ^ flip
+                table_pieces.append((len(buffers), 0, table_half, (slot * rows_dev, table_half, flip, by)))
+                fresh_pieces.append((len(buffers), table_half, fresh_half, (slot * refresh_dev, fresh_half, flip, by)))
                 buffers.append(rows)
     else:
-        gathered = lax.all_gather(jnp.stack([rows_half] + got_rows), "query", axis=0)
+        got_rows = [rows_half] + [swap(rows_half, "inner", s) for s in range(1, owners_plane)]
+        gathered = lax.all_gather(jnp.stack(got_rows), "query", axis=0)
         gathered = jnp.swapaxes(gathered, 0, 1)
         buffers = [
             gathered[:, :, :table_half].reshape(plane_rows, width),
             gathered[:, :, table_half:].reshape(plane_refresh, width),
         ]
-        table_pieces = [(0, i * 512, 512, (i * 512, 512, None)) for i in range(plane_rows // 512)]
-        fresh_pieces = [(1, i * 512, 512, (i * 512, 512, None)) for i in range(plane_refresh // 512)]
+        table_pieces = [(0, i * 512, 512, (i * 512, 512, None, None)) for i in range(plane_rows // 512)]
+        fresh_pieces = [(1, i * 512, 512, (i * 512, 512, None, None)) for i in range(plane_refresh // 512)]
 
     def shift(pieces, columns):
         return [(a, b, c, (d[0] + columns, *d[1:])) for a, b, c, d in pieces]
@@ -313,11 +343,12 @@
     (packed,) = call(
         pack_kernel, "pack", [jax.ShapeDtypeStruct((pack.shape[0], width), bf16)], place, pack, *buffers, pieces=fresh_pieces
     )
-    arrived = [packed[:cap]]
+    parts = []
     for s in range(1, planes):
         first = cap + (s - 1) * share
-        part = swap(packed[first : first + share], "outer", s)
-        arrived += [part] + [swap(part, "query", flip) for flip in range(1, replicas)]
+        parts.append(swap(packed[first : first + share], "outer", s))
+    parts = jnp.concatenate(parts)
+    arrived = [packed[:cap], parts] + [swap(parts, "query", flip) for flip in range(1, replicas)]
 
     pieces = table_pieces + shift(fresh_pieces, plane_rows)
     mine = None
@@ -327,15 +358,15 @@
             "score",
             [jax.ShapeDtypeStruct((2, query_count // LANES, LANES), f32)],
             place,
-            got_queries[s],
+            *got_queries[s],
             positive[s],
             lw[s : s + 1],
             row_ids,
             scale_plane,
             *buffers,
-            scratch=[pltpu.VMEM((query_count, LANES), f32)] * 4,
-            flops=2 * query_count * all_rows * width,
+            scratch=[pltpu.VMEM((query_count, LANES), f32)] * 4 + [pltpu.VMEM((query_count, width), bf16)],
             pieces=pieces,
+            sources=len(got_queries[s]),
         )
         if s:
             partial = swap(partial, "outer", s)

time: 77.4 us -> 69.4 us (0.90)
  starting transfers between devices: 39 us -> 29.3 us
  waiting for transfers between devices: 11.4 us -> 13.8 us
  Pallas kernels: 21.6 us -> 20.6 us
    ppermute x24 -> x17, starting transfers between devices: 39 us -> 20.1 us  [swap(): lax.ppermute(values, axis, [(i, i ^ flip) for i in range(lax.axis_size(ax...]
    ppermute x0 -> x7, starting transfers between devices: none -> 9.21 us  [the longest x1 3 us: on_device(): near = lax.ppermute(rows_half, axes, first)]
    ppermute x24 -> x17, waiting for transfers between devices: 11.4 us -> 13.8 us  [swap(): lax.ppermute(values, axis, [(i, i ^ flip) for i in range(lax.axis_size(ax...]
    pallas_call x8, Pallas kernels: 21.6 us -> 20.6 us  [call(): pl.pallas_call(functools.partial(kernel, **options), out_shape=tuple(outs...]
    unnamed x18 -> x20, local copies, waits for them, and re-layouts: 2.84 us -> 2.86 us
  transfers between devices with their start and end apart: 24 -> 24, of which waited for: 7 -> 8; matrix products, arithmetic and copies ran while one was open for 2% -> 2% of each run, Pallas kernels for 24% -> 26%
where the time goes in v3:
time: 69.4 us; the launch traced here: 69.1 us
  starting transfers between devices  29.3 us (42%)
  Pallas kernels  20.6 us (30%)
  waiting for transfers between devices  13.8 us (20%)
  local copies, waits for them, and re-layouts  2.95 us (4%)
  other arithmetic  1.41 us (2%)
  between operations  0.94 us (1%)
    pallas_call x8, Pallas kernels, call(): pl.pallas_call(functools.partial(kernel, **options), out_shape=tuple(outs...  20.6 us
    ppermute x17, starting transfers between devices, swap(): lax.ppermute(values, axis, [(i, i ^ flip) for i in range(lax.axis_size(ax...  20.1 us
    ppermute x17, waiting for transfers between devices, swap(): lax.ppermute(values, axis, [(i, i ^ flip) for i in range(lax.axis_size(ax...  13.8 us
    ppermute x1, starting transfers between devices, on_device(): near = lax.ppermute(rows_half, axes, first)  3 us
    unnamed x20, local copies, waits for them, and re-layouts  2.86 us
    ppermute x1, starting transfers between devices, on_device(): far = lax.ppermute(near, axes, second)  1.52 us
    ppermute x1, starting transfers between devices, gather_line(): last = lax.ppermute(from_end, 'outer', outward)  1.47 us
  transfers between devices with their start and end apart: 24, of which 8 were waited for; matrix products, arithmetic and copies ran while one was open for 2% of the time, Pallas kernels for 26%

profile of v3, /device:TPU:0, one launch (start us, length us, event | category | flops | bytes accessed | tf_op | source)
XLA Modules:
  0.0 69.1 jit_solution(16338548858736454460)
XLA Ops:
  0.6 0.0 copy-start.7
  0.6 0.1 pad_add_fusion.place
  0.7 0.7 copy-done.5
  1.4 0.0 copy-done.6
  1.4 1.1 %copy-done = bf16[512,768]{1,0:T(8,128)(2,1)S(1)} copy-done((bf16[512,768]{1,0:T(8,128)(2,1)S(1)}, bf16[512,768]{1,0:T(8,128)(2,1)}, u32[]{:S(2)}) %copy-start) | copy-done | bytes 786456
  2.6 1.0 %copy-done.2 = bf16[256,768]{1,0:T(8,128)(2,1)S(1)} copy-done((bf16[256,768]{1,0:T(8,128)(2,1)S(1)}, bf16[256,768]{1,0:T(8,128)(2,1)}, u32[]{:S(2)}) %copy-start.2) | copy-done | bytes 393240
  3.6 0.8 %prep.1 = (bf16[384,768]{1,0:T(8,128)(2,1)S(1)}, f32[12,128]{1,0:T(8,128)S(1)}) custom-call(s32[3]{0:T(128)S(1)} %pad_add_fusion.place, bf16[512,768]{1,0:T(8,128)(2,1)S(1)} %copy-done, bf16[256,768]{1,0:T(8,128)(2,1)S(1)} %copy-done.2, s32[4,128]{1,0:T(4,128)S(1)} %bitcast.23, s32[2,128]{1,0:T(2,128)S(1)} %bitcast.28), custom_call_target="tpu_custom_call" | custom-call | flops 1 | bytes 1 | tf_op jit(solution)/shard_map/prep/pallas_call | solution.py:215
  4.4 3.0 %collective-permute-start.8 = (bf16[384,768]{1,0:T(8,128)(2,1)S(1)}, bf16[384,768]{1,0:T(8,128)(2,1)S(1)}, u32[]{:S(2)}, u32[]{:S(2)}) collective-permute-start(bf16[384,768]{1,0:T(8,128)(2,1)S(1)} %get-tuple-element.17), channel_id=1, source_target_pairs={{0,2},{1,5},{2,0},{3,7},{4,6},{5,1},{6,4},{7,3},{8,10},{9,13},{10,... | collective-permute-start | bytes 1769480 | tf_op jit(solution)/shard_map/ppermute | solution.py:317
  7.4 1.6 %collective-permute-start = (bf16[256,768]{1,0:T(8,128)(2,1)S(1)}, bf16[256,768]{1,0:T(8,128)(2,1)S(1)}, u32[]{:S(2)}, u32[]{:S(2)}) collective-permute-start(bf16[256,768]{1,0:T(8,128)(2,1)S(1)} %copy-done.4), channel_id=1, source_target_pairs={{0,8},{8,0},{16,24},{24,16},{1,9},{9,1},{17,25},{25,17},{2,10},{10... | collective-permute-start | bytes 1179656 | tf_op jit(solution)/shard_map/ppermute | solution.py:228
  9.0 0.7 collective-permute-start.1
  9.7 0.6 collective-permute-start.2
  10.3 1.5 %collective-permute-start.3 = (f32[12,128]{1,0:T(8,128)S(1)}, f32[12,128]{1,0:T(8,128)S(1)}, u32[]{:S(2)}, u32[]{:S(2)}) collective-permute-start(f32[12,128]{1,0:T(8,128)S(1)} %get-tuple-element.13), channel_id=1, source_target_pairs={{0,4},{2,6},{4,0},{6,2},{1,5},{3,7},{5,1},{7,3},{8,12},{10,14},{12... | collective-permute-start | bytes 18440 | tf_op jit(solution)/shard_map/ppermute | solution.py:228
  11.8 3.7 %collective-permute-done.2 = f32[12,128]{1,0:T(8,128)S(1)} collective-permute-done((f32[12,128]{1,0:T(8,128)S(1)}, f32[12,128]{1,0:T(8,128)S(1)}, u32[]{:S(2)}, u32[]{:S(2)}) %collective-permute-start.2) | collective-permute-done | bytes 6176 | tf_op jit(solution)/shard_map/ppermute | solution.py:228
  15.5 3.0 %collective-permute-start.4 = (f32[12,128]{1,0:T(8,128)S(1)}, f32[12,128]{1,0:T(8,128)S(1)}, u32[]{:S(2)}, u32[]{:S(2)}) collective-permute-start(f32[12,128]{1,0:T(8,128)S(1)} %get-tuple-element.13), channel_id=1, source_target_pairs={{0,6},{2,4},{4,2},{6,0},{1,7},{3,5},{5,3},{7,1},{8,14},{10,12},{12... | collective-permute-start | bytes 18440 | tf_op jit(solution)/shard_map/ppermute | solution.py:228
  18.6 0.0 collective-permute-done.3
  18.6 0.6 collective-permute-start.10
  19.1 0.0 collective-permute-done.8.refs_2_.refs_7_.refs_8_
  19.1 1.5 %collective-permute-start.12 = (bf16[384,768]{1,0:T(8,128)(2,1)S(1)}, bf16[384,768]{1,0:T(8,128)(2,1)S(1)}, u32[]{:S(2)}, u32[]{:S(2)}) collective-permute-start(bf16[384,768]{1,0:T(8,128)(2,1)S(1)} %collective-permute-done.8.refs_2_.refs_7_.refs_8_), channel_id=1, source_target_pairs={{0,4},{1,3},{2,6},{3,1},{4,0},{5,7},{6,2},{7,5},{8,12},{9,11},{10,... | collective-permute-start | bytes 1769480 | tf_op jit(solution)/shard_map/ppermute | solution.py:319
  20.7 0.0 collective-permute-done.4
  20.7 0.0 collective-permute-done.refs_0_
  20.7 0.0 collective-permute-done.1.refs_1_
  20.7 1.9 %collective-permute-start.5 = (f32[3328]{0:T(1024)S(1)}, f32[3328]{0:T(1024)S(1)}, u32[]{:S(2)}, u32[]{:S(2)}) collective-permute-start(f32[3328]{0:T(1024)S(1)} %pad_maximum_fusion.3), channel_id=1, source_target_pairs={{0,8},{8,0},{16,24},{24,16},{1,9},{9,1},{17,25},{25,17},{2,10},{10... | collective-permute-start | bytes 39944 | tf_op jit(solution)/shard_map/ppermute | solution.py:228
  22.6 2.4 %collective-permute-start.6 = (f32[3328]{0:T(1024)S(1)}, f32[3328]{0:T(1024)S(1)}, u32[]{:S(2)}, u32[]{:S(2)}) collective-permute-start(f32[3328]{0:T(1024)S(1)} %pad_maximum_fusion.3), channel_id=1, source_target_pairs={{0,16},{8,24},{16,0},{24,8},{1,17},{9,25},{17,1},{25,9},{2,18},{10... | collective-permute-start | bytes 39944 | tf_op jit(solution)/shard_map/ppermute | solution.py:228
  25.0 0.2 collective-permute-start.7
  25.3 0.0 collective-permute-done.5
  25.3 0.7 collective-permute-start.20
  26.0 1.3 %collective-permute-done.6 = f32[3328]{0:T(1024)S(1)} collective-permute-done((f32[3328]{0:T(1024)S(1)}, f32[3328]{0:T(1024)S(1)}, u32[]{:S(2)}, u32[]{:S(2)}) %collective-permute-start.6) | collective-permute-done | bytes 13344 | tf_op jit(solution)/shard_map/ppermute | solution.py:228
  27.3 1.3 %collective-permute-start.19 = (bf16[256,768]{1,0:T(8,128)(2,1)S(1)}, bf16[256,768]{1,0:T(8,128)(2,1)S(1)}, u32[]{:S(2)}, u32[]{:S(2)}) collective-permute-start(bf16[256,768]{1,0:T(8,128)(2,1)S(1)} %collective-permute-done.1.refs_1_), channel_id=1, source_target_pairs={{8,0},{16,24},{9,1},{17,25},{10,2},{18,26},{11,3},{19,27},{12,4},{... | collective-permute-start | bytes 1179656 | tf_op jit(solution)/shard_map/ppermute | solution.py:240
  28.6 2.1 %collective-permute-done.7 = f32[3328]{0:T(1024)S(1)} collective-permute-done((f32[3328]{0:T(1024)S(1)}, f32[3328]{0:T(1024)S(1)}, u32[]{:S(2)}, u32[]{:S(2)}) %collective-permute-start.7) | collective-permute-done | bytes 13344 | tf_op jit(solution)/shard_map/ppermute | solution.py:228
  30.8 6.4 %meta.1 = (f32[4,3072]{1,0:T(4,128)S(1)}, f32[1,3072]{1,0:T(1,128)S(1)}, bf16[320,1024]{1,0:T(8,128)(2,1)S(1)}, f32[512,512]{1,0:T(8,128)S(1)}, s32[1,512]{1,0:T(1,128)S(1)}) custom-call(s32[3]{0:T(128)S(1)} %pad_add_fusion.place, s32[4,1024]{1,0:T(4,128)S(1)} %maximum_convert_fusion.ref_ids, s32[4,2048]{1,0:T(4,128)S(1)} %fusion.neg, f32[1,2048]{1,0:T(1,128)S(1)} %bitcast.22), custom_call_target="tpu_custom_call" | custom-call | flops 1 | bytes 1 | tf_op jit(solution)/shard_map/meta/pallas_call | solution.py:215
  37.1 0.1 collective-permute-start.9
  37.2 0.0 collective-permute-done.10.refs_4_.refs_9_.refs_10_
  37.2 0.5 collective-permute-start.11
  37.7 0.0 collective-permute-done.12.refs_6_.refs_11_.refs_12_
  37.7 0.1 collective-permute-start.13
  37.9 0.0 collective-permute-done.20.refs_1_
  37.9 1.5 %collective-permute-start.22 = (bf16[256,768]{1,0:T(8,128)(2,1)S(1)}, bf16[256,768]{1,0:T(8,128)(2,1)S(1)}, u32[]{:S(2)}, u32[]{:S(2)}) collective-permute-start(bf16[256,768]{1,0:T(8,128)(2,1)S(1)} %collective-permute-done.20.refs_1_), channel_id=1, source_target_pairs={{8,0},{16,24},{9,1},{17,25},{10,2},{18,26},{11,3},{19,27},{12,4},{... | collective-permute-start | bytes 1179656 | tf_op jit(solution)/shard_map/ppermute | solution.py:241
  39.4 0.0 collective-permute-done.9.refs_3_.refs_8_.refs_9_
  39.4 0.7 collective-permute-done.11.refs_5_.refs_10_.refs_11_
  40.1 0.8 %collective-permute-done.13.refs_7_.refs_12_.refs_13_ = bf16[384,768]{1,0:T(8,128)(2,1)S(1)} collective-permute-done((bf16[384,768]{1,0:T(8,128)(2,1)S(1)}, bf16[384,768]{1,0:T(8,128)(2,1)S(1)}, u32[]{:S(2)}, u32[]{:S(2)}) %collective-permute-start.13) | collective-permute-done | bytes 589856 | tf_op jit(solution)/shard_map/ppermute | solution.py:228
  40.9 1.6 %pack.1 = bf16[320,768]{1,0:T(8,128)(2,1)S(1)} custom-call(s32[3]{0:T(128)S(1)} %pad_add_fusion.place, bf16[320,1024]{1,0:T(8,128)(2,1)S(1)} %get-tuple-element.16.select, bf16[512,768]{1,0:T(8,128)(2,1)S(1)} %copy-done.1, bf16[256,768]{1,0:T(8,128)(2,1)S(1)} %copy-done.3, bf16[384,768]{1,0:T(8,128)(2,1)S(1)} %collective-permute-done.8.refs_2_.refs_7_.refs_8_, ...), custom_call_target="tpu_custom_call" | custom-call | flops 1 | bytes 1 | tf_op jit(solution)/shard_map/pack/pallas_call | solution.py:215
  42.5 1.3 %collective-permute-start.14 = (bf16[64,768]{1,0:T(8,128)(2,1)S(1)}, bf16[64,768]{1,0:T(8,128)(2,1)S(1)}, u32[]{:S(2)}, u32[]{:S(2)}) collective-permute-start(bf16[64,768]{1,0:T(8,128)(2,1)S(1)} %get-tuple-element.25), channel_id=1, source_target_pairs={{0,8},{8,0},{16,24},{24,16},{1,9},{9,1},{17,25},{25,17},{2,10},{10... | collective-permute-start | bytes 294920 | tf_op jit(solution)/shard_map/ppermute | solution.py:228
  43.8 0.6 broadcast_select_fusion
  44.4 0.0 collective-permute-done.19.refs_0_
  44.4 2.6 %score.5 = f32[2,2,128]{2,1,0:T(2,128)S(1)} custom-call(s32[3]{0:T(128)S(1)} %pad_add_fusion.place, bf16[256,768]{1,0:T(8,128)(2,1)S(1)} %collective-permute-done.19.refs_0_, bf16[256,768]{1,0:T(8,128)(2,1)S(1)} %collective-permute-done.20.refs_1_, f32[2,128]{1,0:T(2,128)S(1)} %bitcast.27, f32[1,3072]{1,0:T(1,128)S(1)} %get-tuple-element.26.refs_3_, ...), custom_call_target="tpu_custom_call" | custom-call | flops 1 | bytes 1 | tf_op jit(solution)/shard_map/score/pallas_call | solution.py:215
  46.9 0.6 collective-permute-start.21
  47.6 2.5 %score.4 = f32[2,2,128]{2,1,0:T(2,128)S(1)} custom-call(s32[3]{0:T(128)S(1)} %pad_add_fusion.place, bf16[256,768]{1,0:T(8,128)(2,1)S(1)} %collective-permute-done.refs_0_, f32[2,128]{1,0:T(2,128)S(1)} %bitcast.26, f32[1,3072]{1,0:T(1,128)S(1)} %get-tuple-element.29.refs_2_, f32[1,3072]{1,0:T(1,128)S(1)} %get-tuple-element.21.refs_3_.refs_4_, ...), custom_call_target="tpu_custom_call" | custom-call | flops 1 | bytes 1 | tf_op jit(solution)/shard_map/score/pallas_call | solution.py:215
  50.1 2.1 %collective-permute-start.18 = (f32[2,2,128]{2,1,0:T(2,128)S(1)}, f32[2,2,128]{2,1,0:T(2,128)S(1)}, u32[]{:S(2)}, u32[]{:S(2)}) collective-permute-start(f32[2,2,128]{2,1,0:T(2,128)S(1)} %score.4), channel_id=1, source_target_pairs={{0,8},{8,0},{16,24},{24,16},{1,9},{9,1},{17,25},{25,17},{2,10},{10... | collective-permute-start | bytes 6152 | tf_op jit(solution)/shard_map/ppermute | solution.py:228
  52.2 0.0 collective-permute-done.22.refs_0_
  52.2 2.5 %score.6 = f32[2,2,128]{2,1,0:T(2,128)S(1)} custom-call(s32[3]{0:T(128)S(1)} %pad_add_fusion.place, bf16[256,768]{1,0:T(8,128)(2,1)S(1)} %collective-permute-done.22.refs_0_, bf16[256,768]{1,0:T(8,128)(2,1)S(1)} %collective-permute-done.1.refs_1_, f32[2,128]{1,0:T(2,128)S(1)} %bitcast.25, f32[1,3072]{1,0:T(1,128)S(1)} %get-tuple-element.28.refs_3_, ...), custom_call_target="tpu_custom_call" | custom-call | flops 1 | bytes 1 | tf_op jit(solution)/shard_map/score/pallas_call | solution.py:215
  54.7 1.9 %collective-permute-start.23 = (f32[2,2,128]{2,1,0:T(2,128)S(1)}, f32[2,2,128]{2,1,0:T(2,128)S(1)}, u32[]{:S(2)}, u32[]{:S(2)}) collective-permute-start(f32[2,2,128]{2,1,0:T(2,128)S(1)} %score.6), channel_id=1, source_target_pairs={{0,24},{8,16},{16,8},{24,0},{1,25},{9,17},{17,9},{25,1},{2,26},{10... | collective-permute-start | bytes 6152 | tf_op jit(solution)/shard_map/ppermute | solution.py:228
  56.6 0.0 collective-permute-start.15
  56.6 2.5 %score.7 = f32[2,2,128]{2,1,0:T(2,128)S(1)} custom-call(s32[3]{0:T(128)S(1)} %pad_add_fusion.place, bf16[256,768]{1,0:T(8,128)(2,1)S(1)} %copy-done.4, f32[2,128]{1,0:T(2,128)S(1)} %bitcast.24, f32[1,3072]{1,0:T(1,128)S(1)} %get-tuple-element.27.refs_2_, f32[1,3072]{1,0:T(1,128)S(1)} %get-tuple-element.21.refs_3_.refs_4_, ...), custom_call_target="tpu_custom_call" | custom-call | flops 1 | bytes 1 | tf_op jit(solution)/shard_map/score/pallas_call | solution.py:215
  59.2 0.0 collective-permute-done.14
  59.2 2.4 %collective-permute-start.16 = (bf16[64,768]{1,0:T(8,128)(2,1)S(1)}, bf16[64,768]{1,0:T(8,128)(2,1)S(1)}, u32[]{:S(2)}, u32[]{:S(2)}) collective-permute-start(bf16[64,768]{1,0:T(8,128)(2,1)S(1)} %get-tuple-element.23), channel_id=1, source_target_pairs={{0,24},{8,16},{16,8},{24,0},{1,25},{9,17},{17,9},{25,1},{2,26},{10... | collective-permute-start | bytes 294920 | tf_op jit(solution)/shard_map/ppermute | solution.py:228
  61.5 2.4 %collective-permute-done.15 = bf16[64,768]{1,0:T(8,128)(2,1)S(1)} collective-permute-done((bf16[64,768]{1,0:T(8,128)(2,1)S(1)}, bf16[64,768]{1,0:T(8,128)(2,1)S(1)}, u32[]{:S(2)}, u32[]{:S(2)}) %collective-permute-start.15) | collective-permute-done | bytes 98336 | tf_op jit(solution)/shard_map/ppermute | solution.py:228
  63.9 1.8 %collective-permute-done.16 = bf16[64,768]{1,0:T(8,128)(2,1)S(1)} collective-permute-done((bf16[64,768]{1,0:T(8,128)(2,1)S(1)}, bf16[64,768]{1,0:T(8,128)(2,1)S(1)}, u32[]{:S(2)}, u32[]{:S(2)}) %collective-permute-start.16) | collective-permute-done | bytes 98336 | tf_op jit(solution)/shard_map/ppermute | solution.py:228
  65.8 0.1 collective-permute-start.17
  65.8 0.0 collective-permute-done.21
  65.9 0.0 collective-permute-done.18
  65.9 0.0 collective-permute-done.23
  65.9 0.6 fusion.2
  66.5 0.9 %collective-permute-done.17.refs_2_ = bf16[192,768]{1,0:T(8,128)(2,1)S(1)} collective-permute-done((bf16[192,768]{1,0:T(8,128)(2,1)S(1)}, bf16[192,768]{1,0:T(8,128)(2,1)S(1)}, u32[]{:S(2)}, u32[]{:S(2)}) %collective-permute-start.17) | collective-permute-done | bytes 294944 | tf_op jit(solution)/shard_map/ppermute | solution.py:228
  67.4 1.7 %apply.1 = bf16[512,768]{1,0:T(8,128)(2,1)} custom-call(f32[512,512]{1,0:T(8,128)S(1)} %get-tuple-element.15.select, bf16[512,768]{1,0:T(8,128)(2,1)S(1)} %copy-done.1, bf16[128,768]{1,0:T(8,128)(2,1)S(1)} %slice.93.refs_0_, bf16[192,768]{1,0:T(8,128)(2,1)S(1)} %constant_dynamic-update-slice_fusion.refs_1_, bf16[192,768]{1,0:T(8,128)(2,1)S(1)} %collective-permute-done.17.refs_2_), custom_call_target="tpu_custom_call" | custom-call | flops 1 | bytes 1 | tf_op jit(solution)/shard_map/apply/pallas_call | solution.py:215
  (36 shorter events, 0.3 us)
Async XLA Ops:
  0.6 17.9 %copy-start.7 = (s32[1,2048]{1,0:T(1,128)S(1)}, s32[1,2048]{1,0:T(1,128)}, u32[]{:S(2)}) copy-start(s32[1,2048]{1,0:T(1,128)} %param.11) | copy-start | bytes 24580
  0.7 0.7 copy-start.5
  0.7 0.7 %copy-start.6 = (s32[256]{0:T(256)S(1)}, s32[256]{0:T(256)}, u32[]{:S(2)}) copy-start(s32[256]{0:T(256)} %param.9) | copy-start | bytes 3076
  1.4 1.1 %copy-start = (bf16[512,768]{1,0:T(8,128)(2,1)S(1)}, bf16[512,768]{1,0:T(8,128)(2,1)}, u32[]{:S(2)}) copy-start(bf16[512,768]{1,0:T(8,128)(2,1)} %refs_5_.3) | copy-start | bytes 2359300
  2.6 1.0 %copy-start.2 = (bf16[256,768]{1,0:T(8,128)(2,1)S(1)}, bf16[256,768]{1,0:T(8,128)(2,1)}, u32[]{:S(2)}) copy-start(bf16[256,768]{1,0:T(8,128)(2,1)} %refs_6_.7) | copy-start | bytes 1179652
  3.5 3.9 %copy-start.4 = (bf16[256,768]{1,0:T(8,128)(2,1)S(1)}, bf16[256,768]{1,0:T(8,128)(2,1)}, u32[]{:S(2)}) copy-start(bf16[256,768]{1,0:T(8,128)(2,1)} %refs_0_.3) | copy-start | bytes 1179652
  3.6 15.0 %copy-start.8 = (s32[256]{0:T(256)S(1)}, s32[256]{0:T(256)}, u32[]{:S(2)}) copy-start(s32[256]{0:T(256)} %param.13) | copy-start | bytes 3076
  3.6 37.4 %copy-start.1 = (bf16[512,768]{1,0:T(8,128)(2,1)S(1)}, bf16[512,768]{1,0:T(8,128)(2,1)}, u32[]{:S(2)}) copy-start(bf16[512,768]{1,0:T(8,128)(2,1)} %refs_5_.3) | copy-start | bytes 2359300
  4.4 36.5 %copy-start.3 = (bf16[256,768]{1,0:T(8,128)(2,1)S(1)}, bf16[256,768]{1,0:T(8,128)(2,1)}, u32[]{:S(2)}) copy-start(bf16[256,768]{1,0:T(8,128)(2,1)} %refs_6_.7) | copy-start | bytes 1179652
  4.4 14.7 %collective-permute-start.8 = (bf16[384,768]{1,0:T(8,128)(2,1)S(1)}, bf16[384,768]{1,0:T(8,128)(2,1)S(1)}, u32[]{:S(2)}, u32[]{:S(2)}) collective-permute-start(bf16[384,768]{1,0:T(8,128)(2,1)S(1)} %get-tuple-element.17), channel_id=1, source_target_pairs={{0,2},{1,5},{2,0},{3,7},{4,6},{5,1},{6,4},{7,3},{8,10},{9,13},{10,... | collective-permute-start | bytes 1769480 | tf_op jit(solution)/shard_map/ppermute | solution.py:317
  7.4 13.3 %collective-permute-start = (bf16[256,768]{1,0:T(8,128)(2,1)S(1)}, bf16[256,768]{1,0:T(8,128)(2,1)S(1)}, u32[]{:S(2)}, u32[]{:S(2)}) collective-permute-start(bf16[256,768]{1,0:T(8,128)(2,1)S(1)} %copy-done.4), channel_id=1, source_target_pairs={{0,8},{8,0},{16,24},{24,16},{1,9},{9,1},{17,25},{25,17},{2,10},{10... | collective-permute-start | bytes 1179656 | tf_op jit(solution)/shard_map/ppermute | solution.py:228
  9.0 11.7 %collective-permute-start.1 = (bf16[256,768]{1,0:T(8,128)(2,1)S(1)}, bf16[256,768]{1,0:T(8,128)(2,1)S(1)}, u32[]{:S(2)}, u32[]{:S(2)}) collective-permute-start(bf16[256,768]{1,0:T(8,128)(2,1)S(1)} %copy-done.4), channel_id=1, source_target_pairs={{8,16},{16,8},{9,17},{17,9},{10,18},{18,10},{11,19},{19,11},{12,20... | collective-permute-start | bytes 1179656 | tf_op jit(solution)/shard_map/ppermute | solution.py:237
  9.7 5.9 %collective-permute-start.2 = (f32[12,128]{1,0:T(8,128)S(1)}, f32[12,128]{1,0:T(8,128)S(1)}, u32[]{:S(2)}, u32[]{:S(2)}) collective-permute-start(f32[12,128]{1,0:T(8,128)S(1)} %get-tuple-element.13), channel_id=1, source_target_pairs={{0,2},{2,0},{4,6},{6,4},{1,3},{3,1},{5,7},{7,5},{8,10},{10,8},{12,... | collective-permute-start | bytes 18440 | tf_op jit(solution)/shard_map/ppermute | solution.py:228
  10.3 8.3 %collective-permute-start.3 = (f32[12,128]{1,0:T(8,128)S(1)}, f32[12,128]{1,0:T(8,128)S(1)}, u32[]{:S(2)}, u32[]{:S(2)}) collective-permute-start(f32[12,128]{1,0:T(8,128)S(1)} %get-tuple-element.13), channel_id=1, source_target_pairs={{0,4},{2,6},{4,0},{6,2},{1,5},{3,7},{5,1},{7,3},{8,12},{10,14},{12... | collective-permute-start | bytes 18440 | tf_op jit(solution)/shard_map/ppermute | solution.py:228
  15.5 5.1 %collective-permute-start.4 = (f32[12,128]{1,0:T(8,128)S(1)}, f32[12,128]{1,0:T(8,128)S(1)}, u32[]{:S(2)}, u32[]{:S(2)}) collective-permute-start(f32[12,128]{1,0:T(8,128)S(1)} %get-tuple-element.13), channel_id=1, source_target_pairs={{0,6},{2,4},{4,2},{6,0},{1,7},{3,5},{5,3},{7,1},{8,14},{10,12},{12... | collective-permute-start | bytes 18440 | tf_op jit(solution)/shard_map/ppermute | solution.py:228
  18.6 18.7 %collective-permute-start.10 = (bf16[384,768]{1,0:T(8,128)(2,1)S(1)}, bf16[384,768]{1,0:T(8,128)(2,1)S(1)}, u32[]{:S(2)}, u32[]{:S(2)}) collective-permute-start(bf16[384,768]{1,0:T(8,128)(2,1)S(1)} %get-tuple-element.17), channel_id=1, source_target_pairs={{0,4},{1,3},{2,6},{3,1},{4,0},{5,7},{6,2},{7,5},{8,12},{9,11},{10,... | collective-permute-start | bytes 1769480 | tf_op jit(solution)/shard_map/ppermute | solution.py:318
  19.1 18.6 %collective-permute-start.12 = (bf16[384,768]{1,0:T(8,128)(2,1)S(1)}, bf16[384,768]{1,0:T(8,128)(2,1)S(1)}, u32[]{:S(2)}, u32[]{:S(2)}) collective-permute-start(bf16[384,768]{1,0:T(8,128)(2,1)S(1)} %collective-permute-done.8.refs_2_.refs_7_.refs_8_), channel_id=1, source_target_pairs={{0,4},{1,3},{2,6},{3,1},{4,0},{5,7},{6,2},{7,5},{8,12},{9,11},{10,... | collective-permute-start | bytes 1769480 | tf_op jit(solution)/shard_map/ppermute | solution.py:319
  20.7 4.6 %collective-permute-start.5 = (f32[3328]{0:T(1024)S(1)}, f32[3328]{0:T(1024)S(1)}, u32[]{:S(2)}, u32[]{:S(2)}) collective-permute-start(f32[3328]{0:T(1024)S(1)} %pad_maximum_fusion.3), channel_id=1, source_target_pairs={{0,8},{8,0},{16,24},{24,16},{1,9},{9,1},{17,25},{25,17},{2,10},{10... | collective-permute-start | bytes 39944 | tf_op jit(solution)/shard_map/ppermute | solution.py:228
  22.6 4.7 %collective-permute-start.6 = (f32[3328]{0:T(1024)S(1)}, f32[3328]{0:T(1024)S(1)}, u32[]{:S(2)}, u32[]{:S(2)}) collective-permute-start(f32[3328]{0:T(1024)S(1)} %pad_maximum_fusion.3), channel_id=1, source_target_pairs={{0,16},{8,24},{16,0},{24,8},{1,17},{9,25},{17,1},{25,9},{2,18},{10... | collective-permute-start | bytes 39944 | tf_op jit(solution)/shard_map/ppermute | solution.py:228
  25.0 5.7 %collective-permute-start.7 = (f32[3328]{0:T(1024)S(1)}, f32[3328]{0:T(1024)S(1)}, u32[]{:S(2)}, u32[]{:S(2)}) collective-permute-start(f32[3328]{0:T(1024)S(1)} %pad_maximum_fusion.3), channel_id=1, source_target_pairs={{0,24},{8,16},{16,8},{24,0},{1,25},{9,17},{17,9},{25,1},{2,26},{10... | collective-permute-start | bytes 39944 | tf_op jit(solution)/shard_map/ppermute | solution.py:228
  25.3 12.6 %collective-permute-start.20 = (bf16[256,768]{1,0:T(8,128)(2,1)S(1)}, bf16[256,768]{1,0:T(8,128)(2,1)S(1)}, u32[]{:S(2)}, u32[]{:S(2)}) collective-permute-start(bf16[256,768]{1,0:T(8,128)(2,1)S(1)} %collective-permute-done.refs_0_), channel_id=1, source_target_pairs={{8,16},{16,8},{9,17},{17,9},{10,18},{18,10},{11,19},{19,11},{12,20... | collective-permute-start | bytes 1179656 | tf_op jit(solution)/shard_map/ppermute | solution.py:239
  27.3 17.1 %collective-permute-start.19 = (bf16[256,768]{1,0:T(8,128)(2,1)S(1)}, bf16[256,768]{1,0:T(8,128)(2,1)S(1)}, u32[]{:S(2)}, u32[]{:S(2)}) collective-permute-start(bf16[256,768]{1,0:T(8,128)(2,1)S(1)} %collective-permute-done.1.refs_1_), channel_id=1, source_target_pairs={{8,0},{16,24},{9,1},{17,25},{10,2},{18,26},{11,3},{19,27},{12,4},{... | collective-permute-start | bytes 1179656 | tf_op jit(solution)/shard_map/ppermute | solution.py:240
  37.1 2.2 %collective-permute-start.9 = (bf16[384,768]{1,0:T(8,128)(2,1)S(1)}, bf16[384,768]{1,0:T(8,128)(2,1)S(1)}, u32[]{:S(2)}, u32[]{:S(2)}) collective-permute-start(bf16[384,768]{1,0:T(8,128)(2,1)S(1)} %collective-permute-done.8.refs_2_.refs_7_.refs_8_), channel_id=1, source_target_pairs={{0,1},{1,0},{2,3},{3,2},{4,5},{5,4},{6,7},{7,6},{8,9},{9,8},{10,11... | collective-permute-start | bytes 1769480 | tf_op jit(solution)/shard_map/ppermute | solution.py:228
  37.2 2.8 %collective-permute-start.11 = (bf16[384,768]{1,0:T(8,128)(2,1)S(1)}, bf16[384,768]{1,0:T(8,128)(2,1)S(1)}, u32[]{:S(2)}, u32[]{:S(2)}) collective-permute-start(bf16[384,768]{1,0:T(8,128)(2,1)S(1)} %collective-permute-done.10.refs_4_.refs_9_.refs_10_), channel_id=1, source_target_pairs={{0,1},{1,0},{2,3},{3,2},{4,5},{5,4},{6,7},{7,6},{8,9},{9,8},{10,11... | collective-permute-start | bytes 1769480 | tf_op jit(solution)/shard_map/ppermute | solution.py:228
  37.7 3.2 %collective-permute-start.13 = (bf16[384,768]{1,0:T(8,128)(2,1)S(1)}, bf16[384,768]{1,0:T(8,128)(2,1)S(1)}, u32[]{:S(2)}, u32[]{:S(2)}) collective-permute-start(bf16[384,768]{1,0:T(8,128)(2,1)S(1)} %collective-permute-done.12.refs_6_.refs_11_.refs_12_), channel_id=1, source_target_pairs={{0,1},{1,0},{2,3},{3,2},{4,5},{5,4},{6,7},{7,6},{8,9},{9,8},{10,11... | collective-permute-start | bytes 1769480 | tf_op jit(solution)/shard_map/ppermute | solution.py:228
  37.9 14.3 %collective-permute-start.22 = (bf16[256,768]{1,0:T(8,128)(2,1)S(1)}, bf16[256,768]{1,0:T(8,128)(2,1)S(1)}, u32[]{:S(2)}, u32[]{:S(2)}) collective-permute-start(bf16[256,768]{1,0:T(8,128)(2,1)S(1)} %collective-permute-done.20.refs_1_), channel_id=1, source_target_pairs={{8,0},{16,24},{9,1},{17,25},{10,2},{18,26},{11,3},{19,27},{12,4},{... | collective-permute-start | bytes 1179656 | tf_op jit(solution)/shard_map/ppermute | solution.py:241
  42.5 16.6 %collective-permute-start.14 = (bf16[64,768]{1,0:T(8,128)(2,1)S(1)}, bf16[64,768]{1,0:T(8,128)(2,1)S(1)}, u32[]{:S(2)}, u32[]{:S(2)}) collective-permute-start(bf16[64,768]{1,0:T(8,128)(2,1)S(1)} %get-tuple-element.25), channel_id=1, source_target_pairs={{0,8},{8,0},{16,24},{24,16},{1,9},{9,1},{17,25},{25,17},{2,10},{10... | collective-permute-start | bytes 294920 | tf_op jit(solution)/shard_map/ppermute | solution.py:228
  46.9 18.9 %collective-permute-start.21 = (f32[2,2,128]{2,1,0:T(2,128)S(1)}, f32[2,2,128]{2,1,0:T(2,128)S(1)}, u32[]{:S(2)}, u32[]{:S(2)}) collective-permute-start(f32[2,2,128]{2,1,0:T(2,128)S(1)} %score.5), channel_id=1, source_target_pairs={{0,16},{8,24},{16,0},{24,8},{1,17},{9,25},{17,1},{25,9},{2,18},{10... | collective-permute-start | bytes 6152 | tf_op jit(solution)/shard_map/ppermute | solution.py:228
  50.1 15.8 %collective-permute-start.18 = (f32[2,2,128]{2,1,0:T(2,128)S(1)}, f32[2,2,128]{2,1,0:T(2,128)S(1)}, u32[]{:S(2)}, u32[]{:S(2)}) collective-permute-start(f32[2,2,128]{2,1,0:T(2,128)S(1)} %score.4), channel_id=1, source_target_pairs={{0,8},{8,0},{16,24},{24,16},{1,9},{9,1},{17,25},{25,17},{2,10},{10... | collective-permute-start | bytes 6152 | tf_op jit(solution)/shard_map/ppermute | solution.py:228
  54.7 11.2 %collective-permute-start.23 = (f32[2,2,128]{2,1,0:T(2,128)S(1)}, f32[2,2,128]{2,1,0:T(2,128)S(1)}, u32[]{:S(2)}, u32[]{:S(2)}) collective-permute-start(f32[2,2,128]{2,1,0:T(2,128)S(1)} %score.6), channel_id=1, source_target_pairs={{0,24},{8,16},{16,8},{24,0},{1,25},{9,17},{17,9},{25,1},{2,26},{10... | collective-permute-start | bytes 6152 | tf_op jit(solution)/shard_map/ppermute | solution.py:228
  56.6 7.3 %collective-permute-start.15 = (bf16[64,768]{1,0:T(8,128)(2,1)S(1)}, bf16[64,768]{1,0:T(8,128)(2,1)S(1)}, u32[]{:S(2)}, u32[]{:S(2)}) collective-permute-start(bf16[64,768]{1,0:T(8,128)(2,1)S(1)} %get-tuple-element.24), channel_id=1, source_target_pairs={{0,16},{8,24},{16,0},{24,8},{1,17},{9,25},{17,1},{25,9},{2,18},{10... | collective-permute-start | bytes 294920 | tf_op jit(solution)/shard_map/ppermute | solution.py:228
  59.2 6.6 %collective-permute-start.16 = (bf16[64,768]{1,0:T(8,128)(2,1)S(1)}, bf16[64,768]{1,0:T(8,128)(2,1)S(1)}, u32[]{:S(2)}, u32[]{:S(2)}) collective-permute-start(bf16[64,768]{1,0:T(8,128)(2,1)S(1)} %get-tuple-element.23), channel_id=1, source_target_pairs={{0,24},{8,16},{16,8},{24,0},{1,25},{9,17},{17,9},{25,1},{2,26},{10... | collective-permute-start | bytes 294920 | tf_op jit(solution)/shard_map/ppermute | solution.py:228
  65.8 1.6 %collective-permute-start.17 = (bf16[192,768]{1,0:T(8,128)(2,1)S(1)}, bf16[192,768]{1,0:T(8,128)(2,1)S(1)}, u32[]{:S(2)}, u32[]{:S(2)}) collective-permute-start(bf16[192,768]{1,0:T(8,128)(2,1)S(1)} %constant_dynamic-update-slice_fusion.refs_1_), channel_id=1, source_target_pairs={{0,1},{1,0},{2,3},{3,2},{4,5},{5,4},{6,7},{7,6},{8,9},{9,8},{10,11... | collective-permute-start | bytes 884744 | tf_op jit(solution)/shard_map/ppermute | solution.py:228

commit v4 on v3

v4 whole, which is shorter than its diff:
```python
import functools
import math

import jax
import jax.numpy as jnp
from jax import lax
from jax.experimental import pallas as pl
from jax.experimental.pallas import tpu as pltpu
from jax.sharding import Mesh, PartitionSpec as P

score_scale = 20.0
age_scale = 16.0
epsilon = 1e-06
LOG2E = math.log2(math.e)
MASKED = -1e30
LANES = 128
VMEM_LIMIT = 48 * 1024 * 1024

NT = (((1,), (1,)), ((), ()))
NN = (((1,), (0,)), ((), ()))


def one_hot(ids, count):
    rows = lax.broadcasted_iota(jnp.int32, (count, ids.shape[1]), 0)
    return jnp.where(rows == ids, 1.0, 0.0).astype(jnp.bfloat16)


def split_one_hot(ids, high_count):
    return one_hot(ids >> 7, high_count), one_hot(ids & 127, LANES)


def bitmap(ids, high_count):
    high, low = split_one_hot(ids, high_count)
    return lax.dot_general(low, high, NT, preferred_element_type=jnp.float32)


def as_row(lines):
    return jnp.concatenate([lines[i : i + 1, :] for i in range(lines.shape[0])], axis=1)


def split_terms(values):
    terms = []
    for _ in range(3):
        terms.append(values.astype(jnp.bfloat16))
        values = values - terms[-1].astype(jnp.float32)
    return terms


def prep_kernel(place, table, fresh, rows_out, scale_out, table_in, fresh_in, arrived, *, replicas, encode):
    core = place[2]
    copies = [
        pltpu.make_async_copy(table, table_in, arrived.at[0]),
        pltpu.make_async_copy(fresh, fresh_in, arrived.at[1]),
    ]
    for copy in copies:
        copy.start()
    line, row = 0, 0
    halves = []
    for copy, source in zip(copies, (table_in, fresh_in)):
        copy.wait()
        rows, width = source.shape
        half = rows // replicas
        rows_out[row : row + half, :] = source[pl.ds(pl.multiple_of(core * half, half), half), :]
        row += half
        for block in range(rows // LANES):
            squares = jnp.zeros((LANES, LANES), jnp.float32)
            for chunk in range(width // LANES):
                values = source[block * LANES : (block + 1) * LANES, chunk * LANES : (chunk + 1) * LANES]
                values = values.astype(jnp.float32)
                squares += values * values
            mean = jnp.sum(squares.T, axis=0, keepdims=True) / width
            scale_out[line + block : line + block + 1, :] = lax.rsqrt(mean + epsilon) * (score_scale / width * LOG2E)
        if encode:
            lines = half // LANES
            halves += [(line, i, lines) for i in range(lines)]
        line += rows // LANES
    if encode:
        rows_out[row:, :] = jnp.zeros((16, width), jnp.bfloat16)
        terms = []
        for first, i, lines in halves:
            terms += split_terms(scale_out[pl.ds(first + core * lines + i, 1), :])
        for i, term in enumerate(terms):
            rows_out[row + i : row + i + 1, :LANES] = term


def meta_kernel(place, meta, lw_out, row_out, pack_out, apply_out, own_out, *, planes, cuts, cap, replicas):
    outer, inner, core = place[0], place[1], place[2]
    owners_plane = meta.shape[0] // planes
    refresh_lines, age_lines, neg_lines = (cut // LANES for cut in cuts[:3])
    refresh_dev, rows_dev = cuts[:2]
    plane_rows = owners_plane * rows_dev
    plane_refresh = owners_plane * refresh_dev
    high_count = planes * plane_rows // LANES
    own_owner = outer * owners_plane + inner
    column = lax.broadcasted_iota(jnp.int32, (1, plane_rows), 1)
    table_ids = (outer * owners_plane + (inner ^ (column // rows_dev))) * rows_dev + column % rows_dev

    ref_planes = []
    for plane in range(planes):
        owners = range(plane * owners_plane, (plane + 1) * owners_plane)
        ref_planes.append(jnp.concatenate([as_row(meta[owner, :refresh_lines, :]) for owner in owners], axis=1))
    beside = [outer * owners_plane + (inner ^ s) for s in range(owners_plane)]
    plane_ids = jnp.concatenate([as_row(meta[owner, :refresh_lines, :]) for owner in beside], axis=1)
    first, last = refresh_lines, refresh_lines + age_lines
    plane_ages = jnp.concatenate([as_row(meta[owner, first:last, :]) for owner in beside], axis=1)
    weight = jnp.exp(-plane_ages.astype(jnp.float32) / age_scale).astype(jnp.bfloat16).astype(jnp.float32)
    log_weight = jnp.log2(weight)

    refreshed_map = jnp.zeros((LANES, high_count), jnp.float32)
    for ids in ref_planes:
        refreshed_map += bitmap(ids, high_count)
    refreshed_map = refreshed_map.astype(jnp.bfloat16)

    table_high, table_low = split_one_hot(table_ids, high_count)
    fresh_high, fresh_low = split_one_hot(plane_ids, high_count)

    def lookup(one_map, high, low):
        hit = lax.dot_general(one_map, high, NN, preferred_element_type=jnp.float32)
        return jnp.sum(hit * low.astype(jnp.float32), axis=0, keepdims=True)

    refreshed = lookup(refreshed_map, table_high, table_low) > 0.5
    row_out[:, :plane_rows] = jnp.where(refreshed, -1, table_ids)
    row_out[:, plane_rows:] = plane_ids
    own_out[...] = refreshed[:, :rows_dev].astype(jnp.int32)

    first, last = last, last + neg_lines
    for group in range(planes):
        neg = as_row(meta[(outer ^ group) * owners_plane + inner, first:last, :])
        one_map = bitmap(neg, high_count).astype(jnp.bfloat16)
        in_list = lookup(one_map, table_high, table_low) > 0.5
        lw_out[group : group + 1, :plane_rows] = jnp.where(in_list & ~refreshed, log_weight, MASKED)
        in_list = lookup(one_map, fresh_high, fresh_low) > 0.5
        lw_out[group : group + 1, plane_rows:] = jnp.where(in_list, 0.0, MASKED)

    share = cap // replicas
    before = lax.broadcasted_iota(jnp.int32, (plane_refresh, plane_refresh), 0)
    after = lax.broadcasted_iota(jnp.int32, (plane_refresh, plane_refresh), 1)
    earlier = jnp.where(before < after, 1.0, 0.0).astype(jnp.bfloat16)
    block = refresh_dev
    before_own = (inner ^ (before // block)) * block + before % block
    after_own = (inner ^ (after // block)) * block + after % block
    earlier_own = jnp.where(before_own < after_own, 1.0, 0.0).astype(jnp.bfloat16)
    target_plane = lax.broadcasted_iota(jnp.int32, (planes, plane_refresh), 0)
    send_match = plane_ids // rows_dev == target_plane * owners_plane + inner
    ref_all = jnp.concatenate(ref_planes, axis=0)
    take_match = ref_all // rows_dev == own_owner

    def ranked(match, order):
        ones = jnp.where(match, 1.0, 0.0)
        rank = lax.dot_general(ones.astype(jnp.bfloat16), order, NN, preferred_element_type=jnp.float32)
        return jnp.where(match, rank.astype(jnp.int32), -cap)

    send_rank, take_rank = ranked(send_match, earlier_own), ranked(take_match, earlier)
    take_row = ref_all - own_owner * rows_dev
    for plane in range(planes):
        pack_out[plane * share : (plane + 1) * share, :] = one_hot(send_rank[plane : plane + 1, :] - core * share, share)
        row = one_hot(take_row[plane : plane + 1, :], rows_dev)
        for part in range(replicas):
            slot = one_hot(take_rank[plane : plane + 1, :] - (core ^ part) * share, share)
            first = (part * planes + plane) * share
            apply_out[:, first : first + share] = lax.dot_general(row, slot, NT, preferred_element_type=jnp.float32)


def piece_offset(place, piece):
    column, size, flip, by_core = piece
    if flip is None:
        return column
    column += (place[2] ^ flip) * size
    if by_core is not None:
        column += (place[2] ^ by_core) * size * 2
    return pl.multiple_of(column, size)


def pack_kernel(place, select, *refs, pieces):
    out = refs[-1]
    total = jnp.zeros(out.shape, jnp.float32)
    for source, start, size, column, _ in pieces:
        columns = pl.ds(piece_offset(place, column), size)
        total += lax.dot_general(
            select[:, columns], refs[source][start : start + size, :], NN, preferred_element_type=jnp.float32
        )
    out[...] = total.astype(jnp.bfloat16)


def apply_kernel(select, table, *refs):
    out = refs[-1]
    fresh = jnp.zeros(out.shape, jnp.float32)
    first = 0
    for arrived in refs[:-1]:
        part = select[:, first : first + arrived.shape[0]].astype(jnp.bfloat16)
        fresh += lax.dot_general(part, arrived[...], NN, preferred_element_type=jnp.float32)
        first += arrived.shape[0]
    hit = jnp.sum(select[...], axis=1, keepdims=True) > 0.5
    out[...] = jnp.where(hit, fresh, table[...].astype(jnp.float32)).astype(jnp.bfloat16)


def to_lanes(row):
    return jnp.broadcast_to(row, (LANES, LANES)).T


def score_kernel(place, meta, *refs, pieces, flip, slot, owners_plane, given):
    out, total, pos_total, q_scale, pos_b, chosen = refs[-6:]
    queries = refs[0]
    if given == 2:
        at_end = (place[0] == 0) | (place[0] == 3)
        chosen[...] = jnp.where(at_end, refs[0][...], refs[1][...])
        queries = chosen
    log_weight, row_ids, scale, *refs = refs[given:-6]
    count, width = queries.shape
    owner = (place[0] ^ flip) * owners_plane + place[1]
    for block in range(count // LANES):
        part = slice(block * LANES, (block + 1) * LANES)
        values = queries[part, :].astype(jnp.float32)
        squares = jnp.sum(values * values, axis=1, keepdims=True)
        q_scale[part, :] = jnp.broadcast_to(lax.rsqrt(squares / width + epsilon), (LANES, LANES))
        pos_b[part, :] = to_lanes(meta[owner, slot + block : slot + block + 1, :].astype(jnp.float32))
    total[...] = jnp.zeros_like(total)
    pos_total[...] = jnp.zeros_like(pos_total)
    for source, start, size, column, scale_at in pieces:
        first = piece_offset(place, column)
        raw = lax.dot_general(
            queries[...], refs[source][start : start + size, :], NT, preferred_element_type=jnp.float32
        )
        sums = total[...]
        positives = pos_total[...]
        for chunk in range(size // LANES):
            cols = pl.ds(first + chunk * LANES, LANES)
            part = raw[:, chunk * LANES : (chunk + 1) * LANES]
            if scale_at < 0:
                line = -1 - scale_at + chunk
                row_scale = scale[line : line + 1, :]
            else:
                line = scale_at + 3 * chunk
                row_scale = jnp.sum(refs[source][line : line + 3, :LANES].astype(jnp.float32), axis=0, keepdims=True)
            powers = part * q_scale[...] * row_scale + log_weight[flip : flip + 1, cols]
            sums = sums + jnp.exp2(powers)
            positives = positives + jnp.where(pos_b[...] == row_ids[:, cols].astype(jnp.float32), powers, 0.0)
        total[...] = sums
        pos_total[...] = positives
    for block in range(count // LANES):
        part = slice(block * LANES, (block + 1) * LANES)
        out[0, block : block + 1, :] = jnp.sum(total[part, :].T, axis=0, keepdims=True)
        out[1, block : block + 1, :] = jnp.sum(pos_total[part, :].T, axis=0, keepdims=True)


def whole(memory=pltpu.VMEM):
    return pl.BlockSpec(memory_space=memory)


def call(kernel, name, outs, place, *operands, scratch=(), in_place=False, **options):
    specs = [whole(pl.ANY if in_place else pltpu.VMEM)] * len(operands)
    if place is not None:
        specs = [whole(pltpu.SMEM)] + specs
        operands = (place, *operands)
    return pl.pallas_call(
        functools.partial(kernel, **options),
        out_shape=tuple(outs),
        in_specs=specs,
        out_specs=tuple(whole() for _ in outs),
        scratch_shapes=list(scratch),
        compiler_params=pltpu.CompilerParams(vmem_limit_bytes=VMEM_LIMIT),
        cost_estimate=pl.CostEstimate(flops=1, bytes_accessed=1, transcendentals=0),
        name=name,
    )(*operands)


def swap(values, axis, flip):
    return lax.ppermute(values, axis, [(i, i ^ flip) for i in range(lax.axis_size(axis))])


def on_device(table, ages, refresh_ids, fresh_rows, neg_ids, queries, pos_ids):
    rows_dev, width = table.shape
    refresh_dev = refresh_ids.shape[0]
    planes = lax.axis_size("outer")
    owners_plane = lax.axis_size("inner")
    replicas = lax.axis_size("query")
    owners = planes * owners_plane
    query_count = queries.shape[0]
    list_size = neg_ids.shape[1]
    place = jnp.stack([lax.axis_index(name) for name in ("outer", "inner", "query")]).astype(jnp.int32)
    plane_rows = owners_plane * rows_dev
    plane_refresh = owners_plane * refresh_dev
    all_rows = plane_rows + plane_refresh
    cap = owners_plane * max(2, (2 * refresh_dev + owners - 1) // owners)
    share = cap // replicas
    table_half, fresh_half = rows_dev // replicas, refresh_dev // replicas
    bf16, f32 = jnp.bfloat16, jnp.float32

    meta = jnp.concatenate([refresh_ids, ages, neg_ids[0], pos_ids]).reshape(-1, LANES)
    meta_all = lax.all_to_all(
        jnp.broadcast_to(meta, (owners, *meta.shape)), ("outer", "inner"), split_axis=0, concat_axis=0, tiled=True
    )
    fast = replicas == 2 and owners_plane == 4 and planes == 4
    extra = 16 if fast else 0
    rows_half, scales = call(
        prep_kernel,
        "prep",
        [
            jax.ShapeDtypeStruct((table_half + fresh_half + extra, width), bf16),
            jax.ShapeDtypeStruct(((rows_dev + refresh_dev) // LANES, LANES), f32),
        ],
        place,
        table,
        fresh_rows,
        scratch=[
            pltpu.VMEM(table.shape, bf16),
            pltpu.VMEM(fresh_rows.shape, bf16),
            pltpu.SemaphoreType.DMA((2,)),
        ],
        in_place=True,
        replicas=replicas,
        encode=fast,
    )
    cuts = (refresh_dev, rows_dev, list_size, query_count)
    if fast:
        axes = ("inner", "query")
        first = [(2 * i + c, 2 * (i ^ (1 + c)) + c) for i in range(4) for c in range(2)]
        second = [(2 * i + c, 2 * (i ^ (2 - c)) + c) for i in range(4) for c in range(2)]
        near = lax.ppermute(rows_half, axes, first)
        side = lax.ppermute(rows_half, axes, second)
        middle, outward = [(1, 2), (2, 1)], [(1, 0), (2, 3)]
        beside = swap(queries, "outer", 1)
        across = lax.ppermute(queries, "outer", middle)
        near, meta_all, beside, across = lax.optimization_barrier((near, meta_all, beside, across))
        from_end = lax.ppermute(beside, "outer", middle)
        to_end = lax.ppermute(across, "outer", outward)
        far = lax.ppermute(near, axes, second)
        far, from_end, to_end = lax.optimization_barrier((far, from_end, to_end))
        last = lax.ppermute(from_end, "outer", outward)
        got_queries = [(queries,), (beside,), (to_end, from_end), (last, across)]
        buffers = [table, fresh_rows]
        table_pieces = [(0, 0, rows_dev, (0, rows_dev, None, None), -1)]
        fresh_pieces = [(1, 0, refresh_dev, (0, refresh_dev, None, None), -1 - rows_dev // LANES)]
        for slot, by_core, mine in ((1, 0, near), (1, 1, side), (3, None, far)):
            for flip, rows in enumerate((mine, swap(mine, "query", 1))):
                by = None if by_core is None else by_core ^ flip
                data = table_half + fresh_half
                fresh_at = data + 3 * (table_half // LANES)
                table_pieces.append((len(buffers), 0, table_half, (slot * rows_dev, table_half, flip, by), data))
                fresh_pieces.append(
                    (len(buffers), table_half, fresh_half, (slot * refresh_dev, fresh_half, flip, by), fresh_at)
                )
                buffers.append(rows)
    else:
        got_queries = [(queries,)] + [(swap(queries, "outer", s),) for s in range(1, planes)]
        got_rows = [rows_half] + [swap(rows_half, "inner", s) for s in range(1, owners_plane)]
        gathered = lax.all_gather(jnp.stack(got_rows), "query", axis=0)
        gathered = jnp.swapaxes(gathered, 0, 1)
        buffers = [
            gathered[:, :, :table_half].reshape(plane_rows, width),
            gathered[:, :, table_half:].reshape(plane_refresh, width),
        ]
        scales = []
        for rows in buffers:
            values = rows.astype(f32)
            mean = jnp.sum(values * values, axis=1) / width
            scales.append((lax.rsqrt(mean + epsilon) * (score_scale / width * LOG2E)).reshape(-1, LANES))
        scales = jnp.concatenate(scales)

        def blocks(buffer, count, line):
            starts = range(0, count, 512)
            return [(buffer, i, 512, (i, 512, None, None), -1 - line - i // LANES) for i in starts]

        table_pieces = blocks(0, plane_rows, 0)
        fresh_pieces = blocks(1, plane_refresh, plane_rows // LANES)

    lw, row_ids, pack, apply_to, own = call(
        meta_kernel,
        "meta",
        [
            jax.ShapeDtypeStruct((planes, all_rows), f32),
            jax.ShapeDtypeStruct((1, all_rows), jnp.int32),
            jax.ShapeDtypeStruct((planes * share, plane_refresh), bf16),
            jax.ShapeDtypeStruct((rows_dev, planes * cap), f32),
            jax.ShapeDtypeStruct((1, rows_dev), jnp.int32),
        ],
        place,
        meta_all,
        planes=planes,
        cuts=cuts,
        cap=cap,
        replicas=replicas,
    )
    new_ages = jnp.where(own.reshape(rows_dev) > 0, 0, ages)

    def shift(pieces, columns):
        return [(a, b, c, (d[0] + columns, *d[1:]), e) for a, b, c, d, e in pieces]

    (packed,) = call(
        pack_kernel, "pack", [jax.ShapeDtypeStruct((pack.shape[0], width), bf16)], place, pack, *buffers, pieces=fresh_pieces
    )
    packed, lw = lax.optimization_barrier((packed, lw))
    came = lax.all_to_all(packed.reshape(planes, share, width), "outer", split_axis=0, concat_axis=0, tiled=True)
    came = came.reshape(planes * share, width)
    arrived = [came] + [swap(came, "query", flip) for flip in range(1, replicas)]

    pieces = table_pieces + shift(fresh_pieces, plane_rows)
    mine = None
    for s in [*range(1, planes), 0]:
        (partial,) = call(
            score_kernel,
            "score",
            [jax.ShapeDtypeStruct((2, query_count // LANES, LANES), f32)],
            place,
            meta_all,
            *got_queries[s],
            lw,
            row_ids,
            scales,
            *buffers,
            scratch=[pltpu.VMEM((query_count, LANES), f32)] * 4 + [pltpu.VMEM(queries.shape, bf16)],
            pieces=pieces,
            flip=s,
            slot=sum(cuts[:3]) // LANES,
            owners_plane=owners_plane,
            given=len(got_queries[s]),
        )
        if s:
            partial = swap(partial, "outer", s)
        mine = partial if mine is None else mine + partial
    (new_table,) = call(
        apply_kernel, "apply", [jax.ShapeDtypeStruct(table.shape, bf16)], None, apply_to, table, *arrived
    )
    loss = (jnp.log2(mine[0]) - mine[1]) * math.log(2.0)
    return new_table, new_ages, loss.reshape(query_count)


def solution(mesh):
    owners, replicas = mesh.shape["index"], mesh.shape["query"]
    inner = 1 << (int(math.log2(owners)) // 2)
    split = Mesh(mesh.devices.reshape(owners // inner, inner, replicas), ("outer", "inner", "query"))
    index = ("outer", "inner")
    placed = (
        P(index, None),
        P(index),
        P(index),
        P(index, None),
        P(index, None),
        P(("outer", "inner", "query"), None),
        P(("outer", "inner", "query")),
    )
    return jax.shard_map(
        on_device,
        mesh=split,
        in_specs=placed,
        out_specs=(P(index, None), P(index), P(("outer", "inner", "query"))),
        check_vma=False,
    )
```

time: 69.4 us -> 88.6 us (1.28)
  local copies, waits for them, and re-layouts: 2.95 us -> 12 us
  waiting for transfers between devices: 13.8 us -> 18.5 us
  Pallas kernels: 20.6 us -> 24.2 us
  starting transfers between devices: 29.3 us -> 31 us
    ppermute x17 -> x8, starting transfers between devices: 20.1 us -> 6.93 us  [swap(): lax.ppermute(values, axis, [(i, i ^ flip) for i in range(lax.axis_size(ax...]
    all_to_all x0 -> x2, starting transfers between devices: none -> 12.1 us  [the longest x1 6.07 us: on_device(): lax.all_to_all(packed.reshape(planes, share, width), 'outer', split_axis=...]
    ppermute x17 -> x8, waiting for transfers between devices: 13.8 us -> 2.07 us  [swap(): lax.ppermute(values, axis, [(i, i ^ flip) for i in range(lax.axis_size(ax...]
    ppermute x4, waiting for transfers between devices: 0.01 us -> 8.65 us  [the longest x1 8.64 us: on_device(): to_end = lax.ppermute(across, 'outer', outward)]
    unnamed x20 -> x40, local copies, waits for them, and re-layouts: 2.86 us -> 11.3 us
    all_to_all x0 -> x2, waiting for transfers between devices: none -> 7.79 us  [the longest x1 7.78 us: on_device(): lax.all_to_all(jnp.broadcast_to(meta, (owners, *meta.shape)), ('outer', '...]
    pallas_call x8, Pallas kernels: 20.6 us -> 24.2 us  [call(): pl.pallas_call(functools.partial(kernel, **options), out_shape=tuple(outs...]
    ppermute x1, starting transfers between devices: 0.57 us -> 1.93 us  [on_device(): side = lax.ppermute(rows_half, axes, second)]
  transfers between devices with their start and end apart: 24 -> 17, of which waited for: 8 -> 3; matrix products, arithmetic and copies ran while one was open for 2% -> 2% of each run, Pallas kernels for 26% -> 22%
where the time goes in v4:
time: 88.6 us; the launch traced here: 87.9 us
  starting transfers between devices  31 us (35%)
  Pallas kernels  24.2 us (27%)
  waiting for transfers between devices  18.5 us (21%)
  local copies, waits for them, and re-layouts  12 us (14%)
  other arithmetic  1.27 us (1%)
    pallas_call x8, Pallas kernels, call(): pl.pallas_call(functools.partial(kernel, **options), out_shape=tuple(outs...  24.2 us
    unnamed x40, local copies, waits for them, and re-layouts  11.3 us
    ppermute x1, waiting for transfers between devices, on_device(): to_end = lax.ppermute(across, 'outer', outward)  8.64 us
    all_to_all x1, waiting for transfers between devices, on_device(): lax.all_to_all(jnp.broadcast_to(meta, (owners, *meta.shape)), ('outer', '...  7.78 us
    ppermute x8, starting transfers between devices, swap(): lax.ppermute(values, axis, [(i, i ^ flip) for i in range(lax.axis_size(ax...  6.93 us
    all_to_all x1, starting transfers between devices, on_device(): lax.all_to_all(packed.reshape(planes, share, width), 'outer', split_axis=...  6.07 us
    all_to_all x1, starting transfers between devices, on_device(): lax.all_to_all(jnp.broadcast_to(meta, (owners, *meta.shape)), ('outer', '...  6 us
    ppermute x1, starting transfers between devices, on_device(): near = lax.ppermute(rows_half, axes, first)  3 us
  transfers between devices with their start and end apart: 17, of which 3 were waited for; matrix products, arithmetic and copies ran while one was open for 2% of the time, Pallas kernels for 22%

profile of v4, /device:TPU:0, one launch (start us, length us, event | category | flops | bytes accessed | tf_op | source)
XLA Modules:
  0.0 87.9 jit_solution(5147431198528437626)
XLA Ops:
  0.6 0.0 copy-start.16
  0.6 0.1 pad_add_fusion.place
  0.7 1.1 %copy-done = bf16[512,768]{1,0:T(8,128)(2,1)S(1)} copy-done((bf16[512,768]{1,0:T(8,128)(2,1)S(1)}, bf16[512,768]{1,0:T(8,128)(2,1)}, u32[]{:S(2)}) %copy-start) | copy-done | bytes 786456
  1.9 1.0 %copy-done.6 = bf16[256,768]{1,0:T(8,128)(2,1)S(1)} copy-done((bf16[256,768]{1,0:T(8,128)(2,1)S(1)}, bf16[256,768]{1,0:T(8,128)(2,1)}, u32[]{:S(2)}) %copy-start.6) | copy-done | bytes 393240
  2.9 2.1 %prep.1 = (bf16[400,768]{1,0:T(8,128)(2,1)}, f32[6,128]{1,0:T(8,128)S(1)}) custom-call(s32[3]{0:T(128)S(1)} %pad_add_fusion.place, bf16[512,768]{1,0:T(8,128)(2,1)S(1)} %copy-done, bf16[256,768]{1,0:T(8,128)(2,1)S(1)} %copy-done.6), custom_call_target="tpu_custom_call" | custom-call | flops 1 | bytes 1 | tf_op jit(solution)/shard_map/prep/pallas_call | solution.py:255
  4.9 0.0 copy-start.17
  4.9 0.0 copy-start.18
  5.0 3.0 %collective-permute-start = (bf16[400,768]{1,0:T(8,128)(2,1)}, bf16[400,768]{1,0:T(8,128)(2,1)S(1)}, u32[]{:S(2)}, u32[]{:S(2)}) collective-permute-start(bf16[400,768]{1,0:T(8,128)(2,1)} %get-tuple-element.19), channel_id=1, source_target_pairs={{0,2},{1,5},{2,0},{3,7},{4,6},{5,1},{6,4},{7,3},{8,10},{9,13},{10,... | collective-permute-start | bytes 1843208 | tf_op jit(solution)/shard_map/ppermute | solution.py:319
  8.0 0.0 copy-done.14
  8.0 1.6 %collective-permute-start.1 = (bf16[256,768]{1,0:T(8,128)(2,1)S(1)}, bf16[256,768]{1,0:T(8,128)(2,1)}, u32[]{:S(2)}, u32[]{:S(2)}) collective-permute-start(bf16[256,768]{1,0:T(8,128)(2,1)S(1)} %copy-done.14), channel_id=1, source_target_pairs={{0,8},{8,0},{16,24},{24,16},{1,9},{9,1},{17,25},{25,17},{2,10},{10... | collective-permute-start | bytes 1179656 | tf_op jit(solution)/shard_map/ppermute | solution.py:268
  9.5 1.4 %collective-permute-start.2 = (bf16[256,768]{1,0:T(8,128)(2,1)S(1)}, bf16[256,768]{1,0:T(8,128)(2,1)}, u32[]{:S(2)}, u32[]{:S(2)}) collective-permute-start(bf16[256,768]{1,0:T(8,128)(2,1)S(1)} %copy-done.14), channel_id=1, source_target_pairs={{8,16},{16,8},{9,17},{17,9},{10,18},{18,10},{11,19},{19,11},{12,20... | collective-permute-start | bytes 1179656 | tf_op jit(solution)/shard_map/ppermute | solution.py:323
  11.0 0.0 copy-done.17
  11.0 0.7 broadcast_in_dim.5
  11.7 6.0 %all-to-all-start = ((s32[16,24,128]{2,1,0:T(8,128)}), s32[16,24,128]{2,1,0:T(8,128)S(1)}, u32[]{:S(2)}, u32[]{:S(2)}) async-start(s32[16,24,128]{2,1,0:T(8,128)} %broadcast_in_dim.5), calls=%async_computation | async-start | bytes 393216 | tf_op jit(solution)/shard_map/all_to_all | solution.py:290
  17.7 1.9 %collective-permute-start.4 = (bf16[400,768]{1,0:T(8,128)(2,1)}, bf16[400,768]{1,0:T(8,128)(2,1)S(1)}, u32[]{:S(2)}, u32[]{:S(2)}) collective-permute-start(bf16[400,768]{1,0:T(8,128)(2,1)} %get-tuple-element.19), channel_id=1, source_target_pairs={{0,4},{1,3},{2,6},{3,1},{4,0},{5,7},{6,2},{7,5},{8,12},{9,11},{10,... | collective-permute-start | bytes 1843208 | tf_op jit(solution)/shard_map/ppermute | solution.py:320
  19.6 7.8 %all-to-all-done.meta = s32[16,24,128]{2,1,0:T(8,128)S(1)} async-done(((s32[16,24,128]{2,1,0:T(8,128)}), s32[16,24,128]{2,1,0:T(8,128)S(1)}, u32[]{:S(2)}, u32[]{:S(2)}) %all-to-all-start) | async-done | bytes 196640 | tf_op jit(solution)/shard_map/all_to_all | solution.py:290
  27.4 0.0 collective-permute-done.1.refs_0_
  27.4 0.0 collective-permute-done.2.refs_1_
  27.4 0.0 collective-permute-done.refs_2_.refs_6_.refs_7_
  27.4 1.7 %collective-permute-start.6 = (bf16[400,768]{1,0:T(8,128)(2,1)S(1)}, bf16[400,768]{1,0:T(8,128)(2,1)S(1)}, u32[]{:S(2)}, u32[]{:S(2)}) collective-permute-start(bf16[400,768]{1,0:T(8,128)(2,1)S(1)} %collective-permute-done.refs_2_.refs_6_.refs_7_), channel_id=1, source_target_pairs={{0,4},{1,3},{2,6},{3,1},{4,0},{5,7},{6,2},{7,5},{8,12},{9,11},{10,... | collective-permute-start | bytes 1843208 | tf_op jit(solution)/shard_map/ppermute | solution.py:327
  29.1 1.4 %collective-permute-start.7 = (bf16[256,768]{1,0:T(8,128)(2,1)}, bf16[256,768]{1,0:T(8,128)(2,1)}, u32[]{:S(2)}, u32[]{:S(2)}) collective-permute-start(bf16[256,768]{1,0:T(8,128)(2,1)} %collective-permute-done.1.refs_0_), channel_id=1, source_target_pairs={{8,16},{16,8},{9,17},{17,9},{10,18},{18,10},{11,19},{19,11},{12,20... | collective-permute-start | bytes 1179656 | tf_op jit(solution)/shard_map/ppermute | solution.py:325
  30.5 1.3 %collective-permute-start.8 = (bf16[256,768]{1,0:T(8,128)(2,1)}, bf16[256,768]{1,0:T(8,128)(2,1)S(1)}, u32[]{:S(2)}, u32[]{:S(2)}) collective-permute-start(bf16[256,768]{1,0:T(8,128)(2,1)} %collective-permute-done.2.refs_1_), channel_id=1, source_target_pairs={{8,0},{16,24},{9,1},{17,25},{10,2},{18,26},{11,3},{19,27},{12,4},{... | collective-permute-start | bytes 1179656 | tf_op jit(solution)/shard_map/ppermute | solution.py:326
  31.8 0.1 collective-permute-start.3
  31.9 0.0 collective-permute-done.4.refs_4_.refs_8_.refs_9_
  31.9 0.5 collective-permute-start.5
  32.4 0.0 collective-permute-done.7.refs_1_
  32.4 8.6 %collective-permute-done.8.refs_0_ = bf16[256,768]{1,0:T(8,128)(2,1)S(1)} collective-permute-done((bf16[256,768]{1,0:T(8,128)(2,1)}, bf16[256,768]{1,0:T(8,128)(2,1)S(1)}, u32[]{:S(2)}, u32[]{:S(2)}) %collective-permute-start.8) | collective-permute-done | bytes 393248 | tf_op jit(solution)/shard_map/ppermute | solution.py:326
  41.0 0.7 copy-done.12
  41.8 0.0 collective-permute-done.6.refs_6_.refs_10_.refs_11_
  41.8 0.0 collective-permute-start.9
  41.8 1.3 %collective-permute-start.13 = (bf16[256,768]{1,0:T(8,128)(2,1)}, bf16[256,768]{1,0:T(8,128)(2,1)}, u32[]{:S(2)}, u32[]{:S(2)}) collective-permute-start(bf16[256,768]{1,0:T(8,128)(2,1)} %collective-permute-done.7.refs_1_), channel_id=1, source_target_pairs={{8,0},{16,24},{9,1},{17,25},{10,2},{18,26},{11,3},{19,27},{12,4},{... | collective-permute-start | bytes 1179656 | tf_op jit(solution)/shard_map/ppermute | solution.py:329
  43.1 6.7 %meta.1 = (f32[4,3072]{1,0:T(4,128)S(1)}, s32[1,3072]{1,0:T(1,128)S(1)}, bf16[256,1024]{1,0:T(8,128)(2,1)S(1)}, f32[512,512]{1,0:T(8,128)S(1)}, s32[1,512]{1,0:T(1,128)S(1)}) custom-call(s32[3]{0:T(128)S(1)} %pad_add_fusion.place, s32[16,24,128]{2,1,0:T(8,128)S(1)} %all-to-all-done.meta), custom_call_target="tpu_custom_call" | custom-call | flops 1 | bytes 1 | tf_op jit(solution)/shard_map/meta/pallas_call | solution.py:255
  49.8 1.0 %copy-done.10 = f32[512,512]{1,0:T(8,128)} copy-done((f32[512,512]{1,0:T(8,128)}, f32[512,512]{1,0:T(8,128)S(1)}, u32[]{:S(2)}) %copy-start.10) | copy-done | bytes 1048600
  50.7 0.0 collective-permute-done.3.refs_3_.refs_7_.refs_8_
  50.7 0.0 collective-permute-done.5.refs_5_.refs_9_.refs_10_
  50.8 0.0 collective-permute-done.9.refs_7_.refs_11_.refs_12_
  50.8 0.0 copy-start.7
  50.8 1.3 %copy-done.7 = bf16[256,768]{1,0:T(8,128)(2,1)S(1)} copy-done((bf16[256,768]{1,0:T(8,128)(2,1)S(1)}, bf16[256,768]{1,0:T(8,128)(2,1)}, u32[]{:S(2)}) %copy-start.7) | copy-done | bytes 393240
  52.1 1.4 %pack.1 = bf16[256,768]{1,0:T(8,128)(2,1)S(1)} custom-call(s32[3]{0:T(128)S(1)} %pad_add_fusion.place, bf16[256,1024]{1,0:T(8,128)(2,1)S(1)} %get-tuple-element.22.select, bf16[512,768]{1,0:T(8,128)(2,1)S(1)} %copy-done.1, bf16[256,768]{1,0:T(8,128)(2,1)S(1)} %copy-done.7, bf16[400,768]{1,0:T(8,128)(2,1)S(1)} %collective-permute-done.refs_2_.refs_6_.refs_7_, ...), custom_call_target="tpu_custom_call" | custom-call | flops 1 | bytes 1 | tf_op jit(solution)/shard_map/pack/pallas_call | solution.py:255
  53.5 0.7 copy-done.9
  54.3 6.1 %all-to-all-start.1 = ((bf16[4,64,768]{2,1,0:T(8,128)(2,1)}), bf16[4,64,768]{2,1,0:T(8,128)(2,1)}, u32[]{:S(2)}, u32[]{:S(2)}) async-start(bf16[4,64,768]{2,1,0:T(8,128)(2,1)} %bitcast.10), calls=%async_computation.1 | async-start | bytes 786432 | tf_op jit(solution)/shard_map/all_to_all | solution.py:393
  60.4 1.1 %copy-done.3 = bf16[400,768]{1,0:T(8,128)(2,1)S(1)} copy-done((bf16[400,768]{1,0:T(8,128)(2,1)S(1)}, bf16[400,768]{1,0:T(8,128)(2,1)}, u32[]{:S(2)}) %copy-start.3) | copy-done | bytes 614424
  61.4 1.1 %copy-done.5 = bf16[400,768]{1,0:T(8,128)(2,1)S(1)} copy-done((bf16[400,768]{1,0:T(8,128)(2,1)S(1)}, bf16[400,768]{1,0:T(8,128)(2,1)}, u32[]{:S(2)}) %copy-start.5) | copy-done | bytes 614424
  62.5 1.0 %copy-done.8 = bf16[256,768]{1,0:T(8,128)(2,1)S(1)} copy-done((bf16[256,768]{1,0:T(8,128)(2,1)S(1)}, bf16[256,768]{1,0:T(8,128)(2,1)}, u32[]{:S(2)}) %copy-start.8) | copy-done | bytes 393240
  63.5 1.0 %copy-done.13 = bf16[256,768]{1,0:T(8,128)(2,1)S(1)} copy-done((bf16[256,768]{1,0:T(8,128)(2,1)S(1)}, bf16[256,768]{1,0:T(8,128)(2,1)}, u32[]{:S(2)}) %copy-start.13) | copy-done | bytes 393240
  64.5 3.0 %score.5 = f32[2,2,128]{2,1,0:T(2,128)S(1)} custom-call(s32[3]{0:T(128)S(1)} %pad_add_fusion.place, s32[16,24,128]{2,1,0:T(8,128)S(1)} %all-to-all-done.meta, bf16[256,768]{1,0:T(8,128)(2,1)S(1)} %copy-done.13, bf16[256,768]{1,0:T(8,128)(2,1)} %collective-permute-done.7.refs_1_, f32[4,3072]{1,0:T(4,128)S(1)} %get-tuple-element.30.refs_1_.refs_2_, ...), custom_call_target="tpu_custom_call" | custom-call | flops 1 | bytes 1 | tf_op jit(solution)/shard_map/score/pallas_call | solution.py:255
  67.5 3.1 %collective-permute-start.12 = (f32[2,2,128]{2,1,0:T(2,128)S(1)}, f32[2,2,128]{2,1,0:T(2,128)S(1)}, u32[]{:S(2)}, u32[]{:S(2)}) collective-permute-start(f32[2,2,128]{2,1,0:T(2,128)S(1)} %score.5), channel_id=1, source_target_pairs={{0,16},{8,24},{16,0},{24,8},{1,17},{9,25},{17,1},{25,9},{2,18},{10... | collective-permute-start | bytes 6152 | tf_op jit(solution)/shard_map/ppermute | solution.py:268
  70.6 3.0 %score.4 = f32[2,2,128]{2,1,0:T(2,128)S(1)} custom-call(s32[3]{0:T(128)S(1)} %pad_add_fusion.place, s32[16,24,128]{2,1,0:T(8,128)S(1)} %all-to-all-done.meta, bf16[256,768]{1,0:T(8,128)(2,1)} %collective-permute-done.1.refs_0_, f32[4,3072]{1,0:T(4,128)S(1)} %get-tuple-element.30.refs_1_.refs_2_, s32[1,3072]{1,0:T(1,128)S(1)} %get-tuple-element.31.refs_2_.refs_3_, ...), custom_call_target="tpu_custom_call" | custom-call | flops 1 | bytes 1 | tf_op jit(solution)/shard_map/score/pallas_call | solution.py:255
  73.6 0.0 copy-start.15
  73.6 1.4 %collective-permute-start.11 = (f32[2,2,128]{2,1,0:T(2,128)S(1)}, f32[2,2,128]{2,1,0:T(2,128)S(1)}, u32[]{:S(2)}, u32[]{:S(2)}) collective-permute-start(f32[2,2,128]{2,1,0:T(2,128)S(1)} %score.4), channel_id=1, source_target_pairs={{0,8},{8,0},{16,24},{24,16},{1,9},{9,1},{17,25},{25,17},{2,10},{10... | collective-permute-start | bytes 6152 | tf_op jit(solution)/shard_map/ppermute | solution.py:268
  75.0 0.0 collective-permute-done.13.refs_0_
  75.0 3.1 %score.6 = f32[2,2,128]{2,1,0:T(2,128)S(1)} custom-call(s32[3]{0:T(128)S(1)} %pad_add_fusion.place, s32[16,24,128]{2,1,0:T(8,128)S(1)} %all-to-all-done.meta, bf16[256,768]{1,0:T(8,128)(2,1)} %collective-permute-done.13.refs_0_, bf16[256,768]{1,0:T(8,128)(2,1)} %collective-permute-done.2.refs_1_, f32[4,3072]{1,0:T(4,128)S(1)} %get-tuple-element.30.refs_1_.refs_2_, ...), custom_call_target="tpu_custom_call" | custom-call | flops 1 | bytes 1 | tf_op jit(solution)/shard_map/score/pallas_call | solution.py:255
  78.1 0.2 collective-permute-start.14
  78.3 0.6 broadcast_select_fusion
  78.9 2.5 %score.7 = f32[2,2,128]{2,1,0:T(2,128)S(1)} custom-call(s32[3]{0:T(128)S(1)} %pad_add_fusion.place, s32[16,24,128]{2,1,0:T(8,128)S(1)} %all-to-all-done.meta, bf16[256,768]{1,0:T(8,128)(2,1)S(1)} %copy-done.15, f32[4,3072]{1,0:T(4,128)S(1)} %get-tuple-element.30.refs_1_.refs_2_, s32[1,3072]{1,0:T(1,128)S(1)} %get-tuple-element.31.refs_2_.refs_3_, ...), custom_call_target="tpu_custom_call" | custom-call | flops 1 | bytes 1 | tf_op jit(solution)/shard_map/score/pallas_call | solution.py:255
  81.4 0.0 all-to-all-done.1
  81.4 0.1 collective-permute-start.10
  81.5 0.0 collective-permute-done.12
  81.5 0.0 collective-permute-done.11
  81.5 2.1 %collective-permute-done.14 = f32[2,2,128]{2,1,0:T(2,128)S(1)} collective-permute-done((f32[2,2,128]{2,1,0:T(2,128)S(1)}, f32[2,2,128]{2,1,0:T(2,128)S(1)}, u32[]{:S(2)}, u32[]{:S(2)}) %collective-permute-start.14) | collective-permute-done | bytes 2080 | tf_op jit(solution)/shard_map/ppermute | solution.py:268
  83.6 0.6 fusion.1
  84.2 0.0 collective-permute-done.10.refs_1_
  84.2 1.2 %copy-done.11 = f32[512,512]{1,0:T(8,128)S(1)} copy-done((f32[512,512]{1,0:T(8,128)S(1)}, f32[512,512]{1,0:T(8,128)}, u32[]{:S(2)}) %copy-start.11) | copy-done | bytes 1048600
  85.4 2.5 %apply.1 = bf16[512,768]{1,0:T(8,128)(2,1)} custom-call(f32[512,512]{1,0:T(8,128)S(1)} %copy-done.11, bf16[512,768]{1,0:T(8,128)(2,1)S(1)} %copy-done.1, bf16[256,768]{1,0:T(8,128)(2,1)} %bitcast.6.refs_0_, bf16[256,768]{1,0:T(8,128)(2,1)S(1)} %collective-permute-done.10.refs_1_), custom_call_target="tpu_custom_call" | custom-call | flops 1 | bytes 1 | tf_op jit(solution)/shard_map/apply/pallas_call | solution.py:255
  (25 shorter events, 0.1 us)
Async XLA Ops:
  0.6 10.3 %copy-start.16 = (s32[1,2048]{1,0:T(1,128)S(1)}, s32[1,2048]{1,0:T(1,128)}, u32[]{:S(2)}) copy-start(s32[1,2048]{1,0:T(1,128)} %param.11) | copy-start | bytes 24580
  0.7 1.1 %copy-start = (bf16[512,768]{1,0:T(8,128)(2,1)S(1)}, bf16[512,768]{1,0:T(8,128)(2,1)}, u32[]{:S(2)}) copy-start(bf16[512,768]{1,0:T(8,128)(2,1)} %refs_4_.3) | copy-start | bytes 2359300
  1.9 1.0 %copy-start.6 = (bf16[256,768]{1,0:T(8,128)(2,1)S(1)}, bf16[256,768]{1,0:T(8,128)(2,1)}, u32[]{:S(2)}) copy-start(bf16[256,768]{1,0:T(8,128)(2,1)} %refs_5_.7) | copy-start | bytes 1179652
  2.9 5.1 %copy-start.14 = (bf16[256,768]{1,0:T(8,128)(2,1)S(1)}, bf16[256,768]{1,0:T(8,128)(2,1)}, u32[]{:S(2)}) copy-start(bf16[256,768]{1,0:T(8,128)(2,1)} %refs_0_.3) | copy-start | bytes 1179652
  2.9 8.1 %copy-start.19 = (s32[256]{0:T(256)S(1)}, s32[256]{0:T(256)}, u32[]{:S(2)}) copy-start(s32[256]{0:T(256)} %param.9) | copy-start | bytes 3076
  2.9 47.9 %copy-start.1 = (bf16[512,768]{1,0:T(8,128)(2,1)S(1)}, bf16[512,768]{1,0:T(8,128)(2,1)}, u32[]{:S(2)}) copy-start(bf16[512,768]{1,0:T(8,128)(2,1)} %refs_4_.3) | copy-start | bytes 2359300
  4.9 6.0 %copy-start.17 = (s32[512]{0:T(512)S(1)}, s32[512]{0:T(512)}, u32[]{:S(2)}) copy-start(s32[512]{0:T(512)} %param.8) | copy-start | bytes 6148
  4.9 6.0 %copy-start.18 = (s32[256]{0:T(256)S(1)}, s32[256]{0:T(256)}, u32[]{:S(2)}) copy-start(s32[256]{0:T(256)} %param.13) | copy-start | bytes 3076
  5.0 22.5 %collective-permute-start = (bf16[400,768]{1,0:T(8,128)(2,1)}, bf16[400,768]{1,0:T(8,128)(2,1)S(1)}, u32[]{:S(2)}, u32[]{:S(2)}) collective-permute-start(bf16[400,768]{1,0:T(8,128)(2,1)} %get-tuple-element.19), channel_id=1, source_target_pairs={{0,2},{1,5},{2,0},{3,7},{4,6},{5,1},{6,4},{7,3},{8,10},{9,13},{10,... | collective-permute-start | bytes 1843208 | tf_op jit(solution)/shard_map/ppermute | solution.py:319
  8.0 19.4 %collective-permute-start.1 = (bf16[256,768]{1,0:T(8,128)(2,1)S(1)}, bf16[256,768]{1,0:T(8,128)(2,1)}, u32[]{:S(2)}, u32[]{:S(2)}) collective-permute-start(bf16[256,768]{1,0:T(8,128)(2,1)S(1)} %copy-done.14), channel_id=1, source_target_pairs={{0,8},{8,0},{16,24},{24,16},{1,9},{9,1},{17,25},{25,17},{2,10},{10... | collective-permute-start | bytes 1179656 | tf_op jit(solution)/shard_map/ppermute | solution.py:268
  9.5 17.9 %collective-permute-start.2 = (bf16[256,768]{1,0:T(8,128)(2,1)S(1)}, bf16[256,768]{1,0:T(8,128)(2,1)}, u32[]{:S(2)}, u32[]{:S(2)}) collective-permute-start(bf16[256,768]{1,0:T(8,128)(2,1)S(1)} %copy-done.14), channel_id=1, source_target_pairs={{8,16},{16,8},{9,17},{17,9},{10,18},{18,10},{11,19},{19,11},{12,20... | collective-permute-start | bytes 1179656 | tf_op jit(solution)/shard_map/ppermute | solution.py:323
  11.7 15.7 %all-to-all-start = ((s32[16,24,128]{2,1,0:T(8,128)}), s32[16,24,128]{2,1,0:T(8,128)S(1)}, u32[]{:S(2)}, u32[]{:S(2)}) async-start(s32[16,24,128]{2,1,0:T(8,128)} %broadcast_in_dim.5), calls=%async_computation | async-start | bytes 393216 | tf_op jit(solution)/shard_map/all_to_all | solution.py:290
  17.7 14.2 %collective-permute-start.4 = (bf16[400,768]{1,0:T(8,128)(2,1)}, bf16[400,768]{1,0:T(8,128)(2,1)S(1)}, u32[]{:S(2)}, u32[]{:S(2)}) collective-permute-start(bf16[400,768]{1,0:T(8,128)(2,1)} %get-tuple-element.19), channel_id=1, source_target_pairs={{0,4},{1,3},{2,6},{3,1},{4,0},{5,7},{6,2},{7,5},{8,12},{9,11},{10,... | collective-permute-start | bytes 1843208 | tf_op jit(solution)/shard_map/ppermute | solution.py:320
  27.4 14.4 %collective-permute-start.6 = (bf16[400,768]{1,0:T(8,128)(2,1)S(1)}, bf16[400,768]{1,0:T(8,128)(2,1)S(1)}, u32[]{:S(2)}, u32[]{:S(2)}) collective-permute-start(bf16[400,768]{1,0:T(8,128)(2,1)S(1)} %collective-permute-done.refs_2_.refs_6_.refs_7_), channel_id=1, source_target_pairs={{0,4},{1,3},{2,6},{3,1},{4,0},{5,7},{6,2},{7,5},{8,12},{9,11},{10,... | collective-permute-start | bytes 1843208 | tf_op jit(solution)/shard_map/ppermute | solution.py:327
  29.1 3.3 %collective-permute-start.7 = (bf16[256,768]{1,0:T(8,128)(2,1)}, bf16[256,768]{1,0:T(8,128)(2,1)}, u32[]{:S(2)}, u32[]{:S(2)}) collective-permute-start(bf16[256,768]{1,0:T(8,128)(2,1)} %collective-permute-done.1.refs_0_), channel_id=1, source_target_pairs={{8,16},{16,8},{9,17},{17,9},{10,18},{18,10},{11,19},{19,11},{12,20... | collective-permute-start | bytes 1179656 | tf_op jit(solution)/shard_map/ppermute | solution.py:325
  30.5 10.5 %collective-permute-start.8 = (bf16[256,768]{1,0:T(8,128)(2,1)}, bf16[256,768]{1,0:T(8,128)(2,1)S(1)}, u32[]{:S(2)}, u32[]{:S(2)}) collective-permute-start(bf16[256,768]{1,0:T(8,128)(2,1)} %collective-permute-done.2.refs_1_), channel_id=1, source_target_pairs={{8,0},{16,24},{9,1},{17,25},{10,2},{18,26},{11,3},{19,27},{12,4},{... | collective-permute-start | bytes 1179656 | tf_op jit(solution)/shard_map/ppermute | solution.py:326
  31.8 18.9 %collective-permute-start.3 = (bf16[400,768]{1,0:T(8,128)(2,1)S(1)}, bf16[400,768]{1,0:T(8,128)(2,1)S(1)}, u32[]{:S(2)}, u32[]{:S(2)}) collective-permute-start(bf16[400,768]{1,0:T(8,128)(2,1)S(1)} %collective-permute-done.refs_2_.refs_6_.refs_7_), channel_id=1, source_target_pairs={{0,1},{1,0},{2,3},{3,2},{4,5},{5,4},{6,7},{7,6},{8,9},{9,8},{10,11... | collective-permute-start | bytes 1843208 | tf_op jit(solution)/shard_map/ppermute | solution.py:268
  31.9 18.8 %collective-permute-start.5 = (bf16[400,768]{1,0:T(8,128)(2,1)S(1)}, bf16[400,768]{1,0:T(8,128)(2,1)S(1)}, u32[]{:S(2)}, u32[]{:S(2)}) collective-permute-start(bf16[400,768]{1,0:T(8,128)(2,1)S(1)} %collective-permute-done.4.refs_4_.refs_8_.refs_9_), channel_id=1, source_target_pairs={{0,1},{1,0},{2,3},{3,2},{4,5},{5,4},{6,7},{7,6},{8,9},{9,8},{10,11... | collective-permute-start | bytes 1843208 | tf_op jit(solution)/shard_map/ppermute | solution.py:268
  41.0 0.7 copy-start.12
  41.8 9.0 %collective-permute-start.9 = (bf16[400,768]{1,0:T(8,128)(2,1)S(1)}, bf16[400,768]{1,0:T(8,128)(2,1)S(1)}, u32[]{:S(2)}, u32[]{:S(2)}) collective-permute-start(bf16[400,768]{1,0:T(8,128)(2,1)S(1)} %collective-permute-done.6.refs_6_.refs_10_.refs_11_), channel_id=1, source_target_pairs={{0,1},{1,0},{2,3},{3,2},{4,5},{5,4},{6,7},{7,6},{8,9},{9,8},{10,11... | collective-permute-start | bytes 1843208 | tf_op jit(solution)/shard_map/ppermute | solution.py:268
  41.8 33.2 %collective-permute-start.13 = (bf16[256,768]{1,0:T(8,128)(2,1)}, bf16[256,768]{1,0:T(8,128)(2,1)}, u32[]{:S(2)}, u32[]{:S(2)}) collective-permute-start(bf16[256,768]{1,0:T(8,128)(2,1)} %collective-permute-done.7.refs_1_), channel_id=1, source_target_pairs={{8,0},{16,24},{9,1},{17,25},{10,2},{18,26},{11,3},{19,27},{12,4},{... | collective-permute-start | bytes 1179656 | tf_op jit(solution)/shard_map/ppermute | solution.py:329
  49.8 1.0 %copy-start.10 = (f32[512,512]{1,0:T(8,128)}, f32[512,512]{1,0:T(8,128)S(1)}, u32[]{:S(2)}) copy-start(f32[512,512]{1,0:T(8,128)S(1)} %get-tuple-element.21.select) | copy-start | bytes 3145732
  50.8 2.7 %copy-start.2 = (bf16[400,768]{1,0:T(8,128)(2,1)}, bf16[400,768]{1,0:T(8,128)(2,1)S(1)}, u32[]{:S(2)}) copy-start(bf16[400,768]{1,0:T(8,128)(2,1)S(1)} %collective-permute-done.5.refs_5_.refs_9_.refs_10_) | copy-start | bytes 1843204
  50.8 2.7 %copy-start.4 = (bf16[400,768]{1,0:T(8,128)(2,1)}, bf16[400,768]{1,0:T(8,128)(2,1)S(1)}, u32[]{:S(2)}) copy-start(bf16[400,768]{1,0:T(8,128)(2,1)S(1)} %collective-permute-done.9.refs_7_.refs_11_.refs_12_) | copy-start | bytes 1843204
  50.8 1.3 %copy-start.7 = (bf16[256,768]{1,0:T(8,128)(2,1)S(1)}, bf16[256,768]{1,0:T(8,128)(2,1)}, u32[]{:S(2)}) copy-start(bf16[256,768]{1,0:T(8,128)(2,1)} %refs_5_.7) | copy-start | bytes 1179652
  53.5 0.8 copy-start.9
  54.3 27.2 %all-to-all-start.1 = ((bf16[4,64,768]{2,1,0:T(8,128)(2,1)}), bf16[4,64,768]{2,1,0:T(8,128)(2,1)}, u32[]{:S(2)}, u32[]{:S(2)}) async-start(bf16[4,64,768]{2,1,0:T(8,128)(2,1)} %bitcast.10), calls=%async_computation.1 | async-start | bytes 786432 | tf_op jit(solution)/shard_map/all_to_all | solution.py:393
  60.4 1.1 %copy-start.3 = (bf16[400,768]{1,0:T(8,128)(2,1)S(1)}, bf16[400,768]{1,0:T(8,128)(2,1)}, u32[]{:S(2)}) copy-start(bf16[400,768]{1,0:T(8,128)(2,1)} %copy-done.2) | copy-start | bytes 1843204
  61.4 1.1 %copy-start.5 = (bf16[400,768]{1,0:T(8,128)(2,1)S(1)}, bf16[400,768]{1,0:T(8,128)(2,1)}, u32[]{:S(2)}) copy-start(bf16[400,768]{1,0:T(8,128)(2,1)} %copy-done.4) | copy-start | bytes 1843204
  62.5 1.0 %copy-start.8 = (bf16[256,768]{1,0:T(8,128)(2,1)S(1)}, bf16[256,768]{1,0:T(8,128)(2,1)}, u32[]{:S(2)}) copy-start(bf16[256,768]{1,0:T(8,128)(2,1)} %refs_5_.7) | copy-start | bytes 1179652
  63.5 1.0 %copy-start.13 = (bf16[256,768]{1,0:T(8,128)(2,1)S(1)}, bf16[256,768]{1,0:T(8,128)(2,1)}, u32[]{:S(2)}) copy-start(bf16[256,768]{1,0:T(8,128)(2,1)} %copy-done.12) | copy-start | bytes 1179652
  67.5 14.0 %collective-permute-start.12 = (f32[2,2,128]{2,1,0:T(2,128)S(1)}, f32[2,2,128]{2,1,0:T(2,128)S(1)}, u32[]{:S(2)}, u32[]{:S(2)}) collective-permute-start(f32[2,2,128]{2,1,0:T(2,128)S(1)} %score.5), channel_id=1, source_target_pairs={{0,16},{8,24},{16,0},{24,8},{1,17},{9,25},{17,1},{25,9},{2,18},{10... | collective-permute-start | bytes 6152 | tf_op jit(solution)/shard_map/ppermute | solution.py:268
  73.6 5.3 %copy-start.15 = (bf16[256,768]{1,0:T(8,128)(2,1)S(1)}, bf16[256,768]{1,0:T(8,128)(2,1)}, u32[]{:S(2)}) copy-start(bf16[256,768]{1,0:T(8,128)(2,1)} %refs_0_.3) | copy-start | bytes 1179652
  73.6 7.9 %collective-permute-start.11 = (f32[2,2,128]{2,1,0:T(2,128)S(1)}, f32[2,2,128]{2,1,0:T(2,128)S(1)}, u32[]{:S(2)}, u32[]{:S(2)}) collective-permute-start(f32[2,2,128]{2,1,0:T(2,128)S(1)} %score.4), channel_id=1, source_target_pairs={{0,8},{8,0},{16,24},{24,16},{1,9},{9,1},{17,25},{25,17},{2,10},{10... | collective-permute-start | bytes 6152 | tf_op jit(solution)/shard_map/ppermute | solution.py:268
  78.1 5.4 %collective-permute-start.14 = (f32[2,2,128]{2,1,0:T(2,128)S(1)}, f32[2,2,128]{2,1,0:T(2,128)S(1)}, u32[]{:S(2)}, u32[]{:S(2)}) collective-permute-start(f32[2,2,128]{2,1,0:T(2,128)S(1)} %score.6), channel_id=1, source_target_pairs={{0,24},{8,16},{16,8},{24,0},{1,25},{9,17},{17,9},{25,1},{2,26},{10... | collective-permute-start | bytes 6152 | tf_op jit(solution)/shard_map/ppermute | solution.py:268
  81.4 2.7 %collective-permute-start.10 = (bf16[256,768]{1,0:T(8,128)(2,1)}, bf16[256,768]{1,0:T(8,128)(2,1)S(1)}, u32[]{:S(2)}, u32[]{:S(2)}) collective-permute-start(bf16[256,768]{1,0:T(8,128)(2,1)} %bitcast.6.refs_0_), channel_id=1, source_target_pairs={{0,1},{1,0},{2,3},{3,2},{4,5},{5,4},{6,7},{7,6},{8,9},{9,8},{10,11... | collective-permute-start | bytes 1179656 | tf_op jit(solution)/shard_map/ppermute | solution.py:268
  84.2 1.2 %copy-start.11 = (f32[512,512]{1,0:T(8,128)S(1)}, f32[512,512]{1,0:T(8,128)}, u32[]{:S(2)}) copy-start(f32[512,512]{1,0:T(8,128)} %copy-done.10) | copy-start | bytes 3145732

commit v5 on v4

v5 whole, which is shorter than its diff:
```python
import functools
import math

import jax
import jax.numpy as jnp
from jax import lax
from jax.experimental import pallas as pl
from jax.experimental.pallas import tpu as pltpu
from jax.sharding import Mesh, PartitionSpec as P

score_scale = 20.0
age_scale = 16.0
epsilon = 1e-06
LOG2E = math.log2(math.e)
MASKED = -1e30
LANES = 128

NT = (((1,), (1,)), ((), ()))
NN = (((1,), (0,)), ((), ()))


def one_hot(ids, count):
    rows = lax.broadcasted_iota(jnp.int32, (count, ids.shape[1]), 0)
    return jnp.where(rows == ids, 1.0, 0.0).astype(jnp.bfloat16)


def split_terms(values):
    terms = []
    for _ in range(3):
        terms.append(values.astype(jnp.bfloat16))
        values = values - terms[-1].astype(jnp.float32)
    return terms


def counted(hits):
    count = hits.shape[1]
    before = lax.broadcasted_iota(jnp.int32, (count, count), 0)
    after = lax.broadcasted_iota(jnp.int32, (count, count), 1)
    earlier = jnp.where(before < after, 1.0, 0.0).astype(jnp.bfloat16)
    return lax.dot_general(hits.astype(jnp.bfloat16), earlier, NN, preferred_element_type=jnp.float32)


def small(values):
    return values.astype(jnp.float32).astype(jnp.bfloat16)


def number(values):
    return values.astype(jnp.float32).astype(jnp.int32)


def prep_kernel(
    place, table, fresh, ref_ids, ages, neg, pos, mail, rows_out, scale_out, table_in, fresh_in, arrived,
    *, owners, cap, replicas, encode
):
    core = place[2]
    copies = [
        pltpu.make_async_copy(fresh, fresh_in, arrived.at[0]),
        pltpu.make_async_copy(table, table_in, arrived.at[1]),
    ]
    for copy in copies:
        copy.start()
    rows_dev, width = table.shape
    refresh_dev, list_size = ref_ids.shape[1], neg.shape[1]
    share = cap // replicas

    mail[...] = jnp.zeros_like(mail)
    ids = ref_ids[...]
    lines = [
        jnp.concatenate([small(ids >> 7), small(ids & 127), small(pos[...] >> 7)], axis=1),
        jnp.concatenate([small(pos[...] & 127), small(ages[...])], axis=1),
    ]
    for digits in (neg[...] >> 7, neg[...] & 127):
        for first in range(0, list_size, width):
            lines.append(small(digits[:, first : first + width]))
    for owner in range(owners):
        for i, line in enumerate(lines):
            mail[owner, share + i : share + i + 1, : line.shape[1]] = line

    owner_of = ids // rows_dev
    hits = one_hot(owner_of, owners).astype(jnp.float32)
    rank = jnp.sum(hits * counted(hits), axis=0, keepdims=True).astype(jnp.int32) - core * share
    code = jnp.where((rank >= 0) & (rank < share), owner_of * share + rank, -1)
    select = one_hot(code, owners * share)
    copies[0].wait()
    packed = lax.dot_general(select, fresh_in[...], NN, preferred_element_type=jnp.float32).astype(jnp.bfloat16)
    for owner in range(owners):
        mail[owner, :share, :] = packed[owner * share : (owner + 1) * share, :]

    copies[1].wait()
    line, row = 0, 0
    halves = []
    for source in (table_in, fresh_in):
        rows = source.shape[0]
        half = rows // replicas
        rows_out[row : row + half, :] = source[pl.ds(pl.multiple_of(core * half, half), half), :]
        row += half
        for block in range(rows // LANES):
            squares = jnp.zeros((LANES, LANES), jnp.float32)
            for chunk in range(width // LANES):
                values = source[block * LANES : (block + 1) * LANES, chunk * LANES : (chunk + 1) * LANES]
                values = values.astype(jnp.float32)
                squares += values * values
            mean = jnp.sum(squares.T, axis=0, keepdims=True) / width
            scale_out[line + block : line + block + 1, :] = lax.rsqrt(mean + epsilon) * (score_scale / width * LOG2E)
        if encode:
            halves += [(line, i, half // LANES) for i in range(half // LANES)]
        line += rows // LANES
    if encode:
        rows_out[row:, :] = jnp.zeros((16, width), jnp.bfloat16)
        terms = []
        for first, i, count in halves:
            terms += split_terms(scale_out[pl.ds(first + core * count + i, 1), :])
        for i, term in enumerate(terms):
            rows_out[row + i : row + i + 1, :LANES] = term


def meta_kernel(place, mail, lw_out, row_out, target_out, own_out, *, planes, sizes, cap, replicas):
    outer, inner, core = place[0], place[1], place[2]
    owners, _, width = mail.shape
    owners_plane = owners // planes
    refresh_dev, rows_dev, list_size = sizes
    share = cap // replicas
    plane_rows = owners_plane * rows_dev
    high_count = planes * plane_rows // LANES
    own_owner = outer * owners_plane + inner

    def ref_digits(owner):
        line = number(mail[owner, share : share + 1, : 2 * refresh_dev])
        return line[:, :refresh_dev], line[:, refresh_dev:]

    def joined(pairs):
        return tuple(jnp.concatenate(part, axis=1) for part in zip(*pairs))

    def one_hots(pair):
        return one_hot(pair[0], high_count), one_hot(pair[1], LANES)

    def bitmap(pair):
        high, low = one_hots(pair)
        return lax.dot_general(low, high, NT, preferred_element_type=jnp.float32)

    def lookup(one_map, pair):
        hit = lax.dot_general(one_map.astype(jnp.bfloat16), pair[0], NN, preferred_element_type=jnp.float32)
        return jnp.sum(hit * pair[1].astype(jnp.float32), axis=0, keepdims=True) > 0.5

    beside = [outer * owners_plane + (inner ^ s) for s in range(owners_plane)]
    all_digits = [ref_digits(owner) for owner in range(owners)]
    refreshed_map = bitmap(joined(all_digits))
    plane_digits = joined([ref_digits(owner) for owner in beside])
    column = lax.broadcasted_iota(jnp.int32, (1, plane_rows), 1)
    table_ids = (outer * owners_plane + (inner ^ (column // rows_dev))) * rows_dev + column % rows_dev
    table_hots = one_hots((table_ids >> 7, table_ids & 127))
    fresh_hots = one_hots(plane_digits)

    ages = [number(mail[owner, share + 1 : share + 2, width - rows_dev :]) for owner in beside]
    ages = jnp.concatenate(ages, axis=1).astype(jnp.float32)
    weight = jnp.exp(-ages / age_scale).astype(jnp.bfloat16).astype(jnp.float32)
    refreshed = lookup(refreshed_map, table_hots)
    row_out[:, :plane_rows] = jnp.where(refreshed, -1, table_ids)
    row_out[:, plane_rows:] = plane_digits[0] * LANES + plane_digits[1]
    own_out[...] = refreshed[:, :rows_dev].astype(jnp.int32)
    log_weight = jnp.where(refreshed, MASKED, jnp.log2(weight))

    lines = -(-list_size // width)
    for group in range(planes):
        owner = (outer ^ group) * owners_plane + inner
        digits = []
        for first in (share + 2, share + 2 + lines):
            parts = [mail[owner, first + i : first + i + 1, :] for i in range(lines)]
            digits.append(number(jnp.concatenate(parts, axis=1)[:, :list_size]))
        one_map = bitmap(digits)
        lw_out[group : group + 1, :plane_rows] = jnp.where(lookup(one_map, table_hots), log_weight, MASKED)
        lw_out[group : group + 1, plane_rows:] = jnp.where(lookup(one_map, fresh_hots), 0.0, MASKED)

    local = [high * LANES + low - own_owner * rows_dev for high, low in all_digits]
    local = jnp.concatenate(local, axis=0)
    match = (local >= 0) & (local < rows_dev)
    rank = counted(jnp.where(match, 1.0, 0.0)).astype(jnp.int32)
    slot = jnp.where(match, ((rank // share) ^ core) * share + rank % share, -1)
    for owner in range(owners):
        row = jnp.where(match, local, 0)[owner : owner + 1, :]
        kinds = lax.broadcasted_iota(jnp.int32, (8, refresh_dev), 0)
        digits = jnp.where(kinds == 0, row // 16, jnp.where(kinds == 1, row % 16, 1))
        hits = one_hot(slot[owner : owner + 1, :], cap)
        found = lax.dot_general(small(digits), hits, NT, preferred_element_type=jnp.float32).astype(jnp.int32)
        target = jnp.where(found[2:3, :] > 0, found[0:1, :] * 16 + found[1:2, :], -1)
        for part in range(replicas):
            first = (part * owners + owner) * share
            target_out[:, first : first + share] = target[:, part * share : (part + 1) * share]


def piece_offset(place, piece):
    column, size, flip, by_core = piece
    if flip is None:
        return column
    column += (place[2] ^ flip) * size
    if by_core is not None:
        column += (place[2] ^ by_core) * size * 2
    return pl.multiple_of(column, size)


def apply_kernel(target, table, *refs):
    out = refs[-1]
    rows = lax.broadcasted_iota(jnp.int32, (table.shape[0], target.shape[1]), 0)
    chosen = jnp.where(rows == target[...], 1.0, 0.0)
    share = target.shape[1] // len(refs[:-1]) // refs[0].shape[0]
    arrived = [part[owner, :share, :] for part in refs[:-1] for owner in range(part.shape[0])]
    arrived = jnp.concatenate(arrived, axis=0)
    fresh = lax.dot_general(chosen.astype(jnp.bfloat16), arrived, NN, preferred_element_type=jnp.float32)
    hit = jnp.sum(chosen, axis=1, keepdims=True) > 0.5
    out[...] = jnp.where(hit, fresh, table[...].astype(jnp.float32)).astype(jnp.bfloat16)


def to_lanes(row):
    return jnp.broadcast_to(row, (LANES, LANES)).T


def score_kernel(place, mail, *refs, pieces, flip, share, owners_plane, given):
    out, total, pos_total, q_scale, pos_b, chosen = refs[-6:]
    queries = refs[0]
    if given == 2:
        at_end = (place[0] == 0) | (place[0] == 3)
        chosen[...] = jnp.where(at_end, refs[0][...], refs[1][...])
        queries = chosen
    log_weight, row_ids, scale, *refs = refs[given:-6]
    count, width = queries.shape
    owner = (place[0] ^ flip) * owners_plane + place[1]
    positive = number(mail[owner, share : share + 1, width - count :]) * LANES
    positive = (positive + number(mail[owner, share + 1 : share + 2, :count])).astype(jnp.float32)
    for block in range(count // LANES):
        part = slice(block * LANES, (block + 1) * LANES)
        values = queries[part, :].astype(jnp.float32)
        squares = jnp.sum(values * values, axis=1, keepdims=True)
        q_scale[part, :] = jnp.broadcast_to(lax.rsqrt(squares / width + epsilon), (LANES, LANES))
        pos_b[part, :] = to_lanes(positive[:, part])
    total[...] = jnp.zeros_like(total)
    pos_total[...] = jnp.zeros_like(pos_total)
    for source, start, size, column, scale_at in pieces:
        first = piece_offset(place, column)
        raw = lax.dot_general(
            queries[...], refs[source][start : start + size, :], NT, preferred_element_type=jnp.float32
        )
        sums = total[...]
        positives = pos_total[...]
        for chunk in range(size // LANES):
            cols = pl.ds(first + chunk * LANES, LANES)
            part = raw[:, chunk * LANES : (chunk + 1) * LANES]
            if scale_at < 0:
                line = -1 - scale_at + chunk
                row_scale = scale[line : line + 1, :]
            else:
                line = scale_at + 3 * chunk
                row_scale = jnp.sum(refs[source][line : line + 3, :LANES].astype(jnp.float32), axis=0, keepdims=True)
            powers = part * q_scale[...] * row_scale + log_weight[flip : flip + 1, cols]
            sums = sums + jnp.exp2(powers)
            positives = positives + jnp.where(pos_b[...] == row_ids[:, cols].astype(jnp.float32), powers, 0.0)
        total[...] = sums
        pos_total[...] = positives
    for block in range(count // LANES):
        part = slice(block * LANES, (block + 1) * LANES)
        out[0, block : block + 1, :] = jnp.sum(total[part, :].T, axis=0, keepdims=True)
        out[1, block : block + 1, :] = jnp.sum(pos_total[part, :].T, axis=0, keepdims=True)


def whole(memory=pltpu.VMEM):
    return pl.BlockSpec(memory_space=memory)


def call(kernel, name, outs, place, *operands, scratch=(), in_place=0, vmem=16, **options):
    specs = [whole(pltpu.HBM)] * in_place + [whole()] * (len(operands) - in_place)
    if place is not None:
        specs = [whole(pltpu.SMEM)] + specs
        operands = (place, *operands)
    return pl.pallas_call(
        functools.partial(kernel, **options),
        out_shape=tuple(outs),
        in_specs=specs,
        out_specs=tuple(whole() for _ in outs),
        scratch_shapes=list(scratch),
        compiler_params=pltpu.CompilerParams(vmem_limit_bytes=vmem << 20),
        cost_estimate=pl.CostEstimate(flops=1, bytes_accessed=1, transcendentals=0),
        name=name,
    )(*operands)


def swap(values, axis, flip):
    return lax.ppermute(values, axis, [(i, i ^ flip) for i in range(lax.axis_size(axis))])


def on_device(table, ages, refresh_ids, fresh_rows, neg_ids, queries, pos_ids):
    rows_dev, width = table.shape
    refresh_dev = refresh_ids.shape[0]
    planes = lax.axis_size("outer")
    owners_plane = lax.axis_size("inner")
    replicas = lax.axis_size("query")
    owners = planes * owners_plane
    query_count = queries.shape[0]
    list_size = neg_ids.shape[1]
    place = jnp.stack([lax.axis_index(name) for name in ("outer", "inner", "query")]).astype(jnp.int32)
    plane_rows = owners_plane * rows_dev
    plane_refresh = owners_plane * refresh_dev
    all_rows = plane_rows + plane_refresh
    cap = max(2, (2 * refresh_dev + owners - 1) // owners)
    share = cap // replicas
    table_half, fresh_half = rows_dev // replicas, refresh_dev // replicas
    bf16, f32 = jnp.bfloat16, jnp.float32

    assert 3 * refresh_dev == width and query_count + rows_dev == width and query_count == refresh_dev
    fast = replicas == 2 and owners_plane == 4 and planes == 4
    extra = 16 if fast else 0
    vmem = 16 if fast else 48
    mail, rows_half, scales = call(
        prep_kernel,
        "prep",
        [
            jax.ShapeDtypeStruct((owners, share + 8, width), bf16),
            jax.ShapeDtypeStruct((table_half + fresh_half + extra, width), bf16),
            jax.ShapeDtypeStruct(((rows_dev + refresh_dev) // LANES, LANES), f32),
        ],
        place,
        table,
        fresh_rows,
        refresh_ids.reshape(1, -1),
        ages.reshape(1, -1),
        neg_ids,
        pos_ids.reshape(1, -1),
        scratch=[
            pltpu.VMEM(table.shape, bf16),
            pltpu.VMEM(fresh_rows.shape, bf16),
            pltpu.SemaphoreType.DMA((2,)),
        ],
        in_place=2,
        vmem=vmem,
        owners=owners,
        cap=cap,
        replicas=replicas,
        encode=fast,
    )
    mail = lax.all_to_all(mail, ("outer", "inner"), split_axis=0, concat_axis=0, tiled=True)

    if fast:
        axes = ("inner", "query")
        first = [(2 * i + c, 2 * (i ^ (1 + c)) + c) for i in range(4) for c in range(2)]
        second = [(2 * i + c, 2 * (i ^ (2 - c)) + c) for i in range(4) for c in range(2)]
        near = lax.ppermute(rows_half, axes, first)
        side = lax.ppermute(rows_half, axes, second)
        middle, outward = [(1, 2), (2, 1)], [(1, 0), (2, 3)]
        beside = swap(queries, "outer", 1)
        across = lax.ppermute(queries, "outer", middle)
        near, beside, across = lax.optimization_barrier((near, beside, across))
        from_end = lax.ppermute(beside, "outer", middle)
        to_end = lax.ppermute(across, "outer", outward)
        far = lax.ppermute(near, axes, second)
        far, mail = lax.optimization_barrier((far, mail))
        last = lax.ppermute(from_end, "outer", outward)
        got_queries = [(queries,), (beside,), (to_end, from_end), (last, across)]
        buffers = [table, fresh_rows]
        table_pieces = [(0, 0, rows_dev, (0, rows_dev, None, None), -1)]
        fresh_pieces = [(1, 0, refresh_dev, (0, refresh_dev, None, None), -1 - rows_dev // LANES)]
        for slot, by_core, mine in ((1, 0, near), (1, 1, side), (3, None, far)):
            for flip, rows in enumerate((mine, swap(mine, "query", 1))):
                by = None if by_core is None else by_core ^ flip
                data = table_half + fresh_half
                fresh_at = data + 3 * (table_half // LANES)
                table_pieces.append((len(buffers), 0, table_half, (slot * rows_dev, table_half, flip, by), data))
                fresh_pieces.append(
                    (len(buffers), table_half, fresh_half, (slot * refresh_dev, fresh_half, flip, by), fresh_at)
                )
                buffers.append(rows)
    else:
        got_queries = [(queries,)] + [(swap(queries, "outer", s),) for s in range(1, planes)]
        got_rows = [rows_half] + [swap(rows_half, "inner", s) for s in range(1, owners_plane)]
        gathered = lax.all_gather(jnp.stack(got_rows), "query", axis=0)
        gathered = jnp.swapaxes(gathered, 0, 1)
        buffers = [
            gathered[:, :, :table_half].reshape(plane_rows, width),
            gathered[:, :, table_half:].reshape(plane_refresh, width),
        ]
        scales = []
        for rows in buffers:
            values = rows.astype(f32)
            mean = jnp.sum(values * values, axis=1) / width
            scales.append((lax.rsqrt(mean + epsilon) * (score_scale / width * LOG2E)).reshape(-1, LANES))
        scales = jnp.concatenate(scales)

        def blocks(buffer, count, line):
            starts = range(0, count, 512)
            return [(buffer, i, 512, (i, 512, None, None), -1 - line - i // LANES) for i in starts]

        table_pieces = blocks(0, plane_rows, 0)
        fresh_pieces = blocks(1, plane_refresh, plane_rows // LANES)

    lw, row_ids, target, own = call(
        meta_kernel,
        "meta",
        [
            jax.ShapeDtypeStruct((planes, all_rows), f32),
            jax.ShapeDtypeStruct((1, all_rows), jnp.int32),
            jax.ShapeDtypeStruct((1, owners * cap), jnp.int32),
            jax.ShapeDtypeStruct((1, rows_dev), jnp.int32),
        ],
        place,
        mail,
        vmem=vmem,
        planes=planes,
        sizes=(refresh_dev, rows_dev, list_size),
        cap=cap,
        replicas=replicas,
    )
    new_ages = jnp.where(own.reshape(rows_dev) > 0, 0, ages)
    mails = [mail] + [swap(mail, "query", flip) for flip in range(1, replicas)]

    def shift(pieces, columns):
        return [(a, b, c, (d[0] + columns, *d[1:]), e) for a, b, c, d, e in pieces]

    pieces = table_pieces + shift(fresh_pieces, plane_rows)
    mine = None
    for s in [*range(1, planes), 0]:
        (partial,) = call(
            score_kernel,
            "score",
            [jax.ShapeDtypeStruct((2, query_count // LANES, LANES), f32)],
            place,
            mail,
            *got_queries[s],
            lw,
            row_ids,
            scales,
            *buffers,
            scratch=[pltpu.VMEM((query_count, LANES), f32)] * 4 + [pltpu.VMEM(queries.shape, bf16)],
            vmem=vmem,
            pieces=pieces,
            flip=s,
            share=share,
            owners_plane=owners_plane,
            given=len(got_queries[s]),
        )
        if s:
            partial = swap(partial, "outer", s)
        mine = partial if mine is None else mine + partial
    (new_table,) = call(
        apply_kernel, "apply", [jax.ShapeDtypeStruct(table.shape, bf16)], None, target, table, *mails
    )
    loss = (jnp.log2(mine[0]) - mine[1]) * math.log(2.0)
    return new_table, new_ages, loss.reshape(query_count)


def solution(mesh):
    owners, replicas = mesh.shape["index"], mesh.shape["query"]
    inner = 1 << (int(math.log2(owners)) // 2)
    split = Mesh(mesh.devices.reshape(owners // inner, inner, replicas), ("outer", "inner", "query"))
    index = ("outer", "inner")
    placed = (
        P(index, None),
        P(index),
        P(index),
        P(index, None),
        P(index, None),
        P(("outer", "inner", "query"), None),
        P(("outer", "inner", "query")),
    )
    return jax.shard_map(
        on_device,
        mesh=split,
        in_specs=placed,
        out_specs=(P(index, None), P(index), P(("outer", "inner", "query"))),
        check_vma=False,
    )
```

time: 88.6 us -> 79.3 us (0.90)
  local copies, waits for them, and re-layouts: 12 us -> 2.85 us
  waiting for transfers between devices: 18.5 us -> 27.1 us
  starting transfers between devices: 31 us -> 24.5 us
  Pallas kernels: 24.2 us -> 22.3 us
    ppermute x8, waiting for transfers between devices: 2.07 us -> 15.1 us  [swap(): lax.ppermute(values, axis, [(i, i ^ flip) for i in range(lax.axis_size(ax...]
    unnamed x40 -> x18, local copies, waits for them, and re-layouts: 11.3 us -> 2.85 us
    all_to_all x2 -> x1, waiting for transfers between devices: 7.79 us -> 0.01 us  [on_device(): lax.all_to_all(mail, ('outer', 'inner'), split_axis=0, concat_axis=0, til...]
    all_to_all x2 -> x1, starting transfers between devices: 12.1 us -> 6.07 us  [on_device(): lax.all_to_all(mail, ('outer', 'inner'), split_axis=0, concat_axis=0, til...]
    ppermute x1, waiting for transfers between devices: 0.01 us -> 5.52 us  [on_device(): far = lax.ppermute(near, axes, second)]
    ppermute x1, waiting for transfers between devices: 8.64 us -> 6.47 us  [on_device(): to_end = lax.ppermute(across, 'outer', outward)]
    pallas_call x8 -> x7, Pallas kernels: 24.2 us -> 22.3 us  [call(): pl.pallas_call(functools.partial(kernel, **options), out_shape=tuple(outs...]
  transfers between devices with their start and end apart: 17 -> 16, of which waited for: 3 -> 3; matrix products, arithmetic and copies ran while one was open for 2% -> 1% of each run, Pallas kernels for 22% -> 25%
where the time goes in v5:
time: 79.3 us; the launch traced here: 78.8 us
  waiting for transfers between devices  27.1 us (34%)
  starting transfers between devices  24.5 us (31%)
  Pallas kernels  22.3 us (28%)
  local copies, waits for them, and re-layouts  2.85 us (4%)
  other arithmetic  1.26 us (2%)
  between operations  0.8 us (1%)
    pallas_call x7, Pallas kernels, call(): pl.pallas_call(functools.partial(kernel, **options), out_shape=tuple(outs...  22.3 us
    ppermute x8, waiting for transfers between devices, swap(): lax.ppermute(values, axis, [(i, i ^ flip) for i in range(lax.axis_size(ax...  15.1 us
    ppermute x8, starting transfers between devices, swap(): lax.ppermute(values, axis, [(i, i ^ flip) for i in range(lax.axis_size(ax...  7.14 us
    ppermute x1, waiting for transfers between devices, on_device(): to_end = lax.ppermute(across, 'outer', outward)  6.47 us
    all_to_all x1, starting transfers between devices, on_device(): lax.all_to_all(mail, ('outer', 'inner'), split_axis=0, concat_axis=0, til...  6.07 us
    ppermute x1, waiting for transfers between devices, on_device(): far = lax.ppermute(near, axes, second)  5.52 us
    ppermute x1, starting transfers between devices, on_device(): near = lax.ppermute(rows_half, axes, first)  3 us
    unnamed x18, local copies, waits for them, and re-layouts  2.85 us
  transfers between devices with their start and end apart: 16, of which 3 were waited for; matrix products, arithmetic and copies ran while one was open for 1% of the time, Pallas kernels for 25%

profile of v5, /device:TPU:0, one launch (start us, length us, event | category | flops | bytes accessed | tf_op | source)
XLA Modules:
  0.0 78.8 jit_solution(5068422777022762380)
XLA Ops:
  0.6 0.0 copy-start.5
  0.6 0.1 pad_add_fusion.place
  0.7 0.0 copy-start.8
  0.7 0.0 copy-start.6
  0.7 0.0 copy-start.7
  0.7 0.6 copy-done.5
  1.3 0.1 copy-done.8
  1.4 0.0 copy-done.6
  1.4 0.0 copy-done.7
  1.4 0.0 copy-start
  1.4 1.1 %copy-done = bf16[512,768]{1,0:T(8,128)(2,1)S(1)} copy-done((bf16[512,768]{1,0:T(8,128)(2,1)S(1)}, bf16[512,768]{1,0:T(8,128)(2,1)}, u32[]{:S(2)}) %copy-start) | copy-done | bytes 786456
  2.6 0.0 copy-start.2
  2.6 1.0 %copy-done.2 = bf16[256,768]{1,0:T(8,128)(2,1)S(1)} copy-done((bf16[256,768]{1,0:T(8,128)(2,1)S(1)}, bf16[256,768]{1,0:T(8,128)(2,1)}, u32[]{:S(2)}) %copy-start.2) | copy-done | bytes 393240
  3.6 2.6 %prep.1 = (bf16[16,24,768]{2,1,0:T(8,128)(2,1)}, bf16[400,768]{1,0:T(8,128)(2,1)}, f32[6,128]{1,0:T(8,128)S(1)}) custom-call(s32[3]{0:T(128)S(1)} %pad_add_fusion.place, bf16[512,768]{1,0:T(8,128)(2,1)S(1)} %copy-done, bf16[256,768]{1,0:T(8,128)(2,1)S(1)} %copy-done.2, s32[1,256]{1,0:T(1,128)S(1)} %bitcast.9, s32[1,512]{1,0:T(1,128)S(1)} %bitcast.8, ...), custom_call_target="tpu_custom_call" | custom-call | flops 1 | bytes 1 | tf_op jit(solution)/shard_map/prep/pallas_call | solution.py:273
  6.2 3.0 %collective-permute-start = (bf16[400,768]{1,0:T(8,128)(2,1)}, bf16[400,768]{1,0:T(8,128)(2,1)S(1)}, u32[]{:S(2)}, u32[]{:S(2)}) collective-permute-start(bf16[400,768]{1,0:T(8,128)(2,1)} %get-tuple-element.15), channel_id=1, source_target_pairs={{0,2},{1,5},{2,0},{3,7},{4,6},{5,1},{6,4},{7,3},{8,10},{9,13},{10,... | collective-permute-start | bytes 1843208 | tf_op jit(solution)/shard_map/ppermute | solution.py:344
  9.2 0.0 copy-start.4
  9.2 0.0 copy-start.1
  9.2 6.1 %all-to-all-start = ((bf16[16,24,768]{2,1,0:T(8,128)(2,1)}), bf16[16,24,768]{2,1,0:T(8,128)(2,1)S(1)}, u32[]{:S(2)}, u32[]{:S(2)}) async-start(bf16[16,24,768]{2,1,0:T(8,128)(2,1)} %get-tuple-element.17), calls=%async_computation | async-start | bytes 1179648 | tf_op jit(solution)/shard_map/all_to_all | solution.py:338
  15.3 0.0 copy-done.4
  15.3 0.0 copy-start.3
  15.3 2.0 %collective-permute-start.1 = (bf16[256,768]{1,0:T(8,128)(2,1)S(1)}, bf16[256,768]{1,0:T(8,128)(2,1)}, u32[]{:S(2)}, u32[]{:S(2)}) collective-permute-start(bf16[256,768]{1,0:T(8,128)(2,1)S(1)} %copy-done.4), channel_id=1, source_target_pairs={{0,8},{8,0},{16,24},{24,16},{1,9},{9,1},{17,25},{25,17},{2,10},{10... | collective-permute-start | bytes 1179656 | tf_op jit(solution)/shard_map/ppermute | solution.py:286
  17.3 1.4 %collective-permute-start.2 = (bf16[256,768]{1,0:T(8,128)(2,1)S(1)}, bf16[256,768]{1,0:T(8,128)(2,1)}, u32[]{:S(2)}, u32[]{:S(2)}) collective-permute-start(bf16[256,768]{1,0:T(8,128)(2,1)S(1)} %copy-done.4), channel_id=1, source_target_pairs={{8,16},{16,8},{9,17},{17,9},{10,18},{18,10},{11,19},{19,11},{12,20... | collective-permute-start | bytes 1179656 | tf_op jit(solution)/shard_map/ppermute | solution.py:348
  18.7 1.5 %collective-permute-start.6 = (bf16[400,768]{1,0:T(8,128)(2,1)}, bf16[400,768]{1,0:T(8,128)(2,1)S(1)}, u32[]{:S(2)}, u32[]{:S(2)}) collective-permute-start(bf16[400,768]{1,0:T(8,128)(2,1)} %get-tuple-element.15), channel_id=1, source_target_pairs={{0,4},{1,3},{2,6},{3,1},{4,0},{5,7},{6,2},{7,5},{8,12},{9,11},{10,... | collective-permute-start | bytes 1843208 | tf_op jit(solution)/shard_map/ppermute | solution.py:345
  20.1 15.1 %collective-permute-done.1.refs_0_ = bf16[256,768]{1,0:T(8,128)(2,1)} collective-permute-done((bf16[256,768]{1,0:T(8,128)(2,1)S(1)}, bf16[256,768]{1,0:T(8,128)(2,1)}, u32[]{:S(2)}, u32[]{:S(2)}) %collective-permute-start.1) | collective-permute-done | bytes 393248 | tf_op jit(solution)/shard_map/ppermute | solution.py:286
  35.2 0.0 collective-permute-done.2.refs_1_
  35.2 0.0 collective-permute-done.refs_6_.refs_7_
  35.2 1.5 %collective-permute-start.3 = (bf16[400,768]{1,0:T(8,128)(2,1)S(1)}, bf16[400,768]{1,0:T(8,128)(2,1)}, u32[]{:S(2)}, u32[]{:S(2)}) collective-permute-start(bf16[400,768]{1,0:T(8,128)(2,1)S(1)} %collective-permute-done.refs_6_.refs_7_), channel_id=1, source_target_pairs={{0,4},{1,3},{2,6},{3,1},{4,0},{5,7},{6,2},{7,5},{8,12},{9,11},{10,... | collective-permute-start | bytes 1843208 | tf_op jit(solution)/shard_map/ppermute | solution.py:352
  36.7 1.4 %collective-permute-start.11 = (bf16[256,768]{1,0:T(8,128)(2,1)}, bf16[256,768]{1,0:T(8,128)(2,1)}, u32[]{:S(2)}, u32[]{:S(2)}) collective-permute-start(bf16[256,768]{1,0:T(8,128)(2,1)} %collective-permute-done.1.refs_0_), channel_id=1, source_target_pairs={{8,16},{16,8},{9,17},{17,9},{10,18},{18,10},{11,19},{19,11},{12,20... | collective-permute-start | bytes 1179656 | tf_op jit(solution)/shard_map/ppermute | solution.py:350
  38.1 1.3 %collective-permute-start.10 = (bf16[256,768]{1,0:T(8,128)(2,1)}, bf16[256,768]{1,0:T(8,128)(2,1)}, u32[]{:S(2)}, u32[]{:S(2)}) collective-permute-start(bf16[256,768]{1,0:T(8,128)(2,1)} %collective-permute-done.2.refs_1_), channel_id=1, source_target_pairs={{8,0},{16,24},{9,1},{17,25},{10,2},{18,26},{11,3},{19,27},{12,4},{... | collective-permute-start | bytes 1179656 | tf_op jit(solution)/shard_map/ppermute | solution.py:351
  39.4 0.1 collective-permute-start.5
  39.5 0.0 collective-permute-done.6.refs_8_.refs_9_
  39.5 0.5 collective-permute-start.7
  40.0 0.0 all-to-all-done.mail.refs_0_
  40.0 5.5 %collective-permute-done.3.refs_10_.refs_11_ = bf16[400,768]{1,0:T(8,128)(2,1)} collective-permute-done((bf16[400,768]{1,0:T(8,128)(2,1)S(1)}, bf16[400,768]{1,0:T(8,128)(2,1)}, u32[]{:S(2)}, u32[]{:S(2)}) %collective-permute-start.3) | collective-permute-done | bytes 614432 | tf_op jit(solution)/shard_map/ppermute | solution.py:352
  45.5 0.0 collective-permute-start.8
  45.5 0.0 collective-permute-done.11.refs_1_
  45.5 1.3 %collective-permute-start.13 = (bf16[256,768]{1,0:T(8,128)(2,1)}, bf16[256,768]{1,0:T(8,128)(2,1)S(1)}, u32[]{:S(2)}, u32[]{:S(2)}) collective-permute-start(bf16[256,768]{1,0:T(8,128)(2,1)} %collective-permute-done.11.refs_1_), channel_id=1, source_target_pairs={{8,0},{16,24},{9,1},{17,25},{10,2},{18,26},{11,3},{19,27},{12,4},{... | collective-permute-start | bytes 1179656 | tf_op jit(solution)/shard_map/ppermute | solution.py:354
  46.8 6.5 %collective-permute-done.10.refs_0_ = bf16[256,768]{1,0:T(8,128)(2,1)} collective-permute-done((bf16[256,768]{1,0:T(8,128)(2,1)}, bf16[256,768]{1,0:T(8,128)(2,1)}, u32[]{:S(2)}, u32[]{:S(2)}) %collective-permute-start.10) | collective-permute-done | bytes 393248 | tf_op jit(solution)/shard_map/ppermute | solution.py:351
  53.3 0.0 collective-permute-start.4
  53.3 4.0 %meta.1 = (f32[4,3072]{1,0:T(4,128)S(1)}, s32[1,3072]{1,0:T(1,128)S(1)}, s32[1,512]{1,0:T(1,128)S(1)}, s32[1,512]{1,0:T(1,128)S(1)}) custom-call(s32[3]{0:T(128)S(1)} %pad_add_fusion.place, bf16[16,24,768]{2,1,0:T(8,128)(2,1)S(1)} %all-to-all-done.mail.refs_0_), custom_call_target="tpu_custom_call" | custom-call | flops 1 | bytes 1 | tf_op jit(solution)/shard_map/meta/pallas_call | solution.py:273
  57.3 0.0 collective-permute-done.5.refs_7_.refs_8_
  57.3 0.0 collective-permute-done.7.refs_9_.refs_10_
  57.3 0.0 collective-permute-done.8.refs_11_.refs_12_
  57.4 0.0 copy-done.1
  57.4 0.0 copy-done.3
  57.4 3.7 %score.5 = f32[2,2,128]{2,1,0:T(2,128)S(1)} custom-call(s32[3]{0:T(128)S(1)} %pad_add_fusion.place, bf16[16,24,768]{2,1,0:T(8,128)(2,1)S(1)} %all-to-all-done.mail.refs_0_, bf16[256,768]{1,0:T(8,128)(2,1)} %collective-permute-done.10.refs_0_, bf16[256,768]{1,0:T(8,128)(2,1)} %collective-permute-done.11.refs_1_, ...), custom_call_target="tpu_custom_call" | custom-call | flops 1 | bytes 1 | tf_op jit(solution)/shard_map/score/pallas_call | solution.py:273
  61.0 1.6 %collective-permute-start.12 = (f32[2,2,128]{2,1,0:T(2,128)S(1)}, f32[2,2,128]{2,1,0:T(2,128)S(1)}, u32[]{:S(2)}, u32[]{:S(2)}) collective-permute-start(f32[2,2,128]{2,1,0:T(2,128)S(1)} %score.5), channel_id=1, source_target_pairs={{0,16},{8,24},{16,0},{24,8},{1,17},{9,25},{17,1},{25,9},{2,18},{10... | collective-permute-start | bytes 6152 | tf_op jit(solution)/shard_map/ppermute | solution.py:286
  62.7 3.5 %score.4 = f32[2,2,128]{2,1,0:T(2,128)S(1)} custom-call(s32[3]{0:T(128)S(1)} %pad_add_fusion.place, bf16[16,24,768]{2,1,0:T(8,128)(2,1)S(1)} %all-to-all-done.mail.refs_0_, bf16[256,768]{1,0:T(8,128)(2,1)} %collective-permute-done.1.refs_0_, f32[4,3072]{1,0:T(4,128)S(1)} %get-tuple-element.22.refs_1_.refs_2_, ...), custom_call_target="tpu_custom_call" | custom-call | flops 1 | bytes 1 | tf_op jit(solution)/shard_map/score/pallas_call | solution.py:273
  66.2 1.5 %collective-permute-start.9 = (f32[2,2,128]{2,1,0:T(2,128)S(1)}, f32[2,2,128]{2,1,0:T(2,128)S(1)}, u32[]{:S(2)}, u32[]{:S(2)}) collective-permute-start(f32[2,2,128]{2,1,0:T(2,128)S(1)} %score.4), channel_id=1, source_target_pairs={{0,8},{8,0},{16,24},{24,16},{1,9},{9,1},{17,25},{25,17},{2,10},{10... | collective-permute-start | bytes 6152 | tf_op jit(solution)/shard_map/ppermute | solution.py:286
  67.7 0.0 collective-permute-done.13.refs_0_
  67.7 3.5 %score.6 = f32[2,2,128]{2,1,0:T(2,128)S(1)} custom-call(s32[3]{0:T(128)S(1)} %pad_add_fusion.place, bf16[16,24,768]{2,1,0:T(8,128)(2,1)S(1)} %all-to-all-done.mail.refs_0_, bf16[256,768]{1,0:T(8,128)(2,1)S(1)} %collective-permute-done.13.refs_0_, bf16[256,768]{1,0:T(8,128)(2,1)} %collective-permute-done.2.refs_1_, ...), custom_call_target="tpu_custom_call" | custom-call | flops 1 | bytes 1 | tf_op jit(solution)/shard_map/score/pallas_call | solution.py:273
  71.3 1.4 %collective-permute-start.14 = (f32[2,2,128]{2,1,0:T(2,128)S(1)}, f32[2,2,128]{2,1,0:T(2,128)S(1)}, u32[]{:S(2)}, u32[]{:S(2)}) collective-permute-start(f32[2,2,128]{2,1,0:T(2,128)S(1)} %score.6), channel_id=1, source_target_pairs={{0,24},{8,16},{16,8},{24,0},{1,25},{9,17},{17,9},{25,1},{2,26},{10... | collective-permute-start | bytes 6152 | tf_op jit(solution)/shard_map/ppermute | solution.py:286
  72.7 0.6 broadcast_select_fusion
  73.3 0.0 collective-permute-done.4.refs_1_
  73.3 1.5 %apply.1 = bf16[512,768]{1,0:T(8,128)(2,1)} custom-call(s32[1,512]{1,0:T(1,128)S(1)} %get-tuple-element.19.target, bf16[512,768]{1,0:T(8,128)(2,1)S(1)} %copy-done.1, bf16[16,24,768]{2,1,0:T(8,128)(2,1)S(1)} %all-to-all-done.mail.refs_0_, bf16[16,24,768]{2,1,0:T(8,128)(2,1)S(1)} %collective-permute-done.4.refs_1_), custom_call_target="tpu_custom_call" | custom-call | flops 1 | bytes 1 | tf_op jit(solution)/shard_map/apply/pallas_call | solution.py:273
  74.8 3.4 %score.7 = f32[2,2,128]{2,1,0:T(2,128)S(1)} custom-call(s32[3]{0:T(128)S(1)} %pad_add_fusion.place, bf16[16,24,768]{2,1,0:T(8,128)(2,1)S(1)} %all-to-all-done.mail.refs_0_, bf16[256,768]{1,0:T(8,128)(2,1)S(1)} %copy-done.4, f32[4,3072]{1,0:T(4,128)S(1)} %get-tuple-element.22.refs_1_.refs_2_, s32[1,3072]{1,0:T(1,128)S(1)} %get-tuple-element.23.refs_2_.refs_3_, ...), custom_call_target="tpu_custom_call" | custom-call | flops 1 | bytes 1 | tf_op jit(solution)/shard_map/score/pallas_call | solution.py:273
  78.2 0.0 collective-permute-done.12
  78.2 0.0 collective-permute-done.9
  78.2 0.0 collective-permute-done.14
  78.2 0.6 fusion.1
  (2 shorter events, 0.0 us)
Async XLA Ops:
  0.6 0.7 copy-start.5
  0.7 0.7 copy-start.8
  0.7 0.7 copy-start.6
  0.7 0.7 copy-start.7
  1.4 1.1 %copy-start = (bf16[512,768]{1,0:T(8,128)(2,1)S(1)}, bf16[512,768]{1,0:T(8,128)(2,1)}, u32[]{:S(2)}) copy-start(bf16[512,768]{1,0:T(8,128)(2,1)} %refs_4_.3) | copy-start | bytes 2359300
  2.6 1.0 %copy-start.2 = (bf16[256,768]{1,0:T(8,128)(2,1)S(1)}, bf16[256,768]{1,0:T(8,128)(2,1)}, u32[]{:S(2)}) copy-start(bf16[256,768]{1,0:T(8,128)(2,1)} %refs_5_.7) | copy-start | bytes 1179652
  6.2 29.1 %collective-permute-start = (bf16[400,768]{1,0:T(8,128)(2,1)}, bf16[400,768]{1,0:T(8,128)(2,1)S(1)}, u32[]{:S(2)}, u32[]{:S(2)}) collective-permute-start(bf16[400,768]{1,0:T(8,128)(2,1)} %get-tuple-element.15), channel_id=1, source_target_pairs={{0,2},{1,5},{2,0},{3,7},{4,6},{5,1},{6,4},{7,3},{8,10},{9,13},{10,... | collective-permute-start | bytes 1843208 | tf_op jit(solution)/shard_map/ppermute | solution.py:344
  9.2 6.1 %copy-start.4 = (bf16[256,768]{1,0:T(8,128)(2,1)S(1)}, bf16[256,768]{1,0:T(8,128)(2,1)}, u32[]{:S(2)}) copy-start(bf16[256,768]{1,0:T(8,128)(2,1)} %refs_0_.1) | copy-start | bytes 1179652
  9.2 48.2 %copy-start.1 = (bf16[512,768]{1,0:T(8,128)(2,1)S(1)}, bf16[512,768]{1,0:T(8,128)(2,1)}, u32[]{:S(2)}) copy-start(bf16[512,768]{1,0:T(8,128)(2,1)} %refs_4_.3) | copy-start | bytes 2359300
  9.2 30.8 %all-to-all-start = ((bf16[16,24,768]{2,1,0:T(8,128)(2,1)}), bf16[16,24,768]{2,1,0:T(8,128)(2,1)S(1)}, u32[]{:S(2)}, u32[]{:S(2)}) async-start(bf16[16,24,768]{2,1,0:T(8,128)(2,1)} %get-tuple-element.17), calls=%async_computation | async-start | bytes 1179648 | tf_op jit(solution)/shard_map/all_to_all | solution.py:338
  15.3 42.1 %copy-start.3 = (bf16[256,768]{1,0:T(8,128)(2,1)S(1)}, bf16[256,768]{1,0:T(8,128)(2,1)}, u32[]{:S(2)}) copy-start(bf16[256,768]{1,0:T(8,128)(2,1)} %refs_5_.7) | copy-start | bytes 1179652
  15.3 20.0 %collective-permute-start.1 = (bf16[256,768]{1,0:T(8,128)(2,1)S(1)}, bf16[256,768]{1,0:T(8,128)(2,1)}, u32[]{:S(2)}, u32[]{:S(2)}) collective-permute-start(bf16[256,768]{1,0:T(8,128)(2,1)S(1)} %copy-done.4), channel_id=1, source_target_pairs={{0,8},{8,0},{16,24},{24,16},{1,9},{9,1},{17,25},{25,17},{2,10},{10... | collective-permute-start | bytes 1179656 | tf_op jit(solution)/shard_map/ppermute | solution.py:286
  17.3 18.0 %collective-permute-start.2 = (bf16[256,768]{1,0:T(8,128)(2,1)S(1)}, bf16[256,768]{1,0:T(8,128)(2,1)}, u32[]{:S(2)}, u32[]{:S(2)}) collective-permute-start(bf16[256,768]{1,0:T(8,128)(2,1)S(1)} %copy-done.4), channel_id=1, source_target_pairs={{8,16},{16,8},{9,17},{17,9},{10,18},{18,10},{11,19},{19,11},{12,20... | collective-permute-start | bytes 1179656 | tf_op jit(solution)/shard_map/ppermute | solution.py:348
  18.7 20.8 %collective-permute-start.6 = (bf16[400,768]{1,0:T(8,128)(2,1)}, bf16[400,768]{1,0:T(8,128)(2,1)S(1)}, u32[]{:S(2)}, u32[]{:S(2)}) collective-permute-start(bf16[400,768]{1,0:T(8,128)(2,1)} %get-tuple-element.15), channel_id=1, source_target_pairs={{0,4},{1,3},{2,6},{3,1},{4,0},{5,7},{6,2},{7,5},{8,12},{9,11},{10,... | collective-permute-start | bytes 1843208 | tf_op jit(solution)/shard_map/ppermute | solution.py:345
  35.2 10.3 %collective-permute-start.3 = (bf16[400,768]{1,0:T(8,128)(2,1)S(1)}, bf16[400,768]{1,0:T(8,128)(2,1)}, u32[]{:S(2)}, u32[]{:S(2)}) collective-permute-start(bf16[400,768]{1,0:T(8,128)(2,1)S(1)} %collective-permute-done.refs_6_.refs_7_), channel_id=1, source_target_pairs={{0,4},{1,3},{2,6},{3,1},{4,0},{5,7},{6,2},{7,5},{8,12},{9,11},{10,... | collective-permute-start | bytes 1843208 | tf_op jit(solution)/shard_map/ppermute | solution.py:352
  36.7 8.8 %collective-permute-start.11 = (bf16[256,768]{1,0:T(8,128)(2,1)}, bf16[256,768]{1,0:T(8,128)(2,1)}, u32[]{:S(2)}, u32[]{:S(2)}) collective-permute-start(bf16[256,768]{1,0:T(8,128)(2,1)} %collective-permute-done.1.refs_0_), channel_id=1, source_target_pairs={{8,16},{16,8},{9,17},{17,9},{10,18},{18,10},{11,19},{19,11},{12,20... | collective-permute-start | bytes 1179656 | tf_op jit(solution)/shard_map/ppermute | solution.py:350
  38.1 15.2 %collective-permute-start.10 = (bf16[256,768]{1,0:T(8,128)(2,1)}, bf16[256,768]{1,0:T(8,128)(2,1)}, u32[]{:S(2)}, u32[]{:S(2)}) collective-permute-start(bf16[256,768]{1,0:T(8,128)(2,1)} %collective-permute-done.2.refs_1_), channel_id=1, source_target_pairs={{8,0},{16,24},{9,1},{17,25},{10,2},{18,26},{11,3},{19,27},{12,4},{... | collective-permute-start | bytes 1179656 | tf_op jit(solution)/shard_map/ppermute | solution.py:351
  39.4 17.9 %collective-permute-start.5 = (bf16[400,768]{1,0:T(8,128)(2,1)S(1)}, bf16[400,768]{1,0:T(8,128)(2,1)}, u32[]{:S(2)}, u32[]{:S(2)}) collective-permute-start(bf16[400,768]{1,0:T(8,128)(2,1)S(1)} %collective-permute-done.refs_6_.refs_7_), channel_id=1, source_target_pairs={{0,1},{1,0},{2,3},{3,2},{4,5},{5,4},{6,7},{7,6},{8,9},{9,8},{10,11... | collective-permute-start | bytes 1843208 | tf_op jit(solution)/shard_map/ppermute | solution.py:286
  39.5 17.9 %collective-permute-start.7 = (bf16[400,768]{1,0:T(8,128)(2,1)S(1)}, bf16[400,768]{1,0:T(8,128)(2,1)}, u32[]{:S(2)}, u32[]{:S(2)}) collective-permute-start(bf16[400,768]{1,0:T(8,128)(2,1)S(1)} %collective-permute-done.6.refs_8_.refs_9_), channel_id=1, source_target_pairs={{0,1},{1,0},{2,3},{3,2},{4,5},{5,4},{6,7},{7,6},{8,9},{9,8},{10,11... | collective-permute-start | bytes 1843208 | tf_op jit(solution)/shard_map/ppermute | solution.py:286
  45.5 11.8 %collective-permute-start.8 = (bf16[400,768]{1,0:T(8,128)(2,1)}, bf16[400,768]{1,0:T(8,128)(2,1)S(1)}, u32[]{:S(2)}, u32[]{:S(2)}) collective-permute-start(bf16[400,768]{1,0:T(8,128)(2,1)} %collective-permute-done.3.refs_10_.refs_11_), channel_id=1, source_target_pairs={{0,1},{1,0},{2,3},{3,2},{4,5},{5,4},{6,7},{7,6},{8,9},{9,8},{10,11... | collective-permute-start | bytes 1843208 | tf_op jit(solution)/shard_map/ppermute | solution.py:286
  45.5 22.2 %collective-permute-start.13 = (bf16[256,768]{1,0:T(8,128)(2,1)}, bf16[256,768]{1,0:T(8,128)(2,1)S(1)}, u32[]{:S(2)}, u32[]{:S(2)}) collective-permute-start(bf16[256,768]{1,0:T(8,128)(2,1)} %collective-permute-done.11.refs_1_), channel_id=1, source_target_pairs={{8,0},{16,24},{9,1},{17,25},{10,2},{18,26},{11,3},{19,27},{12,4},{... | collective-permute-start | bytes 1179656 | tf_op jit(solution)/shard_map/ppermute | solution.py:354
  53.3 20.0 %collective-permute-start.4 = (bf16[16,24,768]{2,1,0:T(8,128)(2,1)S(1)}, bf16[16,24,768]{2,1,0:T(8,128)(2,1)S(1)}, u32[]{:S(2)}, u32[]{:S(2)}) collective-permute-start(bf16[16,24,768]{2,1,0:T(8,128)(2,1)S(1)} %all-to-all-done.mail.refs_0_), channel_id=1, source_target_pairs={{0,1},{1,0},{2,3},{3,2},{4,5},{5,4},{6,7},{7,6},{8,9},{9,8},{10,11... | collective-permute-start | bytes 1769480 | tf_op jit(solution)/shard_map/ppermute | solution.py:286
  61.0 17.1 %collective-permute-start.12 = (f32[2,2,128]{2,1,0:T(2,128)S(1)}, f32[2,2,128]{2,1,0:T(2,128)S(1)}, u32[]{:S(2)}, u32[]{:S(2)}) collective-permute-start(f32[2,2,128]{2,1,0:T(2,128)S(1)} %score.5), channel_id=1, source_target_pairs={{0,16},{8,24},{16,0},{24,8},{1,17},{9,25},{17,1},{25,9},{2,18},{10... | collective-permute-start | bytes 6152 | tf_op jit(solution)/shard_map/ppermute | solution.py:286
  66.2 12.0 %collective-permute-start.9 = (f32[2,2,128]{2,1,0:T(2,128)S(1)}, f32[2,2,128]{2,1,0:T(2,128)S(1)}, u32[]{:S(2)}, u32[]{:S(2)}) collective-permute-start(f32[2,2,128]{2,1,0:T(2,128)S(1)} %score.4), channel_id=1, source_target_pairs={{0,8},{8,0},{16,24},{24,16},{1,9},{9,1},{17,25},{25,17},{2,10},{10... | collective-permute-start | bytes 6152 | tf_op jit(solution)/shard_map/ppermute | solution.py:286
  71.3 7.0 %collective-permute-start.14 = (f32[2,2,128]{2,1,0:T(2,128)S(1)}, f32[2,2,128]{2,1,0:T(2,128)S(1)}, u32[]{:S(2)}, u32[]{:S(2)}) collective-permute-start(f32[2,2,128]{2,1,0:T(2,128)S(1)} %score.6), channel_id=1, source_target_pairs={{0,24},{8,16},{16,8},{24,0},{1,25},{9,17},{17,9},{25,1},{2,26},{10... | collective-permute-start | bytes 6152 | tf_op jit(solution)/shard_map/ppermute | solution.py:286

commit v6 on v5

v6 whole, which is shorter than its diff:
```python
import functools
import math

import jax
import jax.numpy as jnp
from jax import lax
from jax.experimental import pallas as pl
from jax.experimental.pallas import tpu as pltpu
from jax.sharding import Mesh, PartitionSpec as P

score_scale = 20.0
age_scale = 16.0
epsilon = 1e-06
LOG2E = math.log2(math.e)
MASKED = -1e30
VMEM_LIMIT = 48 * 1024 * 1024
LANES = 128

NT = (((1,), (1,)), ((), ()))
NN = (((1,), (0,)), ((), ()))


def one_hot(ids, count):
    rows = lax.broadcasted_iota(jnp.int32, (count, ids.shape[1]), 0)
    return jnp.where(rows == ids, 1.0, 0.0).astype(jnp.bfloat16)


def split_terms(values):
    terms = []
    for _ in range(3):
        terms.append(values.astype(jnp.bfloat16))
        values = values - terms[-1].astype(jnp.float32)
    return terms


def counted(hits):
    count = hits.shape[1]
    before = lax.broadcasted_iota(jnp.int32, (count, count), 0)
    after = lax.broadcasted_iota(jnp.int32, (count, count), 1)
    earlier = jnp.where(before < after, 1.0, 0.0).astype(jnp.bfloat16)
    return lax.dot_general(hits.astype(jnp.bfloat16), earlier, NN, preferred_element_type=jnp.float32)


def small(values):
    return values.astype(jnp.float32).astype(jnp.bfloat16)


def prep_kernel(place, table, fresh, rows_out, scale_out, *, replicas, encode):
    core = place[2]
    width = table.shape[1]
    line, row = 0, 0
    halves = []
    for source in (table, fresh):
        rows = source.shape[0]
        half = rows // replicas
        rows_out[row : row + half, :] = source[pl.ds(pl.multiple_of(core * half, half), half), :]
        row += half
        for block in range(rows // LANES):
            squares = jnp.zeros((LANES, LANES), jnp.float32)
            for chunk in range(width // LANES):
                values = source[block * LANES : (block + 1) * LANES, chunk * LANES : (chunk + 1) * LANES]
                values = values.astype(jnp.float32)
                squares += values * values
            mean = jnp.sum(squares.T, axis=0, keepdims=True) / width
            scale_out[line + block : line + block + 1, :] = lax.rsqrt(mean + epsilon) * (score_scale / width * LOG2E)
        if encode:
            halves += [(line, i, half // LANES) for i in range(half // LANES)]
        line += rows // LANES
    if encode:
        rows_out[row:, :] = jnp.zeros((16, width), jnp.bfloat16)
        terms = []
        for first, i, count in halves:
            terms += split_terms(scale_out[pl.ds(first + core * count + i, 1), :])
        for i, term in enumerate(terms):
            rows_out[row + i : row + i + 1, :LANES] = term


def meta_kernel(place, *refs, planes, owners_plane, sizes, cap, replicas):
    outer, inner, core = place[0], place[1], place[2]
    lines, sides = refs[:planes], refs[planes : planes + owners_plane]
    lw_out, row_out, code_out, own_target_out, target_out, own_out = refs[planes + owners_plane :]
    refresh_dev, rows_dev, list_size = sizes
    share = cap // replicas
    plane_rows = owners_plane * rows_dev
    high_count = planes * plane_rows // LANES
    own_owner = outer * owners_plane + inner

    def one_hots(ids):
        return one_hot(ids >> 7, high_count), one_hot(ids & 127, LANES)

    def bitmap(ids):
        high, low = one_hots(ids)
        return lax.dot_general(low, high, NT, preferred_element_type=jnp.float32)

    def lookup(one_map, pair):
        hit = lax.dot_general(one_map.astype(jnp.bfloat16), pair[0], NN, preferred_element_type=jnp.float32)
        return jnp.sum(hit * pair[1].astype(jnp.float32), axis=0, keepdims=True) > 0.5

    def ref_ids(plane, side):
        return sides[side][:, plane * refresh_dev : (plane + 1) * refresh_dev]

    all_refs = planes * refresh_dev
    plane_ids = jnp.concatenate([ref_ids(0, side) for side in range(owners_plane)], axis=1)
    refreshed_map = bitmap(jnp.concatenate([side[:, :all_refs] for side in sides], axis=1))
    column = lax.broadcasted_iota(jnp.int32, (1, plane_rows), 1)
    table_ids = (outer * owners_plane + (inner ^ (column // rows_dev))) * rows_dev + column % rows_dev
    table_hots, fresh_hots = one_hots(table_ids), one_hots(plane_ids)

    ages = jnp.concatenate([side[:, all_refs:] for side in sides], axis=1).astype(jnp.float32)
    weight = jnp.exp(-ages / age_scale).astype(jnp.bfloat16).astype(jnp.float32)
    refreshed = lookup(refreshed_map, table_hots)
    row_out[:, :plane_rows] = jnp.where(refreshed, -1, table_ids).astype(jnp.float32)
    row_out[:, plane_rows:] = plane_ids.astype(jnp.float32)
    own_out[...] = refreshed[:, :rows_dev].astype(jnp.int32)
    log_weight = jnp.where(refreshed, MASKED, jnp.log2(weight))
    for group in range(planes):
        one_map = bitmap(lines[group][:, refresh_dev : refresh_dev + list_size])
        lw_out[group : group + 1, :plane_rows] = jnp.where(lookup(one_map, table_hots), log_weight, MASKED)
        lw_out[group : group + 1, plane_rows:] = jnp.where(lookup(one_map, fresh_hots), 0.0, MASKED)

    pairs = [(plane, side) for plane in range(planes) for side in range(owners_plane)]
    sent_owner = [ref_ids(0, side) // rows_dev - ((outer ^ plane) * owners_plane + inner) for plane, side in pairs]
    taken_owner = [ref_ids(plane, side) // rows_dev - own_owner for plane, side in pairs]
    match = jnp.concatenate(sent_owner + taken_owner, axis=0) == 0
    rank = counted(jnp.where(match, 1.0, 0.0)).astype(jnp.int32)
    rank = jnp.where(match, rank, -cap)
    own_target_out[...] = plane_ids - own_owner * rows_dev
    for i, (plane, side) in enumerate(pairs):
        if plane == 0:
            code_out[:, side * refresh_dev : (side + 1) * refresh_dev] = jnp.full((1, refresh_dev), -1, jnp.int32)
            continue
        base = ((plane - 1) * owners_plane + side) * share
        sent_rank = rank[i : i + 1, :] - core * share
        columns = slice(side * refresh_dev, (side + 1) * refresh_dev)
        here = (sent_rank >= 0) & (sent_rank < share)
        code_out[:, columns] = jnp.where(here, base + sent_rank, code_out[:, columns])
        take_rank = rank[len(pairs) + i : len(pairs) + i + 1, :]
        slot = jnp.where(take_rank < 0, -1, ((take_rank // share) ^ core) * share + take_rank % share)
        row = jnp.where(take_rank < 0, 0, ref_ids(plane, side) - own_owner * rows_dev)
        kinds = lax.broadcasted_iota(jnp.int32, (8, refresh_dev), 0)
        digits = jnp.where(kinds == 0, row // 16, jnp.where(kinds == 1, row % 16, 1))
        found = lax.dot_general(small(digits), one_hot(slot, cap), NT, preferred_element_type=jnp.float32)
        found = found.astype(jnp.int32)
        target = jnp.where(found[2:3, :] > 0, found[0:1, :] * 16 + found[1:2, :], -1)
        for part in range(replicas):
            first = part * (planes - 1) * owners_plane * share + base
            target_out[:, first : first + share] = target[:, part * share : (part + 1) * share]


def piece_offset(place, piece):
    column, size, flip, by_core = piece
    if flip is None:
        return column
    column += (place[2] ^ flip) * size
    if by_core is not None:
        column += (place[2] ^ by_core) * size * 2
    return pl.multiple_of(column, size)


def pack_kernel(place, code, scale, *refs, pieces, all_pieces):
    *buffers, out, scale_out = refs
    total = jnp.zeros(out.shape, jnp.float32)
    for source, start, size, column, _ in pieces:
        select = one_hot(code[:, pl.ds(piece_offset(place, column), size)], out.shape[0])
        total += lax.dot_general(select, buffers[source][start : start + size, :], NN, preferred_element_type=jnp.float32)
    out[...] = total.astype(jnp.bfloat16)
    for source, start, size, column, scale_at in all_pieces:
        first = piece_offset(place, column)
        for chunk in range(size // LANES):
            if scale_at < 0:
                line = -1 - scale_at + chunk
                row = scale[line : line + 1, :]
            else:
                line = scale_at + 3 * chunk
                row = jnp.sum(buffers[source][line : line + 3, :LANES].astype(jnp.float32), axis=0, keepdims=True)
            scale_out[:, pl.ds(first + chunk * LANES, LANES)] = row


def apply_kernel(place, own_target, target, table, *refs, pieces, arrivals):
    out = refs[-1]
    buffers, arrived = refs[: -1 - arrivals], refs[-1 - arrivals : -1]
    parts = [
        (own_target[:, pl.ds(piece_offset(place, column), size)], buffers[source][start : start + size, :])
        for source, start, size, column, _ in pieces
    ]
    first = 0
    for block in arrived:
        parts.append((target[:, first : first + block.shape[0]], block[...]))
        first += block.shape[0]
    fresh = jnp.zeros(out.shape, jnp.float32)
    hit = jnp.zeros((out.shape[0], 1), jnp.float32)
    for to_row, values in parts:
        rows = lax.broadcasted_iota(jnp.int32, (out.shape[0], to_row.shape[1]), 0)
        chosen = jnp.where(rows == to_row, 1.0, 0.0)
        hit += jnp.sum(chosen, axis=1, keepdims=True)
        fresh += lax.dot_general(chosen.astype(jnp.bfloat16), values, NN, preferred_element_type=jnp.float32)
    out[...] = jnp.where(hit > 0.5, fresh, table[...].astype(jnp.float32)).astype(jnp.bfloat16)


def to_lanes(row):
    return jnp.broadcast_to(row, (LANES, LANES)).T


def score_kernel(place, positive, *refs, pieces, flip, given):
    out, total, pos_total, q_scale, pos_b, chosen = refs[-6:]
    queries = refs[0]
    if given == 2:
        at_end = (place[0] == 0) | (place[0] == 3)
        chosen[...] = jnp.where(at_end, refs[0][...], refs[1][...])
        queries = chosen
    log_weight, row_ids, scale, *refs = refs[given:-6]
    count, width = queries.shape
    for block in range(count // LANES):
        part = slice(block * LANES, (block + 1) * LANES)
        values = queries[part, :].astype(jnp.float32)
        squares = jnp.sum(values * values, axis=1, keepdims=True)
        q_scale[part, :] = jnp.broadcast_to(lax.rsqrt(squares / width + epsilon), (LANES, LANES))
        pos_b[part, :] = to_lanes(positive[:, part].astype(jnp.float32))
    total[...] = jnp.zeros_like(total)
    pos_total[...] = jnp.zeros_like(pos_total)
    for source, start, size, column, _ in pieces:
        first = piece_offset(place, column)
        raw = lax.dot_general(
            queries[...], refs[source][start : start + size, :], NT, preferred_element_type=jnp.float32
        )
        for top in range(0, count, 64):
            part = slice(top, top + 64)
            sums, positives = total[part, :], pos_total[part, :]
            for chunk in range(size // LANES):
                cols = pl.ds(first + chunk * LANES, LANES)
                powers = raw[part, chunk * LANES : (chunk + 1) * LANES] * q_scale[part, :]
                powers = powers * scale[:, cols] + log_weight[flip : flip + 1, cols]
                sums = sums + jnp.exp2(powers)
                positives = positives + jnp.where(pos_b[part, :] == row_ids[:, cols], powers, 0.0)
            total[part, :] = sums
            pos_total[part, :] = positives
    for block in range(count // LANES):
        part = slice(block * LANES, (block + 1) * LANES)
        out[0, block : block + 1, :] = jnp.sum(total[part, :].T, axis=0, keepdims=True)
        out[1, block : block + 1, :] = jnp.sum(pos_total[part, :].T, axis=0, keepdims=True)


def whole(memory=pltpu.VMEM):
    return pl.BlockSpec(memory_space=memory)


def call(kernel, name, outs, place, *operands, scratch=(), **options):
    specs = [whole()] * len(operands)
    if place is not None:
        specs = [whole(pltpu.SMEM)] + specs
        operands = (place, *operands)
    return pl.pallas_call(
        functools.partial(kernel, **options),
        out_shape=tuple(outs),
        in_specs=specs,
        out_specs=tuple(whole() for _ in outs),
        scratch_shapes=list(scratch),
        compiler_params=pltpu.CompilerParams(vmem_limit_bytes=VMEM_LIMIT),
        cost_estimate=pl.CostEstimate(flops=1, bytes_accessed=1, transcendentals=0),
        name=name,
    )(*operands)


def swap(values, axis, flip):
    return lax.ppermute(values, axis, [(i, i ^ flip) for i in range(lax.axis_size(axis))])


def on_device(table, ages, refresh_ids, fresh_rows, neg_ids, queries, pos_ids):
    rows_dev, width = table.shape
    refresh_dev = refresh_ids.shape[0]
    planes = lax.axis_size("outer")
    owners_plane = lax.axis_size("inner")
    replicas = lax.axis_size("query")
    owners = planes * owners_plane
    query_count = queries.shape[0]
    list_size = neg_ids.shape[1]
    place = jnp.stack([lax.axis_index(name) for name in ("outer", "inner", "query")]).astype(jnp.int32)
    plane_rows = owners_plane * rows_dev
    plane_refresh = owners_plane * refresh_dev
    all_rows = plane_rows + plane_refresh
    cap = max(2, (2 * refresh_dev + owners - 1) // owners)
    share = cap // replicas
    table_half, fresh_half = rows_dev // replicas, refresh_dev // replicas
    bf16, f32 = jnp.bfloat16, jnp.float32

    line = jnp.concatenate([refresh_ids, neg_ids[0], pos_ids])
    lines = [line] + [swap(line, "outer", s) for s in range(1, planes)]
    side = jnp.concatenate([one[:refresh_dev] for one in lines] + [ages])
    sides = [side] + [swap(side, "inner", s) for s in range(1, owners_plane)]
    positive = [one[refresh_dev + list_size :].reshape(1, -1) for one in lines]

    fast = replicas == 2 and owners_plane == 4 and planes == 4
    extra = 16 if fast else 0
    rows_half, scales = call(
        prep_kernel,
        "prep",
        [
            jax.ShapeDtypeStruct((table_half + fresh_half + extra, width), bf16),
            jax.ShapeDtypeStruct(((rows_dev + refresh_dev) // LANES, LANES), f32),
        ],
        place,
        table,
        fresh_rows,
        replicas=replicas,
        encode=fast,
    )
    rows_half, *sides = lax.optimization_barrier((rows_half, *sides))

    others = (planes - 1) * owners_plane
    lw, row_ids, code, own_target, target, own = call(
        meta_kernel,
        "meta",
        [
            jax.ShapeDtypeStruct((planes, all_rows), f32),
            jax.ShapeDtypeStruct((1, all_rows), f32),
            jax.ShapeDtypeStruct((1, plane_refresh), jnp.int32),
            jax.ShapeDtypeStruct((1, plane_refresh), jnp.int32),
            jax.ShapeDtypeStruct((1, others * cap), jnp.int32),
            jax.ShapeDtypeStruct((1, rows_dev), jnp.int32),
        ],
        place,
        *[one.reshape(1, -1) for one in lines],
        *[one.reshape(1, -1) for one in sides],
        planes=planes,
        owners_plane=owners_plane,
        sizes=(refresh_dev, rows_dev, list_size),
        cap=cap,
        replicas=replicas,
    )
    new_ages = jnp.where(own.reshape(rows_dev) > 0, 0, ages)

    if fast:
        axes = ("inner", "query")
        first = [(2 * i + c, 2 * (i ^ (1 + c)) + c) for i in range(4) for c in range(2)]
        second = [(2 * i + c, 2 * (i ^ (2 - c)) + c) for i in range(4) for c in range(2)]
        near = lax.ppermute(rows_half, axes, first)
        side = lax.ppermute(rows_half, axes, second)
        middle, outward = [(1, 2), (2, 1)], [(1, 0), (2, 3)]
        beside = swap(queries, "outer", 1)
        across = lax.ppermute(queries, "outer", middle)
        near, beside, across, lw = lax.optimization_barrier((near, beside, across, lw))
        from_end = lax.ppermute(beside, "outer", middle)
        to_end = lax.ppermute(across, "outer", outward)
        far = lax.ppermute(near, axes, second)
        far, from_end, to_end = lax.optimization_barrier((far, from_end, to_end))
        last = lax.ppermute(from_end, "outer", outward)
        got_queries = [(queries,), (beside,), (to_end, from_end), (last, across)]
        buffers = [table, fresh_rows]
        table_pieces = [(0, 0, rows_dev, (0, rows_dev, None, None), -1)]
        fresh_pieces = [(1, 0, refresh_dev, (0, refresh_dev, None, None), -1 - rows_dev // LANES)]
        for slot, by_core, mine in ((1, 0, near), (1, 1, side), (3, None, far)):
            for flip, rows in enumerate((mine, swap(mine, "query", 1))):
                by = None if by_core is None else by_core ^ flip
                data = table_half + fresh_half
                fresh_at = data + 3 * (table_half // LANES)
                table_pieces.append((len(buffers), 0, table_half, (slot * rows_dev, table_half, flip, by), data))
                fresh_pieces.append(
                    (len(buffers), table_half, fresh_half, (slot * refresh_dev, fresh_half, flip, by), fresh_at)
                )
                buffers.append(rows)
    else:
        got_queries = [(queries,)] + [(swap(queries, "outer", s),) for s in range(1, planes)]
        got_rows = [rows_half] + [swap(rows_half, "inner", s) for s in range(1, owners_plane)]
        gathered = lax.all_gather(jnp.stack(got_rows), "query", axis=0)
        gathered = jnp.swapaxes(gathered, 0, 1)
        buffers = [
            gathered[:, :, :table_half].reshape(plane_rows, width),
            gathered[:, :, table_half:].reshape(plane_refresh, width),
        ]
        scales = []
        for rows in buffers:
            values = rows.astype(f32)
            mean = jnp.sum(values * values, axis=1) / width
            scales.append((lax.rsqrt(mean + epsilon) * (score_scale / width * LOG2E)).reshape(-1, LANES))
        scales = jnp.concatenate(scales)

        def blocks(buffer, count, line):
            starts = range(0, count, 512)
            return [(buffer, i, 512, (i, 512, None, None), -1 - line - i // LANES) for i in starts]

        table_pieces = blocks(0, plane_rows, 0)
        fresh_pieces = blocks(1, plane_refresh, plane_rows // LANES)

    def shift(pieces, columns):
        return [(a, b, c, (d[0] + columns, *d[1:]), e) for a, b, c, d, e in pieces]

    pieces = table_pieces + shift(fresh_pieces, plane_rows)
    packed, scale_plane = call(
        pack_kernel,
        "pack",
        [jax.ShapeDtypeStruct((others * share, width), bf16), jax.ShapeDtypeStruct((1, all_rows), f32)],
        place,
        code,
        scales,
        *buffers,
        pieces=fresh_pieces,
        all_pieces=pieces,
    )
    size = owners_plane * share
    came = jnp.concatenate([swap(packed[(s - 1) * size : s * size], "outer", s) for s in range(1, planes)])
    arrived = [came] + [swap(came, "query", flip) for flip in range(1, replicas)]
    mine = None
    for s in [*range(1, planes), 0]:
        (partial,) = call(
            score_kernel,
            "score",
            [jax.ShapeDtypeStruct((2, query_count // LANES, LANES), f32)],
            place,
            positive[s],
            *got_queries[s],
            lw,
            row_ids,
            scale_plane,
            *buffers,
            scratch=[pltpu.VMEM((query_count, LANES), f32)] * 4 + [pltpu.VMEM(queries.shape, bf16)],
            pieces=pieces,
            flip=s,
            given=len(got_queries[s]),
        )
        if s:
            partial = swap(partial, "outer", s)
        mine = partial if mine is None else mine + partial
    (new_table,) = call(
        apply_kernel,
        "apply",
        [jax.ShapeDtypeStruct(table.shape, bf16)],
        place,
        own_target,
        target,
        table,
        *buffers,
        *arrived,
        pieces=fresh_pieces,
        arrivals=len(arrived),
    )
    loss = (jnp.log2(mine[0]) - mine[1]) * math.log(2.0)
    return new_table, new_ages, loss.reshape(query_count)


def solution(mesh):
    owners, replicas = mesh.shape["index"], mesh.shape["query"]
    inner = 1 << (int(math.log2(owners)) // 2)
    split = Mesh(mesh.devices.reshape(owners // inner, inner, replicas), ("outer", "inner", "query"))
    index = ("outer", "inner")
    placed = (
        P(index, None),
        P(index),
        P(index),
        P(index, None),
        P(index, None),
        P(("outer", "inner", "query"), None),
        P(("outer", "inner", "query")),
    )
    return jax.shard_map(
        on_device,
        mesh=split,
        in_specs=placed,
        out_specs=(P(index, None), P(index), P(("outer", "inner", "query"))),
        check_vma=False,
    )
```

time: 79.3 us -> 82.2 us (1.037)
  waiting for transfers between devices: 27.1 us -> 32 us
  Pallas kernels: 22.3 us -> 19.8 us
  starting transfers between devices: 24.5 us -> 23.6 us
    ppermute x8 -> x17, starting transfers between devices: 7.14 us -> 16.9 us  [swap(): lax.ppermute(values, axis, [(i, i ^ flip) for i in range(lax.axis_size(ax...]
    ppermute x1, waiting for transfers between devices: 0.01 us -> 8.24 us  [on_device(): near = lax.ppermute(rows_half, axes, first)]
    all_to_all x1 -> x0, starting transfers between devices: 6.07 us -> none  [on_device(): lax.all_to_all(mail, ('outer', 'inner'), split_axis=0, concat_axis=0, til...]
    ppermute x1, waiting for transfers between devices: 5.52 us -> 0.01 us  [on_device(): far = lax.ppermute(near, axes, second)]
    ppermute x1, starting transfers between devices: 3 us -> 0.49 us  [on_device(): near = lax.ppermute(rows_half, axes, first)]
    pallas_call x7 -> x8, Pallas kernels: 22.3 us -> 19.8 us  [call(): pl.pallas_call(functools.partial(kernel, **options), out_shape=tuple(outs...]
    ppermute x1, waiting for transfers between devices: 0.01 us -> 1.76 us  [on_device(): last = lax.ppermute(from_end, 'outer', outward)]
    ppermute x1, waiting for transfers between devices: 6.47 us -> 7.79 us  [on_device(): to_end = lax.ppermute(across, 'outer', outward)]
  transfers between devices with their start and end apart: 16 -> 24, of which waited for: 3 -> 11; matrix products, arithmetic and copies ran while one was open for 1% -> 2% of each run, Pallas kernels for 25% -> 20%
where the time goes in v6:
time: 82.2 us; the launch traced here: 81.9 us
  waiting for transfers between devices  32 us (39%)
  starting transfers between devices  23.6 us (29%)
  Pallas kernels  19.8 us (24%)
  local copies, waits for them, and re-layouts  3.62 us (4%)
  other arithmetic  1.96 us (2%)
  between operations  0.91 us (1%)
    pallas_call x8, Pallas kernels, call(): pl.pallas_call(functools.partial(kernel, **options), out_shape=tuple(outs...  19.8 us
    ppermute x17, starting transfers between devices, swap(): lax.ppermute(values, axis, [(i, i ^ flip) for i in range(lax.axis_size(ax...  16.9 us
    ppermute x17, waiting for transfers between devices, swap(): lax.ppermute(values, axis, [(i, i ^ flip) for i in range(lax.axis_size(ax...  14.2 us
    ppermute x1, waiting for transfers between devices, on_device(): near = lax.ppermute(rows_half, axes, first)  8.24 us
    ppermute x1, waiting for transfers between devices, on_device(): to_end = lax.ppermute(across, 'outer', outward)  7.79 us
    unnamed x17, local copies, waits for them, and re-layouts  3.51 us
    ppermute x1, waiting for transfers between devices, on_device(): last = lax.ppermute(from_end, 'outer', outward)  1.76 us
  transfers between devices with their start and end apart: 24, of which 11 were waited for; matrix products, arithmetic and copies ran while one was open for 2% of the time, Pallas kernels for 20%

profile of v6, /device:TPU:0, one launch (start us, length us, event | category | flops | bytes accessed | tf_op | source)
XLA Modules:
  0.0 81.9 jit_solution(10071644123540958689)
XLA Ops:
  0.6 0.7 copy-done.4
  1.3 0.7 pad_add_fusion
  2.0 3.1 %collective-permute-start = (s32[2560]{0:T(1024)S(1)}, s32[2560]{0:T(1024)S(1)}, u32[]{:S(2)}, u32[]{:S(2)}) collective-permute-start(s32[2560]{0:T(1024)S(1)} %pad_add_fusion), channel_id=1, source_target_pairs={{0,8},{8,0},{16,24},{24,16},{1,9},{9,1},{17,25},{25,17},{2,10},{10... | collective-permute-start | bytes 30728 | tf_op jit(solution)/shard_map/ppermute | solution.py:265
  5.1 2.6 %collective-permute-start.1 = (s32[2560]{0:T(1024)S(1)}, s32[2560]{0:T(1024)S(1)}, u32[]{:S(2)}, u32[]{:S(2)}) collective-permute-start(s32[2560]{0:T(1024)S(1)} %pad_add_fusion), channel_id=1, source_target_pairs={{0,16},{8,24},{16,0},{24,8},{1,17},{9,25},{17,1},{25,9},{2,18},{10... | collective-permute-start | bytes 30728 | tf_op jit(solution)/shard_map/ppermute | solution.py:265
  7.7 0.0 collective-permute-start.2
  7.7 0.0 collective-permute-done
  7.7 2.0 %collective-permute-done.1 = s32[2560]{0:T(1024)S(1)} collective-permute-done((s32[2560]{0:T(1024)S(1)}, s32[2560]{0:T(1024)S(1)}, u32[]{:S(2)}, u32[]{:S(2)}) %collective-permute-start.1) | collective-permute-done | bytes 10272 | tf_op jit(solution)/shard_map/ppermute | solution.py:265
  9.7 3.5 %collective-permute-done.2 = s32[2560]{0:T(1024)S(1)} collective-permute-done((s32[2560]{0:T(1024)S(1)}, s32[2560]{0:T(1024)S(1)}, u32[]{:S(2)}, u32[]{:S(2)}) %collective-permute-start.2) | collective-permute-done | bytes 10272 | tf_op jit(solution)/shard_map/ppermute | solution.py:265
  13.2 0.7 copy-done.5
  13.9 1.5 %collective-permute-start.3 = (s32[1536]{0:T(1024)S(1)}, s32[1536]{0:T(1024)S(1)}, u32[]{:S(2)}, u32[]{:S(2)}) collective-permute-start(s32[1536]{0:T(1024)S(1)} %constant_dynamic-update-slice_fusion.4), channel_id=1, source_target_pairs={{0,2},{2,0},{4,6},{6,4},{1,3},{3,1},{5,7},{7,5},{8,10},{10,8},{12,... | collective-permute-start | bytes 18440 | tf_op jit(solution)/shard_map/ppermute | solution.py:265
  15.4 1.5 %collective-permute-start.4 = (s32[1536]{0:T(1024)S(1)}, s32[1536]{0:T(1024)S(1)}, u32[]{:S(2)}, u32[]{:S(2)}) collective-permute-start(s32[1536]{0:T(1024)S(1)} %constant_dynamic-update-slice_fusion.4), channel_id=1, source_target_pairs={{0,4},{2,6},{4,0},{6,2},{1,5},{3,7},{5,1},{7,3},{8,12},{10,14},{12... | collective-permute-start | bytes 18440 | tf_op jit(solution)/shard_map/ppermute | solution.py:265
  16.9 0.5 collective-permute-start.5
  17.4 0.1 pad_add_fusion.1.place
  17.4 1.1 %copy-done = bf16[512,768]{1,0:T(8,128)(2,1)S(1)} copy-done((bf16[512,768]{1,0:T(8,128)(2,1)S(1)}, bf16[512,768]{1,0:T(8,128)(2,1)}, u32[]{:S(2)}) %copy-start) | copy-done | bytes 786456
  18.6 1.0 %copy-done.2 = bf16[256,768]{1,0:T(8,128)(2,1)S(1)} copy-done((bf16[256,768]{1,0:T(8,128)(2,1)S(1)}, bf16[256,768]{1,0:T(8,128)(2,1)}, u32[]{:S(2)}) %copy-start.2) | copy-done | bytes 393240
  19.6 0.9 %prep.1 = (bf16[400,768]{1,0:T(8,128)(2,1)S(1)}, f32[6,128]{1,0:T(8,128)S(1)}) custom-call(s32[3]{0:T(128)S(1)} %pad_add_fusion.1.place, bf16[512,768]{1,0:T(8,128)(2,1)S(1)} %copy-done, bf16[256,768]{1,0:T(8,128)(2,1)S(1)} %copy-done.2), custom_call_target="tpu_custom_call" | custom-call | flops 1 | bytes 1 | tf_op jit(solution)/shard_map/prep/pallas_call | solution.py:252
  20.4 0.0 collective-permute-done.3
  20.5 0.0 collective-permute-done.4
  20.5 1.1 %collective-permute-done.5 = s32[1536]{0:T(1024)S(1)} collective-permute-done((s32[1536]{0:T(1024)S(1)}, s32[1536]{0:T(1024)S(1)}, u32[]{:S(2)}, u32[]{:S(2)}) %collective-permute-start.5) | collective-permute-done | bytes 6176 | tf_op jit(solution)/shard_map/ppermute | solution.py:265
  21.5 0.5 collective-permute-start.6
  22.0 0.0 collective-permute-start.7
  22.0 0.7 collective-permute-start.8
  22.9 1.6 %collective-permute-start.10 = (bf16[400,768]{1,0:T(8,128)(2,1)S(1)}, bf16[400,768]{1,0:T(8,128)(2,1)S(1)}, u32[]{:S(2)}, u32[]{:S(2)}) collective-permute-start(bf16[400,768]{1,0:T(8,128)(2,1)S(1)} %get-tuple-element.32), channel_id=1, source_target_pairs={{0,4},{1,3},{2,6},{3,1},{4,0},{5,7},{6,2},{7,5},{8,12},{9,11},{10,... | collective-permute-start | bytes 1843208 | tf_op jit(solution)/shard_map/ppermute | solution.py:337
  24.4 4.0 %meta.1 = (f32[4,3072]{1,0:T(4,128)S(1)}, f32[1,3072]{1,0:T(1,128)S(1)}, s32[1,1024]{1,0:T(1,128)S(1)}, s32[1,1024]{1,0:T(1,128)S(1)}, s32[1,384]{1,0:T(1,128)S(1)}, /*index=5*/s32[1,512]{1,0:T(1,128)S(1)}) custom-call(s32[3]{0:T(128)S(1)} %pad_add_fusion.1.place, s32[1,2560]{1,0:T(1,128)S(1)} %reshape.54.refs_0_, s32[1,2560]{1,0:T(1,128)S(1)} %reshape.55.refs_1_, ...), custom_call_target="tpu_custom_call" | custom-call | flops 1 | bytes 1 | tf_op jit(solution)/shard_map/meta/pallas_call | solution.py:252
  28.4 1.7 %collective-permute-done.7.refs_0_ = bf16[256,768]{1,0:T(8,128)(2,1)S(1)} collective-permute-done((bf16[256,768]{1,0:T(8,128)(2,1)S(1)}, bf16[256,768]{1,0:T(8,128)(2,1)S(1)}, u32[]{:S(2)}, u32[]{:S(2)}) %collective-permute-start.7) | collective-permute-done | bytes 393248 | tf_op jit(solution)/shard_map/ppermute | solution.py:265
  30.1 0.0 collective-permute-done.8.refs_1_
  30.1 8.2 %collective-permute-done.6.refs_2_.refs_6_.refs_7_ = bf16[400,768]{1,0:T(8,128)(2,1)S(1)} collective-permute-done((bf16[400,768]{1,0:T(8,128)(2,1)S(1)}, bf16[400,768]{1,0:T(8,128)(2,1)S(1)}, u32[]{:S(2)}, u32[]{:S(2)}) %collective-permute-start.6) | collective-permute-done | bytes 614432 | tf_op jit(solution)/shard_map/ppermute | solution.py:336
  38.3 0.5 collective-permute-start.12
  38.9 0.7 collective-permute-start.13
  39.5 1.3 %collective-permute-start.14 = (bf16[256,768]{1,0:T(8,128)(2,1)S(1)}, bf16[256,768]{1,0:T(8,128)(2,1)S(1)}, u32[]{:S(2)}, u32[]{:S(2)}) collective-permute-start(bf16[256,768]{1,0:T(8,128)(2,1)S(1)} %collective-permute-done.8.refs_1_), channel_id=1, source_target_pairs={{8,0},{16,24},{9,1},{17,25},{10,2},{18,26},{11,3},{19,27},{12,4},{... | collective-permute-start | bytes 1179656 | tf_op jit(solution)/shard_map/ppermute | solution.py:343
  40.8 0.1 collective-permute-start.9
  40.9 0.0 collective-permute-done.10.refs_4_.refs_8_.refs_9_
  40.9 0.5 collective-permute-start.11
  41.4 0.0 collective-permute-done.13.refs_1_
  41.4 7.8 %collective-permute-done.14.refs_0_ = bf16[256,768]{1,0:T(8,128)(2,1)S(1)} collective-permute-done((bf16[256,768]{1,0:T(8,128)(2,1)S(1)}, bf16[256,768]{1,0:T(8,128)(2,1)S(1)}, u32[]{:S(2)}, u32[]{:S(2)}) %collective-permute-start.14) | collective-permute-done | bytes 393248 | tf_op jit(solution)/shard_map/ppermute | solution.py:343
  49.2 0.0 collective-permute-done.12.refs_6_.refs_10_.refs_11_
  49.2 0.0 collective-permute-start.15
  49.2 1.5 %collective-permute-start.22 = (bf16[256,768]{1,0:T(8,128)(2,1)S(1)}, bf16[256,768]{1,0:T(8,128)(2,1)S(1)}, u32[]{:S(2)}, u32[]{:S(2)}) collective-permute-start(bf16[256,768]{1,0:T(8,128)(2,1)S(1)} %collective-permute-done.13.refs_1_), channel_id=1, source_target_pairs={{8,0},{16,24},{9,1},{17,25},{10,2},{18,26},{11,3},{19,27},{12,4},{... | collective-permute-start | bytes 1179656 | tf_op jit(solution)/shard_map/ppermute | solution.py:346
  50.7 0.0 collective-permute-done.9.refs_3_.refs_7_.refs_8_
  50.7 0.0 collective-permute-done.11.refs_5_.refs_9_.refs_10_
  50.7 0.5 collective-permute-done.15.refs_7_.refs_11_.refs_12_
  51.3 1.2 %pack.1 = (bf16[192,768]{1,0:T(8,128)(2,1)S(1)}, f32[1,3072]{1,0:T(1,128)S(1)}) custom-call(s32[3]{0:T(128)S(1)} %pad_add_fusion.1.place, s32[1,1024]{1,0:T(1,128)S(1)} %get-tuple-element.38.code, f32[6,128]{1,0:T(8,128)S(1)} %get-tuple-element.39.scale, bf16[512,768]{1,0:T(8,128)(2,1)S(1)} %copy-done.1, bf16[256,768]{1,0:T(8,128)(2,1)S(1)} %copy-done.2, ...), custom_call_target="tpu_custom_call" | custom-call | flops 1 | bytes 1 | tf_op jit(solution)/shard_map/pack/pallas_call | solution.py:252
  52.5 2.2 %collective-permute-start.16 = (bf16[64,768]{1,0:T(8,128)(2,1)S(1)}, bf16[64,768]{1,0:T(8,128)(2,1)S(1)}, u32[]{:S(2)}, u32[]{:S(2)}) collective-permute-start(bf16[64,768]{1,0:T(8,128)(2,1)S(1)} %get-tuple-element.49), channel_id=1, source_target_pairs={{0,8},{8,0},{16,24},{24,16},{1,9},{9,1},{17,25},{25,17},{2,10},{10... | collective-permute-start | bytes 294920 | tf_op jit(solution)/shard_map/ppermute | solution.py:265
  54.8 0.6 broadcast_select_fusion
  55.3 2.5 %score.5 = f32[2,2,128]{2,1,0:T(2,128)S(1)} custom-call(s32[3]{0:T(128)S(1)} %pad_add_fusion.1.place, s32[1,256]{1,0:T(1,128)S(1)} %bitcast.11, bf16[256,768]{1,0:T(8,128)(2,1)S(1)} %collective-permute-done.14.refs_0_, bf16[256,768]{1,0:T(8,128)(2,1)S(1)} %collective-permute-done.13.refs_1_, f32[4,3072]{1,0:T(4,128)S(1)} %get-tuple-element.42.refs_1_.refs_2_, ...), custom_call_target="tpu_custom_call" | custom-call | flops 1 | bytes 1 | tf_op jit(solution)/shard_map/score/pallas_call | solution.py:252
  57.9 0.1 collective-permute-start.21
  58.0 2.5 %score.4 = f32[2,2,128]{2,1,0:T(2,128)S(1)} custom-call(s32[3]{0:T(128)S(1)} %pad_add_fusion.1.place, s32[1,256]{1,0:T(1,128)S(1)} %bitcast.13, bf16[256,768]{1,0:T(8,128)(2,1)S(1)} %collective-permute-done.7.refs_0_, f32[4,3072]{1,0:T(4,128)S(1)} %get-tuple-element.42.refs_1_.refs_2_, f32[1,3072]{1,0:T(1,128)S(1)} %get-tuple-element.43.refs_2_.refs_3_, ...), custom_call_target="tpu_custom_call" | custom-call | flops 1 | bytes 1 | tf_op jit(solution)/shard_map/score/pallas_call | solution.py:252
  60.5 0.8 %collective-permute-start.20 = (f32[2,2,128]{2,1,0:T(2,128)S(1)}, f32[2,2,128]{2,1,0:T(2,128)S(1)}, u32[]{:S(2)}, u32[]{:S(2)}) collective-permute-start(f32[2,2,128]{2,1,0:T(2,128)S(1)} %score.4), channel_id=1, source_target_pairs={{0,8},{8,0},{16,24},{24,16},{1,9},{9,1},{17,25},{25,17},{2,10},{10... | collective-permute-start | bytes 6152 | tf_op jit(solution)/shard_map/ppermute | solution.py:265
  61.3 1.8 %collective-permute-done.22.refs_0_ = bf16[256,768]{1,0:T(8,128)(2,1)S(1)} collective-permute-done((bf16[256,768]{1,0:T(8,128)(2,1)S(1)}, bf16[256,768]{1,0:T(8,128)(2,1)S(1)}, u32[]{:S(2)}, u32[]{:S(2)}) %collective-permute-start.22) | collective-permute-done | bytes 393248 | tf_op jit(solution)/shard_map/ppermute | solution.py:346
  63.1 2.5 %score.6 = f32[2,2,128]{2,1,0:T(2,128)S(1)} custom-call(s32[3]{0:T(128)S(1)} %pad_add_fusion.1.place, s32[1,256]{1,0:T(1,128)S(1)} %bitcast.10, bf16[256,768]{1,0:T(8,128)(2,1)S(1)} %collective-permute-done.22.refs_0_, bf16[256,768]{1,0:T(8,128)(2,1)S(1)} %collective-permute-done.8.refs_1_, f32[4,3072]{1,0:T(4,128)S(1)} %get-tuple-element.42.refs_1_.refs_2_, ...), custom_call_target="tpu_custom_call" | custom-call | flops 1 | bytes 1 | tf_op jit(solution)/shard_map/score/pallas_call | solution.py:252
  65.6 1.9 %collective-permute-start.23 = (f32[2,2,128]{2,1,0:T(2,128)S(1)}, f32[2,2,128]{2,1,0:T(2,128)S(1)}, u32[]{:S(2)}, u32[]{:S(2)}) collective-permute-start(f32[2,2,128]{2,1,0:T(2,128)S(1)} %score.6), channel_id=1, source_target_pairs={{0,24},{8,16},{16,8},{24,0},{1,25},{9,17},{17,9},{25,1},{2,26},{10... | collective-permute-start | bytes 6152 | tf_op jit(solution)/shard_map/ppermute | solution.py:265
  67.5 0.0 collective-permute-start.17
  67.5 2.5 %score.7 = f32[2,2,128]{2,1,0:T(2,128)S(1)} custom-call(s32[3]{0:T(128)S(1)} %pad_add_fusion.1.place, s32[1,256]{1,0:T(1,128)S(1)} %bitcast.12, bf16[256,768]{1,0:T(8,128)(2,1)S(1)} %copy-done.3, f32[4,3072]{1,0:T(4,128)S(1)} %get-tuple-element.42.refs_1_.refs_2_, f32[1,3072]{1,0:T(1,128)S(1)} %get-tuple-element.43.refs_2_.refs_3_, ...), custom_call_target="tpu_custom_call" | custom-call | flops 1 | bytes 1 | tf_op jit(solution)/shard_map/score/pallas_call | solution.py:252
  70.1 0.0 collective-permute-done.16
  70.1 2.0 %collective-permute-start.18 = (bf16[64,768]{1,0:T(8,128)(2,1)S(1)}, bf16[64,768]{1,0:T(8,128)(2,1)S(1)}, u32[]{:S(2)}, u32[]{:S(2)}) collective-permute-start(bf16[64,768]{1,0:T(8,128)(2,1)S(1)} %get-tuple-element.47), channel_id=1, source_target_pairs={{0,24},{8,16},{16,8},{24,0},{1,25},{9,17},{17,9},{25,1},{2,26},{10... | collective-permute-start | bytes 294920 | tf_op jit(solution)/shard_map/ppermute | solution.py:265
  72.1 2.7 %collective-permute-done.17 = bf16[64,768]{1,0:T(8,128)(2,1)S(1)} collective-permute-done((bf16[64,768]{1,0:T(8,128)(2,1)S(1)}, bf16[64,768]{1,0:T(8,128)(2,1)S(1)}, u32[]{:S(2)}, u32[]{:S(2)}) %collective-permute-start.17) | collective-permute-done | bytes 98336 | tf_op jit(solution)/shard_map/ppermute | solution.py:265
  74.8 1.8 %collective-permute-done.18 = bf16[64,768]{1,0:T(8,128)(2,1)S(1)} collective-permute-done((bf16[64,768]{1,0:T(8,128)(2,1)S(1)}, bf16[64,768]{1,0:T(8,128)(2,1)S(1)}, u32[]{:S(2)}, u32[]{:S(2)}) %collective-permute-start.18) | collective-permute-done | bytes 98336 | tf_op jit(solution)/shard_map/ppermute | solution.py:265
  76.7 0.1 collective-permute-start.19
  76.8 0.0 collective-permute-done.21
  76.8 0.0 collective-permute-done.20
  76.8 0.0 collective-permute-done.23
  76.8 0.6 fusion.1
  77.4 0.9 %collective-permute-done.19.refs_9_ = bf16[192,768]{1,0:T(8,128)(2,1)S(1)} collective-permute-done((bf16[192,768]{1,0:T(8,128)(2,1)S(1)}, bf16[192,768]{1,0:T(8,128)(2,1)S(1)}, u32[]{:S(2)}, u32[]{:S(2)}) %collective-permute-start.19) | collective-permute-done | bytes 294944 | tf_op jit(solution)/shard_map/ppermute | solution.py:265
  78.3 3.5 %apply.1 = bf16[512,768]{1,0:T(8,128)(2,1)} custom-call(s32[3]{0:T(128)S(1)} %pad_add_fusion.1.place, s32[1,1024]{1,0:T(1,128)S(1)} %get-tuple-element.30.own_target, s32[1,384]{1,0:T(1,128)S(1)} %get-tuple-element.31.target, bf16[512,768]{1,0:T(8,128)(2,1)S(1)} %copy-done.1, bf16[512,768]{1,0:T(8,128)(2,1)S(1)} %copy-done.1, ...), custom_call_target="tpu_custom_call" | custom-call | flops 1 | bytes 1 | tf_op jit(solution)/shard_map/apply/pallas_call | solution.py:252
  (30 shorter events, 0.2 us)
Async XLA Ops:
  0.6 0.7 copy-start.4
  2.0 5.7 %copy-start.6 = (s32[256]{0:T(256)S(1)}, s32[256]{0:T(256)}, u32[]{:S(2)}) copy-start(s32[256]{0:T(256)} %param.9) | copy-start | bytes 3076
  2.0 5.7 %collective-permute-start = (s32[2560]{0:T(1024)S(1)}, s32[2560]{0:T(1024)S(1)}, u32[]{:S(2)}, u32[]{:S(2)}) collective-permute-start(s32[2560]{0:T(1024)S(1)} %pad_add_fusion), channel_id=1, source_target_pairs={{0,8},{8,0},{16,24},{24,16},{1,9},{9,1},{17,25},{25,17},{2,10},{10... | collective-permute-start | bytes 30728 | tf_op jit(solution)/shard_map/ppermute | solution.py:265
  5.1 4.6 %collective-permute-start.1 = (s32[2560]{0:T(1024)S(1)}, s32[2560]{0:T(1024)S(1)}, u32[]{:S(2)}, u32[]{:S(2)}) collective-permute-start(s32[2560]{0:T(1024)S(1)} %pad_add_fusion), channel_id=1, source_target_pairs={{0,16},{8,24},{16,0},{24,8},{1,17},{9,25},{17,1},{25,9},{2,18},{10... | collective-permute-start | bytes 30728 | tf_op jit(solution)/shard_map/ppermute | solution.py:265
  7.7 5.5 %collective-permute-start.2 = (s32[2560]{0:T(1024)S(1)}, s32[2560]{0:T(1024)S(1)}, u32[]{:S(2)}, u32[]{:S(2)}) collective-permute-start(s32[2560]{0:T(1024)S(1)} %pad_add_fusion), channel_id=1, source_target_pairs={{0,24},{8,16},{16,8},{24,0},{1,25},{9,17},{17,9},{25,1},{2,26},{10... | collective-permute-start | bytes 30728 | tf_op jit(solution)/shard_map/ppermute | solution.py:265
  13.2 0.7 copy-start.5
  13.9 6.6 %collective-permute-start.3 = (s32[1536]{0:T(1024)S(1)}, s32[1536]{0:T(1024)S(1)}, u32[]{:S(2)}, u32[]{:S(2)}) collective-permute-start(s32[1536]{0:T(1024)S(1)} %constant_dynamic-update-slice_fusion.4), channel_id=1, source_target_pairs={{0,2},{2,0},{4,6},{6,4},{1,3},{3,1},{5,7},{7,5},{8,10},{10,8},{12,... | collective-permute-start | bytes 18440 | tf_op jit(solution)/shard_map/ppermute | solution.py:265
  15.4 5.1 %collective-permute-start.4 = (s32[1536]{0:T(1024)S(1)}, s32[1536]{0:T(1024)S(1)}, u32[]{:S(2)}, u32[]{:S(2)}) collective-permute-start(s32[1536]{0:T(1024)S(1)} %constant_dynamic-update-slice_fusion.4), channel_id=1, source_target_pairs={{0,4},{2,6},{4,0},{6,2},{1,5},{3,7},{5,1},{7,3},{8,12},{10,14},{12... | collective-permute-start | bytes 18440 | tf_op jit(solution)/shard_map/ppermute | solution.py:265
  16.9 4.7 %collective-permute-start.5 = (s32[1536]{0:T(1024)S(1)}, s32[1536]{0:T(1024)S(1)}, u32[]{:S(2)}, u32[]{:S(2)}) collective-permute-start(s32[1536]{0:T(1024)S(1)} %constant_dynamic-update-slice_fusion.4), channel_id=1, source_target_pairs={{0,6},{2,4},{4,2},{6,0},{1,7},{3,5},{5,3},{7,1},{8,14},{10,12},{12... | collective-permute-start | bytes 18440 | tf_op jit(solution)/shard_map/ppermute | solution.py:265
  17.4 1.1 %copy-start = (bf16[512,768]{1,0:T(8,128)(2,1)S(1)}, bf16[512,768]{1,0:T(8,128)(2,1)}, u32[]{:S(2)}) copy-start(bf16[512,768]{1,0:T(8,128)(2,1)} %refs_4_.3) | copy-start | bytes 2359300
  18.6 1.0 %copy-start.2 = (bf16[256,768]{1,0:T(8,128)(2,1)S(1)}, bf16[256,768]{1,0:T(8,128)(2,1)}, u32[]{:S(2)}) copy-start(bf16[256,768]{1,0:T(8,128)(2,1)} %refs_5_.7) | copy-start | bytes 1179652
  19.6 2.5 %copy-start.3 = (bf16[256,768]{1,0:T(8,128)(2,1)S(1)}, bf16[256,768]{1,0:T(8,128)(2,1)}, u32[]{:S(2)}) copy-start(bf16[256,768]{1,0:T(8,128)(2,1)} %refs_0_.5) | copy-start | bytes 1179652
  19.6 31.7 %copy-start.1 = (bf16[512,768]{1,0:T(8,128)(2,1)S(1)}, bf16[512,768]{1,0:T(8,128)(2,1)}, u32[]{:S(2)}) copy-start(bf16[512,768]{1,0:T(8,128)(2,1)} %refs_4_.3) | copy-start | bytes 2359300
  21.5 16.8 %collective-permute-start.6 = (bf16[400,768]{1,0:T(8,128)(2,1)S(1)}, bf16[400,768]{1,0:T(8,128)(2,1)S(1)}, u32[]{:S(2)}, u32[]{:S(2)}) collective-permute-start(bf16[400,768]{1,0:T(8,128)(2,1)S(1)} %get-tuple-element.32), channel_id=1, source_target_pairs={{0,2},{1,5},{2,0},{3,7},{4,6},{5,1},{6,4},{7,3},{8,10},{9,13},{10,... | collective-permute-start | bytes 1843208 | tf_op jit(solution)/shard_map/ppermute | solution.py:336
  22.0 8.1 %collective-permute-start.7 = (bf16[256,768]{1,0:T(8,128)(2,1)S(1)}, bf16[256,768]{1,0:T(8,128)(2,1)S(1)}, u32[]{:S(2)}, u32[]{:S(2)}) collective-permute-start(bf16[256,768]{1,0:T(8,128)(2,1)S(1)} %copy-done.3), channel_id=1, source_target_pairs={{0,8},{8,0},{16,24},{24,16},{1,9},{9,1},{17,25},{25,17},{2,10},{10... | collective-permute-start | bytes 1179656 | tf_op jit(solution)/shard_map/ppermute | solution.py:265
  22.0 8.1 %collective-permute-start.8 = (bf16[256,768]{1,0:T(8,128)(2,1)S(1)}, bf16[256,768]{1,0:T(8,128)(2,1)S(1)}, u32[]{:S(2)}, u32[]{:S(2)}) collective-permute-start(bf16[256,768]{1,0:T(8,128)(2,1)S(1)} %copy-done.3), channel_id=1, source_target_pairs={{8,16},{16,8},{9,17},{17,9},{10,18},{18,10},{11,19},{19,11},{12,20... | collective-permute-start | bytes 1179656 | tf_op jit(solution)/shard_map/ppermute | solution.py:340
  22.9 18.1 %collective-permute-start.10 = (bf16[400,768]{1,0:T(8,128)(2,1)S(1)}, bf16[400,768]{1,0:T(8,128)(2,1)S(1)}, u32[]{:S(2)}, u32[]{:S(2)}) collective-permute-start(bf16[400,768]{1,0:T(8,128)(2,1)S(1)} %get-tuple-element.32), channel_id=1, source_target_pairs={{0,4},{1,3},{2,6},{3,1},{4,0},{5,7},{6,2},{7,5},{8,12},{9,11},{10,... | collective-permute-start | bytes 1843208 | tf_op jit(solution)/shard_map/ppermute | solution.py:337
  38.3 10.9 %collective-permute-start.12 = (bf16[400,768]{1,0:T(8,128)(2,1)S(1)}, bf16[400,768]{1,0:T(8,128)(2,1)S(1)}, u32[]{:S(2)}, u32[]{:S(2)}) collective-permute-start(bf16[400,768]{1,0:T(8,128)(2,1)S(1)} %collective-permute-done.6.refs_2_.refs_6_.refs_7_), channel_id=1, source_target_pairs={{0,4},{1,3},{2,6},{3,1},{4,0},{5,7},{6,2},{7,5},{8,12},{9,11},{10,... | collective-permute-start | bytes 1843208 | tf_op jit(solution)/shard_map/ppermute | solution.py:344
  38.9 2.6 %collective-permute-start.13 = (bf16[256,768]{1,0:T(8,128)(2,1)S(1)}, bf16[256,768]{1,0:T(8,128)(2,1)S(1)}, u32[]{:S(2)}, u32[]{:S(2)}) collective-permute-start(bf16[256,768]{1,0:T(8,128)(2,1)S(1)} %collective-permute-done.7.refs_0_), channel_id=1, source_target_pairs={{8,16},{16,8},{9,17},{17,9},{10,18},{18,10},{11,19},{19,11},{12,20... | collective-permute-start | bytes 1179656 | tf_op jit(solution)/shard_map/ppermute | solution.py:342
  39.5 9.7 %collective-permute-start.14 = (bf16[256,768]{1,0:T(8,128)(2,1)S(1)}, bf16[256,768]{1,0:T(8,128)(2,1)S(1)}, u32[]{:S(2)}, u32[]{:S(2)}) collective-permute-start(bf16[256,768]{1,0:T(8,128)(2,1)S(1)} %collective-permute-done.8.refs_1_), channel_id=1, source_target_pairs={{8,0},{16,24},{9,1},{17,25},{10,2},{18,26},{11,3},{19,27},{12,4},{... | collective-permute-start | bytes 1179656 | tf_op jit(solution)/shard_map/ppermute | solution.py:343
  40.8 9.9 %collective-permute-start.9 = (bf16[400,768]{1,0:T(8,128)(2,1)S(1)}, bf16[400,768]{1,0:T(8,128)(2,1)S(1)}, u32[]{:S(2)}, u32[]{:S(2)}) collective-permute-start(bf16[400,768]{1,0:T(8,128)(2,1)S(1)} %collective-permute-done.6.refs_2_.refs_6_.refs_7_), channel_id=1, source_target_pairs={{0,1},{1,0},{2,3},{3,2},{4,5},{5,4},{6,7},{7,6},{8,9},{9,8},{10,11... | collective-permute-start | bytes 1843208 | tf_op jit(solution)/shard_map/ppermute | solution.py:265
  40.9 9.8 %collective-permute-start.11 = (bf16[400,768]{1,0:T(8,128)(2,1)S(1)}, bf16[400,768]{1,0:T(8,128)(2,1)S(1)}, u32[]{:S(2)}, u32[]{:S(2)}) collective-permute-start(bf16[400,768]{1,0:T(8,128)(2,1)S(1)} %collective-permute-done.10.refs_4_.refs_8_.refs_9_), channel_id=1, source_target_pairs={{0,1},{1,0},{2,3},{3,2},{4,5},{5,4},{6,7},{7,6},{8,9},{9,8},{10,11... | collective-permute-start | bytes 1843208 | tf_op jit(solution)/shard_map/ppermute | solution.py:265
  49.2 2.0 %collective-permute-start.15 = (bf16[400,768]{1,0:T(8,128)(2,1)S(1)}, bf16[400,768]{1,0:T(8,128)(2,1)S(1)}, u32[]{:S(2)}, u32[]{:S(2)}) collective-permute-start(bf16[400,768]{1,0:T(8,128)(2,1)S(1)} %collective-permute-done.12.refs_6_.refs_10_.refs_11_), channel_id=1, source_target_pairs={{0,1},{1,0},{2,3},{3,2},{4,5},{5,4},{6,7},{7,6},{8,9},{9,8},{10,11... | collective-permute-start | bytes 1843208 | tf_op jit(solution)/shard_map/ppermute | solution.py:265
  49.2 13.8 %collective-permute-start.22 = (bf16[256,768]{1,0:T(8,128)(2,1)S(1)}, bf16[256,768]{1,0:T(8,128)(2,1)S(1)}, u32[]{:S(2)}, u32[]{:S(2)}) collective-permute-start(bf16[256,768]{1,0:T(8,128)(2,1)S(1)} %collective-permute-done.13.refs_1_), channel_id=1, source_target_pairs={{8,0},{16,24},{9,1},{17,25},{10,2},{18,26},{11,3},{19,27},{12,4},{... | collective-permute-start | bytes 1179656 | tf_op jit(solution)/shard_map/ppermute | solution.py:346
  52.5 17.5 %collective-permute-start.16 = (bf16[64,768]{1,0:T(8,128)(2,1)S(1)}, bf16[64,768]{1,0:T(8,128)(2,1)S(1)}, u32[]{:S(2)}, u32[]{:S(2)}) collective-permute-start(bf16[64,768]{1,0:T(8,128)(2,1)S(1)} %get-tuple-element.49), channel_id=1, source_target_pairs={{0,8},{8,0},{16,24},{24,16},{1,9},{9,1},{17,25},{25,17},{2,10},{10... | collective-permute-start | bytes 294920 | tf_op jit(solution)/shard_map/ppermute | solution.py:265
  57.9 18.9 %collective-permute-start.21 = (f32[2,2,128]{2,1,0:T(2,128)S(1)}, f32[2,2,128]{2,1,0:T(2,128)S(1)}, u32[]{:S(2)}, u32[]{:S(2)}) collective-permute-start(f32[2,2,128]{2,1,0:T(2,128)S(1)} %score.5), channel_id=1, source_target_pairs={{0,16},{8,24},{16,0},{24,8},{1,17},{9,25},{17,1},{25,9},{2,18},{10... | collective-permute-start | bytes 6152 | tf_op jit(solution)/shard_map/ppermute | solution.py:265
  60.5 16.3 %collective-permute-start.20 = (f32[2,2,128]{2,1,0:T(2,128)S(1)}, f32[2,2,128]{2,1,0:T(2,128)S(1)}, u32[]{:S(2)}, u32[]{:S(2)}) collective-permute-start(f32[2,2,128]{2,1,0:T(2,128)S(1)} %score.4), channel_id=1, source_target_pairs={{0,8},{8,0},{16,24},{24,16},{1,9},{9,1},{17,25},{25,17},{2,10},{10... | collective-permute-start | bytes 6152 | tf_op jit(solution)/shard_map/ppermute | solution.py:265
  65.6 11.1 %collective-permute-start.23 = (f32[2,2,128]{2,1,0:T(2,128)S(1)}, f32[2,2,128]{2,1,0:T(2,128)S(1)}, u32[]{:S(2)}, u32[]{:S(2)}) collective-permute-start(f32[2,2,128]{2,1,0:T(2,128)S(1)} %score.6), channel_id=1, source_target_pairs={{0,24},{8,16},{16,8},{24,0},{1,25},{9,17},{17,9},{25,1},{2,26},{10... | collective-permute-start | bytes 6152 | tf_op jit(solution)/shard_map/ppermute | solution.py:265
  67.5 7.3 %collective-permute-start.17 = (bf16[64,768]{1,0:T(8,128)(2,1)S(1)}, bf16[64,768]{1,0:T(8,128)(2,1)S(1)}, u32[]{:S(2)}, u32[]{:S(2)}) collective-permute-start(bf16[64,768]{1,0:T(8,128)(2,1)S(1)} %get-tuple-element.48), channel_id=1, source_target_pairs={{0,16},{8,24},{16,0},{24,8},{1,17},{9,25},{17,1},{25,9},{2,18},{10... | collective-permute-start | bytes 294920 | tf_op jit(solution)/shard_map/ppermute | solution.py:265
  70.1 6.6 %collective-permute-start.18 = (bf16[64,768]{1,0:T(8,128)(2,1)S(1)}, bf16[64,768]{1,0:T(8,128)(2,1)S(1)}, u32[]{:S(2)}, u32[]{:S(2)}) collective-permute-start(bf16[64,768]{1,0:T(8,128)(2,1)S(1)} %get-tuple-element.47), channel_id=1, source_target_pairs={{0,24},{8,16},{16,8},{24,0},{1,25},{9,17},{17,9},{25,1},{2,26},{10... | collective-permute-start | bytes 294920 | tf_op jit(solution)/shard_map/ppermute | solution.py:265
  76.7 1.6 %collective-permute-start.19 = (bf16[192,768]{1,0:T(8,128)(2,1)S(1)}, bf16[192,768]{1,0:T(8,128)(2,1)S(1)}, u32[]{:S(2)}, u32[]{:S(2)}) collective-permute-start(bf16[192,768]{1,0:T(8,128)(2,1)S(1)} %constant_dynamic-update-slice_fusion.1.refs_8_), channel_id=1, source_target_pairs={{0,1},{1,0},{2,3},{3,2},{4,5},{5,4},{6,7},{7,6},{8,9},{9,8},{10,11... | collective-permute-start | bytes 884744 | tf_op jit(solution)/shard_map/ppermute | solution.py:265

commit v7 on v6

--- a/solution.py
+++ b/solution.py
@@ -176,7 +176,7 @@
             scale_out[:, pl.ds(first + chunk * LANES, LANES)] = row
 
 
-def apply_kernel(place, own_target, target, table, *refs, pieces, arrivals):
+def apply_kernel(place, own_target, target, refreshed, table, *refs, pieces, arrivals):
     out = refs[-1]
     buffers, arrived = refs[: -1 - arrivals], refs[-1 - arrivals : -1]
     parts = [
@@ -188,13 +188,16 @@
         parts.append((target[:, first : first + block.shape[0]], block[...]))
         first += block.shape[0]
     fresh = jnp.zeros(out.shape, jnp.float32)
-    hit = jnp.zeros((out.shape[0], 1), jnp.float32)
     for to_row, values in parts:
         rows = lax.broadcasted_iota(jnp.int32, (out.shape[0], to_row.shape[1]), 0)
-        chosen = jnp.where(rows == to_row, 1.0, 0.0)
-        hit += jnp.sum(chosen, axis=1, keepdims=True)
-        fresh += lax.dot_general(chosen.astype(jnp.bfloat16), values, NN, preferred_element_type=jnp.float32)
-    out[...] = jnp.where(hit > 0.5, fresh, table[...].astype(jnp.float32)).astype(jnp.bfloat16)
+        chosen = jnp.where(rows == to_row, 1.0, 0.0).astype(jnp.bfloat16)
+        fresh += lax.dot_general(chosen, values, NN, preferred_element_type=jnp.float32)
+    for top in range(0, out.shape[0], LANES):
+        part = slice(top, top + LANES)
+        hit = to_lanes(refreshed[:, part].astype(jnp.float32)) > 0.5
+        for left in range(0, out.shape[1], LANES):
+            cols = slice(left, left + LANES)
+            out[part, cols] = jnp.where(hit, fresh[part, cols], table[part, cols].astype(jnp.float32)).astype(jnp.bfloat16)
 
 
 def to_lanes(row):
@@ -218,20 +221,28 @@
         pos_b[part, :] = to_lanes(positive[:, part].astype(jnp.float32))
     total[...] = jnp.zeros_like(total)
     pos_total[...] = jnp.zeros_like(pos_total)
-    for source, start, size, column, _ in pieces:
+
+    def product(piece):
+        source, start, size = piece[:3]
+        rows = refs[source][start : start + size, :]
+        return lax.dot_general(queries[...], rows, NT, preferred_element_type=jnp.float32)
+
+    following = product(pieces[0])
+    for i, (_, _, size, column, _) in enumerate(pieces):
+        raw = following
+        if i + 1 < len(pieces):
+            following = product(pieces[i + 1])
         first = piece_offset(place, column)
-        raw = lax.dot_general(
-            queries[...], refs[source][start : start + size, :], NT, preferred_element_type=jnp.float32
-        )
         for top in range(0, count, 64):
             part = slice(top, top + 64)
             sums, positives = total[part, :], pos_total[part, :]
+            query_scale, wanted = q_scale[part, :], pos_b[part, :]
             for chunk in range(size // LANES):
                 cols = pl.ds(first + chunk * LANES, LANES)
-                powers = raw[part, chunk * LANES : (chunk + 1) * LANES] * q_scale[part, :]
+                powers = raw[part, chunk * LANES : (chunk + 1) * LANES] * query_scale
                 powers = powers * scale[:, cols] + log_weight[flip : flip + 1, cols]
                 sums = sums + jnp.exp2(powers)
-                positives = positives + jnp.where(pos_b[part, :] == row_ids[:, cols], powers, 0.0)
+                positives = positives + jnp.where(wanted == row_ids[:, cols], powers, 0.0)
             total[part, :] = sums
             pos_total[part, :] = positives
     for block in range(count // LANES):
@@ -304,7 +315,6 @@
         replicas=replicas,
         encode=fast,
     )
-    rows_half, *sides = lax.optimization_barrier((rows_half, *sides))
 
     others = (planes - 1) * owners_plane
     lw, row_ids, code, own_target, target, own = call(
@@ -334,21 +344,21 @@
         first = [(2 * i + c, 2 * (i ^ (1 + c)) + c) for i in range(4) for c in range(2)]
         second = [(2 * i + c, 2 * (i ^ (2 - c)) + c) for i in range(4) for c in range(2)]
         near = lax.ppermute(rows_half, axes, first)
-        side = lax.ppermute(rows_half, axes, second)
+        side_rows = lax.ppermute(rows_half, axes, second)
         middle, outward = [(1, 2), (2, 1)], [(1, 0), (2, 3)]
         beside = swap(queries, "outer", 1)
         across = lax.ppermute(queries, "outer", middle)
-        near, beside, across, lw = lax.optimization_barrier((near, beside, across, lw))
+        near, side_rows, beside, across, *lines = lax.optimization_barrier((near, side_rows, beside, across, *lines))
         from_end = lax.ppermute(beside, "outer", middle)
         to_end = lax.ppermute(across, "outer", outward)
         far = lax.ppermute(near, axes, second)
-        far, from_end, to_end = lax.optimization_barrier((far, from_end, to_end))
+        far, from_end, to_end, lw = lax.optimization_barrier((far, from_end, to_end, lw))
         last = lax.ppermute(from_end, "outer", outward)
         got_queries = [(queries,), (beside,), (to_end, from_end), (last, across)]
         buffers = [table, fresh_rows]
         table_pieces = [(0, 0, rows_dev, (0, rows_dev, None, None), -1)]
         fresh_pieces = [(1, 0, refresh_dev, (0, refresh_dev, None, None), -1 - rows_dev // LANES)]
-        for slot, by_core, mine in ((1, 0, near), (1, 1, side), (3, None, far)):
+        for slot, by_core, mine in ((1, 0, near), (1, 1, side_rows), (3, None, far)):
             for flip, rows in enumerate((mine, swap(mine, "query", 1))):
                 by = None if by_core is None else by_core ^ flip
                 data = table_half + fresh_half
@@ -398,16 +408,15 @@
     )
     size = owners_plane * share
     came = jnp.concatenate([swap(packed[(s - 1) * size : s * size], "outer", s) for s in range(1, planes)])
-    arrived = [came] + [swap(came, "query", flip) for flip in range(1, replicas)]
-    mine = None
-    for s in [*range(1, planes), 0]:
+
+    def score(s, given):
         (partial,) = call(
             score_kernel,
             "score",
             [jax.ShapeDtypeStruct((2, query_count // LANES, LANES), f32)],
             place,
             positive[s],
-            *got_queries[s],
+            *given,
             lw,
             row_ids,
             scale_plane,
@@ -415,11 +424,20 @@
             scratch=[pltpu.VMEM((query_count, LANES), f32)] * 4 + [pltpu.VMEM(queries.shape, bf16)],
             pieces=pieces,
             flip=s,
-            given=len(got_queries[s]),
+            given=len(given),
         )
-        if s:
-            partial = swap(partial, "outer", s)
-        mine = partial if mine is None else mine + partial
+        return partial
+
+    first = score(1, got_queries[1])
+    late = [one for group in got_queries[2:] for one in group]
+    came, first, *late = lax.optimization_barrier((came, first, *late))
+    arrived = [came] + [swap(came, "query", flip) for flip in range(1, replicas)]
+    mine = swap(first, "outer", 1)
+    each = len(late) // (planes - 2)
+    for s in range(2, planes):
+        mine = mine + swap(score(s, late[(s - 2) * each : (s - 1) * each]), "outer", s)
+    own_queries, *arrived = lax.optimization_barrier((queries, *arrived))
+    mine = mine + score(0, [own_queries])
     (new_table,) = call(
         apply_kernel,
         "apply",
@@ -427,6 +445,7 @@
         place,
         own_target,
         target,
+        own,
         table,
         *buffers,
         *arrived,

time: 82.2 us -> 83.2 us (1.012)
  starting transfers between devices: 23.6 us -> 37 us
  waiting for transfers between devices: 32 us -> 20.5 us
    ppermute x17, starting transfers between devices: 16.9 us -> 27.9 us  [swap(): lax.ppermute(values, axis, [(i, i ^ flip) for i in range(lax.axis_size(ax...]
    ppermute x1, waiting for transfers between devices: 8.24 us -> 0.01 us  [on_device(): near = lax.ppermute(rows_half, axes, first)]
    ppermute x1, waiting for transfers between devices: 7.79 us -> 0.01 us  [on_device(): to_end = lax.ppermute(across, 'outer', outward)]
    ppermute x17, waiting for transfers between devices: 14.2 us -> 20.4 us  [swap(): lax.ppermute(values, axis, [(i, i ^ flip) for i in range(lax.axis_size(ax...]
    ppermute x1, starting transfers between devices: 0.49 us -> 2.94 us  [on_device(): near = lax.ppermute(rows_half, axes, first)]
    ppermute x1, waiting for transfers between devices: 1.76 us -> 0.01 us  [on_device(): last = lax.ppermute(from_end, 'outer', outward)]
    unnamed x17 -> x19, local copies, waits for them, and re-layouts: 3.51 us -> 2.82 us
  transfers between devices with their start and end apart: 24 -> 24, of which waited for: 11 -> 9; matrix products, arithmetic and copies ran while one was open for 2% -> 1% of each run, Pallas kernels for 20% -> 18%
where the time goes in v7:
time: 83.2 us; the launch traced here: 83 us
  starting transfers between devices  37 us (44%)
  waiting for transfers between devices  20.5 us (25%)
  Pallas kernels  20.4 us (25%)
  local copies, waits for them, and re-layouts  2.92 us (4%)
  other arithmetic  1.29 us (2%)
  between operations  0.9 us (1%)
    ppermute x17, starting transfers between devices, swap(): lax.ppermute(values, axis, [(i, i ^ flip) for i in range(lax.axis_size(ax...  27.9 us
    ppermute x17, waiting for transfers between devices, swap(): lax.ppermute(values, axis, [(i, i ^ flip) for i in range(lax.axis_size(ax...  20.4 us
    pallas_call x8, Pallas kernels, call(): pl.pallas_call(functools.partial(kernel, **options), out_shape=tuple(outs...  20.4 us
    ppermute x1, starting transfers between devices, on_device(): near = lax.ppermute(rows_half, axes, first)  2.94 us
    unnamed x19, local copies, waits for them, and re-layouts  2.82 us
  transfers between devices with their start and end apart: 24, of which 9 were waited for; matrix products, arithmetic and copies ran while one was open for 1% of the time, Pallas kernels for 18%

profile of v7, /device:TPU:0, one launch (start us, length us, event | category | flops | bytes accessed | tf_op | source)
XLA Modules:
  0.0 83.0 jit_solution(10286690541206781861)
XLA Ops:
  0.6 0.0 copy-start.7
  0.6 0.1 pad_add_fusion.1.place
  0.7 1.1 %copy-done = bf16[512,768]{1,0:T(8,128)(2,1)S(1)} copy-done((bf16[512,768]{1,0:T(8,128)(2,1)S(1)}, bf16[512,768]{1,0:T(8,128)(2,1)}, u32[]{:S(2)}) %copy-start) | copy-done | bytes 786456
  1.9 1.0 %copy-done.2 = bf16[256,768]{1,0:T(8,128)(2,1)S(1)} copy-done((bf16[256,768]{1,0:T(8,128)(2,1)S(1)}, bf16[256,768]{1,0:T(8,128)(2,1)}, u32[]{:S(2)}) %copy-start.2) | copy-done | bytes 393240
  2.9 1.7 %prep.1 = (bf16[400,768]{1,0:T(8,128)(2,1)}, f32[6,128]{1,0:T(8,128)S(1)}) custom-call(s32[3]{0:T(128)S(1)} %pad_add_fusion.1.place, bf16[512,768]{1,0:T(8,128)(2,1)S(1)} %copy-done, bf16[256,768]{1,0:T(8,128)(2,1)S(1)} %copy-done.2), custom_call_target="tpu_custom_call" | custom-call | flops 1 | bytes 1 | tf_op jit(solution)/shard_map/prep/pallas_call | solution.py:263
  4.6 2.9 %collective-permute-start.6 = (bf16[400,768]{1,0:T(8,128)(2,1)}, bf16[400,768]{1,0:T(8,128)(2,1)S(1)}, u32[]{:S(2)}, u32[]{:S(2)}) collective-permute-start(bf16[400,768]{1,0:T(8,128)(2,1)} %get-tuple-element.33), channel_id=1, source_target_pairs={{0,2},{1,5},{2,0},{3,7},{4,6},{5,1},{6,4},{7,3},{8,10},{9,13},{10,... | collective-permute-start | bytes 1843208 | tf_op jit(solution)/shard_map/ppermute | solution.py:346
  7.5 1.5 %collective-permute-start.7 = (bf16[400,768]{1,0:T(8,128)(2,1)}, bf16[400,768]{1,0:T(8,128)(2,1)S(1)}, u32[]{:S(2)}, u32[]{:S(2)}) collective-permute-start(bf16[400,768]{1,0:T(8,128)(2,1)} %get-tuple-element.33), channel_id=1, source_target_pairs={{0,4},{1,3},{2,6},{3,1},{4,0},{5,7},{6,2},{7,5},{8,12},{9,11},{10,... | collective-permute-start | bytes 1843208 | tf_op jit(solution)/shard_map/ppermute | solution.py:347
  9.0 1.6 %collective-permute-start.8 = (bf16[256,768]{1,0:T(8,128)(2,1)}, bf16[256,768]{1,0:T(8,128)(2,1)S(1)}, u32[]{:S(2)}, u32[]{:S(2)}) collective-permute-start(bf16[256,768]{1,0:T(8,128)(2,1)} %refs_0_.4), channel_id=1, source_target_pairs={{0,8},{8,0},{16,24},{24,16},{1,9},{9,1},{17,25},{25,17},{2,10},{10... | collective-permute-start | bytes 1179656 | tf_op jit(solution)/shard_map/ppermute | solution.py:276
  10.6 0.7 collective-permute-start.9
  11.3 4.4 %collective-permute-start = (s32[2560]{0:T(1024)S(1)}, s32[2560]{0:T(1024)S(1)}, u32[]{:S(2)}, u32[]{:S(2)}) collective-permute-start(s32[2560]{0:T(1024)S(1)} %pad_add_fusion), channel_id=1, source_target_pairs={{0,8},{8,0},{16,24},{24,16},{1,9},{9,1},{17,25},{25,17},{2,10},{10... | collective-permute-start | bytes 30728 | tf_op jit(solution)/shard_map/ppermute | solution.py:276
  15.8 4.0 %collective-permute-done = s32[2560]{0:T(1024)S(1)} collective-permute-done((s32[2560]{0:T(1024)S(1)}, s32[2560]{0:T(1024)S(1)}, u32[]{:S(2)}, u32[]{:S(2)}) %collective-permute-start) | collective-permute-done | bytes 10272 | tf_op jit(solution)/shard_map/ppermute | solution.py:276
  19.8 2.6 %collective-permute-start.1 = (s32[2560]{0:T(1024)S(1)}, s32[2560]{0:T(1024)S(1)}, u32[]{:S(2)}, u32[]{:S(2)}) collective-permute-start(s32[2560]{0:T(1024)S(1)} %pad_add_fusion), channel_id=1, source_target_pairs={{0,16},{8,24},{16,0},{24,8},{1,17},{9,25},{17,1},{25,9},{2,18},{10... | collective-permute-start | bytes 30728 | tf_op jit(solution)/shard_map/ppermute | solution.py:276
  22.4 2.0 %collective-permute-done.1 = s32[2560]{0:T(1024)S(1)} collective-permute-done((s32[2560]{0:T(1024)S(1)}, s32[2560]{0:T(1024)S(1)}, u32[]{:S(2)}, u32[]{:S(2)}) %collective-permute-start.1) | collective-permute-done | bytes 10272 | tf_op jit(solution)/shard_map/ppermute | solution.py:276
  24.4 3.8 %collective-permute-start.2 = (s32[2560]{0:T(1024)S(1)}, s32[2560]{0:T(1024)S(1)}, u32[]{:S(2)}, u32[]{:S(2)}) collective-permute-start(s32[2560]{0:T(1024)S(1)} %pad_add_fusion), channel_id=1, source_target_pairs={{0,24},{8,16},{16,8},{24,0},{1,25},{9,17},{17,9},{25,1},{2,26},{10... | collective-permute-start | bytes 30728 | tf_op jit(solution)/shard_map/ppermute | solution.py:276
  28.1 1.7 %collective-permute-done.2 = s32[2560]{0:T(1024)S(1)} collective-permute-done((s32[2560]{0:T(1024)S(1)}, s32[2560]{0:T(1024)S(1)}, u32[]{:S(2)}, u32[]{:S(2)}) %collective-permute-start.2) | collective-permute-done | bytes 10272 | tf_op jit(solution)/shard_map/ppermute | solution.py:276
  29.9 0.0 collective-permute-done.8.refs_0_
  29.9 0.0 collective-permute-done.9.refs_1_
  29.9 0.0 collective-permute-done.6.refs_2_.refs_6_.refs_7_
  29.9 0.0 collective-permute-done.7.refs_4_.refs_8_.refs_9_
  29.9 0.6 collective-permute-start.12
  30.5 0.7 collective-permute-start.13
  31.2 1.3 %collective-permute-start.14 = (bf16[256,768]{1,0:T(8,128)(2,1)S(1)}, bf16[256,768]{1,0:T(8,128)(2,1)S(1)}, u32[]{:S(2)}, u32[]{:S(2)}) collective-permute-start(bf16[256,768]{1,0:T(8,128)(2,1)S(1)} %collective-permute-done.9.refs_1_), channel_id=1, source_target_pairs={{8,0},{16,24},{9,1},{17,25},{10,2},{18,26},{11,3},{19,27},{12,4},{... | collective-permute-start | bytes 1179656 | tf_op jit(solution)/shard_map/ppermute | solution.py:353
  32.5 0.0 copy-start.6
  32.5 0.7 copy-done.6
  33.2 0.5 collective-permute-start.3
  33.6 1.6 %collective-permute-start.4 = (s32[1536]{0:T(1024)S(1)}, s32[1536]{0:T(1024)S(1)}, u32[]{:S(2)}, u32[]{:S(2)}) collective-permute-start(s32[1536]{0:T(1024)S(1)} %constant_dynamic-update-slice_fusion), channel_id=1, source_target_pairs={{0,4},{2,6},{4,0},{6,2},{1,5},{3,7},{5,1},{7,3},{8,12},{10,14},{12... | collective-permute-start | bytes 18440 | tf_op jit(solution)/shard_map/ppermute | solution.py:276
  35.2 1.6 %collective-permute-done.3 = s32[1536]{0:T(1024)S(1)} collective-permute-done((s32[1536]{0:T(1024)S(1)}, s32[1536]{0:T(1024)S(1)}, u32[]{:S(2)}, u32[]{:S(2)}) %collective-permute-start.3) | collective-permute-done | bytes 6176 | tf_op jit(solution)/shard_map/ppermute | solution.py:276
  36.8 1.5 %collective-permute-start.5 = (s32[1536]{0:T(1024)S(1)}, s32[1536]{0:T(1024)S(1)}, u32[]{:S(2)}, u32[]{:S(2)}) collective-permute-start(s32[1536]{0:T(1024)S(1)} %constant_dynamic-update-slice_fusion), channel_id=1, source_target_pairs={{0,6},{2,4},{4,2},{6,0},{1,7},{3,5},{5,3},{7,1},{8,14},{10,12},{12... | collective-permute-start | bytes 18440 | tf_op jit(solution)/shard_map/ppermute | solution.py:276
  38.4 1.9 %collective-permute-done.4 = s32[1536]{0:T(1024)S(1)} collective-permute-done((s32[1536]{0:T(1024)S(1)}, s32[1536]{0:T(1024)S(1)}, u32[]{:S(2)}, u32[]{:S(2)}) %collective-permute-start.4) | collective-permute-done | bytes 6176 | tf_op jit(solution)/shard_map/ppermute | solution.py:276
  40.3 1.1 %collective-permute-done.5 = s32[1536]{0:T(1024)S(1)} collective-permute-done((s32[1536]{0:T(1024)S(1)}, s32[1536]{0:T(1024)S(1)}, u32[]{:S(2)}, u32[]{:S(2)}) %collective-permute-start.5) | collective-permute-done | bytes 6176 | tf_op jit(solution)/shard_map/ppermute | solution.py:276
  41.4 4.0 %meta.1 = (f32[4,3072]{1,0:T(4,128)S(1)}, f32[1,3072]{1,0:T(1,128)S(1)}, s32[1,1024]{1,0:T(1,128)S(1)}, s32[1,1024]{1,0:T(1,128)S(1)}, s32[1,384]{1,0:T(1,128)S(1)}, /*index=5*/s32[1,512]{1,0:T(1,128)S(1)}) custom-call(s32[3]{0:T(128)S(1)} %pad_add_fusion.1.place, s32[1,2560]{1,0:T(1,128)S(1)} %reshape.54.refs_0_, s32[1,2560]{1,0:T(1,128)S(1)} %reshape.55.refs_1_, ...), custom_call_target="tpu_custom_call" | custom-call | flops 1 | bytes 1 | tf_op jit(solution)/shard_map/meta/pallas_call | solution.py:263
  45.4 0.1 collective-permute-start.10
  45.4 0.5 collective-permute-start.11
  45.9 0.0 collective-permute-done.13.refs_1_
  45.9 0.0 collective-permute-done.14.refs_0_
  45.9 0.0 collective-permute-done.12.refs_6_.refs_10_.refs_11_
  45.9 0.1 collective-permute-start.15
  46.1 1.5 %collective-permute-start.19 = (bf16[256,768]{1,0:T(8,128)(2,1)S(1)}, bf16[256,768]{1,0:T(8,128)(2,1)S(1)}, u32[]{:S(2)}, u32[]{:S(2)}) collective-permute-start(bf16[256,768]{1,0:T(8,128)(2,1)S(1)} %collective-permute-done.13.refs_1_), channel_id=1, source_target_pairs={{8,0},{16,24},{9,1},{17,25},{10,2},{18,26},{11,3},{19,27},{12,4},{... | collective-permute-start | bytes 1179656 | tf_op jit(solution)/shard_map/ppermute | solution.py:356
  47.5 0.0 collective-permute-done.10.refs_3_.refs_7_.refs_8_
  47.5 0.8 collective-permute-done.11.refs_5_.refs_9_.refs_10_
  48.3 0.9 %collective-permute-done.15.refs_7_.refs_11_.refs_12_ = bf16[400,768]{1,0:T(8,128)(2,1)S(1)} collective-permute-done((bf16[400,768]{1,0:T(8,128)(2,1)S(1)}, bf16[400,768]{1,0:T(8,128)(2,1)S(1)}, u32[]{:S(2)}, u32[]{:S(2)}) %collective-permute-start.15) | collective-permute-done | bytes 614432 | tf_op jit(solution)/shard_map/ppermute | solution.py:276
  49.2 1.2 %pack.1 = (bf16[192,768]{1,0:T(8,128)(2,1)S(1)}, f32[1,3072]{1,0:T(1,128)S(1)}) custom-call(s32[3]{0:T(128)S(1)} %pad_add_fusion.1.place, s32[1,1024]{1,0:T(1,128)S(1)} %get-tuple-element.40.code, f32[6,128]{1,0:T(8,128)S(1)} %get-tuple-element.41.scale, bf16[512,768]{1,0:T(8,128)(2,1)S(1)} %copy-done.1, bf16[256,768]{1,0:T(8,128)(2,1)S(1)} %copy-done.3, ...), custom_call_target="tpu_custom_call" | custom-call | flops 1 | bytes 1 | tf_op jit(solution)/shard_map/pack/pallas_call | solution.py:263
  50.5 2.7 %collective-permute-start.16 = (bf16[64,768]{1,0:T(8,128)(2,1)S(1)}, bf16[64,768]{1,0:T(8,128)(2,1)S(1)}, u32[]{:S(2)}, u32[]{:S(2)}) collective-permute-start(bf16[64,768]{1,0:T(8,128)(2,1)S(1)} %get-tuple-element.57), channel_id=1, source_target_pairs={{0,8},{8,0},{16,24},{24,16},{1,9},{9,1},{17,25},{25,17},{2,10},{10... | collective-permute-start | bytes 294920 | tf_op jit(solution)/shard_map/ppermute | solution.py:276
  53.2 2.5 %collective-permute-start.17 = (bf16[64,768]{1,0:T(8,128)(2,1)S(1)}, bf16[64,768]{1,0:T(8,128)(2,1)S(1)}, u32[]{:S(2)}, u32[]{:S(2)}) collective-permute-start(bf16[64,768]{1,0:T(8,128)(2,1)S(1)} %get-tuple-element.59), channel_id=1, source_target_pairs={{0,16},{8,24},{16,0},{24,8},{1,17},{9,25},{17,1},{25,9},{2,18},{10... | collective-permute-start | bytes 294920 | tf_op jit(solution)/shard_map/ppermute | solution.py:276
  55.7 1.4 %collective-permute-start.18 = (bf16[64,768]{1,0:T(8,128)(2,1)S(1)}, bf16[64,768]{1,0:T(8,128)(2,1)S(1)}, u32[]{:S(2)}, u32[]{:S(2)}) collective-permute-start(bf16[64,768]{1,0:T(8,128)(2,1)S(1)} %get-tuple-element.58), channel_id=1, source_target_pairs={{0,24},{8,16},{16,8},{24,0},{1,25},{9,17},{17,9},{25,1},{2,26},{10... | collective-permute-start | bytes 294920 | tf_op jit(solution)/shard_map/ppermute | solution.py:276
  57.1 2.5 %score.4 = f32[2,2,128]{2,1,0:T(2,128)S(1)} custom-call(s32[3]{0:T(128)S(1)} %pad_add_fusion.1.place, s32[1,256]{1,0:T(1,128)S(1)} %bitcast.13, bf16[256,768]{1,0:T(8,128)(2,1)S(1)} %collective-permute-done.8.refs_0_, f32[4,3072]{1,0:T(4,128)S(1)} %get-tuple-element.43.refs_1_.refs_2_, f32[1,3072]{1,0:T(1,128)S(1)} %get-tuple-element.44.refs_2_.refs_3_, ...), custom_call_target="tpu_custom_call" | custom-call | flops 1 | bytes 1 | tf_op jit(solution)/shard_map/score/pallas_call | solution.py:263
  59.6 6.5 %collective-permute-done.16 = bf16[64,768]{1,0:T(8,128)(2,1)S(1)} collective-permute-done((bf16[64,768]{1,0:T(8,128)(2,1)S(1)}, bf16[64,768]{1,0:T(8,128)(2,1)S(1)}, u32[]{:S(2)}, u32[]{:S(2)}) %collective-permute-start.16) | collective-permute-done | bytes 98336 | tf_op jit(solution)/shard_map/ppermute | solution.py:276
  66.0 0.0 collective-permute-done.17
  66.0 0.0 collective-permute-done.18
  66.1 0.0 collective-permute-done.19.refs_0_
  66.1 0.1 collective-permute-start.20
  66.2 2.5 %score.5 = f32[2,2,128]{2,1,0:T(2,128)S(1)} custom-call(s32[3]{0:T(128)S(1)} %pad_add_fusion.1.place, s32[1,256]{1,0:T(1,128)S(1)} %bitcast.11, bf16[256,768]{1,0:T(8,128)(2,1)S(1)} %collective-permute-done.14.refs_0_, bf16[256,768]{1,0:T(8,128)(2,1)S(1)} %collective-permute-done.13.refs_1_, f32[4,3072]{1,0:T(4,128)S(1)} %get-tuple-element.43.refs_1_.refs_2_, ...), custom_call_target="tpu_custom_call" | custom-call | flops 1 | bytes 1 | tf_op jit(solution)/shard_map/score/pallas_call | solution.py:263
  68.7 2.0 %collective-permute-start.22 = (f32[2,2,128]{2,1,0:T(2,128)S(1)}, f32[2,2,128]{2,1,0:T(2,128)S(1)}, u32[]{:S(2)}, u32[]{:S(2)}) collective-permute-start(f32[2,2,128]{2,1,0:T(2,128)S(1)} %score.5), channel_id=1, source_target_pairs={{0,16},{8,24},{16,0},{24,8},{1,17},{9,25},{17,1},{25,9},{2,18},{10... | collective-permute-start | bytes 6152 | tf_op jit(solution)/shard_map/ppermute | solution.py:276
  70.7 2.5 %score.6 = f32[2,2,128]{2,1,0:T(2,128)S(1)} custom-call(s32[3]{0:T(128)S(1)} %pad_add_fusion.1.place, s32[1,256]{1,0:T(1,128)S(1)} %bitcast.10, bf16[256,768]{1,0:T(8,128)(2,1)S(1)} %collective-permute-done.19.refs_0_, bf16[256,768]{1,0:T(8,128)(2,1)S(1)} %collective-permute-done.9.refs_1_, f32[4,3072]{1,0:T(4,128)S(1)} %get-tuple-element.43.refs_1_.refs_2_, ...), custom_call_target="tpu_custom_call" | custom-call | flops 1 | bytes 1 | tf_op jit(solution)/shard_map/score/pallas_call | solution.py:263
  73.2 2.0 %collective-permute-start.23 = (f32[2,2,128]{2,1,0:T(2,128)S(1)}, f32[2,2,128]{2,1,0:T(2,128)S(1)}, u32[]{:S(2)}, u32[]{:S(2)}) collective-permute-start(f32[2,2,128]{2,1,0:T(2,128)S(1)} %score.6), channel_id=1, source_target_pairs={{0,24},{8,16},{16,8},{24,0},{1,25},{9,17},{17,9},{25,1},{2,26},{10... | collective-permute-start | bytes 6152 | tf_op jit(solution)/shard_map/ppermute | solution.py:276
  75.2 0.6 collective-permute-start.21
  75.8 0.6 broadcast_select_fusion
  76.4 0.0 collective-permute-done.20.refs_9_
  76.4 2.5 %score.7 = f32[2,2,128]{2,1,0:T(2,128)S(1)} custom-call(s32[3]{0:T(128)S(1)} %pad_add_fusion.1.place, s32[1,256]{1,0:T(1,128)S(1)} %bitcast.12, bf16[256,768]{1,0:T(8,128)(2,1)S(1)} %copy-done.4, f32[4,3072]{1,0:T(4,128)S(1)} %get-tuple-element.43.refs_1_.refs_2_, f32[1,3072]{1,0:T(1,128)S(1)} %get-tuple-element.44.refs_2_.refs_3_, ...), custom_call_target="tpu_custom_call" | custom-call | flops 1 | bytes 1 | tf_op jit(solution)/shard_map/score/pallas_call | solution.py:263
  78.9 0.0 collective-permute-done.22
  79.0 0.0 collective-permute-done.23
  79.0 0.0 collective-permute-done.21
  79.0 0.6 fusion.1
  79.6 3.4 %apply.1 = bf16[512,768]{1,0:T(8,128)(2,1)} custom-call(s32[3]{0:T(128)S(1)} %pad_add_fusion.1.place, s32[1,1024]{1,0:T(1,128)S(1)} %get-tuple-element.30.own_target, s32[1,384]{1,0:T(1,128)S(1)} %get-tuple-element.31.target, s32[1,512]{1,0:T(1,128)S(1)} %get-tuple-element.32.refreshed, bf16[512,768]{1,0:T(8,128)(2,1)S(1)} %copy-done.1, ...), custom_call_target="tpu_custom_call" | custom-call | flops 1 | bytes 1 | tf_op jit(solution)/shard_map/apply/pallas_call | solution.py:263
  (32 shorter events, 0.2 us)
Async XLA Ops:
  0.6 10.6 %copy-start.7 = (s32[1,2048]{1,0:T(1,128)S(1)}, s32[1,2048]{1,0:T(1,128)}, u32[]{:S(2)}) copy-start(s32[1,2048]{1,0:T(1,128)} %param.11) | copy-start | bytes 24580
  0.7 1.1 %copy-start = (bf16[512,768]{1,0:T(8,128)(2,1)S(1)}, bf16[512,768]{1,0:T(8,128)(2,1)}, u32[]{:S(2)}) copy-start(bf16[512,768]{1,0:T(8,128)(2,1)} %refs_4_.3) | copy-start | bytes 2359300
  1.9 1.0 %copy-start.2 = (bf16[256,768]{1,0:T(8,128)(2,1)S(1)}, bf16[256,768]{1,0:T(8,128)(2,1)}, u32[]{:S(2)}) copy-start(bf16[256,768]{1,0:T(8,128)(2,1)} %refs_5_.7) | copy-start | bytes 1179652
  2.9 46.3 %copy-start.1 = (bf16[512,768]{1,0:T(8,128)(2,1)S(1)}, bf16[512,768]{1,0:T(8,128)(2,1)}, u32[]{:S(2)}) copy-start(bf16[512,768]{1,0:T(8,128)(2,1)} %refs_4_.3) | copy-start | bytes 2359300
  2.9 46.3 %copy-start.3 = (bf16[256,768]{1,0:T(8,128)(2,1)S(1)}, bf16[256,768]{1,0:T(8,128)(2,1)}, u32[]{:S(2)}) copy-start(bf16[256,768]{1,0:T(8,128)(2,1)} %refs_5_.7) | copy-start | bytes 1179652
  4.6 6.7 %copy-start.8 = (s32[256]{0:T(256)S(1)}, s32[256]{0:T(256)}, u32[]{:S(2)}) copy-start(s32[256]{0:T(256)} %param.9) | copy-start | bytes 3076
  4.6 6.7 %copy-start.5 = (s32[256]{0:T(256)S(1)}, s32[256]{0:T(256)}, u32[]{:S(2)}) copy-start(s32[256]{0:T(256)} %param.13) | copy-start | bytes 3076
  4.6 25.3 %collective-permute-start.6 = (bf16[400,768]{1,0:T(8,128)(2,1)}, bf16[400,768]{1,0:T(8,128)(2,1)S(1)}, u32[]{:S(2)}, u32[]{:S(2)}) collective-permute-start(bf16[400,768]{1,0:T(8,128)(2,1)} %get-tuple-element.33), channel_id=1, source_target_pairs={{0,2},{1,5},{2,0},{3,7},{4,6},{5,1},{6,4},{7,3},{8,10},{9,13},{10,... | collective-permute-start | bytes 1843208 | tf_op jit(solution)/shard_map/ppermute | solution.py:346
  7.5 22.4 %collective-permute-start.7 = (bf16[400,768]{1,0:T(8,128)(2,1)}, bf16[400,768]{1,0:T(8,128)(2,1)S(1)}, u32[]{:S(2)}, u32[]{:S(2)}) collective-permute-start(bf16[400,768]{1,0:T(8,128)(2,1)} %get-tuple-element.33), channel_id=1, source_target_pairs={{0,4},{1,3},{2,6},{3,1},{4,0},{5,7},{6,2},{7,5},{8,12},{9,11},{10,... | collective-permute-start | bytes 1843208 | tf_op jit(solution)/shard_map/ppermute | solution.py:347
  9.0 20.9 %collective-permute-start.8 = (bf16[256,768]{1,0:T(8,128)(2,1)}, bf16[256,768]{1,0:T(8,128)(2,1)S(1)}, u32[]{:S(2)}, u32[]{:S(2)}) collective-permute-start(bf16[256,768]{1,0:T(8,128)(2,1)} %refs_0_.4), channel_id=1, source_target_pairs={{0,8},{8,0},{16,24},{24,16},{1,9},{9,1},{17,25},{25,17},{2,10},{10... | collective-permute-start | bytes 1179656 | tf_op jit(solution)/shard_map/ppermute | solution.py:276
  10.6 19.3 %collective-permute-start.9 = (bf16[256,768]{1,0:T(8,128)(2,1)}, bf16[256,768]{1,0:T(8,128)(2,1)S(1)}, u32[]{:S(2)}, u32[]{:S(2)}) collective-permute-start(bf16[256,768]{1,0:T(8,128)(2,1)} %refs_0_.4), channel_id=1, source_target_pairs={{8,16},{16,8},{9,17},{17,9},{10,18},{18,10},{11,19},{19,11},{12,20... | collective-permute-start | bytes 1179656 | tf_op jit(solution)/shard_map/ppermute | solution.py:350
  11.3 8.5 %collective-permute-start = (s32[2560]{0:T(1024)S(1)}, s32[2560]{0:T(1024)S(1)}, u32[]{:S(2)}, u32[]{:S(2)}) collective-permute-start(s32[2560]{0:T(1024)S(1)} %pad_add_fusion), channel_id=1, source_target_pairs={{0,8},{8,0},{16,24},{24,16},{1,9},{9,1},{17,25},{25,17},{2,10},{10... | collective-permute-start | bytes 30728 | tf_op jit(solution)/shard_map/ppermute | solution.py:276
  19.8 4.6 %collective-permute-start.1 = (s32[2560]{0:T(1024)S(1)}, s32[2560]{0:T(1024)S(1)}, u32[]{:S(2)}, u32[]{:S(2)}) collective-permute-start(s32[2560]{0:T(1024)S(1)} %pad_add_fusion), channel_id=1, source_target_pairs={{0,16},{8,24},{16,0},{24,8},{1,17},{9,25},{17,1},{25,9},{2,18},{10... | collective-permute-start | bytes 30728 | tf_op jit(solution)/shard_map/ppermute | solution.py:276
  24.4 5.5 %collective-permute-start.2 = (s32[2560]{0:T(1024)S(1)}, s32[2560]{0:T(1024)S(1)}, u32[]{:S(2)}, u32[]{:S(2)}) collective-permute-start(s32[2560]{0:T(1024)S(1)} %pad_add_fusion), channel_id=1, source_target_pairs={{0,24},{8,16},{16,8},{24,0},{1,25},{9,17},{17,9},{25,1},{2,26},{10... | collective-permute-start | bytes 30728 | tf_op jit(solution)/shard_map/ppermute | solution.py:276
  29.9 16.0 %collective-permute-start.12 = (bf16[400,768]{1,0:T(8,128)(2,1)S(1)}, bf16[400,768]{1,0:T(8,128)(2,1)S(1)}, u32[]{:S(2)}, u32[]{:S(2)}) collective-permute-start(bf16[400,768]{1,0:T(8,128)(2,1)S(1)} %collective-permute-done.6.refs_2_.refs_6_.refs_7_), channel_id=1, source_target_pairs={{0,4},{1,3},{2,6},{3,1},{4,0},{5,7},{6,2},{7,5},{8,12},{9,11},{10,... | collective-permute-start | bytes 1843208 | tf_op jit(solution)/shard_map/ppermute | solution.py:354
  30.5 15.4 %collective-permute-start.13 = (bf16[256,768]{1,0:T(8,128)(2,1)S(1)}, bf16[256,768]{1,0:T(8,128)(2,1)S(1)}, u32[]{:S(2)}, u32[]{:S(2)}) collective-permute-start(bf16[256,768]{1,0:T(8,128)(2,1)S(1)} %collective-permute-done.8.refs_0_), channel_id=1, source_target_pairs={{8,16},{16,8},{9,17},{17,9},{10,18},{18,10},{11,19},{19,11},{12,20... | collective-permute-start | bytes 1179656 | tf_op jit(solution)/shard_map/ppermute | solution.py:352
  31.2 14.8 %collective-permute-start.14 = (bf16[256,768]{1,0:T(8,128)(2,1)S(1)}, bf16[256,768]{1,0:T(8,128)(2,1)S(1)}, u32[]{:S(2)}, u32[]{:S(2)}) collective-permute-start(bf16[256,768]{1,0:T(8,128)(2,1)S(1)} %collective-permute-done.9.refs_1_), channel_id=1, source_target_pairs={{8,0},{16,24},{9,1},{17,25},{10,2},{18,26},{11,3},{19,27},{12,4},{... | collective-permute-start | bytes 1179656 | tf_op jit(solution)/shard_map/ppermute | solution.py:353
  32.5 0.7 copy-start.6
  33.2 3.7 %collective-permute-start.3 = (s32[1536]{0:T(1024)S(1)}, s32[1536]{0:T(1024)S(1)}, u32[]{:S(2)}, u32[]{:S(2)}) collective-permute-start(s32[1536]{0:T(1024)S(1)} %constant_dynamic-update-slice_fusion), channel_id=1, source_target_pairs={{0,2},{2,0},{4,6},{6,4},{1,3},{3,1},{5,7},{7,5},{8,10},{10,8},{12,... | collective-permute-start | bytes 18440 | tf_op jit(solution)/shard_map/ppermute | solution.py:276
  33.6 6.7 %collective-permute-start.4 = (s32[1536]{0:T(1024)S(1)}, s32[1536]{0:T(1024)S(1)}, u32[]{:S(2)}, u32[]{:S(2)}) collective-permute-start(s32[1536]{0:T(1024)S(1)} %constant_dynamic-update-slice_fusion), channel_id=1, source_target_pairs={{0,4},{2,6},{4,0},{6,2},{1,5},{3,7},{5,1},{7,3},{8,12},{10,14},{12... | collective-permute-start | bytes 18440 | tf_op jit(solution)/shard_map/ppermute | solution.py:276
  36.8 4.5 %collective-permute-start.5 = (s32[1536]{0:T(1024)S(1)}, s32[1536]{0:T(1024)S(1)}, u32[]{:S(2)}, u32[]{:S(2)}) collective-permute-start(s32[1536]{0:T(1024)S(1)} %constant_dynamic-update-slice_fusion), channel_id=1, source_target_pairs={{0,6},{2,4},{4,2},{6,0},{1,7},{3,5},{5,3},{7,1},{8,14},{10,12},{12... | collective-permute-start | bytes 18440 | tf_op jit(solution)/shard_map/ppermute | solution.py:276
  45.4 2.2 %collective-permute-start.10 = (bf16[400,768]{1,0:T(8,128)(2,1)S(1)}, bf16[400,768]{1,0:T(8,128)(2,1)S(1)}, u32[]{:S(2)}, u32[]{:S(2)}) collective-permute-start(bf16[400,768]{1,0:T(8,128)(2,1)S(1)} %collective-permute-done.6.refs_2_.refs_6_.refs_7_), channel_id=1, source_target_pairs={{0,1},{1,0},{2,3},{3,2},{4,5},{5,4},{6,7},{7,6},{8,9},{9,8},{10,11... | collective-permute-start | bytes 1843208 | tf_op jit(solution)/shard_map/ppermute | solution.py:276
  45.4 2.9 %collective-permute-start.11 = (bf16[400,768]{1,0:T(8,128)(2,1)S(1)}, bf16[400,768]{1,0:T(8,128)(2,1)S(1)}, u32[]{:S(2)}, u32[]{:S(2)}) collective-permute-start(bf16[400,768]{1,0:T(8,128)(2,1)S(1)} %collective-permute-done.7.refs_4_.refs_8_.refs_9_), channel_id=1, source_target_pairs={{0,1},{1,0},{2,3},{3,2},{4,5},{5,4},{6,7},{7,6},{8,9},{9,8},{10,11... | collective-permute-start | bytes 1843208 | tf_op jit(solution)/shard_map/ppermute | solution.py:276
  45.9 3.3 %collective-permute-start.15 = (bf16[400,768]{1,0:T(8,128)(2,1)S(1)}, bf16[400,768]{1,0:T(8,128)(2,1)S(1)}, u32[]{:S(2)}, u32[]{:S(2)}) collective-permute-start(bf16[400,768]{1,0:T(8,128)(2,1)S(1)} %collective-permute-done.12.refs_6_.refs_10_.refs_11_), channel_id=1, source_target_pairs={{0,1},{1,0},{2,3},{3,2},{4,5},{5,4},{6,7},{7,6},{8,9},{9,8},{10,11... | collective-permute-start | bytes 1843208 | tf_op jit(solution)/shard_map/ppermute | solution.py:276
  46.1 20.0 %collective-permute-start.19 = (bf16[256,768]{1,0:T(8,128)(2,1)S(1)}, bf16[256,768]{1,0:T(8,128)(2,1)S(1)}, u32[]{:S(2)}, u32[]{:S(2)}) collective-permute-start(bf16[256,768]{1,0:T(8,128)(2,1)S(1)} %collective-permute-done.13.refs_1_), channel_id=1, source_target_pairs={{8,0},{16,24},{9,1},{17,25},{10,2},{18,26},{11,3},{19,27},{12,4},{... | collective-permute-start | bytes 1179656 | tf_op jit(solution)/shard_map/ppermute | solution.py:356
  50.5 15.5 %collective-permute-start.16 = (bf16[64,768]{1,0:T(8,128)(2,1)S(1)}, bf16[64,768]{1,0:T(8,128)(2,1)S(1)}, u32[]{:S(2)}, u32[]{:S(2)}) collective-permute-start(bf16[64,768]{1,0:T(8,128)(2,1)S(1)} %get-tuple-element.57), channel_id=1, source_target_pairs={{0,8},{8,0},{16,24},{24,16},{1,9},{9,1},{17,25},{25,17},{2,10},{10... | collective-permute-start | bytes 294920 | tf_op jit(solution)/shard_map/ppermute | solution.py:276
  53.2 12.8 %collective-permute-start.17 = (bf16[64,768]{1,0:T(8,128)(2,1)S(1)}, bf16[64,768]{1,0:T(8,128)(2,1)S(1)}, u32[]{:S(2)}, u32[]{:S(2)}) collective-permute-start(bf16[64,768]{1,0:T(8,128)(2,1)S(1)} %get-tuple-element.59), channel_id=1, source_target_pairs={{0,16},{8,24},{16,0},{24,8},{1,17},{9,25},{17,1},{25,9},{2,18},{10... | collective-permute-start | bytes 294920 | tf_op jit(solution)/shard_map/ppermute | solution.py:276
  55.7 10.3 %collective-permute-start.18 = (bf16[64,768]{1,0:T(8,128)(2,1)S(1)}, bf16[64,768]{1,0:T(8,128)(2,1)S(1)}, u32[]{:S(2)}, u32[]{:S(2)}) collective-permute-start(bf16[64,768]{1,0:T(8,128)(2,1)S(1)} %get-tuple-element.58), channel_id=1, source_target_pairs={{0,24},{8,16},{16,8},{24,0},{1,25},{9,17},{17,9},{25,1},{2,26},{10... | collective-permute-start | bytes 294920 | tf_op jit(solution)/shard_map/ppermute | solution.py:276
  66.1 10.4 %collective-permute-start.20 = (bf16[192,768]{1,0:T(8,128)(2,1)S(1)}, bf16[192,768]{1,0:T(8,128)(2,1)S(1)}, u32[]{:S(2)}, u32[]{:S(2)}) collective-permute-start(bf16[192,768]{1,0:T(8,128)(2,1)S(1)} %pad_maximum_fusion.refs_8_), channel_id=1, source_target_pairs={{0,1},{1,0},{2,3},{3,2},{4,5},{5,4},{6,7},{7,6},{8,9},{9,8},{10,11... | collective-permute-start | bytes 884744 | tf_op jit(solution)/shard_map/ppermute | solution.py:276
  68.7 10.2 %collective-permute-start.22 = (f32[2,2,128]{2,1,0:T(2,128)S(1)}, f32[2,2,128]{2,1,0:T(2,128)S(1)}, u32[]{:S(2)}, u32[]{:S(2)}) collective-permute-start(f32[2,2,128]{2,1,0:T(2,128)S(1)} %score.5), channel_id=1, source_target_pairs={{0,16},{8,24},{16,0},{24,8},{1,17},{9,25},{17,1},{25,9},{2,18},{10... | collective-permute-start | bytes 6152 | tf_op jit(solution)/shard_map/ppermute | solution.py:276
  70.7 5.7 %copy-start.4 = (bf16[256,768]{1,0:T(8,128)(2,1)S(1)}, bf16[256,768]{1,0:T(8,128)(2,1)}, u32[]{:S(2)}) copy-start(bf16[256,768]{1,0:T(8,128)(2,1)} %refs_0_.4) | copy-start | bytes 1179652
  73.2 5.7 %collective-permute-start.23 = (f32[2,2,128]{2,1,0:T(2,128)S(1)}, f32[2,2,128]{2,1,0:T(2,128)S(1)}, u32[]{:S(2)}, u32[]{:S(2)}) collective-permute-start(f32[2,2,128]{2,1,0:T(2,128)S(1)} %score.6), channel_id=1, source_target_pairs={{0,24},{8,16},{16,8},{24,0},{1,25},{9,17},{17,9},{25,1},{2,26},{10... | collective-permute-start | bytes 6152 | tf_op jit(solution)/shard_map/ppermute | solution.py:276
  75.2 3.7 %collective-permute-start.21 = (f32[2,2,128]{2,1,0:T(2,128)S(1)}, f32[2,2,128]{2,1,0:T(2,128)S(1)}, u32[]{:S(2)}, u32[]{:S(2)}) collective-permute-start(f32[2,2,128]{2,1,0:T(2,128)S(1)} %score.4), channel_id=1, source_target_pairs={{0,8},{8,0},{16,24},{24,16},{1,9},{9,1},{17,25},{25,17},{2,10},{10... | collective-permute-start | bytes 6152 | tf_op jit(solution)/shard_map/ppermute | solution.py:276

commit v8 on v7

--- a/solution.py
+++ b/solution.py
@@ -45,8 +45,9 @@
     return values.astype(jnp.float32).astype(jnp.bfloat16)
 
 
-def prep_kernel(place, table, fresh, rows_out, scale_out, *, replicas, encode):
+def prep_kernel(place, table, fresh, *refs, replicas, encode):
     core = place[2]
+    rows_out, scale_out = refs[-2:]
     width = table.shape[1]
     line, row = 0, 0
     halves = []
@@ -73,13 +74,43 @@
             terms += split_terms(scale_out[pl.ds(first + core * count + i, 1), :])
         for i, term in enumerate(terms):
             rows_out[row + i : row + i + 1, :LANES] = term
-
-
-def meta_kernel(place, *refs, planes, owners_plane, sizes, cap, replicas):
+        *ids, ages = refs[:-2]
+        ids = jnp.concatenate([one[...] for one in ids], axis=1)
+        for at, values in ((9, ids >> 7), (11, ids & 127), (13, ages[...])):
+            for i, left in enumerate(range(0, values.shape[1], width)):
+                part = small(values[:, left : left + width])
+                rows_out[row + at + i : row + at + i + 1, : part.shape[1]] = part
+
+
+def unpacked(rows, first, id_count, age_count):
+    width = rows.shape[1]
+
+    def read(at, count):
+        parts = [number(rows[first + at + i : first + at + i + 1, :]) for i in range(-(-count // width))]
+        return jnp.concatenate(parts, axis=1)[:, :count]
+
+    return read(9, id_count) * LANES + read(11, id_count), read(13, age_count)
+
+
+def number(values):
+    return values.astype(jnp.float32).astype(jnp.int32)
+
+
+def meta_kernel(place, *refs, planes, owners_plane, sizes, cap, replicas, extra):
     outer, inner, core = place[0], place[1], place[2]
-    lines, sides = refs[:planes], refs[planes : planes + owners_plane]
-    lw_out, row_out, code_out, own_target_out, target_out, own_out = refs[planes + owners_plane :]
     refresh_dev, rows_dev, list_size = sizes
+    all_refs = planes * refresh_dev
+    lines, own_ages = refs[:planes], refs[planes]
+    sides = refs[planes + 1 : planes + owners_plane]
+    lw_out, row_out, code_out, own_target_out, target_out, own_out, ages_out = refs[planes + owners_plane :]
+    if extra:
+        near, beside, far = [unpacked(side, extra, all_refs, rows_dev) for side in sides]
+        swapped = [(jnp.where(core == 0, a, b), jnp.where(core == 0, b, a)) for a, b in zip(near, beside)]
+        sides = [tuple(pair[0] for pair in swapped), tuple(pair[1] for pair in swapped), far]
+    else:
+        sides = [(side[:, :all_refs], side[:, all_refs:]) for side in sides]
+    own_ids = jnp.concatenate([line[:, :refresh_dev] for line in lines], axis=1)
+    sides = [(own_ids, own_ages[...]), *sides]
     share = cap // replicas
     plane_rows = owners_plane * rows_dev
     high_count = planes * plane_rows // LANES
@@ -97,21 +128,21 @@
         return jnp.sum(hit * pair[1].astype(jnp.float32), axis=0, keepdims=True) > 0.5
 
     def ref_ids(plane, side):
-        return sides[side][:, plane * refresh_dev : (plane + 1) * refresh_dev]
-
-    all_refs = planes * refresh_dev
+        return sides[side][0][:, plane * refresh_dev : (plane + 1) * refresh_dev]
+
     plane_ids = jnp.concatenate([ref_ids(0, side) for side in range(owners_plane)], axis=1)
-    refreshed_map = bitmap(jnp.concatenate([side[:, :all_refs] for side in sides], axis=1))
+    refreshed_map = bitmap(jnp.concatenate([side[0] for side in sides], axis=1))
     column = lax.broadcasted_iota(jnp.int32, (1, plane_rows), 1)
     table_ids = (outer * owners_plane + (inner ^ (column // rows_dev))) * rows_dev + column % rows_dev
     table_hots, fresh_hots = one_hots(table_ids), one_hots(plane_ids)
 
-    ages = jnp.concatenate([side[:, all_refs:] for side in sides], axis=1).astype(jnp.float32)
+    ages = jnp.concatenate([side[1] for side in sides], axis=1).astype(jnp.float32)
     weight = jnp.exp(-ages / age_scale).astype(jnp.bfloat16).astype(jnp.float32)
     refreshed = lookup(refreshed_map, table_hots)
     row_out[:, :plane_rows] = jnp.where(refreshed, -1, table_ids).astype(jnp.float32)
     row_out[:, plane_rows:] = plane_ids.astype(jnp.float32)
     own_out[...] = refreshed[:, :rows_dev].astype(jnp.int32)
+    ages_out[...] = jnp.where(refreshed[:, :rows_dev], 0, own_ages[...])
     log_weight = jnp.where(refreshed, MASKED, jnp.log2(weight))
     for group in range(planes):
         one_map = bitmap(lines[group][:, refresh_dev : refresh_dev + list_size])
@@ -159,11 +190,12 @@
 
 def pack_kernel(place, code, scale, *refs, pieces, all_pieces):
     *buffers, out, scale_out = refs
-    total = jnp.zeros(out.shape, jnp.float32)
-    for source, start, size, column, _ in pieces:
-        select = one_hot(code[:, pl.ds(piece_offset(place, column), size)], out.shape[0])
-        total += lax.dot_general(select, buffers[source][start : start + size, :], NN, preferred_element_type=jnp.float32)
-    out[...] = total.astype(jnp.bfloat16)
+    selects = [
+        one_hot(code[:, pl.ds(piece_offset(place, column), size)], out.shape[0]) for _, _, size, column, _ in pieces
+    ]
+    values = [buffers[source][start : start + size, :] for source, start, size, _, _ in pieces]
+    select, values = jnp.concatenate(selects, axis=1), jnp.concatenate(values, axis=0)
+    out[...] = lax.dot_general(select, values, NN, preferred_element_type=jnp.float32).astype(jnp.bfloat16)
     for source, start, size, column, scale_at in all_pieces:
         first = piece_offset(place, column)
         for chunk in range(size // LANES):
@@ -179,19 +211,13 @@
 def apply_kernel(place, own_target, target, refreshed, table, *refs, pieces, arrivals):
     out = refs[-1]
     buffers, arrived = refs[: -1 - arrivals], refs[-1 - arrivals : -1]
-    parts = [
-        (own_target[:, pl.ds(piece_offset(place, column), size)], buffers[source][start : start + size, :])
-        for source, start, size, column, _ in pieces
-    ]
-    first = 0
-    for block in arrived:
-        parts.append((target[:, first : first + block.shape[0]], block[...]))
-        first += block.shape[0]
-    fresh = jnp.zeros(out.shape, jnp.float32)
-    for to_row, values in parts:
-        rows = lax.broadcasted_iota(jnp.int32, (out.shape[0], to_row.shape[1]), 0)
-        chosen = jnp.where(rows == to_row, 1.0, 0.0).astype(jnp.bfloat16)
-        fresh += lax.dot_general(chosen, values, NN, preferred_element_type=jnp.float32)
+    to_rows = [own_target[:, pl.ds(piece_offset(place, column), size)] for _, _, size, column, _ in pieces]
+    values = [buffers[source][start : start + size, :] for source, start, size, _, _ in pieces]
+    to_row = jnp.concatenate([*to_rows, target[...]], axis=1)
+    values = jnp.concatenate([*values, *[block[...] for block in arrived]], axis=0)
+    rows = lax.broadcasted_iota(jnp.int32, (out.shape[0], to_row.shape[1]), 0)
+    chosen = jnp.where(rows == to_row, 1.0, 0.0).astype(jnp.bfloat16)
+    fresh = lax.dot_general(chosen, values, NN, preferred_element_type=jnp.float32)
     for top in range(0, out.shape[0], LANES):
         part = slice(top, top + LANES)
         hit = to_lanes(refreshed[:, part].astype(jnp.float32)) > 0.5
@@ -296,9 +322,9 @@
 
     line = jnp.concatenate([refresh_ids, neg_ids[0], pos_ids])
     lines = [line] + [swap(line, "outer", s) for s in range(1, planes)]
-    side = jnp.concatenate([one[:refresh_dev] for one in lines] + [ages])
-    sides = [side] + [swap(side, "inner", s) for s in range(1, owners_plane)]
     positive = [one[refresh_dev + list_size :].reshape(1, -1) for one in lines]
+    ref_lines = [one[:refresh_dev].reshape(1, -1) for one in lines]
+    own_ages = ages.reshape(1, -1)
 
     fast = replicas == 2 and owners_plane == 4 and planes == 4
     extra = 16 if fast else 0
@@ -312,33 +338,13 @@
         place,
         table,
         fresh_rows,
+        *(ref_lines if fast else []),
+        own_ages,
         replicas=replicas,
         encode=fast,
     )
 
     others = (planes - 1) * owners_plane
-    lw, row_ids, code, own_target, target, own = call(
-        meta_kernel,
-        "meta",
-        [
-            jax.ShapeDtypeStruct((planes, all_rows), f32),
-            jax.ShapeDtypeStruct((1, all_rows), f32),
-            jax.ShapeDtypeStruct((1, plane_refresh), jnp.int32),
-            jax.ShapeDtypeStruct((1, plane_refresh), jnp.int32),
-            jax.ShapeDtypeStruct((1, others * cap), jnp.int32),
-            jax.ShapeDtypeStruct((1, rows_dev), jnp.int32),
-        ],
-        place,
-        *[one.reshape(1, -1) for one in lines],
-        *[one.reshape(1, -1) for one in sides],
-        planes=planes,
-        owners_plane=owners_plane,
-        sizes=(refresh_dev, rows_dev, list_size),
-        cap=cap,
-        replicas=replicas,
-    )
-    new_ages = jnp.where(own.reshape(rows_dev) > 0, 0, ages)
-
     if fast:
         axes = ("inner", "query")
         first = [(2 * i + c, 2 * (i ^ (1 + c)) + c) for i in range(4) for c in range(2)]
@@ -348,11 +354,12 @@
         middle, outward = [(1, 2), (2, 1)], [(1, 0), (2, 3)]
         beside = swap(queries, "outer", 1)
         across = lax.ppermute(queries, "outer", middle)
-        near, side_rows, beside, across, *lines = lax.optimization_barrier((near, side_rows, beside, across, *lines))
+        near, side_rows, beside, across = lax.optimization_barrier((near, side_rows, beside, across))
         from_end = lax.ppermute(beside, "outer", middle)
         to_end = lax.ppermute(across, "outer", outward)
         far = lax.ppermute(near, axes, second)
-        far, from_end, to_end, lw = lax.optimization_barrier((far, from_end, to_end, lw))
+        far, from_end, to_end = lax.optimization_barrier((far, from_end, to_end))
+        sides = [near, side_rows, far]
         last = lax.ppermute(from_end, "outer", outward)
         got_queries = [(queries,), (beside,), (to_end, from_end), (last, across)]
         buffers = [table, fresh_rows]
@@ -370,6 +377,8 @@
                 buffers.append(rows)
     else:
         got_queries = [(queries,)] + [(swap(queries, "outer", s),) for s in range(1, planes)]
+        side = jnp.concatenate([*[one[0] for one in ref_lines], ages])
+        sides = [swap(side, "inner", s).reshape(1, -1) for s in range(1, owners_plane)]
         got_rows = [rows_half] + [swap(rows_half, "inner", s) for s in range(1, owners_plane)]
         gathered = lax.all_gather(jnp.stack(got_rows), "query", axis=0)
         gathered = jnp.swapaxes(gathered, 0, 1)
@@ -390,6 +399,31 @@
 
         table_pieces = blocks(0, plane_rows, 0)
         fresh_pieces = blocks(1, plane_refresh, plane_rows // LANES)
+
+    lw, row_ids, code, own_target, target, own, new_ages = call(
+        meta_kernel,
+        "meta",
+        [
+            jax.ShapeDtypeStruct((planes, all_rows), f32),
+            jax.ShapeDtypeStruct((1, all_rows), f32),
+            jax.ShapeDtypeStruct((1, plane_refresh), jnp.int32),
+            jax.ShapeDtypeStruct((1, plane_refresh), jnp.int32),
+            jax.ShapeDtypeStruct((1, others * cap), jnp.int32),
+            jax.ShapeDtypeStruct((1, rows_dev), jnp.int32),
+            jax.ShapeDtypeStruct((1, rows_dev), jnp.int32),
+        ],
+        place,
+        *[one.reshape(1, -1) for one in lines],
+        own_ages,
+        *sides,
+        planes=planes,
+        owners_plane=owners_plane,
+        sizes=(refresh_dev, rows_dev, list_size),
+        cap=cap,
+        replicas=replicas,
+        extra=table_half + fresh_half if fast else 0,
+    )
+    new_ages = new_ages.reshape(rows_dev)
 
     def shift(pieces, columns):
         return [(a, b, c, (d[0] + columns, *d[1:]), e) for a, b, c, d, e in pieces]
@@ -428,16 +462,14 @@
         )
         return partial
 
-    first = score(1, got_queries[1])
+    first, own_part = score(1, got_queries[1]), score(0, got_queries[0])
     late = [one for group in got_queries[2:] for one in group]
-    came, first, *late = lax.optimization_barrier((came, first, *late))
+    came, first, own_part, *late = lax.optimization_barrier((came, first, own_part, *late))
     arrived = [came] + [swap(came, "query", flip) for flip in range(1, replicas)]
-    mine = swap(first, "outer", 1)
+    mine = own_part + swap(first, "outer", 1)
     each = len(late) // (planes - 2)
     for s in range(2, planes):
         mine = mine + swap(score(s, late[(s - 2) * each : (s - 1) * each]), "outer", s)
-    own_queries, *arrived = lax.optimization_barrier((queries, *arrived))
-    mine = mine + score(0, [own_queries])
     (new_table,) = call(
         apply_kernel,
         "apply",
@@ -452,6 +484,7 @@
         pieces=fresh_pieces,
         arrivals=len(arrived),
     )
+    mine, new_table = lax.optimization_barrier((mine, new_table))
     loss = (jnp.log2(mine[0]) - mine[1]) * math.log(2.0)
     return new_table, new_ages, loss.reshape(query_count)
 

time: 83.2 us -> 81.3 us (0.977)
  starting transfers between devices: 37 us -> 25 us
  waiting for transfers between devices: 20.5 us -> 30.2 us
  local copies, waits for them, and re-layouts: 2.92 us -> 4.23 us
  Pallas kernels: 20.4 us -> 19.3 us
    ppermute x1, waiting for transfers between devices: 0.01 us -> 10.8 us  [on_device(): to_end = lax.ppermute(across, 'outer', outward)]
    ppermute x17 -> x14, starting transfers between devices: 27.9 us -> 17.3 us  [swap(): lax.ppermute(values, axis, [(i, i ^ flip) for i in range(lax.axis_size(ax...]
    ppermute x17 -> x14, waiting for transfers between devices: 20.4 us -> 15.8 us  [swap(): lax.ppermute(values, axis, [(i, i ^ flip) for i in range(lax.axis_size(ax...]
    ppermute x1, waiting for transfers between devices: 0.01 us -> 3.52 us  [on_device(): near = lax.ppermute(rows_half, axes, first)]
    ppermute x1, starting transfers between devices: 2.94 us -> 1.56 us  [on_device(): near = lax.ppermute(rows_half, axes, first)]
    unnamed x19 -> x14, local copies, waits for them, and re-layouts: 2.82 us -> 4.17 us
    pallas_call x8, Pallas kernels: 20.4 us -> 19.3 us  [call(): pl.pallas_call(functools.partial(kernel, **options), out_shape=tuple(outs...]
  transfers between devices with their start and end apart: 24 -> 21, of which waited for: 9 -> 8; matrix products, arithmetic and copies ran while one was open for 1% -> 0% of each run, Pallas kernels for 18% -> 19%
where the time goes in v8:
time: 81.3 us; the launch traced here: 80.9 us
  waiting for transfers between devices  30.2 us (37%)
  starting transfers between devices  25 us (31%)
  Pallas kernels  19.3 us (24%)
  local copies, waits for them, and re-layouts  4.23 us (5%)
  other arithmetic  1.39 us (2%)
  between operations  0.82 us (1%)
    pallas_call x8, Pallas kernels, call(): pl.pallas_call(functools.partial(kernel, **options), out_shape=tuple(outs...  19.3 us
    ppermute x14, starting transfers between devices, swap(): lax.ppermute(values, axis, [(i, i ^ flip) for i in range(lax.axis_size(ax...  17.3 us
    ppermute x14, waiting for transfers between devices, swap(): lax.ppermute(values, axis, [(i, i ^ flip) for i in range(lax.axis_size(ax...  15.8 us
    ppermute x1, waiting for transfers between devices, on_device(): to_end = lax.ppermute(across, 'outer', outward)  10.8 us
    unnamed x14, local copies, waits for them, and re-layouts  4.17 us
    ppermute x1, waiting for transfers between devices, on_device(): near = lax.ppermute(rows_half, axes, first)  3.52 us
  transfers between devices with their start and end apart: 21, of which 8 were waited for; matrix products, arithmetic and copies ran while one was open for 0% of the time, Pallas kernels for 19%

profile of v8, /device:TPU:0, one launch (start us, length us, event | category | flops | bytes accessed | tf_op | source)
XLA Modules:
  0.0 80.9 jit_solution(9560886978773793939)
XLA Ops:
  0.6 0.0 copy-start.5
  0.6 0.7 copy-done.5
  1.3 0.7 pad_add_fusion
  2.0 5.0 %collective-permute-start.2 = (s32[2560]{0:T(1024)S(1)}, s32[2560]{0:T(1024)S(1)}, u32[]{:S(2)}, u32[]{:S(2)}) collective-permute-start(s32[2560]{0:T(1024)S(1)} %pad_add_fusion), channel_id=1, source_target_pairs={{0,24},{8,16},{16,8},{24,0},{1,25},{9,17},{17,9},{25,1},{2,26},{10... | collective-permute-start | bytes 30728 | tf_op jit(solution)/shard_map/ppermute | solution.py:302
  7.1 0.0 collective-permute-start
  7.1 0.6 collective-permute-start.1
  7.7 0.1 pad_add_fusion.1.place
  7.8 1.0 %collective-permute-done.2 = s32[2560]{0:T(1024)S(1)} collective-permute-done((s32[2560]{0:T(1024)S(1)}, s32[2560]{0:T(1024)S(1)}, u32[]{:S(2)}, u32[]{:S(2)}) %collective-permute-start.2) | collective-permute-done | bytes 10272 | tf_op jit(solution)/shard_map/ppermute | solution.py:302
  8.8 2.0 %collective-permute-done = s32[2560]{0:T(1024)S(1)} collective-permute-done((s32[2560]{0:T(1024)S(1)}, s32[2560]{0:T(1024)S(1)}, u32[]{:S(2)}, u32[]{:S(2)}) %collective-permute-start) | collective-permute-done | bytes 10272 | tf_op jit(solution)/shard_map/ppermute | solution.py:302
  10.8 0.9 %collective-permute-done.1 = s32[2560]{0:T(1024)S(1)} collective-permute-done((s32[2560]{0:T(1024)S(1)}, s32[2560]{0:T(1024)S(1)}, u32[]{:S(2)}, u32[]{:S(2)}) %collective-permute-start.1) | collective-permute-done | bytes 10272 | tf_op jit(solution)/shard_map/ppermute | solution.py:302
  11.7 0.0 copy-start.4
  11.7 0.7 copy-done.4
  12.4 1.1 %copy-done = bf16[512,768]{1,0:T(8,128)(2,1)S(1)} copy-done((bf16[512,768]{1,0:T(8,128)(2,1)S(1)}, bf16[512,768]{1,0:T(8,128)(2,1)}, u32[]{:S(2)}) %copy-start) | copy-done | bytes 786456
  13.5 1.0 %copy-done.2 = bf16[256,768]{1,0:T(8,128)(2,1)S(1)} copy-done((bf16[256,768]{1,0:T(8,128)(2,1)S(1)}, bf16[256,768]{1,0:T(8,128)(2,1)}, u32[]{:S(2)}) %copy-start.2) | copy-done | bytes 393240
  14.5 0.9 %prep.1 = (bf16[400,768]{1,0:T(8,128)(2,1)S(1)}, f32[6,128]{1,0:T(8,128)S(1)}) custom-call(s32[3]{0:T(128)S(1)} %pad_add_fusion.1.place, bf16[512,768]{1,0:T(8,128)(2,1)S(1)} %copy-done, bf16[256,768]{1,0:T(8,128)(2,1)S(1)} %copy-done.2, s32[1,256]{1,0:T(1,128)S(1)} %bitcast.20, s32[1,256]{1,0:T(1,128)S(1)} %bitcast.22, s32[1,256]{1,0:T(1,128)S(1)} %bitcast.23, ...), custom_call_target="tpu_custom_call" | custom-call | flops 1 | bytes 1 | tf_op jit(solution)/shard_map/prep/pallas_call | solution.py:289
  15.4 1.6 %collective-permute-start.3 = (bf16[400,768]{1,0:T(8,128)(2,1)S(1)}, bf16[400,768]{1,0:T(8,128)(2,1)S(1)}, u32[]{:S(2)}, u32[]{:S(2)}) collective-permute-start(bf16[400,768]{1,0:T(8,128)(2,1)S(1)} %get-tuple-element.30), channel_id=1, source_target_pairs={{0,2},{1,5},{2,0},{3,7},{4,6},{5,1},{6,4},{7,3},{8,10},{9,13},{10,... | collective-permute-start | bytes 1843208 | tf_op jit(solution)/shard_map/ppermute | solution.py:352
  16.9 1.5 %collective-permute-start.4 = (bf16[400,768]{1,0:T(8,128)(2,1)S(1)}, bf16[400,768]{1,0:T(8,128)(2,1)S(1)}, u32[]{:S(2)}, u32[]{:S(2)}) collective-permute-start(bf16[400,768]{1,0:T(8,128)(2,1)S(1)} %get-tuple-element.30), channel_id=1, source_target_pairs={{0,4},{1,3},{2,6},{3,1},{4,0},{5,7},{6,2},{7,5},{8,12},{9,11},{10,... | collective-permute-start | bytes 1843208 | tf_op jit(solution)/shard_map/ppermute | solution.py:353
  18.4 0.0 copy-done.3
  18.4 2.0 %collective-permute-start.5 = (bf16[256,768]{1,0:T(8,128)(2,1)S(1)}, bf16[256,768]{1,0:T(8,128)(2,1)S(1)}, u32[]{:S(2)}, u32[]{:S(2)}) collective-permute-start(bf16[256,768]{1,0:T(8,128)(2,1)S(1)} %copy-done.3), channel_id=1, source_target_pairs={{0,8},{8,0},{16,24},{24,16},{1,9},{9,1},{17,25},{25,17},{2,10},{10... | collective-permute-start | bytes 1179656 | tf_op jit(solution)/shard_map/ppermute | solution.py:302
  20.5 0.7 collective-permute-start.6
  21.2 6.2 %collective-permute-done.5.refs_0_ = bf16[256,768]{1,0:T(8,128)(2,1)S(1)} collective-permute-done((bf16[256,768]{1,0:T(8,128)(2,1)S(1)}, bf16[256,768]{1,0:T(8,128)(2,1)S(1)}, u32[]{:S(2)}, u32[]{:S(2)}) %collective-permute-start.5) | collective-permute-done | bytes 393248 | tf_op jit(solution)/shard_map/ppermute | solution.py:302
  27.3 0.0 collective-permute-done.6.refs_1_
  27.3 3.5 %collective-permute-done.3.refs_5_.refs_2_.refs_6_.refs_7_ = bf16[400,768]{1,0:T(8,128)(2,1)S(1)} collective-permute-done((bf16[400,768]{1,0:T(8,128)(2,1)S(1)}, bf16[400,768]{1,0:T(8,128)(2,1)S(1)}, u32[]{:S(2)}, u32[]{:S(2)}) %collective-permute-start.3) | collective-permute-done | bytes 614432 | tf_op jit(solution)/shard_map/ppermute | solution.py:352
  30.8 0.0 collective-permute-done.4.refs_6_.refs_4_.refs_8_.refs_9_
  30.8 0.5 collective-permute-start.7
  31.3 0.7 collective-permute-start.8
  32.0 1.3 %collective-permute-start.9 = (bf16[256,768]{1,0:T(8,128)(2,1)S(1)}, bf16[256,768]{1,0:T(8,128)(2,1)S(1)}, u32[]{:S(2)}, u32[]{:S(2)}) collective-permute-start(bf16[256,768]{1,0:T(8,128)(2,1)S(1)} %collective-permute-done.6.refs_1_), channel_id=1, source_target_pairs={{8,0},{16,24},{9,1},{17,25},{10,2},{18,26},{11,3},{19,27},{12,4},{... | collective-permute-start | bytes 1179656 | tf_op jit(solution)/shard_map/ppermute | solution.py:359
  33.3 0.1 collective-permute-start.10
  33.4 0.5 collective-permute-start.11
  33.9 0.0 collective-permute-done.8.refs_1_
  33.9 10.8 %collective-permute-done.9.refs_0_ = bf16[256,768]{1,0:T(8,128)(2,1)S(1)} collective-permute-done((bf16[256,768]{1,0:T(8,128)(2,1)S(1)}, bf16[256,768]{1,0:T(8,128)(2,1)S(1)}, u32[]{:S(2)}, u32[]{:S(2)}) %collective-permute-start.9) | collective-permute-done | bytes 393248 | tf_op jit(solution)/shard_map/ppermute | solution.py:359
  44.7 0.0 collective-permute-done.7.refs_7_.refs_6_.refs_10_.refs_11_
  44.7 0.0 collective-permute-start.12
  44.8 0.0 copy-start.1
  44.8 1.4 %collective-permute-start.16 = (bf16[256,768]{1,0:T(8,128)(2,1)S(1)}, bf16[256,768]{1,0:T(8,128)(2,1)S(1)}, u32[]{:S(2)}, u32[]{:S(2)}) collective-permute-start(bf16[256,768]{1,0:T(8,128)(2,1)S(1)} %collective-permute-done.8.refs_1_), channel_id=1, source_target_pairs={{8,0},{16,24},{9,1},{17,25},{10,2},{18,26},{11,3},{19,27},{12,4},{... | collective-permute-start | bytes 1179656 | tf_op jit(solution)/shard_map/ppermute | solution.py:363
  46.2 4.2 %meta.1 = (f32[4,3072]{1,0:T(4,128)S(1)}, f32[1,3072]{1,0:T(1,128)S(1)}, s32[1,1024]{1,0:T(1,128)S(1)}, s32[1,1024]{1,0:T(1,128)S(1)}, s32[1,384]{1,0:T(1,128)S(...) custom-call(s32[3]{0:T(128)S(1)} %pad_add_fusion.1.place, s32[1,2560]{1,0:T(1,128)S(1)} %reshape.57.refs_0_, ...), custom_call_target="tpu_custom_call" | custom-call | flops 1 | bytes 1 | tf_op jit(solution)/shard_map/meta/pallas_call | solution.py:289
  50.4 0.0 collective-permute-done.10.refs_3_.refs_7_.refs_8_
  50.4 0.0 collective-permute-done.11.refs_5_.refs_9_.refs_10_
  50.4 0.0 collective-permute-done.12.refs_7_.refs_11_.refs_12_
  50.4 0.0 copy-done.1
  50.4 1.1 %pack.1 = (bf16[192,768]{1,0:T(8,128)(2,1)S(1)}, f32[1,3072]{1,0:T(1,128)S(1)}) custom-call(s32[3]{0:T(128)S(1)} %pad_add_fusion.1.place, s32[1,1024]{1,0:T(1,128)S(1)} %get-tuple-element.36.code, f32[6,128]{1,0:T(8,128)S(1)} %get-tuple-element.37.scale, bf16[512,768]{1,0:T(8,128)(2,1)S(1)} %copy-done.1, bf16[256,768]{1,0:T(8,128)(2,1)S(1)} %copy-done.2, ...), custom_call_target="tpu_custom_call" | custom-call | flops 1 | bytes 1 | tf_op jit(solution)/shard_map/pack/pallas_call | solution.py:289
  51.5 2.7 %collective-permute-start.15 = (bf16[64,768]{1,0:T(8,128)(2,1)S(1)}, bf16[64,768]{1,0:T(8,128)(2,1)S(1)}, u32[]{:S(2)}, u32[]{:S(2)}) collective-permute-start(bf16[64,768]{1,0:T(8,128)(2,1)S(1)} %get-tuple-element.58), channel_id=1, source_target_pairs={{0,24},{8,16},{16,8},{24,0},{1,25},{9,17},{17,9},{25,1},{2,26},{10... | collective-permute-start | bytes 294920 | tf_op jit(solution)/shard_map/ppermute | solution.py:302
  54.2 1.5 %collective-permute-start.14 = (bf16[64,768]{1,0:T(8,128)(2,1)S(1)}, bf16[64,768]{1,0:T(8,128)(2,1)S(1)}, u32[]{:S(2)}, u32[]{:S(2)}) collective-permute-start(bf16[64,768]{1,0:T(8,128)(2,1)S(1)} %get-tuple-element.59), channel_id=1, source_target_pairs={{0,16},{8,24},{16,0},{24,8},{1,17},{9,25},{17,1},{25,9},{2,18},{10... | collective-permute-start | bytes 294920 | tf_op jit(solution)/shard_map/ppermute | solution.py:302
  55.7 0.3 collective-permute-start.13
  56.0 2.6 %score.4 = f32[2,2,128]{2,1,0:T(2,128)S(1)} custom-call(s32[3]{0:T(128)S(1)} %pad_add_fusion.1.place, s32[1,256]{1,0:T(1,128)S(1)} %bitcast.25, bf16[256,768]{1,0:T(8,128)(2,1)S(1)} %collective-permute-done.5.refs_0_, f32[4,3072]{1,0:T(4,128)S(1)} %get-tuple-element.39.refs_1_.refs_2_, f32[1,3072]{1,0:T(1,128)S(1)} %get-tuple-element.40.refs_2_.refs_3_, ...), custom_call_target="tpu_custom_call" | custom-call | flops 1 | bytes 1 | tf_op jit(solution)/shard_map/score/pallas_call | solution.py:289
  58.6 0.0 copy-start.6
  58.6 0.7 copy-done.6
  59.3 2.6 %score.5 = f32[2,2,128]{2,1,0:T(2,128)S(1)} custom-call(s32[3]{0:T(128)S(1)} %pad_add_fusion.1.place, s32[1,256]{1,0:T(1,128)S(1)} %bitcast.24, bf16[256,768]{1,0:T(8,128)(2,1)S(1)} %copy-done.3, f32[4,3072]{1,0:T(4,128)S(1)} %get-tuple-element.39.refs_1_.refs_2_, f32[1,3072]{1,0:T(1,128)S(1)} %get-tuple-element.40.refs_2_.refs_3_, ...), custom_call_target="tpu_custom_call" | custom-call | flops 1 | bytes 1 | tf_op jit(solution)/shard_map/score/pallas_call | solution.py:289
  61.9 0.0 collective-permute-done.15
  61.9 3.0 %collective-permute-done.14 = bf16[64,768]{1,0:T(8,128)(2,1)S(1)} collective-permute-done((bf16[64,768]{1,0:T(8,128)(2,1)S(1)}, bf16[64,768]{1,0:T(8,128)(2,1)S(1)}, u32[]{:S(2)}, u32[]{:S(2)}) %collective-permute-start.14) | collective-permute-done | bytes 98336 | tf_op jit(solution)/shard_map/ppermute | solution.py:302
  64.9 0.0 collective-permute-done.13
  64.9 0.0 collective-permute-done.16.refs_0_
  65.0 0.1 collective-permute-start.20
  65.1 2.6 %score.7 = f32[2,2,128]{2,1,0:T(2,128)S(1)} custom-call(s32[3]{0:T(128)S(1)} %pad_add_fusion.1.place, s32[1,256]{1,0:T(1,128)S(1)} %bitcast.18, bf16[256,768]{1,0:T(8,128)(2,1)S(1)} %collective-permute-done.16.refs_0_, bf16[256,768]{1,0:T(8,128)(2,1)S(1)} %collective-permute-done.6.refs_1_, f32[4,3072]{1,0:T(4,128)S(1)} %get-tuple-element.39.refs_1_.refs_2_, ...), custom_call_target="tpu_custom_call" | custom-call | flops 1 | bytes 1 | tf_op jit(solution)/shard_map/score/pallas_call | solution.py:289
  67.6 2.7 %collective-permute-start.19 = (f32[2,2,128]{2,1,0:T(2,128)S(1)}, f32[2,2,128]{2,1,0:T(2,128)S(1)}, u32[]{:S(2)}, u32[]{:S(2)}) collective-permute-start(f32[2,2,128]{2,1,0:T(2,128)S(1)} %score.7), channel_id=1, source_target_pairs={{0,24},{8,16},{16,8},{24,0},{1,25},{9,17},{17,9},{25,1},{2,26},{10... | collective-permute-start | bytes 6152 | tf_op jit(solution)/shard_map/ppermute | solution.py:302
  70.3 2.6 %score.6 = f32[2,2,128]{2,1,0:T(2,128)S(1)} custom-call(s32[3]{0:T(128)S(1)} %pad_add_fusion.1.place, s32[1,256]{1,0:T(1,128)S(1)} %bitcast.19, bf16[256,768]{1,0:T(8,128)(2,1)S(1)} %collective-permute-done.9.refs_0_, bf16[256,768]{1,0:T(8,128)(2,1)S(1)} %collective-permute-done.8.refs_1_, f32[4,3072]{1,0:T(4,128)S(1)} %get-tuple-element.39.refs_1_.refs_2_, ...), custom_call_target="tpu_custom_call" | custom-call | flops 1 | bytes 1 | tf_op jit(solution)/shard_map/score/pallas_call | solution.py:289
  72.9 0.1 collective-permute-start.18
  73.0 1.7 %collective-permute-start.17 = (f32[2,2,128]{2,1,0:T(2,128)S(1)}, f32[2,2,128]{2,1,0:T(2,128)S(1)}, u32[]{:S(2)}, u32[]{:S(2)}) collective-permute-start(f32[2,2,128]{2,1,0:T(2,128)S(1)} %score.4), channel_id=1, source_target_pairs={{0,8},{8,0},{16,24},{24,16},{1,9},{9,1},{17,25},{25,17},{2,10},{10... | collective-permute-start | bytes 6152 | tf_op jit(solution)/shard_map/ppermute | solution.py:302
  74.7 0.0 collective-permute-done.19
  74.7 2.7 %collective-permute-done.18 = f32[2,2,128]{2,1,0:T(2,128)S(1)} collective-permute-done((f32[2,2,128]{2,1,0:T(2,128)S(1)}, f32[2,2,128]{2,1,0:T(2,128)S(1)}, u32[]{:S(2)}, u32[]{:S(2)}) %collective-permute-start.18) | collective-permute-done | bytes 2080 | tf_op jit(solution)/shard_map/ppermute | solution.py:302
  77.5 0.0 collective-permute-done.17
  77.5 0.0 collective-permute-done.20.refs_9_
  77.5 2.8 %apply.1 = bf16[512,768]{1,0:T(8,128)(2,1)} custom-call(s32[3]{0:T(128)S(1)} %pad_add_fusion.1.place, s32[1,1024]{1,0:T(1,128)S(1)} %get-tuple-element.50.own_target, s32[1,384]{1,0:T(1,128)S(1)} %get-tuple-element.51.target, s32[1,512]{1,0:T(1,128)S(1)} %get-tuple-element.52.refreshed, bf16[512,768]{1,0:T(8,128)(2,1)S(1)} %copy-done.1, ...), custom_call_target="tpu_custom_call" | custom-call | flops 1 | bytes 1 | tf_op jit(solution)/shard_map/apply/pallas_call | solution.py:289
  80.3 0.6 multiply_bitcast_fusion
  (13 shorter events, 0.1 us)
Async XLA Ops:
  0.6 0.7 copy-start.5
  2.0 6.7 %collective-permute-start.2 = (s32[2560]{0:T(1024)S(1)}, s32[2560]{0:T(1024)S(1)}, u32[]{:S(2)}, u32[]{:S(2)}) collective-permute-start(s32[2560]{0:T(1024)S(1)} %pad_add_fusion), channel_id=1, source_target_pairs={{0,24},{8,16},{16,8},{24,0},{1,25},{9,17},{17,9},{25,1},{2,26},{10... | collective-permute-start | bytes 30728 | tf_op jit(solution)/shard_map/ppermute | solution.py:302
  7.1 3.7 %collective-permute-start = (s32[2560]{0:T(1024)S(1)}, s32[2560]{0:T(1024)S(1)}, u32[]{:S(2)}, u32[]{:S(2)}) collective-permute-start(s32[2560]{0:T(1024)S(1)} %pad_add_fusion), channel_id=1, source_target_pairs={{0,8},{8,0},{16,24},{24,16},{1,9},{9,1},{17,25},{25,17},{2,10},{10... | collective-permute-start | bytes 30728 | tf_op jit(solution)/shard_map/ppermute | solution.py:302
  7.1 4.6 %collective-permute-start.1 = (s32[2560]{0:T(1024)S(1)}, s32[2560]{0:T(1024)S(1)}, u32[]{:S(2)}, u32[]{:S(2)}) collective-permute-start(s32[2560]{0:T(1024)S(1)} %pad_add_fusion), channel_id=1, source_target_pairs={{0,16},{8,24},{16,0},{24,8},{1,17},{9,25},{17,1},{25,9},{2,18},{10... | collective-permute-start | bytes 30728 | tf_op jit(solution)/shard_map/ppermute | solution.py:302
  11.7 0.7 copy-start.4
  12.4 1.1 %copy-start = (bf16[512,768]{1,0:T(8,128)(2,1)S(1)}, bf16[512,768]{1,0:T(8,128)(2,1)}, u32[]{:S(2)}) copy-start(bf16[512,768]{1,0:T(8,128)(2,1)} %refs_0_.5) | copy-start | bytes 2359300
  13.5 1.0 %copy-start.2 = (bf16[256,768]{1,0:T(8,128)(2,1)S(1)}, bf16[256,768]{1,0:T(8,128)(2,1)}, u32[]{:S(2)}) copy-start(bf16[256,768]{1,0:T(8,128)(2,1)} %refs_1_.3) | copy-start | bytes 1179652
  14.5 4.0 %copy-start.3 = (bf16[256,768]{1,0:T(8,128)(2,1)S(1)}, bf16[256,768]{1,0:T(8,128)(2,1)}, u32[]{:S(2)}) copy-start(bf16[256,768]{1,0:T(8,128)(2,1)} %refs_0_.4) | copy-start | bytes 1179652
  15.4 15.5 %collective-permute-start.3 = (bf16[400,768]{1,0:T(8,128)(2,1)S(1)}, bf16[400,768]{1,0:T(8,128)(2,1)S(1)}, u32[]{:S(2)}, u32[]{:S(2)}) collective-permute-start(bf16[400,768]{1,0:T(8,128)(2,1)S(1)} %get-tuple-element.30), channel_id=1, source_target_pairs={{0,2},{1,5},{2,0},{3,7},{4,6},{5,1},{6,4},{7,3},{8,10},{9,13},{10,... | collective-permute-start | bytes 1843208 | tf_op jit(solution)/shard_map/ppermute | solution.py:352
  16.9 13.9 %collective-permute-start.4 = (bf16[400,768]{1,0:T(8,128)(2,1)S(1)}, bf16[400,768]{1,0:T(8,128)(2,1)S(1)}, u32[]{:S(2)}, u32[]{:S(2)}) collective-permute-start(bf16[400,768]{1,0:T(8,128)(2,1)S(1)} %get-tuple-element.30), channel_id=1, source_target_pairs={{0,4},{1,3},{2,6},{3,1},{4,0},{5,7},{6,2},{7,5},{8,12},{9,11},{10,... | collective-permute-start | bytes 1843208 | tf_op jit(solution)/shard_map/ppermute | solution.py:353
  18.4 8.9 %collective-permute-start.5 = (bf16[256,768]{1,0:T(8,128)(2,1)S(1)}, bf16[256,768]{1,0:T(8,128)(2,1)S(1)}, u32[]{:S(2)}, u32[]{:S(2)}) collective-permute-start(bf16[256,768]{1,0:T(8,128)(2,1)S(1)} %copy-done.3), channel_id=1, source_target_pairs={{0,8},{8,0},{16,24},{24,16},{1,9},{9,1},{17,25},{25,17},{2,10},{10... | collective-permute-start | bytes 1179656 | tf_op jit(solution)/shard_map/ppermute | solution.py:302
  20.5 6.8 %collective-permute-start.6 = (bf16[256,768]{1,0:T(8,128)(2,1)S(1)}, bf16[256,768]{1,0:T(8,128)(2,1)S(1)}, u32[]{:S(2)}, u32[]{:S(2)}) collective-permute-start(bf16[256,768]{1,0:T(8,128)(2,1)S(1)} %copy-done.3), channel_id=1, source_target_pairs={{8,16},{16,8},{9,17},{17,9},{10,18},{18,10},{11,19},{19,11},{12,20... | collective-permute-start | bytes 1179656 | tf_op jit(solution)/shard_map/ppermute | solution.py:356
  30.8 13.9 %collective-permute-start.7 = (bf16[400,768]{1,0:T(8,128)(2,1)S(1)}, bf16[400,768]{1,0:T(8,128)(2,1)S(1)}, u32[]{:S(2)}, u32[]{:S(2)}) collective-permute-start(bf16[400,768]{1,0:T(8,128)(2,1)S(1)} %collective-permute-done.3.refs_5_.refs_2_.refs_6_.refs_7_), channel_id=1, source_target_pairs={{0,4},{1,3},{2,6},{3,1},{4,0},{5,7},{6,2},{7,5},{8,12},{9,11},{10,... | collective-permute-start | bytes 1843208 | tf_op jit(solution)/shard_map/ppermute | solution.py:360
  31.3 2.6 %collective-permute-start.8 = (bf16[256,768]{1,0:T(8,128)(2,1)S(1)}, bf16[256,768]{1,0:T(8,128)(2,1)S(1)}, u32[]{:S(2)}, u32[]{:S(2)}) collective-permute-start(bf16[256,768]{1,0:T(8,128)(2,1)S(1)} %collective-permute-done.5.refs_0_), channel_id=1, source_target_pairs={{8,16},{16,8},{9,17},{17,9},{10,18},{18,10},{11,19},{19,11},{12,20... | collective-permute-start | bytes 1179656 | tf_op jit(solution)/shard_map/ppermute | solution.py:358
  32.0 12.7 %collective-permute-start.9 = (bf16[256,768]{1,0:T(8,128)(2,1)S(1)}, bf16[256,768]{1,0:T(8,128)(2,1)S(1)}, u32[]{:S(2)}, u32[]{:S(2)}) collective-permute-start(bf16[256,768]{1,0:T(8,128)(2,1)S(1)} %collective-permute-done.6.refs_1_), channel_id=1, source_target_pairs={{8,0},{16,24},{9,1},{17,25},{10,2},{18,26},{11,3},{19,27},{12,4},{... | collective-permute-start | bytes 1179656 | tf_op jit(solution)/shard_map/ppermute | solution.py:359
  33.3 17.1 %collective-permute-start.10 = (bf16[400,768]{1,0:T(8,128)(2,1)S(1)}, bf16[400,768]{1,0:T(8,128)(2,1)S(1)}, u32[]{:S(2)}, u32[]{:S(2)}) collective-permute-start(bf16[400,768]{1,0:T(8,128)(2,1)S(1)} %collective-permute-done.3.refs_5_.refs_2_.refs_6_.refs_7_), channel_id=1, source_target_pairs={{0,1},{1,0},{2,3},{3,2},{4,5},{5,4},{6,7},{7,6},{8,9},{9,8},{10,11... | collective-permute-start | bytes 1843208 | tf_op jit(solution)/shard_map/ppermute | solution.py:302
  33.4 17.0 %collective-permute-start.11 = (bf16[400,768]{1,0:T(8,128)(2,1)S(1)}, bf16[400,768]{1,0:T(8,128)(2,1)S(1)}, u32[]{:S(2)}, u32[]{:S(2)}) collective-permute-start(bf16[400,768]{1,0:T(8,128)(2,1)S(1)} %collective-permute-done.4.refs_6_.refs_4_.refs_8_.refs_9_), channel_id=1, source_target_pairs={{0,1},{1,0},{2,3},{3,2},{4,5},{5,4},{6,7},{7,6},{8,9},{9,8},{10,11... | collective-permute-start | bytes 1843208 | tf_op jit(solution)/shard_map/ppermute | solution.py:302
  44.7 5.7 %collective-permute-start.12 = (bf16[400,768]{1,0:T(8,128)(2,1)S(1)}, bf16[400,768]{1,0:T(8,128)(2,1)S(1)}, u32[]{:S(2)}, u32[]{:S(2)}) collective-permute-start(bf16[400,768]{1,0:T(8,128)(2,1)S(1)} %collective-permute-done.7.refs_7_.refs_6_.refs_10_.refs_11_), channel_id=1, source_target_pairs={{0,1},{1,0},{2,3},{3,2},{4,5},{5,4},{6,7},{7,6},{8,9},{9,8},{10,11... | collective-permute-start | bytes 1843208 | tf_op jit(solution)/shard_map/ppermute | solution.py:302
  44.8 5.6 %copy-start.1 = (bf16[512,768]{1,0:T(8,128)(2,1)S(1)}, bf16[512,768]{1,0:T(8,128)(2,1)}, u32[]{:S(2)}) copy-start(bf16[512,768]{1,0:T(8,128)(2,1)} %refs_0_.5) | copy-start | bytes 2359300
  44.8 20.2 %collective-permute-start.16 = (bf16[256,768]{1,0:T(8,128)(2,1)S(1)}, bf16[256,768]{1,0:T(8,128)(2,1)S(1)}, u32[]{:S(2)}, u32[]{:S(2)}) collective-permute-start(bf16[256,768]{1,0:T(8,128)(2,1)S(1)} %collective-permute-done.8.refs_1_), channel_id=1, source_target_pairs={{8,0},{16,24},{9,1},{17,25},{10,2},{18,26},{11,3},{19,27},{12,4},{... | collective-permute-start | bytes 1179656 | tf_op jit(solution)/shard_map/ppermute | solution.py:363
  51.5 10.3 %collective-permute-start.15 = (bf16[64,768]{1,0:T(8,128)(2,1)S(1)}, bf16[64,768]{1,0:T(8,128)(2,1)S(1)}, u32[]{:S(2)}, u32[]{:S(2)}) collective-permute-start(bf16[64,768]{1,0:T(8,128)(2,1)S(1)} %get-tuple-element.58), channel_id=1, source_target_pairs={{0,24},{8,16},{16,8},{24,0},{1,25},{9,17},{17,9},{25,1},{2,26},{10... | collective-permute-start | bytes 294920 | tf_op jit(solution)/shard_map/ppermute | solution.py:302
  54.2 10.7 %collective-permute-start.14 = (bf16[64,768]{1,0:T(8,128)(2,1)S(1)}, bf16[64,768]{1,0:T(8,128)(2,1)S(1)}, u32[]{:S(2)}, u32[]{:S(2)}) collective-permute-start(bf16[64,768]{1,0:T(8,128)(2,1)S(1)} %get-tuple-element.59), channel_id=1, source_target_pairs={{0,16},{8,24},{16,0},{24,8},{1,17},{9,25},{17,1},{25,9},{2,18},{10... | collective-permute-start | bytes 294920 | tf_op jit(solution)/shard_map/ppermute | solution.py:302
  55.7 9.2 %collective-permute-start.13 = (bf16[64,768]{1,0:T(8,128)(2,1)S(1)}, bf16[64,768]{1,0:T(8,128)(2,1)S(1)}, u32[]{:S(2)}, u32[]{:S(2)}) collective-permute-start(bf16[64,768]{1,0:T(8,128)(2,1)S(1)} %get-tuple-element.57), channel_id=1, source_target_pairs={{0,8},{8,0},{16,24},{24,16},{1,9},{9,1},{17,25},{25,17},{2,10},{10... | collective-permute-start | bytes 294920 | tf_op jit(solution)/shard_map/ppermute | solution.py:302
  58.6 0.7 copy-start.6
  65.0 12.5 %collective-permute-start.20 = (bf16[192,768]{1,0:T(8,128)(2,1)S(1)}, bf16[192,768]{1,0:T(8,128)(2,1)S(1)}, u32[]{:S(2)}, u32[]{:S(2)}) collective-permute-start(bf16[192,768]{1,0:T(8,128)(2,1)S(1)} %pad_maximum_fusion.refs_8_), channel_id=1, source_target_pairs={{0,1},{1,0},{2,3},{3,2},{4,5},{5,4},{6,7},{7,6},{8,9},{9,8},{10,11... | collective-permute-start | bytes 884744 | tf_op jit(solution)/shard_map/ppermute | solution.py:302
  67.6 7.1 %collective-permute-start.19 = (f32[2,2,128]{2,1,0:T(2,128)S(1)}, f32[2,2,128]{2,1,0:T(2,128)S(1)}, u32[]{:S(2)}, u32[]{:S(2)}) collective-permute-start(f32[2,2,128]{2,1,0:T(2,128)S(1)} %score.7), channel_id=1, source_target_pairs={{0,24},{8,16},{16,8},{24,0},{1,25},{9,17},{17,9},{25,1},{2,26},{10... | collective-permute-start | bytes 6152 | tf_op jit(solution)/shard_map/ppermute | solution.py:302
  72.9 4.5 %collective-permute-start.18 = (f32[2,2,128]{2,1,0:T(2,128)S(1)}, f32[2,2,128]{2,1,0:T(2,128)S(1)}, u32[]{:S(2)}, u32[]{:S(2)}) collective-permute-start(f32[2,2,128]{2,1,0:T(2,128)S(1)} %score.6), channel_id=1, source_target_pairs={{0,16},{8,24},{16,0},{24,8},{1,17},{9,25},{17,1},{25,9},{2,18},{10... | collective-permute-start | bytes 6152 | tf_op jit(solution)/shard_map/ppermute | solution.py:302
  73.0 4.5 %collective-permute-start.17 = (f32[2,2,128]{2,1,0:T(2,128)S(1)}, f32[2,2,128]{2,1,0:T(2,128)S(1)}, u32[]{:S(2)}, u32[]{:S(2)}) collective-permute-start(f32[2,2,128]{2,1,0:T(2,128)S(1)} %score.4), channel_id=1, source_target_pairs={{0,8},{8,0},{16,24},{24,16},{1,9},{9,1},{17,25},{25,17},{2,10},{10... | collective-permute-start | bytes 6152 | tf_op jit(solution)/shard_map/ppermute | solution.py:302

commit v9 on v8

v9 whole, which is shorter than its diff:
```python
import functools
import math

import jax
import jax.numpy as jnp
from jax import lax
from jax.experimental import pallas as pl
from jax.experimental.pallas import tpu as pltpu
from jax.sharding import Mesh, PartitionSpec as P

score_scale = 20.0
age_scale = 16.0
epsilon = 1e-06
LOG2E = math.log2(math.e)
MASKED = -1e30
VMEM_LIMIT = 48 * 1024 * 1024
EXTRA = 16
IDS_ROW = 9
AGES_ROW = 11
LANES = 128

NT = (((1,), (1,)), ((), ()))
NN = (((1,), (0,)), ((), ()))


def one_hot(ids, count):
    rows = lax.broadcasted_iota(jnp.int32, (count, ids.shape[1]), 0)
    return jnp.where(rows == ids, 1.0, 0.0).astype(jnp.bfloat16)


def split_terms(values):
    terms = []
    for _ in range(3):
        terms.append(values.astype(jnp.bfloat16))
        values = values - terms[-1].astype(jnp.float32)
    return terms


def counted(hits):
    count = hits.shape[1]
    before = lax.broadcasted_iota(jnp.int32, (count, count), 0)
    after = lax.broadcasted_iota(jnp.int32, (count, count), 1)
    earlier = jnp.where(before < after, 1.0, 0.0).astype(jnp.bfloat16)
    return lax.dot_general(hits.astype(jnp.bfloat16), earlier, NN, preferred_element_type=jnp.float32)


def small(values):
    return values.astype(jnp.float32).astype(jnp.bfloat16)


def number(values):
    return values.astype(jnp.float32).astype(jnp.int32)


def put(out, row, values):
    width = out.shape[1]
    for i, left in enumerate(range(0, values.shape[1], width)):
        part = small(values[:, left : left + width])
        out[row + i : row + i + 1, : part.shape[1]] = part


def take(rows, row, count):
    width = rows.shape[1]
    parts = [number(rows[row + i : row + i + 1, :]) for i in range(-(-count // width))]
    return jnp.concatenate(parts, axis=1)[:, :count]


def put_ids(out, row, ids):
    lines = -(-ids.shape[1] // out.shape[1])
    put(out, row, ids >> 7)
    put(out, row + lines, ids & 127)


def take_ids(rows, row, count):
    lines = -(-count // rows.shape[1])
    return take(rows, row, count) * LANES + take(rows, row + lines, count)


def prep_kernel(
    place, queries, table, fresh, ref_ids, ages, neg, pos, queries_out, rows_out, scale_out, *, replicas, encode
):
    core = place[2]
    count, width = queries.shape
    queries_out[:count, :] = queries[...]
    queries_out[count:, :] = jnp.zeros((EXTRA, width), jnp.bfloat16)
    put_ids(queries_out, count, neg[...])
    put_ids(queries_out, count + 2 * -(-neg.shape[1] // width), pos[...])
    line, row = 0, 0
    halves = []
    for source in (table, fresh):
        rows = source.shape[0]
        half = rows // replicas
        rows_out[row : row + half, :] = source[pl.ds(pl.multiple_of(core * half, half), half), :]
        row += half
        for block in range(rows // LANES):
            squares = jnp.zeros((LANES, LANES), jnp.float32)
            for chunk in range(width // LANES):
                values = source[block * LANES : (block + 1) * LANES, chunk * LANES : (chunk + 1) * LANES]
                values = values.astype(jnp.float32)
                squares += values * values
            mean = jnp.sum(squares.T, axis=0, keepdims=True) / width
            scale_out[line + block : line + block + 1, :] = lax.rsqrt(mean + epsilon) * (score_scale / width * LOG2E)
        halves += [(line, i, half // LANES) for i in range(half // LANES)]
        line += rows // LANES
    rows_out[row:, :] = jnp.zeros((EXTRA, width), jnp.bfloat16)
    if encode:
        terms = []
        for first, i, count in halves:
            terms += split_terms(scale_out[pl.ds(first + core * count + i, 1), :])
        for i, term in enumerate(terms):
            rows_out[row + i : row + i + 1, :LANES] = term
    put_ids(rows_out, row + IDS_ROW, ref_ids[...])
    put(rows_out, row + AGES_ROW, ages[...])


def in_order(place, values, fast):
    if not fast:
        return values
    own, near, side, far = values
    core = place[2]
    return [own, jnp.where(core == 0, near, side), jnp.where(core == 0, side, near), far]


def owner_ranks(rows, refresh_dev, cap):
    match = jnp.concatenate(rows, axis=0) == 0
    rank = counted(jnp.where(match, 1.0, 0.0)).astype(jnp.int32)
    return jnp.where(match, rank, -cap)


def pack_kernel(
    place, ref_ids, scale, *refs, sides, pieces, all_pieces, planes, rows_dev, cap, replicas, fast
):
    outer, inner, core = place[0], place[1], place[2]
    buffers, outs = refs[: -planes - 1], refs[-planes - 1 : -2]
    scale_out, ids_out = refs[-2:]
    refresh_dev = ref_ids.shape[1]
    owners_plane = len(sides) + 1
    share = cap // replicas
    ids = [ref_ids[...]] + [take_ids(buffers[i], row + IDS_ROW, refresh_dev) for i, row in sides]
    ids = in_order(place, ids, fast)
    pairs = [(plane, side) for plane in range(1, planes) for side in range(owners_plane)]
    rank = owner_ranks(
        [ids[side] // rows_dev - ((outer ^ plane) * owners_plane + inner) for plane, side in pairs], refresh_dev, cap
    )
    rank = rank - core * share
    codes = [jnp.full((1, refresh_dev), -1, jnp.int32)] * owners_plane
    for i, (plane, side) in enumerate(pairs):
        here = (rank[i : i + 1, :] >= 0) & (rank[i : i + 1, :] < share)
        base = ((plane - 1) * owners_plane + side) * share
        codes[side] = jnp.where(here, base + rank[i : i + 1, :], codes[side])
    code = jnp.concatenate(codes, axis=1)
    plane_ids = jnp.concatenate(ids, axis=1)
    ids_out[...] = plane_ids

    selects = []
    for _, _, size, column, _ in pieces:
        if column[2] is None:
            part = code[:, column[0] : column[0] + size]
        else:
            part = None
            for option in range(2):
                at = column[0] + (option ^ column[2]) * size
                at += 0 if column[3] is None else (option ^ column[3]) * size * 2
                one = code[:, at : at + size]
                part = one if part is None else jnp.where(core == 0, part, one)
        selects.append(one_hot(part, len(outs) * owners_plane * share))
    values = [buffers[source][start : start + size, :] for source, start, size, _, _ in pieces]
    select, values = jnp.concatenate(selects, axis=1), jnp.concatenate(values, axis=0)
    packed = lax.dot_general(select, values, NN, preferred_element_type=jnp.float32).astype(jnp.bfloat16)
    size = owners_plane * share
    for i, out in enumerate(outs):
        out[:size, :] = packed[i * size : (i + 1) * size, :]
        out[size:, :] = jnp.zeros((EXTRA, out.shape[1]), jnp.bfloat16)
        put_ids(out, size, plane_ids)
    for source, start, size, column, scale_at in all_pieces:
        first = piece_offset(place, column)
        for chunk in range(size // LANES):
            if scale_at < 0:
                line = -1 - scale_at + chunk
                row = scale[line : line + 1, :]
            else:
                line = scale_at + 3 * chunk
                row = jnp.sum(buffers[source][line : line + 3, :LANES].astype(jnp.float32), axis=0, keepdims=True)
            scale_out[:, pl.ds(first + chunk * LANES, LANES)] = row


def one_hots(ids, high_count):
    return one_hot(ids >> 7, high_count), one_hot(ids & 127, LANES)


def bitmap(ids, high_count):
    high, low = one_hots(ids, high_count)
    return lax.dot_general(low, high, NT, preferred_element_type=jnp.float32).astype(jnp.bfloat16)


def lookup(one_map, pair):
    hit = lax.dot_general(one_map, pair[0], NN, preferred_element_type=jnp.float32)
    return jnp.sum(hit * pair[1].astype(jnp.float32), axis=0, keepdims=True)


def column_ids(place, owners_plane, rows_dev):
    column = lax.broadcasted_iota(jnp.int32, (1, owners_plane * rows_dev), 1)
    return (place[0] * owners_plane + (place[1] ^ (column // rows_dev))) * rows_dev + column % rows_dev


def list_row(place, blocks, count, list_size):
    lists = [take_ids(block, count, list_size) for block in blocks]
    if len(lists) == 1:
        return lists[0]
    return jnp.where((place[0] == 0) | (place[0] == 3), lists[0], lists[1])


def lists_kernel(place, plane_ids, neg, *refs, given, planes, owners_plane, rows_dev, count):
    out = refs[-1]
    high_count = planes * owners_plane * rows_dev // LANES
    pair = one_hots(jnp.concatenate([column_ids(place, owners_plane, rows_dev), plane_ids[...]], axis=1), high_count)
    first = 0
    out[0:1, :] = lookup(bitmap(neg[...], high_count), pair)
    for i, number_of in enumerate(given):
        ids = list_row(place, refs[first : first + number_of], count, neg.shape[1])
        out[i + 1 : i + 2, :] = lookup(bitmap(ids, high_count), pair)
        first += number_of


def meta_kernel(
    place, plane_ids, ages, hits, *refs, arrivals, given, sides, planes, owners_plane, rows_dev, list_size, count, cap,
    replicas, fast
):
    outer, inner, core = place[0], place[1], place[2]
    lw_out, row_out, own_target_out, target_out, own_out, ages_out = refs[-6:]
    came, blocks, buffers = refs[:arrivals], refs[arrivals : arrivals + given], refs[arrivals + given : -6]
    share = cap // replicas
    plane_rows = owners_plane * rows_dev
    plane_refresh = plane_ids.shape[1]
    refresh_dev = plane_refresh // owners_plane
    high_count = planes * plane_rows // LANES
    own_owner = outer * owners_plane + inner

    ids = [plane_ids[...]] + [take_ids(block, owners_plane * share, plane_refresh) for block in came]
    table_ids = column_ids(place, owners_plane, rows_dev)
    pair = one_hots(jnp.concatenate([table_ids, ids[0]], axis=1), high_count)
    refreshed = lookup(bitmap(jnp.concatenate(ids, axis=1), high_count), (pair[0][:, :plane_rows], pair[1][:, :plane_rows]))
    refreshed = refreshed > 0.5
    row_out[:, :plane_rows] = jnp.where(refreshed, -1, table_ids).astype(jnp.float32)
    row_out[:, plane_rows:] = ids[0].astype(jnp.float32)
    own_out[...] = refreshed[:, :rows_dev].astype(jnp.int32)
    ages_out[...] = jnp.where(refreshed[:, :rows_dev], 0, ages[...])

    all_ages = [ages[...]] + [take(buffers[i], row + AGES_ROW, rows_dev) for i, row in sides]
    all_ages = jnp.concatenate(in_order(place, all_ages, fast), axis=1).astype(jnp.float32)
    weight = jnp.exp(-all_ages / age_scale).astype(jnp.bfloat16).astype(jnp.float32)
    log_weight = jnp.where(refreshed, MASKED, jnp.log2(weight))
    log_weight = jnp.concatenate([log_weight, jnp.zeros((1, plane_refresh), jnp.float32)], axis=1)
    for group in range(planes):
        if group < planes - 1:
            hit = hits[group : group + 1, :]
        else:
            hit = lookup(bitmap(list_row(place, blocks, count, list_size), high_count), pair)
        lw_out[group : group + 1, :] = jnp.where(hit > 0.5, log_weight, MASKED)

    own_target_out[...] = ids[0] - own_owner * rows_dev
    pairs = [(plane, side) for plane in range(1, planes) for side in range(owners_plane)]
    part_ids = [ids[plane][:, side * refresh_dev : (side + 1) * refresh_dev] for plane, side in pairs]
    rank = owner_ranks([one // rows_dev - own_owner for one in part_ids], refresh_dev, cap)
    for i, (plane, side) in enumerate(pairs):
        base = ((plane - 1) * owners_plane + side) * share
        took = rank[i : i + 1, :]
        slot = jnp.where(took < 0, -1, ((took // share) ^ core) * share + took % share)
        row = jnp.where(took < 0, 0, part_ids[i] - own_owner * rows_dev)
        kinds = lax.broadcasted_iota(jnp.int32, (8, refresh_dev), 0)
        digits = jnp.where(kinds == 0, row // 16, jnp.where(kinds == 1, row % 16, 1))
        found = lax.dot_general(small(digits), one_hot(slot, cap), NT, preferred_element_type=jnp.float32)
        found = found.astype(jnp.int32)
        target = jnp.where(found[2:3, :] > 0, found[0:1, :] * 16 + found[1:2, :], -1)
        for part in range(replicas):
            first = part * (planes - 1) * owners_plane * share + base
            target_out[:, first : first + share] = target[:, part * share : (part + 1) * share]


def piece_offset(place, piece):
    column, size, flip, by_core = piece
    if flip is None:
        return column
    column += (place[2] ^ flip) * size
    if by_core is not None:
        column += (place[2] ^ by_core) * size * 2
    return pl.multiple_of(column, size)


def apply_kernel(place, own_target, target, refreshed, table, *refs, pieces, arrivals):
    out = refs[-1]
    buffers, arrived = refs[: -1 - arrivals], refs[-1 - arrivals : -1]
    to_rows = [own_target[:, pl.ds(piece_offset(place, column), size)] for _, _, size, column, _ in pieces]
    values = [buffers[source][start : start + size, :] for source, start, size, _, _ in pieces]
    to_row = jnp.concatenate([*to_rows, target[...]], axis=1)
    values = jnp.concatenate([*values, *[block[...] for block in arrived]], axis=0)
    rows = lax.broadcasted_iota(jnp.int32, (out.shape[0], to_row.shape[1]), 0)
    chosen = jnp.where(rows == to_row, 1.0, 0.0).astype(jnp.bfloat16)
    fresh = lax.dot_general(chosen, values, NN, preferred_element_type=jnp.float32)
    for top in range(0, out.shape[0], LANES):
        part = slice(top, top + LANES)
        hit = to_lanes(refreshed[:, part].astype(jnp.float32)) > 0.5
        for left in range(0, out.shape[1], LANES):
            cols = slice(left, left + LANES)
            out[part, cols] = jnp.where(hit, fresh[part, cols], table[part, cols].astype(jnp.float32)).astype(jnp.bfloat16)


def to_lanes(row):
    return jnp.broadcast_to(row, (LANES, LANES)).T


def score_kernel(place, *refs, pieces, flip, given, list_size):
    out, total, pos_total, q_scale, pos_b, chosen = refs[-6:]
    count, width = chosen.shape
    log_weight, row_ids, scale = refs[given : given + 3]
    row = count + 2 * -(-list_size // width)
    positive = [take_ids(block, row, count) for block in refs[:given]]
    if given == 2:
        at_end = (place[0] == 0) | (place[0] == 3)
        chosen[...] = jnp.where(at_end, refs[0][:count, :], refs[1][:count, :])
        queries, positive = chosen, jnp.where(at_end, *positive)
    else:
        queries, positive = refs[0].at[:count, :], positive[0]
    refs = refs[given + 3 : -6]
    for block in range(count // LANES):
        part = slice(block * LANES, (block + 1) * LANES)
        values = queries[part, :].astype(jnp.float32)
        squares = jnp.sum(values * values, axis=1, keepdims=True)
        q_scale[part, :] = jnp.broadcast_to(lax.rsqrt(squares / width + epsilon), (LANES, LANES))
        pos_b[part, :] = to_lanes(positive[:, part].astype(jnp.float32))
    total[...] = jnp.zeros_like(total)
    pos_total[...] = jnp.zeros_like(pos_total)

    def product(piece):
        source, start, size = piece[:3]
        rows = refs[source][start : start + size, :]
        return lax.dot_general(queries[...], rows, NT, preferred_element_type=jnp.float32)

    following = product(pieces[0])
    for i, (_, _, size, column, _) in enumerate(pieces):
        raw = following
        if i + 1 < len(pieces):
            following = product(pieces[i + 1])
        first = piece_offset(place, column)
        for top in range(0, count, 64):
            part = slice(top, top + 64)
            sums, positives = total[part, :], pos_total[part, :]
            query_scale, wanted = q_scale[part, :], pos_b[part, :]
            for chunk in range(size // LANES):
                cols = pl.ds(first + chunk * LANES, LANES)
                powers = raw[part, chunk * LANES : (chunk + 1) * LANES] * query_scale
                powers = powers * scale[:, cols] + log_weight[flip : flip + 1, cols]
                sums = sums + jnp.exp2(powers)
                positives = positives + jnp.where(wanted == row_ids[:, cols], powers, 0.0)
            total[part, :] = sums
            pos_total[part, :] = positives
    for block in range(count // LANES):
        part = slice(block * LANES, (block + 1) * LANES)
        out[0, block : block + 1, :] = jnp.sum(total[part, :].T, axis=0, keepdims=True)
        out[1, block : block + 1, :] = jnp.sum(pos_total[part, :].T, axis=0, keepdims=True)


def whole(memory=pltpu.VMEM):
    return pl.BlockSpec(memory_space=memory)


def call(kernel, name, outs, place, *operands, scratch=(), **options):
    specs = [whole()] * len(operands)
    if place is not None:
        specs = [whole(pltpu.SMEM)] + specs
        operands = (place, *operands)
    return pl.pallas_call(
        functools.partial(kernel, **options),
        out_shape=tuple(outs),
        in_specs=specs,
        out_specs=tuple(whole() for _ in outs),
        scratch_shapes=list(scratch),
        compiler_params=pltpu.CompilerParams(vmem_limit_bytes=VMEM_LIMIT),
        cost_estimate=pl.CostEstimate(flops=1, bytes_accessed=1, transcendentals=0),
        name=name,
    )(*operands)


def swap(values, axis, flip):
    return lax.ppermute(values, axis, [(i, i ^ flip) for i in range(lax.axis_size(axis))])


def on_device(table, ages, refresh_ids, fresh_rows, neg_ids, queries, pos_ids):
    rows_dev, width = table.shape
    refresh_dev = refresh_ids.shape[0]
    planes = lax.axis_size("outer")
    owners_plane = lax.axis_size("inner")
    replicas = lax.axis_size("query")
    owners = planes * owners_plane
    query_count = queries.shape[0]
    list_size = neg_ids.shape[1]
    place = jnp.stack([lax.axis_index(name) for name in ("outer", "inner", "query")]).astype(jnp.int32)
    plane_rows = owners_plane * rows_dev
    plane_refresh = owners_plane * refresh_dev
    all_rows = plane_rows + plane_refresh
    cap = max(2, (2 * refresh_dev + owners - 1) // owners)
    share = cap // replicas
    table_half, fresh_half = rows_dev // replicas, refresh_dev // replicas
    bf16, f32 = jnp.bfloat16, jnp.float32

    fast = replicas == 2 and owners_plane == 4 and planes == 4
    own_ids, own_ages = refresh_ids.reshape(1, -1), ages.reshape(1, -1)
    query_block, rows_half, scales = call(
        prep_kernel,
        "prep",
        [
            jax.ShapeDtypeStruct((query_count + EXTRA, width), bf16),
            jax.ShapeDtypeStruct((table_half + fresh_half + EXTRA, width), bf16),
            jax.ShapeDtypeStruct(((rows_dev + refresh_dev) // LANES, LANES), f32),
        ],
        place,
        queries,
        table,
        fresh_rows,
        own_ids,
        own_ages,
        neg_ids,
        pos_ids.reshape(1, -1),
        replicas=replicas,
        encode=fast,
    )
    others = (planes - 1) * owners_plane

    if fast:
        axes = ("inner", "query")
        first = [(2 * i + c, 2 * (i ^ (1 + c)) + c) for i in range(4) for c in range(2)]
        second = [(2 * i + c, 2 * (i ^ (2 - c)) + c) for i in range(4) for c in range(2)]
        near = lax.ppermute(rows_half, axes, first)
        side_rows = lax.ppermute(rows_half, axes, second)
        middle, outward = [(1, 2), (2, 1)], [(1, 0), (2, 3)]
        beside = swap(query_block, "outer", 1)
        across = lax.ppermute(query_block, "outer", middle)
        near, beside, across = lax.optimization_barrier((near, beside, across))
        from_end = lax.ppermute(beside, "outer", middle)
        to_end = lax.ppermute(across, "outer", outward)
        far = lax.ppermute(near, axes, second)
        far, from_end, to_end = lax.optimization_barrier((far, from_end, to_end))
        last = lax.ppermute(from_end, "outer", outward)
        got_queries = [(query_block,), (beside,), (to_end, from_end), (last, across)]
        sides = [(i, table_half + fresh_half) for i in (2, 4, 6)]
        buffers = [table, fresh_rows]
        table_pieces = [(0, 0, rows_dev, (0, rows_dev, None, None), -1)]
        fresh_pieces = [(1, 0, refresh_dev, (0, refresh_dev, None, None), -1 - rows_dev // LANES)]
        for slot, by_core, mine in ((1, 0, near), (1, 1, side_rows), (3, None, far)):
            for flip, rows in enumerate((mine, swap(mine, "query", 1))):
                by = None if by_core is None else by_core ^ flip
                data = table_half + fresh_half
                fresh_at = data + 3 * (table_half // LANES)
                table_pieces.append((len(buffers), 0, table_half, (slot * rows_dev, table_half, flip, by), data))
                fresh_pieces.append(
                    (len(buffers), table_half, fresh_half, (slot * refresh_dev, fresh_half, flip, by), fresh_at)
                )
                buffers.append(rows)
    else:
        got_queries = [(query_block,)] + [(swap(query_block, "outer", s),) for s in range(1, planes)]
        got_rows = [rows_half] + [swap(rows_half, "inner", s) for s in range(1, owners_plane)]
        data = table_half + fresh_half
        gathered = lax.all_gather(jnp.stack(got_rows), "query", axis=0)
        gathered = jnp.swapaxes(gathered, 0, 1)
        buffers = [
            gathered[:, :, :table_half].reshape(plane_rows, width),
            gathered[:, :, table_half:data].reshape(plane_refresh, width),
            *[one[data:] for one in got_rows[1:]],
        ]
        sides = [(i + 1, 0) for i in range(1, owners_plane)]
        scales = []
        for rows in buffers[:2]:
            values = rows.astype(f32)
            mean = jnp.sum(values * values, axis=1) / width
            scales.append((lax.rsqrt(mean + epsilon) * (score_scale / width * LOG2E)).reshape(-1, LANES))
        scales = jnp.concatenate(scales)

        def blocks(buffer, count, line):
            starts = range(0, count, 512)
            return [(buffer, i, 512, (i, 512, None, None), -1 - line - i // LANES) for i in starts]

        table_pieces = blocks(0, plane_rows, 0)
        fresh_pieces = blocks(1, plane_refresh, plane_rows // LANES)

    def shift(pieces, columns):
        return [(a, b, c, (d[0] + columns, *d[1:]), e) for a, b, c, d, e in pieces]

    pieces = table_pieces + shift(fresh_pieces, plane_rows)
    size = owners_plane * share
    *packed, scale_plane, plane_ids = call(
        pack_kernel,
        "pack",
        [jax.ShapeDtypeStruct((size + EXTRA, width), bf16)] * (planes - 1)
        + [jax.ShapeDtypeStruct((1, all_rows), f32), jax.ShapeDtypeStruct((1, plane_refresh), jnp.int32)],
        place,
        own_ids,
        scales,
        *buffers,
        sides=sides,
        pieces=fresh_pieces,
        all_pieces=pieces,
        planes=planes,
        rows_dev=rows_dev,
        cap=cap,
        replicas=replicas,
        fast=fast,
    )
    came = [swap(packed[s - 1], "outer", s) for s in range(1, planes)]
    early = [one for group in got_queries[1:-1] for one in group]
    plane_ids, *packed = lax.optimization_barrier((plane_ids, *packed))
    (hits,) = call(
        lists_kernel,
        "lists",
        [jax.ShapeDtypeStruct((planes - 1, all_rows), f32)],
        place,
        plane_ids,
        neg_ids,
        *early,
        given=[len(group) for group in got_queries[1:-1]],
        planes=planes,
        owners_plane=owners_plane,
        rows_dev=rows_dev,
        count=query_count,
    )
    hits, *came = lax.optimization_barrier((hits, *came))
    lw, row_ids, own_target, target, own, new_ages = call(
        meta_kernel,
        "meta",
        [
            jax.ShapeDtypeStruct((planes, all_rows), f32),
            jax.ShapeDtypeStruct((1, all_rows), f32),
            jax.ShapeDtypeStruct((1, plane_refresh), jnp.int32),
            jax.ShapeDtypeStruct((1, others * cap), jnp.int32),
            jax.ShapeDtypeStruct((1, rows_dev), jnp.int32),
            jax.ShapeDtypeStruct((1, rows_dev), jnp.int32),
        ],
        place,
        plane_ids,
        own_ages,
        hits,
        *came,
        *got_queries[-1],
        *buffers,
        arrivals=planes - 1,
        given=len(got_queries[-1]),
        sides=sides,
        planes=planes,
        owners_plane=owners_plane,
        rows_dev=rows_dev,
        list_size=list_size,
        count=query_count,
        cap=cap,
        replicas=replicas,
        fast=fast,
    )
    new_ages = new_ages.reshape(rows_dev)
    came = jnp.concatenate([one[:size] for one in came])
    arrived = [came] + [swap(came, "query", flip) for flip in range(1, replicas)]

    def score(s, given):
        (partial,) = call(
            score_kernel,
            "score",
            [jax.ShapeDtypeStruct((2, query_count // LANES, LANES), f32)],
            place,
            *given,
            lw,
            row_ids,
            scale_plane,
            *buffers,
            scratch=[pltpu.VMEM((query_count, LANES), f32)] * 4 + [pltpu.VMEM(queries.shape, bf16)],
            pieces=pieces,
            flip=s,
            given=len(given),
            list_size=list_size,
        )
        return partial

    mine = None
    for s in [*range(1, planes), 0]:
        partial = score(s, got_queries[s])
        if s:
            partial = swap(partial, "outer", s)
        mine = partial if mine is None else mine + partial
    (new_table,) = call(
        apply_kernel,
        "apply",
        [jax.ShapeDtypeStruct(table.shape, bf16)],
        place,
        own_target,
        target,
        own,
        table,
        *buffers,
        *arrived,
        pieces=fresh_pieces,
        arrivals=len(arrived),
    )
    mine, new_table = lax.optimization_barrier((mine, new_table))
    loss = (jnp.log2(mine[0]) - mine[1]) * math.log(2.0)
    return new_table, new_ages, loss.reshape(query_count)


def solution(mesh):
    owners, replicas = mesh.shape["index"], mesh.shape["query"]
    inner = 1 << (int(math.log2(owners)) // 2)
    split = Mesh(mesh.devices.reshape(owners // inner, inner, replicas), ("outer", "inner", "query"))
    index = ("outer", "inner")
    placed = (
        P(index, None),
        P(index),
        P(index),
        P(index, None),
        P(index, None),
        P(("outer", "inner", "query"), None),
        P(("outer", "inner", "query")),
    )
    return jax.shard_map(
        on_device,
        mesh=split,
        in_specs=placed,
        out_specs=(P(index, None), P(index), P(("outer", "inner", "query"))),
        check_vma=False,
    )
```

time: 81.3 us -> 84.9 us (1.044)
  waiting for transfers between devices: 30.2 us -> 33.1 us
  local copies, waits for them, and re-layouts: 4.23 us -> 6.15 us
  starting transfers between devices: 25 us -> 23.3 us
  Pallas kernels: 19.3 us -> 20.4 us
    ppermute x14 -> x11, starting transfers between devices: 17.3 us -> 11.3 us  [swap(): lax.ppermute(values, axis, [(i, i ^ flip) for i in range(lax.axis_size(ax...]
    ppermute x14 -> x11, waiting for transfers between devices: 15.8 us -> 19.5 us  [swap(): lax.ppermute(values, axis, [(i, i ^ flip) for i in range(lax.axis_size(ax...]
    ppermute x1, starting transfers between devices: 0.51 us -> 3.57 us  [on_device(): far = lax.ppermute(near, axes, second)]
    ppermute x1, waiting for transfers between devices: 3.52 us -> 0.9 us  [on_device(): near = lax.ppermute(rows_half, axes, first)]
    ppermute x1, waiting for transfers between devices: 10.8 us -> 12.7 us  [on_device(): to_end = lax.ppermute(across, 'outer', outward)]
    ppermute x1, starting transfers between devices: 1.56 us -> 3 us  [on_device(): near = lax.ppermute(rows_half, axes, first)]
    pallas_call x8 -> x9, Pallas kernels: 19.3 us -> 20.4 us  [call(): pl.pallas_call(functools.partial(kernel, **options), out_shape=tuple(outs...]
    unnamed x14 -> x22, local copies, waits for them, and re-layouts: 4.17 us -> 5.26 us
  transfers between devices with their start and end apart: 21 -> 18, of which waited for: 8 -> 5; matrix products, arithmetic and copies ran while one was open for 0% -> 0% of each run, Pallas kernels for 19% -> 20%
where the time goes in v9:
time: 84.9 us; the launch traced here: 84.5 us
  waiting for transfers between devices  33.1 us (39%)
  starting transfers between devices  23.3 us (27%)
  Pallas kernels  20.4 us (24%)
  local copies, waits for them, and re-layouts  6.15 us (7%)
    pallas_call x9, Pallas kernels, call(): pl.pallas_call(functools.partial(kernel, **options), out_shape=tuple(outs...  20.4 us
    ppermute x11, waiting for transfers between devices, swap(): lax.ppermute(values, axis, [(i, i ^ flip) for i in range(lax.axis_size(ax...  19.5 us
    ppermute x1, waiting for transfers between devices, on_device(): to_end = lax.ppermute(across, 'outer', outward)  12.7 us
    ppermute x11, starting transfers between devices, swap(): lax.ppermute(values, axis, [(i, i ^ flip) for i in range(lax.axis_size(ax...  11.3 us
    unnamed x22, local copies, waits for them, and re-layouts  5.26 us
    ppermute x1, starting transfers between devices, on_device(): far = lax.ppermute(near, axes, second)  3.57 us
    ppermute x1, starting transfers between devices, on_device(): near = lax.ppermute(rows_half, axes, first)  3 us
  transfers between devices with their start and end apart: 18, of which 5 were waited for; matrix products, arithmetic and copies ran while one was open for 0% of the time, Pallas kernels for 20%

profile of v9, /device:TPU:0, one launch (start us, length us, event | category | flops | bytes accessed | tf_op | source)
XLA Modules:
  0.0 84.5 jit_solution(2034471427395841773)
XLA Ops:
  0.6 0.0 copy-start.7
  0.6 0.1 pad_add_fusion.place
  0.7 0.0 copy-start.10
  0.7 0.0 copy-start.8
  0.7 0.0 copy-start.9
  0.7 0.6 copy-done.7
  1.3 0.1 copy-done.10
  1.4 0.0 copy-done.8
  1.4 0.0 copy-done.9
  1.4 0.0 copy-start
  1.4 1.1 %copy-done = bf16[512,768]{1,0:T(8,128)(2,1)S(1)} copy-done((bf16[512,768]{1,0:T(8,128)(2,1)S(1)}, bf16[512,768]{1,0:T(8,128)(2,1)}, u32[]{:S(2)}) %copy-start) | copy-done | bytes 786456
  2.6 1.0 %copy-done.2 = bf16[256,768]{1,0:T(8,128)(2,1)S(1)} copy-done((bf16[256,768]{1,0:T(8,128)(2,1)S(1)}, bf16[256,768]{1,0:T(8,128)(2,1)}, u32[]{:S(2)}) %copy-start.2) | copy-done | bytes 393240
  3.6 1.0 %copy-done.6 = bf16[256,768]{1,0:T(8,128)(2,1)S(1)} copy-done((bf16[256,768]{1,0:T(8,128)(2,1)S(1)}, bf16[256,768]{1,0:T(8,128)(2,1)}, u32[]{:S(2)}) %copy-start.6) | copy-done | bytes 393240
  4.6 0.9 %prep.1 = (bf16[272,768]{1,0:T(8,128)(2,1)S(1)}, bf16[400,768]{1,0:T(8,128)(2,1)S(1)}, f32[6,128]{1,0:T(8,128)S(1)}) custom-call(s32[3]{0:T(128)S(1)} %pad_add_fusion.place, bf16[256,768]{1,0:T(8,128)(2,1)S(1)} %copy-done.6, bf16[512,768]{1,0:T(8,128)(2,1)S(1)} %copy-done, bf16[256,768]{1,0:T(8,128)(2,1)S(1)} %copy-done.2, s32[1,256]{1,0:T(1,128)S(1)} %bitcast.11, ...), custom_call_target="tpu_custom_call" | custom-call | flops 1 | bytes 1 | tf_op jit(solution)/shard_map/prep/pallas_call | solution.py:372
  5.5 3.0 %collective-permute-start = (bf16[400,768]{1,0:T(8,128)(2,1)S(1)}, bf16[400,768]{1,0:T(8,128)(2,1)S(1)}, u32[]{:S(2)}, u32[]{:S(2)}) collective-permute-start(bf16[400,768]{1,0:T(8,128)(2,1)S(1)} %get-tuple-element.30), channel_id=1, source_target_pairs={{0,2},{1,5},{2,0},{3,7},{4,6},{5,1},{6,4},{7,3},{8,10},{9,13},{10,... | collective-permute-start | bytes 1843208 | tf_op jit(solution)/shard_map/ppermute | solution.py:433
  8.5 1.6 %collective-permute-start.1 = (bf16[272,768]{1,0:T(8,128)(2,1)S(1)}, bf16[272,768]{1,0:T(8,128)(2,1)S(1)}, u32[]{:S(2)}, u32[]{:S(2)}) collective-permute-start(bf16[272,768]{1,0:T(8,128)(2,1)S(1)} %get-tuple-element.31.refs_0_), channel_id=1, source_target_pairs={{0,8},{8,0},{16,24},{24,16},{1,9},{9,1},{17,25},{25,17},{2,10},{10... | collective-permute-start | bytes 1253384 | tf_op jit(solution)/shard_map/ppermute | solution.py:385
  10.0 0.7 collective-permute-start.2
  10.7 1.6 %collective-permute-start.4 = (bf16[400,768]{1,0:T(8,128)(2,1)S(1)}, bf16[400,768]{1,0:T(8,128)(2,1)S(1)}, u32[]{:S(2)}, u32[]{:S(2)}) collective-permute-start(bf16[400,768]{1,0:T(8,128)(2,1)S(1)} %get-tuple-element.30), channel_id=1, source_target_pairs={{0,4},{1,3},{2,6},{3,1},{4,0},{5,7},{6,2},{7,5},{8,12},{9,11},{10,... | collective-permute-start | bytes 1843208 | tf_op jit(solution)/shard_map/ppermute | solution.py:434
  12.3 7.3 %collective-permute-done.1.refs_0_ = bf16[272,768]{1,0:T(8,128)(2,1)S(1)} collective-permute-done((bf16[272,768]{1,0:T(8,128)(2,1)S(1)}, bf16[272,768]{1,0:T(8,128)(2,1)S(1)}, u32[]{:S(2)}, u32[]{:S(2)}) %collective-permute-start.1) | collective-permute-done | bytes 417824 | tf_op jit(solution)/shard_map/ppermute | solution.py:385
  19.6 0.0 collective-permute-done.2.refs_4_.refs_1_
  19.6 0.9 %collective-permute-done.refs_2_.refs_7_.refs_6_ = bf16[400,768]{1,0:T(8,128)(2,1)S(1)} collective-permute-done((bf16[400,768]{1,0:T(8,128)(2,1)S(1)}, bf16[400,768]{1,0:T(8,128)(2,1)S(1)}, u32[]{:S(2)}, u32[]{:S(2)}) %collective-permute-start) | collective-permute-done | bytes 614432 | tf_op jit(solution)/shard_map/ppermute | solution.py:433
  20.5 3.6 %collective-permute-start.6 = (bf16[400,768]{1,0:T(8,128)(2,1)S(1)}, bf16[400,768]{1,0:T(8,128)(2,1)S(1)}, u32[]{:S(2)}, u32[]{:S(2)}) collective-permute-start(bf16[400,768]{1,0:T(8,128)(2,1)S(1)} %collective-permute-done.refs_2_.refs_7_.refs_6_), channel_id=1, source_target_pairs={{0,4},{1,3},{2,6},{3,1},{4,0},{5,7},{6,2},{7,5},{8,12},{9,11},{10,... | collective-permute-start | bytes 1843208 | tf_op jit(solution)/shard_map/ppermute | solution.py:441
  24.1 0.7 collective-permute-start.7
  24.7 1.3 %collective-permute-start.8 = (bf16[272,768]{1,0:T(8,128)(2,1)S(1)}, bf16[272,768]{1,0:T(8,128)(2,1)S(1)}, u32[]{:S(2)}, u32[]{:S(2)}) collective-permute-start(bf16[272,768]{1,0:T(8,128)(2,1)S(1)} %collective-permute-done.2.refs_4_.refs_1_), channel_id=1, source_target_pairs={{8,0},{16,24},{9,1},{17,25},{10,2},{18,26},{11,3},{19,27},{12,4},{... | collective-permute-start | bytes 1253384 | tf_op jit(solution)/shard_map/ppermute | solution.py:440
  26.0 0.1 collective-permute-start.3
  26.1 0.0 collective-permute-done.4.refs_4_.refs_9_.refs_8_
  26.1 0.5 collective-permute-start.5
  26.6 0.0 collective-permute-done.7.refs_2_.refs_1_
  26.6 12.7 %collective-permute-done.8.refs_1_.refs_0_ = bf16[272,768]{1,0:T(8,128)(2,1)S(1)} collective-permute-done((bf16[272,768]{1,0:T(8,128)(2,1)S(1)}, bf16[272,768]{1,0:T(8,128)(2,1)S(1)}, u32[]{:S(2)}, u32[]{:S(2)}) %collective-permute-start.8) | collective-permute-done | bytes 417824 | tf_op jit(solution)/shard_map/ppermute | solution.py:440
  39.3 0.0 collective-permute-done.6.refs_6_.refs_11_.refs_10_
  39.3 0.0 collective-permute-start.9
  39.3 1.3 %collective-permute-start.13 = (bf16[272,768]{1,0:T(8,128)(2,1)S(1)}, bf16[272,768]{1,0:T(8,128)(2,1)S(1)}, u32[]{:S(2)}, u32[]{:S(2)}) collective-permute-start(bf16[272,768]{1,0:T(8,128)(2,1)S(1)} %collective-permute-done.7.refs_2_.refs_1_), channel_id=1, source_target_pairs={{8,0},{16,24},{9,1},{17,25},{10,2},{18,26},{11,3},{19,27},{12,4},{... | collective-permute-start | bytes 1253384 | tf_op jit(solution)/shard_map/ppermute | solution.py:443
  40.6 0.0 collective-permute-done.3.refs_3_.refs_8_.refs_7_
  40.6 0.0 collective-permute-done.5.refs_5_.refs_10_.refs_9_
  40.6 0.7 collective-permute-done.9.refs_7_.refs_12_.refs_11_
  41.3 0.0 copy-done.1
  41.3 0.0 copy-done.3
  41.3 1.2 %pack.1 = (bf16[80,768]{1,0:T(8,128)(2,1)S(1)}, bf16[80,768]{1,0:T(8,128)(2,1)S(1)}, bf16[80,768]{1,0:T(8,128)(2,1)S(1)}, f32[1,3072]{1,0:T(1,128)S(1)}, s32[1,1024]{1,0:T(1,128)S(1)}) custom-call(s32[3]{0:T(128)S(1)} %pad_add_fusion.place, s32[1,256]{1,0:T(1,128)S(1)} %bitcast.12, f32[6,128]{1,0:T(8,128)S(1)} %get-tuple-element.33.scale, ...), custom_call_target="tpu_custom_call" | custom-call | flops 1 | bytes 1 | tf_op jit(solution)/shard_map/pack/pallas_call | solution.py:372
  42.6 2.0 %collective-permute-start.10 = (bf16[80,768]{1,0:T(8,128)(2,1)S(1)}, bf16[80,768]{1,0:T(8,128)(2,1)S(1)}, u32[]{:S(2)}, u32[]{:S(2)}) collective-permute-start(bf16[80,768]{1,0:T(8,128)(2,1)S(1)} %get-tuple-element.38), channel_id=1, source_target_pairs={{0,8},{8,0},{16,24},{24,16},{1,9},{9,1},{17,25},{25,17},{2,10},{10... | collective-permute-start | bytes 368648 | tf_op jit(solution)/shard_map/ppermute | solution.py:385
  44.6 0.1 collective-permute-start.11
  44.7 2.3 %collective-permute-start.12 = (bf16[80,768]{1,0:T(8,128)(2,1)S(1)}, bf16[80,768]{1,0:T(8,128)(2,1)S(1)}, u32[]{:S(2)}, u32[]{:S(2)}) collective-permute-start(bf16[80,768]{1,0:T(8,128)(2,1)S(1)} %get-tuple-element.40), channel_id=1, source_target_pairs={{0,24},{8,16},{16,8},{24,0},{1,25},{9,17},{17,9},{25,1},{2,26},{10... | collective-permute-start | bytes 368648 | tf_op jit(solution)/shard_map/ppermute | solution.py:385
  47.0 2.6 %lists.1.hits = f32[3,3072]{1,0:T(4,128)S(1)} custom-call(s32[3]{0:T(128)S(1)} %pad_add_fusion.place, s32[1,1024]{1,0:T(1,128)S(1)} %get-tuple-element.41.plane_ids, s32[1,2048]{1,0:T(1,128)S(1)} %copy-done.7, bf16[272,768]{1,0:T(8,128)(2,1)S(1)} %collective-permute-done.1.refs_0_, bf16[272,768]{1,0:T(8,128)(2,1)S(1)} %collective-permute-done.8.refs_1_.refs_0_, ...), custom_call_target="tpu_custom_call" | custom-call | flops 1 | bytes 1 | tf_op jit(solution)/shard_map/lists/pallas_call | solution.py:372
  49.6 11.5 %collective-permute-done.10.refs_0_ = bf16[80,768]{1,0:T(8,128)(2,1)S(1)} collective-permute-done((bf16[80,768]{1,0:T(8,128)(2,1)S(1)}, bf16[80,768]{1,0:T(8,128)(2,1)S(1)}, u32[]{:S(2)}, u32[]{:S(2)}) %collective-permute-start.10) | collective-permute-done | bytes 122912 | tf_op jit(solution)/shard_map/ppermute | solution.py:385
  61.1 0.0 collective-permute-done.11.refs_1_
  61.1 0.0 collective-permute-done.12.refs_2_
  61.2 0.6 copy-done.4
  61.8 0.9 %slice-done = bf16[64,768]{1,0:T(8,128)(2,1)S(1)} async-done(((bf16[80,768]{1,0:T(8,128)(2,1)}), bf16[64,768]{1,0:T(8,128)(2,1)S(1)}, s32[]{:S(2)}) %slice-start) | async-done | bytes 98328 | tf_op jit(solution)/shard_map/slice | solution.py:557
  62.7 0.1 collective-permute-start.17
  62.8 0.0 collective-permute-done.13.refs_3_.refs_0_
  62.8 0.8 copy-done.5
  63.6 2.6 %meta.1 = (f32[4,3072]{1,0:T(4,128)S(1)}, f32[1,3072]{1,0:T(1,128)S(1)}, s32[1,1024]{1,0:T(1,128)S(1)}, s32[1,384]{1,0:T(1,128)S(1)}, s32[1,512]{1,0:T(1,128)S(1)}, /*index=5*/s32[1,512]{1,0:T(1,128)}) custom-call(s32[3]{0:T(128)S(1)} %pad_add_fusion.place, s32[1,1024]{1,0:T(1,128)S(1)} %get-tuple-element.41.plane_ids, s32[1,512]{1,0:T(1,128)S(1)} %bitcast.10, ...), custom_call_target="tpu_custom_call" | custom-call | flops 1 | bytes 1 | tf_op jit(solution)/shard_map/meta/pallas_call | solution.py:372
  66.2 2.6 %score.6 = f32[2,2,128]{2,1,0:T(2,128)S(1)} custom-call(s32[3]{0:T(128)S(1)} %pad_add_fusion.place, bf16[272,768]{1,0:T(8,128)(2,1)S(1)} %collective-permute-done.13.refs_3_.refs_0_, bf16[272,768]{1,0:T(8,128)(2,1)S(1)} %collective-permute-done.2.refs_4_.refs_1_, f32[4,3072]{1,0:T(4,128)S(1)} %get-tuple-element.48.refs_1_.refs_2_, ...), custom_call_target="tpu_custom_call" | custom-call | flops 1 | bytes 1 | tf_op jit(solution)/shard_map/score/pallas_call | solution.py:372
  68.8 1.6 %collective-permute-start.16 = (f32[2,2,128]{2,1,0:T(2,128)S(1)}, f32[2,2,128]{2,1,0:T(2,128)S(1)}, u32[]{:S(2)}, u32[]{:S(2)}) collective-permute-start(f32[2,2,128]{2,1,0:T(2,128)S(1)} %score.6), channel_id=1, source_target_pairs={{0,24},{8,16},{16,8},{24,0},{1,25},{9,17},{17,9},{25,1},{2,26},{10... | collective-permute-start | bytes 6152 | tf_op jit(solution)/shard_map/ppermute | solution.py:385
  70.4 2.6 %score.4 = f32[2,2,128]{2,1,0:T(2,128)S(1)} custom-call(s32[3]{0:T(128)S(1)} %pad_add_fusion.place, bf16[272,768]{1,0:T(8,128)(2,1)S(1)} %collective-permute-done.1.refs_0_, f32[4,3072]{1,0:T(4,128)S(1)} %get-tuple-element.48.refs_1_.refs_2_, f32[1,3072]{1,0:T(1,128)S(1)} %get-tuple-element.49.refs_2_.refs_3_, ...), custom_call_target="tpu_custom_call" | custom-call | flops 1 | bytes 1 | tf_op jit(solution)/shard_map/score/pallas_call | solution.py:372
  72.9 0.1 collective-permute-start.14
  73.0 2.6 %score.5 = f32[2,2,128]{2,1,0:T(2,128)S(1)} custom-call(s32[3]{0:T(128)S(1)} %pad_add_fusion.place, bf16[272,768]{1,0:T(8,128)(2,1)S(1)} %collective-permute-done.8.refs_1_.refs_0_, bf16[272,768]{1,0:T(8,128)(2,1)S(1)} %collective-permute-done.7.refs_2_.refs_1_, f32[4,3072]{1,0:T(4,128)S(1)} %get-tuple-element.48.refs_1_.refs_2_, ...), custom_call_target="tpu_custom_call" | custom-call | flops 1 | bytes 1 | tf_op jit(solution)/shard_map/score/pallas_call | solution.py:372
  75.6 2.9 %collective-permute-start.15 = (f32[2,2,128]{2,1,0:T(2,128)S(1)}, f32[2,2,128]{2,1,0:T(2,128)S(1)}, u32[]{:S(2)}, u32[]{:S(2)}) collective-permute-start(f32[2,2,128]{2,1,0:T(2,128)S(1)} %score.5), channel_id=1, source_target_pairs={{0,16},{8,24},{16,0},{24,8},{1,17},{9,25},{17,1},{25,9},{2,18},{10... | collective-permute-start | bytes 6152 | tf_op jit(solution)/shard_map/ppermute | solution.py:385
  78.5 2.6 %score.7 = f32[2,2,128]{2,1,0:T(2,128)S(1)} custom-call(s32[3]{0:T(128)S(1)} %pad_add_fusion.place, bf16[272,768]{1,0:T(8,128)(2,1)S(1)} %get-tuple-element.31.refs_0_, f32[4,3072]{1,0:T(4,128)S(1)} %get-tuple-element.48.refs_1_.refs_2_, f32[1,3072]{1,0:T(1,128)S(1)} %get-tuple-element.49.refs_2_.refs_3_, f32[1,3072]{1,0:T(1,128)S(1)} %get-tuple-element.50.refs_3_.refs_4_, ...), custom_call_target="tpu_custom_call" | custom-call | flops 1 | bytes 1 | tf_op jit(solution)/shard_map/score/pallas_call | solution.py:372
  81.1 0.0 collective-permute-done.16
  81.1 0.0 collective-permute-done.14
  81.1 0.0 collective-permute-done.15
  81.1 0.0 collective-permute-done.17.refs_9_
  81.1 2.8 %apply.1 = bf16[512,768]{1,0:T(8,128)(2,1)} custom-call(s32[3]{0:T(128)S(1)} %pad_add_fusion.place, s32[1,1024]{1,0:T(1,128)S(1)} %get-tuple-element.51.own_target, s32[1,384]{1,0:T(1,128)S(1)} %get-tuple-element.52.target, s32[1,512]{1,0:T(1,128)S(1)} %get-tuple-element.53.refreshed, bf16[512,768]{1,0:T(8,128)(2,1)S(1)} %copy-done.1, ...), custom_call_target="tpu_custom_call" | custom-call | flops 1 | bytes 1 | tf_op jit(solution)/shard_map/apply/pallas_call | solution.py:372
  83.9 0.6 multiply_bitcast_fusion
  (11 shorter events, 0.1 us)
Async XLA Ops:
  0.6 0.7 copy-start.7
  0.7 0.7 copy-start.10
  0.7 0.7 copy-start.8
  0.7 0.7 copy-start.9
  1.4 1.1 %copy-start = (bf16[512,768]{1,0:T(8,128)(2,1)S(1)}, bf16[512,768]{1,0:T(8,128)(2,1)}, u32[]{:S(2)}) copy-start(bf16[512,768]{1,0:T(8,128)(2,1)} %refs_0_.3) | copy-start | bytes 2359300
  2.6 1.0 %copy-start.2 = (bf16[256,768]{1,0:T(8,128)(2,1)S(1)}, bf16[256,768]{1,0:T(8,128)(2,1)}, u32[]{:S(2)}) copy-start(bf16[256,768]{1,0:T(8,128)(2,1)} %refs_1_.3) | copy-start | bytes 1179652
  3.6 1.0 %copy-start.6 = (bf16[256,768]{1,0:T(8,128)(2,1)S(1)}, bf16[256,768]{1,0:T(8,128)(2,1)}, u32[]{:S(2)}) copy-start(bf16[256,768]{1,0:T(8,128)(2,1)} %queries.1) | copy-start | bytes 1179652
  4.6 36.8 %copy-start.1 = (bf16[512,768]{1,0:T(8,128)(2,1)S(1)}, bf16[512,768]{1,0:T(8,128)(2,1)}, u32[]{:S(2)}) copy-start(bf16[512,768]{1,0:T(8,128)(2,1)} %refs_0_.3) | copy-start | bytes 2359300
  4.6 36.8 %copy-start.3 = (bf16[256,768]{1,0:T(8,128)(2,1)S(1)}, bf16[256,768]{1,0:T(8,128)(2,1)}, u32[]{:S(2)}) copy-start(bf16[256,768]{1,0:T(8,128)(2,1)} %refs_1_.3) | copy-start | bytes 1179652
  5.5 15.0 %collective-permute-start = (bf16[400,768]{1,0:T(8,128)(2,1)S(1)}, bf16[400,768]{1,0:T(8,128)(2,1)S(1)}, u32[]{:S(2)}, u32[]{:S(2)}) collective-permute-start(bf16[400,768]{1,0:T(8,128)(2,1)S(1)} %get-tuple-element.30), channel_id=1, source_target_pairs={{0,2},{1,5},{2,0},{3,7},{4,6},{5,1},{6,4},{7,3},{8,10},{9,13},{10,... | collective-permute-start | bytes 1843208 | tf_op jit(solution)/shard_map/ppermute | solution.py:433
  8.5 11.1 %collective-permute-start.1 = (bf16[272,768]{1,0:T(8,128)(2,1)S(1)}, bf16[272,768]{1,0:T(8,128)(2,1)S(1)}, u32[]{:S(2)}, u32[]{:S(2)}) collective-permute-start(bf16[272,768]{1,0:T(8,128)(2,1)S(1)} %get-tuple-element.31.refs_0_), channel_id=1, source_target_pairs={{0,8},{8,0},{16,24},{24,16},{1,9},{9,1},{17,25},{25,17},{2,10},{10... | collective-permute-start | bytes 1253384 | tf_op jit(solution)/shard_map/ppermute | solution.py:385
  10.0 9.6 %collective-permute-start.2 = (bf16[272,768]{1,0:T(8,128)(2,1)S(1)}, bf16[272,768]{1,0:T(8,128)(2,1)S(1)}, u32[]{:S(2)}, u32[]{:S(2)}) collective-permute-start(bf16[272,768]{1,0:T(8,128)(2,1)S(1)} %get-tuple-element.31.refs_0_), channel_id=1, source_target_pairs={{8,16},{16,8},{9,17},{17,9},{10,18},{18,10},{11,19},{19,11},{12,20... | collective-permute-start | bytes 1253384 | tf_op jit(solution)/shard_map/ppermute | solution.py:437
  10.7 15.4 %collective-permute-start.4 = (bf16[400,768]{1,0:T(8,128)(2,1)S(1)}, bf16[400,768]{1,0:T(8,128)(2,1)S(1)}, u32[]{:S(2)}, u32[]{:S(2)}) collective-permute-start(bf16[400,768]{1,0:T(8,128)(2,1)S(1)} %get-tuple-element.30), channel_id=1, source_target_pairs={{0,4},{1,3},{2,6},{3,1},{4,0},{5,7},{6,2},{7,5},{8,12},{9,11},{10,... | collective-permute-start | bytes 1843208 | tf_op jit(solution)/shard_map/ppermute | solution.py:434
  20.5 18.8 %collective-permute-start.6 = (bf16[400,768]{1,0:T(8,128)(2,1)S(1)}, bf16[400,768]{1,0:T(8,128)(2,1)S(1)}, u32[]{:S(2)}, u32[]{:S(2)}) collective-permute-start(bf16[400,768]{1,0:T(8,128)(2,1)S(1)} %collective-permute-done.refs_2_.refs_7_.refs_6_), channel_id=1, source_target_pairs={{0,4},{1,3},{2,6},{3,1},{4,0},{5,7},{6,2},{7,5},{8,12},{9,11},{10,... | collective-permute-start | bytes 1843208 | tf_op jit(solution)/shard_map/ppermute | solution.py:441
  24.1 2.6 %collective-permute-start.7 = (bf16[272,768]{1,0:T(8,128)(2,1)S(1)}, bf16[272,768]{1,0:T(8,128)(2,1)S(1)}, u32[]{:S(2)}, u32[]{:S(2)}) collective-permute-start(bf16[272,768]{1,0:T(8,128)(2,1)S(1)} %collective-permute-done.1.refs_0_), channel_id=1, source_target_pairs={{8,16},{16,8},{9,17},{17,9},{10,18},{18,10},{11,19},{19,11},{12,20... | collective-permute-start | bytes 1253384 | tf_op jit(solution)/shard_map/ppermute | solution.py:439
  24.7 14.5 %collective-permute-start.8 = (bf16[272,768]{1,0:T(8,128)(2,1)S(1)}, bf16[272,768]{1,0:T(8,128)(2,1)S(1)}, u32[]{:S(2)}, u32[]{:S(2)}) collective-permute-start(bf16[272,768]{1,0:T(8,128)(2,1)S(1)} %collective-permute-done.2.refs_4_.refs_1_), channel_id=1, source_target_pairs={{8,0},{16,24},{9,1},{17,25},{10,2},{18,26},{11,3},{19,27},{12,4},{... | collective-permute-start | bytes 1253384 | tf_op jit(solution)/shard_map/ppermute | solution.py:440
  26.0 14.5 %collective-permute-start.3 = (bf16[400,768]{1,0:T(8,128)(2,1)S(1)}, bf16[400,768]{1,0:T(8,128)(2,1)S(1)}, u32[]{:S(2)}, u32[]{:S(2)}) collective-permute-start(bf16[400,768]{1,0:T(8,128)(2,1)S(1)} %collective-permute-done.refs_2_.refs_7_.refs_6_), channel_id=1, source_target_pairs={{0,1},{1,0},{2,3},{3,2},{4,5},{5,4},{6,7},{7,6},{8,9},{9,8},{10,11... | collective-permute-start | bytes 1843208 | tf_op jit(solution)/shard_map/ppermute | solution.py:385
  26.1 14.5 %collective-permute-start.5 = (bf16[400,768]{1,0:T(8,128)(2,1)S(1)}, bf16[400,768]{1,0:T(8,128)(2,1)S(1)}, u32[]{:S(2)}, u32[]{:S(2)}) collective-permute-start(bf16[400,768]{1,0:T(8,128)(2,1)S(1)} %collective-permute-done.4.refs_4_.refs_9_.refs_8_), channel_id=1, source_target_pairs={{0,1},{1,0},{2,3},{3,2},{4,5},{5,4},{6,7},{7,6},{8,9},{9,8},{10,11... | collective-permute-start | bytes 1843208 | tf_op jit(solution)/shard_map/ppermute | solution.py:385
  39.3 2.0 %collective-permute-start.9 = (bf16[400,768]{1,0:T(8,128)(2,1)S(1)}, bf16[400,768]{1,0:T(8,128)(2,1)S(1)}, u32[]{:S(2)}, u32[]{:S(2)}) collective-permute-start(bf16[400,768]{1,0:T(8,128)(2,1)S(1)} %collective-permute-done.6.refs_6_.refs_11_.refs_10_), channel_id=1, source_target_pairs={{0,1},{1,0},{2,3},{3,2},{4,5},{5,4},{6,7},{7,6},{8,9},{9,8},{10,11... | collective-permute-start | bytes 1843208 | tf_op jit(solution)/shard_map/ppermute | solution.py:385
  39.3 23.5 %collective-permute-start.13 = (bf16[272,768]{1,0:T(8,128)(2,1)S(1)}, bf16[272,768]{1,0:T(8,128)(2,1)S(1)}, u32[]{:S(2)}, u32[]{:S(2)}) collective-permute-start(bf16[272,768]{1,0:T(8,128)(2,1)S(1)} %collective-permute-done.7.refs_2_.refs_1_), channel_id=1, source_target_pairs={{8,0},{16,24},{9,1},{17,25},{10,2},{18,26},{11,3},{19,27},{12,4},{... | collective-permute-start | bytes 1253384 | tf_op jit(solution)/shard_map/ppermute | solution.py:443
  42.6 18.6 %collective-permute-start.10 = (bf16[80,768]{1,0:T(8,128)(2,1)S(1)}, bf16[80,768]{1,0:T(8,128)(2,1)S(1)}, u32[]{:S(2)}, u32[]{:S(2)}) collective-permute-start(bf16[80,768]{1,0:T(8,128)(2,1)S(1)} %get-tuple-element.38), channel_id=1, source_target_pairs={{0,8},{8,0},{16,24},{24,16},{1,9},{9,1},{17,25},{25,17},{2,10},{10... | collective-permute-start | bytes 368648 | tf_op jit(solution)/shard_map/ppermute | solution.py:385
  44.6 16.5 %collective-permute-start.11 = (bf16[80,768]{1,0:T(8,128)(2,1)S(1)}, bf16[80,768]{1,0:T(8,128)(2,1)S(1)}, u32[]{:S(2)}, u32[]{:S(2)}) collective-permute-start(bf16[80,768]{1,0:T(8,128)(2,1)S(1)} %get-tuple-element.39), channel_id=1, source_target_pairs={{0,16},{8,24},{16,0},{24,8},{1,17},{9,25},{17,1},{25,9},{2,18},{10... | collective-permute-start | bytes 368648 | tf_op jit(solution)/shard_map/ppermute | solution.py:385
  44.7 16.4 %collective-permute-start.12 = (bf16[80,768]{1,0:T(8,128)(2,1)S(1)}, bf16[80,768]{1,0:T(8,128)(2,1)S(1)}, u32[]{:S(2)}, u32[]{:S(2)}) collective-permute-start(bf16[80,768]{1,0:T(8,128)(2,1)S(1)} %get-tuple-element.40), channel_id=1, source_target_pairs={{0,24},{8,16},{16,8},{24,0},{1,25},{9,17},{17,9},{25,1},{2,26},{10... | collective-permute-start | bytes 368648 | tf_op jit(solution)/shard_map/ppermute | solution.py:385
  61.1 0.6 copy-start.4
  61.8 0.9 %slice-start = ((bf16[80,768]{1,0:T(8,128)(2,1)}), bf16[64,768]{1,0:T(8,128)(2,1)S(1)}, s32[]{:S(2)}) async-start(bf16[80,768]{1,0:T(8,128)(2,1)} %copy-done.4), calls=%async_computation | async-start | bytes 196608 | tf_op jit(solution)/shard_map/slice | solution.py:557
  62.7 0.9 %copy-start.5 = (bf16[80,768]{1,0:T(8,128)(2,1)S(1)}, bf16[80,768]{1,0:T(8,128)(2,1)}, u32[]{:S(2)}) copy-start(bf16[80,768]{1,0:T(8,128)(2,1)} %copy-done.4) | copy-start | bytes 368644
  62.7 18.4 %collective-permute-start.17 = (bf16[192,768]{1,0:T(8,128)(2,1)S(1)}, bf16[192,768]{1,0:T(8,128)(2,1)S(1)}, u32[]{:S(2)}, u32[]{:S(2)}) collective-permute-start(bf16[192,768]{1,0:T(8,128)(2,1)S(1)} %pad_maximum_fusion.refs_8_), channel_id=1, source_target_pairs={{0,1},{1,0},{2,3},{3,2},{4,5},{5,4},{6,7},{7,6},{8,9},{9,8},{10,11... | collective-permute-start | bytes 884744 | tf_op jit(solution)/shard_map/ppermute | solution.py:385
  68.8 12.3 %collective-permute-start.16 = (f32[2,2,128]{2,1,0:T(2,128)S(1)}, f32[2,2,128]{2,1,0:T(2,128)S(1)}, u32[]{:S(2)}, u32[]{:S(2)}) collective-permute-start(f32[2,2,128]{2,1,0:T(2,128)S(1)} %score.6), channel_id=1, source_target_pairs={{0,24},{8,16},{16,8},{24,0},{1,25},{9,17},{17,9},{25,1},{2,26},{10... | collective-permute-start | bytes 6152 | tf_op jit(solution)/shard_map/ppermute | solution.py:385
  72.9 8.2 %collective-permute-start.14 = (f32[2,2,128]{2,1,0:T(2,128)S(1)}, f32[2,2,128]{2,1,0:T(2,128)S(1)}, u32[]{:S(2)}, u32[]{:S(2)}) collective-permute-start(f32[2,2,128]{2,1,0:T(2,128)S(1)} %score.4), channel_id=1, source_target_pairs={{0,8},{8,0},{16,24},{24,16},{1,9},{9,1},{17,25},{25,17},{2,10},{10... | collective-permute-start | bytes 6152 | tf_op jit(solution)/shard_map/ppermute | solution.py:385
  75.6 5.5 %collective-permute-start.15 = (f32[2,2,128]{2,1,0:T(2,128)S(1)}, f32[2,2,128]{2,1,0:T(2,128)S(1)}, u32[]{:S(2)}, u32[]{:S(2)}) collective-permute-start(f32[2,2,128]{2,1,0:T(2,128)S(1)} %score.5), channel_id=1, source_target_pairs={{0,16},{8,24},{16,0},{24,8},{1,17},{9,25},{17,1},{25,9},{2,18},{10... | collective-permute-start | bytes 6152 | tf_op jit(solution)/shard_map/ppermute | solution.py:385

commit v10 on v9

v10 whole, which is shorter than its diff:
```python
import functools
import math

import jax
import jax.numpy as jnp
from jax import lax
from jax.experimental import pallas as pl
from jax.experimental.pallas import tpu as pltpu
from jax.sharding import Mesh, PartitionSpec as P

score_scale = 20.0
age_scale = 16.0
epsilon = 1e-06
LOG2E = math.log2(math.e)
MASKED = -1e30
VMEM_LIMIT = 48 * 1024 * 1024
EXTRA = 16
AGES_ROW = 9
LANES = 128

NT = (((1,), (1,)), ((), ()))
NN = (((1,), (0,)), ((), ()))


def one_hot(ids, count):
    rows = lax.broadcasted_iota(jnp.int32, (count, ids.shape[1]), 0)
    return jnp.where(rows == ids, 1.0, 0.0).astype(jnp.bfloat16)


def split_terms(values):
    terms = []
    for _ in range(3):
        terms.append(values.astype(jnp.bfloat16))
        values = values - terms[-1].astype(jnp.float32)
    return terms


def counted(hits):
    count = hits.shape[1]
    before = lax.broadcasted_iota(jnp.int32, (count, count), 0)
    after = lax.broadcasted_iota(jnp.int32, (count, count), 1)
    earlier = jnp.where(before < after, 1.0, 0.0).astype(jnp.bfloat16)
    return lax.dot_general(hits.astype(jnp.bfloat16), earlier, NN, preferred_element_type=jnp.float32)


def small(values):
    return values.astype(jnp.float32).astype(jnp.bfloat16)


def number(values):
    return values.astype(jnp.float32).astype(jnp.int32)


def put(out, row, values):
    width = out.shape[1]
    for i, left in enumerate(range(0, values.shape[1], width)):
        part = small(values[:, left : left + width])
        out[row + i : row + i + 1, : part.shape[1]] = part


def take(rows, row, count):
    width = rows.shape[1]
    parts = [number(rows[row + i : row + i + 1, :]) for i in range(-(-count // width))]
    return jnp.concatenate(parts, axis=1)[:, :count]


def put_ids(out, row, ids):
    lines = -(-ids.shape[1] // out.shape[1])
    put(out, row, ids >> 7)
    put(out, row + lines, ids & 127)


def take_ids(rows, row, count):
    lines = -(-count // rows.shape[1])
    return take(rows, row, count) * LANES + take(rows, row + lines, count)


def prep_kernel(
    place, table, fresh, ref_ids, ages, neg, pos, rows_out, scale_out, *mail, owners_plane, cap, replicas, encode
):
    outer, inner, core = place[0], place[1], place[2]
    width = table.shape[1]
    refresh_dev, rows_dev = fresh.shape[0], table.shape[0]
    planes, share = len(mail), cap // replicas
    pairs = [(plane, side) for plane in range(planes) for side in range(owners_plane)]
    ids = ref_ids[...]
    owner_of = ids // rows_dev
    rank = owner_ranks(
        [owner_of - ((outer ^ plane) * owners_plane + (inner ^ side)) for plane, side in pairs], refresh_dev, cap
    )
    rank = rank - core * share
    code = jnp.full((1, refresh_dev), -1, jnp.int32)
    for i in range(len(pairs)):
        here = (rank[i : i + 1, :] >= 0) & (rank[i : i + 1, :] < share)
        code = jnp.where(here, i * share + rank[i : i + 1, :], code)
    select = one_hot(code, len(pairs) * share)
    packed = lax.dot_general(select, fresh[...], NN, preferred_element_type=jnp.float32).astype(jnp.bfloat16)
    size = owners_plane * share
    for i, out in enumerate(mail):
        out[:size, :] = packed[i * size : (i + 1) * size, :]
        out[size:, :] = jnp.zeros((EXTRA, width), jnp.bfloat16)
        row = size
        for values in (neg[...], pos[...], ids):
            put_ids(out, row, values)
            row += 2 * -(-values.shape[1] // width)

    line, row = 0, 0
    halves = []
    for source in (table, fresh):
        rows = source.shape[0]
        half = rows // replicas
        rows_out[row : row + half, :] = source[pl.ds(pl.multiple_of(core * half, half), half), :]
        row += half
        for block in range(rows // LANES):
            squares = jnp.zeros((LANES, LANES), jnp.float32)
            for chunk in range(width // LANES):
                values = source[block * LANES : (block + 1) * LANES, chunk * LANES : (chunk + 1) * LANES]
                values = values.astype(jnp.float32)
                squares += values * values
            mean = jnp.sum(squares.T, axis=0, keepdims=True) / width
            scale_out[line + block : line + block + 1, :] = lax.rsqrt(mean + epsilon) * (score_scale / width * LOG2E)
        halves += [(line, i, half // LANES) for i in range(half // LANES)]
        line += rows // LANES
    rows_out[row:, :] = jnp.zeros((EXTRA, width), jnp.bfloat16)
    if encode:
        terms = []
        for first, i, count in halves:
            terms += split_terms(scale_out[pl.ds(first + core * count + i, 1), :])
        for i, term in enumerate(terms):
            rows_out[row + i : row + i + 1, :LANES] = term
    put(rows_out, row + AGES_ROW, ages[...])


def relay_kernel(*refs, planes, owners_plane, share, list_size, count, refresh_dev):
    mail, outs = refs[:planes], refs[planes:]
    size = owners_plane * share
    width = mail[0].shape[1]
    row = size + 2 * (-(-list_size // width) + -(-count // width))
    ids = jnp.concatenate([take_ids(block, row, refresh_dev) for block in mail], axis=1)
    for side, out in enumerate(outs):
        for plane, block in enumerate(mail):
            out[plane * share : (plane + 1) * share, :] = block[side * share : (side + 1) * share, :]
        out[planes * share :, :] = jnp.zeros((EXTRA, width), jnp.bfloat16)
        put_ids(out, planes * share, ids)


def in_order(place, values, fast):
    if not fast:
        return values
    own, near, side, far = values
    core = place[2]
    return [own, jnp.where(core == 0, near, side), jnp.where(core == 0, side, near), far]


def owner_ranks(rows, refresh_dev, cap):
    match = jnp.concatenate(rows, axis=0) == 0
    rank = counted(jnp.where(match, 1.0, 0.0)).astype(jnp.int32)
    return jnp.where(match, rank, -cap)


def one_hots(ids, high_count):
    return one_hot(ids >> 7, high_count), one_hot(ids & 127, LANES)


def bitmap(ids, high_count):
    high, low = one_hots(ids, high_count)
    return lax.dot_general(low, high, NT, preferred_element_type=jnp.float32).astype(jnp.bfloat16)


def lookup(one_map, pair):
    hit = lax.dot_general(one_map, pair[0], NN, preferred_element_type=jnp.float32)
    return jnp.sum(hit * pair[1].astype(jnp.float32), axis=0, keepdims=True)


def column_ids(place, owners_plane, rows_dev):
    column = lax.broadcasted_iota(jnp.int32, (1, owners_plane * rows_dev), 1)
    return (place[0] * owners_plane + (place[1] ^ (column // rows_dev))) * rows_dev + column % rows_dev


def meta_kernel(
    place, ages, scale, *refs, sides, pieces, planes, owners_plane, rows_dev, refresh_dev, list_size, count, cap, replicas,
    fast
):
    outer, inner, core = place[0], place[1], place[2]
    lw_out, row_out, scale_out, pos_out, target_out, own_out, ages_out = refs[-7:]
    mail, relayed, buffers = refs[:planes], refs[planes : planes + owners_plane], refs[planes + owners_plane : -7]
    share = cap // replicas
    plane_rows = owners_plane * rows_dev
    high_count = planes * plane_rows // LANES
    own_owner = outer * owners_plane + inner

    ids = [take_ids(block, planes * share, planes * refresh_dev) for block in relayed]
    plane_ids = jnp.concatenate([one[:, :refresh_dev] for one in ids], axis=1)
    table_ids = column_ids(place, owners_plane, rows_dev)
    pair = one_hots(jnp.concatenate([table_ids, plane_ids], axis=1), high_count)
    refreshed = lookup(bitmap(jnp.concatenate(ids, axis=1), high_count), (pair[0][:, :plane_rows], pair[1][:, :plane_rows]))
    refreshed = refreshed > 0.5
    row_out[:, :plane_rows] = jnp.where(refreshed, -1, table_ids).astype(jnp.float32)
    row_out[:, plane_rows:] = plane_ids.astype(jnp.float32)
    own_out[...] = refreshed[:, :rows_dev].astype(jnp.int32)
    ages_out[...] = jnp.where(refreshed[:, :rows_dev], 0, ages[...])

    all_ages = [ages[...]] + [take(buffers[i], row + AGES_ROW, rows_dev) for i, row in sides]
    all_ages = jnp.concatenate(in_order(place, all_ages, fast), axis=1).astype(jnp.float32)
    weight = jnp.exp(-all_ages / age_scale).astype(jnp.bfloat16).astype(jnp.float32)
    log_weight = jnp.where(refreshed, MASKED, jnp.log2(weight))
    log_weight = jnp.concatenate([log_weight, jnp.zeros((1, plane_ids.shape[1]), jnp.float32)], axis=1)
    for group, block in enumerate(mail):
        row = owners_plane * share
        hit = lookup(bitmap(take_ids(block, row, list_size), high_count), pair)
        lw_out[group : group + 1, :] = jnp.where(hit > 0.5, log_weight, MASKED)
        row += 2 * -(-list_size // block.shape[1])
        pos_out[group : group + 1, :] = take_ids(block, row, count).astype(jnp.float32)

    pairs = [(side, plane) for side in range(owners_plane) for plane in range(planes)]
    part_ids = [ids[side][:, plane * refresh_dev : (plane + 1) * refresh_dev] for side, plane in pairs]
    rank = owner_ranks([one // rows_dev - own_owner for one in part_ids], refresh_dev, cap)
    for i in range(len(pairs)):
        took = rank[i : i + 1, :]
        slot = jnp.where(took < 0, -1, ((took // share) ^ core) * share + took % share)
        row = jnp.where(took < 0, 0, part_ids[i] - own_owner * rows_dev)
        kinds = lax.broadcasted_iota(jnp.int32, (8, refresh_dev), 0)
        digits = jnp.where(kinds == 0, row // 16, jnp.where(kinds == 1, row % 16, 1))
        found = lax.dot_general(small(digits), one_hot(slot, cap), NT, preferred_element_type=jnp.float32)
        found = found.astype(jnp.int32)
        target = jnp.where(found[2:3, :] > 0, found[0:1, :] * 16 + found[1:2, :], -1)
        for part in range(replicas):
            first = (part * len(pairs) + i) * share
            target_out[:, first : first + share] = target[:, part * share : (part + 1) * share]

    for source, start, size, column, scale_at in pieces:
        first = piece_offset(place, column)
        for chunk in range(size // LANES):
            if scale_at < 0:
                line = -1 - scale_at + chunk
                row = scale[line : line + 1, :]
            else:
                line = scale_at + 3 * chunk
                row = jnp.sum(buffers[source][line : line + 3, :LANES].astype(jnp.float32), axis=0, keepdims=True)
            scale_out[:, pl.ds(first + chunk * LANES, LANES)] = row


def piece_offset(place, piece):
    column, size, flip, by_core = piece
    if flip is None:
        return column
    column += (place[2] ^ flip) * size
    if by_core is not None:
        column += (place[2] ^ by_core) * size * 2
    return pl.multiple_of(column, size)


def apply_kernel(target, refreshed, table, *refs):
    *arrived, out = refs
    values = jnp.concatenate([block[...] for block in arrived], axis=0)
    rows = lax.broadcasted_iota(jnp.int32, (out.shape[0], values.shape[0]), 0)
    chosen = jnp.where(rows == target[...], 1.0, 0.0).astype(jnp.bfloat16)
    fresh = lax.dot_general(chosen, values, NN, preferred_element_type=jnp.float32)
    for top in range(0, out.shape[0], LANES):
        part = slice(top, top + LANES)
        hit = to_lanes(refreshed[:, part].astype(jnp.float32)) > 0.5
        for left in range(0, out.shape[1], LANES):
            cols = slice(left, left + LANES)
            out[part, cols] = jnp.where(hit, fresh[part, cols], table[part, cols].astype(jnp.float32)).astype(jnp.bfloat16)


def to_lanes(row):
    return jnp.broadcast_to(row, (LANES, LANES)).T


def score_kernel(place, *refs, pieces, flip, given):
    out, total, pos_total, q_scale, pos_b, chosen = refs[-6:]
    positives_row, log_weight, row_ids, scale = refs[given : given + 4]
    positive = positives_row[flip : flip + 1, :]
    queries = refs[0]
    count, width = queries.shape
    if given == 2:
        at_end = (place[0] == 0) | (place[0] == 3)
        chosen[...] = jnp.where(at_end, refs[0][...], refs[1][...])
        queries = chosen
    refs = refs[given + 4 : -6]
    for block in range(count // LANES):
        part = slice(block * LANES, (block + 1) * LANES)
        values = queries[part, :].astype(jnp.float32)
        squares = jnp.sum(values * values, axis=1, keepdims=True)
        q_scale[part, :] = jnp.broadcast_to(lax.rsqrt(squares / width + epsilon), (LANES, LANES))
        pos_b[part, :] = to_lanes(positive[:, part])
    total[...] = jnp.zeros_like(total)
    pos_total[...] = jnp.zeros_like(pos_total)

    def product(piece):
        source, start, size = piece[:3]
        rows = refs[source][start : start + size, :]
        return lax.dot_general(queries[...], rows, NT, preferred_element_type=jnp.float32)

    following = product(pieces[0])
    for i, (_, _, size, column, _) in enumerate(pieces):
        raw = following
        if i + 1 < len(pieces):
            following = product(pieces[i + 1])
        first = piece_offset(place, column)
        for top in range(0, count, 64):
            part = slice(top, top + 64)
            sums, positives = total[part, :], pos_total[part, :]
            query_scale, wanted = q_scale[part, :], pos_b[part, :]
            for chunk in range(size // LANES):
                cols = pl.ds(first + chunk * LANES, LANES)
                powers = raw[part, chunk * LANES : (chunk + 1) * LANES] * query_scale
                powers = powers * scale[:, cols] + log_weight[flip : flip + 1, cols]
                sums = sums + jnp.exp2(powers)
                positives = positives + jnp.where(wanted == row_ids[:, cols], powers, 0.0)
            total[part, :] = sums
            pos_total[part, :] = positives
    for block in range(count // LANES):
        part = slice(block * LANES, (block + 1) * LANES)
        out[0, block : block + 1, :] = jnp.sum(total[part, :].T, axis=0, keepdims=True)
        out[1, block : block + 1, :] = jnp.sum(pos_total[part, :].T, axis=0, keepdims=True)


def whole(memory=pltpu.VMEM):
    return pl.BlockSpec(memory_space=memory)


def call(kernel, name, outs, place, *operands, scratch=(), **options):
    specs = [whole()] * len(operands)
    if place is not None:
        specs = [whole(pltpu.SMEM)] + specs
        operands = (place, *operands)
    return pl.pallas_call(
        functools.partial(kernel, **options),
        out_shape=tuple(outs),
        in_specs=specs,
        out_specs=tuple(whole() for _ in outs),
        scratch_shapes=list(scratch),
        compiler_params=pltpu.CompilerParams(vmem_limit_bytes=VMEM_LIMIT),
        cost_estimate=pl.CostEstimate(flops=1, bytes_accessed=1, transcendentals=0),
        name=name,
    )(*operands)


def swap(values, axis, flip):
    return lax.ppermute(values, axis, [(i, i ^ flip) for i in range(lax.axis_size(axis))])


def on_device(table, ages, refresh_ids, fresh_rows, neg_ids, queries, pos_ids):
    rows_dev, width = table.shape
    refresh_dev = refresh_ids.shape[0]
    planes = lax.axis_size("outer")
    owners_plane = lax.axis_size("inner")
    replicas = lax.axis_size("query")
    owners = planes * owners_plane
    query_count = queries.shape[0]
    list_size = neg_ids.shape[1]
    place = jnp.stack([lax.axis_index(name) for name in ("outer", "inner", "query")]).astype(jnp.int32)
    plane_rows = owners_plane * rows_dev
    plane_refresh = owners_plane * refresh_dev
    all_rows = plane_rows + plane_refresh
    cap = max(2, (2 * refresh_dev + owners - 1) // owners)
    share = cap // replicas
    table_half, fresh_half = rows_dev // replicas, refresh_dev // replicas
    bf16, f32 = jnp.bfloat16, jnp.float32

    fast = replicas == 2 and owners_plane == 4 and planes == 4
    own_ages = ages.reshape(1, -1)
    size = owners_plane * share
    rows_half, scales, *mail = call(
        prep_kernel,
        "prep",
        [
            jax.ShapeDtypeStruct((table_half + fresh_half + EXTRA, width), bf16),
            jax.ShapeDtypeStruct(((rows_dev + refresh_dev) // LANES, LANES), f32),
        ]
        + [jax.ShapeDtypeStruct((size + EXTRA, width), bf16)] * planes,
        place,
        table,
        fresh_rows,
        refresh_ids.reshape(1, -1),
        own_ages,
        neg_ids,
        pos_ids.reshape(1, -1),
        owners_plane=owners_plane,
        cap=cap,
        replicas=replicas,
        encode=fast,
    )
    mail = [mail[0]] + [swap(mail[s], "outer", s) for s in range(1, planes)]

    if fast:
        axes = ("inner", "query")
        first = [(2 * i + c, 2 * (i ^ (1 + c)) + c) for i in range(4) for c in range(2)]
        second = [(2 * i + c, 2 * (i ^ (2 - c)) + c) for i in range(4) for c in range(2)]
        near = lax.ppermute(rows_half, axes, first)
        side_rows = lax.ppermute(rows_half, axes, second)
        middle, outward = [(1, 2), (2, 1)], [(1, 0), (2, 3)]
        beside = swap(queries, "outer", 1)
        across = lax.ppermute(queries, "outer", middle)
        beside, across, *mail = lax.optimization_barrier((beside, across, *mail))
        from_end = lax.ppermute(beside, "outer", middle)
        to_end = lax.ppermute(across, "outer", outward)
        far = lax.ppermute(near, axes, second)
        far, from_end, to_end = lax.optimization_barrier((far, from_end, to_end))
        last = lax.ppermute(from_end, "outer", outward)
        got_queries = [(queries,), (beside,), (to_end, from_end), (last, across)]
        sides = [(i, table_half + fresh_half) for i in (2, 4, 6)]
        buffers = [table, fresh_rows]
        table_pieces = [(0, 0, rows_dev, (0, rows_dev, None, None), -1)]
        fresh_pieces = [(1, 0, refresh_dev, (0, refresh_dev, None, None), -1 - rows_dev // LANES)]
        for slot, by_core, mine in ((1, 0, near), (1, 1, side_rows), (3, None, far)):
            for flip, rows in enumerate((mine, swap(mine, "query", 1))):
                by = None if by_core is None else by_core ^ flip
                data = table_half + fresh_half
                fresh_at = data + 3 * (table_half // LANES)
                table_pieces.append((len(buffers), 0, table_half, (slot * rows_dev, table_half, flip, by), data))
                fresh_pieces.append(
                    (len(buffers), table_half, fresh_half, (slot * refresh_dev, fresh_half, flip, by), fresh_at)
                )
                buffers.append(rows)
    else:
        got_queries = [(queries,)] + [(swap(queries, "outer", s),) for s in range(1, planes)]
        got_rows = [rows_half] + [swap(rows_half, "inner", s) for s in range(1, owners_plane)]
        data = table_half + fresh_half
        gathered = lax.all_gather(jnp.stack(got_rows), "query", axis=0)
        gathered = jnp.swapaxes(gathered, 0, 1)
        buffers = [
            gathered[:, :, :table_half].reshape(plane_rows, width),
            gathered[:, :, table_half:data].reshape(plane_refresh, width),
            *[one[data:] for one in got_rows[1:]],
        ]
        sides = [(i + 1, 0) for i in range(1, owners_plane)]
        scales = []
        for rows in buffers[:2]:
            values = rows.astype(f32)
            mean = jnp.sum(values * values, axis=1) / width
            scales.append((lax.rsqrt(mean + epsilon) * (score_scale / width * LOG2E)).reshape(-1, LANES))
        scales = jnp.concatenate(scales)

        def blocks(buffer, count, line):
            starts = range(0, count, 512)
            return [(buffer, i, 512, (i, 512, None, None), -1 - line - i // LANES) for i in starts]

        table_pieces = blocks(0, plane_rows, 0)
        fresh_pieces = blocks(1, plane_refresh, plane_rows // LANES)

    def shift(pieces, columns):
        return [(a, b, c, (d[0] + columns, *d[1:]), e) for a, b, c, d, e in pieces]

    pieces = table_pieces + shift(fresh_pieces, plane_rows)
    relayed = call(
        relay_kernel,
        "relay",
        [jax.ShapeDtypeStruct((planes * share + EXTRA, width), bf16)] * owners_plane,
        None,
        *mail,
        planes=planes,
        owners_plane=owners_plane,
        share=share,
        list_size=list_size,
        count=query_count,
        refresh_dev=refresh_dev,
    )
    relayed = [relayed[0]] + [swap(relayed[s], "inner", s) for s in range(1, owners_plane)]
    lw, row_ids, scale_plane, positive, target, own, new_ages = call(
        meta_kernel,
        "meta",
        [
            jax.ShapeDtypeStruct((planes, all_rows), f32),
            jax.ShapeDtypeStruct((1, all_rows), f32),
            jax.ShapeDtypeStruct((1, all_rows), f32),
            jax.ShapeDtypeStruct((planes, query_count), f32),
            jax.ShapeDtypeStruct((1, owners * cap), jnp.int32),
            jax.ShapeDtypeStruct((1, rows_dev), jnp.int32),
            jax.ShapeDtypeStruct((1, rows_dev), jnp.int32),
        ],
        place,
        own_ages,
        scales,
        *mail,
        *relayed,
        *buffers,
        sides=sides,
        pieces=pieces,
        planes=planes,
        owners_plane=owners_plane,
        rows_dev=rows_dev,
        refresh_dev=refresh_dev,
        list_size=list_size,
        count=query_count,
        cap=cap,
        replicas=replicas,
        fast=fast,
    )
    new_ages = new_ages.reshape(rows_dev)
    came = jnp.concatenate([one[: planes * share] for one in relayed])
    arrived = [came] + [swap(came, "query", flip) for flip in range(1, replicas)]

    def score(s, given):
        (partial,) = call(
            score_kernel,
            "score",
            [jax.ShapeDtypeStruct((2, query_count // LANES, LANES), f32)],
            place,
            *given,
            positive,
            lw,
            row_ids,
            scale_plane,
            *buffers,
            scratch=[pltpu.VMEM((query_count, LANES), f32)] * 4 + [pltpu.VMEM(queries.shape, bf16)],
            pieces=pieces,
            flip=s,
            given=len(given),
        )
        return partial

    (new_table,) = call(
        apply_kernel, "apply", [jax.ShapeDtypeStruct(table.shape, bf16)], None, target, own, table, *arrived
    )
    partials = [swap(score(s, got_queries[s]), "outer", s) for s in range(1, planes - 1)] + [score(0, got_queries[0])]
    new_table, *tied = lax.optimization_barrier((new_table, *partials, *got_queries[-1]))
    partials, last_queries = tied[: planes - 1], tied[planes - 1 :]
    mine = sum(partials[1:], partials[0])
    mine = mine + swap(score(planes - 1, last_queries), "outer", planes - 1)
    loss = (jnp.log2(mine[0]) - mine[1]) * math.log(2.0)
    return new_table, new_ages, loss.reshape(query_count)


def solution(mesh):
    owners, replicas = mesh.shape["index"], mesh.shape["query"]
    inner = 1 << (int(math.log2(owners)) // 2)
    split = Mesh(mesh.devices.reshape(owners // inner, inner, replicas), ("outer", "inner", "query"))
    index = ("outer", "inner")
    placed = (
        P(index, None),
        P(index),
        P(index),
        P(index, None),
        P(index, None),
        P(("outer", "inner", "query"), None),
        P(("outer", "inner", "query")),
    )
    return jax.shard_map(
        on_device,
        mesh=split,
        in_specs=placed,
        out_specs=(P(index, None), P(index), P(("outer", "inner", "query"))),
        check_vma=False,
    )
```

time: 84.9 us -> 75.5 us (0.89)
  waiting for transfers between devices: 33.1 us -> 24 us
  starting transfers between devices: 23.3 us -> 29.4 us
  local copies, waits for them, and re-layouts: 6.15 us -> 2.89 us
  Pallas kernels: 20.4 us -> 17.4 us
    ppermute x11 -> x14, starting transfers between devices: 11.3 us -> 20.3 us  [swap(): lax.ppermute(values, axis, [(i, i ^ flip) for i in range(lax.axis_size(ax...]
    ppermute x1, waiting for transfers between devices: 12.7 us -> 4.36 us  [on_device(): to_end = lax.ppermute(across, 'outer', outward)]
    pallas_call x9 -> x8, Pallas kernels: 20.4 us -> 17.4 us  [call(): pl.pallas_call(functools.partial(kernel, **options), out_shape=tuple(outs...]
    unnamed x22 -> x18, local copies, waits for them, and re-layouts: 5.26 us -> 2.85 us
    ppermute x1, starting transfers between devices: 3.57 us -> 1.52 us  [on_device(): far = lax.ppermute(near, axes, second)]
    ppermute x1, starting transfers between devices: 1.58 us -> 0.51 us  [on_device(): side_rows = lax.ppermute(rows_half, axes, second)]
    ppermute x1, waiting for transfers between devices: 0.9 us -> 0.01 us  [on_device(): near = lax.ppermute(rows_half, axes, first)]
    slice x4, local copies, waits for them, and re-layouts: 0.9 us -> 0.03 us  [on_device(): came = jnp.concatenate([one[:planes * share] for one in relayed])]
  transfers between devices with their start and end apart: 18 -> 21, of which waited for: 5 -> 7; matrix products, arithmetic and copies ran while one was open for 0% -> 0% of each run, Pallas kernels for 20% -> 18%
where the time goes in v10:
time: 75.5 us; the launch traced here: 75.2 us
  starting transfers between devices  29.4 us (39%)
  waiting for transfers between devices  24 us (32%)
  Pallas kernels  17.4 us (23%)
  local copies, waits for them, and re-layouts  2.89 us (4%)
  between operations  0.79 us (1%)
    ppermute x14, starting transfers between devices, swap(): lax.ppermute(values, axis, [(i, i ^ flip) for i in range(lax.axis_size(ax...  20.3 us
    ppermute x14, waiting for transfers between devices, swap(): lax.ppermute(values, axis, [(i, i ^ flip) for i in range(lax.axis_size(ax...  19.6 us
    pallas_call x8, Pallas kernels, call(): pl.pallas_call(functools.partial(kernel, **options), out_shape=tuple(outs...  17.4 us
    ppermute x1, waiting for transfers between devices, on_device(): to_end = lax.ppermute(across, 'outer', outward)  4.36 us
    ppermute x1, starting transfers between devices, on_device(): near = lax.ppermute(rows_half, axes, first)  3 us
    unnamed x18, local copies, waits for them, and re-layouts  2.85 us
    ppermute x1, starting transfers between devices, on_device(): far = lax.ppermute(near, axes, second)  1.52 us
  transfers between devices with their start and end apart: 21, of which 7 were waited for; matrix products, arithmetic and copies ran while one was open for 0% of the time, Pallas kernels for 18%

profile of v10, /device:TPU:0, one launch (start us, length us, event | category | flops | bytes accessed | tf_op | source)
XLA Modules:
  0.0 75.2 jit_solution(905904792751575556)
XLA Ops:
  0.6 0.0 copy-start.6
  0.6 0.1 pad_add_fusion.place
  0.7 0.0 copy-start.8
  0.7 0.6 copy-done.6
  1.3 0.1 copy-done.8
  1.4 0.0 copy-done.5
  1.4 0.0 copy-done.7
  1.4 1.1 %copy-done = bf16[512,768]{1,0:T(8,128)(2,1)S(1)} copy-done((bf16[512,768]{1,0:T(8,128)(2,1)S(1)}, bf16[512,768]{1,0:T(8,128)(2,1)}, u32[]{:S(2)}) %copy-start) | copy-done | bytes 786456
  2.6 1.0 %copy-done.2 = bf16[256,768]{1,0:T(8,128)(2,1)S(1)} copy-done((bf16[256,768]{1,0:T(8,128)(2,1)S(1)}, bf16[256,768]{1,0:T(8,128)(2,1)}, u32[]{:S(2)}) %copy-start.2) | copy-done | bytes 393240
  3.6 1.1 %prep.1 = (bf16[400,768]{1,0:T(8,128)(2,1)S(1)}, f32[6,128]{1,0:T(8,128)S(1)}, bf16[80,768]{1,0:T(8,128)(2,1)S(1)}, bf16[80,768]{1,0:T(8,128)(2,1)S(1)}, bf16[80...) custom-call(s32[3]{0:T(128)S(1)} %pad_add_fusion.place, bf16[512,768]{1,0:T(8,128)(2,1)S(1)} %copy-done, ...), custom_call_target="tpu_custom_call" | custom-call | flops 1 | bytes 1 | tf_op jit(solution)/shard_map/prep/pallas_call | solution.py:329
  4.6 3.0 %collective-permute-start.8 = (bf16[400,768]{1,0:T(8,128)(2,1)S(1)}, bf16[400,768]{1,0:T(8,128)(2,1)S(1)}, u32[]{:S(2)}, u32[]{:S(2)}) collective-permute-start(bf16[400,768]{1,0:T(8,128)(2,1)S(1)} %get-tuple-element.48), channel_id=1, source_target_pairs={{0,2},{1,5},{2,0},{3,7},{4,6},{5,1},{6,4},{7,3},{8,10},{9,13},{10,... | collective-permute-start | bytes 1843208 | tf_op jit(solution)/shard_map/ppermute | solution.py:392
  7.6 0.0 copy-done.4
  7.7 1.6 %collective-permute-start = (bf16[256,768]{1,0:T(8,128)(2,1)S(1)}, bf16[256,768]{1,0:T(8,128)(2,1)S(1)}, u32[]{:S(2)}, u32[]{:S(2)}) collective-permute-start(bf16[256,768]{1,0:T(8,128)(2,1)S(1)} %copy-done.4), channel_id=1, source_target_pairs={{0,8},{8,0},{16,24},{24,16},{1,9},{9,1},{17,25},{25,17},{2,10},{10... | collective-permute-start | bytes 1179656 | tf_op jit(solution)/shard_map/ppermute | solution.py:342
  9.2 0.7 collective-permute-start.1
  9.9 4.4 %collective-permute-start.2 = (bf16[80,768]{1,0:T(8,128)(2,1)S(1)}, bf16[80,768]{1,0:T(8,128)(2,1)S(1)}, u32[]{:S(2)}, u32[]{:S(2)}) collective-permute-start(bf16[80,768]{1,0:T(8,128)(2,1)S(1)} %get-tuple-element.37), channel_id=1, source_target_pairs={{0,8},{8,0},{16,24},{24,16},{1,9},{9,1},{17,25},{25,17},{2,10},{10... | collective-permute-start | bytes 368648 | tf_op jit(solution)/shard_map/ppermute | solution.py:342
  14.4 0.0 collective-permute-start.3
  14.4 6.9 %collective-permute-done.2.refs_1_ = bf16[80,768]{1,0:T(8,128)(2,1)S(1)} collective-permute-done((bf16[80,768]{1,0:T(8,128)(2,1)S(1)}, bf16[80,768]{1,0:T(8,128)(2,1)S(1)}, u32[]{:S(2)}, u32[]{:S(2)}) %collective-permute-start.2) | collective-permute-done | bytes 122912 | tf_op jit(solution)/shard_map/ppermute | solution.py:342
  21.3 0.5 collective-permute-start.10
  21.8 0.0 collective-permute-done.8.refs_10_.refs_7_.refs_8_
  21.8 1.5 %collective-permute-start.12 = (bf16[400,768]{1,0:T(8,128)(2,1)S(1)}, bf16[400,768]{1,0:T(8,128)(2,1)S(1)}, u32[]{:S(2)}, u32[]{:S(2)}) collective-permute-start(bf16[400,768]{1,0:T(8,128)(2,1)S(1)} %collective-permute-done.8.refs_10_.refs_7_.refs_8_), channel_id=1, source_target_pairs={{0,4},{1,3},{2,6},{3,1},{4,0},{5,7},{6,2},{7,5},{8,12},{9,11},{10,... | collective-permute-start | bytes 1843208 | tf_op jit(solution)/shard_map/ppermute | solution.py:400
  23.3 4.2 %collective-permute-done.3.refs_2_ = bf16[80,768]{1,0:T(8,128)(2,1)S(1)} collective-permute-done((bf16[80,768]{1,0:T(8,128)(2,1)S(1)}, bf16[80,768]{1,0:T(8,128)(2,1)S(1)}, u32[]{:S(2)}, u32[]{:S(2)}) %collective-permute-start.3) | collective-permute-done | bytes 122912 | tf_op jit(solution)/shard_map/ppermute | solution.py:342
  27.6 3.6 %collective-permute-start.4 = (bf16[80,768]{1,0:T(8,128)(2,1)S(1)}, bf16[80,768]{1,0:T(8,128)(2,1)S(1)}, u32[]{:S(2)}, u32[]{:S(2)}) collective-permute-start(bf16[80,768]{1,0:T(8,128)(2,1)S(1)} %get-tuple-element.39), channel_id=1, source_target_pairs={{0,24},{8,16},{16,8},{24,0},{1,25},{9,17},{17,9},{25,1},{2,26},{10... | collective-permute-start | bytes 368648 | tf_op jit(solution)/shard_map/ppermute | solution.py:342
  31.2 3.1 %collective-permute-done.4.refs_3_ = bf16[80,768]{1,0:T(8,128)(2,1)S(1)} collective-permute-done((bf16[80,768]{1,0:T(8,128)(2,1)S(1)}, bf16[80,768]{1,0:T(8,128)(2,1)S(1)}, u32[]{:S(2)}, u32[]{:S(2)}) %collective-permute-start.4) | collective-permute-done | bytes 122912 | tf_op jit(solution)/shard_map/ppermute | solution.py:342
  34.3 0.0 collective-permute-done.refs_0_
  34.3 0.0 collective-permute-done.1.refs_1_
  34.3 0.7 collective-permute-start.13
  35.0 1.3 %collective-permute-start.14 = (bf16[256,768]{1,0:T(8,128)(2,1)S(1)}, bf16[256,768]{1,0:T(8,128)(2,1)S(1)}, u32[]{:S(2)}, u32[]{:S(2)}) collective-permute-start(bf16[256,768]{1,0:T(8,128)(2,1)S(1)} %collective-permute-done.1.refs_1_), channel_id=1, source_target_pairs={{8,0},{16,24},{9,1},{17,25},{10,2},{18,26},{11,3},{19,27},{12,4},{... | collective-permute-start | bytes 1179656 | tf_op jit(solution)/shard_map/ppermute | solution.py:399
  36.3 0.1 relay.1
  36.4 1.6 %collective-permute-start.5 = (bf16[80,768]{1,0:T(8,128)(2,1)S(1)}, bf16[80,768]{1,0:T(8,128)(2,1)S(1)}, u32[]{:S(2)}, u32[]{:S(2)}) collective-permute-start(bf16[80,768]{1,0:T(8,128)(2,1)S(1)} %get-tuple-element.45), channel_id=1, source_target_pairs={{0,2},{2,0},{4,6},{6,4},{1,3},{3,1},{5,7},{7,5},{8,10},{10,8},{12,... | collective-permute-start | bytes 368648 | tf_op jit(solution)/shard_map/ppermute | solution.py:342
  38.0 0.0 collective-permute-done.10.refs_12_.refs_9_.refs_10_
  38.0 1.3 %collective-permute-start.6 = (bf16[80,768]{1,0:T(8,128)(2,1)S(1)}, bf16[80,768]{1,0:T(8,128)(2,1)S(1)}, u32[]{:S(2)}, u32[]{:S(2)}) collective-permute-start(bf16[80,768]{1,0:T(8,128)(2,1)S(1)} %get-tuple-element.46), channel_id=1, source_target_pairs={{0,4},{2,6},{4,0},{6,2},{1,5},{3,7},{5,1},{7,3},{8,12},{10,14},{12... | collective-permute-start | bytes 368648 | tf_op jit(solution)/shard_map/ppermute | solution.py:342
  39.3 0.0 collective-permute-done.13.refs_1_
  39.3 1.4 %collective-permute-start.7 = (bf16[80,768]{1,0:T(8,128)(2,1)S(1)}, bf16[80,768]{1,0:T(8,128)(2,1)S(1)}, u32[]{:S(2)}, u32[]{:S(2)}) collective-permute-start(bf16[80,768]{1,0:T(8,128)(2,1)S(1)} %get-tuple-element.47), channel_id=1, source_target_pairs={{0,6},{2,4},{4,2},{6,0},{1,7},{3,5},{5,3},{7,1},{8,14},{10,12},{12... | collective-permute-start | bytes 368648 | tf_op jit(solution)/shard_map/ppermute | solution.py:342
  40.7 4.4 %collective-permute-done.14.refs_0_ = bf16[256,768]{1,0:T(8,128)(2,1)S(1)} collective-permute-done((bf16[256,768]{1,0:T(8,128)(2,1)S(1)}, bf16[256,768]{1,0:T(8,128)(2,1)S(1)}, u32[]{:S(2)}, u32[]{:S(2)}) %collective-permute-start.14) | collective-permute-done | bytes 393248 | tf_op jit(solution)/shard_map/ppermute | solution.py:399
  45.1 0.0 collective-permute-start.9
  45.1 0.0 collective-permute-done.12.refs_14_.refs_11_.refs_12_
  45.1 0.5 collective-permute-start.11
  45.6 0.0 collective-permute-done.5.refs_5_
  45.6 0.1 collective-permute-start.15
  45.7 0.0 collective-permute-done.6.refs_6_
  45.7 0.0 collective-permute-done.7.refs_7_
  45.8 0.0 copy-start.3
  45.8 0.5 collective-permute-start.16
  46.3 1.5 %collective-permute-start.19 = (bf16[256,768]{1,0:T(8,128)(2,1)S(1)}, bf16[256,768]{1,0:T(8,128)(2,1)S(1)}, u32[]{:S(2)}, u32[]{:S(2)}) collective-permute-start(bf16[256,768]{1,0:T(8,128)(2,1)S(1)} %collective-permute-done.13.refs_1_), channel_id=1, source_target_pairs={{8,0},{16,24},{9,1},{17,25},{10,2},{18,26},{11,3},{19,27},{12,4},{... | collective-permute-start | bytes 1179656 | tf_op jit(solution)/shard_map/ppermute | solution.py:402
  47.8 0.0 collective-permute-done.9.refs_11_.refs_8_.refs_9_
  47.8 0.2 collective-permute-done.11.refs_13_.refs_10_.refs_11_
  48.0 0.9 %collective-permute-done.15.refs_15_.refs_12_.refs_13_ = bf16[400,768]{1,0:T(8,128)(2,1)S(1)} collective-permute-done((bf16[400,768]{1,0:T(8,128)(2,1)S(1)}, bf16[400,768]{1,0:T(8,128)(2,1)S(1)}, u32[]{:S(2)}, u32[]{:S(2)}) %collective-permute-start.15) | collective-permute-done | bytes 614432 | tf_op jit(solution)/shard_map/ppermute | solution.py:342
  48.9 0.0 copy-done.1
  48.9 0.0 copy-done.3
  48.9 4.5 %meta.1 = (f32[4,3072]{1,0:T(4,128)S(1)}, f32[1,3072]{1,0:T(1,128)S(1)}, f32[1,3072]{1,0:T(1,128)S(1)}, f32[4,256]{1,0:T(4,128)S(1)}, s32[1,512]{1,0:T(1,128)S(1...) custom-call(s32[3]{0:T(128)S(1)} %pad_add_fusion.place, s32[1,512]{1,0:T(1,128)S(1)} %bitcast.10, ...), custom_call_target="tpu_custom_call" | custom-call | flops 1 | bytes 1 | tf_op jit(solution)/shard_map/meta/pallas_call | solution.py:329
  53.4 2.6 %score.5 = f32[2,2,128]{2,1,0:T(2,128)S(1)} custom-call(s32[3]{0:T(128)S(1)} %pad_add_fusion.place, bf16[256,768]{1,0:T(8,128)(2,1)S(1)} %collective-permute-done.14.refs_0_, bf16[256,768]{1,0:T(8,128)(2,1)S(1)} %collective-permute-done.13.refs_1_, f32[4,256]{1,0:T(4,128)S(1)} %get-tuple-element.54.refs_1_.refs_2_, ...), custom_call_target="tpu_custom_call" | custom-call | flops 1 | bytes 1 | tf_op jit(solution)/shard_map/score/pallas_call | solution.py:329
  56.0 3.6 %collective-permute-start.18 = (f32[2,2,128]{2,1,0:T(2,128)S(1)}, f32[2,2,128]{2,1,0:T(2,128)S(1)}, u32[]{:S(2)}, u32[]{:S(2)}) collective-permute-start(f32[2,2,128]{2,1,0:T(2,128)S(1)} %score.5), channel_id=1, source_target_pairs={{0,16},{8,24},{16,0},{24,8},{1,17},{9,25},{17,1},{25,9},{2,18},{10... | collective-permute-start | bytes 6152 | tf_op jit(solution)/shard_map/ppermute | solution.py:342
  59.6 2.6 %score.4 = f32[2,2,128]{2,1,0:T(2,128)S(1)} custom-call(s32[3]{0:T(128)S(1)} %pad_add_fusion.place, bf16[256,768]{1,0:T(8,128)(2,1)S(1)} %collective-permute-done.refs_0_, f32[4,256]{1,0:T(4,128)S(1)} %get-tuple-element.54.refs_1_.refs_2_, f32[4,3072]{1,0:T(4,128)S(1)} %get-tuple-element.55.refs_2_.refs_3_, f32[1,3072]{1,0:T(1,128)S(1)} %get-tuple-element.56.refs_3_.refs_4_, ...), custom_call_target="tpu_custom_call" | custom-call | flops 1 | bytes 1 | tf_op jit(solution)/shard_map/score/pallas_call | solution.py:329
  62.2 0.3 collective-permute-start.17
  62.5 2.6 %score.6 = f32[2,2,128]{2,1,0:T(2,128)S(1)} custom-call(s32[3]{0:T(128)S(1)} %pad_add_fusion.place, bf16[256,768]{1,0:T(8,128)(2,1)S(1)} %copy-done.4, f32[4,256]{1,0:T(4,128)S(1)} %get-tuple-element.54.refs_1_.refs_2_, f32[4,3072]{1,0:T(4,128)S(1)} %get-tuple-element.55.refs_2_.refs_3_, f32[1,3072]{1,0:T(1,128)S(1)} %get-tuple-element.56.refs_3_.refs_4_, ...), custom_call_target="tpu_custom_call" | custom-call | flops 1 | bytes 1 | tf_op jit(solution)/shard_map/score/pallas_call | solution.py:329
  65.1 0.0 collective-permute-done.16.refs_1_
  65.1 1.5 %apply.1 = bf16[512,768]{1,0:T(8,128)(2,1)} custom-call(s32[1,512]{1,0:T(1,128)S(1)} %get-tuple-element.52.target, s32[1,512]{1,0:T(1,128)S(1)} %get-tuple-element.53.refreshed, bf16[512,768]{1,0:T(8,128)(2,1)S(1)} %copy-done.1, bf16[256,768]{1,0:T(8,128)(2,1)S(1)} %pad_maximum_fusion.refs_0_, bf16[256,768]{1,0:T(8,128)(2,1)S(1)} %collective-permute-done.16.refs_1_), custom_call_target="tpu_custom_call" | custom-call | flops 1 | bytes 1 | tf_op jit(solution)/shard_map/apply/pallas_call | solution.py:329
  66.6 0.0 collective-permute-done.19.refs_0_
  66.6 0.0 collective-permute-done.18
  66.6 0.0 collective-permute-done.17
  66.6 2.6 %score.7 = f32[2,2,128]{2,1,0:T(2,128)S(1)} custom-call(s32[3]{0:T(128)S(1)} %pad_add_fusion.place, bf16[256,768]{1,0:T(8,128)(2,1)S(1)} %collective-permute-done.19.refs_0_, bf16[256,768]{1,0:T(8,128)(2,1)S(1)} %collective-permute-done.1.refs_1_, f32[4,256]{1,0:T(4,128)S(1)} %get-tuple-element.54.refs_1_.refs_2_, ...), custom_call_target="tpu_custom_call" | custom-call | flops 1 | bytes 1 | tf_op jit(solution)/shard_map/score/pallas_call | solution.py:329
  69.2 1.3 %collective-permute-start.20 = (f32[2,2,128]{2,1,0:T(2,128)S(1)}, f32[2,2,128]{2,1,0:T(2,128)S(1)}, u32[]{:S(2)}, u32[]{:S(2)}) collective-permute-start(f32[2,2,128]{2,1,0:T(2,128)S(1)} %score.7), channel_id=1, source_target_pairs={{0,24},{8,16},{16,8},{24,0},{1,25},{9,17},{17,9},{25,1},{2,26},{10... | collective-permute-start | bytes 6152 | tf_op jit(solution)/shard_map/ppermute | solution.py:342
  70.4 4.2 %collective-permute-done.20 = f32[2,2,128]{2,1,0:T(2,128)S(1)} collective-permute-done((f32[2,2,128]{2,1,0:T(2,128)S(1)}, f32[2,2,128]{2,1,0:T(2,128)S(1)}, u32[]{:S(2)}, u32[]{:S(2)}) %collective-permute-start.20) | collective-permute-done | bytes 2080 | tf_op jit(solution)/shard_map/ppermute | solution.py:342
  74.6 0.6 fusion.1
  (12 shorter events, 0.1 us)
Async XLA Ops:
  0.6 0.7 copy-start.6
  0.7 0.7 copy-start.8
  0.7 0.7 copy-start.5
  0.7 0.7 copy-start.7
  1.4 1.1 %copy-start = (bf16[512,768]{1,0:T(8,128)(2,1)S(1)}, bf16[512,768]{1,0:T(8,128)(2,1)}, u32[]{:S(2)}) copy-start(bf16[512,768]{1,0:T(8,128)(2,1)} %refs_6_.7) | copy-start | bytes 2359300
  2.6 1.0 %copy-start.2 = (bf16[256,768]{1,0:T(8,128)(2,1)S(1)}, bf16[256,768]{1,0:T(8,128)(2,1)}, u32[]{:S(2)}) copy-start(bf16[256,768]{1,0:T(8,128)(2,1)} %refs_7_.3) | copy-start | bytes 1179652
  3.6 4.1 %copy-start.4 = (bf16[256,768]{1,0:T(8,128)(2,1)S(1)}, bf16[256,768]{1,0:T(8,128)(2,1)}, u32[]{:S(2)}) copy-start(bf16[256,768]{1,0:T(8,128)(2,1)} %refs_0_.1) | copy-start | bytes 1179652
  4.6 17.2 %collective-permute-start.8 = (bf16[400,768]{1,0:T(8,128)(2,1)S(1)}, bf16[400,768]{1,0:T(8,128)(2,1)S(1)}, u32[]{:S(2)}, u32[]{:S(2)}) collective-permute-start(bf16[400,768]{1,0:T(8,128)(2,1)S(1)} %get-tuple-element.48), channel_id=1, source_target_pairs={{0,2},{1,5},{2,0},{3,7},{4,6},{5,1},{6,4},{7,3},{8,10},{9,13},{10,... | collective-permute-start | bytes 1843208 | tf_op jit(solution)/shard_map/ppermute | solution.py:392
  7.7 26.7 %collective-permute-start = (bf16[256,768]{1,0:T(8,128)(2,1)S(1)}, bf16[256,768]{1,0:T(8,128)(2,1)S(1)}, u32[]{:S(2)}, u32[]{:S(2)}) collective-permute-start(bf16[256,768]{1,0:T(8,128)(2,1)S(1)} %copy-done.4), channel_id=1, source_target_pairs={{0,8},{8,0},{16,24},{24,16},{1,9},{9,1},{17,25},{25,17},{2,10},{10... | collective-permute-start | bytes 1179656 | tf_op jit(solution)/shard_map/ppermute | solution.py:342
  9.2 25.1 %collective-permute-start.1 = (bf16[256,768]{1,0:T(8,128)(2,1)S(1)}, bf16[256,768]{1,0:T(8,128)(2,1)S(1)}, u32[]{:S(2)}, u32[]{:S(2)}) collective-permute-start(bf16[256,768]{1,0:T(8,128)(2,1)S(1)} %copy-done.4), channel_id=1, source_target_pairs={{8,16},{16,8},{9,17},{17,9},{10,18},{18,10},{11,19},{19,11},{12,20... | collective-permute-start | bytes 1179656 | tf_op jit(solution)/shard_map/ppermute | solution.py:396
  9.9 11.4 %collective-permute-start.2 = (bf16[80,768]{1,0:T(8,128)(2,1)S(1)}, bf16[80,768]{1,0:T(8,128)(2,1)S(1)}, u32[]{:S(2)}, u32[]{:S(2)}) collective-permute-start(bf16[80,768]{1,0:T(8,128)(2,1)S(1)} %get-tuple-element.37), channel_id=1, source_target_pairs={{0,8},{8,0},{16,24},{24,16},{1,9},{9,1},{17,25},{25,17},{2,10},{10... | collective-permute-start | bytes 368648 | tf_op jit(solution)/shard_map/ppermute | solution.py:342
  14.4 13.2 %collective-permute-start.3 = (bf16[80,768]{1,0:T(8,128)(2,1)S(1)}, bf16[80,768]{1,0:T(8,128)(2,1)S(1)}, u32[]{:S(2)}, u32[]{:S(2)}) collective-permute-start(bf16[80,768]{1,0:T(8,128)(2,1)S(1)} %get-tuple-element.38), channel_id=1, source_target_pairs={{0,16},{8,24},{16,0},{24,8},{1,17},{9,25},{17,1},{25,9},{2,18},{10... | collective-permute-start | bytes 368648 | tf_op jit(solution)/shard_map/ppermute | solution.py:342
  21.3 16.7 %collective-permute-start.10 = (bf16[400,768]{1,0:T(8,128)(2,1)S(1)}, bf16[400,768]{1,0:T(8,128)(2,1)S(1)}, u32[]{:S(2)}, u32[]{:S(2)}) collective-permute-start(bf16[400,768]{1,0:T(8,128)(2,1)S(1)} %get-tuple-element.48), channel_id=1, source_target_pairs={{0,4},{1,3},{2,6},{3,1},{4,0},{5,7},{6,2},{7,5},{8,12},{9,11},{10,... | collective-permute-start | bytes 1843208 | tf_op jit(solution)/shard_map/ppermute | solution.py:393
  21.8 23.3 %collective-permute-start.12 = (bf16[400,768]{1,0:T(8,128)(2,1)S(1)}, bf16[400,768]{1,0:T(8,128)(2,1)S(1)}, u32[]{:S(2)}, u32[]{:S(2)}) collective-permute-start(bf16[400,768]{1,0:T(8,128)(2,1)S(1)} %collective-permute-done.8.refs_10_.refs_7_.refs_8_), channel_id=1, source_target_pairs={{0,4},{1,3},{2,6},{3,1},{4,0},{5,7},{6,2},{7,5},{8,12},{9,11},{10,... | collective-permute-start | bytes 1843208 | tf_op jit(solution)/shard_map/ppermute | solution.py:400
  27.6 6.8 %collective-permute-start.4 = (bf16[80,768]{1,0:T(8,128)(2,1)S(1)}, bf16[80,768]{1,0:T(8,128)(2,1)S(1)}, u32[]{:S(2)}, u32[]{:S(2)}) collective-permute-start(bf16[80,768]{1,0:T(8,128)(2,1)S(1)} %get-tuple-element.39), channel_id=1, source_target_pairs={{0,24},{8,16},{16,8},{24,0},{1,25},{9,17},{17,9},{25,1},{2,26},{10... | collective-permute-start | bytes 368648 | tf_op jit(solution)/shard_map/ppermute | solution.py:342
  34.3 4.9 %collective-permute-start.13 = (bf16[256,768]{1,0:T(8,128)(2,1)S(1)}, bf16[256,768]{1,0:T(8,128)(2,1)S(1)}, u32[]{:S(2)}, u32[]{:S(2)}) collective-permute-start(bf16[256,768]{1,0:T(8,128)(2,1)S(1)} %collective-permute-done.refs_0_), channel_id=1, source_target_pairs={{8,16},{16,8},{9,17},{17,9},{10,18},{18,10},{11,19},{19,11},{12,20... | collective-permute-start | bytes 1179656 | tf_op jit(solution)/shard_map/ppermute | solution.py:398
  35.0 10.1 %collective-permute-start.14 = (bf16[256,768]{1,0:T(8,128)(2,1)S(1)}, bf16[256,768]{1,0:T(8,128)(2,1)S(1)}, u32[]{:S(2)}, u32[]{:S(2)}) collective-permute-start(bf16[256,768]{1,0:T(8,128)(2,1)S(1)} %collective-permute-done.1.refs_1_), channel_id=1, source_target_pairs={{8,0},{16,24},{9,1},{17,25},{10,2},{18,26},{11,3},{19,27},{12,4},{... | collective-permute-start | bytes 1179656 | tf_op jit(solution)/shard_map/ppermute | solution.py:399
  36.4 9.2 %collective-permute-start.5 = (bf16[80,768]{1,0:T(8,128)(2,1)S(1)}, bf16[80,768]{1,0:T(8,128)(2,1)S(1)}, u32[]{:S(2)}, u32[]{:S(2)}) collective-permute-start(bf16[80,768]{1,0:T(8,128)(2,1)S(1)} %get-tuple-element.45), channel_id=1, source_target_pairs={{0,2},{2,0},{4,6},{6,4},{1,3},{3,1},{5,7},{7,5},{8,10},{10,8},{12,... | collective-permute-start | bytes 368648 | tf_op jit(solution)/shard_map/ppermute | solution.py:342
  38.0 7.7 %collective-permute-start.6 = (bf16[80,768]{1,0:T(8,128)(2,1)S(1)}, bf16[80,768]{1,0:T(8,128)(2,1)S(1)}, u32[]{:S(2)}, u32[]{:S(2)}) collective-permute-start(bf16[80,768]{1,0:T(8,128)(2,1)S(1)} %get-tuple-element.46), channel_id=1, source_target_pairs={{0,4},{2,6},{4,0},{6,2},{1,5},{3,7},{5,1},{7,3},{8,12},{10,14},{12... | collective-permute-start | bytes 368648 | tf_op jit(solution)/shard_map/ppermute | solution.py:342
  39.3 6.5 %collective-permute-start.7 = (bf16[80,768]{1,0:T(8,128)(2,1)S(1)}, bf16[80,768]{1,0:T(8,128)(2,1)S(1)}, u32[]{:S(2)}, u32[]{:S(2)}) collective-permute-start(bf16[80,768]{1,0:T(8,128)(2,1)S(1)} %get-tuple-element.47), channel_id=1, source_target_pairs={{0,6},{2,4},{4,2},{6,0},{1,7},{3,5},{5,3},{7,1},{8,14},{10,12},{12... | collective-permute-start | bytes 368648 | tf_op jit(solution)/shard_map/ppermute | solution.py:342
  45.1 2.7 %collective-permute-start.9 = (bf16[400,768]{1,0:T(8,128)(2,1)S(1)}, bf16[400,768]{1,0:T(8,128)(2,1)S(1)}, u32[]{:S(2)}, u32[]{:S(2)}) collective-permute-start(bf16[400,768]{1,0:T(8,128)(2,1)S(1)} %collective-permute-done.8.refs_10_.refs_7_.refs_8_), channel_id=1, source_target_pairs={{0,1},{1,0},{2,3},{3,2},{4,5},{5,4},{6,7},{7,6},{8,9},{9,8},{10,11... | collective-permute-start | bytes 1843208 | tf_op jit(solution)/shard_map/ppermute | solution.py:342
  45.1 2.9 %collective-permute-start.11 = (bf16[400,768]{1,0:T(8,128)(2,1)S(1)}, bf16[400,768]{1,0:T(8,128)(2,1)S(1)}, u32[]{:S(2)}, u32[]{:S(2)}) collective-permute-start(bf16[400,768]{1,0:T(8,128)(2,1)S(1)} %collective-permute-done.10.refs_12_.refs_9_.refs_10_), channel_id=1, source_target_pairs={{0,1},{1,0},{2,3},{3,2},{4,5},{5,4},{6,7},{7,6},{8,9},{9,8},{10,11... | collective-permute-start | bytes 1843208 | tf_op jit(solution)/shard_map/ppermute | solution.py:342
  45.6 3.3 %collective-permute-start.15 = (bf16[400,768]{1,0:T(8,128)(2,1)S(1)}, bf16[400,768]{1,0:T(8,128)(2,1)S(1)}, u32[]{:S(2)}, u32[]{:S(2)}) collective-permute-start(bf16[400,768]{1,0:T(8,128)(2,1)S(1)} %collective-permute-done.12.refs_14_.refs_11_.refs_12_), channel_id=1, source_target_pairs={{0,1},{1,0},{2,3},{3,2},{4,5},{5,4},{6,7},{7,6},{8,9},{9,8},{10,11... | collective-permute-start | bytes 1843208 | tf_op jit(solution)/shard_map/ppermute | solution.py:342
  45.7 3.2 %copy-start.1 = (bf16[512,768]{1,0:T(8,128)(2,1)S(1)}, bf16[512,768]{1,0:T(8,128)(2,1)}, u32[]{:S(2)}) copy-start(bf16[512,768]{1,0:T(8,128)(2,1)} %refs_6_.7) | copy-start | bytes 2359300
  45.8 3.1 %copy-start.3 = (bf16[256,768]{1,0:T(8,128)(2,1)S(1)}, bf16[256,768]{1,0:T(8,128)(2,1)}, u32[]{:S(2)}) copy-start(bf16[256,768]{1,0:T(8,128)(2,1)} %refs_7_.3) | copy-start | bytes 1179652
  45.8 19.3 %collective-permute-start.16 = (bf16[256,768]{1,0:T(8,128)(2,1)S(1)}, bf16[256,768]{1,0:T(8,128)(2,1)S(1)}, u32[]{:S(2)}, u32[]{:S(2)}) collective-permute-start(bf16[256,768]{1,0:T(8,128)(2,1)S(1)} %pad_maximum_fusion.refs_0_), channel_id=1, source_target_pairs={{0,1},{1,0},{2,3},{3,2},{4,5},{5,4},{6,7},{7,6},{8,9},{9,8},{10,11... | collective-permute-start | bytes 1179656 | tf_op jit(solution)/shard_map/ppermute | solution.py:342
  46.3 20.3 %collective-permute-start.19 = (bf16[256,768]{1,0:T(8,128)(2,1)S(1)}, bf16[256,768]{1,0:T(8,128)(2,1)S(1)}, u32[]{:S(2)}, u32[]{:S(2)}) collective-permute-start(bf16[256,768]{1,0:T(8,128)(2,1)S(1)} %collective-permute-done.13.refs_1_), channel_id=1, source_target_pairs={{8,0},{16,24},{9,1},{17,25},{10,2},{18,26},{11,3},{19,27},{12,4},{... | collective-permute-start | bytes 1179656 | tf_op jit(solution)/shard_map/ppermute | solution.py:402
  56.0 10.6 %collective-permute-start.18 = (f32[2,2,128]{2,1,0:T(2,128)S(1)}, f32[2,2,128]{2,1,0:T(2,128)S(1)}, u32[]{:S(2)}, u32[]{:S(2)}) collective-permute-start(f32[2,2,128]{2,1,0:T(2,128)S(1)} %score.5), channel_id=1, source_target_pairs={{0,16},{8,24},{16,0},{24,8},{1,17},{9,25},{17,1},{25,9},{2,18},{10... | collective-permute-start | bytes 6152 | tf_op jit(solution)/shard_map/ppermute | solution.py:342
  62.2 4.4 %collective-permute-start.17 = (f32[2,2,128]{2,1,0:T(2,128)S(1)}, f32[2,2,128]{2,1,0:T(2,128)S(1)}, u32[]{:S(2)}, u32[]{:S(2)}) collective-permute-start(f32[2,2,128]{2,1,0:T(2,128)S(1)} %score.4), channel_id=1, source_target_pairs={{0,8},{8,0},{16,24},{24,16},{1,9},{9,1},{17,25},{25,17},{2,10},{10... | collective-permute-start | bytes 6152 | tf_op jit(solution)/shard_map/ppermute | solution.py:342
  69.2 5.4 %collective-permute-start.20 = (f32[2,2,128]{2,1,0:T(2,128)S(1)}, f32[2,2,128]{2,1,0:T(2,128)S(1)}, u32[]{:S(2)}, u32[]{:S(2)}) collective-permute-start(f32[2,2,128]{2,1,0:T(2,128)S(1)} %score.7), channel_id=1, source_target_pairs={{0,24},{8,16},{16,8},{24,0},{1,25},{9,17},{17,9},{25,1},{2,26},{10... | collective-permute-start | bytes 6152 | tf_op jit(solution)/shard_map/ppermute | solution.py:342

commit v11 on v10

--- a/solution.py
+++ b/solution.py
@@ -24,6 +24,10 @@
 
 def one_hot(ids, count):
     rows = lax.broadcasted_iota(jnp.int32, (count, ids.shape[1]), 0)
+    if count <= 256:
+        ids = jnp.where((ids < 0) | (ids >= count), -1, ids)
+        rows, ids = rows.astype(jnp.float32).astype(jnp.bfloat16), ids.astype(jnp.float32).astype(jnp.bfloat16)
+        return jnp.where(rows == ids, jnp.bfloat16(1), jnp.bfloat16(0))
     return jnp.where(rows == ids, 1.0, 0.0).astype(jnp.bfloat16)
 
 
@@ -177,8 +181,14 @@
     return (place[0] * owners_plane + (place[1] ^ (column // rows_dev))) * rows_dev + column % rows_dev
 
 
+def lists_kernel(*refs, first, list_size, high_count):
+    *mail, out = refs
+    for group, block in enumerate(mail):
+        out[group, :, :] = bitmap(take_ids(block, first, list_size), high_count)
+
+
 def meta_kernel(
-    place, ages, scale, *refs, sides, pieces, planes, owners_plane, rows_dev, refresh_dev, list_size, count, cap, replicas,
+    place, maps, ages, scale, *refs, sides, pieces, planes, owners_plane, rows_dev, refresh_dev, list_size, count, cap, replicas,
     fast
 ):
     outer, inner, core = place[0], place[1], place[2]
@@ -207,7 +217,7 @@
     log_weight = jnp.concatenate([log_weight, jnp.zeros((1, plane_ids.shape[1]), jnp.float32)], axis=1)
     for group, block in enumerate(mail):
         row = owners_plane * share
-        hit = lookup(bitmap(take_ids(block, row, list_size), high_count), pair)
+        hit = lookup(maps[group, :, :], pair)
         lw_out[group : group + 1, :] = jnp.where(hit > 0.5, log_weight, MASKED)
         row += 2 * -(-list_size // block.shape[1])
         pos_out[group : group + 1, :] = take_ids(block, row, count).astype(jnp.float32)
@@ -288,23 +298,27 @@
     total[...] = jnp.zeros_like(total)
     pos_total[...] = jnp.zeros_like(pos_total)
 
-    def product(piece):
-        source, start, size = piece[:3]
-        rows = refs[source][start : start + size, :]
+    def product(group):
+        rows = [refs[source][start : start + size, :] for source, start, size, _, _ in group]
+        rows = rows[0] if len(rows) == 1 else jnp.concatenate(rows, axis=0)
         return lax.dot_general(queries[...], rows, NT, preferred_element_type=jnp.float32)
 
-    following = product(pieces[0])
-    for i, (_, _, size, column, _) in enumerate(pieces):
+    narrow = [piece for piece in pieces if piece[2] < 256]
+    groups = [[piece] for piece in pieces if piece[2] >= 256] + [narrow[i : i + 2] for i in range(0, len(narrow), 2)]
+    following = product(groups[0])
+    for i, group in enumerate(groups):
         raw = following
-        if i + 1 < len(pieces):
-            following = product(pieces[i + 1])
-        first = piece_offset(place, column)
+        if i + 1 < len(groups):
+            following = product(groups[i + 1])
+        columns = []
+        for _, _, size, column, _ in group:
+            columns += [piece_offset(place, column) + chunk * LANES for chunk in range(size // LANES)]
         for top in range(0, count, 64):
             part = slice(top, top + 64)
             sums, positives = total[part, :], pos_total[part, :]
             query_scale, wanted = q_scale[part, :], pos_b[part, :]
-            for chunk in range(size // LANES):
-                cols = pl.ds(first + chunk * LANES, LANES)
+            for chunk, first in enumerate(columns):
+                cols = pl.ds(first, LANES)
                 powers = raw[part, chunk * LANES : (chunk + 1) * LANES] * query_scale
                 powers = powers * scale[:, cols] + log_weight[flip : flip + 1, cols]
                 sums = sums + jnp.exp2(powers)
@@ -385,6 +399,18 @@
     )
     mail = [mail[0]] + [swap(mail[s], "outer", s) for s in range(1, planes)]
 
+    high_count = owners * rows_dev // LANES
+    (maps,) = call(
+        lists_kernel,
+        "lists",
+        [jax.ShapeDtypeStruct((planes, LANES, high_count), bf16)],
+        None,
+        *mail,
+        first=size,
+        list_size=list_size,
+        high_count=high_count,
+    )
+
     if fast:
         axes = ("inner", "query")
         first = [(2 * i + c, 2 * (i ^ (1 + c)) + c) for i in range(4) for c in range(2)]
@@ -392,15 +418,14 @@
         near = lax.ppermute(rows_half, axes, first)
         side_rows = lax.ppermute(rows_half, axes, second)
         middle, outward = [(1, 2), (2, 1)], [(1, 0), (2, 3)]
-        beside = swap(queries, "outer", 1)
-        across = lax.ppermute(queries, "outer", middle)
-        beside, across, *mail = lax.optimization_barrier((beside, across, *mail))
+        beside, across = swap(queries, "outer", 1), swap(queries, "outer", 3)
+        beside, across, near, maps, *mail = lax.optimization_barrier((beside, across, near, maps, *mail))
         from_end = lax.ppermute(beside, "outer", middle)
         to_end = lax.ppermute(across, "outer", outward)
         far = lax.ppermute(near, axes, second)
         far, from_end, to_end = lax.optimization_barrier((far, from_end, to_end))
-        last = lax.ppermute(from_end, "outer", outward)
-        got_queries = [(queries,), (beside,), (to_end, from_end), (last, across)]
+        got_queries = [(queries,), (beside,), (across,), (to_end, from_end)]
+        flips = [0, 1, 3, 2]
         sides = [(i, table_half + fresh_half) for i in (2, 4, 6)]
         buffers = [table, fresh_rows]
         table_pieces = [(0, 0, rows_dev, (0, rows_dev, None, None), -1)]
@@ -417,6 +442,7 @@
                 buffers.append(rows)
     else:
         got_queries = [(queries,)] + [(swap(queries, "outer", s),) for s in range(1, planes)]
+        flips = range(planes)
         got_rows = [rows_half] + [swap(rows_half, "inner", s) for s in range(1, owners_plane)]
         data = table_half + fresh_half
         gathered = lax.all_gather(jnp.stack(got_rows), "query", axis=0)
@@ -472,6 +498,7 @@
             jax.ShapeDtypeStruct((1, rows_dev), jnp.int32),
         ],
         place,
+        maps,
         own_ages,
         scales,
         *mail,
@@ -493,7 +520,8 @@
     came = jnp.concatenate([one[: planes * share] for one in relayed])
     arrived = [came] + [swap(came, "query", flip) for flip in range(1, replicas)]
 
-    def score(s, given):
+    def score(i, given):
+        s = flips[i]
         (partial,) = call(
             score_kernel,
             "score",
@@ -515,11 +543,12 @@
     (new_table,) = call(
         apply_kernel, "apply", [jax.ShapeDtypeStruct(table.shape, bf16)], None, target, own, table, *arrived
     )
-    partials = [swap(score(s, got_queries[s]), "outer", s) for s in range(1, planes - 1)] + [score(0, got_queries[0])]
+    partials = [swap(score(i, got_queries[i]), "outer", flips[i]) for i in range(1, planes - 1)]
+    partials.append(score(0, got_queries[0]))
     new_table, *tied = lax.optimization_barrier((new_table, *partials, *got_queries[-1]))
     partials, last_queries = tied[: planes - 1], tied[planes - 1 :]
     mine = sum(partials[1:], partials[0])
-    mine = mine + swap(score(planes - 1, last_queries), "outer", planes - 1)
+    mine = mine + swap(score(planes - 1, last_queries), "outer", flips[-1])
     loss = (jnp.log2(mine[0]) - mine[1]) * math.log(2.0)
     return new_table, new_ages, loss.reshape(query_count)
 

time: 75.5 us -> 82.7 us (1.095)
  waiting for transfers between devices: 24 us -> 35.7 us
  starting transfers between devices: 29.4 us -> 26.4 us
  Pallas kernels: 17.4 us -> 16 us
    ppermute x14 -> x15, waiting for transfers between devices: 19.6 us -> 24.3 us  [swap(): lax.ppermute(values, axis, [(i, i ^ flip) for i in range(lax.axis_size(ax...]
    ppermute x1, waiting for transfers between devices: 0.01 us -> 4.19 us  [on_device(): side_rows = lax.ppermute(rows_half, axes, second)]
    ppermute x2 -> x0, starting transfers between devices: 2.13 us -> none  [the longest x1 1.46 us: on_device(): last = lax.ppermute(from_end, 'outer', outward)]
    ppermute x1, starting transfers between devices: 0.51 us -> 2.49 us  [on_device(): side_rows = lax.ppermute(rows_half, axes, second)]
    ppermute x1, waiting for transfers between devices: 0.01 us -> 1.85 us  [on_device(): far = lax.ppermute(near, axes, second)]
    ppermute x14 -> x15, starting transfers between devices: 20.3 us -> 18.8 us  [swap(): lax.ppermute(values, axis, [(i, i ^ flip) for i in range(lax.axis_size(ax...]
    ppermute x1, starting transfers between devices: 1.52 us -> 0.07 us  [on_device(): far = lax.ppermute(near, axes, second)]
    pallas_call x8 -> x9, Pallas kernels: 17.4 us -> 16 us  [call(): pl.pallas_call(functools.partial(kernel, **options), out_shape=tuple(outs...]
  transfers between devices with their start and end apart: 21 -> 20, of which waited for: 7 -> 9; matrix products, arithmetic and copies ran while one was open for 0% -> 0% of each run, Pallas kernels for 18% -> 15%
where the time goes in v11:
time: 82.7 us; the launch traced here: 82.4 us
  waiting for transfers between devices  35.7 us (43%)
  starting transfers between devices  26.4 us (32%)
  Pallas kernels  16 us (19%)
  local copies, waits for them, and re-layouts  2.89 us (3%)
    ppermute x15, waiting for transfers between devices, swap(): lax.ppermute(values, axis, [(i, i ^ flip) for i in range(lax.axis_size(ax...  24.3 us
    ppermute x15, starting transfers between devices, swap(): lax.ppermute(values, axis, [(i, i ^ flip) for i in range(lax.axis_size(ax...  18.8 us
    pallas_call x9, Pallas kernels, call(): pl.pallas_call(functools.partial(kernel, **options), out_shape=tuple(outs...  16 us
    ppermute x1, waiting for transfers between devices, on_device(): to_end = lax.ppermute(across, 'outer', outward)  5.33 us
    ppermute x1, waiting for transfers between devices, on_device(): side_rows = lax.ppermute(rows_half, axes, second)  4.19 us
    ppermute x1, starting transfers between devices, on_device(): near = lax.ppermute(rows_half, axes, first)  3 us
    unnamed x18, local copies, waits for them, and re-layouts  2.85 us
    ppermute x1, starting transfers between devices, on_device(): side_rows = lax.ppermute(rows_half, axes, second)  2.49 us
  transfers between devices with their start and end apart: 20, of which 9 were waited for; matrix products, arithmetic and copies ran while one was open for 0% of the time, Pallas kernels for 15%

profile of v11, /device:TPU:0, one launch (start us, length us, event | category | flops | bytes accessed | tf_op | source)
XLA Modules:
  0.0 82.4 jit_solution(8398689969509440616)
XLA Ops:
  0.6 0.0 copy-start.6
  0.6 0.1 pad_add_fusion.place
  0.7 0.0 copy-start.8
  0.7 0.0 copy-start.5
  0.7 0.6 copy-done.6
  1.3 0.1 copy-done.8
  1.4 0.0 copy-done.5
  1.4 0.0 copy-done.7
  1.4 1.1 %copy-done = bf16[512,768]{1,0:T(8,128)(2,1)S(1)} copy-done((bf16[512,768]{1,0:T(8,128)(2,1)S(1)}, bf16[512,768]{1,0:T(8,128)(2,1)}, u32[]{:S(2)}) %copy-start) | copy-done | bytes 786456
  2.6 1.0 %copy-done.2 = bf16[256,768]{1,0:T(8,128)(2,1)S(1)} copy-done((bf16[256,768]{1,0:T(8,128)(2,1)S(1)}, bf16[256,768]{1,0:T(8,128)(2,1)}, u32[]{:S(2)}) %copy-start.2) | copy-done | bytes 393240
  3.6 1.1 %prep.1 = (bf16[400,768]{1,0:T(8,128)(2,1)S(1)}, f32[6,128]{1,0:T(8,128)S(1)}, bf16[80,768]{1,0:T(8,128)(2,1)S(1)}, bf16[80,768]{1,0:T(8,128)(2,1)S(1)}, bf16[80...) custom-call(s32[3]{0:T(128)S(1)} %pad_add_fusion.place, bf16[512,768]{1,0:T(8,128)(2,1)S(1)} %copy-done, ...), custom_call_target="tpu_custom_call" | custom-call | flops 1 | bytes 1 | tf_op jit(solution)/shard_map/prep/pallas_call | solution.py:343
  4.6 3.0 %collective-permute-start.2 = (bf16[400,768]{1,0:T(8,128)(2,1)S(1)}, bf16[400,768]{1,0:T(8,128)(2,1)S(1)}, u32[]{:S(2)}, u32[]{:S(2)}) collective-permute-start(bf16[400,768]{1,0:T(8,128)(2,1)S(1)} %get-tuple-element.37), channel_id=1, source_target_pairs={{0,2},{1,5},{2,0},{3,7},{4,6},{5,1},{6,4},{7,3},{8,10},{9,13},{10,... | collective-permute-start | bytes 1843208 | tf_op jit(solution)/shard_map/ppermute | solution.py:418
  7.6 0.0 copy-done.4
  7.6 1.6 %collective-permute-start = (bf16[256,768]{1,0:T(8,128)(2,1)S(1)}, bf16[256,768]{1,0:T(8,128)(2,1)S(1)}, u32[]{:S(2)}, u32[]{:S(2)}) collective-permute-start(bf16[256,768]{1,0:T(8,128)(2,1)S(1)} %copy-done.4), channel_id=1, source_target_pairs={{0,8},{8,0},{16,24},{24,16},{1,9},{9,1},{17,25},{25,17},{2,10},{10... | collective-permute-start | bytes 1179656 | tf_op jit(solution)/shard_map/ppermute | solution.py:356
  9.2 2.5 %collective-permute-start.1 = (bf16[256,768]{1,0:T(8,128)(2,1)S(1)}, bf16[256,768]{1,0:T(8,128)(2,1)S(1)}, u32[]{:S(2)}, u32[]{:S(2)}) collective-permute-start(bf16[256,768]{1,0:T(8,128)(2,1)S(1)} %copy-done.4), channel_id=1, source_target_pairs={{0,24},{8,16},{16,8},{24,0},{1,25},{9,17},{17,9},{25,1},{2,26},{10... | collective-permute-start | bytes 1179656 | tf_op jit(solution)/shard_map/ppermute | solution.py:356
  11.7 0.7 collective-permute-start.3
  12.4 1.2 %collective-permute-start.4 = (bf16[80,768]{1,0:T(8,128)(2,1)S(1)}, bf16[80,768]{1,0:T(8,128)(2,1)S(1)}, u32[]{:S(2)}, u32[]{:S(2)}) collective-permute-start(bf16[80,768]{1,0:T(8,128)(2,1)S(1)} %get-tuple-element.40), channel_id=1, source_target_pairs={{0,16},{8,24},{16,0},{24,8},{1,17},{9,25},{17,1},{25,9},{2,18},{10... | collective-permute-start | bytes 368648 | tf_op jit(solution)/shard_map/ppermute | solution.py:356
  13.6 17.3 %collective-permute-done.3.refs_1_ = bf16[80,768]{1,0:T(8,128)(2,1)S(1)} collective-permute-done((bf16[80,768]{1,0:T(8,128)(2,1)S(1)}, bf16[80,768]{1,0:T(8,128)(2,1)S(1)}, u32[]{:S(2)}, u32[]{:S(2)}) %collective-permute-start.3) | collective-permute-done | bytes 122912 | tf_op jit(solution)/shard_map/ppermute | solution.py:356
  30.9 3.3 %collective-permute-start.5 = (bf16[80,768]{1,0:T(8,128)(2,1)S(1)}, bf16[80,768]{1,0:T(8,128)(2,1)S(1)}, u32[]{:S(2)}, u32[]{:S(2)}) collective-permute-start(bf16[80,768]{1,0:T(8,128)(2,1)S(1)} %get-tuple-element.41), channel_id=1, source_target_pairs={{0,24},{8,16},{16,8},{24,0},{1,25},{9,17},{17,9},{25,1},{2,26},{10... | collective-permute-start | bytes 368648 | tf_op jit(solution)/shard_map/ppermute | solution.py:356
  34.2 1.8 %collective-permute-done.4.refs_2_ = bf16[80,768]{1,0:T(8,128)(2,1)S(1)} collective-permute-done((bf16[80,768]{1,0:T(8,128)(2,1)S(1)}, bf16[80,768]{1,0:T(8,128)(2,1)S(1)}, u32[]{:S(2)}, u32[]{:S(2)}) %collective-permute-start.4) | collective-permute-done | bytes 122912 | tf_op jit(solution)/shard_map/ppermute | solution.py:356
  36.0 2.5 %collective-permute-start.10 = (bf16[400,768]{1,0:T(8,128)(2,1)S(1)}, bf16[400,768]{1,0:T(8,128)(2,1)S(1)}, u32[]{:S(2)}, u32[]{:S(2)}) collective-permute-start(bf16[400,768]{1,0:T(8,128)(2,1)S(1)} %get-tuple-element.37), channel_id=1, source_target_pairs={{0,4},{1,3},{2,6},{3,1},{4,0},{5,7},{6,2},{7,5},{8,12},{9,11},{10,... | collective-permute-start | bytes 1843208 | tf_op jit(solution)/shard_map/ppermute | solution.py:419
  38.5 0.0 collective-permute-done.5.refs_3_
  38.5 0.7 lists.1.maps
  39.2 0.0 collective-permute-done.refs_0_
  39.2 0.0 collective-permute-done.1.refs_0_
  39.2 0.0 collective-permute-done.2.refs_10_.refs_7_.refs_8_
  39.2 0.1 collective-permute-start.12
  39.3 0.7 collective-permute-start.13
  40.0 1.3 %collective-permute-start.14 = (bf16[256,768]{1,0:T(8,128)(2,1)S(1)}, bf16[256,768]{1,0:T(8,128)(2,1)S(1)}, u32[]{:S(2)}, u32[]{:S(2)}) collective-permute-start(bf16[256,768]{1,0:T(8,128)(2,1)S(1)} %collective-permute-done.1.refs_0_), channel_id=1, source_target_pairs={{8,0},{16,24},{9,1},{17,25},{10,2},{18,26},{11,3},{19,27},{12,4},{... | collective-permute-start | bytes 1179656 | tf_op jit(solution)/shard_map/ppermute | solution.py:424
  41.3 0.1 relay.1
  41.4 2.2 %collective-permute-start.6 = (bf16[80,768]{1,0:T(8,128)(2,1)S(1)}, bf16[80,768]{1,0:T(8,128)(2,1)S(1)}, u32[]{:S(2)}, u32[]{:S(2)}) collective-permute-start(bf16[80,768]{1,0:T(8,128)(2,1)S(1)} %get-tuple-element.49), channel_id=1, source_target_pairs={{0,2},{2,0},{4,6},{6,4},{1,3},{3,1},{5,7},{7,5},{8,10},{10,8},{12,... | collective-permute-start | bytes 368648 | tf_op jit(solution)/shard_map/ppermute | solution.py:356
  43.6 4.2 %collective-permute-done.10.refs_12_.refs_9_.refs_10_ = bf16[400,768]{1,0:T(8,128)(2,1)S(1)} collective-permute-done((bf16[400,768]{1,0:T(8,128)(2,1)S(1)}, bf16[400,768]{1,0:T(8,128)(2,1)S(1)}, u32[]{:S(2)}, u32[]{:S(2)}) %collective-permute-start.10) | collective-permute-done | bytes 614432 | tf_op jit(solution)/shard_map/ppermute | solution.py:419
  47.8 2.2 %collective-permute-start.7 = (bf16[80,768]{1,0:T(8,128)(2,1)S(1)}, bf16[80,768]{1,0:T(8,128)(2,1)S(1)}, u32[]{:S(2)}, u32[]{:S(2)}) collective-permute-start(bf16[80,768]{1,0:T(8,128)(2,1)S(1)} %get-tuple-element.50), channel_id=1, source_target_pairs={{0,4},{2,6},{4,0},{6,2},{1,5},{3,7},{5,1},{7,3},{8,12},{10,14},{12... | collective-permute-start | bytes 368648 | tf_op jit(solution)/shard_map/ppermute | solution.py:356
  50.0 0.0 collective-permute-done.13.refs_1_
  50.0 0.0 collective-permute-start.8
  50.0 5.3 %collective-permute-done.14.refs_0_ = bf16[256,768]{1,0:T(8,128)(2,1)S(1)} collective-permute-done((bf16[256,768]{1,0:T(8,128)(2,1)S(1)}, bf16[256,768]{1,0:T(8,128)(2,1)S(1)}, u32[]{:S(2)}, u32[]{:S(2)}) %collective-permute-start.14) | collective-permute-done | bytes 393248 | tf_op jit(solution)/shard_map/ppermute | solution.py:424
  55.3 0.0 collective-permute-start.9
  55.3 1.8 %collective-permute-done.12.refs_14_.refs_11_.refs_12_ = bf16[400,768]{1,0:T(8,128)(2,1)S(1)} collective-permute-done((bf16[400,768]{1,0:T(8,128)(2,1)S(1)}, bf16[400,768]{1,0:T(8,128)(2,1)S(1)}, u32[]{:S(2)}, u32[]{:S(2)}) %collective-permute-start.12) | collective-permute-done | bytes 614432 | tf_op jit(solution)/shard_map/ppermute | solution.py:425
  57.2 0.0 collective-permute-start.11
  57.2 0.0 collective-permute-done.6.refs_5_
  57.2 0.5 collective-permute-start.15
  57.7 0.8 collective-permute-done.7.refs_6_
  58.5 0.0 collective-permute-done.8.refs_7_
  58.5 0.0 copy-start.3
  58.6 0.1 collective-permute-start.16
  58.6 0.0 collective-permute-done.9.refs_11_.refs_8_.refs_9_
  58.6 0.5 collective-permute-done.11.refs_13_.refs_10_.refs_11_
  59.2 0.9 %collective-permute-done.15.refs_15_.refs_12_.refs_13_ = bf16[400,768]{1,0:T(8,128)(2,1)S(1)} collective-permute-done((bf16[400,768]{1,0:T(8,128)(2,1)S(1)}, bf16[400,768]{1,0:T(8,128)(2,1)S(1)}, u32[]{:S(2)}, u32[]{:S(2)}) %collective-permute-start.15) | collective-permute-done | bytes 614432 | tf_op jit(solution)/shard_map/ppermute | solution.py:356
  60.1 0.0 copy-done.1
  60.1 0.0 copy-done.3
  60.1 3.4 %meta.1 = (f32[4,3072]{1,0:T(4,128)S(1)}, f32[1,3072]{1,0:T(1,128)S(1)}, f32[1,3072]{1,0:T(1,128)S(1)}, f32[4,256]{1,0:T(4,128)S(1)}, s32[1,512]{1,0:T(1,128)S(1...) custom-call(s32[3]{0:T(128)S(1)} %pad_add_fusion.place, bf16[4,128,64]{2,1,0:T(8,128)(2,1)S(1)} %lists.1.maps, ...), custom_call_target="tpu_custom_call" | custom-call | flops 1 | bytes 1 | tf_op jit(solution)/shard_map/meta/pallas_call | solution.py:343
  63.5 2.3 %score.5 = f32[2,2,128]{2,1,0:T(2,128)S(1)} custom-call(s32[3]{0:T(128)S(1)} %pad_add_fusion.place, bf16[256,768]{1,0:T(8,128)(2,1)S(1)} %collective-permute-done.1.refs_0_, f32[4,256]{1,0:T(4,128)S(1)} %get-tuple-element.58.refs_1_.refs_2_, f32[4,3072]{1,0:T(4,128)S(1)} %get-tuple-element.59.refs_2_.refs_3_, ...), custom_call_target="tpu_custom_call" | custom-call | flops 1 | bytes 1 | tf_op jit(solution)/shard_map/score/pallas_call | solution.py:343
  65.9 2.9 %collective-permute-start.18 = (f32[2,2,128]{2,1,0:T(2,128)S(1)}, f32[2,2,128]{2,1,0:T(2,128)S(1)}, u32[]{:S(2)}, u32[]{:S(2)}) collective-permute-start(f32[2,2,128]{2,1,0:T(2,128)S(1)} %score.5), channel_id=1, source_target_pairs={{0,24},{8,16},{16,8},{24,0},{1,25},{9,17},{17,9},{25,1},{2,26},{10... | collective-permute-start | bytes 6152 | tf_op jit(solution)/shard_map/ppermute | solution.py:356
  68.8 2.3 %score.4 = f32[2,2,128]{2,1,0:T(2,128)S(1)} custom-call(s32[3]{0:T(128)S(1)} %pad_add_fusion.place, bf16[256,768]{1,0:T(8,128)(2,1)S(1)} %collective-permute-done.refs_0_, f32[4,256]{1,0:T(4,128)S(1)} %get-tuple-element.58.refs_1_.refs_2_, f32[4,3072]{1,0:T(4,128)S(1)} %get-tuple-element.59.refs_2_.refs_3_, f32[1,3072]{1,0:T(1,128)S(1)} %get-tuple-element.60.refs_3_.refs_4_, ...), custom_call_target="tpu_custom_call" | custom-call | flops 1 | bytes 1 | tf_op jit(solution)/shard_map/score/pallas_call | solution.py:343
  71.1 0.1 collective-permute-start.17
  71.2 2.3 %score.6 = f32[2,2,128]{2,1,0:T(2,128)S(1)} custom-call(s32[3]{0:T(128)S(1)} %pad_add_fusion.place, bf16[256,768]{1,0:T(8,128)(2,1)S(1)} %copy-done.4, f32[4,256]{1,0:T(4,128)S(1)} %get-tuple-element.58.refs_1_.refs_2_, f32[4,3072]{1,0:T(4,128)S(1)} %get-tuple-element.59.refs_2_.refs_3_, f32[1,3072]{1,0:T(1,128)S(1)} %get-tuple-element.60.refs_3_.refs_4_, ...), custom_call_target="tpu_custom_call" | custom-call | flops 1 | bytes 1 | tf_op jit(solution)/shard_map/score/pallas_call | solution.py:343
  73.5 0.0 collective-permute-done.16.refs_1_
  73.5 1.5 %apply.1 = bf16[512,768]{1,0:T(8,128)(2,1)} custom-call(s32[1,512]{1,0:T(1,128)S(1)} %get-tuple-element.56.target, s32[1,512]{1,0:T(1,128)S(1)} %get-tuple-element.57.refreshed, bf16[512,768]{1,0:T(8,128)(2,1)S(1)} %copy-done.1, bf16[256,768]{1,0:T(8,128)(2,1)S(1)} %pad_maximum_fusion.refs_0_, bf16[256,768]{1,0:T(8,128)(2,1)S(1)} %collective-permute-done.16.refs_1_), custom_call_target="tpu_custom_call" | custom-call | flops 1 | bytes 1 | tf_op jit(solution)/shard_map/apply/pallas_call | solution.py:343
  75.0 0.0 collective-permute-done.18
  75.0 0.0 collective-permute-done.17
  75.0 2.3 %score.7 = f32[2,2,128]{2,1,0:T(2,128)S(1)} custom-call(s32[3]{0:T(128)S(1)} %pad_add_fusion.place, bf16[256,768]{1,0:T(8,128)(2,1)S(1)} %collective-permute-done.14.refs_0_, bf16[256,768]{1,0:T(8,128)(2,1)S(1)} %collective-permute-done.13.refs_1_, f32[4,256]{1,0:T(4,128)S(1)} %get-tuple-element.58.refs_1_.refs_2_, ...), custom_call_target="tpu_custom_call" | custom-call | flops 1 | bytes 1 | tf_op jit(solution)/shard_map/score/pallas_call | solution.py:343
  77.3 1.6 %collective-permute-start.19 = (f32[2,2,128]{2,1,0:T(2,128)S(1)}, f32[2,2,128]{2,1,0:T(2,128)S(1)}, u32[]{:S(2)}, u32[]{:S(2)}) collective-permute-start(f32[2,2,128]{2,1,0:T(2,128)S(1)} %score.7), channel_id=1, source_target_pairs={{0,16},{8,24},{16,0},{24,8},{1,17},{9,25},{17,1},{25,9},{2,18},{10... | collective-permute-start | bytes 6152 | tf_op jit(solution)/shard_map/ppermute | solution.py:356
  78.9 3.0 %collective-permute-done.19 = f32[2,2,128]{2,1,0:T(2,128)S(1)} collective-permute-done((f32[2,2,128]{2,1,0:T(2,128)S(1)}, f32[2,2,128]{2,1,0:T(2,128)S(1)}, u32[]{:S(2)}, u32[]{:S(2)}) %collective-permute-start.19) | collective-permute-done | bytes 2080 | tf_op jit(solution)/shard_map/ppermute | solution.py:356
  81.9 0.6 fusion.1
  (11 shorter events, 0.1 us)
Async XLA Ops:
  0.6 0.7 copy-start.6
  0.7 0.7 copy-start.8
  0.7 0.7 copy-start.5
  0.7 0.7 copy-start.7
  1.4 1.1 %copy-start = (bf16[512,768]{1,0:T(8,128)(2,1)S(1)}, bf16[512,768]{1,0:T(8,128)(2,1)}, u32[]{:S(2)}) copy-start(bf16[512,768]{1,0:T(8,128)(2,1)} %refs_6_.7) | copy-start | bytes 2359300
  2.6 1.0 %copy-start.2 = (bf16[256,768]{1,0:T(8,128)(2,1)S(1)}, bf16[256,768]{1,0:T(8,128)(2,1)}, u32[]{:S(2)}) copy-start(bf16[256,768]{1,0:T(8,128)(2,1)} %refs_7_.1) | copy-start | bytes 1179652
  3.6 4.1 %copy-start.4 = (bf16[256,768]{1,0:T(8,128)(2,1)S(1)}, bf16[256,768]{1,0:T(8,128)(2,1)}, u32[]{:S(2)}) copy-start(bf16[256,768]{1,0:T(8,128)(2,1)} %refs_0_.1) | copy-start | bytes 1179652
  4.6 34.6 %collective-permute-start.2 = (bf16[400,768]{1,0:T(8,128)(2,1)S(1)}, bf16[400,768]{1,0:T(8,128)(2,1)S(1)}, u32[]{:S(2)}, u32[]{:S(2)}) collective-permute-start(bf16[400,768]{1,0:T(8,128)(2,1)S(1)} %get-tuple-element.37), channel_id=1, source_target_pairs={{0,2},{1,5},{2,0},{3,7},{4,6},{5,1},{6,4},{7,3},{8,10},{9,13},{10,... | collective-permute-start | bytes 1843208 | tf_op jit(solution)/shard_map/ppermute | solution.py:418
  7.6 31.6 %collective-permute-start = (bf16[256,768]{1,0:T(8,128)(2,1)S(1)}, bf16[256,768]{1,0:T(8,128)(2,1)S(1)}, u32[]{:S(2)}, u32[]{:S(2)}) collective-permute-start(bf16[256,768]{1,0:T(8,128)(2,1)S(1)} %copy-done.4), channel_id=1, source_target_pairs={{0,8},{8,0},{16,24},{24,16},{1,9},{9,1},{17,25},{25,17},{2,10},{10... | collective-permute-start | bytes 1179656 | tf_op jit(solution)/shard_map/ppermute | solution.py:356
  9.2 30.0 %collective-permute-start.1 = (bf16[256,768]{1,0:T(8,128)(2,1)S(1)}, bf16[256,768]{1,0:T(8,128)(2,1)S(1)}, u32[]{:S(2)}, u32[]{:S(2)}) collective-permute-start(bf16[256,768]{1,0:T(8,128)(2,1)S(1)} %copy-done.4), channel_id=1, source_target_pairs={{0,24},{8,16},{16,8},{24,0},{1,25},{9,17},{17,9},{25,1},{2,26},{10... | collective-permute-start | bytes 1179656 | tf_op jit(solution)/shard_map/ppermute | solution.py:356
  11.7 19.2 %collective-permute-start.3 = (bf16[80,768]{1,0:T(8,128)(2,1)S(1)}, bf16[80,768]{1,0:T(8,128)(2,1)S(1)}, u32[]{:S(2)}, u32[]{:S(2)}) collective-permute-start(bf16[80,768]{1,0:T(8,128)(2,1)S(1)} %get-tuple-element.39), channel_id=1, source_target_pairs={{0,8},{8,0},{16,24},{24,16},{1,9},{9,1},{17,25},{25,17},{2,10},{10... | collective-permute-start | bytes 368648 | tf_op jit(solution)/shard_map/ppermute | solution.py:356
  12.4 23.6 %collective-permute-start.4 = (bf16[80,768]{1,0:T(8,128)(2,1)S(1)}, bf16[80,768]{1,0:T(8,128)(2,1)S(1)}, u32[]{:S(2)}, u32[]{:S(2)}) collective-permute-start(bf16[80,768]{1,0:T(8,128)(2,1)S(1)} %get-tuple-element.40), channel_id=1, source_target_pairs={{0,16},{8,24},{16,0},{24,8},{1,17},{9,25},{17,1},{25,9},{2,18},{10... | collective-permute-start | bytes 368648 | tf_op jit(solution)/shard_map/ppermute | solution.py:356
  30.9 7.6 %collective-permute-start.5 = (bf16[80,768]{1,0:T(8,128)(2,1)S(1)}, bf16[80,768]{1,0:T(8,128)(2,1)S(1)}, u32[]{:S(2)}, u32[]{:S(2)}) collective-permute-start(bf16[80,768]{1,0:T(8,128)(2,1)S(1)} %get-tuple-element.41), channel_id=1, source_target_pairs={{0,24},{8,16},{16,8},{24,0},{1,25},{9,17},{17,9},{25,1},{2,26},{10... | collective-permute-start | bytes 368648 | tf_op jit(solution)/shard_map/ppermute | solution.py:356
  36.0 11.8 %collective-permute-start.10 = (bf16[400,768]{1,0:T(8,128)(2,1)S(1)}, bf16[400,768]{1,0:T(8,128)(2,1)S(1)}, u32[]{:S(2)}, u32[]{:S(2)}) collective-permute-start(bf16[400,768]{1,0:T(8,128)(2,1)S(1)} %get-tuple-element.37), channel_id=1, source_target_pairs={{0,4},{1,3},{2,6},{3,1},{4,0},{5,7},{6,2},{7,5},{8,12},{9,11},{10,... | collective-permute-start | bytes 1843208 | tf_op jit(solution)/shard_map/ppermute | solution.py:419
  39.2 17.9 %collective-permute-start.12 = (bf16[400,768]{1,0:T(8,128)(2,1)S(1)}, bf16[400,768]{1,0:T(8,128)(2,1)S(1)}, u32[]{:S(2)}, u32[]{:S(2)}) collective-permute-start(bf16[400,768]{1,0:T(8,128)(2,1)S(1)} %collective-permute-done.2.refs_10_.refs_7_.refs_8_), channel_id=1, source_target_pairs={{0,4},{1,3},{2,6},{3,1},{4,0},{5,7},{6,2},{7,5},{8,12},{9,11},{10,... | collective-permute-start | bytes 1843208 | tf_op jit(solution)/shard_map/ppermute | solution.py:425
  39.3 10.6 %collective-permute-start.13 = (bf16[256,768]{1,0:T(8,128)(2,1)S(1)}, bf16[256,768]{1,0:T(8,128)(2,1)S(1)}, u32[]{:S(2)}, u32[]{:S(2)}) collective-permute-start(bf16[256,768]{1,0:T(8,128)(2,1)S(1)} %collective-permute-done.refs_0_), channel_id=1, source_target_pairs={{8,16},{16,8},{9,17},{17,9},{10,18},{18,10},{11,19},{19,11},{12,20... | collective-permute-start | bytes 1179656 | tf_op jit(solution)/shard_map/ppermute | solution.py:423
  40.0 15.3 %collective-permute-start.14 = (bf16[256,768]{1,0:T(8,128)(2,1)S(1)}, bf16[256,768]{1,0:T(8,128)(2,1)S(1)}, u32[]{:S(2)}, u32[]{:S(2)}) collective-permute-start(bf16[256,768]{1,0:T(8,128)(2,1)S(1)} %collective-permute-done.1.refs_0_), channel_id=1, source_target_pairs={{8,0},{16,24},{9,1},{17,25},{10,2},{18,26},{11,3},{19,27},{12,4},{... | collective-permute-start | bytes 1179656 | tf_op jit(solution)/shard_map/ppermute | solution.py:424
  41.4 15.8 %collective-permute-start.6 = (bf16[80,768]{1,0:T(8,128)(2,1)S(1)}, bf16[80,768]{1,0:T(8,128)(2,1)S(1)}, u32[]{:S(2)}, u32[]{:S(2)}) collective-permute-start(bf16[80,768]{1,0:T(8,128)(2,1)S(1)} %get-tuple-element.49), channel_id=1, source_target_pairs={{0,2},{2,0},{4,6},{6,4},{1,3},{3,1},{5,7},{7,5},{8,10},{10,8},{12,... | collective-permute-start | bytes 368648 | tf_op jit(solution)/shard_map/ppermute | solution.py:356
  47.8 10.7 %collective-permute-start.7 = (bf16[80,768]{1,0:T(8,128)(2,1)S(1)}, bf16[80,768]{1,0:T(8,128)(2,1)S(1)}, u32[]{:S(2)}, u32[]{:S(2)}) collective-permute-start(bf16[80,768]{1,0:T(8,128)(2,1)S(1)} %get-tuple-element.50), channel_id=1, source_target_pairs={{0,4},{2,6},{4,0},{6,2},{1,5},{3,7},{5,1},{7,3},{8,12},{10,14},{12... | collective-permute-start | bytes 368648 | tf_op jit(solution)/shard_map/ppermute | solution.py:356
  50.0 8.5 %collective-permute-start.8 = (bf16[80,768]{1,0:T(8,128)(2,1)S(1)}, bf16[80,768]{1,0:T(8,128)(2,1)S(1)}, u32[]{:S(2)}, u32[]{:S(2)}) collective-permute-start(bf16[80,768]{1,0:T(8,128)(2,1)S(1)} %get-tuple-element.51), channel_id=1, source_target_pairs={{0,6},{2,4},{4,2},{6,0},{1,7},{3,5},{5,3},{7,1},{8,14},{10,12},{12... | collective-permute-start | bytes 368648 | tf_op jit(solution)/shard_map/ppermute | solution.py:356
  55.3 3.3 %collective-permute-start.9 = (bf16[400,768]{1,0:T(8,128)(2,1)S(1)}, bf16[400,768]{1,0:T(8,128)(2,1)S(1)}, u32[]{:S(2)}, u32[]{:S(2)}) collective-permute-start(bf16[400,768]{1,0:T(8,128)(2,1)S(1)} %collective-permute-done.2.refs_10_.refs_7_.refs_8_), channel_id=1, source_target_pairs={{0,1},{1,0},{2,3},{3,2},{4,5},{5,4},{6,7},{7,6},{8,9},{9,8},{10,11... | collective-permute-start | bytes 1843208 | tf_op jit(solution)/shard_map/ppermute | solution.py:356
  57.2 2.0 %collective-permute-start.11 = (bf16[400,768]{1,0:T(8,128)(2,1)S(1)}, bf16[400,768]{1,0:T(8,128)(2,1)S(1)}, u32[]{:S(2)}, u32[]{:S(2)}) collective-permute-start(bf16[400,768]{1,0:T(8,128)(2,1)S(1)} %collective-permute-done.10.refs_12_.refs_9_.refs_10_), channel_id=1, source_target_pairs={{0,1},{1,0},{2,3},{3,2},{4,5},{5,4},{6,7},{7,6},{8,9},{9,8},{10,11... | collective-permute-start | bytes 1843208 | tf_op jit(solution)/shard_map/ppermute | solution.py:356
  57.2 2.9 %collective-permute-start.15 = (bf16[400,768]{1,0:T(8,128)(2,1)S(1)}, bf16[400,768]{1,0:T(8,128)(2,1)S(1)}, u32[]{:S(2)}, u32[]{:S(2)}) collective-permute-start(bf16[400,768]{1,0:T(8,128)(2,1)S(1)} %collective-permute-done.12.refs_14_.refs_11_.refs_12_), channel_id=1, source_target_pairs={{0,1},{1,0},{2,3},{3,2},{4,5},{5,4},{6,7},{7,6},{8,9},{9,8},{10,11... | collective-permute-start | bytes 1843208 | tf_op jit(solution)/shard_map/ppermute | solution.py:356
  57.7 2.4 %copy-start.1 = (bf16[512,768]{1,0:T(8,128)(2,1)S(1)}, bf16[512,768]{1,0:T(8,128)(2,1)}, u32[]{:S(2)}) copy-start(bf16[512,768]{1,0:T(8,128)(2,1)} %refs_6_.7) | copy-start | bytes 2359300
  58.5 1.6 %copy-start.3 = (bf16[256,768]{1,0:T(8,128)(2,1)S(1)}, bf16[256,768]{1,0:T(8,128)(2,1)}, u32[]{:S(2)}) copy-start(bf16[256,768]{1,0:T(8,128)(2,1)} %refs_7_.1) | copy-start | bytes 1179652
  58.6 14.9 %collective-permute-start.16 = (bf16[256,768]{1,0:T(8,128)(2,1)S(1)}, bf16[256,768]{1,0:T(8,128)(2,1)S(1)}, u32[]{:S(2)}, u32[]{:S(2)}) collective-permute-start(bf16[256,768]{1,0:T(8,128)(2,1)S(1)} %pad_maximum_fusion.refs_0_), channel_id=1, source_target_pairs={{0,1},{1,0},{2,3},{3,2},{4,5},{5,4},{6,7},{7,6},{8,9},{9,8},{10,11... | collective-permute-start | bytes 1179656 | tf_op jit(solution)/shard_map/ppermute | solution.py:356
  65.9 9.1 %collective-permute-start.18 = (f32[2,2,128]{2,1,0:T(2,128)S(1)}, f32[2,2,128]{2,1,0:T(2,128)S(1)}, u32[]{:S(2)}, u32[]{:S(2)}) collective-permute-start(f32[2,2,128]{2,1,0:T(2,128)S(1)} %score.5), channel_id=1, source_target_pairs={{0,24},{8,16},{16,8},{24,0},{1,25},{9,17},{17,9},{25,1},{2,26},{10... | collective-permute-start | bytes 6152 | tf_op jit(solution)/shard_map/ppermute | solution.py:356
  71.1 3.9 %collective-permute-start.17 = (f32[2,2,128]{2,1,0:T(2,128)S(1)}, f32[2,2,128]{2,1,0:T(2,128)S(1)}, u32[]{:S(2)}, u32[]{:S(2)}) collective-permute-start(f32[2,2,128]{2,1,0:T(2,128)S(1)} %score.4), channel_id=1, source_target_pairs={{0,8},{8,0},{16,24},{24,16},{1,9},{9,1},{17,25},{25,17},{2,10},{10... | collective-permute-start | bytes 6152 | tf_op jit(solution)/shard_map/ppermute | solution.py:356
  77.3 4.5 %collective-permute-start.19 = (f32[2,2,128]{2,1,0:T(2,128)S(1)}, f32[2,2,128]{2,1,0:T(2,128)S(1)}, u32[]{:S(2)}, u32[]{:S(2)}) collective-permute-start(f32[2,2,128]{2,1,0:T(2,128)S(1)} %score.7), channel_id=1, source_target_pairs={{0,16},{8,24},{16,0},{24,8},{1,17},{9,25},{17,1},{25,9},{2,18},{10... | collective-permute-start | bytes 6152 | tf_op jit(solution)/shard_map/ppermute | solution.py:356

commit v12 on v11

--- a/solution.py
+++ b/solution.py
@@ -80,7 +80,7 @@
 
 
 def prep_kernel(
-    place, table, fresh, ref_ids, ages, neg, pos, rows_out, scale_out, *mail, owners_plane, cap, replicas, encode
+    place, table, fresh, ref_ids, neg, pos, rows_out, scale_out, *mail, owners_plane, cap, replicas, encode
 ):
     outer, inner, core = place[0], place[1], place[2]
     width = table.shape[1]
@@ -132,10 +132,9 @@
             terms += split_terms(scale_out[pl.ds(first + core * count + i, 1), :])
         for i, term in enumerate(terms):
             rows_out[row + i : row + i + 1, :LANES] = term
-    put(rows_out, row + AGES_ROW, ages[...])
-
-
-def relay_kernel(*refs, planes, owners_plane, share, list_size, count, refresh_dev):
+
+
+def relay_kernel(ages, *refs, planes, owners_plane, share, list_size, count, refresh_dev):
     mail, outs = refs[:planes], refs[planes:]
     size = owners_plane * share
     width = mail[0].shape[1]
@@ -146,14 +145,7 @@
             out[plane * share : (plane + 1) * share, :] = block[side * share : (side + 1) * share, :]
         out[planes * share :, :] = jnp.zeros((EXTRA, width), jnp.bfloat16)
         put_ids(out, planes * share, ids)
-
-
-def in_order(place, values, fast):
-    if not fast:
-        return values
-    own, near, side, far = values
-    core = place[2]
-    return [own, jnp.where(core == 0, near, side), jnp.where(core == 0, side, near), far]
+        put(out, planes * share + AGES_ROW, ages[...])
 
 
 def owner_ranks(rows, refresh_dev, cap):
@@ -188,12 +180,11 @@
 
 
 def meta_kernel(
-    place, maps, ages, scale, *refs, sides, pieces, planes, owners_plane, rows_dev, refresh_dev, list_size, count, cap, replicas,
-    fast
+    place, maps, ages, *refs, planes, owners_plane, rows_dev, refresh_dev, list_size, count, cap, replicas
 ):
     outer, inner, core = place[0], place[1], place[2]
-    lw_out, row_out, scale_out, pos_out, target_out, own_out, ages_out = refs[-7:]
-    mail, relayed, buffers = refs[:planes], refs[planes : planes + owners_plane], refs[planes + owners_plane : -7]
+    lw_out, row_out, pos_out, target_out, own_out, ages_out = refs[-6:]
+    mail, relayed = refs[:planes], refs[planes:-6]
     share = cap // replicas
     plane_rows = owners_plane * rows_dev
     high_count = planes * plane_rows // LANES
@@ -210,8 +201,8 @@
     own_out[...] = refreshed[:, :rows_dev].astype(jnp.int32)
     ages_out[...] = jnp.where(refreshed[:, :rows_dev], 0, ages[...])
 
-    all_ages = [ages[...]] + [take(buffers[i], row + AGES_ROW, rows_dev) for i, row in sides]
-    all_ages = jnp.concatenate(in_order(place, all_ages, fast), axis=1).astype(jnp.float32)
+    all_ages = [take(block, planes * share + AGES_ROW, rows_dev) for block in relayed]
+    all_ages = jnp.concatenate(all_ages, axis=1).astype(jnp.float32)
     weight = jnp.exp(-all_ages / age_scale).astype(jnp.bfloat16).astype(jnp.float32)
     log_weight = jnp.where(refreshed, MASKED, jnp.log2(weight))
     log_weight = jnp.concatenate([log_weight, jnp.zeros((1, plane_ids.shape[1]), jnp.float32)], axis=1)
@@ -238,17 +229,6 @@
             first = (part * len(pairs) + i) * share
             target_out[:, first : first + share] = target[:, part * share : (part + 1) * share]
 
-    for source, start, size, column, scale_at in pieces:
-        first = piece_offset(place, column)
-        for chunk in range(size // LANES):
-            if scale_at < 0:
-                line = -1 - scale_at + chunk
-                row = scale[line : line + 1, :]
-            else:
-                line = scale_at + 3 * chunk
-                row = jnp.sum(buffers[source][line : line + 3, :LANES].astype(jnp.float32), axis=0, keepdims=True)
-            scale_out[:, pl.ds(first + chunk * LANES, LANES)] = row
-
 
 def piece_offset(place, piece):
     column, size, flip, by_core = piece
@@ -278,8 +258,9 @@
     return jnp.broadcast_to(row, (LANES, LANES)).T
 
 
-def score_kernel(place, *refs, pieces, flip, given):
+def score_kernel(place, *refs, pieces, flip, given, follows):
     out, total, pos_total, q_scale, pos_b, chosen = refs[-6:]
+    before, refs = (refs[0], refs[1:]) if follows else (None, refs)
     positives_row, log_weight, row_ids, scale = refs[given : given + 4]
     positive = positives_row[flip : flip + 1, :]
     queries = refs[0]
@@ -311,24 +292,33 @@
         if i + 1 < len(groups):
             following = product(groups[i + 1])
         columns = []
-        for _, _, size, column, _ in group:
-            columns += [piece_offset(place, column) + chunk * LANES for chunk in range(size // LANES)]
+        for source, _, size, column, scale_at in group:
+            for chunk in range(size // LANES):
+                if scale_at < 0:
+                    line = -1 - scale_at + chunk
+                    row_scale = scale[line : line + 1, :]
+                else:
+                    line = scale_at + 3 * chunk
+                    row_scale = refs[source][line : line + 3, :LANES].astype(jnp.float32)
+                    row_scale = jnp.sum(row_scale, axis=0, keepdims=True)
+                columns.append((piece_offset(place, column) + chunk * LANES, row_scale))
         for top in range(0, count, 64):
             part = slice(top, top + 64)
             sums, positives = total[part, :], pos_total[part, :]
             query_scale, wanted = q_scale[part, :], pos_b[part, :]
-            for chunk, first in enumerate(columns):
+            for chunk, (first, row_scale) in enumerate(columns):
                 cols = pl.ds(first, LANES)
                 powers = raw[part, chunk * LANES : (chunk + 1) * LANES] * query_scale
-                powers = powers * scale[:, cols] + log_weight[flip : flip + 1, cols]
+                powers = powers * row_scale + log_weight[flip : flip + 1, cols]
                 sums = sums + jnp.exp2(powers)
                 positives = positives + jnp.where(wanted == row_ids[:, cols], powers, 0.0)
             total[part, :] = sums
             pos_total[part, :] = positives
     for block in range(count // LANES):
         part = slice(block * LANES, (block + 1) * LANES)
-        out[0, block : block + 1, :] = jnp.sum(total[part, :].T, axis=0, keepdims=True)
-        out[1, block : block + 1, :] = jnp.sum(pos_total[part, :].T, axis=0, keepdims=True)
+        for i, sums in enumerate((total, pos_total)):
+            row = jnp.sum(sums[part, :].T, axis=0, keepdims=True)
+            out[i, block : block + 1, :] = row + before[i, block : block + 1, :] if follows else row
 
 
 def whole(memory=pltpu.VMEM):
@@ -389,7 +379,6 @@
         table,
         fresh_rows,
         refresh_ids.reshape(1, -1),
-        own_ages,
         neg_ids,
         pos_ids.reshape(1, -1),
         owners_plane=owners_plane,
@@ -398,6 +387,8 @@
         encode=fast,
     )
     mail = [mail[0]] + [swap(mail[s], "outer", s) for s in range(1, planes)]
+    bare = queries
+    queries, *mail = lax.optimization_barrier((queries, *mail))
 
     high_count = owners * rows_dev // LANES
     (maps,) = call(
@@ -411,35 +402,111 @@
         high_count=high_count,
     )
 
+    relayed = call(
+        relay_kernel,
+        "relay",
+        [jax.ShapeDtypeStruct((planes * share + EXTRA, width), bf16)] * owners_plane,
+        None,
+        own_ages,
+        *mail,
+        planes=planes,
+        owners_plane=owners_plane,
+        share=share,
+        list_size=list_size,
+        count=query_count,
+        refresh_dev=refresh_dev,
+    )
+    relayed = [relayed[0]] + [swap(relayed[s], "inner", s) for s in range(1, owners_plane)]
+    lw, row_ids, positive, target, own, new_ages = call(
+        meta_kernel,
+        "meta",
+        [
+            jax.ShapeDtypeStruct((planes, all_rows), f32),
+            jax.ShapeDtypeStruct((1, all_rows), f32),
+            jax.ShapeDtypeStruct((planes, query_count), f32),
+            jax.ShapeDtypeStruct((1, owners * cap), jnp.int32),
+            jax.ShapeDtypeStruct((1, rows_dev), jnp.int32),
+            jax.ShapeDtypeStruct((1, rows_dev), jnp.int32),
+        ],
+        place,
+        maps,
+        own_ages,
+        *mail,
+        *relayed,
+        planes=planes,
+        owners_plane=owners_plane,
+        rows_dev=rows_dev,
+        refresh_dev=refresh_dev,
+        list_size=list_size,
+        count=query_count,
+        cap=cap,
+        replicas=replicas,
+    )
+
+    def shift(pieces, columns):
+        return [(a, b, c, (d[0] + columns, *d[1:]), e) for a, b, c, d, e in pieces]
+
+    def score(i, given, buffers, pieces, before=()):
+        (partial,) = call(
+            score_kernel,
+            "score",
+            [jax.ShapeDtypeStruct((2, query_count // LANES, LANES), f32)],
+            place,
+            *before,
+            *given,
+            positive,
+            lw,
+            row_ids,
+            scales,
+            *buffers,
+            scratch=[pltpu.VMEM((query_count, LANES), f32)] * 4 + [pltpu.VMEM(queries.shape, bf16)],
+            pieces=pieces,
+            flip=flips[i],
+            given=len(given),
+            follows=len(before),
+        )
+        return partial
+
     if fast:
         axes = ("inner", "query")
         first = [(2 * i + c, 2 * (i ^ (1 + c)) + c) for i in range(4) for c in range(2)]
         second = [(2 * i + c, 2 * (i ^ (2 - c)) + c) for i in range(4) for c in range(2)]
         near = lax.ppermute(rows_half, axes, first)
-        side_rows = lax.ppermute(rows_half, axes, second)
+        behind, *_ = lax.optimization_barrier((rows_half, *relayed))
+        side_rows = lax.ppermute(behind, axes, second)
         middle, outward = [(1, 2), (2, 1)], [(1, 0), (2, 3)]
         beside, across = swap(queries, "outer", 1), swap(queries, "outer", 3)
-        beside, across, near, maps, *mail = lax.optimization_barrier((beside, across, near, maps, *mail))
+        near, beside, across, lw = lax.optimization_barrier((near, beside, across, lw))
         from_end = lax.ppermute(beside, "outer", middle)
         to_end = lax.ppermute(across, "outer", outward)
         far = lax.ppermute(near, axes, second)
-        far, from_end, to_end = lax.optimization_barrier((far, from_end, to_end))
-        got_queries = [(queries,), (beside,), (across,), (to_end, from_end)]
+        got_queries = [(bare,), (beside,), (across,)]
         flips = [0, 1, 3, 2]
-        sides = [(i, table_half + fresh_half) for i in (2, 4, 6)]
         buffers = [table, fresh_rows]
         table_pieces = [(0, 0, rows_dev, (0, rows_dev, None, None), -1)]
         fresh_pieces = [(1, 0, refresh_dev, (0, refresh_dev, None, None), -1 - rows_dev // LANES)]
-        for slot, by_core, mine in ((1, 0, near), (1, 1, side_rows), (3, None, far)):
+
+        def add_pieces(slot, by_core, mine):
+            data = table_half + fresh_half
+            fresh_at = data + 3 * (table_half // LANES)
             for flip, rows in enumerate((mine, swap(mine, "query", 1))):
                 by = None if by_core is None else by_core ^ flip
-                data = table_half + fresh_half
-                fresh_at = data + 3 * (table_half // LANES)
                 table_pieces.append((len(buffers), 0, table_half, (slot * rows_dev, table_half, flip, by), data))
                 fresh_pieces.append(
                     (len(buffers), table_half, fresh_half, (slot * refresh_dev, fresh_half, flip, by), fresh_at)
                 )
                 buffers.append(rows)
+
+        add_pieces(1, 0, near)
+        add_pieces(1, 1, side_rows)
+        early = table_pieces + shift(fresh_pieces, plane_rows)
+        partials = [score(i, got_queries[i], list(buffers), early) for i in range(planes - 1)]
+        far, from_end, to_end, *partials = lax.optimization_barrier((far, from_end, to_end, *partials))
+        got_queries.append((to_end, from_end))
+        add_pieces(3, None, far)
+        pieces = table_pieces + shift(fresh_pieces, plane_rows)
+        late = [piece for piece in pieces if piece not in early]
+        partials = [score(i, got_queries[i], buffers, late, [partials[i]]) for i in range(planes - 1)]
     else:
         got_queries = [(queries,)] + [(swap(queries, "outer", s),) for s in range(1, planes)]
         flips = range(planes)
@@ -450,11 +517,9 @@
         buffers = [
             gathered[:, :, :table_half].reshape(plane_rows, width),
             gathered[:, :, table_half:data].reshape(plane_refresh, width),
-            *[one[data:] for one in got_rows[1:]],
         ]
-        sides = [(i + 1, 0) for i in range(1, owners_plane)]
         scales = []
-        for rows in buffers[:2]:
+        for rows in buffers:
             values = rows.astype(f32)
             mean = jnp.sum(values * values, axis=1) / width
             scales.append((lax.rsqrt(mean + epsilon) * (score_scale / width * LOG2E)).reshape(-1, LANES))
@@ -466,89 +531,22 @@
 
         table_pieces = blocks(0, plane_rows, 0)
         fresh_pieces = blocks(1, plane_refresh, plane_rows // LANES)
-
-    def shift(pieces, columns):
-        return [(a, b, c, (d[0] + columns, *d[1:]), e) for a, b, c, d, e in pieces]
+        pieces = table_pieces + shift(fresh_pieces, plane_rows)
+        partials = [score(i, got_queries[i], buffers, pieces) for i in range(planes - 1)]
 
     pieces = table_pieces + shift(fresh_pieces, plane_rows)
-    relayed = call(
-        relay_kernel,
-        "relay",
-        [jax.ShapeDtypeStruct((planes * share + EXTRA, width), bf16)] * owners_plane,
-        None,
-        *mail,
-        planes=planes,
-        owners_plane=owners_plane,
-        share=share,
-        list_size=list_size,
-        count=query_count,
-        refresh_dev=refresh_dev,
-    )
-    relayed = [relayed[0]] + [swap(relayed[s], "inner", s) for s in range(1, owners_plane)]
-    lw, row_ids, scale_plane, positive, target, own, new_ages = call(
-        meta_kernel,
-        "meta",
-        [
-            jax.ShapeDtypeStruct((planes, all_rows), f32),
-            jax.ShapeDtypeStruct((1, all_rows), f32),
-            jax.ShapeDtypeStruct((1, all_rows), f32),
-            jax.ShapeDtypeStruct((planes, query_count), f32),
-            jax.ShapeDtypeStruct((1, owners * cap), jnp.int32),
-            jax.ShapeDtypeStruct((1, rows_dev), jnp.int32),
-            jax.ShapeDtypeStruct((1, rows_dev), jnp.int32),
-        ],
-        place,
-        maps,
-        own_ages,
-        scales,
-        *mail,
-        *relayed,
-        *buffers,
-        sides=sides,
-        pieces=pieces,
-        planes=planes,
-        owners_plane=owners_plane,
-        rows_dev=rows_dev,
-        refresh_dev=refresh_dev,
-        list_size=list_size,
-        count=query_count,
-        cap=cap,
-        replicas=replicas,
-        fast=fast,
-    )
     new_ages = new_ages.reshape(rows_dev)
     came = jnp.concatenate([one[: planes * share] for one in relayed])
     arrived = [came] + [swap(came, "query", flip) for flip in range(1, replicas)]
 
-    def score(i, given):
-        s = flips[i]
-        (partial,) = call(
-            score_kernel,
-            "score",
-            [jax.ShapeDtypeStruct((2, query_count // LANES, LANES), f32)],
-            place,
-            *given,
-            positive,
-            lw,
-            row_ids,
-            scale_plane,
-            *buffers,
-            scratch=[pltpu.VMEM((query_count, LANES), f32)] * 4 + [pltpu.VMEM(queries.shape, bf16)],
-            pieces=pieces,
-            flip=s,
-            given=len(given),
-        )
-        return partial
-
     (new_table,) = call(
         apply_kernel, "apply", [jax.ShapeDtypeStruct(table.shape, bf16)], None, target, own, table, *arrived
     )
-    partials = [swap(score(i, got_queries[i]), "outer", flips[i]) for i in range(1, planes - 1)]
-    partials.append(score(0, got_queries[0]))
+    partials = [partials[0]] + [swap(partials[i], "outer", flips[i]) for i in range(1, planes - 1)]
     new_table, *tied = lax.optimization_barrier((new_table, *partials, *got_queries[-1]))
     partials, last_queries = tied[: planes - 1], tied[planes - 1 :]
     mine = sum(partials[1:], partials[0])
-    mine = mine + swap(score(planes - 1, last_queries), "outer", flips[-1])
+    mine = mine + swap(score(planes - 1, last_queries, buffers, pieces), "outer", flips[-1])
     loss = (jnp.log2(mine[0]) - mine[1]) * math.log(2.0)
     return new_table, new_ages, loss.reshape(query_count)
 

time: 82.7 us -> 81.7 us (0.988)
  starting transfers between devices: 26.4 us -> 23.8 us
  Pallas kernels: 16 us -> 18.2 us
  waiting for transfers between devices: 35.7 us -> 34.2 us
  local copies, waits for them, and re-layouts: 2.89 us -> 3.78 us
    ppermute x1, waiting for transfers between devices: 4.19 us -> 0.01 us  [on_device(): side_rows = lax.ppermute(behind, axes, second)]
    ppermute x15, waiting for transfers between devices: 24.3 us -> 27.7 us  [swap(): lax.ppermute(values, axis, [(i, i ^ flip) for i in range(lax.axis_size(ax...]
    pallas_call x9 -> x12, Pallas kernels: 16 us -> 18.2 us  [call(): pl.pallas_call(functools.partial(kernel, **options), out_shape=tuple(outs...]
    ppermute x1, starting transfers between devices: 2.49 us -> 0.6 us  [on_device(): side_rows = lax.ppermute(behind, axes, second)]
    ppermute x1, waiting for transfers between devices: 1.85 us -> 0.01 us  [on_device(): far = lax.ppermute(near, axes, second)]
    ppermute x1, starting transfers between devices: 3 us -> 1.49 us  [on_device(): near = lax.ppermute(rows_half, axes, first)]
    ppermute x1, waiting for transfers between devices: 5.33 us -> 6.43 us  [on_device(): to_end = lax.ppermute(across, 'outer', outward)]
    slice x4 -> x6, local copies, waits for them, and re-layouts: 0.03 us -> 0.93 us  [on_device(): came = jnp.concatenate([one[:planes * share] for one in relayed])]
  transfers between devices with their start and end apart: 20 -> 20, of which waited for: 9 -> 12; matrix products, arithmetic and copies ran while one was open for 0% -> 0% of each run, Pallas kernels for 15% -> 18%
where the time goes in v12:
time: 81.7 us; the launch traced here: 81.4 us
  waiting for transfers between devices  34.2 us (42%)
  starting transfers between devices  23.8 us (29%)
  Pallas kernels  18.2 us (22%)
  local copies, waits for them, and re-layouts  3.78 us (5%)
  between operations  0.82 us (1%)
    ppermute x15, waiting for transfers between devices, swap(): lax.ppermute(values, axis, [(i, i ^ flip) for i in range(lax.axis_size(ax...  27.7 us
    ppermute x15, starting transfers between devices, swap(): lax.ppermute(values, axis, [(i, i ^ flip) for i in range(lax.axis_size(ax...  19.1 us
    pallas_call x12, Pallas kernels, call(): pl.pallas_call(functools.partial(kernel, **options), out_shape=tuple(outs...  18.2 us
    ppermute x1, waiting for transfers between devices, on_device(): to_end = lax.ppermute(across, 'outer', outward)  6.43 us
    unnamed x22, local copies, waits for them, and re-layouts  2.85 us
  transfers between devices with their start and end apart: 20, of which 12 were waited for; matrix products, arithmetic and copies ran while one was open for 0% of the time, Pallas kernels for 18%

profile of v12, /device:TPU:0, one launch (start us, length us, event | category | flops | bytes accessed | tf_op | source)
XLA Modules:
  0.0 81.4 jit_solution(3806608951599448437)
XLA Ops:
  0.6 0.1 pad_add_fusion.place
  0.7 0.6 copy-done.7
  1.3 0.1 copy-done.10
  1.4 0.0 copy-done.9
  1.4 1.1 %copy-done = bf16[512,768]{1,0:T(8,128)(2,1)S(1)} copy-done((bf16[512,768]{1,0:T(8,128)(2,1)S(1)}, bf16[512,768]{1,0:T(8,128)(2,1)}, u32[]{:S(2)}) %copy-start) | copy-done | bytes 786456
  2.6 1.0 %copy-done.2 = bf16[256,768]{1,0:T(8,128)(2,1)S(1)} copy-done((bf16[256,768]{1,0:T(8,128)(2,1)S(1)}, bf16[256,768]{1,0:T(8,128)(2,1)}, u32[]{:S(2)}) %copy-start.2) | copy-done | bytes 393240
  3.6 1.1 %prep.1 = (bf16[400,768]{1,0:T(8,128)(2,1)S(1)}, f32[6,128]{1,0:T(8,128)S(1)}, bf16[80,768]{1,0:T(8,128)(2,1)S(1)}, bf16[80,768]{1,0:T(8,128)(2,1)S(1)}, bf16[80...) custom-call(s32[3]{0:T(128)S(1)} %pad_add_fusion.place, bf16[512,768]{1,0:T(8,128)(2,1)S(1)} %copy-done, ...), custom_call_target="tpu_custom_call" | custom-call | flops 1 | bytes 1 | tf_op jit(solution)/shard_map/prep/pallas_call | solution.py:333
  4.6 0.0 copy-start.4
  4.6 3.1 %collective-permute-start = (bf16[80,768]{1,0:T(8,128)(2,1)S(1)}, bf16[80,768]{1,0:T(8,128)(2,1)S(1)}, u32[]{:S(2)}, u32[]{:S(2)}) collective-permute-start(bf16[80,768]{1,0:T(8,128)(2,1)S(1)} %get-tuple-element.42), channel_id=1, source_target_pairs={{0,8},{8,0},{16,24},{24,16},{1,9},{9,1},{17,25},{25,17},{2,10},{10... | collective-permute-start | bytes 368648 | tf_op jit(solution)/shard_map/ppermute | solution.py:346
  7.7 2.6 %collective-permute-start.1 = (bf16[80,768]{1,0:T(8,128)(2,1)S(1)}, bf16[80,768]{1,0:T(8,128)(2,1)S(1)}, u32[]{:S(2)}, u32[]{:S(2)}) collective-permute-start(bf16[80,768]{1,0:T(8,128)(2,1)S(1)} %get-tuple-element.43), channel_id=1, source_target_pairs={{0,16},{8,24},{16,0},{24,8},{1,17},{9,25},{17,1},{25,9},{2,18},{10... | collective-permute-start | bytes 368648 | tf_op jit(solution)/shard_map/ppermute | solution.py:346
  10.3 0.0 collective-permute-start.2
  10.3 2.1 %collective-permute-done.refs_1_ = bf16[80,768]{1,0:T(8,128)(2,1)S(1)} collective-permute-done((bf16[80,768]{1,0:T(8,128)(2,1)S(1)}, bf16[80,768]{1,0:T(8,128)(2,1)S(1)}, u32[]{:S(2)}, u32[]{:S(2)}) %collective-permute-start) | collective-permute-done | bytes 122912 | tf_op jit(solution)/shard_map/ppermute | solution.py:346
  12.4 7.7 %collective-permute-done.1.refs_2_ = bf16[80,768]{1,0:T(8,128)(2,1)S(1)} collective-permute-done((bf16[80,768]{1,0:T(8,128)(2,1)S(1)}, bf16[80,768]{1,0:T(8,128)(2,1)S(1)}, u32[]{:S(2)}, u32[]{:S(2)}) %collective-permute-start.1) | collective-permute-done | bytes 122912 | tf_op jit(solution)/shard_map/ppermute | solution.py:346
  20.0 0.0 collective-permute-done.2.refs_3_
  20.0 0.1 relay.1
  20.1 1.6 %collective-permute-start.3 = (bf16[80,768]{1,0:T(8,128)(2,1)S(1)}, bf16[80,768]{1,0:T(8,128)(2,1)S(1)}, u32[]{:S(2)}, u32[]{:S(2)}) collective-permute-start(bf16[80,768]{1,0:T(8,128)(2,1)S(1)} %get-tuple-element.50), channel_id=1, source_target_pairs={{0,2},{2,0},{4,6},{6,4},{1,3},{3,1},{5,7},{7,5},{8,10},{10,8},{12,... | collective-permute-start | bytes 368648 | tf_op jit(solution)/shard_map/ppermute | solution.py:346
  21.7 1.5 %collective-permute-start.4 = (bf16[80,768]{1,0:T(8,128)(2,1)S(1)}, bf16[80,768]{1,0:T(8,128)(2,1)S(1)}, u32[]{:S(2)}, u32[]{:S(2)}) collective-permute-start(bf16[80,768]{1,0:T(8,128)(2,1)S(1)} %get-tuple-element.51), channel_id=1, source_target_pairs={{0,4},{2,6},{4,0},{6,2},{1,5},{3,7},{5,1},{7,3},{8,12},{10,14},{12... | collective-permute-start | bytes 368648 | tf_op jit(solution)/shard_map/ppermute | solution.py:346
  23.2 0.5 collective-permute-start.5
  23.7 1.5 %collective-permute-start.7 = (bf16[400,768]{1,0:T(8,128)(2,1)S(1)}, bf16[400,768]{1,0:T(8,128)(2,1)S(1)}, u32[]{:S(2)}, u32[]{:S(2)}) collective-permute-start(bf16[400,768]{1,0:T(8,128)(2,1)S(1)} %get-tuple-element.65), channel_id=1, source_target_pairs={{0,2},{1,5},{2,0},{3,7},{4,6},{5,1},{6,4},{7,3},{8,10},{9,13},{10,... | collective-permute-start | bytes 1843208 | tf_op jit(solution)/shard_map/ppermute | solution.py:474
  25.2 0.2 collective-permute-done.3.refs_5_
  25.3 3.0 %collective-permute-done.4.refs_6_ = bf16[80,768]{1,0:T(8,128)(2,1)S(1)} collective-permute-done((bf16[80,768]{1,0:T(8,128)(2,1)S(1)}, bf16[80,768]{1,0:T(8,128)(2,1)S(1)}, u32[]{:S(2)}, u32[]{:S(2)}) %collective-permute-start.4) | collective-permute-done | bytes 122912 | tf_op jit(solution)/shard_map/ppermute | solution.py:346
  28.3 1.9 %collective-permute-done.5.refs_7_ = bf16[80,768]{1,0:T(8,128)(2,1)S(1)} collective-permute-done((bf16[80,768]{1,0:T(8,128)(2,1)S(1)}, bf16[80,768]{1,0:T(8,128)(2,1)S(1)}, u32[]{:S(2)}, u32[]{:S(2)}) %collective-permute-start.5) | collective-permute-done | bytes 122912 | tf_op jit(solution)/shard_map/ppermute | solution.py:346
  30.2 0.6 collective-permute-start.14
  30.8 2.3 %collective-permute-start.8 = (bf16[256,768]{1,0:T(8,128)(2,1)S(1)}, bf16[256,768]{1,0:T(8,128)(2,1)S(1)}, u32[]{:S(2)}, u32[]{:S(2)}) collective-permute-start(bf16[256,768]{1,0:T(8,128)(2,1)S(1)} %copy-done.4), channel_id=1, source_target_pairs={{0,8},{8,0},{16,24},{24,16},{1,9},{9,1},{17,25},{25,17},{2,10},{10... | collective-permute-start | bytes 1179656 | tf_op jit(solution)/shard_map/ppermute | solution.py:346
  33.1 2.8 %collective-permute-start.9 = (bf16[256,768]{1,0:T(8,128)(2,1)S(1)}, bf16[256,768]{1,0:T(8,128)(2,1)S(1)}, u32[]{:S(2)}, u32[]{:S(2)}) collective-permute-start(bf16[256,768]{1,0:T(8,128)(2,1)S(1)} %copy-done.4), channel_id=1, source_target_pairs={{0,24},{8,16},{16,8},{24,0},{1,25},{9,17},{17,9},{25,1},{2,26},{10... | collective-permute-start | bytes 1179656 | tf_op jit(solution)/shard_map/ppermute | solution.py:346
  35.9 0.7 lists.1.maps
  36.6 0.0 copy-start.3
  36.6 3.0 %meta.1 = (f32[4,3072]{1,0:T(4,128)S(1)}, f32[1,3072]{1,0:T(1,128)S(1)}, f32[4,256]{1,0:T(4,128)S(1)}, s32[1,512]{1,0:T(1,128)S(1)}, s32[1,512]{1,0:T(1,128)S(1)}, /*index=5*/s32[1,512]{1,0:T(1,128)}) custom-call(s32[3]{0:T(128)S(1)} %pad_add_fusion.place, bf16[4,128,64]{2,1,0:T(8,128)(2,1)S(1)} %lists.1.maps, s32[1,512]{1,0:T(1,128)S(1)} %bitcast.10, ...), custom_call_target="tpu_custom_call" | custom-call | flops 1 | bytes 1 | tf_op jit(solution)/shard_map/meta/pallas_call | solution.py:333
  39.6 2.7 %collective-permute-done.8.refs_0_.refs_1_ = bf16[256,768]{1,0:T(8,128)(2,1)S(1)} collective-permute-done((bf16[256,768]{1,0:T(8,128)(2,1)S(1)}, bf16[256,768]{1,0:T(8,128)(2,1)S(1)}, u32[]{:S(2)}, u32[]{:S(2)}) %collective-permute-start.8) | collective-permute-done | bytes 393248 | tf_op jit(solution)/shard_map/ppermute | solution.py:346
  42.3 6.9 %collective-permute-done.9.refs_0_.refs_1_ = bf16[256,768]{1,0:T(8,128)(2,1)S(1)} collective-permute-done((bf16[256,768]{1,0:T(8,128)(2,1)S(1)}, bf16[256,768]{1,0:T(8,128)(2,1)S(1)}, u32[]{:S(2)}, u32[]{:S(2)}) %collective-permute-start.9) | collective-permute-done | bytes 393248 | tf_op jit(solution)/shard_map/ppermute | solution.py:346
  49.1 0.0 collective-permute-done.7.refs_7_.refs_8_
  49.1 0.0 collective-permute-start.13
  49.2 0.0 collective-permute-done.14.refs_9_.refs_10_
  49.2 0.5 collective-permute-start.15
  49.7 0.5 collective-permute-start.10
  50.1 0.7 collective-permute-start.11
  50.8 1.5 %collective-permute-start.12 = (bf16[256,768]{1,0:T(8,128)(2,1)S(1)}, bf16[256,768]{1,0:T(8,128)(2,1)S(1)}, u32[]{:S(2)}, u32[]{:S(2)}) collective-permute-start(bf16[256,768]{1,0:T(8,128)(2,1)S(1)} %collective-permute-done.9.refs_0_.refs_1_), channel_id=1, source_target_pairs={{8,0},{16,24},{9,1},{17,25},{10,2},{18,26},{11,3},{19,27},{12,4},{... | collective-permute-start | bytes 1179656 | tf_op jit(solution)/shard_map/ppermute | solution.py:481
  52.3 0.0 collective-permute-done.13.refs_8_.refs_9_
  52.3 0.0 collective-permute-done.15.refs_10_.refs_11_
  52.3 2.0 %score.9.refs_0_ = f32[2,2,128]{2,1,0:T(2,128)S(1)} custom-call(s32[3]{0:T(128)S(1)} %pad_add_fusion.place, bf16[256,768]{1,0:T(8,128)(2,1)S(1)} %collective-permute-done.9.refs_0_.refs_1_, f32[4,256]{1,0:T(4,128)S(1)} %get-tuple-element.61.refs_1_.refs_2_, f32[4,3072]{1,0:T(4,128)S(1)} %get-tuple-element.62.refs_2_.refs_3_, ...), custom_call_target="tpu_custom_call" | custom-call | flops 1 | bytes 1 | tf_op jit(solution)/shard_map/score/pallas_call | solution.py:333
  54.3 2.0 %score.8.refs_0_ = f32[2,2,128]{2,1,0:T(2,128)S(1)} custom-call(s32[3]{0:T(128)S(1)} %pad_add_fusion.place, bf16[256,768]{1,0:T(8,128)(2,1)S(1)} %collective-permute-done.8.refs_0_.refs_1_, f32[4,256]{1,0:T(4,128)S(1)} %get-tuple-element.61.refs_1_.refs_2_, f32[4,3072]{1,0:T(4,128)S(1)} %get-tuple-element.62.refs_2_.refs_3_, ...), custom_call_target="tpu_custom_call" | custom-call | flops 1 | bytes 1 | tf_op jit(solution)/shard_map/score/pallas_call | solution.py:333
  56.3 2.0 %score.7.refs_0_ = f32[2,2,128]{2,1,0:T(2,128)S(1)} custom-call(s32[3]{0:T(128)S(1)} %pad_add_fusion.place, bf16[256,768]{1,0:T(8,128)(2,1)S(1)} %copy-done.4, f32[4,256]{1,0:T(4,128)S(1)} %get-tuple-element.61.refs_1_.refs_2_, f32[4,3072]{1,0:T(4,128)S(1)} %get-tuple-element.62.refs_2_.refs_3_, f32[1,3072]{1,0:T(1,128)S(1)} %get-tuple-element.63.refs_3_.refs_4_, ...), custom_call_target="tpu_custom_call" | custom-call | flops 1 | bytes 1 | tf_op jit(solution)/shard_map/score/pallas_call | solution.py:333
  58.2 0.0 collective-permute-done.11.refs_1_
  58.2 6.4 %collective-permute-done.12.refs_0_ = bf16[256,768]{1,0:T(8,128)(2,1)S(1)} collective-permute-done((bf16[256,768]{1,0:T(8,128)(2,1)S(1)}, bf16[256,768]{1,0:T(8,128)(2,1)S(1)}, u32[]{:S(2)}, u32[]{:S(2)}) %collective-permute-start.12) | collective-permute-done | bytes 393248 | tf_op jit(solution)/shard_map/ppermute | solution.py:481
  64.7 0.0 collective-permute-done.10.refs_12_
  64.7 0.1 collective-permute-start.16
  64.8 0.0 slice-start
  64.8 0.0 slice-start.1
  64.8 0.9 %slice-done = bf16[64,768]{1,0:T(8,128)(2,1)S(1)} async-done(((bf16[80,768]{1,0:T(8,128)(2,1)}), bf16[64,768]{1,0:T(8,128)(2,1)S(1)}, s32[]{:S(2)}) %slice-start) | async-done | bytes 98328 | tf_op jit(solution)/shard_map/slice | solution.py:539
  65.7 0.0 slice-done.1
  65.8 0.5 collective-permute-start.6
  66.3 0.5 collective-permute-done.16.refs_13_
  66.7 1.2 %score.12 = f32[2,2,128]{2,1,0:T(2,128)S(1)} custom-call(s32[3]{0:T(128)S(1)} %pad_add_fusion.place, f32[2,2,128]{2,1,0:T(2,128)S(1)} %score.9.refs_0_, bf16[256,768]{1,0:T(8,128)(2,1)S(1)} %collective-permute-done.9.refs_0_.refs_1_, f32[4,256]{1,0:T(4,128)S(1)} %get-tuple-element.61.refs_1_.refs_2_, f32[4,3072]{1,0:T(4,128)S(1)} %get-tuple-element.62.refs_2_.refs_3_, ...), custom_call_target="tpu_custom_call" | custom-call | flops 1 | bytes 1 | tf_op jit(solution)/shard_map/score/pallas_call | solution.py:333
  68.0 1.1 %collective-permute-start.18 = (f32[2,2,128]{2,1,0:T(2,128)S(1)}, f32[2,2,128]{2,1,0:T(2,128)S(1)}, u32[]{:S(2)}, u32[]{:S(2)}) collective-permute-start(f32[2,2,128]{2,1,0:T(2,128)S(1)} %score.12), channel_id=1, source_target_pairs={{0,24},{8,16},{16,8},{24,0},{1,25},{9,17},{17,9},{25,1},{2,26},{10... | collective-permute-start | bytes 6152 | tf_op jit(solution)/shard_map/ppermute | solution.py:346
  69.1 1.2 %score.11 = f32[2,2,128]{2,1,0:T(2,128)S(1)} custom-call(s32[3]{0:T(128)S(1)} %pad_add_fusion.place, f32[2,2,128]{2,1,0:T(2,128)S(1)} %score.8.refs_0_, bf16[256,768]{1,0:T(8,128)(2,1)S(1)} %collective-permute-done.8.refs_0_.refs_1_, f32[4,256]{1,0:T(4,128)S(1)} %get-tuple-element.61.refs_1_.refs_2_, f32[4,3072]{1,0:T(4,128)S(1)} %get-tuple-element.62.refs_2_.refs_3_, ...), custom_call_target="tpu_custom_call" | custom-call | flops 1 | bytes 1 | tf_op jit(solution)/shard_map/score/pallas_call | solution.py:333
  70.4 0.1 collective-permute-start.17
  70.4 1.5 %apply.1 = bf16[512,768]{1,0:T(8,128)(2,1)} custom-call(s32[1,512]{1,0:T(1,128)S(1)} %get-tuple-element.53.target, s32[1,512]{1,0:T(1,128)S(1)} %get-tuple-element.54.refreshed, bf16[512,768]{1,0:T(8,128)(2,1)S(1)} %copy-done.1, bf16[256,768]{1,0:T(8,128)(2,1)S(1)} %pad_maximum_fusion.refs_0_, bf16[256,768]{1,0:T(8,128)(2,1)S(1)} %collective-permute-done.6.refs_1_), custom_call_target="tpu_custom_call" | custom-call | flops 1 | bytes 1 | tf_op jit(solution)/shard_map/apply/pallas_call | solution.py:333
  71.9 1.2 %score.10 = f32[2,2,128]{2,1,0:T(2,128)S(1)} custom-call(s32[3]{0:T(128)S(1)} %pad_add_fusion.place, f32[2,2,128]{2,1,0:T(2,128)S(1)} %score.7.refs_0_, bf16[256,768]{1,0:T(8,128)(2,1)S(1)} %copy-done.4, f32[4,256]{1,0:T(4,128)S(1)} %get-tuple-element.61.refs_1_.refs_2_, f32[4,3072]{1,0:T(4,128)S(1)} %get-tuple-element.62.refs_2_.refs_3_, ...), custom_call_target="tpu_custom_call" | custom-call | flops 1 | bytes 1 | tf_op jit(solution)/shard_map/score/pallas_call | solution.py:333
  73.1 0.3 collective-permute-done.18
  73.4 0.6 collective-permute-done.17
  74.0 2.3 %score.13 = f32[2,2,128]{2,1,0:T(2,128)S(1)} custom-call(s32[3]{0:T(128)S(1)} %pad_add_fusion.place, bf16[256,768]{1,0:T(8,128)(2,1)S(1)} %collective-permute-done.12.refs_0_, bf16[256,768]{1,0:T(8,128)(2,1)S(1)} %collective-permute-done.11.refs_1_, f32[4,256]{1,0:T(4,128)S(1)} %get-tuple-element.61.refs_1_.refs_2_, ...), custom_call_target="tpu_custom_call" | custom-call | flops 1 | bytes 1 | tf_op jit(solution)/shard_map/score/pallas_call | solution.py:333
  76.3 2.5 %collective-permute-start.19 = (f32[2,2,128]{2,1,0:T(2,128)S(1)}, f32[2,2,128]{2,1,0:T(2,128)S(1)}, u32[]{:S(2)}, u32[]{:S(2)}) collective-permute-start(f32[2,2,128]{2,1,0:T(2,128)S(1)} %score.13), channel_id=1, source_target_pairs={{0,16},{8,24},{16,0},{24,8},{1,17},{9,25},{17,1},{25,9},{2,18},{10... | collective-permute-start | bytes 6152 | tf_op jit(solution)/shard_map/ppermute | solution.py:346
  78.8 2.0 %collective-permute-done.19 = f32[2,2,128]{2,1,0:T(2,128)S(1)} collective-permute-done((f32[2,2,128]{2,1,0:T(2,128)S(1)}, f32[2,2,128]{2,1,0:T(2,128)S(1)}, u32[]{:S(2)}, u32[]{:S(2)}) %collective-permute-start.19) | collective-permute-done | bytes 2080 | tf_op jit(solution)/shard_map/ppermute | solution.py:346
  80.9 0.6 fusion.1
  (20 shorter events, 0.1 us)
Async XLA Ops:
  0.6 0.7 copy-start.7
  0.7 0.7 copy-start.10
  0.7 0.7 copy-start.9
  1.4 1.1 %copy-start = (bf16[512,768]{1,0:T(8,128)(2,1)S(1)}, bf16[512,768]{1,0:T(8,128)(2,1)}, u32[]{:S(2)}) copy-start(bf16[512,768]{1,0:T(8,128)(2,1)} %refs_6_.13) | copy-start | bytes 2359300
  2.6 1.0 %copy-start.2 = (bf16[256,768]{1,0:T(8,128)(2,1)S(1)}, bf16[256,768]{1,0:T(8,128)(2,1)}, u32[]{:S(2)}) copy-start(bf16[256,768]{1,0:T(8,128)(2,1)} %refs_7_.7) | copy-start | bytes 1179652
  3.5 16.5 %copy-start.8 = (s32[512]{0:T(512)S(1)}, s32[512]{0:T(512)}, u32[]{:S(2)}) copy-start(s32[512]{0:T(512)} %param.8) | copy-start | bytes 6148
  4.6 26.2 %copy-start.4 = (bf16[256,768]{1,0:T(8,128)(2,1)S(1)}, bf16[256,768]{1,0:T(8,128)(2,1)}, u32[]{:S(2)}) copy-start(bf16[256,768]{1,0:T(8,128)(2,1)} %refs_1_.1) | copy-start | bytes 1179652
  4.6 7.8 %collective-permute-start = (bf16[80,768]{1,0:T(8,128)(2,1)S(1)}, bf16[80,768]{1,0:T(8,128)(2,1)S(1)}, u32[]{:S(2)}, u32[]{:S(2)}) collective-permute-start(bf16[80,768]{1,0:T(8,128)(2,1)S(1)} %get-tuple-element.42), channel_id=1, source_target_pairs={{0,8},{8,0},{16,24},{24,16},{1,9},{9,1},{17,25},{25,17},{2,10},{10... | collective-permute-start | bytes 368648 | tf_op jit(solution)/shard_map/ppermute | solution.py:346
  7.7 12.3 %collective-permute-start.1 = (bf16[80,768]{1,0:T(8,128)(2,1)S(1)}, bf16[80,768]{1,0:T(8,128)(2,1)S(1)}, u32[]{:S(2)}, u32[]{:S(2)}) collective-permute-start(bf16[80,768]{1,0:T(8,128)(2,1)S(1)} %get-tuple-element.43), channel_id=1, source_target_pairs={{0,16},{8,24},{16,0},{24,8},{1,17},{9,25},{17,1},{25,9},{2,18},{10... | collective-permute-start | bytes 368648 | tf_op jit(solution)/shard_map/ppermute | solution.py:346
  10.3 9.7 %collective-permute-start.2 = (bf16[80,768]{1,0:T(8,128)(2,1)S(1)}, bf16[80,768]{1,0:T(8,128)(2,1)S(1)}, u32[]{:S(2)}, u32[]{:S(2)}) collective-permute-start(bf16[80,768]{1,0:T(8,128)(2,1)S(1)} %get-tuple-element.44), channel_id=1, source_target_pairs={{0,24},{8,16},{16,8},{24,0},{1,25},{9,17},{17,9},{25,1},{2,26},{10... | collective-permute-start | bytes 368648 | tf_op jit(solution)/shard_map/ppermute | solution.py:346
  20.1 5.2 %collective-permute-start.3 = (bf16[80,768]{1,0:T(8,128)(2,1)S(1)}, bf16[80,768]{1,0:T(8,128)(2,1)S(1)}, u32[]{:S(2)}, u32[]{:S(2)}) collective-permute-start(bf16[80,768]{1,0:T(8,128)(2,1)S(1)} %get-tuple-element.50), channel_id=1, source_target_pairs={{0,2},{2,0},{4,6},{6,4},{1,3},{3,1},{5,7},{7,5},{8,10},{10,8},{12,... | collective-permute-start | bytes 368648 | tf_op jit(solution)/shard_map/ppermute | solution.py:346
  21.7 6.6 %collective-permute-start.4 = (bf16[80,768]{1,0:T(8,128)(2,1)S(1)}, bf16[80,768]{1,0:T(8,128)(2,1)S(1)}, u32[]{:S(2)}, u32[]{:S(2)}) collective-permute-start(bf16[80,768]{1,0:T(8,128)(2,1)S(1)} %get-tuple-element.51), channel_id=1, source_target_pairs={{0,4},{2,6},{4,0},{6,2},{1,5},{3,7},{5,1},{7,3},{8,12},{10,14},{12... | collective-permute-start | bytes 368648 | tf_op jit(solution)/shard_map/ppermute | solution.py:346
  23.2 7.0 %collective-permute-start.5 = (bf16[80,768]{1,0:T(8,128)(2,1)S(1)}, bf16[80,768]{1,0:T(8,128)(2,1)S(1)}, u32[]{:S(2)}, u32[]{:S(2)}) collective-permute-start(bf16[80,768]{1,0:T(8,128)(2,1)S(1)} %get-tuple-element.52), channel_id=1, source_target_pairs={{0,6},{2,4},{4,2},{6,0},{1,7},{3,5},{5,3},{7,1},{8,14},{10,12},{12... | collective-permute-start | bytes 368648 | tf_op jit(solution)/shard_map/ppermute | solution.py:346
  23.7 25.5 %collective-permute-start.7 = (bf16[400,768]{1,0:T(8,128)(2,1)S(1)}, bf16[400,768]{1,0:T(8,128)(2,1)S(1)}, u32[]{:S(2)}, u32[]{:S(2)}) collective-permute-start(bf16[400,768]{1,0:T(8,128)(2,1)S(1)} %get-tuple-element.65), channel_id=1, source_target_pairs={{0,2},{1,5},{2,0},{3,7},{4,6},{5,1},{6,4},{7,3},{8,10},{9,13},{10,... | collective-permute-start | bytes 1843208 | tf_op jit(solution)/shard_map/ppermute | solution.py:474
  25.3 39.5 %copy-start.5 = (bf16[80,768]{1,0:T(8,128)(2,1)}, bf16[80,768]{1,0:T(8,128)(2,1)S(1)}, u32[]{:S(2)}) copy-start(bf16[80,768]{1,0:T(8,128)(2,1)S(1)} %collective-permute-done.3.refs_5_) | copy-start | bytes 368644
  28.3 36.5 %copy-start.6 = (bf16[80,768]{1,0:T(8,128)(2,1)}, bf16[80,768]{1,0:T(8,128)(2,1)S(1)}, u32[]{:S(2)}) copy-start(bf16[80,768]{1,0:T(8,128)(2,1)S(1)} %collective-permute-done.4.refs_6_) | copy-start | bytes 368644
  30.2 22.1 %copy-start.1 = (bf16[512,768]{1,0:T(8,128)(2,1)S(1)}, bf16[512,768]{1,0:T(8,128)(2,1)}, u32[]{:S(2)}) copy-start(bf16[512,768]{1,0:T(8,128)(2,1)} %refs_6_.13) | copy-start | bytes 2359300
  30.2 18.9 %collective-permute-start.14 = (bf16[400,768]{1,0:T(8,128)(2,1)S(1)}, bf16[400,768]{1,0:T(8,128)(2,1)S(1)}, u32[]{:S(2)}, u32[]{:S(2)}) collective-permute-start(bf16[400,768]{1,0:T(8,128)(2,1)S(1)} %get-tuple-element.65), channel_id=1, source_target_pairs={{0,4},{1,3},{2,6},{3,1},{4,0},{5,7},{6,2},{7,5},{8,12},{9,11},{10,... | collective-permute-start | bytes 1843208 | tf_op jit(solution)/shard_map/ppermute | solution.py:476
  30.8 11.4 %collective-permute-start.8 = (bf16[256,768]{1,0:T(8,128)(2,1)S(1)}, bf16[256,768]{1,0:T(8,128)(2,1)S(1)}, u32[]{:S(2)}, u32[]{:S(2)}) collective-permute-start(bf16[256,768]{1,0:T(8,128)(2,1)S(1)} %copy-done.4), channel_id=1, source_target_pairs={{0,8},{8,0},{16,24},{24,16},{1,9},{9,1},{17,25},{25,17},{2,10},{10... | collective-permute-start | bytes 1179656 | tf_op jit(solution)/shard_map/ppermute | solution.py:346
  33.1 16.0 %collective-permute-start.9 = (bf16[256,768]{1,0:T(8,128)(2,1)S(1)}, bf16[256,768]{1,0:T(8,128)(2,1)S(1)}, u32[]{:S(2)}, u32[]{:S(2)}) collective-permute-start(bf16[256,768]{1,0:T(8,128)(2,1)S(1)} %copy-done.4), channel_id=1, source_target_pairs={{0,24},{8,16},{16,8},{24,0},{1,25},{9,17},{17,9},{25,1},{2,26},{10... | collective-permute-start | bytes 1179656 | tf_op jit(solution)/shard_map/ppermute | solution.py:346
  36.6 15.7 %copy-start.3 = (bf16[256,768]{1,0:T(8,128)(2,1)S(1)}, bf16[256,768]{1,0:T(8,128)(2,1)}, u32[]{:S(2)}) copy-start(bf16[256,768]{1,0:T(8,128)(2,1)} %refs_7_.7) | copy-start | bytes 1179652
  49.1 3.1 %collective-permute-start.13 = (bf16[400,768]{1,0:T(8,128)(2,1)S(1)}, bf16[400,768]{1,0:T(8,128)(2,1)S(1)}, u32[]{:S(2)}, u32[]{:S(2)}) collective-permute-start(bf16[400,768]{1,0:T(8,128)(2,1)S(1)} %collective-permute-done.7.refs_7_.refs_8_), channel_id=1, source_target_pairs={{0,1},{1,0},{2,3},{3,2},{4,5},{5,4},{6,7},{7,6},{8,9},{9,8},{10,11... | collective-permute-start | bytes 1843208 | tf_op jit(solution)/shard_map/ppermute | solution.py:346
  49.2 3.1 %collective-permute-start.15 = (bf16[400,768]{1,0:T(8,128)(2,1)S(1)}, bf16[400,768]{1,0:T(8,128)(2,1)S(1)}, u32[]{:S(2)}, u32[]{:S(2)}) collective-permute-start(bf16[400,768]{1,0:T(8,128)(2,1)S(1)} %collective-permute-done.14.refs_9_.refs_10_), channel_id=1, source_target_pairs={{0,1},{1,0},{2,3},{3,2},{4,5},{5,4},{6,7},{7,6},{8,9},{9,8},{10,11... | collective-permute-start | bytes 1843208 | tf_op jit(solution)/shard_map/ppermute | solution.py:346
  49.7 15.0 %collective-permute-start.10 = (bf16[400,768]{1,0:T(8,128)(2,1)S(1)}, bf16[400,768]{1,0:T(8,128)(2,1)S(1)}, u32[]{:S(2)}, u32[]{:S(2)}) collective-permute-start(bf16[400,768]{1,0:T(8,128)(2,1)S(1)} %collective-permute-done.7.refs_7_.refs_8_), channel_id=1, source_target_pairs={{0,4},{1,3},{2,6},{3,1},{4,0},{5,7},{6,2},{7,5},{8,12},{9,11},{10,... | collective-permute-start | bytes 1843208 | tf_op jit(solution)/shard_map/ppermute | solution.py:482
  50.1 8.1 %collective-permute-start.11 = (bf16[256,768]{1,0:T(8,128)(2,1)S(1)}, bf16[256,768]{1,0:T(8,128)(2,1)S(1)}, u32[]{:S(2)}, u32[]{:S(2)}) collective-permute-start(bf16[256,768]{1,0:T(8,128)(2,1)S(1)} %collective-permute-done.8.refs_0_.refs_1_), channel_id=1, source_target_pairs={{8,16},{16,8},{9,17},{17,9},{10,18},{18,10},{11,19},{19,11},{12,20... | collective-permute-start | bytes 1179656 | tf_op jit(solution)/shard_map/ppermute | solution.py:480
  50.8 13.9 %collective-permute-start.12 = (bf16[256,768]{1,0:T(8,128)(2,1)S(1)}, bf16[256,768]{1,0:T(8,128)(2,1)S(1)}, u32[]{:S(2)}, u32[]{:S(2)}) collective-permute-start(bf16[256,768]{1,0:T(8,128)(2,1)S(1)} %collective-permute-done.9.refs_0_.refs_1_), channel_id=1, source_target_pairs={{8,0},{16,24},{9,1},{17,25},{10,2},{18,26},{11,3},{19,27},{12,4},{... | collective-permute-start | bytes 1179656 | tf_op jit(solution)/shard_map/ppermute | solution.py:481
  64.7 2.0 %collective-permute-start.16 = (bf16[400,768]{1,0:T(8,128)(2,1)S(1)}, bf16[400,768]{1,0:T(8,128)(2,1)S(1)}, u32[]{:S(2)}, u32[]{:S(2)}) collective-permute-start(bf16[400,768]{1,0:T(8,128)(2,1)S(1)} %collective-permute-done.10.refs_12_), channel_id=1, source_target_pairs={{0,1},{1,0},{2,3},{3,2},{4,5},{5,4},{6,7},{7,6},{8,9},{9,8},{10,11... | collective-permute-start | bytes 1843208 | tf_op jit(solution)/shard_map/ppermute | solution.py:346
  64.8 0.9 %slice-start = ((bf16[80,768]{1,0:T(8,128)(2,1)}), bf16[64,768]{1,0:T(8,128)(2,1)S(1)}, s32[]{:S(2)}) async-start(bf16[80,768]{1,0:T(8,128)(2,1)} %copy-done.5), calls=%async_computation | async-start | bytes 196608 | tf_op jit(solution)/shard_map/slice | solution.py:539
  64.8 0.9 %slice-start.1 = ((bf16[80,768]{1,0:T(8,128)(2,1)}), bf16[64,768]{1,0:T(8,128)(2,1)S(1)}, s32[]{:S(2)}) async-start(bf16[80,768]{1,0:T(8,128)(2,1)} %copy-done.6), calls=%async_computation.1 | async-start | bytes 196608 | tf_op jit(solution)/shard_map/slice | solution.py:539
  65.8 4.6 %collective-permute-start.6 = (bf16[256,768]{1,0:T(8,128)(2,1)S(1)}, bf16[256,768]{1,0:T(8,128)(2,1)S(1)}, u32[]{:S(2)}, u32[]{:S(2)}) collective-permute-start(bf16[256,768]{1,0:T(8,128)(2,1)S(1)} %pad_maximum_fusion.refs_0_), channel_id=1, source_target_pairs={{0,1},{1,0},{2,3},{3,2},{4,5},{5,4},{6,7},{7,6},{8,9},{9,8},{10,11... | collective-permute-start | bytes 1179656 | tf_op jit(solution)/shard_map/ppermute | solution.py:346
  68.0 5.4 %collective-permute-start.18 = (f32[2,2,128]{2,1,0:T(2,128)S(1)}, f32[2,2,128]{2,1,0:T(2,128)S(1)}, u32[]{:S(2)}, u32[]{:S(2)}) collective-permute-start(f32[2,2,128]{2,1,0:T(2,128)S(1)} %score.12), channel_id=1, source_target_pairs={{0,24},{8,16},{16,8},{24,0},{1,25},{9,17},{17,9},{25,1},{2,26},{10... | collective-permute-start | bytes 6152 | tf_op jit(solution)/shard_map/ppermute | solution.py:346
  70.4 3.6 %collective-permute-start.17 = (f32[2,2,128]{2,1,0:T(2,128)S(1)}, f32[2,2,128]{2,1,0:T(2,128)S(1)}, u32[]{:S(2)}, u32[]{:S(2)}) collective-permute-start(f32[2,2,128]{2,1,0:T(2,128)S(1)} %score.11), channel_id=1, source_target_pairs={{0,8},{8,0},{16,24},{24,16},{1,9},{9,1},{17,25},{25,17},{2,10},{10... | collective-permute-start | bytes 6152 | tf_op jit(solution)/shard_map/ppermute | solution.py:346
  76.3 4.5 %collective-permute-start.19 = (f32[2,2,128]{2,1,0:T(2,128)S(1)}, f32[2,2,128]{2,1,0:T(2,128)S(1)}, u32[]{:S(2)}, u32[]{:S(2)}) collective-permute-start(f32[2,2,128]{2,1,0:T(2,128)S(1)} %score.13), channel_id=1, source_target_pairs={{0,16},{8,24},{16,0},{24,8},{1,17},{9,25},{17,1},{25,9},{2,18},{10... | collective-permute-start | bytes 6152 | tf_op jit(solution)/shard_map/ppermute | solution.py:346

commit v13 on v12

--- a/solution.py
+++ b/solution.py
@@ -388,7 +388,7 @@
     )
     mail = [mail[0]] + [swap(mail[s], "outer", s) for s in range(1, planes)]
     bare = queries
-    queries, *mail = lax.optimization_barrier((queries, *mail))
+    queries, mail[1] = lax.optimization_barrier((queries, mail[1]))
 
     high_count = owners * rows_dev // LANES
     (maps,) = call(
@@ -443,6 +443,13 @@
         replicas=replicas,
     )
 
+    new_ages = new_ages.reshape(rows_dev)
+    came = jnp.concatenate([one[: planes * share] for one in relayed])
+    arrived = [came] + [swap(came, "query", flip) for flip in range(1, replicas)]
+    (new_table,) = call(
+        apply_kernel, "apply", [jax.ShapeDtypeStruct(table.shape, bf16)], None, target, own, table, *arrived
+    )
+
     def shift(pieces, columns):
         return [(a, b, c, (d[0] + columns, *d[1:]), e) for a, b, c, d, e in pieces]
 
@@ -472,8 +479,7 @@
         first = [(2 * i + c, 2 * (i ^ (1 + c)) + c) for i in range(4) for c in range(2)]
         second = [(2 * i + c, 2 * (i ^ (2 - c)) + c) for i in range(4) for c in range(2)]
         near = lax.ppermute(rows_half, axes, first)
-        behind, *_ = lax.optimization_barrier((rows_half, *relayed))
-        side_rows = lax.ppermute(behind, axes, second)
+        side_rows = lax.ppermute(rows_half, axes, second)
         middle, outward = [(1, 2), (2, 1)], [(1, 0), (2, 3)]
         beside, across = swap(queries, "outer", 1), swap(queries, "outer", 3)
         near, beside, across, lw = lax.optimization_barrier((near, beside, across, lw))
@@ -501,7 +507,7 @@
         add_pieces(1, 1, side_rows)
         early = table_pieces + shift(fresh_pieces, plane_rows)
         partials = [score(i, got_queries[i], list(buffers), early) for i in range(planes - 1)]
-        far, from_end, to_end, *partials = lax.optimization_barrier((far, from_end, to_end, *partials))
+        far, from_end, to_end, new_table, *partials = lax.optimization_barrier((far, from_end, to_end, new_table, *partials))
         got_queries.append((to_end, from_end))
         add_pieces(3, None, far)
         pieces = table_pieces + shift(fresh_pieces, plane_rows)
@@ -535,13 +541,6 @@
         partials = [score(i, got_queries[i], buffers, pieces) for i in range(planes - 1)]
 
     pieces = table_pieces + shift(fresh_pieces, plane_rows)
-    new_ages = new_ages.reshape(rows_dev)
-    came = jnp.concatenate([one[: planes * share] for one in relayed])
-    arrived = [came] + [swap(came, "query", flip) for flip in range(1, replicas)]
-
-    (new_table,) = call(
-        apply_kernel, "apply", [jax.ShapeDtypeStruct(table.shape, bf16)], None, target, own, table, *arrived
-    )
     partials = [partials[0]] + [swap(partials[i], "outer", flips[i]) for i in range(1, planes - 1)]
     new_table, *tied = lax.optimization_barrier((new_table, *partials, *got_queries[-1]))
     partials, last_queries = tied[: planes - 1], tied[planes - 1 :]

time: 81.7 us -> 83.6 us (1.023)
  waiting for transfers between devices: 34.2 us -> 35.4 us
    ppermute x15, waiting for transfers between devices: 27.7 us -> 30.9 us  [swap(): lax.ppermute(values, axis, [(i, i ^ flip) for i in range(lax.axis_size(ax...]
    ppermute x1, waiting for transfers between devices: 6.43 us -> 4.49 us  [on_device(): to_end = lax.ppermute(across, 'outer', outward)]
    ppermute x1, starting transfers between devices: 0.6 us -> 1.52 us  [on_device(): side_rows = lax.ppermute(rows_half, axes, second)]
    ppermute x15, starting transfers between devices: 19.1 us -> 18.2 us  [swap(): lax.ppermute(values, axis, [(i, i ^ flip) for i in range(lax.axis_size(ax...]
    unnamed x22 -> x26, local copies, waits for them, and re-layouts: 2.85 us -> 3.58 us
  transfers between devices with their start and end apart: 20 -> 20, of which waited for: 12 -> 8; matrix products, arithmetic and copies ran while one was open for 0% -> 0% of each run, Pallas kernels for 18% -> 16%
where the time goes in v13:
time: 83.6 us; the launch traced here: 83.3 us
  waiting for transfers between devices  35.4 us (42%)
  starting transfers between devices  23.6 us (28%)
  Pallas kernels  18.2 us (22%)
  local copies, waits for them, and re-layouts  4.52 us (5%)
    ppermute x15, waiting for transfers between devices, swap(): lax.ppermute(values, axis, [(i, i ^ flip) for i in range(lax.axis_size(ax...  30.9 us
    pallas_call x12, Pallas kernels, call(): pl.pallas_call(functools.partial(kernel, **options), out_shape=tuple(outs...  18.2 us
    ppermute x15, starting transfers between devices, swap(): lax.ppermute(values, axis, [(i, i ^ flip) for i in range(lax.axis_size(ax...  18.2 us
    ppermute x1, waiting for transfers between devices, on_device(): to_end = lax.ppermute(across, 'outer', outward)  4.49 us
    unnamed x26, local copies, waits for them, and re-layouts  3.58 us
    ppermute x1, starting transfers between devices, on_device(): near = lax.ppermute(rows_half, axes, first)  1.71 us
  transfers between devices with their start and end apart: 20, of which 8 were waited for; matrix products, arithmetic and copies ran while one was open for 0% of the time, Pallas kernels for 16%

profile of v13, /device:TPU:0, one launch (start us, length us, event | category | flops | bytes accessed | tf_op | source)
XLA Modules:
  0.0 83.3 jit_solution(13440396759190647978)
XLA Ops:
  0.6 0.1 pad_add_fusion.place
  0.7 0.6 copy-done.9
  1.3 0.1 copy-done.12
  1.4 0.0 copy-done.11
  1.4 1.1 %copy-done = bf16[512,768]{1,0:T(8,128)(2,1)S(1)} copy-done((bf16[512,768]{1,0:T(8,128)(2,1)S(1)}, bf16[512,768]{1,0:T(8,128)(2,1)}, u32[]{:S(2)}) %copy-start) | copy-done | bytes 786456
  2.6 1.0 %copy-done.2 = bf16[256,768]{1,0:T(8,128)(2,1)S(1)} copy-done((bf16[256,768]{1,0:T(8,128)(2,1)S(1)}, bf16[256,768]{1,0:T(8,128)(2,1)}, u32[]{:S(2)}) %copy-start.2) | copy-done | bytes 393240
  3.6 1.1 %prep.1 = (bf16[400,768]{1,0:T(8,128)(2,1)S(1)}, f32[6,128]{1,0:T(8,128)S(1)}, bf16[80,768]{1,0:T(8,128)(2,1)S(1)}, bf16[80,768]{1,0:T(8,128)(2,1)S(1)}, bf16[80...) custom-call(s32[3]{0:T(128)S(1)} %pad_add_fusion.place, bf16[512,768]{1,0:T(8,128)(2,1)S(1)} %copy-done, ...), custom_call_target="tpu_custom_call" | custom-call | flops 1 | bytes 1 | tf_op jit(solution)/shard_map/prep/pallas_call | solution.py:333
  4.6 0.0 copy-start.4
  4.6 3.1 %collective-permute-start.1 = (bf16[80,768]{1,0:T(8,128)(2,1)S(1)}, bf16[80,768]{1,0:T(8,128)(2,1)S(1)}, u32[]{:S(2)}, u32[]{:S(2)}) collective-permute-start(bf16[80,768]{1,0:T(8,128)(2,1)S(1)} %get-tuple-element.39), channel_id=1, source_target_pairs={{0,8},{8,0},{16,24},{24,16},{1,9},{9,1},{17,25},{25,17},{2,10},{10... | collective-permute-start | bytes 368648 | tf_op jit(solution)/shard_map/ppermute | solution.py:346
  7.7 2.6 %collective-permute-start.4 = (bf16[80,768]{1,0:T(8,128)(2,1)S(1)}, bf16[80,768]{1,0:T(8,128)(2,1)S(1)}, u32[]{:S(2)}, u32[]{:S(2)}) collective-permute-start(bf16[80,768]{1,0:T(8,128)(2,1)S(1)} %get-tuple-element.43), channel_id=1, source_target_pairs={{0,16},{8,24},{16,0},{24,8},{1,17},{9,25},{17,1},{25,9},{2,18},{10... | collective-permute-start | bytes 368648 | tf_op jit(solution)/shard_map/ppermute | solution.py:346
  10.3 0.0 collective-permute-start.5
  10.3 1.7 %collective-permute-start = (bf16[400,768]{1,0:T(8,128)(2,1)S(1)}, bf16[400,768]{1,0:T(8,128)(2,1)S(1)}, u32[]{:S(2)}, u32[]{:S(2)}) collective-permute-start(bf16[400,768]{1,0:T(8,128)(2,1)S(1)} %get-tuple-element.38), channel_id=1, source_target_pairs={{0,2},{1,5},{2,0},{3,7},{4,6},{5,1},{6,4},{7,3},{8,10},{9,13},{10,... | collective-permute-start | bytes 1843208 | tf_op jit(solution)/shard_map/ppermute | solution.py:481
  12.0 1.5 %collective-permute-start.14 = (bf16[400,768]{1,0:T(8,128)(2,1)S(1)}, bf16[400,768]{1,0:T(8,128)(2,1)S(1)}, u32[]{:S(2)}, u32[]{:S(2)}) collective-permute-start(bf16[400,768]{1,0:T(8,128)(2,1)S(1)} %get-tuple-element.38), channel_id=1, source_target_pairs={{0,4},{1,3},{2,6},{3,1},{4,0},{5,7},{6,2},{7,5},{8,12},{9,11},{10,... | collective-permute-start | bytes 1843208 | tf_op jit(solution)/shard_map/ppermute | solution.py:482
  13.6 0.0 collective-permute-done.1.refs_1_
  13.6 6.5 %collective-permute-done.4.refs_2_ = bf16[80,768]{1,0:T(8,128)(2,1)S(1)} collective-permute-done((bf16[80,768]{1,0:T(8,128)(2,1)S(1)}, bf16[80,768]{1,0:T(8,128)(2,1)S(1)}, u32[]{:S(2)}, u32[]{:S(2)}) %collective-permute-start.4) | collective-permute-done | bytes 122912 | tf_op jit(solution)/shard_map/ppermute | solution.py:346
  20.0 0.0 collective-permute-done.5.refs_3_
  20.1 0.1 relay.1
  20.1 1.6 %collective-permute-start.6 = (bf16[80,768]{1,0:T(8,128)(2,1)S(1)}, bf16[80,768]{1,0:T(8,128)(2,1)S(1)}, u32[]{:S(2)}, u32[]{:S(2)}) collective-permute-start(bf16[80,768]{1,0:T(8,128)(2,1)S(1)} %get-tuple-element.46), channel_id=1, source_target_pairs={{0,2},{2,0},{4,6},{6,4},{1,3},{3,1},{5,7},{7,5},{8,10},{10,8},{12,... | collective-permute-start | bytes 368648 | tf_op jit(solution)/shard_map/ppermute | solution.py:346
  21.7 1.5 %collective-permute-start.7 = (bf16[80,768]{1,0:T(8,128)(2,1)S(1)}, bf16[80,768]{1,0:T(8,128)(2,1)S(1)}, u32[]{:S(2)}, u32[]{:S(2)}) collective-permute-start(bf16[80,768]{1,0:T(8,128)(2,1)S(1)} %get-tuple-element.47), channel_id=1, source_target_pairs={{0,4},{2,6},{4,0},{6,2},{1,5},{3,7},{5,1},{7,3},{8,12},{10,14},{12... | collective-permute-start | bytes 368648 | tf_op jit(solution)/shard_map/ppermute | solution.py:346
  23.2 0.5 collective-permute-start.8
  23.7 5.9 %collective-permute-done.6.refs_5_ = bf16[80,768]{1,0:T(8,128)(2,1)S(1)} collective-permute-done((bf16[80,768]{1,0:T(8,128)(2,1)S(1)}, bf16[80,768]{1,0:T(8,128)(2,1)S(1)}, u32[]{:S(2)}, u32[]{:S(2)}) %collective-permute-start.6) | collective-permute-done | bytes 122912 | tf_op jit(solution)/shard_map/ppermute | solution.py:346
  29.6 3.9 %collective-permute-start.3 = (bf16[256,768]{1,0:T(8,128)(2,1)S(1)}, bf16[256,768]{1,0:T(8,128)(2,1)S(1)}, u32[]{:S(2)}, u32[]{:S(2)}) collective-permute-start(bf16[256,768]{1,0:T(8,128)(2,1)S(1)} %copy-done.4), channel_id=1, source_target_pairs={{0,24},{8,16},{16,8},{24,0},{1,25},{9,17},{17,9},{25,1},{2,26},{10... | collective-permute-start | bytes 1179656 | tf_op jit(solution)/shard_map/ppermute | solution.py:346
  33.5 0.0 collective-permute-done.7.refs_6_
  33.5 0.0 collective-permute-start.2
  33.5 0.6 copy-done.7
  34.1 0.0 collective-permute-done.8.refs_7_
  34.1 0.9 %slice-done = bf16[64,768]{1,0:T(8,128)(2,1)S(1)} async-done(((bf16[80,768]{1,0:T(8,128)(2,1)}), bf16[64,768]{1,0:T(8,128)(2,1)S(1)}, s32[]{:S(2)}) %slice-start) | async-done | bytes 98328 | tf_op jit(solution)/shard_map/slice | solution.py:447
  35.0 0.0 slice-done.1
  35.1 0.0 copy-start.1
  35.1 0.1 collective-permute-start.12
  35.2 0.7 lists.1.maps
  35.9 0.1 copy-done.6
  36.0 0.1 copy-done.8
  36.0 3.0 %meta.1 = (f32[4,3072]{1,0:T(4,128)S(1)}, f32[1,3072]{1,0:T(1,128)S(1)}, f32[4,256]{1,0:T(4,128)S(1)}, s32[1,512]{1,0:T(1,128)S(1)}, s32[1,512]{1,0:T(1,128)S(1)}, /*index=5*/s32[1,512]{1,0:T(1,128)}) custom-call(s32[3]{0:T(128)S(1)} %pad_add_fusion.place, bf16[4,128,64]{2,1,0:T(8,128)(2,1)S(1)} %lists.1.maps, s32[1,512]{1,0:T(1,128)S(1)} %bitcast.10, ...), custom_call_target="tpu_custom_call" | custom-call | flops 1 | bytes 1 | tf_op jit(solution)/shard_map/meta/pallas_call | solution.py:333
  39.0 4.6 %collective-permute-done.3.refs_0_.refs_1_ = bf16[256,768]{1,0:T(8,128)(2,1)S(1)} collective-permute-done((bf16[256,768]{1,0:T(8,128)(2,1)S(1)}, bf16[256,768]{1,0:T(8,128)(2,1)S(1)}, u32[]{:S(2)}, u32[]{:S(2)}) %collective-permute-start.3) | collective-permute-done | bytes 393248 | tf_op jit(solution)/shard_map/ppermute | solution.py:346
  43.6 6.8 %collective-permute-done.2.refs_0_.refs_1_ = bf16[256,768]{1,0:T(8,128)(2,1)S(1)} collective-permute-done((bf16[256,768]{1,0:T(8,128)(2,1)S(1)}, bf16[256,768]{1,0:T(8,128)(2,1)S(1)}, u32[]{:S(2)}, u32[]{:S(2)}) %collective-permute-start.2) | collective-permute-done | bytes 393248 | tf_op jit(solution)/shard_map/ppermute | solution.py:346
  50.3 0.0 collective-permute-done.refs_7_.refs_8_
  50.3 0.0 collective-permute-done.14.refs_9_.refs_10_
  50.3 0.0 collective-permute-start.15
  50.3 0.5 collective-permute-start.13
  50.8 0.7 collective-permute-start.10
  51.5 1.5 %collective-permute-start.11 = (bf16[256,768]{1,0:T(8,128)(2,1)S(1)}, bf16[256,768]{1,0:T(8,128)(2,1)S(1)}, u32[]{:S(2)}, u32[]{:S(2)}) collective-permute-start(bf16[256,768]{1,0:T(8,128)(2,1)S(1)} %collective-permute-done.3.refs_0_.refs_1_), channel_id=1, source_target_pairs={{8,0},{16,24},{9,1},{17,25},{10,2},{18,26},{11,3},{19,27},{12,4},{... | collective-permute-start | bytes 1179656 | tf_op jit(solution)/shard_map/ppermute | solution.py:487
  53.0 0.0 copy-start.3
  53.0 1.5 %apply.1 = bf16[512,768]{1,0:T(8,128)(2,1)} custom-call(s32[1,512]{1,0:T(1,128)S(1)} %get-tuple-element.53.target, s32[1,512]{1,0:T(1,128)S(1)} %get-tuple-element.54.refreshed, bf16[512,768]{1,0:T(8,128)(2,1)S(1)} %copy-done.1, bf16[256,768]{1,0:T(8,128)(2,1)S(1)} %pad_maximum_fusion.refs_0_, bf16[256,768]{1,0:T(8,128)(2,1)S(1)} %collective-permute-done.12.refs_1_), custom_call_target="tpu_custom_call" | custom-call | flops 1 | bytes 1 | tf_op jit(solution)/shard_map/apply/pallas_call | solution.py:333
  54.5 0.0 collective-permute-done.15.refs_10_.refs_11_
  54.5 0.0 collective-permute-done.13.refs_8_.refs_9_
  54.5 2.0 %score.9.refs_0_ = f32[2,2,128]{2,1,0:T(2,128)S(1)} custom-call(s32[3]{0:T(128)S(1)} %pad_add_fusion.place, bf16[256,768]{1,0:T(8,128)(2,1)S(1)} %collective-permute-done.3.refs_0_.refs_1_, f32[4,256]{1,0:T(4,128)S(1)} %get-tuple-element.55.refs_1_.refs_2_, f32[4,3072]{1,0:T(4,128)S(1)} %get-tuple-element.56.refs_2_.refs_3_, ...), custom_call_target="tpu_custom_call" | custom-call | flops 1 | bytes 1 | tf_op jit(solution)/shard_map/score/pallas_call | solution.py:333
  56.5 2.0 %score.8.refs_0_ = f32[2,2,128]{2,1,0:T(2,128)S(1)} custom-call(s32[3]{0:T(128)S(1)} %pad_add_fusion.place, bf16[256,768]{1,0:T(8,128)(2,1)S(1)} %collective-permute-done.2.refs_0_.refs_1_, f32[4,256]{1,0:T(4,128)S(1)} %get-tuple-element.55.refs_1_.refs_2_, f32[4,3072]{1,0:T(4,128)S(1)} %get-tuple-element.56.refs_2_.refs_3_, ...), custom_call_target="tpu_custom_call" | custom-call | flops 1 | bytes 1 | tf_op jit(solution)/shard_map/score/pallas_call | solution.py:333
  58.5 2.0 %score.7.refs_0_ = f32[2,2,128]{2,1,0:T(2,128)S(1)} custom-call(s32[3]{0:T(128)S(1)} %pad_add_fusion.place, bf16[256,768]{1,0:T(8,128)(2,1)S(1)} %copy-done.4, f32[4,256]{1,0:T(4,128)S(1)} %get-tuple-element.55.refs_1_.refs_2_, f32[4,3072]{1,0:T(4,128)S(1)} %get-tuple-element.56.refs_2_.refs_3_, f32[1,3072]{1,0:T(1,128)S(1)} %get-tuple-element.57.refs_3_.refs_4_, ...), custom_call_target="tpu_custom_call" | custom-call | flops 1 | bytes 1 | tf_op jit(solution)/shard_map/score/pallas_call | solution.py:333
  60.5 4.5 %collective-permute-done.11.refs_0_ = bf16[256,768]{1,0:T(8,128)(2,1)S(1)} collective-permute-done((bf16[256,768]{1,0:T(8,128)(2,1)S(1)}, bf16[256,768]{1,0:T(8,128)(2,1)S(1)}, u32[]{:S(2)}, u32[]{:S(2)}) %collective-permute-start.11) | collective-permute-done | bytes 393248 | tf_op jit(solution)/shard_map/ppermute | solution.py:487
  64.9 0.0 collective-permute-done.9.refs_12_
  64.9 0.3 collective-permute-start.16
  65.2 1.7 %collective-permute-done.16.refs_13_ = bf16[400,768]{1,0:T(8,128)(2,1)S(1)} collective-permute-done((bf16[400,768]{1,0:T(8,128)(2,1)S(1)}, bf16[400,768]{1,0:T(8,128)(2,1)S(1)}, u32[]{:S(2)}, u32[]{:S(2)}) %collective-permute-start.16) | collective-permute-done | bytes 614432 | tf_op jit(solution)/shard_map/ppermute | solution.py:346
  67.0 1.2 %score.11 = f32[2,2,128]{2,1,0:T(2,128)S(1)} custom-call(s32[3]{0:T(128)S(1)} %pad_add_fusion.place, f32[2,2,128]{2,1,0:T(2,128)S(1)} %score.8.refs_0_, bf16[256,768]{1,0:T(8,128)(2,1)S(1)} %collective-permute-done.2.refs_0_.refs_1_, f32[4,256]{1,0:T(4,128)S(1)} %get-tuple-element.55.refs_1_.refs_2_, f32[4,3072]{1,0:T(4,128)S(1)} %get-tuple-element.56.refs_2_.refs_3_, ...), custom_call_target="tpu_custom_call" | custom-call | flops 1 | bytes 1 | tf_op jit(solution)/shard_map/score/pallas_call | solution.py:333
  68.2 0.9 %collective-permute-start.17 = (f32[2,2,128]{2,1,0:T(2,128)S(1)}, f32[2,2,128]{2,1,0:T(2,128)S(1)}, u32[]{:S(2)}, u32[]{:S(2)}) collective-permute-start(f32[2,2,128]{2,1,0:T(2,128)S(1)} %score.11), channel_id=1, source_target_pairs={{0,8},{8,0},{16,24},{24,16},{1,9},{9,1},{17,25},{25,17},{2,10},{10... | collective-permute-start | bytes 6152 | tf_op jit(solution)/shard_map/ppermute | solution.py:346
  69.1 1.2 %score.12 = f32[2,2,128]{2,1,0:T(2,128)S(1)} custom-call(s32[3]{0:T(128)S(1)} %pad_add_fusion.place, f32[2,2,128]{2,1,0:T(2,128)S(1)} %score.9.refs_0_, bf16[256,768]{1,0:T(8,128)(2,1)S(1)} %collective-permute-done.3.refs_0_.refs_1_, f32[4,256]{1,0:T(4,128)S(1)} %get-tuple-element.55.refs_1_.refs_2_, f32[4,3072]{1,0:T(4,128)S(1)} %get-tuple-element.56.refs_2_.refs_3_, ...), custom_call_target="tpu_custom_call" | custom-call | flops 1 | bytes 1 | tf_op jit(solution)/shard_map/score/pallas_call | solution.py:333
  70.4 2.3 %collective-permute-start.18 = (f32[2,2,128]{2,1,0:T(2,128)S(1)}, f32[2,2,128]{2,1,0:T(2,128)S(1)}, u32[]{:S(2)}, u32[]{:S(2)}) collective-permute-start(f32[2,2,128]{2,1,0:T(2,128)S(1)} %score.12), channel_id=1, source_target_pairs={{0,24},{8,16},{16,8},{24,0},{1,25},{9,17},{17,9},{25,1},{2,26},{10... | collective-permute-start | bytes 6152 | tf_op jit(solution)/shard_map/ppermute | solution.py:346
  72.7 1.2 %score.10 = f32[2,2,128]{2,1,0:T(2,128)S(1)} custom-call(s32[3]{0:T(128)S(1)} %pad_add_fusion.place, f32[2,2,128]{2,1,0:T(2,128)S(1)} %score.7.refs_0_, bf16[256,768]{1,0:T(8,128)(2,1)S(1)} %copy-done.4, f32[4,256]{1,0:T(4,128)S(1)} %get-tuple-element.55.refs_1_.refs_2_, f32[4,3072]{1,0:T(4,128)S(1)} %get-tuple-element.56.refs_2_.refs_3_, ...), custom_call_target="tpu_custom_call" | custom-call | flops 1 | bytes 1 | tf_op jit(solution)/shard_map/score/pallas_call | solution.py:333
  73.9 0.0 collective-permute-done.17
  73.9 1.9 %collective-permute-done.18 = f32[2,2,128]{2,1,0:T(2,128)S(1)} collective-permute-done((f32[2,2,128]{2,1,0:T(2,128)S(1)}, f32[2,2,128]{2,1,0:T(2,128)S(1)}, u32[]{:S(2)}, u32[]{:S(2)}) %collective-permute-start.18) | collective-permute-done | bytes 2080 | tf_op jit(solution)/shard_map/ppermute | solution.py:346
  75.8 2.3 %score.13 = f32[2,2,128]{2,1,0:T(2,128)S(1)} custom-call(s32[3]{0:T(128)S(1)} %pad_add_fusion.place, bf16[256,768]{1,0:T(8,128)(2,1)S(1)} %collective-permute-done.11.refs_0_, bf16[256,768]{1,0:T(8,128)(2,1)S(1)} %collective-permute-done.10.refs_1_, f32[4,256]{1,0:T(4,128)S(1)} %get-tuple-element.55.refs_1_.refs_2_, ...), custom_call_target="tpu_custom_call" | custom-call | flops 1 | bytes 1 | tf_op jit(solution)/shard_map/score/pallas_call | solution.py:333
  78.1 1.0 %collective-permute-start.19 = (f32[2,2,128]{2,1,0:T(2,128)S(1)}, f32[2,2,128]{2,1,0:T(2,128)S(1)}, u32[]{:S(2)}, u32[]{:S(2)}) collective-permute-start(f32[2,2,128]{2,1,0:T(2,128)S(1)} %score.13), channel_id=1, source_target_pairs={{0,16},{8,24},{16,0},{24,8},{1,17},{9,25},{17,1},{25,9},{2,18},{10... | collective-permute-start | bytes 6152 | tf_op jit(solution)/shard_map/ppermute | solution.py:346
  79.2 3.5 %collective-permute-done.19 = f32[2,2,128]{2,1,0:T(2,128)S(1)} collective-permute-done((f32[2,2,128]{2,1,0:T(2,128)S(1)}, f32[2,2,128]{2,1,0:T(2,128)S(1)}, u32[]{:S(2)}, u32[]{:S(2)}) %collective-permute-start.19) | collective-permute-done | bytes 2080 | tf_op jit(solution)/shard_map/ppermute | solution.py:346
  82.7 0.6 fusion.1
  (24 shorter events, 0.1 us)
Async XLA Ops:
  0.6 0.7 copy-start.9
  0.7 0.7 copy-start.12
  0.7 0.7 copy-start.11
  1.4 1.1 %copy-start = (bf16[512,768]{1,0:T(8,128)(2,1)S(1)}, bf16[512,768]{1,0:T(8,128)(2,1)}, u32[]{:S(2)}) copy-start(bf16[512,768]{1,0:T(8,128)(2,1)} %refs_6_.13) | copy-start | bytes 2359300
  2.6 1.0 %copy-start.2 = (bf16[256,768]{1,0:T(8,128)(2,1)S(1)}, bf16[256,768]{1,0:T(8,128)(2,1)}, u32[]{:S(2)}) copy-start(bf16[256,768]{1,0:T(8,128)(2,1)} %refs_7_.7) | copy-start | bytes 1179652
  3.5 16.5 %copy-start.10 = (s32[512]{0:T(512)S(1)}, s32[512]{0:T(512)}, u32[]{:S(2)}) copy-start(s32[512]{0:T(512)} %param.8) | copy-start | bytes 6148
  4.6 25.0 %copy-start.4 = (bf16[256,768]{1,0:T(8,128)(2,1)S(1)}, bf16[256,768]{1,0:T(8,128)(2,1)}, u32[]{:S(2)}) copy-start(bf16[256,768]{1,0:T(8,128)(2,1)} %refs_1_.1) | copy-start | bytes 1179652
  4.6 8.9 %collective-permute-start.1 = (bf16[80,768]{1,0:T(8,128)(2,1)S(1)}, bf16[80,768]{1,0:T(8,128)(2,1)S(1)}, u32[]{:S(2)}, u32[]{:S(2)}) collective-permute-start(bf16[80,768]{1,0:T(8,128)(2,1)S(1)} %get-tuple-element.39), channel_id=1, source_target_pairs={{0,8},{8,0},{16,24},{24,16},{1,9},{9,1},{17,25},{25,17},{2,10},{10... | collective-permute-start | bytes 368648 | tf_op jit(solution)/shard_map/ppermute | solution.py:346
  7.7 12.3 %collective-permute-start.4 = (bf16[80,768]{1,0:T(8,128)(2,1)S(1)}, bf16[80,768]{1,0:T(8,128)(2,1)S(1)}, u32[]{:S(2)}, u32[]{:S(2)}) collective-permute-start(bf16[80,768]{1,0:T(8,128)(2,1)S(1)} %get-tuple-element.43), channel_id=1, source_target_pairs={{0,16},{8,24},{16,0},{24,8},{1,17},{9,25},{17,1},{25,9},{2,18},{10... | collective-permute-start | bytes 368648 | tf_op jit(solution)/shard_map/ppermute | solution.py:346
  10.3 9.7 %collective-permute-start.5 = (bf16[80,768]{1,0:T(8,128)(2,1)S(1)}, bf16[80,768]{1,0:T(8,128)(2,1)S(1)}, u32[]{:S(2)}, u32[]{:S(2)}) collective-permute-start(bf16[80,768]{1,0:T(8,128)(2,1)S(1)} %get-tuple-element.44), channel_id=1, source_target_pairs={{0,24},{8,16},{16,8},{24,0},{1,25},{9,17},{17,9},{25,1},{2,26},{10... | collective-permute-start | bytes 368648 | tf_op jit(solution)/shard_map/ppermute | solution.py:346
  10.3 40.0 %collective-permute-start = (bf16[400,768]{1,0:T(8,128)(2,1)S(1)}, bf16[400,768]{1,0:T(8,128)(2,1)S(1)}, u32[]{:S(2)}, u32[]{:S(2)}) collective-permute-start(bf16[400,768]{1,0:T(8,128)(2,1)S(1)} %get-tuple-element.38), channel_id=1, source_target_pairs={{0,2},{1,5},{2,0},{3,7},{4,6},{5,1},{6,4},{7,3},{8,10},{9,13},{10,... | collective-permute-start | bytes 1843208 | tf_op jit(solution)/shard_map/ppermute | solution.py:481
  12.0 38.3 %collective-permute-start.14 = (bf16[400,768]{1,0:T(8,128)(2,1)S(1)}, bf16[400,768]{1,0:T(8,128)(2,1)S(1)}, u32[]{:S(2)}, u32[]{:S(2)}) collective-permute-start(bf16[400,768]{1,0:T(8,128)(2,1)S(1)} %get-tuple-element.38), channel_id=1, source_target_pairs={{0,4},{1,3},{2,6},{3,1},{4,0},{5,7},{6,2},{7,5},{8,12},{9,11},{10,... | collective-permute-start | bytes 1843208 | tf_op jit(solution)/shard_map/ppermute | solution.py:482
  20.1 9.5 %collective-permute-start.6 = (bf16[80,768]{1,0:T(8,128)(2,1)S(1)}, bf16[80,768]{1,0:T(8,128)(2,1)S(1)}, u32[]{:S(2)}, u32[]{:S(2)}) collective-permute-start(bf16[80,768]{1,0:T(8,128)(2,1)S(1)} %get-tuple-element.46), channel_id=1, source_target_pairs={{0,2},{2,0},{4,6},{6,4},{1,3},{3,1},{5,7},{7,5},{8,10},{10,8},{12,... | collective-permute-start | bytes 368648 | tf_op jit(solution)/shard_map/ppermute | solution.py:346
  21.7 11.8 %collective-permute-start.7 = (bf16[80,768]{1,0:T(8,128)(2,1)S(1)}, bf16[80,768]{1,0:T(8,128)(2,1)S(1)}, u32[]{:S(2)}, u32[]{:S(2)}) collective-permute-start(bf16[80,768]{1,0:T(8,128)(2,1)S(1)} %get-tuple-element.47), channel_id=1, source_target_pairs={{0,4},{2,6},{4,0},{6,2},{1,5},{3,7},{5,1},{7,3},{8,12},{10,14},{12... | collective-permute-start | bytes 368648 | tf_op jit(solution)/shard_map/ppermute | solution.py:346
  23.2 10.9 %collective-permute-start.8 = (bf16[80,768]{1,0:T(8,128)(2,1)S(1)}, bf16[80,768]{1,0:T(8,128)(2,1)S(1)}, u32[]{:S(2)}, u32[]{:S(2)}) collective-permute-start(bf16[80,768]{1,0:T(8,128)(2,1)S(1)} %get-tuple-element.48), channel_id=1, source_target_pairs={{0,6},{2,4},{4,2},{6,0},{1,7},{3,5},{5,3},{7,1},{8,14},{10,12},{12... | collective-permute-start | bytes 368648 | tf_op jit(solution)/shard_map/ppermute | solution.py:346
  29.6 3.9 %copy-start.5 = (bf16[80,768]{1,0:T(8,128)(2,1)}, bf16[80,768]{1,0:T(8,128)(2,1)S(1)}, u32[]{:S(2)}) copy-start(bf16[80,768]{1,0:T(8,128)(2,1)S(1)} %collective-permute-done.6.refs_5_) | copy-start | bytes 368644
  29.6 13.9 %collective-permute-start.3 = (bf16[256,768]{1,0:T(8,128)(2,1)S(1)}, bf16[256,768]{1,0:T(8,128)(2,1)S(1)}, u32[]{:S(2)}, u32[]{:S(2)}) collective-permute-start(bf16[256,768]{1,0:T(8,128)(2,1)S(1)} %copy-done.4), channel_id=1, source_target_pairs={{0,24},{8,16},{16,8},{24,0},{1,25},{9,17},{17,9},{25,1},{2,26},{10... | collective-permute-start | bytes 1179656 | tf_op jit(solution)/shard_map/ppermute | solution.py:346
  33.5 0.6 copy-start.7
  33.5 16.8 %collective-permute-start.2 = (bf16[256,768]{1,0:T(8,128)(2,1)S(1)}, bf16[256,768]{1,0:T(8,128)(2,1)S(1)}, u32[]{:S(2)}, u32[]{:S(2)}) collective-permute-start(bf16[256,768]{1,0:T(8,128)(2,1)S(1)} %copy-done.4), channel_id=1, source_target_pairs={{0,8},{8,0},{16,24},{24,16},{1,9},{9,1},{17,25},{25,17},{2,10},{10... | collective-permute-start | bytes 1179656 | tf_op jit(solution)/shard_map/ppermute | solution.py:346
  34.1 0.9 %slice-start = ((bf16[80,768]{1,0:T(8,128)(2,1)}), bf16[64,768]{1,0:T(8,128)(2,1)S(1)}, s32[]{:S(2)}) async-start(bf16[80,768]{1,0:T(8,128)(2,1)} %copy-done.5), calls=%async_computation | async-start | bytes 196608 | tf_op jit(solution)/shard_map/slice | solution.py:447
  34.1 0.9 %slice-start.1 = ((bf16[80,768]{1,0:T(8,128)(2,1)}), bf16[64,768]{1,0:T(8,128)(2,1)S(1)}, s32[]{:S(2)}) async-start(bf16[80,768]{1,0:T(8,128)(2,1)} %copy-done.7), calls=%async_computation.1 | async-start | bytes 196608 | tf_op jit(solution)/shard_map/slice | solution.py:447
  35.1 0.9 %copy-start.6 = (bf16[80,768]{1,0:T(8,128)(2,1)S(1)}, bf16[80,768]{1,0:T(8,128)(2,1)}, u32[]{:S(2)}) copy-start(bf16[80,768]{1,0:T(8,128)(2,1)} %copy-done.5) | copy-start | bytes 368644
  35.1 1.0 %copy-start.8 = (bf16[80,768]{1,0:T(8,128)(2,1)S(1)}, bf16[80,768]{1,0:T(8,128)(2,1)}, u32[]{:S(2)}) copy-start(bf16[80,768]{1,0:T(8,128)(2,1)} %copy-done.7) | copy-start | bytes 368644
  35.1 17.9 %copy-start.1 = (bf16[512,768]{1,0:T(8,128)(2,1)S(1)}, bf16[512,768]{1,0:T(8,128)(2,1)}, u32[]{:S(2)}) copy-start(bf16[512,768]{1,0:T(8,128)(2,1)} %refs_6_.13) | copy-start | bytes 2359300
  35.1 16.4 %collective-permute-start.12 = (bf16[256,768]{1,0:T(8,128)(2,1)S(1)}, bf16[256,768]{1,0:T(8,128)(2,1)S(1)}, u32[]{:S(2)}, u32[]{:S(2)}) collective-permute-start(bf16[256,768]{1,0:T(8,128)(2,1)S(1)} %pad_maximum_fusion.refs_0_), channel_id=1, source_target_pairs={{0,1},{1,0},{2,3},{3,2},{4,5},{5,4},{6,7},{7,6},{8,9},{9,8},{10,11... | collective-permute-start | bytes 1179656 | tf_op jit(solution)/shard_map/ppermute | solution.py:346
  50.3 4.2 %collective-permute-start.15 = (bf16[400,768]{1,0:T(8,128)(2,1)S(1)}, bf16[400,768]{1,0:T(8,128)(2,1)S(1)}, u32[]{:S(2)}, u32[]{:S(2)}) collective-permute-start(bf16[400,768]{1,0:T(8,128)(2,1)S(1)} %collective-permute-done.14.refs_9_.refs_10_), channel_id=1, source_target_pairs={{0,1},{1,0},{2,3},{3,2},{4,5},{5,4},{6,7},{7,6},{8,9},{9,8},{10,11... | collective-permute-start | bytes 1843208 | tf_op jit(solution)/shard_map/ppermute | solution.py:346
  50.3 4.2 %collective-permute-start.13 = (bf16[400,768]{1,0:T(8,128)(2,1)S(1)}, bf16[400,768]{1,0:T(8,128)(2,1)S(1)}, u32[]{:S(2)}, u32[]{:S(2)}) collective-permute-start(bf16[400,768]{1,0:T(8,128)(2,1)S(1)} %collective-permute-done.refs_7_.refs_8_), channel_id=1, source_target_pairs={{0,1},{1,0},{2,3},{3,2},{4,5},{5,4},{6,7},{7,6},{8,9},{9,8},{10,11... | collective-permute-start | bytes 1843208 | tf_op jit(solution)/shard_map/ppermute | solution.py:346
  50.8 14.1 %collective-permute-start.9 = (bf16[400,768]{1,0:T(8,128)(2,1)S(1)}, bf16[400,768]{1,0:T(8,128)(2,1)S(1)}, u32[]{:S(2)}, u32[]{:S(2)}) collective-permute-start(bf16[400,768]{1,0:T(8,128)(2,1)S(1)} %collective-permute-done.refs_7_.refs_8_), channel_id=1, source_target_pairs={{0,4},{1,3},{2,6},{3,1},{4,0},{5,7},{6,2},{7,5},{8,12},{9,11},{10,... | collective-permute-start | bytes 1843208 | tf_op jit(solution)/shard_map/ppermute | solution.py:488
  50.8 9.6 %collective-permute-start.10 = (bf16[256,768]{1,0:T(8,128)(2,1)S(1)}, bf16[256,768]{1,0:T(8,128)(2,1)S(1)}, u32[]{:S(2)}, u32[]{:S(2)}) collective-permute-start(bf16[256,768]{1,0:T(8,128)(2,1)S(1)} %collective-permute-done.2.refs_0_.refs_1_), channel_id=1, source_target_pairs={{8,16},{16,8},{9,17},{17,9},{10,18},{18,10},{11,19},{19,11},{12,20... | collective-permute-start | bytes 1179656 | tf_op jit(solution)/shard_map/ppermute | solution.py:486
  51.5 13.4 %collective-permute-start.11 = (bf16[256,768]{1,0:T(8,128)(2,1)S(1)}, bf16[256,768]{1,0:T(8,128)(2,1)S(1)}, u32[]{:S(2)}, u32[]{:S(2)}) collective-permute-start(bf16[256,768]{1,0:T(8,128)(2,1)S(1)} %collective-permute-done.3.refs_0_.refs_1_), channel_id=1, source_target_pairs={{8,0},{16,24},{9,1},{17,25},{10,2},{18,26},{11,3},{19,27},{12,4},{... | collective-permute-start | bytes 1179656 | tf_op jit(solution)/shard_map/ppermute | solution.py:487
  53.0 1.5 %copy-start.3 = (bf16[256,768]{1,0:T(8,128)(2,1)S(1)}, bf16[256,768]{1,0:T(8,128)(2,1)}, u32[]{:S(2)}) copy-start(bf16[256,768]{1,0:T(8,128)(2,1)} %refs_7_.7) | copy-start | bytes 1179652
  64.9 2.0 %collective-permute-start.16 = (bf16[400,768]{1,0:T(8,128)(2,1)S(1)}, bf16[400,768]{1,0:T(8,128)(2,1)S(1)}, u32[]{:S(2)}, u32[]{:S(2)}) collective-permute-start(bf16[400,768]{1,0:T(8,128)(2,1)S(1)} %collective-permute-done.9.refs_12_), channel_id=1, source_target_pairs={{0,1},{1,0},{2,3},{3,2},{4,5},{5,4},{6,7},{7,6},{8,9},{9,8},{10,11... | collective-permute-start | bytes 1843208 | tf_op jit(solution)/shard_map/ppermute | solution.py:346
  68.2 5.7 %collective-permute-start.17 = (f32[2,2,128]{2,1,0:T(2,128)S(1)}, f32[2,2,128]{2,1,0:T(2,128)S(1)}, u32[]{:S(2)}, u32[]{:S(2)}) collective-permute-start(f32[2,2,128]{2,1,0:T(2,128)S(1)} %score.11), channel_id=1, source_target_pairs={{0,8},{8,0},{16,24},{24,16},{1,9},{9,1},{17,25},{25,17},{2,10},{10... | collective-permute-start | bytes 6152 | tf_op jit(solution)/shard_map/ppermute | solution.py:346
  70.4 5.4 %collective-permute-start.18 = (f32[2,2,128]{2,1,0:T(2,128)S(1)}, f32[2,2,128]{2,1,0:T(2,128)S(1)}, u32[]{:S(2)}, u32[]{:S(2)}) collective-permute-start(f32[2,2,128]{2,1,0:T(2,128)S(1)} %score.12), channel_id=1, source_target_pairs={{0,24},{8,16},{16,8},{24,0},{1,25},{9,17},{17,9},{25,1},{2,26},{10... | collective-permute-start | bytes 6152 | tf_op jit(solution)/shard_map/ppermute | solution.py:346
  78.1 4.5 %collective-permute-start.19 = (f32[2,2,128]{2,1,0:T(2,128)S(1)}, f32[2,2,128]{2,1,0:T(2,128)S(1)}, u32[]{:S(2)}, u32[]{:S(2)}) collective-permute-start(f32[2,2,128]{2,1,0:T(2,128)S(1)} %score.13), channel_id=1, source_target_pairs={{0,16},{8,24},{16,0},{24,8},{1,17},{9,25},{17,1},{25,9},{2,18},{10... | collective-permute-start | bytes 6152 | tf_op jit(solution)/shard_map/ppermute | solution.py:346

commit v14 on v13

--- a/solution.py
+++ b/solution.py
@@ -80,7 +80,7 @@
 
 
 def prep_kernel(
-    place, table, fresh, ref_ids, neg, pos, rows_out, scale_out, *mail, owners_plane, cap, replicas, encode
+    place, queries, table, fresh, ref_ids, neg, pos, rows_out, scale_out, *mail, owners_plane, cap, replicas, encode
 ):
     outer, inner, core = place[0], place[1], place[2]
     width = table.shape[1]
@@ -101,9 +101,12 @@
     packed = lax.dot_general(select, fresh[...], NN, preferred_element_type=jnp.float32).astype(jnp.bfloat16)
     size = owners_plane * share
     for i, out in enumerate(mail):
-        out[:size, :] = packed[i * size : (i + 1) * size, :]
-        out[size:, :] = jnp.zeros((EXTRA, width), jnp.bfloat16)
-        row = size
+        lead = out.shape[0] - size - EXTRA
+        if lead:
+            out[:lead, :] = queries[...]
+        row = lead + size
+        out[lead:row, :] = packed[i * size : (i + 1) * size, :]
+        out[row:, :] = jnp.zeros((EXTRA, width), jnp.bfloat16)
         for values in (neg[...], pos[...], ids):
             put_ids(out, row, values)
             row += 2 * -(-values.shape[1] // width)
@@ -134,13 +137,14 @@
             rows_out[row + i : row + i + 1, :LANES] = term
 
 
-def relay_kernel(ages, *refs, planes, owners_plane, share, list_size, count, refresh_dev):
-    mail, outs = refs[:planes], refs[planes:]
+def relay_kernel(place, ages, *refs, planes, owners_plane, share, list_size, count, refresh_dev):
+    *mail, whole_out = refs
     size = owners_plane * share
     width = mail[0].shape[1]
     row = size + 2 * (-(-list_size // width) + -(-count // width))
     ids = jnp.concatenate([take_ids(block, row, refresh_dev) for block in mail], axis=1)
-    for side, out in enumerate(outs):
+    for side in range(owners_plane):
+        out = whole_out.at[place[1] ^ side]
         for plane, block in enumerate(mail):
             out[plane * share : (plane + 1) * share, :] = block[side * share : (side + 1) * share, :]
         out[planes * share :, :] = jnp.zeros((EXTRA, width), jnp.bfloat16)
@@ -184,7 +188,7 @@
 ):
     outer, inner, core = place[0], place[1], place[2]
     lw_out, row_out, pos_out, target_out, own_out, ages_out = refs[-6:]
-    mail, relayed = refs[:planes], refs[planes:-6]
+    mail, relayed = refs[:planes], [refs[planes].at[inner ^ side] for side in range(owners_plane)]
     share = cap // replicas
     plane_rows = owners_plane * rows_dev
     high_count = planes * plane_rows // LANES
@@ -240,9 +244,10 @@
     return pl.multiple_of(column, size)
 
 
-def apply_kernel(target, refreshed, table, *refs):
+def apply_kernel(place, target, refreshed, table, *refs, size):
     *arrived, out = refs
-    values = jnp.concatenate([block[...] for block in arrived], axis=0)
+    blocks = [block[place[1] ^ side, :size, :] for block in arrived for side in range(block.shape[0])]
+    values = jnp.concatenate(blocks, axis=0)
     rows = lax.broadcasted_iota(jnp.int32, (out.shape[0], values.shape[0]), 0)
     chosen = jnp.where(rows == target[...], 1.0, 0.0).astype(jnp.bfloat16)
     fresh = lax.dot_general(chosen, values, NN, preferred_element_type=jnp.float32)
@@ -258,9 +263,8 @@
     return jnp.broadcast_to(row, (LANES, LANES)).T
 
 
-def score_kernel(place, *refs, pieces, flip, given, follows):
+def score_kernel(place, *refs, pieces, flip, given):
     out, total, pos_total, q_scale, pos_b, chosen = refs[-6:]
-    before, refs = (refs[0], refs[1:]) if follows else (None, refs)
     positives_row, log_weight, row_ids, scale = refs[given : given + 4]
     positive = positives_row[flip : flip + 1, :]
     queries = refs[0]
@@ -318,7 +322,7 @@
         part = slice(block * LANES, (block + 1) * LANES)
         for i, sums in enumerate((total, pos_total)):
             row = jnp.sum(sums[part, :].T, axis=0, keepdims=True)
-            out[i, block : block + 1, :] = row + before[i, block : block + 1, :] if follows else row
+            out[i, block : block + 1, :] = row
 
 
 def whole(memory=pltpu.VMEM):
@@ -374,8 +378,12 @@
             jax.ShapeDtypeStruct((table_half + fresh_half + EXTRA, width), bf16),
             jax.ShapeDtypeStruct(((rows_dev + refresh_dev) // LANES, LANES), f32),
         ]
-        + [jax.ShapeDtypeStruct((size + EXTRA, width), bf16)] * planes,
+        + [
+            jax.ShapeDtypeStruct((size + EXTRA + query_count * (fast and s in (1, 3)), width), bf16)
+            for s in range(planes)
+        ],
         place,
+        queries,
         table,
         fresh_rows,
         refresh_ids.reshape(1, -1),
@@ -387,8 +395,17 @@
         encode=fast,
     )
     mail = [mail[0]] + [swap(mail[s], "outer", s) for s in range(1, planes)]
-    bare = queries
-    queries, mail[1] = lax.optimization_barrier((queries, mail[1]))
+    if fast:
+        axes = ("inner", "query")
+        first = [(2 * i + c, 2 * (i ^ (1 + c)) + c) for i in range(4) for c in range(2)]
+        second = [(2 * i + c, 2 * (i ^ (2 - c)) + c) for i in range(4) for c in range(2)]
+        near = lax.ppermute(rows_half, axes, first)
+        side_rows = lax.ppermute(rows_half, axes, second)
+        near, side_rows, *mail = lax.optimization_barrier((near, side_rows, *mail))
+        far = lax.ppermute(near, axes, second)
+        near_other, side_other = swap(near, "query", 1), swap(side_rows, "query", 1)
+        beside, mail[1] = mail[1][:query_count], mail[1][query_count:]
+        across, mail[3] = mail[3][:query_count], mail[3][query_count:]
 
     high_count = owners * rows_dev // LANES
     (maps,) = call(
@@ -402,11 +419,11 @@
         high_count=high_count,
     )
 
-    relayed = call(
+    (relayed,) = call(
         relay_kernel,
         "relay",
-        [jax.ShapeDtypeStruct((planes * share + EXTRA, width), bf16)] * owners_plane,
-        None,
+        [jax.ShapeDtypeStruct((owners_plane, planes * share + EXTRA, width), bf16)],
+        place,
         own_ages,
         *mail,
         planes=planes,
@@ -416,7 +433,7 @@
         count=query_count,
         refresh_dev=refresh_dev,
     )
-    relayed = [relayed[0]] + [swap(relayed[s], "inner", s) for s in range(1, owners_plane)]
+    relayed = lax.all_to_all(relayed, "inner", split_axis=0, concat_axis=0, tiled=True)
     lw, row_ids, positive, target, own, new_ages = call(
         meta_kernel,
         "meta",
@@ -432,7 +449,7 @@
         maps,
         own_ages,
         *mail,
-        *relayed,
+        relayed,
         planes=planes,
         owners_plane=owners_plane,
         rows_dev=rows_dev,
@@ -444,22 +461,28 @@
     )
 
     new_ages = new_ages.reshape(rows_dev)
-    came = jnp.concatenate([one[: planes * share] for one in relayed])
-    arrived = [came] + [swap(came, "query", flip) for flip in range(1, replicas)]
+    arrived = [relayed] + [swap(relayed, "query", flip) for flip in range(1, replicas)]
     (new_table,) = call(
-        apply_kernel, "apply", [jax.ShapeDtypeStruct(table.shape, bf16)], None, target, own, table, *arrived
+        apply_kernel,
+        "apply",
+        [jax.ShapeDtypeStruct(table.shape, bf16)],
+        place,
+        target,
+        own,
+        table,
+        *arrived,
+        size=planes * share,
     )
 
     def shift(pieces, columns):
         return [(a, b, c, (d[0] + columns, *d[1:]), e) for a, b, c, d, e in pieces]
 
-    def score(i, given, buffers, pieces, before=()):
+    def score(i, given, buffers, pieces):
         (partial,) = call(
             score_kernel,
             "score",
             [jax.ShapeDtypeStruct((2, query_count // LANES, LANES), f32)],
             place,
-            *before,
             *given,
             positive,
             lw,
@@ -470,32 +493,23 @@
             pieces=pieces,
             flip=flips[i],
             given=len(given),
-            follows=len(before),
         )
         return partial
 
     if fast:
-        axes = ("inner", "query")
-        first = [(2 * i + c, 2 * (i ^ (1 + c)) + c) for i in range(4) for c in range(2)]
-        second = [(2 * i + c, 2 * (i ^ (2 - c)) + c) for i in range(4) for c in range(2)]
-        near = lax.ppermute(rows_half, axes, first)
-        side_rows = lax.ppermute(rows_half, axes, second)
         middle, outward = [(1, 2), (2, 1)], [(1, 0), (2, 3)]
-        beside, across = swap(queries, "outer", 1), swap(queries, "outer", 3)
-        near, beside, across, lw = lax.optimization_barrier((near, beside, across, lw))
         from_end = lax.ppermute(beside, "outer", middle)
         to_end = lax.ppermute(across, "outer", outward)
-        far = lax.ppermute(near, axes, second)
-        got_queries = [(bare,), (beside,), (across,)]
+        got_queries = [(queries,), (beside,), (across,), (to_end, from_end)]
         flips = [0, 1, 3, 2]
         buffers = [table, fresh_rows]
         table_pieces = [(0, 0, rows_dev, (0, rows_dev, None, None), -1)]
         fresh_pieces = [(1, 0, refresh_dev, (0, refresh_dev, None, None), -1 - rows_dev // LANES)]
 
-        def add_pieces(slot, by_core, mine):
+        def add_pieces(slot, by_core, *both):
             data = table_half + fresh_half
             fresh_at = data + 3 * (table_half // LANES)
-            for flip, rows in enumerate((mine, swap(mine, "query", 1))):
+            for flip, rows in enumerate(both):
                 by = None if by_core is None else by_core ^ flip
                 table_pieces.append((len(buffers), 0, table_half, (slot * rows_dev, table_half, flip, by), data))
                 fresh_pieces.append(
@@ -503,16 +517,9 @@
                 )
                 buffers.append(rows)
 
-        add_pieces(1, 0, near)
-        add_pieces(1, 1, side_rows)
-        early = table_pieces + shift(fresh_pieces, plane_rows)
-        partials = [score(i, got_queries[i], list(buffers), early) for i in range(planes - 1)]
-        far, from_end, to_end, new_table, *partials = lax.optimization_barrier((far, from_end, to_end, new_table, *partials))
-        got_queries.append((to_end, from_end))
-        add_pieces(3, None, far)
-        pieces = table_pieces + shift(fresh_pieces, plane_rows)
-        late = [piece for piece in pieces if piece not in early]
-        partials = [score(i, got_queries[i], buffers, late, [partials[i]]) for i in range(planes - 1)]
+        add_pieces(1, 0, near, near_other)
+        add_pieces(1, 1, side_rows, side_other)
+        add_pieces(3, None, far, swap(far, "query", 1))
     else:
         got_queries = [(queries,)] + [(swap(queries, "outer", s),) for s in range(1, planes)]
         flips = range(planes)
@@ -537,10 +544,13 @@
 
         table_pieces = blocks(0, plane_rows, 0)
         fresh_pieces = blocks(1, plane_refresh, plane_rows // LANES)
-        pieces = table_pieces + shift(fresh_pieces, plane_rows)
-        partials = [score(i, got_queries[i], buffers, pieces) for i in range(planes - 1)]
 
     pieces = table_pieces + shift(fresh_pieces, plane_rows)
+    pieces = table_pieces + shift(fresh_pieces, plane_rows)
+    partials = [score(i, got_queries[i], buffers, pieces) for i in range(2)]
+    *partials, given = lax.optimization_barrier((*partials, tuple(got_queries[-1])))
+    got_queries[-1] = given
+    partials += [score(i, got_queries[i], buffers, pieces) for i in range(2, planes - 1)]
     partials = [partials[0]] + [swap(partials[i], "outer", flips[i]) for i in range(1, planes - 1)]
     new_table, *tied = lax.optimization_barrier((new_table, *partials, *got_queries[-1]))
     partials, last_queries = tied[: planes - 1], tied[planes - 1 :]

time: 83.6 us -> 93.1 us (1.11)
  waiting for transfers between devices: 35.4 us -> 42.1 us
  Pallas kernels: 18.2 us -> 20.6 us
  local copies, waits for them, and re-layouts: 4.52 us -> 6.08 us
  starting transfers between devices: 23.6 us -> 22.2 us
    ppermute x15 -> x10, starting transfers between devices: 18.2 us -> 10.9 us  [swap(): lax.ppermute(values, axis, [(i, i ^ flip) for i in range(lax.axis_size(ax...]
    all_to_all x0 -> x1, waiting for transfers between devices: none -> 5.33 us  [on_device(): lax.all_to_all(relayed, 'inner', split_axis=0, concat_axis=0, tiled=True)]
    all_to_all x0 -> x1, starting transfers between devices: none -> 4.13 us  [on_device(): lax.all_to_all(relayed, 'inner', split_axis=0, concat_axis=0, tiled=True)]
    ppermute x1, waiting for transfers between devices: 4.49 us -> 1.27 us  [on_device(): to_end = lax.ppermute(across, 'outer', outward)]
    ppermute x1, waiting for transfers between devices: 0.01 us -> 2.83 us  [on_device(): far = lax.ppermute(near, axes, second)]
    pallas_call x12 -> x9, Pallas kernels: 18.2 us -> 20.6 us  [call(): pl.pallas_call(functools.partial(kernel, **options), out_shape=tuple(outs...]
    ppermute x15 -> x10, waiting for transfers between devices: 30.9 us -> 32.7 us  [swap(): lax.ppermute(values, axis, [(i, i ^ flip) for i in range(lax.axis_size(ax...]
    ppermute x1, starting transfers between devices: 1.52 us -> 3.03 us  [on_device(): side_rows = lax.ppermute(rows_half, axes, second)]
  transfers between devices with their start and end apart: 20 -> 16, of which waited for: 8 -> 6; matrix products, arithmetic and copies ran while one was open for 0% -> 1% of each run, Pallas kernels for 16% -> 18%
where the time goes in v14:
time: 93.1 us; the launch traced here: 92.5 us
  waiting for transfers between devices  42.1 us (45%)
  starting transfers between devices  22.2 us (24%)
  Pallas kernels  20.6 us (22%)
  local copies, waits for them, and re-layouts  6.08 us (7%)
    ppermute x10, waiting for transfers between devices, swap(): lax.ppermute(values, axis, [(i, i ^ flip) for i in range(lax.axis_size(ax...  32.7 us
    pallas_call x9, Pallas kernels, call(): pl.pallas_call(functools.partial(kernel, **options), out_shape=tuple(outs...  20.6 us
    ppermute x10, starting transfers between devices, swap(): lax.ppermute(values, axis, [(i, i ^ flip) for i in range(lax.axis_size(ax...  10.9 us
    all_to_all x1, waiting for transfers between devices, on_device(): lax.all_to_all(relayed, 'inner', split_axis=0, concat_axis=0, tiled=True)  5.33 us
    unnamed x30, local copies, waits for them, and re-layouts  4.96 us
    all_to_all x1, starting transfers between devices, on_device(): lax.all_to_all(relayed, 'inner', split_axis=0, concat_axis=0, tiled=True)  4.13 us
    ppermute x1, starting transfers between devices, on_device(): side_rows = lax.ppermute(rows_half, axes, second)  3.03 us
    ppermute x1, waiting for transfers between devices, on_device(): far = lax.ppermute(near, axes, second)  2.83 us
  transfers between devices with their start and end apart: 16, of which 6 were waited for; matrix products, arithmetic and copies ran while one was open for 1% of the time, Pallas kernels for 18%

profile of v14, /device:TPU:0, one launch (start us, length us, event | category | flops | bytes accessed | tf_op | source)
XLA Modules:
  0.0 92.5 jit_solution(13202105968356206849)
XLA Ops:
  0.6 0.0 copy-start.8
  0.6 0.1 pad_add_fusion.place
  0.7 0.6 copy-done.8
  1.3 0.1 copy-done.11
  1.4 0.0 copy-done.10
  1.4 1.1 %copy-done = bf16[512,768]{1,0:T(8,128)(2,1)S(1)} copy-done((bf16[512,768]{1,0:T(8,128)(2,1)S(1)}, bf16[512,768]{1,0:T(8,128)(2,1)}, u32[]{:S(2)}) %copy-start) | copy-done | bytes 786456
  2.6 1.0 %copy-done.2 = bf16[256,768]{1,0:T(8,128)(2,1)S(1)} copy-done((bf16[256,768]{1,0:T(8,128)(2,1)S(1)}, bf16[256,768]{1,0:T(8,128)(2,1)}, u32[]{:S(2)}) %copy-start.2) | copy-done | bytes 393240
  3.6 1.0 %copy-done.4 = bf16[256,768]{1,0:T(8,128)(2,1)S(1)} copy-done((bf16[256,768]{1,0:T(8,128)(2,1)S(1)}, bf16[256,768]{1,0:T(8,128)(2,1)}, u32[]{:S(2)}) %copy-start.4) | copy-done | bytes 393240
  4.5 1.1 %prep.1 = (bf16[400,768]{1,0:T(8,128)(2,1)S(1)}, f32[6,128]{1,0:T(8,128)S(1)}, bf16[80,768]{1,0:T(8,128)(2,1)S(1)}, bf16[336,768]{1,0:T(8,128)(2,1)S(1)}, bf16[8...) custom-call(s32[3]{0:T(128)S(1)} %pad_add_fusion.place, bf16[256,768]{1,0:T(8,128)(2,1)S(1)} %copy-done.4, ...), custom_call_target="tpu_custom_call" | custom-call | flops 1 | bytes 1 | tf_op jit(solution)/shard_map/prep/pallas_call | solution.py:337
  5.6 3.0 %collective-permute-start.1 = (bf16[400,768]{1,0:T(8,128)(2,1)S(1)}, bf16[400,768]{1,0:T(8,128)(2,1)S(1)}, u32[]{:S(2)}, u32[]{:S(2)}) collective-permute-start(bf16[400,768]{1,0:T(8,128)(2,1)S(1)} %get-tuple-element.31), channel_id=1, source_target_pairs={{0,4},{1,3},{2,6},{3,1},{4,0},{5,7},{6,2},{7,5},{8,12},{9,11},{10,... | collective-permute-start | bytes 1843208 | tf_op jit(solution)/shard_map/ppermute | solution.py:403
  8.7 1.5 %collective-permute-start = (bf16[400,768]{1,0:T(8,128)(2,1)S(1)}, bf16[400,768]{1,0:T(8,128)(2,1)S(1)}, u32[]{:S(2)}, u32[]{:S(2)}) collective-permute-start(bf16[400,768]{1,0:T(8,128)(2,1)S(1)} %get-tuple-element.31), channel_id=1, source_target_pairs={{0,2},{1,5},{2,0},{3,7},{4,6},{5,1},{6,4},{7,3},{8,10},{9,13},{10,... | collective-permute-start | bytes 1843208 | tf_op jit(solution)/shard_map/ppermute | solution.py:402
  10.1 1.6 %collective-permute-start.2 = (bf16[336,768]{1,0:T(8,128)(2,1)S(1)}, bf16[336,768]{1,0:T(8,128)(2,1)S(1)}, u32[]{:S(2)}, u32[]{:S(2)}) collective-permute-start(bf16[336,768]{1,0:T(8,128)(2,1)S(1)} %get-tuple-element.33), channel_id=1, source_target_pairs={{0,8},{8,0},{16,24},{24,16},{1,9},{9,1},{17,25},{25,17},{2,10},{10... | collective-permute-start | bytes 1548296 | tf_op jit(solution)/shard_map/ppermute | solution.py:350
  11.7 2.5 %collective-permute-start.4 = (bf16[336,768]{1,0:T(8,128)(2,1)S(1)}, bf16[336,768]{1,0:T(8,128)(2,1)S(1)}, u32[]{:S(2)}, u32[]{:S(2)}) collective-permute-start(bf16[336,768]{1,0:T(8,128)(2,1)S(1)} %get-tuple-element.35), channel_id=1, source_target_pairs={{0,24},{8,16},{16,8},{24,0},{1,25},{9,17},{17,9},{25,1},{2,26},{10... | collective-permute-start | bytes 1548296 | tf_op jit(solution)/shard_map/ppermute | solution.py:350
  14.2 0.1 collective-permute-start.3
  14.3 27.2 %collective-permute-done.3.refs_2_ = bf16[80,768]{1,0:T(8,128)(2,1)S(1)} collective-permute-done((bf16[80,768]{1,0:T(8,128)(2,1)S(1)}, bf16[80,768]{1,0:T(8,128)(2,1)S(1)}, u32[]{:S(2)}, u32[]{:S(2)}) %collective-permute-start.3) | collective-permute-done | bytes 122912 | tf_op jit(solution)/shard_map/ppermute | solution.py:350
  41.5 0.0 collective-permute-done.2
  41.6 0.0 collective-permute-done.4
  41.6 0.0 copy-start.13
  41.6 0.0 collective-permute-done.1.refs_9_.refs_10_
  41.6 0.0 collective-permute-done.refs_7_.refs_8_
  41.6 0.6 collective-permute-start.8
  42.2 0.0 collective-permute-start.7
  42.2 0.2 copy-done.12
  42.4 0.2 copy-done.13
  42.6 0.0 copy-done.6
  42.6 0.7 copy-done.9
  43.2 1.4 %relay.1 = bf16[4,80,768]{2,1,0:T(8,128)(2,1)} custom-call(s32[3]{0:T(128)S(1)} %pad_add_fusion.place, s32[1,512]{1,0:T(1,128)S(1)} %bitcast.9, bf16[80,768]{1,0:T(8,128)(2,1)S(1)} %get-tuple-element.36.refs_0_, bf16[80,768]{1,0:T(8,128)(2,1)S(1)} %slice.18.refs_1_, bf16[80,768]{1,0:T(8,128)(2,1)S(1)} %collective-permute-done.3.refs_2_, ...), custom_call_target="tpu_custom_call" | custom-call | flops 1 | bytes 1 | tf_op jit(solution)/shard_map/relay/pallas_call | solution.py:337
  44.6 4.1 %all-to-all-start = ((bf16[4,80,768]{2,1,0:T(8,128)(2,1)}), bf16[4,80,768]{2,1,0:T(8,128)(2,1)}, u32[]{:S(2)}, u32[]{:S(2)}) async-start(bf16[4,80,768]{2,1,0:T(8,128)(2,1)} %relay.1), calls=%async_computation | async-start | bytes 983040 | tf_op jit(solution)/shard_map/all_to_all | solution.py:436
  48.8 0.2 collective-permute-start.6
  49.0 2.8 %collective-permute-done.8.refs_11_.refs_12_ = bf16[400,768]{1,0:T(8,128)(2,1)S(1)} collective-permute-done((bf16[400,768]{1,0:T(8,128)(2,1)S(1)}, bf16[400,768]{1,0:T(8,128)(2,1)S(1)}, u32[]{:S(2)}, u32[]{:S(2)}) %collective-permute-start.8) | collective-permute-done | bytes 614432 | tf_op jit(solution)/shard_map/ppermute | solution.py:405
  51.8 0.0 collective-permute-start.9
  51.8 5.3 %all-to-all-done.refs_4_.refs_0_ = bf16[4,80,768]{2,1,0:T(8,128)(2,1)} async-done(((bf16[4,80,768]{2,1,0:T(8,128)(2,1)}), bf16[4,80,768]{2,1,0:T(8,128)(2,1)}, u32[]{:S(2)}, u32[]{:S(2)}) %all-to-all-start) | async-done | bytes 491552 | tf_op jit(solution)/shard_map/all_to_all | solution.py:436
  57.2 0.0 collective-permute-start.5
  57.2 1.1 %slice.20.refs_0_ = bf16[256,768]{1,0:T(8,128)(2,1)S(1)} slice(bf16[336,768]{1,0:T(8,128)(2,1)} %copy-done.12), slice={[0:256], [0:768]} | slice | bytes 786432 | tf_op jit(solution)/shard_map/slice | solution.py:407
  58.3 0.1 copy-done.14
  58.4 0.0 copy-start.1
  58.4 1.4 %collective-permute-start.10 = (bf16[256,768]{1,0:T(8,128)(2,1)S(1)}, bf16[256,768]{1,0:T(8,128)(2,1)S(1)}, u32[]{:S(2)}, u32[]{:S(2)}) collective-permute-start(bf16[256,768]{1,0:T(8,128)(2,1)S(1)} %slice.21.refs_0_), channel_id=1, source_target_pairs={{8,0},{16,24},{9,1},{17,25},{10,2},{18,26},{11,3},{19,27},{12,4},{... | collective-permute-start | bytes 1179656 | tf_op jit(solution)/shard_map/ppermute | solution.py:502
  59.8 0.0 collective-permute-done.7.refs_10_.refs_11_
  59.8 0.7 collective-permute-start.11
  60.5 0.0 copy-done.7
  60.5 0.7 lists.1.maps
  61.2 0.0 copy-start.3
  61.2 3.5 %meta.1 = (f32[4,3072]{1,0:T(4,128)S(1)}, f32[1,3072]{1,0:T(1,128)S(1)}, f32[4,256]{1,0:T(4,128)S(1)}, s32[1,512]{1,0:T(1,128)S(1)}, s32[1,512]{1,0:T(1,128)S(1)}, /*index=5*/s32[1,512]{1,0:T(1,128)}) custom-call(s32[3]{0:T(128)S(1)} %pad_add_fusion.place, bf16[4,128,64]{2,1,0:T(8,128)(2,1)S(1)} %lists.1.maps, s32[1,512]{1,0:T(1,128)S(1)} %bitcast.10, ...), custom_call_target="tpu_custom_call" | custom-call | flops 1 | bytes 1 | tf_op jit(solution)/shard_map/meta/pallas_call | solution.py:337
  64.8 0.0 collective-permute-done.6.refs_8_.refs_9_
  64.8 0.0 collective-permute-done.9.refs_12_.refs_13_
  64.8 0.0 copy-done.1
  64.8 0.0 copy-done.3
  64.8 0.0 copy-start.5
  64.8 2.9 %score.5 = f32[2,2,128]{2,1,0:T(2,128)S(1)} custom-call(s32[3]{0:T(128)S(1)} %pad_add_fusion.place, bf16[256,768]{1,0:T(8,128)(2,1)S(1)} %slice.20.refs_0_, f32[4,256]{1,0:T(4,128)S(1)} %get-tuple-element.42.refs_1_.refs_2_, f32[4,3072]{1,0:T(4,128)S(1)} %get-tuple-element.43.refs_2_.refs_3_, f32[1,3072]{1,0:T(1,128)S(1)} %get-tuple-element.44.refs_3_.refs_4_, ...), custom_call_target="tpu_custom_call" | custom-call | flops 1 | bytes 1 | tf_op jit(solution)/shard_map/score/pallas_call | solution.py:337
  67.7 0.0 copy-done.5
  67.7 2.9 %score.4 = f32[2,2,128]{2,1,0:T(2,128)S(1)} custom-call(s32[3]{0:T(128)S(1)} %pad_add_fusion.place, bf16[256,768]{1,0:T(8,128)(2,1)S(1)} %copy-done.5, f32[4,256]{1,0:T(4,128)S(1)} %get-tuple-element.42.refs_1_.refs_2_, f32[4,3072]{1,0:T(4,128)S(1)} %get-tuple-element.43.refs_2_.refs_3_, f32[1,3072]{1,0:T(1,128)S(1)} %get-tuple-element.44.refs_3_.refs_4_, ...), custom_call_target="tpu_custom_call" | custom-call | flops 1 | bytes 1 | tf_op jit(solution)/shard_map/score/pallas_call | solution.py:337
  70.6 1.3 %collective-permute-done.10.refs_0_ = bf16[256,768]{1,0:T(8,128)(2,1)S(1)} collective-permute-done((bf16[256,768]{1,0:T(8,128)(2,1)S(1)}, bf16[256,768]{1,0:T(8,128)(2,1)S(1)}, u32[]{:S(2)}, u32[]{:S(2)}) %collective-permute-start.10) | collective-permute-done | bytes 393248 | tf_op jit(solution)/shard_map/ppermute | solution.py:502
  71.9 0.0 collective-permute-done.11.refs_1_
  71.9 4.4 %collective-permute-start.12 = (f32[2,2,128]{2,1,0:T(2,128)S(1)}, f32[2,2,128]{2,1,0:T(2,128)S(1)}, u32[]{:S(2)}, u32[]{:S(2)}) collective-permute-start(f32[2,2,128]{2,1,0:T(2,128)S(1)} %score.5), channel_id=1, source_target_pairs={{0,8},{8,0},{16,24},{24,16},{1,9},{9,1},{17,25},{25,17},{2,10},{10... | collective-permute-start | bytes 6152 | tf_op jit(solution)/shard_map/ppermute | solution.py:350
  76.3 2.8 %score.6 = f32[2,2,128]{2,1,0:T(2,128)S(1)} custom-call(s32[3]{0:T(128)S(1)} %pad_add_fusion.place, bf16[256,768]{1,0:T(8,128)(2,1)S(1)} %slice.21.refs_0_, f32[4,256]{1,0:T(4,128)S(1)} %get-tuple-element.42.refs_1_.refs_2_, f32[4,3072]{1,0:T(4,128)S(1)} %get-tuple-element.43.refs_2_.refs_3_, f32[1,3072]{1,0:T(1,128)S(1)} %get-tuple-element.44.refs_3_.refs_4_, ...), custom_call_target="tpu_custom_call" | custom-call | flops 1 | bytes 1 | tf_op jit(solution)/shard_map/score/pallas_call | solution.py:337
  79.1 2.0 %collective-permute-start.13 = (f32[2,2,128]{2,1,0:T(2,128)S(1)}, f32[2,2,128]{2,1,0:T(2,128)S(1)}, u32[]{:S(2)}, u32[]{:S(2)}) collective-permute-start(f32[2,2,128]{2,1,0:T(2,128)S(1)} %score.6), channel_id=1, source_target_pairs={{0,24},{8,16},{16,8},{24,0},{1,25},{9,17},{17,9},{25,1},{2,26},{10... | collective-permute-start | bytes 6152 | tf_op jit(solution)/shard_map/ppermute | solution.py:350
  81.0 0.0 collective-permute-done.5.refs_1_
  81.0 2.5 %apply.1 = bf16[512,768]{1,0:T(8,128)(2,1)} custom-call(s32[3]{0:T(128)S(1)} %pad_add_fusion.place, s32[1,512]{1,0:T(1,128)S(1)} %get-tuple-element.40.target, s32[1,512]{1,0:T(1,128)S(1)} %get-tuple-element.41.refreshed, bf16[512,768]{1,0:T(8,128)(2,1)S(1)} %copy-done.1, bf16[4,80,768]{2,1,0:T(8,128)(2,1)} %all-to-all-done.refs_4_.refs_0_, ...), custom_call_target="tpu_custom_call" | custom-call | flops 1 | bytes 1 | tf_op jit(solution)/shard_map/apply/pallas_call | solution.py:337
  83.5 0.0 collective-permute-done.12
  83.5 1.0 %collective-permute-done.13 = f32[2,2,128]{2,1,0:T(2,128)S(1)} collective-permute-done((f32[2,2,128]{2,1,0:T(2,128)S(1)}, f32[2,2,128]{2,1,0:T(2,128)S(1)}, u32[]{:S(2)}, u32[]{:S(2)}) %collective-permute-start.13) | collective-permute-done | bytes 2080 | tf_op jit(solution)/shard_map/ppermute | solution.py:350
  84.5 2.8 %score.7 = f32[2,2,128]{2,1,0:T(2,128)S(1)} custom-call(s32[3]{0:T(128)S(1)} %pad_add_fusion.place, bf16[256,768]{1,0:T(8,128)(2,1)S(1)} %collective-permute-done.10.refs_0_, bf16[256,768]{1,0:T(8,128)(2,1)S(1)} %collective-permute-done.11.refs_1_, f32[4,256]{1,0:T(4,128)S(1)} %get-tuple-element.42.refs_1_.refs_2_, ...), custom_call_target="tpu_custom_call" | custom-call | flops 1 | bytes 1 | tf_op jit(solution)/shard_map/score/pallas_call | solution.py:337
  87.3 0.1 collective-permute-start.14
  87.4 4.5 %collective-permute-done.14 = f32[2,2,128]{2,1,0:T(2,128)S(1)} collective-permute-done((f32[2,2,128]{2,1,0:T(2,128)S(1)}, f32[2,2,128]{2,1,0:T(2,128)S(1)}, u32[]{:S(2)}, u32[]{:S(2)}) %collective-permute-start.14) | collective-permute-done | bytes 2080 | tf_op jit(solution)/shard_map/ppermute | solution.py:350
  91.9 0.6 fusion.1
  (14 shorter events, 0.1 us)
Async XLA Ops:
  0.6 0.7 copy-start.8
  0.7 0.7 copy-start.11
  0.7 0.7 copy-start.10
  1.4 1.1 %copy-start = (bf16[512,768]{1,0:T(8,128)(2,1)S(1)}, bf16[512,768]{1,0:T(8,128)(2,1)}, u32[]{:S(2)}) copy-start(bf16[512,768]{1,0:T(8,128)(2,1)} %refs_6_.7) | copy-start | bytes 2359300
  2.6 1.0 %copy-start.2 = (bf16[256,768]{1,0:T(8,128)(2,1)S(1)}, bf16[256,768]{1,0:T(8,128)(2,1)}, u32[]{:S(2)}) copy-start(bf16[256,768]{1,0:T(8,128)(2,1)} %refs_7_.1) | copy-start | bytes 1179652
  3.5 1.0 %copy-start.4 = (bf16[256,768]{1,0:T(8,128)(2,1)S(1)}, bf16[256,768]{1,0:T(8,128)(2,1)}, u32[]{:S(2)}) copy-start(bf16[256,768]{1,0:T(8,128)(2,1)} %refs_0_.1) | copy-start | bytes 1179652
  5.6 35.9 %collective-permute-start.1 = (bf16[400,768]{1,0:T(8,128)(2,1)S(1)}, bf16[400,768]{1,0:T(8,128)(2,1)S(1)}, u32[]{:S(2)}, u32[]{:S(2)}) collective-permute-start(bf16[400,768]{1,0:T(8,128)(2,1)S(1)} %get-tuple-element.31), channel_id=1, source_target_pairs={{0,4},{1,3},{2,6},{3,1},{4,0},{5,7},{6,2},{7,5},{8,12},{9,11},{10,... | collective-permute-start | bytes 1843208 | tf_op jit(solution)/shard_map/ppermute | solution.py:403
  8.7 32.9 %collective-permute-start = (bf16[400,768]{1,0:T(8,128)(2,1)S(1)}, bf16[400,768]{1,0:T(8,128)(2,1)S(1)}, u32[]{:S(2)}, u32[]{:S(2)}) collective-permute-start(bf16[400,768]{1,0:T(8,128)(2,1)S(1)} %get-tuple-element.31), channel_id=1, source_target_pairs={{0,2},{1,5},{2,0},{3,7},{4,6},{5,1},{6,4},{7,3},{8,10},{9,13},{10,... | collective-permute-start | bytes 1843208 | tf_op jit(solution)/shard_map/ppermute | solution.py:402
  10.1 31.4 %collective-permute-start.2 = (bf16[336,768]{1,0:T(8,128)(2,1)S(1)}, bf16[336,768]{1,0:T(8,128)(2,1)S(1)}, u32[]{:S(2)}, u32[]{:S(2)}) collective-permute-start(bf16[336,768]{1,0:T(8,128)(2,1)S(1)} %get-tuple-element.33), channel_id=1, source_target_pairs={{0,8},{8,0},{16,24},{24,16},{1,9},{9,1},{17,25},{25,17},{2,10},{10... | collective-permute-start | bytes 1548296 | tf_op jit(solution)/shard_map/ppermute | solution.py:350
  11.7 29.8 %collective-permute-start.4 = (bf16[336,768]{1,0:T(8,128)(2,1)S(1)}, bf16[336,768]{1,0:T(8,128)(2,1)S(1)}, u32[]{:S(2)}, u32[]{:S(2)}) collective-permute-start(bf16[336,768]{1,0:T(8,128)(2,1)S(1)} %get-tuple-element.35), channel_id=1, source_target_pairs={{0,24},{8,16},{16,8},{24,0},{1,25},{9,17},{17,9},{25,1},{2,26},{10... | collective-permute-start | bytes 1548296 | tf_op jit(solution)/shard_map/ppermute | solution.py:350
  14.2 27.3 %collective-permute-start.3 = (bf16[80,768]{1,0:T(8,128)(2,1)S(1)}, bf16[80,768]{1,0:T(8,128)(2,1)S(1)}, u32[]{:S(2)}, u32[]{:S(2)}) collective-permute-start(bf16[80,768]{1,0:T(8,128)(2,1)S(1)} %get-tuple-element.34), channel_id=1, source_target_pairs={{0,16},{8,24},{16,0},{24,8},{1,17},{9,25},{17,1},{25,9},{2,18},{10... | collective-permute-start | bytes 368648 | tf_op jit(solution)/shard_map/ppermute | solution.py:350
  41.5 1.0 %copy-start.6 = (bf16[80,768]{1,0:T(8,128)(2,1)}, bf16[80,768]{1,0:T(8,128)(2,1)S(1)}, u32[]{:S(2)}) copy-start(bf16[80,768]{1,0:T(8,128)(2,1)S(1)} %collective-permute-done.3.refs_2_) | copy-start | bytes 368644
  41.5 0.8 copy-start.12
  41.6 1.0 %copy-start.13 = (bf16[336,768]{1,0:T(8,128)(2,1)}, bf16[336,768]{1,0:T(8,128)(2,1)S(1)}, u32[]{:S(2)}) copy-start(bf16[336,768]{1,0:T(8,128)(2,1)S(1)} %collective-permute-done.4) | copy-start | bytes 1548292
  41.6 10.3 %collective-permute-start.8 = (bf16[400,768]{1,0:T(8,128)(2,1)S(1)}, bf16[400,768]{1,0:T(8,128)(2,1)S(1)}, u32[]{:S(2)}, u32[]{:S(2)}) collective-permute-start(bf16[400,768]{1,0:T(8,128)(2,1)S(1)} %collective-permute-done.refs_7_.refs_8_), channel_id=1, source_target_pairs={{0,4},{1,3},{2,6},{3,1},{4,0},{5,7},{6,2},{7,5},{8,12},{9,11},{10,... | collective-permute-start | bytes 1843208 | tf_op jit(solution)/shard_map/ppermute | solution.py:405
  42.2 17.6 %collective-permute-start.7 = (bf16[400,768]{1,0:T(8,128)(2,1)S(1)}, bf16[400,768]{1,0:T(8,128)(2,1)S(1)}, u32[]{:S(2)}, u32[]{:S(2)}) collective-permute-start(bf16[400,768]{1,0:T(8,128)(2,1)S(1)} %collective-permute-done.1.refs_9_.refs_10_), channel_id=1, source_target_pairs={{0,1},{1,0},{2,3},{3,2},{4,5},{5,4},{6,7},{7,6},{8,9},{9,8},{10,11... | collective-permute-start | bytes 1843208 | tf_op jit(solution)/shard_map/ppermute | solution.py:350
  42.5 0.7 copy-start.9
  44.6 12.5 %all-to-all-start = ((bf16[4,80,768]{2,1,0:T(8,128)(2,1)}), bf16[4,80,768]{2,1,0:T(8,128)(2,1)}, u32[]{:S(2)}, u32[]{:S(2)}) async-start(bf16[4,80,768]{2,1,0:T(8,128)(2,1)} %relay.1), calls=%async_computation | async-start | bytes 983040 | tf_op jit(solution)/shard_map/all_to_all | solution.py:436
  48.8 16.0 %collective-permute-start.6 = (bf16[400,768]{1,0:T(8,128)(2,1)S(1)}, bf16[400,768]{1,0:T(8,128)(2,1)S(1)}, u32[]{:S(2)}, u32[]{:S(2)}) collective-permute-start(bf16[400,768]{1,0:T(8,128)(2,1)S(1)} %collective-permute-done.refs_7_.refs_8_), channel_id=1, source_target_pairs={{0,1},{1,0},{2,3},{3,2},{4,5},{5,4},{6,7},{7,6},{8,9},{9,8},{10,11... | collective-permute-start | bytes 1843208 | tf_op jit(solution)/shard_map/ppermute | solution.py:350
  51.8 12.9 %collective-permute-start.9 = (bf16[400,768]{1,0:T(8,128)(2,1)S(1)}, bf16[400,768]{1,0:T(8,128)(2,1)}, u32[]{:S(2)}, u32[]{:S(2)}) collective-permute-start(bf16[400,768]{1,0:T(8,128)(2,1)S(1)} %collective-permute-done.8.refs_11_.refs_12_), channel_id=1, source_target_pairs={{0,1},{1,0},{2,3},{3,2},{4,5},{5,4},{6,7},{7,6},{8,9},{9,8},{10,11... | collective-permute-start | bytes 1843208 | tf_op jit(solution)/shard_map/ppermute | solution.py:350
  57.2 1.2 %copy-start.14 = (bf16[336,768]{1,0:T(8,128)(2,1)S(1)}, bf16[336,768]{1,0:T(8,128)(2,1)}, u32[]{:S(2)}) copy-start(bf16[336,768]{1,0:T(8,128)(2,1)} %copy-done.13) | copy-start | bytes 1548292
  57.2 23.9 %collective-permute-start.5 = (bf16[4,80,768]{2,1,0:T(8,128)(2,1)}, bf16[4,80,768]{2,1,0:T(8,128)(2,1)S(1)}, u32[]{:S(2)}, u32[]{:S(2)}) collective-permute-start(bf16[4,80,768]{2,1,0:T(8,128)(2,1)} %all-to-all-done.refs_4_.refs_0_), channel_id=1, source_target_pairs={{0,1},{1,0},{2,3},{3,2},{4,5},{5,4},{6,7},{7,6},{8,9},{9,8},{10,11... | collective-permute-start | bytes 1474568 | tf_op jit(solution)/shard_map/ppermute | solution.py:350
  58.3 2.2 %copy-start.7 = (bf16[80,768]{1,0:T(8,128)(2,1)S(1)}, bf16[80,768]{1,0:T(8,128)(2,1)}, u32[]{:S(2)}) copy-start(bf16[80,768]{1,0:T(8,128)(2,1)} %copy-done.6) | copy-start | bytes 368644
  58.4 6.4 %copy-start.1 = (bf16[512,768]{1,0:T(8,128)(2,1)S(1)}, bf16[512,768]{1,0:T(8,128)(2,1)}, u32[]{:S(2)}) copy-start(bf16[512,768]{1,0:T(8,128)(2,1)} %refs_6_.7) | copy-start | bytes 2359300
  58.4 13.5 %collective-permute-start.10 = (bf16[256,768]{1,0:T(8,128)(2,1)S(1)}, bf16[256,768]{1,0:T(8,128)(2,1)S(1)}, u32[]{:S(2)}, u32[]{:S(2)}) collective-permute-start(bf16[256,768]{1,0:T(8,128)(2,1)S(1)} %slice.21.refs_0_), channel_id=1, source_target_pairs={{8,0},{16,24},{9,1},{17,25},{10,2},{18,26},{11,3},{19,27},{12,4},{... | collective-permute-start | bytes 1179656 | tf_op jit(solution)/shard_map/ppermute | solution.py:502
  59.8 12.0 %collective-permute-start.11 = (bf16[256,768]{1,0:T(8,128)(2,1)S(1)}, bf16[256,768]{1,0:T(8,128)(2,1)S(1)}, u32[]{:S(2)}, u32[]{:S(2)}) collective-permute-start(bf16[256,768]{1,0:T(8,128)(2,1)S(1)} %slice.20.refs_0_), channel_id=1, source_target_pairs={{8,16},{16,8},{9,17},{17,9},{10,18},{18,10},{11,19},{19,11},{12,20... | collective-permute-start | bytes 1179656 | tf_op jit(solution)/shard_map/ppermute | solution.py:501
  61.2 3.6 %copy-start.3 = (bf16[256,768]{1,0:T(8,128)(2,1)S(1)}, bf16[256,768]{1,0:T(8,128)(2,1)}, u32[]{:S(2)}) copy-start(bf16[256,768]{1,0:T(8,128)(2,1)} %refs_7_.1) | copy-start | bytes 1179652
  64.8 2.9 %copy-start.5 = (bf16[256,768]{1,0:T(8,128)(2,1)S(1)}, bf16[256,768]{1,0:T(8,128)(2,1)}, u32[]{:S(2)}) copy-start(bf16[256,768]{1,0:T(8,128)(2,1)} %refs_0_.1) | copy-start | bytes 1179652
  71.9 11.7 %collective-permute-start.12 = (f32[2,2,128]{2,1,0:T(2,128)S(1)}, f32[2,2,128]{2,1,0:T(2,128)S(1)}, u32[]{:S(2)}, u32[]{:S(2)}) collective-permute-start(f32[2,2,128]{2,1,0:T(2,128)S(1)} %score.5), channel_id=1, source_target_pairs={{0,8},{8,0},{16,24},{24,16},{1,9},{9,1},{17,25},{25,17},{2,10},{10... | collective-permute-start | bytes 6152 | tf_op jit(solution)/shard_map/ppermute | solution.py:350
  79.1 5.4 %collective-permute-start.13 = (f32[2,2,128]{2,1,0:T(2,128)S(1)}, f32[2,2,128]{2,1,0:T(2,128)S(1)}, u32[]{:S(2)}, u32[]{:S(2)}) collective-permute-start(f32[2,2,128]{2,1,0:T(2,128)S(1)} %score.6), channel_id=1, source_target_pairs={{0,24},{8,16},{16,8},{24,0},{1,25},{9,17},{17,9},{25,1},{2,26},{10... | collective-permute-start | bytes 6152 | tf_op jit(solution)/shard_map/ppermute | solution.py:350
  87.3 4.5 %collective-permute-start.14 = (f32[2,2,128]{2,1,0:T(2,128)S(1)}, f32[2,2,128]{2,1,0:T(2,128)S(1)}, u32[]{:S(2)}, u32[]{:S(2)}) collective-permute-start(f32[2,2,128]{2,1,0:T(2,128)S(1)} %score.7), channel_id=1, source_target_pairs={{0,16},{8,24},{16,0},{24,8},{1,17},{9,25},{17,1},{25,9},{2,18},{10... | collective-permute-start | bytes 6152 | tf_op jit(solution)/shard_map/ppermute | solution.py:350

commit v15 on v3

--- a/solution.py
+++ b/solution.py
@@ -22,16 +22,43 @@
 
 def one_hot(ids, count):
     rows = lax.broadcasted_iota(jnp.int32, (count, ids.shape[1]), 0)
+    if count <= 256:
+        ids = jnp.where((ids < 0) | (ids >= count), -1, ids)
+        rows, ids = rows.astype(jnp.float32).astype(jnp.bfloat16), ids.astype(jnp.float32).astype(jnp.bfloat16)
+        return jnp.where(rows == ids, jnp.bfloat16(1), jnp.bfloat16(0))
     return jnp.where(rows == ids, 1.0, 0.0).astype(jnp.bfloat16)
 
 
-def split_one_hot(ids, high_count):
+def counted(hits):
+    count = hits.shape[1]
+    before = lax.broadcasted_iota(jnp.int32, (count, count), 0)
+    after = lax.broadcasted_iota(jnp.int32, (count, count), 1)
+    earlier = jnp.where(before < after, 1.0, 0.0).astype(jnp.bfloat16)
+    return lax.dot_general(hits.astype(jnp.bfloat16), earlier, NN, preferred_element_type=jnp.float32)
+
+
+def small(values):
+    return values.astype(jnp.float32).astype(jnp.bfloat16)
+
+
+def owner_ranks(rows, refresh_dev, cap):
+    match = jnp.concatenate(rows, axis=0) == 0
+    rank = counted(jnp.where(match, 1.0, 0.0)).astype(jnp.int32)
+    return jnp.where(match, rank, -cap)
+
+
+def one_hots(ids, high_count):
     return one_hot(ids >> 7, high_count), one_hot(ids & 127, LANES)
 
 
 def bitmap(ids, high_count):
-    high, low = split_one_hot(ids, high_count)
-    return lax.dot_general(low, high, NT, preferred_element_type=jnp.float32)
+    high, low = one_hots(ids, high_count)
+    return lax.dot_general(low, high, NT, preferred_element_type=jnp.float32).astype(jnp.bfloat16)
+
+
+def lookup(one_map, pair):
+    hit = lax.dot_general(one_map, pair[0], NN, preferred_element_type=jnp.float32)
+    return jnp.sum(hit * pair[1].astype(jnp.float32), axis=0, keepdims=True)
 
 
 def prep_kernel(place, table, fresh, ages, ref_ids, rows_out, meta_out, *, replicas):
@@ -60,7 +87,8 @@
 
 
 def meta_kernel(
-    place, ref_ids, neg, log_weight, lw_out, row_out, pack_out, apply_out, own_out, *, rows_dev, refresh_dev, cap, replicas
+    place, ref_ids, neg, log_weight, ages, lw_out, row_out, code_out, target_out, own_out, ages_out,
+    *, rows_dev, refresh_dev, cap, replicas
 ):
     outer, inner, core = place[0], place[1], place[2]
     planes, plane_refresh = ref_ids.shape
@@ -68,64 +96,54 @@
     owners_plane = plane_rows // rows_dev
     high_count = planes * plane_rows // LANES
     own_owner = outer * owners_plane + inner
+    share = cap // replicas
     plane_ids = ref_ids[0:1, :]
     column = lax.broadcasted_iota(jnp.int32, (1, plane_rows), 1)
     table_ids = (outer * owners_plane + (inner ^ (column // rows_dev))) * rows_dev + column % rows_dev
 
-    refreshed_map = jnp.zeros((LANES, high_count), jnp.float32)
-    for plane in range(planes):
-        refreshed_map += bitmap(ref_ids[plane : plane + 1, :], high_count)
-    refreshed_map = refreshed_map.astype(jnp.bfloat16)
-
-    table_high, table_low = split_one_hot(table_ids, high_count)
-    fresh_high, fresh_low = split_one_hot(plane_ids, high_count)
-
-    def lookup(one_map, high, low):
-        hit = lax.dot_general(one_map, high, NN, preferred_element_type=jnp.float32)
-        return jnp.sum(hit * low.astype(jnp.float32), axis=0, keepdims=True)
-
-    refreshed = lookup(refreshed_map, table_high, table_low) > 0.5
+    pair = one_hots(jnp.concatenate([table_ids, plane_ids], axis=1), high_count)
+    all_ids = jnp.concatenate([ref_ids[plane : plane + 1, :] for plane in range(planes)], axis=1)
+    refreshed = lookup(bitmap(all_ids, high_count), (pair[0][:, :plane_rows], pair[1][:, :plane_rows])) > 0.5
     row_out[:, :plane_rows] = jnp.where(refreshed, -1, table_ids).astype(jnp.float32)
     row_out[:, plane_rows:] = plane_ids.astype(jnp.float32)
     own_out[...] = refreshed[:, :rows_dev].astype(jnp.int32)
-
+    ages_out[...] = jnp.where(refreshed[:, :rows_dev], 0, ages[...])
+    weights = jnp.where(refreshed, MASKED, log_weight[...])
+    weights = jnp.concatenate([weights, jnp.zeros((1, plane_refresh), jnp.float32)], axis=1)
     for group in range(planes):
-        one_map = bitmap(neg[group : group + 1, :], high_count).astype(jnp.bfloat16)
-        in_list = lookup(one_map, table_high, table_low) > 0.5
-        lw_out[group : group + 1, :plane_rows] = jnp.where(in_list & ~refreshed, log_weight[...], MASKED)
-        in_list = lookup(one_map, fresh_high, fresh_low) > 0.5
-        lw_out[group : group + 1, plane_rows:] = jnp.where(in_list, 0.0, MASKED)
-
-    share = cap // replicas
-    earlier = jnp.where(
-        lax.broadcasted_iota(jnp.int32, (plane_refresh, plane_refresh), 0)
-        < lax.broadcasted_iota(jnp.int32, (plane_refresh, plane_refresh), 1),
-        1.0,
-        0.0,
-    ).astype(jnp.bfloat16)
-    target_plane = outer ^ lax.broadcasted_iota(jnp.int32, (planes, plane_refresh), 0)
-    send_match = plane_ids // rows_dev == target_plane * owners_plane + inner
-    take_match = ref_ids[...] // rows_dev == own_owner
-
-    def ranked(match):
-        ones = jnp.where(match, 1.0, 0.0)
-        rank = lax.dot_general(ones.astype(jnp.bfloat16), earlier, NN, preferred_element_type=jnp.float32)
-        return jnp.where(match, rank.astype(jnp.int32), -cap)
-
-    send_rank, take_rank = ranked(send_match), ranked(take_match)
-    take_row = ref_ids[...] - own_owner * rows_dev
-    pack_out[:cap, :] = one_hot(send_rank[0:1, :], cap)
-    for plane in range(1, planes):
-        first = cap + (plane - 1) * share
-        pack_out[first : first + share, :] = one_hot(send_rank[plane : plane + 1, :] - core * share, share)
-    for plane in range(planes):
-        row = one_hot(take_row[plane : plane + 1, :], rows_dev)
-        for part in range(1 if plane == 0 else replicas):
-            size = cap if plane == 0 else share
-            skip = 0 if plane == 0 else (core ^ part) * share
-            slot = one_hot(take_rank[plane : plane + 1, :] - skip, size)
-            first = plane and cap + (part * (planes - 1) + plane - 1) * share
-            apply_out[:, first : first + size] = lax.dot_general(row, slot, NT, preferred_element_type=jnp.float32)
+        hit = lookup(bitmap(neg[group : group + 1, :], high_count), pair)
+        lw_out[group : group + 1, :] = jnp.where(hit > 0.5, weights, MASKED)
+
+    pairs = [(plane, side) for plane in range(planes) for side in range(owners_plane)]
+
+    def ids_of(plane, side):
+        return ref_ids[plane : plane + 1, side * refresh_dev : (side + 1) * refresh_dev]
+
+    sent = [ids_of(0, side) // rows_dev - ((outer ^ plane) * owners_plane + inner) for plane, side in pairs]
+    taken = [ids_of(plane, side) // rows_dev - own_owner for plane, side in pairs]
+    rank = owner_ranks(sent + taken, refresh_dev, cap)
+    own_slots = owners_plane * cap
+    codes = [jnp.full((1, refresh_dev), -1, jnp.int32)] * owners_plane
+    for i, (plane, side) in enumerate(pairs):
+        size = share if plane else cap
+        base = own_slots + ((plane - 1) * owners_plane + side) * share if plane else side * cap
+        sends = rank[i : i + 1, :] - (core * share if plane else 0)
+        codes[side] = jnp.where((sends >= 0) & (sends < size), base + sends, codes[side])
+        took = rank[len(pairs) + i : len(pairs) + i + 1, :]
+        slot = jnp.where(took < 0, -1, ((took // share) ^ core) * share + took % share if plane else took)
+        row = jnp.where(took < 0, 0, ids_of(plane, side) - own_owner * rows_dev)
+        kinds = lax.broadcasted_iota(jnp.int32, (8, refresh_dev), 0)
+        digits = jnp.where(kinds == 0, row // 16, jnp.where(kinds == 1, row % 16, 1))
+        found = lax.dot_general(small(digits), one_hot(slot, cap), NT, preferred_element_type=jnp.float32)
+        found = found.astype(jnp.int32)
+        target = jnp.where(found[2:3, :] > 0, found[0:1, :] * 16 + found[1:2, :], -1)
+        if plane == 0:
+            target_out[:, base : base + cap] = target
+            continue
+        for part in range(replicas):
+            first = base + part * (planes - 1) * owners_plane * share
+            target_out[:, first : first + share] = target[:, part * share : (part + 1) * share]
+    code_out[...] = jnp.concatenate(codes, axis=1)
 
 
 def piece_offset(place, piece):
@@ -138,27 +156,28 @@
     return pl.multiple_of(column, size)
 
 
-def pack_kernel(place, select, *refs, pieces):
-    out = refs[-1]
-    total = jnp.zeros(out.shape, jnp.float32)
-    for source, start, size, column in pieces:
-        columns = pl.ds(piece_offset(place, column), size)
-        total += lax.dot_general(
-            select[:, columns], refs[source][start : start + size, :], NN, preferred_element_type=jnp.float32
-        )
-    out[...] = total.astype(jnp.bfloat16)
-
-
-def apply_kernel(select, table, *refs):
-    out = refs[-1]
-    fresh = jnp.zeros(out.shape, jnp.float32)
-    first = 0
-    for arrived in refs[:-1]:
-        part = select[:, first : first + arrived.shape[0]].astype(jnp.bfloat16)
-        fresh += lax.dot_general(part, arrived[...], NN, preferred_element_type=jnp.float32)
-        first += arrived.shape[0]
-    hit = jnp.sum(select[...], axis=1, keepdims=True) > 0.5
-    out[...] = jnp.where(hit, fresh, table[...].astype(jnp.float32)).astype(jnp.bfloat16)
+def pack_kernel(place, code, *refs, pieces):
+    *buffers, out = refs
+    selects = [
+        one_hot(code[:, pl.ds(piece_offset(place, column), size)], out.shape[0]) for _, _, size, column in pieces
+    ]
+    values = [buffers[source][start : start + size, :] for source, start, size, _ in pieces]
+    select, values = jnp.concatenate(selects, axis=1), jnp.concatenate(values, axis=0)
+    out[...] = lax.dot_general(select, values, NN, preferred_element_type=jnp.float32).astype(jnp.bfloat16)
+
+
+def apply_kernel(target, refreshed, table, *refs):
+    *arrived, out = refs
+    values = jnp.concatenate([block[...] for block in arrived], axis=0)
+    rows = lax.broadcasted_iota(jnp.int32, (out.shape[0], values.shape[0]), 0)
+    chosen = jnp.where(rows == target[...], 1.0, 0.0).astype(jnp.bfloat16)
+    fresh = lax.dot_general(chosen, values, NN, preferred_element_type=jnp.float32)
+    for top in range(0, out.shape[0], LANES):
+        part = slice(top, top + LANES)
+        hit = to_lanes(refreshed[:, part].astype(jnp.float32)) > 0.5
+        for left in range(0, out.shape[1], LANES):
+            cols = slice(left, left + LANES)
+            out[part, cols] = jnp.where(hit, fresh[part, cols], table[part, cols].astype(jnp.float32)).astype(jnp.bfloat16)
 
 
 def to_lanes(row):
@@ -182,21 +201,35 @@
         pos_b[part, :] = to_lanes(positive[block : block + 1, :])
     total[...] = jnp.zeros_like(total)
     pos_total[...] = jnp.zeros_like(pos_total)
-    for source, start, size, column in pieces:
-        first = piece_offset(place, column)
-        raw = lax.dot_general(
-            queries[...], refs[sources + 4 + source][start : start + size, :], NT, preferred_element_type=jnp.float32
-        )
-        sums = total[...]
-        positives = pos_total[...]
-        for chunk in range(size // LANES):
-            cols = pl.ds(first + chunk * LANES, LANES)
-            part = raw[:, chunk * LANES : (chunk + 1) * LANES]
-            powers = part * q_scale[...] * scale[:, cols] + log_weight[:, cols]
-            sums = sums + jnp.exp2(powers)
-            positives = positives + jnp.where(pos_b[...] == row_ids[:, cols], powers, 0.0)
-        total[...] = sums
-        pos_total[...] = positives
+    refs = refs[sources + 4 : -6]
+
+    def product(group):
+        rows = [refs[source][start : start + size, :] for source, start, size, _ in group]
+        rows = rows[0] if len(rows) == 1 else jnp.concatenate(rows, axis=0)
+        return lax.dot_general(queries[...], rows, NT, preferred_element_type=jnp.float32)
+
+    narrow = [piece for piece in pieces if piece[2] < 256]
+    groups = [[piece] for piece in pieces if piece[2] >= 256] + [narrow[i : i + 2] for i in range(0, len(narrow), 2)]
+    following = product(groups[0])
+    for i, group in enumerate(groups):
+        raw = following
+        if i + 1 < len(groups):
+            following = product(groups[i + 1])
+        columns = []
+        for _, _, size, column in group:
+            columns += [piece_offset(place, column) + chunk * LANES for chunk in range(size // LANES)]
+        for top in range(0, count, 64):
+            part = slice(top, top + 64)
+            sums, positives = total[part, :], pos_total[part, :]
+            query_scale, wanted = q_scale[part, :], pos_b[part, :]
+            for chunk, first in enumerate(columns):
+                cols = pl.ds(first, LANES)
+                powers = raw[part, chunk * LANES : (chunk + 1) * LANES] * query_scale
+                powers = powers * scale[:, cols] + log_weight[:, cols]
+                sums = sums + jnp.exp2(powers)
+                positives = positives + jnp.where(wanted == row_ids[:, cols], powers, 0.0)
+            total[part, :] = sums
+            pos_total[part, :] = positives
     for block in range(count // LANES):
         part = slice(block * LANES, (block + 1) * LANES)
         out[0, block : block + 1, :] = jnp.sum(total[part, :].T, axis=0, keepdims=True)
@@ -255,7 +288,7 @@
     plane_rows = owners_plane * rows_dev
     plane_refresh = owners_plane * refresh_dev
     all_rows = plane_rows + plane_refresh
-    cap = owners_plane * max(2, (2 * refresh_dev + owners - 1) // owners)
+    cap = max(2, (2 * refresh_dev + owners - 1) // owners)
     share = cap // replicas
     table_half, fresh_half = rows_dev // replicas, refresh_dev // replicas
     bf16, f32 = jnp.bfloat16, jnp.float32
@@ -289,32 +322,36 @@
     neg_line = lines[:, plane_refresh : plane_refresh + list_size].astype(jnp.int32)
     positive = lines[:, plane_refresh + list_size :].reshape(planes, -1, LANES)
 
-    lw, row_ids, pack, apply_to, own = call(
+    own_slots, part_slots = owners_plane * cap, owners_plane * share
+    lw, row_ids, code, target, own, new_ages = call(
         meta_kernel,
         "meta",
         [
             jax.ShapeDtypeStruct((planes, all_rows), f32),
             jax.ShapeDtypeStruct((1, all_rows), f32),
-            jax.ShapeDtypeStruct((cap + (planes - 1) * share, plane_refresh), bf16),
-            jax.ShapeDtypeStruct((rows_dev, planes * cap), f32),
+            jax.ShapeDtypeStruct((1, plane_refresh), jnp.int32),
+            jax.ShapeDtypeStruct((1, planes * own_slots), jnp.int32),
+            jax.ShapeDtypeStruct((1, rows_dev), jnp.int32),
             jax.ShapeDtypeStruct((1, rows_dev), jnp.int32),
         ],
         place,
         ref_all,
         neg_line,
         log_weight_plane,
+        ages.reshape(1, -1),
         rows_dev=rows_dev,
         refresh_dev=refresh_dev,
         cap=cap,
         replicas=replicas,
     )
-    new_ages = jnp.where(own.reshape(rows_dev) > 0, 0, ages)
+    new_ages = new_ages.reshape(rows_dev)
 
     if replicas == 2 and owners_plane == 4:
         axes = ("inner", "query")
         first = [(2 * i + c, 2 * (i ^ (1 + c)) + c) for i in range(4) for c in range(2)]
         second = [(2 * i + c, 2 * (i ^ (2 - c)) + c) for i in range(4) for c in range(2)]
         near = lax.ppermute(rows_half, axes, first)
+        near, rows_half, _ = lax.optimization_barrier((near, rows_half, metas))
         side = lax.ppermute(rows_half, axes, second)
         far = lax.ppermute(near, axes, second)
         buffers = [table, fresh_rows]
@@ -341,14 +378,21 @@
         return [(a, b, c, (d[0] + columns, *d[1:])) for a, b, c, d in pieces]
 
     (packed,) = call(
-        pack_kernel, "pack", [jax.ShapeDtypeStruct((pack.shape[0], width), bf16)], place, pack, *buffers, pieces=fresh_pieces
+        pack_kernel,
+        "pack",
+        [jax.ShapeDtypeStruct((own_slots + (planes - 1) * part_slots, width), bf16)],
+        place,
+        code,
+        *buffers,
+        pieces=fresh_pieces,
     )
     parts = []
     for s in range(1, planes):
-        first = cap + (s - 1) * share
-        parts.append(swap(packed[first : first + share], "outer", s))
-    parts = jnp.concatenate(parts)
-    arrived = [packed[:cap], parts] + [swap(parts, "query", flip) for flip in range(1, replicas)]
+        first = own_slots + (s - 1) * part_slots
+        parts.append(swap(packed[first : first + part_slots], "outer", s))
+    parts, *given = lax.optimization_barrier((jnp.concatenate(parts), *got_queries[-1]))
+    got_queries[-1] = tuple(given)
+    arrived = [packed[:own_slots], parts] + [swap(parts, "query", flip) for flip in range(1, replicas)]
 
     pieces = table_pieces + shift(fresh_pieces, plane_rows)
     mine = None
@@ -372,7 +416,7 @@
             partial = swap(partial, "outer", s)
         mine = partial if mine is None else mine + partial
     (new_table,) = call(
-        apply_kernel, "apply", [jax.ShapeDtypeStruct(table.shape, bf16)], None, apply_to, table, *arrived
+        apply_kernel, "apply", [jax.ShapeDtypeStruct(table.shape, bf16)], None, target, own, table, *arrived
     )
     loss = (jnp.log2(mine[0]) - mine[1]) * math.log(2.0)
     return new_table, new_ages, loss.reshape(query_count)

time: 69.4 us -> 73.4 us (1.058)
  waiting for transfers between devices: 13.8 us -> 18.6 us
  Pallas kernels: 20.6 us -> 16.4 us
  starting transfers between devices: 29.3 us -> 33.5 us
    pallas_call x8, Pallas kernels: 20.6 us -> 16.4 us  [call(): pl.pallas_call(functools.partial(kernel, **options), out_shape=tuple(outs...]
    ppermute x17, waiting for transfers between devices: 13.8 us -> 17.9 us  [swap(): lax.ppermute(values, axis, [(i, i ^ flip) for i in range(lax.axis_size(ax...]
    ppermute x17, starting transfers between devices: 20.1 us -> 24.3 us  [swap(): lax.ppermute(values, axis, [(i, i ^ flip) for i in range(lax.axis_size(ax...]
    unnamed x20 -> x16, local copies, waits for them, and re-layouts: 2.86 us -> 2.84 us
  transfers between devices with their start and end apart: 24 -> 24, of which waited for: 8 -> 9; matrix products, arithmetic and copies ran while one was open for 2% -> 1% of each run, Pallas kernels for 26% -> 19%
where the time goes in v15:
time: 73.4 us; the launch traced here: 73.2 us
  starting transfers between devices  33.5 us (46%)
  waiting for transfers between devices  18.6 us (25%)
  Pallas kernels  16.4 us (22%)
  local copies, waits for them, and re-layouts  2.98 us (4%)
  between operations  0.93 us (1%)
  other arithmetic  0.78 us (1%)
    ppermute x17, starting transfers between devices, swap(): lax.ppermute(values, axis, [(i, i ^ flip) for i in range(lax.axis_size(ax...  24.3 us
    ppermute x17, waiting for transfers between devices, swap(): lax.ppermute(values, axis, [(i, i ^ flip) for i in range(lax.axis_size(ax...  17.9 us
    pallas_call x8, Pallas kernels, call(): pl.pallas_call(functools.partial(kernel, **options), out_shape=tuple(outs...  16.4 us
    ppermute x1, starting transfers between devices, on_device(): near = lax.ppermute(rows_half, axes, first)  3 us
    unnamed x16, local copies, waits for them, and re-layouts  2.84 us
    ppermute x1, starting transfers between devices, gather_line(): last = lax.ppermute(from_end, 'outer', outward)  1.47 us
  transfers between devices with their start and end apart: 24, of which 9 were waited for; matrix products, arithmetic and copies ran while one was open for 1% of the time, Pallas kernels for 19%

profile of v15, /device:TPU:0, one launch (start us, length us, event | category | flops | bytes accessed | tf_op | source)
XLA Modules:
  0.0 73.2 jit_solution(4217982920766248518)
XLA Ops:
  0.6 0.1 pad_add_fusion.place
  0.7 0.7 copy-done.4
  1.4 0.0 copy-done.5
  1.4 1.1 %copy-done = bf16[512,768]{1,0:T(8,128)(2,1)S(1)} copy-done((bf16[512,768]{1,0:T(8,128)(2,1)S(1)}, bf16[512,768]{1,0:T(8,128)(2,1)}, u32[]{:S(2)}) %copy-start) | copy-done | bytes 786456
  2.5 1.0 %copy-done.2 = bf16[256,768]{1,0:T(8,128)(2,1)S(1)} copy-done((bf16[256,768]{1,0:T(8,128)(2,1)S(1)}, bf16[256,768]{1,0:T(8,128)(2,1)}, u32[]{:S(2)}) %copy-start.2) | copy-done | bytes 393240
  3.5 0.8 %prep.1 = (bf16[384,768]{1,0:T(8,128)(2,1)S(1)}, f32[12,128]{1,0:T(8,128)S(1)}) custom-call(s32[3]{0:T(128)S(1)} %pad_add_fusion.place, bf16[512,768]{1,0:T(8,128)(2,1)S(1)} %copy-done, bf16[256,768]{1,0:T(8,128)(2,1)S(1)} %copy-done.2, s32[4,128]{1,0:T(4,128)S(1)} %bitcast.23, s32[2,128]{1,0:T(2,128)S(1)} %bitcast.30), custom_call_target="tpu_custom_call" | custom-call | flops 1 | bytes 1 | tf_op jit(solution)/shard_map/prep/pallas_call | solution.py:248
  4.4 3.0 %collective-permute-start.8 = (bf16[384,768]{1,0:T(8,128)(2,1)S(1)}, bf16[384,768]{1,0:T(8,128)(2,1)S(1)}, u32[]{:S(2)}, u32[]{:S(2)}) collective-permute-start(bf16[384,768]{1,0:T(8,128)(2,1)S(1)} %get-tuple-element.26), channel_id=1, source_target_pairs={{0,2},{1,5},{2,0},{3,7},{4,6},{5,1},{6,4},{7,3},{8,10},{9,13},{10,... | collective-permute-start | bytes 1769480 | tf_op jit(solution)/shard_map/ppermute | solution.py:353
  7.4 0.1 collective-permute-start.2
  7.5 2.0 %collective-permute-start.3 = (f32[12,128]{1,0:T(8,128)S(1)}, f32[12,128]{1,0:T(8,128)S(1)}, u32[]{:S(2)}, u32[]{:S(2)}) collective-permute-start(f32[12,128]{1,0:T(8,128)S(1)} %get-tuple-element.19), channel_id=1, source_target_pairs={{0,4},{2,6},{4,0},{6,2},{1,5},{3,7},{5,1},{7,3},{8,12},{10,14},{12... | collective-permute-start | bytes 18440 | tf_op jit(solution)/shard_map/ppermute | solution.py:261
  9.4 1.4 %collective-permute-start.4 = (f32[12,128]{1,0:T(8,128)S(1)}, f32[12,128]{1,0:T(8,128)S(1)}, u32[]{:S(2)}, u32[]{:S(2)}) collective-permute-start(f32[12,128]{1,0:T(8,128)S(1)} %get-tuple-element.19), channel_id=1, source_target_pairs={{0,6},{2,4},{4,2},{6,0},{1,7},{3,5},{5,3},{7,1},{8,14},{10,12},{12... | collective-permute-start | bytes 18440 | tf_op jit(solution)/shard_map/ppermute | solution.py:261
  10.9 0.0 copy-done.3
  10.9 1.6 %collective-permute-start = (bf16[256,768]{1,0:T(8,128)(2,1)S(1)}, bf16[256,768]{1,0:T(8,128)(2,1)S(1)}, u32[]{:S(2)}, u32[]{:S(2)}) collective-permute-start(bf16[256,768]{1,0:T(8,128)(2,1)S(1)} %copy-done.3), channel_id=1, source_target_pairs={{0,8},{8,0},{16,24},{24,16},{1,9},{9,1},{17,25},{25,17},{2,10},{10... | collective-permute-start | bytes 1179656 | tf_op jit(solution)/shard_map/ppermute | solution.py:261
  12.5 3.1 %collective-permute-done.2 = f32[12,128]{1,0:T(8,128)S(1)} collective-permute-done((f32[12,128]{1,0:T(8,128)S(1)}, f32[12,128]{1,0:T(8,128)S(1)}, u32[]{:S(2)}, u32[]{:S(2)}) %collective-permute-start.2) | collective-permute-done | bytes 6176 | tf_op jit(solution)/shard_map/ppermute | solution.py:261
  15.5 0.7 collective-permute-start.1
  16.2 0.0 collective-permute-done.3
  16.2 0.8 %collective-permute-done.4 = f32[12,128]{1,0:T(8,128)S(1)} collective-permute-done((f32[12,128]{1,0:T(8,128)S(1)}, f32[12,128]{1,0:T(8,128)S(1)}, u32[]{:S(2)}, u32[]{:S(2)}) %collective-permute-start.4) | collective-permute-done | bytes 6176 | tf_op jit(solution)/shard_map/ppermute | solution.py:261
  17.0 0.0 copy-start.7
  17.0 0.0 collective-permute-done.8.refs_2_.refs_7_.refs_8_
  17.0 1.3 %collective-permute-start.12 = (bf16[384,768]{1,0:T(8,128)(2,1)S(1)}, bf16[384,768]{1,0:T(8,128)(2,1)S(1)}, u32[]{:S(2)}, u32[]{:S(2)}) collective-permute-start(bf16[384,768]{1,0:T(8,128)(2,1)S(1)} %collective-permute-done.8.refs_2_.refs_7_.refs_8_), channel_id=1, source_target_pairs={{0,4},{1,3},{2,6},{3,1},{4,0},{5,7},{6,2},{7,5},{8,12},{9,11},{10,... | collective-permute-start | bytes 1769480 | tf_op jit(solution)/shard_map/ppermute | solution.py:356
  18.3 0.8 %collective-permute-start.10 = (bf16[384,768]{1,0:T(8,128)(2,1)S(1)}, bf16[384,768]{1,0:T(8,128)(2,1)S(1)}, u32[]{:S(2)}, u32[]{:S(2)}) collective-permute-start(bf16[384,768]{1,0:T(8,128)(2,1)S(1)} %get-tuple-element.26), channel_id=1, source_target_pairs={{0,4},{1,3},{2,6},{3,1},{4,0},{5,7},{6,2},{7,5},{8,12},{9,11},{10,... | collective-permute-start | bytes 1769480 | tf_op jit(solution)/shard_map/ppermute | solution.py:355
  19.2 1.5 %collective-permute-done.refs_0_ = bf16[256,768]{1,0:T(8,128)(2,1)S(1)} collective-permute-done((bf16[256,768]{1,0:T(8,128)(2,1)S(1)}, bf16[256,768]{1,0:T(8,128)(2,1)S(1)}, u32[]{:S(2)}, u32[]{:S(2)}) %collective-permute-start) | collective-permute-done | bytes 393248 | tf_op jit(solution)/shard_map/ppermute | solution.py:261
  20.6 0.0 collective-permute-done.1.refs_1_
  20.6 7.3 %collective-permute-start.5 = (f32[3328]{0:T(1024)S(1)}, f32[3328]{0:T(1024)S(1)}, u32[]{:S(2)}, u32[]{:S(2)}) collective-permute-start(f32[3328]{0:T(1024)S(1)} %pad_maximum_fusion.5), channel_id=1, source_target_pairs={{0,8},{8,0},{16,24},{24,16},{1,9},{9,1},{17,25},{25,17},{2,10},{10... | collective-permute-start | bytes 39944 | tf_op jit(solution)/shard_map/ppermute | solution.py:261
  28.0 1.0 %collective-permute-start.6 = (f32[3328]{0:T(1024)S(1)}, f32[3328]{0:T(1024)S(1)}, u32[]{:S(2)}, u32[]{:S(2)}) collective-permute-start(f32[3328]{0:T(1024)S(1)} %pad_maximum_fusion.5), channel_id=1, source_target_pairs={{0,16},{8,24},{16,0},{24,8},{1,17},{9,25},{17,1},{25,9},{2,18},{10... | collective-permute-start | bytes 39944 | tf_op jit(solution)/shard_map/ppermute | solution.py:261
  29.0 1.5 %collective-permute-start.7 = (f32[3328]{0:T(1024)S(1)}, f32[3328]{0:T(1024)S(1)}, u32[]{:S(2)}, u32[]{:S(2)}) collective-permute-start(f32[3328]{0:T(1024)S(1)} %pad_maximum_fusion.5), channel_id=1, source_target_pairs={{0,24},{8,16},{16,8},{24,0},{1,25},{9,17},{17,9},{25,1},{2,26},{10... | collective-permute-start | bytes 39944 | tf_op jit(solution)/shard_map/ppermute | solution.py:261
  30.5 0.0 collective-permute-done.5
  30.5 0.7 collective-permute-start.17
  31.2 1.4 %collective-permute-done.6 = f32[3328]{0:T(1024)S(1)} collective-permute-done((f32[3328]{0:T(1024)S(1)}, f32[3328]{0:T(1024)S(1)}, u32[]{:S(2)}, u32[]{:S(2)}) %collective-permute-start.6) | collective-permute-done | bytes 13344 | tf_op jit(solution)/shard_map/ppermute | solution.py:261
  32.6 0.0 collective-permute-start.9
  32.6 0.0 collective-permute-done.12.refs_6_.refs_11_.refs_12_
  32.6 0.5 collective-permute-start.13
  33.1 0.2 collective-permute-done.10.refs_4_.refs_9_.refs_10_
  33.3 0.0 collective-permute-start.11
  33.4 1.2 %collective-permute-done.7 = f32[3328]{0:T(1024)S(1)} collective-permute-done((f32[3328]{0:T(1024)S(1)}, f32[3328]{0:T(1024)S(1)}, u32[]{:S(2)}, u32[]{:S(2)}) %collective-permute-start.7) | collective-permute-done | bytes 13344 | tf_op jit(solution)/shard_map/ppermute | solution.py:261
  34.5 1.3 %collective-permute-start.21 = (bf16[256,768]{1,0:T(8,128)(2,1)S(1)}, bf16[256,768]{1,0:T(8,128)(2,1)S(1)}, u32[]{:S(2)}, u32[]{:S(2)}) collective-permute-start(bf16[256,768]{1,0:T(8,128)(2,1)S(1)} %collective-permute-done.1.refs_1_), channel_id=1, source_target_pairs={{8,0},{16,24},{9,1},{17,25},{10,2},{18,26},{11,3},{19,27},{12,4},{... | collective-permute-start | bytes 1179656 | tf_op jit(solution)/shard_map/ppermute | solution.py:273
  35.9 4.0 %meta.1 = (f32[4,3072]{1,0:T(4,128)S(1)}, f32[1,3072]{1,0:T(1,128)S(1)}, s32[1,1024]{1,0:T(1,128)S(1)}, s32[1,512]{1,0:T(1,128)S(1)}, s32[1,512]{1,0:T(1,128)S(1)}, /*index=5*/s32[1,512]{1,0:T(1,128)}) custom-call(s32[3]{0:T(128)S(1)} %pad_add_fusion.place, s32[4,1024]{1,0:T(4,128)S(1)} %maximum_convert_fusion.ref_ids, s32[4,2048]{1,0:T(4,128)S(1)} %fusion.neg, ...), custom_call_target="tpu_custom_call" | custom-call | flops 1 | bytes 1 | tf_op jit(solution)/shard_map/meta/pallas_call | solution.py:248
  39.9 0.0 collective-permute-done.17.refs_1_
  39.9 1.5 %collective-permute-start.18 = (bf16[256,768]{1,0:T(8,128)(2,1)S(1)}, bf16[256,768]{1,0:T(8,128)(2,1)S(1)}, u32[]{:S(2)}, u32[]{:S(2)}) collective-permute-start(bf16[256,768]{1,0:T(8,128)(2,1)S(1)} %collective-permute-done.17.refs_1_), channel_id=1, source_target_pairs={{8,0},{16,24},{9,1},{17,25},{10,2},{18,26},{11,3},{19,27},{12,4},{... | collective-permute-start | bytes 1179656 | tf_op jit(solution)/shard_map/ppermute | solution.py:274
  41.4 0.0 collective-permute-done.9.refs_3_.refs_8_.refs_9_
  41.4 0.0 collective-permute-done.13.refs_7_.refs_12_.refs_13_
  41.4 0.0 collective-permute-done.11.refs_5_.refs_10_.refs_11_
  41.4 1.2 %pack.1 = bf16[320,768]{1,0:T(8,128)(2,1)S(1)} custom-call(s32[3]{0:T(128)S(1)} %pad_add_fusion.place, s32[1,1024]{1,0:T(1,128)S(1)} %get-tuple-element.23.code, bf16[512,768]{1,0:T(8,128)(2,1)S(1)} %copy-done.1, bf16[256,768]{1,0:T(8,128)(2,1)S(1)} %copy-done.2, bf16[384,768]{1,0:T(8,128)(2,1)S(1)} %collective-permute-done.8.refs_2_.refs_7_.refs_8_, ...), custom_call_target="tpu_custom_call" | custom-call | flops 1 | bytes 1 | tf_op jit(solution)/shard_map/pack/pallas_call | solution.py:248
  42.7 3.1 %collective-permute-start.14 = (bf16[64,768]{1,0:T(8,128)(2,1)S(1)}, bf16[64,768]{1,0:T(8,128)(2,1)S(1)}, u32[]{:S(2)}, u32[]{:S(2)}) collective-permute-start(bf16[64,768]{1,0:T(8,128)(2,1)S(1)} %get-tuple-element.35), channel_id=1, source_target_pairs={{0,8},{8,0},{16,24},{24,16},{1,9},{9,1},{17,25},{25,17},{2,10},{10... | collective-permute-start | bytes 294920 | tf_op jit(solution)/shard_map/ppermute | solution.py:261
  45.8 0.7 collective-permute-start.15
  46.5 1.7 %collective-permute-start.16 = (bf16[64,768]{1,0:T(8,128)(2,1)S(1)}, bf16[64,768]{1,0:T(8,128)(2,1)S(1)}, u32[]{:S(2)}, u32[]{:S(2)}) collective-permute-start(bf16[64,768]{1,0:T(8,128)(2,1)S(1)} %get-tuple-element.36), channel_id=1, source_target_pairs={{0,24},{8,16},{16,8},{24,0},{1,25},{9,17},{17,9},{25,1},{2,26},{10... | collective-permute-start | bytes 294920 | tf_op jit(solution)/shard_map/ppermute | solution.py:261
  48.3 0.5 collective-permute-done.21.refs_0_
  48.8 2.2 %score.5 = f32[2,2,128]{2,1,0:T(2,128)S(1)} custom-call(s32[3]{0:T(128)S(1)} %pad_add_fusion.place, bf16[256,768]{1,0:T(8,128)(2,1)S(1)} %collective-permute-done.21.refs_0_, bf16[256,768]{1,0:T(8,128)(2,1)S(1)} %collective-permute-done.17.refs_1_, f32[2,128]{1,0:T(2,128)S(1)} %bitcast.29, f32[1,3072]{1,0:T(1,128)S(1)} %get-tuple-element.38.refs_3_, ...), custom_call_target="tpu_custom_call" | custom-call | flops 1 | bytes 1 | tf_op jit(solution)/shard_map/score/pallas_call | solution.py:248
  51.0 1.3 %collective-permute-start.22 = (f32[2,2,128]{2,1,0:T(2,128)S(1)}, f32[2,2,128]{2,1,0:T(2,128)S(1)}, u32[]{:S(2)}, u32[]{:S(2)}) collective-permute-start(f32[2,2,128]{2,1,0:T(2,128)S(1)} %score.5), channel_id=1, source_target_pairs={{0,16},{8,24},{16,0},{24,8},{1,17},{9,25},{17,1},{25,9},{2,18},{10... | collective-permute-start | bytes 6152 | tf_op jit(solution)/shard_map/ppermute | solution.py:261
  52.3 2.2 %score.4 = f32[2,2,128]{2,1,0:T(2,128)S(1)} custom-call(s32[3]{0:T(128)S(1)} %pad_add_fusion.place, bf16[256,768]{1,0:T(8,128)(2,1)S(1)} %collective-permute-done.refs_0_, f32[2,128]{1,0:T(2,128)S(1)} %bitcast.27, f32[1,3072]{1,0:T(1,128)S(1)} %get-tuple-element.41.refs_2_, f32[1,3072]{1,0:T(1,128)S(1)} %get-tuple-element.32.refs_3_.refs_4_, ...), custom_call_target="tpu_custom_call" | custom-call | flops 1 | bytes 1 | tf_op jit(solution)/shard_map/score/pallas_call | solution.py:248
  54.5 8.8 %collective-permute-done.14 = bf16[64,768]{1,0:T(8,128)(2,1)S(1)} collective-permute-done((bf16[64,768]{1,0:T(8,128)(2,1)S(1)}, bf16[64,768]{1,0:T(8,128)(2,1)S(1)}, u32[]{:S(2)}, u32[]{:S(2)}) %collective-permute-start.14) | collective-permute-done | bytes 98336 | tf_op jit(solution)/shard_map/ppermute | solution.py:261
  63.4 0.0 collective-permute-start.20
  63.4 0.0 collective-permute-done.15
  63.4 0.0 collective-permute-done.16
  63.4 0.0 collective-permute-done.18.refs_0_
  63.4 2.2 %score.6 = f32[2,2,128]{2,1,0:T(2,128)S(1)} custom-call(s32[3]{0:T(128)S(1)} %pad_add_fusion.place, bf16[256,768]{1,0:T(8,128)(2,1)S(1)} %collective-permute-done.18.refs_0_, bf16[256,768]{1,0:T(8,128)(2,1)S(1)} %collective-permute-done.1.refs_1_, f32[2,128]{1,0:T(2,128)S(1)} %bitcast.26, f32[1,3072]{1,0:T(1,128)S(1)} %get-tuple-element.40.refs_3_, ...), custom_call_target="tpu_custom_call" | custom-call | flops 1 | bytes 1 | tf_op jit(solution)/shard_map/score/pallas_call | solution.py:248
  65.7 1.9 %collective-permute-start.23 = (f32[2,2,128]{2,1,0:T(2,128)S(1)}, f32[2,2,128]{2,1,0:T(2,128)S(1)}, u32[]{:S(2)}, u32[]{:S(2)}) collective-permute-start(f32[2,2,128]{2,1,0:T(2,128)S(1)} %score.6), channel_id=1, source_target_pairs={{0,24},{8,16},{16,8},{24,0},{1,25},{9,17},{17,9},{25,1},{2,26},{10... | collective-permute-start | bytes 6152 | tf_op jit(solution)/shard_map/ppermute | solution.py:261
  67.6 2.2 %score.7 = f32[2,2,128]{2,1,0:T(2,128)S(1)} custom-call(s32[3]{0:T(128)S(1)} %pad_add_fusion.place, bf16[256,768]{1,0:T(8,128)(2,1)S(1)} %copy-done.3, f32[2,128]{1,0:T(2,128)S(1)} %bitcast.28, f32[1,3072]{1,0:T(1,128)S(1)} %get-tuple-element.39.refs_2_, f32[1,3072]{1,0:T(1,128)S(1)} %get-tuple-element.32.refs_3_.refs_4_, ...), custom_call_target="tpu_custom_call" | custom-call | flops 1 | bytes 1 | tf_op jit(solution)/shard_map/score/pallas_call | solution.py:248
  69.8 0.1 collective-permute-start.19
  69.9 0.0 collective-permute-done.22
  69.9 0.0 collective-permute-done.20
  69.9 1.2 %collective-permute-done.23 = f32[2,2,128]{2,1,0:T(2,128)S(1)} collective-permute-done((f32[2,2,128]{2,1,0:T(2,128)S(1)}, f32[2,2,128]{2,1,0:T(2,128)S(1)}, u32[]{:S(2)}, u32[]{:S(2)}) %collective-permute-start.23) | collective-permute-done | bytes 2080 | tf_op jit(solution)/shard_map/ppermute | solution.py:261
  71.1 0.6 fusion.2
  71.7 0.0 collective-permute-done.19.refs_2_
  71.7 1.5 %apply.1 = bf16[512,768]{1,0:T(8,128)(2,1)} custom-call(s32[1,512]{1,0:T(1,128)S(1)} %get-tuple-element.21.target, s32[1,512]{1,0:T(1,128)S(1)} %get-tuple-element.22.refreshed, bf16[512,768]{1,0:T(8,128)(2,1)S(1)} %copy-done.1, bf16[128,768]{1,0:T(8,128)(2,1)S(1)} %slice.95.refs_0_, bf16[192,768]{1,0:T(8,128)(2,1)S(1)} %pad_maximum_fusion.refs_1_, ...), custom_call_target="tpu_custom_call" | custom-call | flops 1 | bytes 1 | tf_op jit(solution)/shard_map/apply/pallas_call | solution.py:248
  (32 shorter events, 0.3 us)
Async XLA Ops:
  0.7 0.7 copy-start.4
  0.7 0.7 copy-start.5
  1.4 1.1 %copy-start = (bf16[512,768]{1,0:T(8,128)(2,1)S(1)}, bf16[512,768]{1,0:T(8,128)(2,1)}, u32[]{:S(2)}) copy-start(bf16[512,768]{1,0:T(8,128)(2,1)} %refs_5_.3) | copy-start | bytes 2359300
  2.5 1.0 %copy-start.2 = (bf16[256,768]{1,0:T(8,128)(2,1)S(1)}, bf16[256,768]{1,0:T(8,128)(2,1)}, u32[]{:S(2)}) copy-start(bf16[256,768]{1,0:T(8,128)(2,1)} %refs_6_.7) | copy-start | bytes 1179652
  3.5 7.3 %copy-start.3 = (bf16[256,768]{1,0:T(8,128)(2,1)S(1)}, bf16[256,768]{1,0:T(8,128)(2,1)}, u32[]{:S(2)}) copy-start(bf16[256,768]{1,0:T(8,128)(2,1)} %refs_0_.3) | copy-start | bytes 1179652
  3.5 37.9 %copy-start.1 = (bf16[512,768]{1,0:T(8,128)(2,1)S(1)}, bf16[512,768]{1,0:T(8,128)(2,1)}, u32[]{:S(2)}) copy-start(bf16[512,768]{1,0:T(8,128)(2,1)} %refs_5_.3) | copy-start | bytes 2359300
  4.4 12.6 %collective-permute-start.8 = (bf16[384,768]{1,0:T(8,128)(2,1)S(1)}, bf16[384,768]{1,0:T(8,128)(2,1)S(1)}, u32[]{:S(2)}, u32[]{:S(2)}) collective-permute-start(bf16[384,768]{1,0:T(8,128)(2,1)S(1)} %get-tuple-element.26), channel_id=1, source_target_pairs={{0,2},{1,5},{2,0},{3,7},{4,6},{5,1},{6,4},{7,3},{8,10},{9,13},{10,... | collective-permute-start | bytes 1769480 | tf_op jit(solution)/shard_map/ppermute | solution.py:353
  7.4 8.1 %collective-permute-start.2 = (f32[12,128]{1,0:T(8,128)S(1)}, f32[12,128]{1,0:T(8,128)S(1)}, u32[]{:S(2)}, u32[]{:S(2)}) collective-permute-start(f32[12,128]{1,0:T(8,128)S(1)} %get-tuple-element.19), channel_id=1, source_target_pairs={{0,2},{2,0},{4,6},{6,4},{1,3},{3,1},{5,7},{7,5},{8,10},{10,8},{12,... | collective-permute-start | bytes 18440 | tf_op jit(solution)/shard_map/ppermute | solution.py:261
  7.5 8.7 %collective-permute-start.3 = (f32[12,128]{1,0:T(8,128)S(1)}, f32[12,128]{1,0:T(8,128)S(1)}, u32[]{:S(2)}, u32[]{:S(2)}) collective-permute-start(f32[12,128]{1,0:T(8,128)S(1)} %get-tuple-element.19), channel_id=1, source_target_pairs={{0,4},{2,6},{4,0},{6,2},{1,5},{3,7},{5,1},{7,3},{8,12},{10,14},{12... | collective-permute-start | bytes 18440 | tf_op jit(solution)/shard_map/ppermute | solution.py:261
  9.4 7.6 %collective-permute-start.4 = (f32[12,128]{1,0:T(8,128)S(1)}, f32[12,128]{1,0:T(8,128)S(1)}, u32[]{:S(2)}, u32[]{:S(2)}) collective-permute-start(f32[12,128]{1,0:T(8,128)S(1)} %get-tuple-element.19), channel_id=1, source_target_pairs={{0,6},{2,4},{4,2},{6,0},{1,7},{3,5},{5,3},{7,1},{8,14},{10,12},{12... | collective-permute-start | bytes 18440 | tf_op jit(solution)/shard_map/ppermute | solution.py:261
  10.9 9.8 %collective-permute-start = (bf16[256,768]{1,0:T(8,128)(2,1)S(1)}, bf16[256,768]{1,0:T(8,128)(2,1)S(1)}, u32[]{:S(2)}, u32[]{:S(2)}) collective-permute-start(bf16[256,768]{1,0:T(8,128)(2,1)S(1)} %copy-done.3), channel_id=1, source_target_pairs={{0,8},{8,0},{16,24},{24,16},{1,9},{9,1},{17,25},{25,17},{2,10},{10... | collective-permute-start | bytes 1179656 | tf_op jit(solution)/shard_map/ppermute | solution.py:261
  15.5 5.1 %collective-permute-start.1 = (bf16[256,768]{1,0:T(8,128)(2,1)S(1)}, bf16[256,768]{1,0:T(8,128)(2,1)S(1)}, u32[]{:S(2)}, u32[]{:S(2)}) collective-permute-start(bf16[256,768]{1,0:T(8,128)(2,1)S(1)} %copy-done.3), channel_id=1, source_target_pairs={{8,16},{16,8},{9,17},{17,9},{10,18},{18,10},{11,19},{19,11},{12,20... | collective-permute-start | bytes 1179656 | tf_op jit(solution)/shard_map/ppermute | solution.py:270
  17.0 2.1 %copy-start.6 = (s32[1,2048]{1,0:T(1,128)S(1)}, s32[1,2048]{1,0:T(1,128)}, u32[]{:S(2)}) copy-start(s32[1,2048]{1,0:T(1,128)} %param.11) | copy-start | bytes 24580
  17.0 2.1 %copy-start.7 = (s32[256]{0:T(256)S(1)}, s32[256]{0:T(256)}, u32[]{:S(2)}) copy-start(s32[256]{0:T(256)} %param.13) | copy-start | bytes 3076
  17.0 15.6 %collective-permute-start.12 = (bf16[384,768]{1,0:T(8,128)(2,1)S(1)}, bf16[384,768]{1,0:T(8,128)(2,1)S(1)}, u32[]{:S(2)}, u32[]{:S(2)}) collective-permute-start(bf16[384,768]{1,0:T(8,128)(2,1)S(1)} %collective-permute-done.8.refs_2_.refs_7_.refs_8_), channel_id=1, source_target_pairs={{0,4},{1,3},{2,6},{3,1},{4,0},{5,7},{6,2},{7,5},{8,12},{9,11},{10,... | collective-permute-start | bytes 1769480 | tf_op jit(solution)/shard_map/ppermute | solution.py:356
  18.3 15.0 %collective-permute-start.10 = (bf16[384,768]{1,0:T(8,128)(2,1)S(1)}, bf16[384,768]{1,0:T(8,128)(2,1)S(1)}, u32[]{:S(2)}, u32[]{:S(2)}) collective-permute-start(bf16[384,768]{1,0:T(8,128)(2,1)S(1)} %get-tuple-element.26), channel_id=1, source_target_pairs={{0,4},{1,3},{2,6},{3,1},{4,0},{5,7},{6,2},{7,5},{8,12},{9,11},{10,... | collective-permute-start | bytes 1769480 | tf_op jit(solution)/shard_map/ppermute | solution.py:355
  20.6 9.9 %collective-permute-start.5 = (f32[3328]{0:T(1024)S(1)}, f32[3328]{0:T(1024)S(1)}, u32[]{:S(2)}, u32[]{:S(2)}) collective-permute-start(f32[3328]{0:T(1024)S(1)} %pad_maximum_fusion.5), channel_id=1, source_target_pairs={{0,8},{8,0},{16,24},{24,16},{1,9},{9,1},{17,25},{25,17},{2,10},{10... | collective-permute-start | bytes 39944 | tf_op jit(solution)/shard_map/ppermute | solution.py:261
  28.0 4.6 %collective-permute-start.6 = (f32[3328]{0:T(1024)S(1)}, f32[3328]{0:T(1024)S(1)}, u32[]{:S(2)}, u32[]{:S(2)}) collective-permute-start(f32[3328]{0:T(1024)S(1)} %pad_maximum_fusion.5), channel_id=1, source_target_pairs={{0,16},{8,24},{16,0},{24,8},{1,17},{9,25},{17,1},{25,9},{2,18},{10... | collective-permute-start | bytes 39944 | tf_op jit(solution)/shard_map/ppermute | solution.py:261
  29.0 5.5 %collective-permute-start.7 = (f32[3328]{0:T(1024)S(1)}, f32[3328]{0:T(1024)S(1)}, u32[]{:S(2)}, u32[]{:S(2)}) collective-permute-start(f32[3328]{0:T(1024)S(1)} %pad_maximum_fusion.5), channel_id=1, source_target_pairs={{0,24},{8,16},{16,8},{24,0},{1,25},{9,17},{17,9},{25,1},{2,26},{10... | collective-permute-start | bytes 39944 | tf_op jit(solution)/shard_map/ppermute | solution.py:261
  30.5 9.4 %collective-permute-start.17 = (bf16[256,768]{1,0:T(8,128)(2,1)S(1)}, bf16[256,768]{1,0:T(8,128)(2,1)S(1)}, u32[]{:S(2)}, u32[]{:S(2)}) collective-permute-start(bf16[256,768]{1,0:T(8,128)(2,1)S(1)} %collective-permute-done.refs_0_), channel_id=1, source_target_pairs={{8,16},{16,8},{9,17},{17,9},{10,18},{18,10},{11,19},{19,11},{12,20... | collective-permute-start | bytes 1179656 | tf_op jit(solution)/shard_map/ppermute | solution.py:272
  32.6 8.8 %collective-permute-start.9 = (bf16[384,768]{1,0:T(8,128)(2,1)S(1)}, bf16[384,768]{1,0:T(8,128)(2,1)S(1)}, u32[]{:S(2)}, u32[]{:S(2)}) collective-permute-start(bf16[384,768]{1,0:T(8,128)(2,1)S(1)} %collective-permute-done.8.refs_2_.refs_7_.refs_8_), channel_id=1, source_target_pairs={{0,1},{1,0},{2,3},{3,2},{4,5},{5,4},{6,7},{7,6},{8,9},{9,8},{10,11... | collective-permute-start | bytes 1769480 | tf_op jit(solution)/shard_map/ppermute | solution.py:261
  32.6 8.8 %collective-permute-start.13 = (bf16[384,768]{1,0:T(8,128)(2,1)S(1)}, bf16[384,768]{1,0:T(8,128)(2,1)S(1)}, u32[]{:S(2)}, u32[]{:S(2)}) collective-permute-start(bf16[384,768]{1,0:T(8,128)(2,1)S(1)} %collective-permute-done.12.refs_6_.refs_11_.refs_12_), channel_id=1, source_target_pairs={{0,1},{1,0},{2,3},{3,2},{4,5},{5,4},{6,7},{7,6},{8,9},{9,8},{10,11... | collective-permute-start | bytes 1769480 | tf_op jit(solution)/shard_map/ppermute | solution.py:261
  33.3 8.1 %collective-permute-start.11 = (bf16[384,768]{1,0:T(8,128)(2,1)S(1)}, bf16[384,768]{1,0:T(8,128)(2,1)S(1)}, u32[]{:S(2)}, u32[]{:S(2)}) collective-permute-start(bf16[384,768]{1,0:T(8,128)(2,1)S(1)} %collective-permute-done.10.refs_4_.refs_9_.refs_10_), channel_id=1, source_target_pairs={{0,1},{1,0},{2,3},{3,2},{4,5},{5,4},{6,7},{7,6},{8,9},{9,8},{10,11... | collective-permute-start | bytes 1769480 | tf_op jit(solution)/shard_map/ppermute | solution.py:261
  34.5 14.2 %collective-permute-start.21 = (bf16[256,768]{1,0:T(8,128)(2,1)S(1)}, bf16[256,768]{1,0:T(8,128)(2,1)S(1)}, u32[]{:S(2)}, u32[]{:S(2)}) collective-permute-start(bf16[256,768]{1,0:T(8,128)(2,1)S(1)} %collective-permute-done.1.refs_1_), channel_id=1, source_target_pairs={{8,0},{16,24},{9,1},{17,25},{10,2},{18,26},{11,3},{19,27},{12,4},{... | collective-permute-start | bytes 1179656 | tf_op jit(solution)/shard_map/ppermute | solution.py:273
  39.9 23.5 %collective-permute-start.18 = (bf16[256,768]{1,0:T(8,128)(2,1)S(1)}, bf16[256,768]{1,0:T(8,128)(2,1)S(1)}, u32[]{:S(2)}, u32[]{:S(2)}) collective-permute-start(bf16[256,768]{1,0:T(8,128)(2,1)S(1)} %collective-permute-done.17.refs_1_), channel_id=1, source_target_pairs={{8,0},{16,24},{9,1},{17,25},{10,2},{18,26},{11,3},{19,27},{12,4},{... | collective-permute-start | bytes 1179656 | tf_op jit(solution)/shard_map/ppermute | solution.py:274
  42.7 20.7 %collective-permute-start.14 = (bf16[64,768]{1,0:T(8,128)(2,1)S(1)}, bf16[64,768]{1,0:T(8,128)(2,1)S(1)}, u32[]{:S(2)}, u32[]{:S(2)}) collective-permute-start(bf16[64,768]{1,0:T(8,128)(2,1)S(1)} %get-tuple-element.35), channel_id=1, source_target_pairs={{0,8},{8,0},{16,24},{24,16},{1,9},{9,1},{17,25},{25,17},{2,10},{10... | collective-permute-start | bytes 294920 | tf_op jit(solution)/shard_map/ppermute | solution.py:261
  45.8 17.6 %collective-permute-start.15 = (bf16[64,768]{1,0:T(8,128)(2,1)S(1)}, bf16[64,768]{1,0:T(8,128)(2,1)S(1)}, u32[]{:S(2)}, u32[]{:S(2)}) collective-permute-start(bf16[64,768]{1,0:T(8,128)(2,1)S(1)} %get-tuple-element.37), channel_id=1, source_target_pairs={{0,16},{8,24},{16,0},{24,8},{1,17},{9,25},{17,1},{25,9},{2,18},{10... | collective-permute-start | bytes 294920 | tf_op jit(solution)/shard_map/ppermute | solution.py:261
  46.5 16.9 %collective-permute-start.16 = (bf16[64,768]{1,0:T(8,128)(2,1)S(1)}, bf16[64,768]{1,0:T(8,128)(2,1)S(1)}, u32[]{:S(2)}, u32[]{:S(2)}) collective-permute-start(bf16[64,768]{1,0:T(8,128)(2,1)S(1)} %get-tuple-element.36), channel_id=1, source_target_pairs={{0,24},{8,16},{16,8},{24,0},{1,25},{9,17},{17,9},{25,1},{2,26},{10... | collective-permute-start | bytes 294920 | tf_op jit(solution)/shard_map/ppermute | solution.py:261
  51.0 18.9 %collective-permute-start.22 = (f32[2,2,128]{2,1,0:T(2,128)S(1)}, f32[2,2,128]{2,1,0:T(2,128)S(1)}, u32[]{:S(2)}, u32[]{:S(2)}) collective-permute-start(f32[2,2,128]{2,1,0:T(2,128)S(1)} %score.5), channel_id=1, source_target_pairs={{0,16},{8,24},{16,0},{24,8},{1,17},{9,25},{17,1},{25,9},{2,18},{10... | collective-permute-start | bytes 6152 | tf_op jit(solution)/shard_map/ppermute | solution.py:261
  63.4 6.5 %collective-permute-start.20 = (f32[2,2,128]{2,1,0:T(2,128)S(1)}, f32[2,2,128]{2,1,0:T(2,128)S(1)}, u32[]{:S(2)}, u32[]{:S(2)}) collective-permute-start(f32[2,2,128]{2,1,0:T(2,128)S(1)} %score.4), channel_id=1, source_target_pairs={{0,8},{8,0},{16,24},{24,16},{1,9},{9,1},{17,25},{25,17},{2,10},{10... | collective-permute-start | bytes 6152 | tf_op jit(solution)/shard_map/ppermute | solution.py:261
  65.7 5.4 %collective-permute-start.23 = (f32[2,2,128]{2,1,0:T(2,128)S(1)}, f32[2,2,128]{2,1,0:T(2,128)S(1)}, u32[]{:S(2)}, u32[]{:S(2)}) collective-permute-start(f32[2,2,128]{2,1,0:T(2,128)S(1)} %score.6), channel_id=1, source_target_pairs={{0,24},{8,16},{16,8},{24,0},{1,25},{9,17},{17,9},{25,1},{2,26},{10... | collective-permute-start | bytes 6152 | tf_op jit(solution)/shard_map/ppermute | solution.py:261
  69.8 1.9 %collective-permute-start.19 = (bf16[192,768]{1,0:T(8,128)(2,1)S(1)}, bf16[192,768]{1,0:T(8,128)(2,1)S(1)}, u32[]{:S(2)}, u32[]{:S(2)}) collective-permute-start(bf16[192,768]{1,0:T(8,128)(2,1)S(1)} %pad_maximum_fusion.refs_1_), channel_id=1, source_target_pairs={{0,1},{1,0},{2,3},{3,2},{4,5},{5,4},{6,7},{7,6},{8,9},{9,8},{10,11... | collective-permute-start | bytes 884744 | tf_op jit(solution)/shard_map/ppermute | solution.py:261

commit v16 on v15

--- a/solution.py
+++ b/solution.py
@@ -268,7 +268,7 @@
     middle, outward = [(1, 2), (2, 1)], [(1, 0), (2, 3)]
     beside = swap(values, "outer", 1)
     across = lax.ppermute(values, "outer", middle)
-    beside, across, small = lax.optimization_barrier((beside, across, small))
+    beside, across, *small = lax.optimization_barrier((beside, across, *small))
     from_end = lax.ppermute(beside, "outer", middle)
     to_end = lax.ppermute(across, "outer", outward)
     last = lax.ppermute(from_end, "outer", outward)
@@ -315,9 +315,10 @@
     ref_plane, log_weight_plane = piece(0), piece(1)
     scale_plane = jnp.concatenate([piece(2), piece(3)], axis=1)
     line = jnp.concatenate([ref_plane[0], neg_ids[0].astype(f32), pos_ids.astype(f32)])
-    got_queries, line = gather_line(queries, line)
+    lines = [line] + [swap(line, "outer", s) for s in range(1, planes)]
+    got_queries, lines = gather_line(queries, lines)
     got_queries = [(queries,)] + got_queries
-    lines = jnp.stack([line] + [swap(line, "outer", s) for s in range(1, planes)])
+    lines = jnp.stack(lines)
     ref_all = lines[:, :plane_refresh].astype(jnp.int32)
     neg_line = lines[:, plane_refresh : plane_refresh + list_size].astype(jnp.int32)
     positive = lines[:, plane_refresh + list_size :].reshape(planes, -1, LANES)
@@ -386,17 +387,15 @@
         *buffers,
         pieces=fresh_pieces,
     )
+    packed, row_ids = lax.optimization_barrier((packed, row_ids))
     parts = []
     for s in range(1, planes):
         first = own_slots + (s - 1) * part_slots
         parts.append(swap(packed[first : first + part_slots], "outer", s))
-    parts, *given = lax.optimization_barrier((jnp.concatenate(parts), *got_queries[-1]))
-    got_queries[-1] = tuple(given)
-    arrived = [packed[:own_slots], parts] + [swap(parts, "query", flip) for flip in range(1, replicas)]
-
+    parts = jnp.concatenate(parts)
     pieces = table_pieces + shift(fresh_pieces, plane_rows)
-    mine = None
-    for s in [*range(1, planes), 0]:
+
+    def score(s):
         (partial,) = call(
             score_kernel,
             "score",
@@ -412,9 +411,15 @@
             pieces=pieces,
             sources=len(got_queries[s]),
         )
-        if s:
-            partial = swap(partial, "outer", s)
-        mine = partial if mine is None else mine + partial
+        return partial
+
+    mine = score(0)
+    for s in range(1, planes - 1):
+        mine = mine + swap(score(s), "outer", s)
+    parts, own_part, *given = lax.optimization_barrier((parts, mine, *got_queries[-1]))
+    mine, got_queries[-1] = own_part, tuple(given)
+    arrived = [packed[:own_slots], parts] + [swap(parts, "query", flip) for flip in range(1, replicas)]
+    mine = mine + swap(score(planes - 1), "outer", planes - 1)
     (new_table,) = call(
         apply_kernel, "apply", [jax.ShapeDtypeStruct(table.shape, bf16)], None, target, own, table, *arrived
     )

time: 73.4 us -> 73.6 us (level)
  waiting for transfers between devices: 18.6 us -> 21.5 us
  starting transfers between devices: 33.5 us -> 30.7 us
    ppermute x17, waiting for transfers between devices: 17.9 us -> 10.7 us  [swap(): lax.ppermute(values, axis, [(i, i ^ flip) for i in range(lax.axis_size(ax...]
    ppermute x1, waiting for transfers between devices: 0.17 us -> 6.32 us  [on_device(): side = lax.ppermute(rows_half, axes, second)]
    ppermute x1, waiting for transfers between devices: 0.01 us -> 3.82 us  [on_device(): near = lax.ppermute(rows_half, axes, first)]
    ppermute x1, starting transfers between devices: 3 us -> 1.56 us  [on_device(): near = lax.ppermute(rows_half, axes, first)]
    ppermute x17, starting transfers between devices: 24.3 us -> 23 us  [swap(): lax.ppermute(values, axis, [(i, i ^ flip) for i in range(lax.axis_size(ax...]
  transfers between devices with their start and end apart: 24 -> 24, of which waited for: 9 -> 8; matrix products, arithmetic and copies ran while one was open for 1% -> 1% of each run, Pallas kernels for 19% -> 19%
where the time goes in v16:
time: 73.6 us; the launch traced here: 73.3 us
  starting transfers between devices  30.7 us (42%)
  waiting for transfers between devices  21.5 us (29%)
  Pallas kernels  16.4 us (22%)
  local copies, waits for them, and re-layouts  2.97 us (4%)
  between operations  0.92 us (1%)
  other arithmetic  0.78 us (1%)
    ppermute x17, starting transfers between devices, swap(): lax.ppermute(values, axis, [(i, i ^ flip) for i in range(lax.axis_size(ax...  23 us
    pallas_call x8, Pallas kernels, call(): pl.pallas_call(functools.partial(kernel, **options), out_shape=tuple(outs...  16.4 us
    ppermute x17, waiting for transfers between devices, swap(): lax.ppermute(values, axis, [(i, i ^ flip) for i in range(lax.axis_size(ax...  10.7 us
    ppermute x1, waiting for transfers between devices, on_device(): side = lax.ppermute(rows_half, axes, second)  6.32 us
    ppermute x1, waiting for transfers between devices, on_device(): near = lax.ppermute(rows_half, axes, first)  3.82 us
    unnamed x16, local copies, waits for them, and re-layouts  2.84 us
    ppermute x1, starting transfers between devices, on_device(): near = lax.ppermute(rows_half, axes, first)  1.56 us
    ppermute x1, starting transfers between devices, on_device(): far = lax.ppermute(near, axes, second)  1.52 us
  transfers between devices with their start and end apart: 24, of which 8 were waited for; matrix products, arithmetic and copies ran while one was open for 1% of the time, Pallas kernels for 19%

profile of v16, /device:TPU:0, one launch (start us, length us, event | category | flops | bytes accessed | tf_op | source)
XLA Modules:
  0.0 73.3 jit_solution(7715542292553036166)
XLA Ops:
  0.6 0.1 pad_add_fusion.place
  0.7 0.7 copy-done.4
  1.4 0.0 copy-done.5
  1.4 1.1 %copy-done = bf16[512,768]{1,0:T(8,128)(2,1)S(1)} copy-done((bf16[512,768]{1,0:T(8,128)(2,1)S(1)}, bf16[512,768]{1,0:T(8,128)(2,1)}, u32[]{:S(2)}) %copy-start) | copy-done | bytes 786456
  2.6 1.0 %copy-done.2 = bf16[256,768]{1,0:T(8,128)(2,1)S(1)} copy-done((bf16[256,768]{1,0:T(8,128)(2,1)S(1)}, bf16[256,768]{1,0:T(8,128)(2,1)}, u32[]{:S(2)}) %copy-start.2) | copy-done | bytes 393240
  3.6 0.8 %prep.1 = (bf16[384,768]{1,0:T(8,128)(2,1)S(1)}, f32[12,128]{1,0:T(8,128)S(1)}) custom-call(s32[3]{0:T(128)S(1)} %pad_add_fusion.place, bf16[512,768]{1,0:T(8,128)(2,1)S(1)} %copy-done, bf16[256,768]{1,0:T(8,128)(2,1)S(1)} %copy-done.2, s32[4,128]{1,0:T(4,128)S(1)} %bitcast.23, s32[2,128]{1,0:T(2,128)S(1)} %bitcast.30), custom_call_target="tpu_custom_call" | custom-call | flops 1 | bytes 1 | tf_op jit(solution)/shard_map/prep/pallas_call | solution.py:248
  4.4 3.0 %collective-permute-start.2 = (f32[12,128]{1,0:T(8,128)S(1)}, f32[12,128]{1,0:T(8,128)S(1)}, u32[]{:S(2)}, u32[]{:S(2)}) collective-permute-start(f32[12,128]{1,0:T(8,128)S(1)} %get-tuple-element.25), channel_id=1, source_target_pairs={{0,2},{2,0},{4,6},{6,4},{1,3},{3,1},{5,7},{7,5},{8,10},{10,8},{12,... | collective-permute-start | bytes 18440 | tf_op jit(solution)/shard_map/ppermute | solution.py:261
  7.4 1.5 %collective-permute-start.3 = (f32[12,128]{1,0:T(8,128)S(1)}, f32[12,128]{1,0:T(8,128)S(1)}, u32[]{:S(2)}, u32[]{:S(2)}) collective-permute-start(f32[12,128]{1,0:T(8,128)S(1)} %get-tuple-element.25), channel_id=1, source_target_pairs={{0,4},{2,6},{4,0},{6,2},{1,5},{3,7},{5,1},{7,3},{8,12},{10,14},{12... | collective-permute-start | bytes 18440 | tf_op jit(solution)/shard_map/ppermute | solution.py:261
  8.9 0.0 collective-permute-start.4
  9.0 0.0 copy-done.3
  9.0 2.0 %collective-permute-start = (bf16[256,768]{1,0:T(8,128)(2,1)S(1)}, bf16[256,768]{1,0:T(8,128)(2,1)S(1)}, u32[]{:S(2)}, u32[]{:S(2)}) collective-permute-start(bf16[256,768]{1,0:T(8,128)(2,1)S(1)} %copy-done.3), channel_id=1, source_target_pairs={{0,8},{8,0},{16,24},{24,16},{1,9},{9,1},{17,25},{25,17},{2,10},{10... | collective-permute-start | bytes 1179656 | tf_op jit(solution)/shard_map/ppermute | solution.py:261
  11.0 0.7 collective-permute-start.1
  11.7 0.0 copy-done.7
  11.7 0.0 collective-permute-done.2
  11.7 1.6 %collective-permute-start.8 = (bf16[384,768]{1,0:T(8,128)(2,1)S(1)}, bf16[384,768]{1,0:T(8,128)(2,1)S(1)}, u32[]{:S(2)}, u32[]{:S(2)}) collective-permute-start(bf16[384,768]{1,0:T(8,128)(2,1)S(1)} %get-tuple-element.35), channel_id=1, source_target_pairs={{0,2},{1,5},{2,0},{3,7},{4,6},{5,1},{6,4},{7,3},{8,10},{9,13},{10,... | collective-permute-start | bytes 1769480 | tf_op jit(solution)/shard_map/ppermute | solution.py:354
  13.3 0.0 collective-permute-done.3
  13.3 0.3 collective-permute-done.4
  13.6 4.2 %collective-permute-start.5 = (f32[3328]{0:T(1024)S(1)}, f32[3328]{0:T(1024)S(1)}, u32[]{:S(2)}, u32[]{:S(2)}) collective-permute-start(f32[3328]{0:T(1024)S(1)} %pad_maximum_fusion.5), channel_id=1, source_target_pairs={{0,8},{8,0},{16,24},{24,16},{1,9},{9,1},{17,25},{25,17},{2,10},{10... | collective-permute-start | bytes 39944 | tf_op jit(solution)/shard_map/ppermute | solution.py:261
  17.8 0.1 collective-permute-start.6
  17.9 3.8 %collective-permute-done.8.refs_2_.refs_7_.refs_8_ = bf16[384,768]{1,0:T(8,128)(2,1)S(1)} collective-permute-done((bf16[384,768]{1,0:T(8,128)(2,1)S(1)}, bf16[384,768]{1,0:T(8,128)(2,1)S(1)}, u32[]{:S(2)}, u32[]{:S(2)}) %collective-permute-start.8) | collective-permute-done | bytes 589856 | tf_op jit(solution)/shard_map/ppermute | solution.py:354
  21.7 2.5 %collective-permute-start.7 = (f32[3328]{0:T(1024)S(1)}, f32[3328]{0:T(1024)S(1)}, u32[]{:S(2)}, u32[]{:S(2)}) collective-permute-start(f32[3328]{0:T(1024)S(1)} %pad_maximum_fusion.5), channel_id=1, source_target_pairs={{0,24},{8,16},{16,8},{24,0},{1,25},{9,17},{17,9},{25,1},{2,26},{10... | collective-permute-start | bytes 39944 | tf_op jit(solution)/shard_map/ppermute | solution.py:261
  24.2 0.0 collective-permute-done.5
  24.2 1.5 %collective-permute-start.12 = (bf16[384,768]{1,0:T(8,128)(2,1)S(1)}, bf16[384,768]{1,0:T(8,128)(2,1)S(1)}, u32[]{:S(2)}, u32[]{:S(2)}) collective-permute-start(bf16[384,768]{1,0:T(8,128)(2,1)S(1)} %collective-permute-done.8.refs_2_.refs_7_.refs_8_), channel_id=1, source_target_pairs={{0,4},{1,3},{2,6},{3,1},{4,0},{5,7},{6,2},{7,5},{8,12},{9,11},{10,... | collective-permute-start | bytes 1769480 | tf_op jit(solution)/shard_map/ppermute | solution.py:357
  25.7 0.0 collective-permute-done.6
  25.7 0.5 collective-permute-start.10
  26.2 1.0 %collective-permute-done.7 = f32[3328]{0:T(1024)S(1)} collective-permute-done((f32[3328]{0:T(1024)S(1)}, f32[3328]{0:T(1024)S(1)}, u32[]{:S(2)}, u32[]{:S(2)}) %collective-permute-start.7) | collective-permute-done | bytes 13344 | tf_op jit(solution)/shard_map/ppermute | solution.py:261
  27.2 0.0 collective-permute-done.refs_0_
  27.2 0.0 collective-permute-done.1.refs_1_
  27.3 1.3 %collective-permute-start.18 = (bf16[256,768]{1,0:T(8,128)(2,1)S(1)}, bf16[256,768]{1,0:T(8,128)(2,1)S(1)}, u32[]{:S(2)}, u32[]{:S(2)}) collective-permute-start(bf16[256,768]{1,0:T(8,128)(2,1)S(1)} %collective-permute-done.1.refs_1_), channel_id=1, source_target_pairs={{8,0},{16,24},{9,1},{17,25},{10,2},{18,26},{11,3},{19,27},{12,4},{... | collective-permute-start | bytes 1179656 | tf_op jit(solution)/shard_map/ppermute | solution.py:273
  28.6 0.7 collective-permute-start.19
  29.4 4.0 %meta.1 = (f32[4,3072]{1,0:T(4,128)S(1)}, f32[1,3072]{1,0:T(1,128)S(1)}, s32[1,1024]{1,0:T(1,128)S(1)}, s32[1,512]{1,0:T(1,128)S(1)}, s32[1,512]{1,0:T(1,128)S(1)}, /*index=5*/s32[1,512]{1,0:T(1,128)}) custom-call(s32[3]{0:T(128)S(1)} %pad_add_fusion.place, s32[4,1024]{1,0:T(4,128)S(1)} %maximum_convert_fusion.ref_ids, s32[4,2048]{1,0:T(4,128)S(1)} %fusion.neg, ...), custom_call_target="tpu_custom_call" | custom-call | flops 1 | bytes 1 | tf_op jit(solution)/shard_map/meta/pallas_call | solution.py:248
  33.4 0.1 collective-permute-start.9
  33.4 0.6 collective-permute-done.12.refs_6_.refs_11_.refs_12_
  34.0 0.0 collective-permute-start.13
  34.0 6.3 %collective-permute-done.10.refs_4_.refs_9_.refs_10_ = bf16[384,768]{1,0:T(8,128)(2,1)S(1)} collective-permute-done((bf16[384,768]{1,0:T(8,128)(2,1)S(1)}, bf16[384,768]{1,0:T(8,128)(2,1)S(1)}, u32[]{:S(2)}, u32[]{:S(2)}) %collective-permute-start.10) | collective-permute-done | bytes 589856 | tf_op jit(solution)/shard_map/ppermute | solution.py:356
  40.4 0.0 collective-permute-start.11
  40.4 0.0 collective-permute-done.19.refs_1_
  40.4 1.5 %collective-permute-start.21 = (bf16[256,768]{1,0:T(8,128)(2,1)S(1)}, bf16[256,768]{1,0:T(8,128)(2,1)S(1)}, u32[]{:S(2)}, u32[]{:S(2)}) collective-permute-start(bf16[256,768]{1,0:T(8,128)(2,1)S(1)} %collective-permute-done.19.refs_1_), channel_id=1, source_target_pairs={{8,0},{16,24},{9,1},{17,25},{10,2},{18,26},{11,3},{19,27},{12,4},{... | collective-permute-start | bytes 1179656 | tf_op jit(solution)/shard_map/ppermute | solution.py:274
  41.9 0.0 collective-permute-done.9.refs_3_.refs_8_.refs_9_
  41.9 0.0 collective-permute-done.13.refs_7_.refs_12_.refs_13_
  41.9 0.4 collective-permute-done.11.refs_5_.refs_10_.refs_11_
  42.4 1.2 %pack.1 = bf16[320,768]{1,0:T(8,128)(2,1)S(1)} custom-call(s32[3]{0:T(128)S(1)} %pad_add_fusion.place, s32[1,1024]{1,0:T(1,128)S(1)} %get-tuple-element.32.code, bf16[512,768]{1,0:T(8,128)(2,1)S(1)} %copy-done.1, bf16[256,768]{1,0:T(8,128)(2,1)S(1)} %copy-done.2, bf16[384,768]{1,0:T(8,128)(2,1)S(1)} %collective-permute-done.8.refs_2_.refs_7_.refs_8_, ...), custom_call_target="tpu_custom_call" | custom-call | flops 1 | bytes 1 | tf_op jit(solution)/shard_map/pack/pallas_call | solution.py:248
  43.6 2.2 %score.5 = f32[2,2,128]{2,1,0:T(2,128)S(1)} custom-call(s32[3]{0:T(128)S(1)} %pad_add_fusion.place, bf16[256,768]{1,0:T(8,128)(2,1)S(1)} %collective-permute-done.refs_0_, f32[2,128]{1,0:T(2,128)S(1)} %bitcast.28, f32[1,3072]{1,0:T(1,128)S(1)} %get-tuple-element.52.refs_2_, f32[1,3072]{1,0:T(1,128)S(1)} %get-tuple-element.39.refs_3_.refs_4_, ...), custom_call_target="tpu_custom_call" | custom-call | flops 1 | bytes 1 | tf_op jit(solution)/shard_map/score/pallas_call | solution.py:248
  45.8 2.3 %collective-permute-start.17 = (f32[2,2,128]{2,1,0:T(2,128)S(1)}, f32[2,2,128]{2,1,0:T(2,128)S(1)}, u32[]{:S(2)}, u32[]{:S(2)}) collective-permute-start(f32[2,2,128]{2,1,0:T(2,128)S(1)} %score.5), channel_id=1, source_target_pairs={{0,8},{8,0},{16,24},{24,16},{1,9},{9,1},{17,25},{25,17},{2,10},{10... | collective-permute-start | bytes 6152 | tf_op jit(solution)/shard_map/ppermute | solution.py:261
  48.1 0.0 collective-permute-done.18.refs_0_
  48.1 2.2 %score.6 = f32[2,2,128]{2,1,0:T(2,128)S(1)} custom-call(s32[3]{0:T(128)S(1)} %pad_add_fusion.place, bf16[256,768]{1,0:T(8,128)(2,1)S(1)} %collective-permute-done.18.refs_0_, bf16[256,768]{1,0:T(8,128)(2,1)S(1)} %collective-permute-done.19.refs_1_, f32[2,128]{1,0:T(2,128)S(1)} %bitcast.27, f32[1,3072]{1,0:T(1,128)S(1)} %get-tuple-element.51.refs_3_, ...), custom_call_target="tpu_custom_call" | custom-call | flops 1 | bytes 1 | tf_op jit(solution)/shard_map/score/pallas_call | solution.py:248
  50.4 1.2 %collective-permute-start.20 = (f32[2,2,128]{2,1,0:T(2,128)S(1)}, f32[2,2,128]{2,1,0:T(2,128)S(1)}, u32[]{:S(2)}, u32[]{:S(2)}) collective-permute-start(f32[2,2,128]{2,1,0:T(2,128)S(1)} %score.6), channel_id=1, source_target_pairs={{0,16},{8,24},{16,0},{24,8},{1,17},{9,25},{17,1},{25,9},{2,18},{10... | collective-permute-start | bytes 6152 | tf_op jit(solution)/shard_map/ppermute | solution.py:261
  51.6 2.1 %collective-permute-start.14 = (bf16[64,768]{1,0:T(8,128)(2,1)S(1)}, bf16[64,768]{1,0:T(8,128)(2,1)S(1)}, u32[]{:S(2)}, u32[]{:S(2)}) collective-permute-start(bf16[64,768]{1,0:T(8,128)(2,1)S(1)} %get-tuple-element.47), channel_id=1, source_target_pairs={{0,8},{8,0},{16,24},{24,16},{1,9},{9,1},{17,25},{25,17},{2,10},{10... | collective-permute-start | bytes 294920 | tf_op jit(solution)/shard_map/ppermute | solution.py:261
  53.7 0.0 collective-permute-start.15
  53.7 2.2 %score.4 = f32[2,2,128]{2,1,0:T(2,128)S(1)} custom-call(s32[3]{0:T(128)S(1)} %pad_add_fusion.place, bf16[256,768]{1,0:T(8,128)(2,1)S(1)} %copy-done.3, f32[2,128]{1,0:T(2,128)S(1)} %bitcast.26, f32[1,3072]{1,0:T(1,128)S(1)} %get-tuple-element.53.refs_2_, f32[1,3072]{1,0:T(1,128)S(1)} %get-tuple-element.39.refs_3_.refs_4_, ...), custom_call_target="tpu_custom_call" | custom-call | flops 1 | bytes 1 | tf_op jit(solution)/shard_map/score/pallas_call | solution.py:248
  55.9 0.0 collective-permute-done.17
  55.9 2.5 %collective-permute-start.16 = (bf16[64,768]{1,0:T(8,128)(2,1)S(1)}, bf16[64,768]{1,0:T(8,128)(2,1)S(1)}, u32[]{:S(2)}, u32[]{:S(2)}) collective-permute-start(bf16[64,768]{1,0:T(8,128)(2,1)S(1)} %get-tuple-element.48), channel_id=1, source_target_pairs={{0,24},{8,16},{16,8},{24,0},{1,25},{9,17},{17,9},{25,1},{2,26},{10... | collective-permute-start | bytes 294920 | tf_op jit(solution)/shard_map/ppermute | solution.py:261
  58.4 0.0 collective-permute-done.20
  58.4 0.0 collective-permute-done.14
  58.4 5.0 %collective-permute-done.15 = bf16[64,768]{1,0:T(8,128)(2,1)S(1)} collective-permute-done((bf16[64,768]{1,0:T(8,128)(2,1)S(1)}, bf16[64,768]{1,0:T(8,128)(2,1)S(1)}, u32[]{:S(2)}, u32[]{:S(2)}) %collective-permute-start.15) | collective-permute-done | bytes 98336 | tf_op jit(solution)/shard_map/ppermute | solution.py:261
  63.5 0.0 collective-permute-done.16
  63.5 0.0 collective-permute-done.21.refs_0_
  63.5 0.1 collective-permute-start.22
  63.6 2.2 %score.7 = f32[2,2,128]{2,1,0:T(2,128)S(1)} custom-call(s32[3]{0:T(128)S(1)} %pad_add_fusion.place, bf16[256,768]{1,0:T(8,128)(2,1)S(1)} %collective-permute-done.21.refs_0_, bf16[256,768]{1,0:T(8,128)(2,1)S(1)} %collective-permute-done.1.refs_1_, f32[2,128]{1,0:T(2,128)S(1)} %bitcast.29, f32[1,3072]{1,0:T(1,128)S(1)} %get-tuple-element.50.refs_3_, ...), custom_call_target="tpu_custom_call" | custom-call | flops 1 | bytes 1 | tf_op jit(solution)/shard_map/score/pallas_call | solution.py:248
  65.8 1.5 %collective-permute-start.23 = (f32[2,2,128]{2,1,0:T(2,128)S(1)}, f32[2,2,128]{2,1,0:T(2,128)S(1)}, u32[]{:S(2)}, u32[]{:S(2)}) collective-permute-start(f32[2,2,128]{2,1,0:T(2,128)S(1)} %score.7), channel_id=1, source_target_pairs={{0,24},{8,16},{16,8},{24,0},{1,25},{9,17},{17,9},{25,1},{2,26},{10... | collective-permute-start | bytes 6152 | tf_op jit(solution)/shard_map/ppermute | solution.py:261
  67.4 3.9 %collective-permute-done.23 = f32[2,2,128]{2,1,0:T(2,128)S(1)} collective-permute-done((f32[2,2,128]{2,1,0:T(2,128)S(1)}, f32[2,2,128]{2,1,0:T(2,128)S(1)}, u32[]{:S(2)}, u32[]{:S(2)}) %collective-permute-start.23) | collective-permute-done | bytes 2080 | tf_op jit(solution)/shard_map/ppermute | solution.py:261
  71.3 0.6 fusion.2
  71.9 0.0 collective-permute-done.22.refs_2_
  71.9 1.5 %apply.1 = bf16[512,768]{1,0:T(8,128)(2,1)} custom-call(s32[1,512]{1,0:T(1,128)S(1)} %get-tuple-element.30.target, s32[1,512]{1,0:T(1,128)S(1)} %get-tuple-element.31.refreshed, bf16[512,768]{1,0:T(8,128)(2,1)S(1)} %copy-done.1, bf16[128,768]{1,0:T(8,128)(2,1)S(1)} %slice.77.refs_0_, bf16[192,768]{1,0:T(8,128)(2,1)S(1)} %pad_maximum_fusion.refs_1_, ...), custom_call_target="tpu_custom_call" | custom-call | flops 1 | bytes 1 | tf_op jit(solution)/shard_map/apply/pallas_call | solution.py:248
  (33 shorter events, 0.3 us)
Async XLA Ops:
  0.6 11.0 %copy-start.6 = (s32[1,2048]{1,0:T(1,128)S(1)}, s32[1,2048]{1,0:T(1,128)}, u32[]{:S(2)}) copy-start(s32[1,2048]{1,0:T(1,128)} %param.11) | copy-start | bytes 24580
  0.7 0.7 copy-start.4
  0.7 0.7 copy-start.5
  1.4 1.1 %copy-start = (bf16[512,768]{1,0:T(8,128)(2,1)S(1)}, bf16[512,768]{1,0:T(8,128)(2,1)}, u32[]{:S(2)}) copy-start(bf16[512,768]{1,0:T(8,128)(2,1)} %refs_6_.7) | copy-start | bytes 2359300
  2.6 1.0 %copy-start.2 = (bf16[256,768]{1,0:T(8,128)(2,1)S(1)}, bf16[256,768]{1,0:T(8,128)(2,1)}, u32[]{:S(2)}) copy-start(bf16[256,768]{1,0:T(8,128)(2,1)} %refs_7_.3) | copy-start | bytes 1179652
  3.5 5.4 %copy-start.3 = (bf16[256,768]{1,0:T(8,128)(2,1)S(1)}, bf16[256,768]{1,0:T(8,128)(2,1)}, u32[]{:S(2)}) copy-start(bf16[256,768]{1,0:T(8,128)(2,1)} %refs_0_.3) | copy-start | bytes 1179652
  3.6 38.8 %copy-start.1 = (bf16[512,768]{1,0:T(8,128)(2,1)S(1)}, bf16[512,768]{1,0:T(8,128)(2,1)}, u32[]{:S(2)}) copy-start(bf16[512,768]{1,0:T(8,128)(2,1)} %refs_6_.7) | copy-start | bytes 2359300
  4.4 7.3 %copy-start.7 = (s32[256]{0:T(256)S(1)}, s32[256]{0:T(256)}, u32[]{:S(2)}) copy-start(s32[256]{0:T(256)} %param.13) | copy-start | bytes 3076
  4.4 7.3 %collective-permute-start.2 = (f32[12,128]{1,0:T(8,128)S(1)}, f32[12,128]{1,0:T(8,128)S(1)}, u32[]{:S(2)}, u32[]{:S(2)}) collective-permute-start(f32[12,128]{1,0:T(8,128)S(1)} %get-tuple-element.25), channel_id=1, source_target_pairs={{0,2},{2,0},{4,6},{6,4},{1,3},{3,1},{5,7},{7,5},{8,10},{10,8},{12,... | collective-permute-start | bytes 18440 | tf_op jit(solution)/shard_map/ppermute | solution.py:261
  7.4 5.9 %collective-permute-start.3 = (f32[12,128]{1,0:T(8,128)S(1)}, f32[12,128]{1,0:T(8,128)S(1)}, u32[]{:S(2)}, u32[]{:S(2)}) collective-permute-start(f32[12,128]{1,0:T(8,128)S(1)} %get-tuple-element.25), channel_id=1, source_target_pairs={{0,4},{2,6},{4,0},{6,2},{1,5},{3,7},{5,1},{7,3},{8,12},{10,14},{12... | collective-permute-start | bytes 18440 | tf_op jit(solution)/shard_map/ppermute | solution.py:261
  8.9 4.7 %collective-permute-start.4 = (f32[12,128]{1,0:T(8,128)S(1)}, f32[12,128]{1,0:T(8,128)S(1)}, u32[]{:S(2)}, u32[]{:S(2)}) collective-permute-start(f32[12,128]{1,0:T(8,128)S(1)} %get-tuple-element.25), channel_id=1, source_target_pairs={{0,6},{2,4},{4,2},{6,0},{1,7},{3,5},{5,3},{7,1},{8,14},{10,12},{12... | collective-permute-start | bytes 18440 | tf_op jit(solution)/shard_map/ppermute | solution.py:261
  9.0 18.3 %collective-permute-start = (bf16[256,768]{1,0:T(8,128)(2,1)S(1)}, bf16[256,768]{1,0:T(8,128)(2,1)S(1)}, u32[]{:S(2)}, u32[]{:S(2)}) collective-permute-start(bf16[256,768]{1,0:T(8,128)(2,1)S(1)} %copy-done.3), channel_id=1, source_target_pairs={{0,8},{8,0},{16,24},{24,16},{1,9},{9,1},{17,25},{25,17},{2,10},{10... | collective-permute-start | bytes 1179656 | tf_op jit(solution)/shard_map/ppermute | solution.py:261
  11.0 16.2 %collective-permute-start.1 = (bf16[256,768]{1,0:T(8,128)(2,1)S(1)}, bf16[256,768]{1,0:T(8,128)(2,1)S(1)}, u32[]{:S(2)}, u32[]{:S(2)}) collective-permute-start(bf16[256,768]{1,0:T(8,128)(2,1)S(1)} %copy-done.3), channel_id=1, source_target_pairs={{8,16},{16,8},{9,17},{17,9},{10,18},{18,10},{11,19},{19,11},{12,20... | collective-permute-start | bytes 1179656 | tf_op jit(solution)/shard_map/ppermute | solution.py:270
  11.7 9.9 %collective-permute-start.8 = (bf16[384,768]{1,0:T(8,128)(2,1)S(1)}, bf16[384,768]{1,0:T(8,128)(2,1)S(1)}, u32[]{:S(2)}, u32[]{:S(2)}) collective-permute-start(bf16[384,768]{1,0:T(8,128)(2,1)S(1)} %get-tuple-element.35), channel_id=1, source_target_pairs={{0,2},{1,5},{2,0},{3,7},{4,6},{5,1},{6,4},{7,3},{8,10},{9,13},{10,... | collective-permute-start | bytes 1769480 | tf_op jit(solution)/shard_map/ppermute | solution.py:354
  13.6 10.5 %collective-permute-start.5 = (f32[3328]{0:T(1024)S(1)}, f32[3328]{0:T(1024)S(1)}, u32[]{:S(2)}, u32[]{:S(2)}) collective-permute-start(f32[3328]{0:T(1024)S(1)} %pad_maximum_fusion.5), channel_id=1, source_target_pairs={{0,8},{8,0},{16,24},{24,16},{1,9},{9,1},{17,25},{25,17},{2,10},{10... | collective-permute-start | bytes 39944 | tf_op jit(solution)/shard_map/ppermute | solution.py:261
  17.8 7.9 %collective-permute-start.6 = (f32[3328]{0:T(1024)S(1)}, f32[3328]{0:T(1024)S(1)}, u32[]{:S(2)}, u32[]{:S(2)}) collective-permute-start(f32[3328]{0:T(1024)S(1)} %pad_maximum_fusion.5), channel_id=1, source_target_pairs={{0,16},{8,24},{16,0},{24,8},{1,17},{9,25},{17,1},{25,9},{2,18},{10... | collective-permute-start | bytes 39944 | tf_op jit(solution)/shard_map/ppermute | solution.py:261
  21.7 5.5 %collective-permute-start.7 = (f32[3328]{0:T(1024)S(1)}, f32[3328]{0:T(1024)S(1)}, u32[]{:S(2)}, u32[]{:S(2)}) collective-permute-start(f32[3328]{0:T(1024)S(1)} %pad_maximum_fusion.5), channel_id=1, source_target_pairs={{0,24},{8,16},{16,8},{24,0},{1,25},{9,17},{17,9},{25,1},{2,26},{10... | collective-permute-start | bytes 39944 | tf_op jit(solution)/shard_map/ppermute | solution.py:261
  24.2 9.9 %collective-permute-start.12 = (bf16[384,768]{1,0:T(8,128)(2,1)S(1)}, bf16[384,768]{1,0:T(8,128)(2,1)S(1)}, u32[]{:S(2)}, u32[]{:S(2)}) collective-permute-start(bf16[384,768]{1,0:T(8,128)(2,1)S(1)} %collective-permute-done.8.refs_2_.refs_7_.refs_8_), channel_id=1, source_target_pairs={{0,4},{1,3},{2,6},{3,1},{4,0},{5,7},{6,2},{7,5},{8,12},{9,11},{10,... | collective-permute-start | bytes 1769480 | tf_op jit(solution)/shard_map/ppermute | solution.py:357
  25.7 14.7 %collective-permute-start.10 = (bf16[384,768]{1,0:T(8,128)(2,1)S(1)}, bf16[384,768]{1,0:T(8,128)(2,1)S(1)}, u32[]{:S(2)}, u32[]{:S(2)}) collective-permute-start(bf16[384,768]{1,0:T(8,128)(2,1)S(1)} %get-tuple-element.35), channel_id=1, source_target_pairs={{0,4},{1,3},{2,6},{3,1},{4,0},{5,7},{6,2},{7,5},{8,12},{9,11},{10,... | collective-permute-start | bytes 1769480 | tf_op jit(solution)/shard_map/ppermute | solution.py:356
  27.3 20.8 %collective-permute-start.18 = (bf16[256,768]{1,0:T(8,128)(2,1)S(1)}, bf16[256,768]{1,0:T(8,128)(2,1)S(1)}, u32[]{:S(2)}, u32[]{:S(2)}) collective-permute-start(bf16[256,768]{1,0:T(8,128)(2,1)S(1)} %collective-permute-done.1.refs_1_), channel_id=1, source_target_pairs={{8,0},{16,24},{9,1},{17,25},{10,2},{18,26},{11,3},{19,27},{12,4},{... | collective-permute-start | bytes 1179656 | tf_op jit(solution)/shard_map/ppermute | solution.py:273
  28.6 11.8 %collective-permute-start.19 = (bf16[256,768]{1,0:T(8,128)(2,1)S(1)}, bf16[256,768]{1,0:T(8,128)(2,1)S(1)}, u32[]{:S(2)}, u32[]{:S(2)}) collective-permute-start(bf16[256,768]{1,0:T(8,128)(2,1)S(1)} %collective-permute-done.refs_0_), channel_id=1, source_target_pairs={{8,16},{16,8},{9,17},{17,9},{10,18},{18,10},{11,19},{19,11},{12,20... | collective-permute-start | bytes 1179656 | tf_op jit(solution)/shard_map/ppermute | solution.py:272
  33.4 8.5 %collective-permute-start.9 = (bf16[384,768]{1,0:T(8,128)(2,1)S(1)}, bf16[384,768]{1,0:T(8,128)(2,1)S(1)}, u32[]{:S(2)}, u32[]{:S(2)}) collective-permute-start(bf16[384,768]{1,0:T(8,128)(2,1)S(1)} %collective-permute-done.8.refs_2_.refs_7_.refs_8_), channel_id=1, source_target_pairs={{0,1},{1,0},{2,3},{3,2},{4,5},{5,4},{6,7},{7,6},{8,9},{9,8},{10,11... | collective-permute-start | bytes 1769480 | tf_op jit(solution)/shard_map/ppermute | solution.py:261
  34.0 7.9 %collective-permute-start.13 = (bf16[384,768]{1,0:T(8,128)(2,1)S(1)}, bf16[384,768]{1,0:T(8,128)(2,1)S(1)}, u32[]{:S(2)}, u32[]{:S(2)}) collective-permute-start(bf16[384,768]{1,0:T(8,128)(2,1)S(1)} %collective-permute-done.12.refs_6_.refs_11_.refs_12_), channel_id=1, source_target_pairs={{0,1},{1,0},{2,3},{3,2},{4,5},{5,4},{6,7},{7,6},{8,9},{9,8},{10,11... | collective-permute-start | bytes 1769480 | tf_op jit(solution)/shard_map/ppermute | solution.py:261
  40.4 2.0 %collective-permute-start.11 = (bf16[384,768]{1,0:T(8,128)(2,1)S(1)}, bf16[384,768]{1,0:T(8,128)(2,1)S(1)}, u32[]{:S(2)}, u32[]{:S(2)}) collective-permute-start(bf16[384,768]{1,0:T(8,128)(2,1)S(1)} %collective-permute-done.10.refs_4_.refs_9_.refs_10_), channel_id=1, source_target_pairs={{0,1},{1,0},{2,3},{3,2},{4,5},{5,4},{6,7},{7,6},{8,9},{9,8},{10,11... | collective-permute-start | bytes 1769480 | tf_op jit(solution)/shard_map/ppermute | solution.py:261
  40.4 23.1 %collective-permute-start.21 = (bf16[256,768]{1,0:T(8,128)(2,1)S(1)}, bf16[256,768]{1,0:T(8,128)(2,1)S(1)}, u32[]{:S(2)}, u32[]{:S(2)}) collective-permute-start(bf16[256,768]{1,0:T(8,128)(2,1)S(1)} %collective-permute-done.19.refs_1_), channel_id=1, source_target_pairs={{8,0},{16,24},{9,1},{17,25},{10,2},{18,26},{11,3},{19,27},{12,4},{... | collective-permute-start | bytes 1179656 | tf_op jit(solution)/shard_map/ppermute | solution.py:274
  45.8 10.1 %collective-permute-start.17 = (f32[2,2,128]{2,1,0:T(2,128)S(1)}, f32[2,2,128]{2,1,0:T(2,128)S(1)}, u32[]{:S(2)}, u32[]{:S(2)}) collective-permute-start(f32[2,2,128]{2,1,0:T(2,128)S(1)} %score.5), channel_id=1, source_target_pairs={{0,8},{8,0},{16,24},{24,16},{1,9},{9,1},{17,25},{25,17},{2,10},{10... | collective-permute-start | bytes 6152 | tf_op jit(solution)/shard_map/ppermute | solution.py:261
  50.4 8.0 %collective-permute-start.20 = (f32[2,2,128]{2,1,0:T(2,128)S(1)}, f32[2,2,128]{2,1,0:T(2,128)S(1)}, u32[]{:S(2)}, u32[]{:S(2)}) collective-permute-start(f32[2,2,128]{2,1,0:T(2,128)S(1)} %score.6), channel_id=1, source_target_pairs={{0,16},{8,24},{16,0},{24,8},{1,17},{9,25},{17,1},{25,9},{2,18},{10... | collective-permute-start | bytes 6152 | tf_op jit(solution)/shard_map/ppermute | solution.py:261
  51.6 6.8 %collective-permute-start.14 = (bf16[64,768]{1,0:T(8,128)(2,1)S(1)}, bf16[64,768]{1,0:T(8,128)(2,1)S(1)}, u32[]{:S(2)}, u32[]{:S(2)}) collective-permute-start(bf16[64,768]{1,0:T(8,128)(2,1)S(1)} %get-tuple-element.47), channel_id=1, source_target_pairs={{0,8},{8,0},{16,24},{24,16},{1,9},{9,1},{17,25},{25,17},{2,10},{10... | collective-permute-start | bytes 294920 | tf_op jit(solution)/shard_map/ppermute | solution.py:261
  53.7 9.8 %collective-permute-start.15 = (bf16[64,768]{1,0:T(8,128)(2,1)S(1)}, bf16[64,768]{1,0:T(8,128)(2,1)S(1)}, u32[]{:S(2)}, u32[]{:S(2)}) collective-permute-start(bf16[64,768]{1,0:T(8,128)(2,1)S(1)} %get-tuple-element.49), channel_id=1, source_target_pairs={{0,16},{8,24},{16,0},{24,8},{1,17},{9,25},{17,1},{25,9},{2,18},{10... | collective-permute-start | bytes 294920 | tf_op jit(solution)/shard_map/ppermute | solution.py:261
  55.9 7.5 %collective-permute-start.16 = (bf16[64,768]{1,0:T(8,128)(2,1)S(1)}, bf16[64,768]{1,0:T(8,128)(2,1)S(1)}, u32[]{:S(2)}, u32[]{:S(2)}) collective-permute-start(bf16[64,768]{1,0:T(8,128)(2,1)S(1)} %get-tuple-element.48), channel_id=1, source_target_pairs={{0,24},{8,16},{16,8},{24,0},{1,25},{9,17},{17,9},{25,1},{2,26},{10... | collective-permute-start | bytes 294920 | tf_op jit(solution)/shard_map/ppermute | solution.py:261
  63.5 8.4 %collective-permute-start.22 = (bf16[192,768]{1,0:T(8,128)(2,1)S(1)}, bf16[192,768]{1,0:T(8,128)(2,1)S(1)}, u32[]{:S(2)}, u32[]{:S(2)}) collective-permute-start(bf16[192,768]{1,0:T(8,128)(2,1)S(1)} %pad_maximum_fusion.refs_1_), channel_id=1, source_target_pairs={{0,1},{1,0},{2,3},{3,2},{4,5},{5,4},{6,7},{7,6},{8,9},{9,8},{10,11... | collective-permute-start | bytes 884744 | tf_op jit(solution)/shard_map/ppermute | solution.py:261
  65.8 5.4 %collective-permute-start.23 = (f32[2,2,128]{2,1,0:T(2,128)S(1)}, f32[2,2,128]{2,1,0:T(2,128)S(1)}, u32[]{:S(2)}, u32[]{:S(2)}) collective-permute-start(f32[2,2,128]{2,1,0:T(2,128)S(1)} %score.7), channel_id=1, source_target_pairs={{0,24},{8,16},{16,8},{24,0},{1,25},{9,17},{17,9},{25,1},{2,26},{10... | collective-permute-start | bytes 6152 | tf_op jit(solution)/shard_map/ppermute | solution.py:261

commit v17 on v16

--- a/solution.py
+++ b/solution.py
@@ -413,12 +413,13 @@
         )
         return partial
 
-    mine = score(0)
+    partials = [score(s) for s in range(planes - 1)]
+    parts, own_part, *given = lax.optimization_barrier((parts, partials[0], *got_queries[-1]))
+    got_queries[-1] = tuple(given)
+    arrived = [packed[:own_slots], parts] + [swap(parts, "query", flip) for flip in range(1, replicas)]
+    mine = own_part
     for s in range(1, planes - 1):
-        mine = mine + swap(score(s), "outer", s)
-    parts, own_part, *given = lax.optimization_barrier((parts, mine, *got_queries[-1]))
-    mine, got_queries[-1] = own_part, tuple(given)
-    arrived = [packed[:own_slots], parts] + [swap(parts, "query", flip) for flip in range(1, replicas)]
+        mine = mine + swap(partials[s], "outer", s)
     mine = mine + swap(score(planes - 1), "outer", planes - 1)
     (new_table,) = call(
         apply_kernel, "apply", [jax.ShapeDtypeStruct(table.shape, bf16)], None, target, own, table, *arrived

time: 73.6 us -> 79.7 us (1.083)
  starting transfers between devices: 30.7 us -> 36.8 us
    ppermute x17, waiting for transfers between devices: 10.7 us -> 21.5 us  [swap(): lax.ppermute(values, axis, [(i, i ^ flip) for i in range(lax.axis_size(ax...]
    ppermute x1, waiting for transfers between devices: 6.32 us -> 0.01 us  [on_device(): side = lax.ppermute(rows_half, axes, second)]
    ppermute x17, starting transfers between devices: 23 us -> 27.6 us  [swap(): lax.ppermute(values, axis, [(i, i ^ flip) for i in range(lax.axis_size(ax...]
    ppermute x1, waiting for transfers between devices: 3.82 us -> 0.01 us  [on_device(): near = lax.ppermute(rows_half, axes, first)]
    ppermute x1, starting transfers between devices: 1.56 us -> 3 us  [on_device(): near = lax.ppermute(rows_half, axes, first)]
    ppermute x1, starting transfers between devices: 0.51 us -> 1.53 us  [on_device(): side = lax.ppermute(rows_half, axes, second)]
    ppermute x1, starting transfers between devices: 1.52 us -> 0.56 us  [on_device(): far = lax.ppermute(near, axes, second)]
  transfers between devices with their start and end apart: 24 -> 24, of which waited for: 8 -> 7; matrix products, arithmetic and copies ran while one was open for 1% -> 1% of each run, Pallas kernels for 19% -> 18%
where the time goes in v17:
time: 79.7 us; the launch traced here: 79.5 us
  starting transfers between devices  36.8 us (46%)
  waiting for transfers between devices  21.5 us (27%)
  Pallas kernels  16.4 us (21%)
  local copies, waits for them, and re-layouts  2.98 us (4%)
  between operations  0.96 us (1%)
    ppermute x17, starting transfers between devices, swap(): lax.ppermute(values, axis, [(i, i ^ flip) for i in range(lax.axis_size(ax...  27.6 us
    ppermute x17, waiting for transfers between devices, swap(): lax.ppermute(values, axis, [(i, i ^ flip) for i in range(lax.axis_size(ax...  21.5 us
    pallas_call x8, Pallas kernels, call(): pl.pallas_call(functools.partial(kernel, **options), out_shape=tuple(outs...  16.4 us
    ppermute x1, starting transfers between devices, on_device(): near = lax.ppermute(rows_half, axes, first)  3 us
    unnamed x16, local copies, waits for them, and re-layouts  2.84 us
  transfers between devices with their start and end apart: 24, of which 7 were waited for; matrix products, arithmetic and copies ran while one was open for 1% of the time, Pallas kernels for 18%

profile of v17, /device:TPU:0, one launch (start us, length us, event | category | flops | bytes accessed | tf_op | source)
XLA Modules:
  0.0 79.5 jit_solution(16777885484410490872)
XLA Ops:
  0.6 0.1 pad_add_fusion.place
  0.7 0.7 copy-done.4
  1.4 0.0 copy-done.5
  1.4 1.1 %copy-done = bf16[512,768]{1,0:T(8,128)(2,1)S(1)} copy-done((bf16[512,768]{1,0:T(8,128)(2,1)S(1)}, bf16[512,768]{1,0:T(8,128)(2,1)}, u32[]{:S(2)}) %copy-start) | copy-done | bytes 786456
  2.5 1.0 %copy-done.2 = bf16[256,768]{1,0:T(8,128)(2,1)S(1)} copy-done((bf16[256,768]{1,0:T(8,128)(2,1)S(1)}, bf16[256,768]{1,0:T(8,128)(2,1)}, u32[]{:S(2)}) %copy-start.2) | copy-done | bytes 393240
  3.5 0.8 %prep.1 = (bf16[384,768]{1,0:T(8,128)(2,1)S(1)}, f32[12,128]{1,0:T(8,128)S(1)}) custom-call(s32[3]{0:T(128)S(1)} %pad_add_fusion.place, bf16[512,768]{1,0:T(8,128)(2,1)S(1)} %copy-done, bf16[256,768]{1,0:T(8,128)(2,1)S(1)} %copy-done.2, s32[4,128]{1,0:T(4,128)S(1)} %bitcast.23, s32[2,128]{1,0:T(2,128)S(1)} %bitcast.30), custom_call_target="tpu_custom_call" | custom-call | flops 1 | bytes 1 | tf_op jit(solution)/shard_map/prep/pallas_call | solution.py:248
  4.4 3.0 %collective-permute-start.8 = (bf16[384,768]{1,0:T(8,128)(2,1)S(1)}, bf16[384,768]{1,0:T(8,128)(2,1)S(1)}, u32[]{:S(2)}, u32[]{:S(2)}) collective-permute-start(bf16[384,768]{1,0:T(8,128)(2,1)S(1)} %get-tuple-element.35), channel_id=1, source_target_pairs={{0,2},{1,5},{2,0},{3,7},{4,6},{5,1},{6,4},{7,3},{8,10},{9,13},{10,... | collective-permute-start | bytes 1769480 | tf_op jit(solution)/shard_map/ppermute | solution.py:354
  7.4 0.1 collective-permute-start.2
  7.5 2.0 %collective-permute-start.3 = (f32[12,128]{1,0:T(8,128)S(1)}, f32[12,128]{1,0:T(8,128)S(1)}, u32[]{:S(2)}, u32[]{:S(2)}) collective-permute-start(f32[12,128]{1,0:T(8,128)S(1)} %get-tuple-element.25), channel_id=1, source_target_pairs={{0,4},{2,6},{4,0},{6,2},{1,5},{3,7},{5,1},{7,3},{8,12},{10,14},{12... | collective-permute-start | bytes 18440 | tf_op jit(solution)/shard_map/ppermute | solution.py:261
  9.4 1.4 %collective-permute-start.4 = (f32[12,128]{1,0:T(8,128)S(1)}, f32[12,128]{1,0:T(8,128)S(1)}, u32[]{:S(2)}, u32[]{:S(2)}) collective-permute-start(f32[12,128]{1,0:T(8,128)S(1)} %get-tuple-element.25), channel_id=1, source_target_pairs={{0,6},{2,4},{4,2},{6,0},{1,7},{3,5},{5,3},{7,1},{8,14},{10,12},{12... | collective-permute-start | bytes 18440 | tf_op jit(solution)/shard_map/ppermute | solution.py:261
  10.9 4.6 %collective-permute-done.2 = f32[12,128]{1,0:T(8,128)S(1)} collective-permute-done((f32[12,128]{1,0:T(8,128)S(1)}, f32[12,128]{1,0:T(8,128)S(1)}, u32[]{:S(2)}, u32[]{:S(2)}) %collective-permute-start.2) | collective-permute-done | bytes 6176 | tf_op jit(solution)/shard_map/ppermute | solution.py:261
  15.5 0.0 collective-permute-done.3
  15.5 1.5 %collective-permute-done.4 = f32[12,128]{1,0:T(8,128)S(1)} collective-permute-done((f32[12,128]{1,0:T(8,128)S(1)}, f32[12,128]{1,0:T(8,128)S(1)}, u32[]{:S(2)}, u32[]{:S(2)}) %collective-permute-start.4) | collective-permute-done | bytes 6176 | tf_op jit(solution)/shard_map/ppermute | solution.py:261
  17.0 0.0 copy-start.7
  17.0 0.0 collective-permute-done.8.refs_2_.refs_7_.refs_8_
  17.0 0.6 collective-permute-start.12
  17.6 1.5 %collective-permute-start.10 = (bf16[384,768]{1,0:T(8,128)(2,1)S(1)}, bf16[384,768]{1,0:T(8,128)(2,1)S(1)}, u32[]{:S(2)}, u32[]{:S(2)}) collective-permute-start(bf16[384,768]{1,0:T(8,128)(2,1)S(1)} %get-tuple-element.35), channel_id=1, source_target_pairs={{0,4},{1,3},{2,6},{3,1},{4,0},{5,7},{6,2},{7,5},{8,12},{9,11},{10,... | collective-permute-start | bytes 1769480 | tf_op jit(solution)/shard_map/ppermute | solution.py:356
  19.1 1.6 %collective-permute-start = (bf16[256,768]{1,0:T(8,128)(2,1)S(1)}, bf16[256,768]{1,0:T(8,128)(2,1)S(1)}, u32[]{:S(2)}, u32[]{:S(2)}) collective-permute-start(bf16[256,768]{1,0:T(8,128)(2,1)S(1)} %copy-done.3), channel_id=1, source_target_pairs={{0,8},{8,0},{16,24},{24,16},{1,9},{9,1},{17,25},{25,17},{2,10},{10... | collective-permute-start | bytes 1179656 | tf_op jit(solution)/shard_map/ppermute | solution.py:261
  20.7 0.7 collective-permute-start.1
  21.5 4.4 %collective-permute-start.5 = (f32[3328]{0:T(1024)S(1)}, f32[3328]{0:T(1024)S(1)}, u32[]{:S(2)}, u32[]{:S(2)}) collective-permute-start(f32[3328]{0:T(1024)S(1)} %pad_maximum_fusion.5), channel_id=1, source_target_pairs={{0,8},{8,0},{16,24},{24,16},{1,9},{9,1},{17,25},{25,17},{2,10},{10... | collective-permute-start | bytes 39944 | tf_op jit(solution)/shard_map/ppermute | solution.py:261
  25.9 1.9 %collective-permute-done.5 = f32[3328]{0:T(1024)S(1)} collective-permute-done((f32[3328]{0:T(1024)S(1)}, f32[3328]{0:T(1024)S(1)}, u32[]{:S(2)}, u32[]{:S(2)}) %collective-permute-start.5) | collective-permute-done | bytes 13344 | tf_op jit(solution)/shard_map/ppermute | solution.py:261
  27.8 2.9 %collective-permute-start.6 = (f32[3328]{0:T(1024)S(1)}, f32[3328]{0:T(1024)S(1)}, u32[]{:S(2)}, u32[]{:S(2)}) collective-permute-start(f32[3328]{0:T(1024)S(1)} %pad_maximum_fusion.5), channel_id=1, source_target_pairs={{0,16},{8,24},{16,0},{24,8},{1,17},{9,25},{17,1},{25,9},{2,18},{10... | collective-permute-start | bytes 39944 | tf_op jit(solution)/shard_map/ppermute | solution.py:261
  30.7 1.7 %collective-permute-done.6 = f32[3328]{0:T(1024)S(1)} collective-permute-done((f32[3328]{0:T(1024)S(1)}, f32[3328]{0:T(1024)S(1)}, u32[]{:S(2)}, u32[]{:S(2)}) %collective-permute-start.6) | collective-permute-done | bytes 13344 | tf_op jit(solution)/shard_map/ppermute | solution.py:261
  32.5 3.9 %collective-permute-start.7 = (f32[3328]{0:T(1024)S(1)}, f32[3328]{0:T(1024)S(1)}, u32[]{:S(2)}, u32[]{:S(2)}) collective-permute-start(f32[3328]{0:T(1024)S(1)} %pad_maximum_fusion.5), channel_id=1, source_target_pairs={{0,24},{8,16},{16,8},{24,0},{1,25},{9,17},{17,9},{25,1},{2,26},{10... | collective-permute-start | bytes 39944 | tf_op jit(solution)/shard_map/ppermute | solution.py:261
  36.4 1.8 %collective-permute-done.7 = f32[3328]{0:T(1024)S(1)} collective-permute-done((f32[3328]{0:T(1024)S(1)}, f32[3328]{0:T(1024)S(1)}, u32[]{:S(2)}, u32[]{:S(2)}) %collective-permute-start.7) | collective-permute-done | bytes 13344 | tf_op jit(solution)/shard_map/ppermute | solution.py:261
  38.2 0.0 collective-permute-done.refs_0_
  38.2 0.0 collective-permute-done.1.refs_1_
  38.2 0.7 collective-permute-start.17
  38.9 0.1 collective-permute-start.9
  39.0 0.0 collective-permute-done.12.refs_6_.refs_11_.refs_12_
  39.0 0.5 collective-permute-start.13
  39.5 0.0 collective-permute-done.10.refs_4_.refs_9_.refs_10_
  39.5 0.1 collective-permute-start.11
  39.7 1.3 %collective-permute-start.21 = (bf16[256,768]{1,0:T(8,128)(2,1)S(1)}, bf16[256,768]{1,0:T(8,128)(2,1)S(1)}, u32[]{:S(2)}, u32[]{:S(2)}) collective-permute-start(bf16[256,768]{1,0:T(8,128)(2,1)S(1)} %collective-permute-done.1.refs_1_), channel_id=1, source_target_pairs={{8,0},{16,24},{9,1},{17,25},{10,2},{18,26},{11,3},{19,27},{12,4},{... | collective-permute-start | bytes 1179656 | tf_op jit(solution)/shard_map/ppermute | solution.py:273
  41.0 4.0 %meta.1 = (f32[4,3072]{1,0:T(4,128)S(1)}, f32[1,3072]{1,0:T(1,128)S(1)}, s32[1,1024]{1,0:T(1,128)S(1)}, s32[1,512]{1,0:T(1,128)S(1)}, s32[1,512]{1,0:T(1,128)S(1)}, /*index=5*/s32[1,512]{1,0:T(1,128)}) custom-call(s32[3]{0:T(128)S(1)} %pad_add_fusion.place, s32[4,1024]{1,0:T(4,128)S(1)} %maximum_convert_fusion.ref_ids, s32[4,2048]{1,0:T(4,128)S(1)} %fusion.neg, ...), custom_call_target="tpu_custom_call" | custom-call | flops 1 | bytes 1 | tf_op jit(solution)/shard_map/meta/pallas_call | solution.py:248
  45.0 0.0 collective-permute-done.17.refs_1_
  45.0 1.5 %collective-permute-start.18 = (bf16[256,768]{1,0:T(8,128)(2,1)S(1)}, bf16[256,768]{1,0:T(8,128)(2,1)S(1)}, u32[]{:S(2)}, u32[]{:S(2)}) collective-permute-start(bf16[256,768]{1,0:T(8,128)(2,1)S(1)} %collective-permute-done.17.refs_1_), channel_id=1, source_target_pairs={{8,0},{16,24},{9,1},{17,25},{10,2},{18,26},{11,3},{19,27},{12,4},{... | collective-permute-start | bytes 1179656 | tf_op jit(solution)/shard_map/ppermute | solution.py:274
  46.5 0.0 collective-permute-done.9.refs_3_.refs_8_.refs_9_
  46.5 0.0 collective-permute-done.13.refs_7_.refs_12_.refs_13_
  46.5 0.0 collective-permute-done.11.refs_5_.refs_10_.refs_11_
  46.5 0.0 copy-done.1
  46.5 1.2 %pack.1 = bf16[320,768]{1,0:T(8,128)(2,1)S(1)} custom-call(s32[3]{0:T(128)S(1)} %pad_add_fusion.place, s32[1,1024]{1,0:T(1,128)S(1)} %get-tuple-element.32.code, bf16[512,768]{1,0:T(8,128)(2,1)S(1)} %copy-done.1, bf16[256,768]{1,0:T(8,128)(2,1)S(1)} %copy-done.2, bf16[384,768]{1,0:T(8,128)(2,1)S(1)} %collective-permute-done.8.refs_2_.refs_7_.refs_8_, ...), custom_call_target="tpu_custom_call" | custom-call | flops 1 | bytes 1 | tf_op jit(solution)/shard_map/pack/pallas_call | solution.py:248
  47.8 3.0 %collective-permute-start.14 = (bf16[64,768]{1,0:T(8,128)(2,1)S(1)}, bf16[64,768]{1,0:T(8,128)(2,1)S(1)}, u32[]{:S(2)}, u32[]{:S(2)}) collective-permute-start(bf16[64,768]{1,0:T(8,128)(2,1)S(1)} %get-tuple-element.47), channel_id=1, source_target_pairs={{0,8},{8,0},{16,24},{24,16},{1,9},{9,1},{17,25},{25,17},{2,10},{10... | collective-permute-start | bytes 294920 | tf_op jit(solution)/shard_map/ppermute | solution.py:261
  50.8 2.1 %collective-permute-start.15 = (bf16[64,768]{1,0:T(8,128)(2,1)S(1)}, bf16[64,768]{1,0:T(8,128)(2,1)S(1)}, u32[]{:S(2)}, u32[]{:S(2)}) collective-permute-start(bf16[64,768]{1,0:T(8,128)(2,1)S(1)} %get-tuple-element.49), channel_id=1, source_target_pairs={{0,16},{8,24},{16,0},{24,8},{1,17},{9,25},{17,1},{25,9},{2,18},{10... | collective-permute-start | bytes 294920 | tf_op jit(solution)/shard_map/ppermute | solution.py:261
  53.0 1.4 %collective-permute-start.16 = (bf16[64,768]{1,0:T(8,128)(2,1)S(1)}, bf16[64,768]{1,0:T(8,128)(2,1)S(1)}, u32[]{:S(2)}, u32[]{:S(2)}) collective-permute-start(bf16[64,768]{1,0:T(8,128)(2,1)S(1)} %get-tuple-element.48), channel_id=1, source_target_pairs={{0,24},{8,16},{16,8},{24,0},{1,25},{9,17},{17,9},{25,1},{2,26},{10... | collective-permute-start | bytes 294920 | tf_op jit(solution)/shard_map/ppermute | solution.py:261
  54.5 2.2 %score.5 = f32[2,2,128]{2,1,0:T(2,128)S(1)} custom-call(s32[3]{0:T(128)S(1)} %pad_add_fusion.place, bf16[256,768]{1,0:T(8,128)(2,1)S(1)} %collective-permute-done.refs_0_, f32[2,128]{1,0:T(2,128)S(1)} %bitcast.28, f32[1,3072]{1,0:T(1,128)S(1)} %get-tuple-element.50.refs_2_, f32[1,3072]{1,0:T(1,128)S(1)} %get-tuple-element.39.refs_3_.refs_4_, ...), custom_call_target="tpu_custom_call" | custom-call | flops 1 | bytes 1 | tf_op jit(solution)/shard_map/score/pallas_call | solution.py:248
  56.7 2.2 %score.4 = f32[2,2,128]{2,1,0:T(2,128)S(1)} custom-call(s32[3]{0:T(128)S(1)} %pad_add_fusion.place, bf16[256,768]{1,0:T(8,128)(2,1)S(1)} %copy-done.3, f32[2,128]{1,0:T(2,128)S(1)} %bitcast.29, f32[1,3072]{1,0:T(1,128)S(1)} %get-tuple-element.53.refs_2_, f32[1,3072]{1,0:T(1,128)S(1)} %get-tuple-element.39.refs_3_.refs_4_, ...), custom_call_target="tpu_custom_call" | custom-call | flops 1 | bytes 1 | tf_op jit(solution)/shard_map/score/pallas_call | solution.py:248
  58.9 0.0 collective-permute-done.21.refs_0_
  58.9 0.6 collective-permute-start.20
  59.6 2.2 %score.6 = f32[2,2,128]{2,1,0:T(2,128)S(1)} custom-call(s32[3]{0:T(128)S(1)} %pad_add_fusion.place, bf16[256,768]{1,0:T(8,128)(2,1)S(1)} %collective-permute-done.21.refs_0_, bf16[256,768]{1,0:T(8,128)(2,1)S(1)} %collective-permute-done.17.refs_1_, f32[2,128]{1,0:T(2,128)S(1)} %bitcast.27, f32[1,3072]{1,0:T(1,128)S(1)} %get-tuple-element.52.refs_3_, ...), custom_call_target="tpu_custom_call" | custom-call | flops 1 | bytes 1 | tf_op jit(solution)/shard_map/score/pallas_call | solution.py:248
  61.8 6.5 %collective-permute-done.14 = bf16[64,768]{1,0:T(8,128)(2,1)S(1)} collective-permute-done((bf16[64,768]{1,0:T(8,128)(2,1)S(1)}, bf16[64,768]{1,0:T(8,128)(2,1)S(1)}, u32[]{:S(2)}, u32[]{:S(2)}) %collective-permute-start.14) | collective-permute-done | bytes 98336 | tf_op jit(solution)/shard_map/ppermute | solution.py:261
  68.3 1.3 %collective-permute-start.22 = (f32[2,2,128]{2,1,0:T(2,128)S(1)}, f32[2,2,128]{2,1,0:T(2,128)S(1)}, u32[]{:S(2)}, u32[]{:S(2)}) collective-permute-start(f32[2,2,128]{2,1,0:T(2,128)S(1)} %score.6), channel_id=1, source_target_pairs={{0,16},{8,24},{16,0},{24,8},{1,17},{9,25},{17,1},{25,9},{2,18},{10... | collective-permute-start | bytes 6152 | tf_op jit(solution)/shard_map/ppermute | solution.py:261
  69.7 0.0 collective-permute-done.15
  69.7 0.0 collective-permute-done.16
  69.7 0.0 collective-permute-done.18.refs_0_
  69.7 2.2 %score.7 = f32[2,2,128]{2,1,0:T(2,128)S(1)} custom-call(s32[3]{0:T(128)S(1)} %pad_add_fusion.place, bf16[256,768]{1,0:T(8,128)(2,1)S(1)} %collective-permute-done.18.refs_0_, bf16[256,768]{1,0:T(8,128)(2,1)S(1)} %collective-permute-done.1.refs_1_, f32[2,128]{1,0:T(2,128)S(1)} %bitcast.26, f32[1,3072]{1,0:T(1,128)S(1)} %get-tuple-element.51.refs_3_, ...), custom_call_target="tpu_custom_call" | custom-call | flops 1 | bytes 1 | tf_op jit(solution)/shard_map/score/pallas_call | solution.py:248
  72.0 2.0 %collective-permute-start.23 = (f32[2,2,128]{2,1,0:T(2,128)S(1)}, f32[2,2,128]{2,1,0:T(2,128)S(1)}, u32[]{:S(2)}, u32[]{:S(2)}) collective-permute-start(f32[2,2,128]{2,1,0:T(2,128)S(1)} %score.7), channel_id=1, source_target_pairs={{0,24},{8,16},{16,8},{24,0},{1,25},{9,17},{17,9},{25,1},{2,26},{10... | collective-permute-start | bytes 6152 | tf_op jit(solution)/shard_map/ppermute | solution.py:261
  74.0 0.1 collective-permute-start.19
  74.0 0.0 collective-permute-done.20
  74.1 0.0 collective-permute-done.22
  74.1 3.3 %collective-permute-done.23 = f32[2,2,128]{2,1,0:T(2,128)S(1)} collective-permute-done((f32[2,2,128]{2,1,0:T(2,128)S(1)}, f32[2,2,128]{2,1,0:T(2,128)S(1)}, u32[]{:S(2)}, u32[]{:S(2)}) %collective-permute-start.23) | collective-permute-done | bytes 2080 | tf_op jit(solution)/shard_map/ppermute | solution.py:261
  77.4 0.6 fusion.2
  78.0 0.0 collective-permute-done.19.refs_2_
  78.0 1.5 %apply.1 = bf16[512,768]{1,0:T(8,128)(2,1)} custom-call(s32[1,512]{1,0:T(1,128)S(1)} %get-tuple-element.30.target, s32[1,512]{1,0:T(1,128)S(1)} %get-tuple-element.31.refreshed, bf16[512,768]{1,0:T(8,128)(2,1)S(1)} %copy-done.1, bf16[128,768]{1,0:T(8,128)(2,1)S(1)} %slice.77.refs_0_, bf16[192,768]{1,0:T(8,128)(2,1)S(1)} %pad_maximum_fusion.refs_1_, ...), custom_call_target="tpu_custom_call" | custom-call | flops 1 | bytes 1 | tf_op jit(solution)/shard_map/apply/pallas_call | solution.py:248
  (32 shorter events, 0.3 us)
Async XLA Ops:
  0.7 0.7 copy-start.4
  0.7 0.7 copy-start.5
  1.4 1.1 %copy-start = (bf16[512,768]{1,0:T(8,128)(2,1)S(1)}, bf16[512,768]{1,0:T(8,128)(2,1)}, u32[]{:S(2)}) copy-start(bf16[512,768]{1,0:T(8,128)(2,1)} %refs_6_.7) | copy-start | bytes 2359300
  2.5 1.0 %copy-start.2 = (bf16[256,768]{1,0:T(8,128)(2,1)S(1)}, bf16[256,768]{1,0:T(8,128)(2,1)}, u32[]{:S(2)}) copy-start(bf16[256,768]{1,0:T(8,128)(2,1)} %refs_7_.3) | copy-start | bytes 1179652
  3.5 15.6 %copy-start.3 = (bf16[256,768]{1,0:T(8,128)(2,1)S(1)}, bf16[256,768]{1,0:T(8,128)(2,1)}, u32[]{:S(2)}) copy-start(bf16[256,768]{1,0:T(8,128)(2,1)} %refs_0_.3) | copy-start | bytes 1179652
  3.5 43.0 %copy-start.1 = (bf16[512,768]{1,0:T(8,128)(2,1)S(1)}, bf16[512,768]{1,0:T(8,128)(2,1)}, u32[]{:S(2)}) copy-start(bf16[512,768]{1,0:T(8,128)(2,1)} %refs_6_.7) | copy-start | bytes 2359300
  4.4 12.6 %collective-permute-start.8 = (bf16[384,768]{1,0:T(8,128)(2,1)S(1)}, bf16[384,768]{1,0:T(8,128)(2,1)S(1)}, u32[]{:S(2)}, u32[]{:S(2)}) collective-permute-start(bf16[384,768]{1,0:T(8,128)(2,1)S(1)} %get-tuple-element.35), channel_id=1, source_target_pairs={{0,2},{1,5},{2,0},{3,7},{4,6},{5,1},{6,4},{7,3},{8,10},{9,13},{10,... | collective-permute-start | bytes 1769480 | tf_op jit(solution)/shard_map/ppermute | solution.py:354
  7.4 8.1 %collective-permute-start.2 = (f32[12,128]{1,0:T(8,128)S(1)}, f32[12,128]{1,0:T(8,128)S(1)}, u32[]{:S(2)}, u32[]{:S(2)}) collective-permute-start(f32[12,128]{1,0:T(8,128)S(1)} %get-tuple-element.25), channel_id=1, source_target_pairs={{0,2},{2,0},{4,6},{6,4},{1,3},{3,1},{5,7},{7,5},{8,10},{10,8},{12,... | collective-permute-start | bytes 18440 | tf_op jit(solution)/shard_map/ppermute | solution.py:261
  7.5 8.1 %collective-permute-start.3 = (f32[12,128]{1,0:T(8,128)S(1)}, f32[12,128]{1,0:T(8,128)S(1)}, u32[]{:S(2)}, u32[]{:S(2)}) collective-permute-start(f32[12,128]{1,0:T(8,128)S(1)} %get-tuple-element.25), channel_id=1, source_target_pairs={{0,4},{2,6},{4,0},{6,2},{1,5},{3,7},{5,1},{7,3},{8,12},{10,14},{12... | collective-permute-start | bytes 18440 | tf_op jit(solution)/shard_map/ppermute | solution.py:261
  9.4 7.6 %collective-permute-start.4 = (f32[12,128]{1,0:T(8,128)S(1)}, f32[12,128]{1,0:T(8,128)S(1)}, u32[]{:S(2)}, u32[]{:S(2)}) collective-permute-start(f32[12,128]{1,0:T(8,128)S(1)} %get-tuple-element.25), channel_id=1, source_target_pairs={{0,6},{2,4},{4,2},{6,0},{1,7},{3,5},{5,3},{7,1},{8,14},{10,12},{12... | collective-permute-start | bytes 18440 | tf_op jit(solution)/shard_map/ppermute | solution.py:261
  17.0 4.4 %copy-start.6 = (s32[1,2048]{1,0:T(1,128)S(1)}, s32[1,2048]{1,0:T(1,128)}, u32[]{:S(2)}) copy-start(s32[1,2048]{1,0:T(1,128)} %param.11) | copy-start | bytes 24580
  17.0 4.4 %copy-start.7 = (s32[256]{0:T(256)S(1)}, s32[256]{0:T(256)}, u32[]{:S(2)}) copy-start(s32[256]{0:T(256)} %param.13) | copy-start | bytes 3076
  17.0 21.9 %collective-permute-start.12 = (bf16[384,768]{1,0:T(8,128)(2,1)S(1)}, bf16[384,768]{1,0:T(8,128)(2,1)S(1)}, u32[]{:S(2)}, u32[]{:S(2)}) collective-permute-start(bf16[384,768]{1,0:T(8,128)(2,1)S(1)} %collective-permute-done.8.refs_2_.refs_7_.refs_8_), channel_id=1, source_target_pairs={{0,4},{1,3},{2,6},{3,1},{4,0},{5,7},{6,2},{7,5},{8,12},{9,11},{10,... | collective-permute-start | bytes 1769480 | tf_op jit(solution)/shard_map/ppermute | solution.py:357
  17.6 21.9 %collective-permute-start.10 = (bf16[384,768]{1,0:T(8,128)(2,1)S(1)}, bf16[384,768]{1,0:T(8,128)(2,1)S(1)}, u32[]{:S(2)}, u32[]{:S(2)}) collective-permute-start(bf16[384,768]{1,0:T(8,128)(2,1)S(1)} %get-tuple-element.35), channel_id=1, source_target_pairs={{0,4},{1,3},{2,6},{3,1},{4,0},{5,7},{6,2},{7,5},{8,12},{9,11},{10,... | collective-permute-start | bytes 1769480 | tf_op jit(solution)/shard_map/ppermute | solution.py:356
  19.1 19.1 %collective-permute-start = (bf16[256,768]{1,0:T(8,128)(2,1)S(1)}, bf16[256,768]{1,0:T(8,128)(2,1)S(1)}, u32[]{:S(2)}, u32[]{:S(2)}) collective-permute-start(bf16[256,768]{1,0:T(8,128)(2,1)S(1)} %copy-done.3), channel_id=1, source_target_pairs={{0,8},{8,0},{16,24},{24,16},{1,9},{9,1},{17,25},{25,17},{2,10},{10... | collective-permute-start | bytes 1179656 | tf_op jit(solution)/shard_map/ppermute | solution.py:261
  20.7 17.5 %collective-permute-start.1 = (bf16[256,768]{1,0:T(8,128)(2,1)S(1)}, bf16[256,768]{1,0:T(8,128)(2,1)S(1)}, u32[]{:S(2)}, u32[]{:S(2)}) collective-permute-start(bf16[256,768]{1,0:T(8,128)(2,1)S(1)} %copy-done.3), channel_id=1, source_target_pairs={{8,16},{16,8},{9,17},{17,9},{10,18},{18,10},{11,19},{19,11},{12,20... | collective-permute-start | bytes 1179656 | tf_op jit(solution)/shard_map/ppermute | solution.py:270
  21.5 6.3 %collective-permute-start.5 = (f32[3328]{0:T(1024)S(1)}, f32[3328]{0:T(1024)S(1)}, u32[]{:S(2)}, u32[]{:S(2)}) collective-permute-start(f32[3328]{0:T(1024)S(1)} %pad_maximum_fusion.5), channel_id=1, source_target_pairs={{0,8},{8,0},{16,24},{24,16},{1,9},{9,1},{17,25},{25,17},{2,10},{10... | collective-permute-start | bytes 39944 | tf_op jit(solution)/shard_map/ppermute | solution.py:261
  27.8 4.6 %collective-permute-start.6 = (f32[3328]{0:T(1024)S(1)}, f32[3328]{0:T(1024)S(1)}, u32[]{:S(2)}, u32[]{:S(2)}) collective-permute-start(f32[3328]{0:T(1024)S(1)} %pad_maximum_fusion.5), channel_id=1, source_target_pairs={{0,16},{8,24},{16,0},{24,8},{1,17},{9,25},{17,1},{25,9},{2,18},{10... | collective-permute-start | bytes 39944 | tf_op jit(solution)/shard_map/ppermute | solution.py:261
  32.5 5.8 %collective-permute-start.7 = (f32[3328]{0:T(1024)S(1)}, f32[3328]{0:T(1024)S(1)}, u32[]{:S(2)}, u32[]{:S(2)}) collective-permute-start(f32[3328]{0:T(1024)S(1)} %pad_maximum_fusion.5), channel_id=1, source_target_pairs={{0,24},{8,16},{16,8},{24,0},{1,25},{9,17},{17,9},{25,1},{2,26},{10... | collective-permute-start | bytes 39944 | tf_op jit(solution)/shard_map/ppermute | solution.py:261
  38.2 6.8 %collective-permute-start.17 = (bf16[256,768]{1,0:T(8,128)(2,1)S(1)}, bf16[256,768]{1,0:T(8,128)(2,1)S(1)}, u32[]{:S(2)}, u32[]{:S(2)}) collective-permute-start(bf16[256,768]{1,0:T(8,128)(2,1)S(1)} %collective-permute-done.refs_0_), channel_id=1, source_target_pairs={{8,16},{16,8},{9,17},{17,9},{10,18},{18,10},{11,19},{19,11},{12,20... | collective-permute-start | bytes 1179656 | tf_op jit(solution)/shard_map/ppermute | solution.py:272
  38.9 7.6 %collective-permute-start.9 = (bf16[384,768]{1,0:T(8,128)(2,1)S(1)}, bf16[384,768]{1,0:T(8,128)(2,1)S(1)}, u32[]{:S(2)}, u32[]{:S(2)}) collective-permute-start(bf16[384,768]{1,0:T(8,128)(2,1)S(1)} %collective-permute-done.8.refs_2_.refs_7_.refs_8_), channel_id=1, source_target_pairs={{0,1},{1,0},{2,3},{3,2},{4,5},{5,4},{6,7},{7,6},{8,9},{9,8},{10,11... | collective-permute-start | bytes 1769480 | tf_op jit(solution)/shard_map/ppermute | solution.py:261
  39.0 7.5 %collective-permute-start.13 = (bf16[384,768]{1,0:T(8,128)(2,1)S(1)}, bf16[384,768]{1,0:T(8,128)(2,1)S(1)}, u32[]{:S(2)}, u32[]{:S(2)}) collective-permute-start(bf16[384,768]{1,0:T(8,128)(2,1)S(1)} %collective-permute-done.12.refs_6_.refs_11_.refs_12_), channel_id=1, source_target_pairs={{0,1},{1,0},{2,3},{3,2},{4,5},{5,4},{6,7},{7,6},{8,9},{9,8},{10,11... | collective-permute-start | bytes 1769480 | tf_op jit(solution)/shard_map/ppermute | solution.py:261
  39.5 7.0 %collective-permute-start.11 = (bf16[384,768]{1,0:T(8,128)(2,1)S(1)}, bf16[384,768]{1,0:T(8,128)(2,1)S(1)}, u32[]{:S(2)}, u32[]{:S(2)}) collective-permute-start(bf16[384,768]{1,0:T(8,128)(2,1)S(1)} %collective-permute-done.10.refs_4_.refs_9_.refs_10_), channel_id=1, source_target_pairs={{0,1},{1,0},{2,3},{3,2},{4,5},{5,4},{6,7},{7,6},{8,9},{9,8},{10,11... | collective-permute-start | bytes 1769480 | tf_op jit(solution)/shard_map/ppermute | solution.py:261
  39.7 19.3 %collective-permute-start.21 = (bf16[256,768]{1,0:T(8,128)(2,1)S(1)}, bf16[256,768]{1,0:T(8,128)(2,1)S(1)}, u32[]{:S(2)}, u32[]{:S(2)}) collective-permute-start(bf16[256,768]{1,0:T(8,128)(2,1)S(1)} %collective-permute-done.1.refs_1_), channel_id=1, source_target_pairs={{8,0},{16,24},{9,1},{17,25},{10,2},{18,26},{11,3},{19,27},{12,4},{... | collective-permute-start | bytes 1179656 | tf_op jit(solution)/shard_map/ppermute | solution.py:273
  45.0 24.7 %collective-permute-start.18 = (bf16[256,768]{1,0:T(8,128)(2,1)S(1)}, bf16[256,768]{1,0:T(8,128)(2,1)S(1)}, u32[]{:S(2)}, u32[]{:S(2)}) collective-permute-start(bf16[256,768]{1,0:T(8,128)(2,1)S(1)} %collective-permute-done.17.refs_1_), channel_id=1, source_target_pairs={{8,0},{16,24},{9,1},{17,25},{10,2},{18,26},{11,3},{19,27},{12,4},{... | collective-permute-start | bytes 1179656 | tf_op jit(solution)/shard_map/ppermute | solution.py:274
  47.8 20.5 %collective-permute-start.14 = (bf16[64,768]{1,0:T(8,128)(2,1)S(1)}, bf16[64,768]{1,0:T(8,128)(2,1)S(1)}, u32[]{:S(2)}, u32[]{:S(2)}) collective-permute-start(bf16[64,768]{1,0:T(8,128)(2,1)S(1)} %get-tuple-element.47), channel_id=1, source_target_pairs={{0,8},{8,0},{16,24},{24,16},{1,9},{9,1},{17,25},{25,17},{2,10},{10... | collective-permute-start | bytes 294920 | tf_op jit(solution)/shard_map/ppermute | solution.py:261
  50.8 18.8 %collective-permute-start.15 = (bf16[64,768]{1,0:T(8,128)(2,1)S(1)}, bf16[64,768]{1,0:T(8,128)(2,1)S(1)}, u32[]{:S(2)}, u32[]{:S(2)}) collective-permute-start(bf16[64,768]{1,0:T(8,128)(2,1)S(1)} %get-tuple-element.49), channel_id=1, source_target_pairs={{0,16},{8,24},{16,0},{24,8},{1,17},{9,25},{17,1},{25,9},{2,18},{10... | collective-permute-start | bytes 294920 | tf_op jit(solution)/shard_map/ppermute | solution.py:261
  53.0 16.7 %collective-permute-start.16 = (bf16[64,768]{1,0:T(8,128)(2,1)S(1)}, bf16[64,768]{1,0:T(8,128)(2,1)S(1)}, u32[]{:S(2)}, u32[]{:S(2)}) collective-permute-start(bf16[64,768]{1,0:T(8,128)(2,1)S(1)} %get-tuple-element.48), channel_id=1, source_target_pairs={{0,24},{8,16},{16,8},{24,0},{1,25},{9,17},{17,9},{25,1},{2,26},{10... | collective-permute-start | bytes 294920 | tf_op jit(solution)/shard_map/ppermute | solution.py:261
  58.9 15.1 %collective-permute-start.20 = (f32[2,2,128]{2,1,0:T(2,128)S(1)}, f32[2,2,128]{2,1,0:T(2,128)S(1)}, u32[]{:S(2)}, u32[]{:S(2)}) collective-permute-start(f32[2,2,128]{2,1,0:T(2,128)S(1)} %score.5), channel_id=1, source_target_pairs={{0,8},{8,0},{16,24},{24,16},{1,9},{9,1},{17,25},{25,17},{2,10},{10... | collective-permute-start | bytes 6152 | tf_op jit(solution)/shard_map/ppermute | solution.py:261
  68.3 5.7 %collective-permute-start.22 = (f32[2,2,128]{2,1,0:T(2,128)S(1)}, f32[2,2,128]{2,1,0:T(2,128)S(1)}, u32[]{:S(2)}, u32[]{:S(2)}) collective-permute-start(f32[2,2,128]{2,1,0:T(2,128)S(1)} %score.6), channel_id=1, source_target_pairs={{0,16},{8,24},{16,0},{24,8},{1,17},{9,25},{17,1},{25,9},{2,18},{10... | collective-permute-start | bytes 6152 | tf_op jit(solution)/shard_map/ppermute | solution.py:261
  72.0 5.4 %collective-permute-start.23 = (f32[2,2,128]{2,1,0:T(2,128)S(1)}, f32[2,2,128]{2,1,0:T(2,128)S(1)}, u32[]{:S(2)}, u32[]{:S(2)}) collective-permute-start(f32[2,2,128]{2,1,0:T(2,128)S(1)} %score.7), channel_id=1, source_target_pairs={{0,24},{8,16},{16,8},{24,0},{1,25},{9,17},{17,9},{25,1},{2,26},{10... | collective-permute-start | bytes 6152 | tf_op jit(solution)/shard_map/ppermute | solution.py:261
  74.0 4.0 %collective-permute-start.19 = (bf16[192,768]{1,0:T(8,128)(2,1)S(1)}, bf16[192,768]{1,0:T(8,128)(2,1)S(1)}, u32[]{:S(2)}, u32[]{:S(2)}) collective-permute-start(bf16[192,768]{1,0:T(8,128)(2,1)S(1)} %pad_maximum_fusion.refs_1_), channel_id=1, source_target_pairs={{0,1},{1,0},{2,3},{3,2},{4,5},{5,4},{6,7},{7,6},{8,9},{9,8},{10,11... | collective-permute-start | bytes 884744 | tf_op jit(solution)/shard_map/ppermute | solution.py:261

commit v18 on v17

--- a/solution.py
+++ b/solution.py
@@ -316,7 +316,16 @@
     scale_plane = jnp.concatenate([piece(2), piece(3)], axis=1)
     line = jnp.concatenate([ref_plane[0], neg_ids[0].astype(f32), pos_ids.astype(f32)])
     lines = [line] + [swap(line, "outer", s) for s in range(1, planes)]
+    fast = replicas == 2 and owners_plane == 4
+    if fast:
+        axes = ("inner", "query")
+        first = [(2 * i + c, 2 * (i ^ (1 + c)) + c) for i in range(4) for c in range(2)]
+        second = [(2 * i + c, 2 * (i ^ (2 - c)) + c) for i in range(4) for c in range(2)]
+        near = lax.ppermute(rows_half, axes, first)
+        lines += [near, rows_half]
     got_queries, lines = gather_line(queries, lines)
+    if fast:
+        *lines, near, rows_half = lines
     got_queries = [(queries,)] + got_queries
     lines = jnp.stack(lines)
     ref_all = lines[:, :plane_refresh].astype(jnp.int32)
@@ -347,14 +356,10 @@
     )
     new_ages = new_ages.reshape(rows_dev)
 
-    if replicas == 2 and owners_plane == 4:
-        axes = ("inner", "query")
-        first = [(2 * i + c, 2 * (i ^ (1 + c)) + c) for i in range(4) for c in range(2)]
-        second = [(2 * i + c, 2 * (i ^ (2 - c)) + c) for i in range(4) for c in range(2)]
-        near = lax.ppermute(rows_half, axes, first)
-        near, rows_half, _ = lax.optimization_barrier((near, rows_half, metas))
+    if fast:
         side = lax.ppermute(rows_half, axes, second)
         far = lax.ppermute(near, axes, second)
+        side, far, lw, got_queries[2] = lax.optimization_barrier((side, far, lw, got_queries[2]))
         buffers = [table, fresh_rows]
         table_pieces = [(0, 0, rows_dev, (0, rows_dev, None, None))]
         fresh_pieces = [(1, 0, refresh_dev, (0, refresh_dev, None, None))]

time: 79.7 us -> 77.9 us (0.977)
  starting transfers between devices: 36.8 us -> 33.6 us
  waiting for transfers between devices: 21.5 us -> 22.9 us
    ppermute x17, waiting for transfers between devices: 21.5 us -> 14.9 us  [swap(): lax.ppermute(values, axis, [(i, i ^ flip) for i in range(lax.axis_size(ax...]
    ppermute x1, waiting for transfers between devices: 0.01 us -> 4.51 us  [on_device(): far = lax.ppermute(near, axes, second)]
    ppermute x1, waiting for transfers between devices: 0.01 us -> 3.45 us  [gather_line(): to_end = lax.ppermute(across, 'outer', outward)]
    ppermute x17, starting transfers between devices: 27.6 us -> 24.4 us  [swap(): lax.ppermute(values, axis, [(i, i ^ flip) for i in range(lax.axis_size(ax...]
  transfers between devices with their start and end apart: 24 -> 24, of which waited for: 7 -> 8; matrix products, arithmetic and copies ran while one was open for 1% -> 1% of each run, Pallas kernels for 18% -> 18%
where the time goes in v18:
time: 77.9 us; the launch traced here: 77.6 us
  starting transfers between devices  33.6 us (43%)
  waiting for transfers between devices  22.9 us (29%)
  Pallas kernels  16.5 us (21%)
  local copies, waits for them, and re-layouts  2.97 us (4%)
  between operations  0.91 us (1%)
  other arithmetic  0.79 us (1%)
    ppermute x17, starting transfers between devices, swap(): lax.ppermute(values, axis, [(i, i ^ flip) for i in range(lax.axis_size(ax...  24.4 us
    pallas_call x8, Pallas kernels, call(): pl.pallas_call(functools.partial(kernel, **options), out_shape=tuple(outs...  16.5 us
    ppermute x17, waiting for transfers between devices, swap(): lax.ppermute(values, axis, [(i, i ^ flip) for i in range(lax.axis_size(ax...  14.9 us
    ppermute x1, waiting for transfers between devices, on_device(): far = lax.ppermute(near, axes, second)  4.51 us
    ppermute x1, waiting for transfers between devices, gather_line(): to_end = lax.ppermute(across, 'outer', outward)  3.45 us
    ppermute x1, starting transfers between devices, on_device(): near = lax.ppermute(rows_half, axes, first)  3 us
    unnamed x16, local copies, waits for them, and re-layouts  2.84 us
    ppermute x1, starting transfers between devices, on_device(): side = lax.ppermute(rows_half, axes, second)  1.69 us
  transfers between devices with their start and end apart: 24, of which 8 were waited for; matrix products, arithmetic and copies ran while one was open for 1% of the time, Pallas kernels for 18%

profile of v18, /device:TPU:0, one launch (start us, length us, event | category | flops | bytes accessed | tf_op | source)
XLA Modules:
  0.0 77.6 jit_solution(5800799242856244033)
XLA Ops:
  0.6 0.0 copy-start.6
  0.6 0.1 pad_add_fusion.place
  0.7 0.7 copy-done.4
  1.4 0.0 copy-done.5
  1.4 1.1 %copy-done = bf16[512,768]{1,0:T(8,128)(2,1)S(1)} copy-done((bf16[512,768]{1,0:T(8,128)(2,1)S(1)}, bf16[512,768]{1,0:T(8,128)(2,1)}, u32[]{:S(2)}) %copy-start) | copy-done | bytes 786456
  2.6 1.0 %copy-done.2 = bf16[256,768]{1,0:T(8,128)(2,1)S(1)} copy-done((bf16[256,768]{1,0:T(8,128)(2,1)S(1)}, bf16[256,768]{1,0:T(8,128)(2,1)}, u32[]{:S(2)}) %copy-start.2) | copy-done | bytes 393240
  3.6 0.8 %prep.1 = (bf16[384,768]{1,0:T(8,128)(2,1)S(1)}, f32[12,128]{1,0:T(8,128)S(1)}) custom-call(s32[3]{0:T(128)S(1)} %pad_add_fusion.place, bf16[512,768]{1,0:T(8,128)(2,1)S(1)} %copy-done, bf16[256,768]{1,0:T(8,128)(2,1)S(1)} %copy-done.2, s32[4,128]{1,0:T(4,128)S(1)} %bitcast.25, s32[2,128]{1,0:T(2,128)S(1)} %bitcast.31), custom_call_target="tpu_custom_call" | custom-call | flops 1 | bytes 1 | tf_op jit(solution)/shard_map/prep/pallas_call | solution.py:248
  4.4 3.0 %collective-permute-start.8 = (bf16[384,768]{1,0:T(8,128)(2,1)S(1)}, bf16[384,768]{1,0:T(8,128)(2,1)S(1)}, u32[]{:S(2)}, u32[]{:S(2)}) collective-permute-start(bf16[384,768]{1,0:T(8,128)(2,1)S(1)} %get-tuple-element.40), channel_id=1, source_target_pairs={{0,2},{1,5},{2,0},{3,7},{4,6},{5,1},{6,4},{7,3},{8,10},{9,13},{10,... | collective-permute-start | bytes 1769480 | tf_op jit(solution)/shard_map/ppermute | solution.py:324
  7.4 1.6 %collective-permute-start = (bf16[256,768]{1,0:T(8,128)(2,1)S(1)}, bf16[256,768]{1,0:T(8,128)(2,1)S(1)}, u32[]{:S(2)}, u32[]{:S(2)}) collective-permute-start(bf16[256,768]{1,0:T(8,128)(2,1)S(1)} %copy-done.3), channel_id=1, source_target_pairs={{0,8},{8,0},{16,24},{24,16},{1,9},{9,1},{17,25},{25,17},{2,10},{10... | collective-permute-start | bytes 1179656 | tf_op jit(solution)/shard_map/ppermute | solution.py:261
  9.0 0.7 collective-permute-start.1
  9.7 0.0 copy-start.7
  9.7 0.6 collective-permute-start.2
  10.3 1.5 %collective-permute-start.3 = (f32[12,128]{1,0:T(8,128)S(1)}, f32[12,128]{1,0:T(8,128)S(1)}, u32[]{:S(2)}, u32[]{:S(2)}) collective-permute-start(f32[12,128]{1,0:T(8,128)S(1)} %get-tuple-element.30), channel_id=1, source_target_pairs={{0,4},{2,6},{4,0},{6,2},{1,5},{3,7},{5,1},{7,3},{8,12},{10,14},{12... | collective-permute-start | bytes 18440 | tf_op jit(solution)/shard_map/ppermute | solution.py:261
  11.8 3.7 %collective-permute-done.2 = f32[12,128]{1,0:T(8,128)S(1)} collective-permute-done((f32[12,128]{1,0:T(8,128)S(1)}, f32[12,128]{1,0:T(8,128)S(1)}, u32[]{:S(2)}, u32[]{:S(2)}) %collective-permute-start.2) | collective-permute-done | bytes 6176 | tf_op jit(solution)/shard_map/ppermute | solution.py:261
  15.5 3.0 %collective-permute-start.4 = (f32[12,128]{1,0:T(8,128)S(1)}, f32[12,128]{1,0:T(8,128)S(1)}, u32[]{:S(2)}, u32[]{:S(2)}) collective-permute-start(f32[12,128]{1,0:T(8,128)S(1)} %get-tuple-element.30), channel_id=1, source_target_pairs={{0,6},{2,4},{4,2},{6,0},{1,7},{3,5},{5,3},{7,1},{8,14},{10,12},{12... | collective-permute-start | bytes 18440 | tf_op jit(solution)/shard_map/ppermute | solution.py:261
  18.5 0.0 collective-permute-done.3
  18.5 1.6 %collective-permute-done.4 = f32[12,128]{1,0:T(8,128)S(1)} collective-permute-done((f32[12,128]{1,0:T(8,128)S(1)}, f32[12,128]{1,0:T(8,128)S(1)}, u32[]{:S(2)}, u32[]{:S(2)}) %collective-permute-start.4) | collective-permute-done | bytes 6176 | tf_op jit(solution)/shard_map/ppermute | solution.py:261
  20.1 2.2 %collective-permute-start.5 = (f32[3328]{0:T(1024)S(1)}, f32[3328]{0:T(1024)S(1)}, u32[]{:S(2)}, u32[]{:S(2)}) collective-permute-start(f32[3328]{0:T(1024)S(1)} %pad_maximum_fusion.4), channel_id=1, source_target_pairs={{0,8},{8,0},{16,24},{24,16},{1,9},{9,1},{17,25},{25,17},{2,10},{10... | collective-permute-start | bytes 39944 | tf_op jit(solution)/shard_map/ppermute | solution.py:261
  22.4 2.5 %collective-permute-start.6 = (f32[3328]{0:T(1024)S(1)}, f32[3328]{0:T(1024)S(1)}, u32[]{:S(2)}, u32[]{:S(2)}) collective-permute-start(f32[3328]{0:T(1024)S(1)} %pad_maximum_fusion.4), channel_id=1, source_target_pairs={{0,16},{8,24},{16,0},{24,8},{1,17},{9,25},{17,1},{25,9},{2,18},{10... | collective-permute-start | bytes 39944 | tf_op jit(solution)/shard_map/ppermute | solution.py:261
  24.9 0.0 collective-permute-done.5
  24.9 3.2 %collective-permute-start.7 = (f32[3328]{0:T(1024)S(1)}, f32[3328]{0:T(1024)S(1)}, u32[]{:S(2)}, u32[]{:S(2)}) collective-permute-start(f32[3328]{0:T(1024)S(1)} %pad_maximum_fusion.4), channel_id=1, source_target_pairs={{0,24},{8,16},{16,8},{24,0},{1,25},{9,17},{17,9},{25,1},{2,26},{10... | collective-permute-start | bytes 39944 | tf_op jit(solution)/shard_map/ppermute | solution.py:261
  28.0 0.0 collective-permute-done.6
  28.0 2.4 %collective-permute-done.7 = f32[3328]{0:T(1024)S(1)} collective-permute-done((f32[3328]{0:T(1024)S(1)}, f32[3328]{0:T(1024)S(1)}, u32[]{:S(2)}, u32[]{:S(2)}) %collective-permute-start.7) | collective-permute-done | bytes 13344 | tf_op jit(solution)/shard_map/ppermute | solution.py:261
  30.4 0.0 collective-permute-done.refs_0_
  30.4 0.0 collective-permute-done.1.refs_1_
  30.4 0.0 collective-permute-done.8.refs_2_.refs_7_.refs_8_
  30.4 1.7 %collective-permute-start.10 = (bf16[384,768]{1,0:T(8,128)(2,1)S(1)}, bf16[384,768]{1,0:T(8,128)(2,1)S(1)}, u32[]{:S(2)}, u32[]{:S(2)}) collective-permute-start(bf16[384,768]{1,0:T(8,128)(2,1)S(1)} %get-tuple-element.40), channel_id=1, source_target_pairs={{0,4},{1,3},{2,6},{3,1},{4,0},{5,7},{6,2},{7,5},{8,12},{9,11},{10,... | collective-permute-start | bytes 1769480 | tf_op jit(solution)/shard_map/ppermute | solution.py:360
  32.1 0.4 collective-permute-start.11
  32.5 1.3 %collective-permute-start.12 = (bf16[256,768]{1,0:T(8,128)(2,1)S(1)}, bf16[256,768]{1,0:T(8,128)(2,1)S(1)}, u32[]{:S(2)}, u32[]{:S(2)}) collective-permute-start(bf16[256,768]{1,0:T(8,128)(2,1)S(1)} %collective-permute-done.1.refs_1_), channel_id=1, source_target_pairs={{8,0},{16,24},{9,1},{17,25},{10,2},{18,26},{11,3},{19,27},{12,4},{... | collective-permute-start | bytes 1179656 | tf_op jit(solution)/shard_map/ppermute | solution.py:273
  33.8 0.7 collective-permute-start.13
  34.5 0.1 collective-permute-start.9
  34.7 4.0 %meta.1 = (f32[4,3072]{1,0:T(4,128)S(1)}, f32[1,3072]{1,0:T(1,128)S(1)}, s32[1,1024]{1,0:T(1,128)S(1)}, s32[1,512]{1,0:T(1,128)S(1)}, s32[1,512]{1,0:T(1,128)S(1)}, /*index=5*/s32[1,512]{1,0:T(1,128)}) custom-call(s32[3]{0:T(128)S(1)} %pad_add_fusion.place, s32[4,1024]{1,0:T(4,128)S(1)} %maximum_convert_fusion.ref_ids, s32[4,2048]{1,0:T(4,128)S(1)} %fusion.neg, ...), custom_call_target="tpu_custom_call" | custom-call | flops 1 | bytes 1 | tf_op jit(solution)/shard_map/meta/pallas_call | solution.py:248
  38.7 3.4 %collective-permute-done.12.refs_0_ = bf16[256,768]{1,0:T(8,128)(2,1)S(1)} collective-permute-done((bf16[256,768]{1,0:T(8,128)(2,1)S(1)}, bf16[256,768]{1,0:T(8,128)(2,1)S(1)}, u32[]{:S(2)}, u32[]{:S(2)}) %collective-permute-start.12) | collective-permute-done | bytes 393248 | tf_op jit(solution)/shard_map/ppermute | solution.py:273
  42.2 0.0 collective-permute-done.13.refs_1_
  42.2 0.0 collective-permute-done.10.refs_4_.refs_9_.refs_10_
  42.2 4.5 %collective-permute-done.11.refs_6_.refs_11_.refs_12_ = bf16[384,768]{1,0:T(8,128)(2,1)S(1)} collective-permute-done((bf16[384,768]{1,0:T(8,128)(2,1)S(1)}, bf16[384,768]{1,0:T(8,128)(2,1)S(1)}, u32[]{:S(2)}, u32[]{:S(2)}) %collective-permute-start.11) | collective-permute-done | bytes 589856 | tf_op jit(solution)/shard_map/ppermute | solution.py:361
  46.7 0.0 collective-permute-start.14
  46.7 0.5 collective-permute-start.15
  47.2 1.5 %collective-permute-start.19 = (bf16[256,768]{1,0:T(8,128)(2,1)S(1)}, bf16[256,768]{1,0:T(8,128)(2,1)S(1)}, u32[]{:S(2)}, u32[]{:S(2)}) collective-permute-start(bf16[256,768]{1,0:T(8,128)(2,1)S(1)} %collective-permute-done.13.refs_1_), channel_id=1, source_target_pairs={{8,0},{16,24},{9,1},{17,25},{10,2},{18,26},{11,3},{19,27},{12,4},{... | collective-permute-start | bytes 1179656 | tf_op jit(solution)/shard_map/ppermute | solution.py:274
  48.7 0.0 collective-permute-done.9.refs_3_.refs_8_.refs_9_
  48.7 0.0 collective-permute-done.14.refs_5_.refs_10_.refs_11_
  48.7 0.8 %collective-permute-done.15.refs_7_.refs_12_.refs_13_ = bf16[384,768]{1,0:T(8,128)(2,1)S(1)} collective-permute-done((bf16[384,768]{1,0:T(8,128)(2,1)S(1)}, bf16[384,768]{1,0:T(8,128)(2,1)S(1)}, u32[]{:S(2)}, u32[]{:S(2)}) %collective-permute-start.15) | collective-permute-done | bytes 589856 | tf_op jit(solution)/shard_map/ppermute | solution.py:261
  49.5 1.2 %pack.1 = bf16[320,768]{1,0:T(8,128)(2,1)S(1)} custom-call(s32[3]{0:T(128)S(1)} %pad_add_fusion.place, s32[1,1024]{1,0:T(1,128)S(1)} %get-tuple-element.38.code, bf16[512,768]{1,0:T(8,128)(2,1)S(1)} %copy-done.1, bf16[256,768]{1,0:T(8,128)(2,1)S(1)} %copy-done.2, bf16[384,768]{1,0:T(8,128)(2,1)S(1)} %collective-permute-done.8.refs_2_.refs_7_.refs_8_, ...), custom_call_target="tpu_custom_call" | custom-call | flops 1 | bytes 1 | tf_op jit(solution)/shard_map/pack/pallas_call | solution.py:248
  50.8 2.0 %collective-permute-start.16 = (bf16[64,768]{1,0:T(8,128)(2,1)S(1)}, bf16[64,768]{1,0:T(8,128)(2,1)S(1)}, u32[]{:S(2)}, u32[]{:S(2)}) collective-permute-start(bf16[64,768]{1,0:T(8,128)(2,1)S(1)} %get-tuple-element.57), channel_id=1, source_target_pairs={{0,8},{8,0},{16,24},{24,16},{1,9},{9,1},{17,25},{25,17},{2,10},{10... | collective-permute-start | bytes 294920 | tf_op jit(solution)/shard_map/ppermute | solution.py:261
  52.8 1.9 %collective-permute-start.17 = (bf16[64,768]{1,0:T(8,128)(2,1)S(1)}, bf16[64,768]{1,0:T(8,128)(2,1)S(1)}, u32[]{:S(2)}, u32[]{:S(2)}) collective-permute-start(bf16[64,768]{1,0:T(8,128)(2,1)S(1)} %get-tuple-element.59), channel_id=1, source_target_pairs={{0,16},{8,24},{16,0},{24,8},{1,17},{9,25},{17,1},{25,9},{2,18},{10... | collective-permute-start | bytes 294920 | tf_op jit(solution)/shard_map/ppermute | solution.py:261
  54.7 1.3 %collective-permute-start.18 = (bf16[64,768]{1,0:T(8,128)(2,1)S(1)}, bf16[64,768]{1,0:T(8,128)(2,1)S(1)}, u32[]{:S(2)}, u32[]{:S(2)}) collective-permute-start(bf16[64,768]{1,0:T(8,128)(2,1)S(1)} %get-tuple-element.58), channel_id=1, source_target_pairs={{0,24},{8,16},{16,8},{24,0},{1,25},{9,17},{17,9},{25,1},{2,26},{10... | collective-permute-start | bytes 294920 | tf_op jit(solution)/shard_map/ppermute | solution.py:261
  56.1 2.2 %score.5 = f32[2,2,128]{2,1,0:T(2,128)S(1)} custom-call(s32[3]{0:T(128)S(1)} %pad_add_fusion.place, bf16[256,768]{1,0:T(8,128)(2,1)S(1)} %collective-permute-done.refs_0_, f32[2,128]{1,0:T(2,128)S(1)} %bitcast.30, f32[1,3072]{1,0:T(1,128)S(1)} %get-tuple-element.60.refs_2_, f32[1,3072]{1,0:T(1,128)S(1)} %get-tuple-element.49.refs_3_.refs_4_, ...), custom_call_target="tpu_custom_call" | custom-call | flops 1 | bytes 1 | tf_op jit(solution)/shard_map/score/pallas_call | solution.py:248
  58.3 0.6 collective-permute-start.21
  58.9 2.2 %score.4 = f32[2,2,128]{2,1,0:T(2,128)S(1)} custom-call(s32[3]{0:T(128)S(1)} %pad_add_fusion.place, bf16[256,768]{1,0:T(8,128)(2,1)S(1)} %copy-done.3, f32[2,128]{1,0:T(2,128)S(1)} %bitcast.29, f32[1,3072]{1,0:T(1,128)S(1)} %get-tuple-element.63.refs_2_, f32[1,3072]{1,0:T(1,128)S(1)} %get-tuple-element.49.refs_3_.refs_4_, ...), custom_call_target="tpu_custom_call" | custom-call | flops 1 | bytes 1 | tf_op jit(solution)/shard_map/score/pallas_call | solution.py:248
  61.2 2.2 %score.6 = f32[2,2,128]{2,1,0:T(2,128)S(1)} custom-call(s32[3]{0:T(128)S(1)} %pad_add_fusion.place, bf16[256,768]{1,0:T(8,128)(2,1)S(1)} %collective-permute-done.12.refs_0_, bf16[256,768]{1,0:T(8,128)(2,1)S(1)} %collective-permute-done.13.refs_1_, f32[2,128]{1,0:T(2,128)S(1)} %bitcast.28, f32[1,3072]{1,0:T(1,128)S(1)} %get-tuple-element.62.refs_3_, ...), custom_call_target="tpu_custom_call" | custom-call | flops 1 | bytes 1 | tf_op jit(solution)/shard_map/score/pallas_call | solution.py:248
  63.4 3.1 %collective-permute-done.16 = bf16[64,768]{1,0:T(8,128)(2,1)S(1)} collective-permute-done((bf16[64,768]{1,0:T(8,128)(2,1)S(1)}, bf16[64,768]{1,0:T(8,128)(2,1)S(1)}, u32[]{:S(2)}, u32[]{:S(2)}) %collective-permute-start.16) | collective-permute-done | bytes 98336 | tf_op jit(solution)/shard_map/ppermute | solution.py:261
  66.5 1.4 %collective-permute-start.22 = (f32[2,2,128]{2,1,0:T(2,128)S(1)}, f32[2,2,128]{2,1,0:T(2,128)S(1)}, u32[]{:S(2)}, u32[]{:S(2)}) collective-permute-start(f32[2,2,128]{2,1,0:T(2,128)S(1)} %score.6), channel_id=1, source_target_pairs={{0,16},{8,24},{16,0},{24,8},{1,17},{9,25},{17,1},{25,9},{2,18},{10... | collective-permute-start | bytes 6152 | tf_op jit(solution)/shard_map/ppermute | solution.py:261
  67.9 0.0 collective-permute-done.17
  67.9 0.0 collective-permute-done.18
  67.9 0.0 collective-permute-done.19.refs_0_
  67.9 2.2 %score.7 = f32[2,2,128]{2,1,0:T(2,128)S(1)} custom-call(s32[3]{0:T(128)S(1)} %pad_add_fusion.place, bf16[256,768]{1,0:T(8,128)(2,1)S(1)} %collective-permute-done.19.refs_0_, bf16[256,768]{1,0:T(8,128)(2,1)S(1)} %collective-permute-done.1.refs_1_, f32[2,128]{1,0:T(2,128)S(1)} %bitcast.27, f32[1,3072]{1,0:T(1,128)S(1)} %get-tuple-element.61.refs_3_, ...), custom_call_target="tpu_custom_call" | custom-call | flops 1 | bytes 1 | tf_op jit(solution)/shard_map/score/pallas_call | solution.py:248
  70.1 2.0 %collective-permute-start.23 = (f32[2,2,128]{2,1,0:T(2,128)S(1)}, f32[2,2,128]{2,1,0:T(2,128)S(1)}, u32[]{:S(2)}, u32[]{:S(2)}) collective-permute-start(f32[2,2,128]{2,1,0:T(2,128)S(1)} %score.7), channel_id=1, source_target_pairs={{0,24},{8,16},{16,8},{24,0},{1,25},{9,17},{17,9},{25,1},{2,26},{10... | collective-permute-start | bytes 6152 | tf_op jit(solution)/shard_map/ppermute | solution.py:261
  72.1 0.1 collective-permute-start.20
  72.2 0.0 collective-permute-done.21
  72.2 0.0 collective-permute-done.22
  72.2 3.3 %collective-permute-done.23 = f32[2,2,128]{2,1,0:T(2,128)S(1)} collective-permute-done((f32[2,2,128]{2,1,0:T(2,128)S(1)}, f32[2,2,128]{2,1,0:T(2,128)S(1)}, u32[]{:S(2)}, u32[]{:S(2)}) %collective-permute-start.23) | collective-permute-done | bytes 2080 | tf_op jit(solution)/shard_map/ppermute | solution.py:261
  75.6 0.6 fusion.2
  76.2 0.0 collective-permute-done.20.refs_2_
  76.2 1.5 %apply.1 = bf16[512,768]{1,0:T(8,128)(2,1)} custom-call(s32[1,512]{1,0:T(1,128)S(1)} %get-tuple-element.36.target, s32[1,512]{1,0:T(1,128)S(1)} %get-tuple-element.37.refreshed, bf16[512,768]{1,0:T(8,128)(2,1)S(1)} %copy-done.1, bf16[128,768]{1,0:T(8,128)(2,1)S(1)} %slice.77.refs_0_, bf16[192,768]{1,0:T(8,128)(2,1)S(1)} %pad_maximum_fusion.refs_1_, ...), custom_call_target="tpu_custom_call" | custom-call | flops 1 | bytes 1 | tf_op jit(solution)/shard_map/apply/pallas_call | solution.py:248
  (31 shorter events, 0.3 us)
Async XLA Ops:
  0.6 17.9 %copy-start.6 = (s32[1,2048]{1,0:T(1,128)S(1)}, s32[1,2048]{1,0:T(1,128)}, u32[]{:S(2)}) copy-start(s32[1,2048]{1,0:T(1,128)} %param.11) | copy-start | bytes 24580
  0.7 0.7 copy-start.4
  0.7 0.7 copy-start.5
  1.4 1.1 %copy-start = (bf16[512,768]{1,0:T(8,128)(2,1)S(1)}, bf16[512,768]{1,0:T(8,128)(2,1)}, u32[]{:S(2)}) copy-start(bf16[512,768]{1,0:T(8,128)(2,1)} %refs_6_.7) | copy-start | bytes 2359300
  2.6 1.0 %copy-start.2 = (bf16[256,768]{1,0:T(8,128)(2,1)S(1)}, bf16[256,768]{1,0:T(8,128)(2,1)}, u32[]{:S(2)}) copy-start(bf16[256,768]{1,0:T(8,128)(2,1)} %refs_7_.3) | copy-start | bytes 1179652
  3.5 3.9 %copy-start.3 = (bf16[256,768]{1,0:T(8,128)(2,1)S(1)}, bf16[256,768]{1,0:T(8,128)(2,1)}, u32[]{:S(2)}) copy-start(bf16[256,768]{1,0:T(8,128)(2,1)} %refs_0_.3) | copy-start | bytes 1179652
  3.6 46.0 %copy-start.1 = (bf16[512,768]{1,0:T(8,128)(2,1)S(1)}, bf16[512,768]{1,0:T(8,128)(2,1)}, u32[]{:S(2)}) copy-start(bf16[512,768]{1,0:T(8,128)(2,1)} %refs_6_.7) | copy-start | bytes 2359300
  4.4 26.0 %collective-permute-start.8 = (bf16[384,768]{1,0:T(8,128)(2,1)S(1)}, bf16[384,768]{1,0:T(8,128)(2,1)S(1)}, u32[]{:S(2)}, u32[]{:S(2)}) collective-permute-start(bf16[384,768]{1,0:T(8,128)(2,1)S(1)} %get-tuple-element.40), channel_id=1, source_target_pairs={{0,2},{1,5},{2,0},{3,7},{4,6},{5,1},{6,4},{7,3},{8,10},{9,13},{10,... | collective-permute-start | bytes 1769480 | tf_op jit(solution)/shard_map/ppermute | solution.py:324
  7.4 23.0 %collective-permute-start = (bf16[256,768]{1,0:T(8,128)(2,1)S(1)}, bf16[256,768]{1,0:T(8,128)(2,1)S(1)}, u32[]{:S(2)}, u32[]{:S(2)}) collective-permute-start(bf16[256,768]{1,0:T(8,128)(2,1)S(1)} %copy-done.3), channel_id=1, source_target_pairs={{0,8},{8,0},{16,24},{24,16},{1,9},{9,1},{17,25},{25,17},{2,10},{10... | collective-permute-start | bytes 1179656 | tf_op jit(solution)/shard_map/ppermute | solution.py:261
  9.0 21.4 %collective-permute-start.1 = (bf16[256,768]{1,0:T(8,128)(2,1)S(1)}, bf16[256,768]{1,0:T(8,128)(2,1)S(1)}, u32[]{:S(2)}, u32[]{:S(2)}) collective-permute-start(bf16[256,768]{1,0:T(8,128)(2,1)S(1)} %copy-done.3), channel_id=1, source_target_pairs={{8,16},{16,8},{9,17},{17,9},{10,18},{18,10},{11,19},{19,11},{12,20... | collective-permute-start | bytes 1179656 | tf_op jit(solution)/shard_map/ppermute | solution.py:270
  9.7 8.9 %copy-start.7 = (s32[256]{0:T(256)S(1)}, s32[256]{0:T(256)}, u32[]{:S(2)}) copy-start(s32[256]{0:T(256)} %param.13) | copy-start | bytes 3076
  9.7 5.9 %collective-permute-start.2 = (f32[12,128]{1,0:T(8,128)S(1)}, f32[12,128]{1,0:T(8,128)S(1)}, u32[]{:S(2)}, u32[]{:S(2)}) collective-permute-start(f32[12,128]{1,0:T(8,128)S(1)} %get-tuple-element.30), channel_id=1, source_target_pairs={{0,2},{2,0},{4,6},{6,4},{1,3},{3,1},{5,7},{7,5},{8,10},{10,8},{12,... | collective-permute-start | bytes 18440 | tf_op jit(solution)/shard_map/ppermute | solution.py:261
  10.3 8.3 %collective-permute-start.3 = (f32[12,128]{1,0:T(8,128)S(1)}, f32[12,128]{1,0:T(8,128)S(1)}, u32[]{:S(2)}, u32[]{:S(2)}) collective-permute-start(f32[12,128]{1,0:T(8,128)S(1)} %get-tuple-element.30), channel_id=1, source_target_pairs={{0,4},{2,6},{4,0},{6,2},{1,5},{3,7},{5,1},{7,3},{8,12},{10,14},{12... | collective-permute-start | bytes 18440 | tf_op jit(solution)/shard_map/ppermute | solution.py:261
  15.5 4.6 %collective-permute-start.4 = (f32[12,128]{1,0:T(8,128)S(1)}, f32[12,128]{1,0:T(8,128)S(1)}, u32[]{:S(2)}, u32[]{:S(2)}) collective-permute-start(f32[12,128]{1,0:T(8,128)S(1)} %get-tuple-element.30), channel_id=1, source_target_pairs={{0,6},{2,4},{4,2},{6,0},{1,7},{3,5},{5,3},{7,1},{8,14},{10,12},{12... | collective-permute-start | bytes 18440 | tf_op jit(solution)/shard_map/ppermute | solution.py:261
  20.1 4.7 %collective-permute-start.5 = (f32[3328]{0:T(1024)S(1)}, f32[3328]{0:T(1024)S(1)}, u32[]{:S(2)}, u32[]{:S(2)}) collective-permute-start(f32[3328]{0:T(1024)S(1)} %pad_maximum_fusion.4), channel_id=1, source_target_pairs={{0,8},{8,0},{16,24},{24,16},{1,9},{9,1},{17,25},{25,17},{2,10},{10... | collective-permute-start | bytes 39944 | tf_op jit(solution)/shard_map/ppermute | solution.py:261
  22.4 5.6 %collective-permute-start.6 = (f32[3328]{0:T(1024)S(1)}, f32[3328]{0:T(1024)S(1)}, u32[]{:S(2)}, u32[]{:S(2)}) collective-permute-start(f32[3328]{0:T(1024)S(1)} %pad_maximum_fusion.4), channel_id=1, source_target_pairs={{0,16},{8,24},{16,0},{24,8},{1,17},{9,25},{17,1},{25,9},{2,18},{10... | collective-permute-start | bytes 39944 | tf_op jit(solution)/shard_map/ppermute | solution.py:261
  24.9 5.5 %collective-permute-start.7 = (f32[3328]{0:T(1024)S(1)}, f32[3328]{0:T(1024)S(1)}, u32[]{:S(2)}, u32[]{:S(2)}) collective-permute-start(f32[3328]{0:T(1024)S(1)} %pad_maximum_fusion.4), channel_id=1, source_target_pairs={{0,24},{8,16},{16,8},{24,0},{1,25},{9,17},{17,9},{25,1},{2,26},{10... | collective-permute-start | bytes 39944 | tf_op jit(solution)/shard_map/ppermute | solution.py:261
  30.4 11.8 %collective-permute-start.10 = (bf16[384,768]{1,0:T(8,128)(2,1)S(1)}, bf16[384,768]{1,0:T(8,128)(2,1)S(1)}, u32[]{:S(2)}, u32[]{:S(2)}) collective-permute-start(bf16[384,768]{1,0:T(8,128)(2,1)S(1)} %get-tuple-element.40), channel_id=1, source_target_pairs={{0,4},{1,3},{2,6},{3,1},{4,0},{5,7},{6,2},{7,5},{8,12},{9,11},{10,... | collective-permute-start | bytes 1769480 | tf_op jit(solution)/shard_map/ppermute | solution.py:360
  32.1 14.6 %collective-permute-start.11 = (bf16[384,768]{1,0:T(8,128)(2,1)S(1)}, bf16[384,768]{1,0:T(8,128)(2,1)S(1)}, u32[]{:S(2)}, u32[]{:S(2)}) collective-permute-start(bf16[384,768]{1,0:T(8,128)(2,1)S(1)} %collective-permute-done.8.refs_2_.refs_7_.refs_8_), channel_id=1, source_target_pairs={{0,4},{1,3},{2,6},{3,1},{4,0},{5,7},{6,2},{7,5},{8,12},{9,11},{10,... | collective-permute-start | bytes 1769480 | tf_op jit(solution)/shard_map/ppermute | solution.py:361
  32.5 9.7 %collective-permute-start.12 = (bf16[256,768]{1,0:T(8,128)(2,1)S(1)}, bf16[256,768]{1,0:T(8,128)(2,1)S(1)}, u32[]{:S(2)}, u32[]{:S(2)}) collective-permute-start(bf16[256,768]{1,0:T(8,128)(2,1)S(1)} %collective-permute-done.1.refs_1_), channel_id=1, source_target_pairs={{8,0},{16,24},{9,1},{17,25},{10,2},{18,26},{11,3},{19,27},{12,4},{... | collective-permute-start | bytes 1179656 | tf_op jit(solution)/shard_map/ppermute | solution.py:273
  33.8 8.4 %collective-permute-start.13 = (bf16[256,768]{1,0:T(8,128)(2,1)S(1)}, bf16[256,768]{1,0:T(8,128)(2,1)S(1)}, u32[]{:S(2)}, u32[]{:S(2)}) collective-permute-start(bf16[256,768]{1,0:T(8,128)(2,1)S(1)} %collective-permute-done.refs_0_), channel_id=1, source_target_pairs={{8,16},{16,8},{9,17},{17,9},{10,18},{18,10},{11,19},{19,11},{12,20... | collective-permute-start | bytes 1179656 | tf_op jit(solution)/shard_map/ppermute | solution.py:272
  34.5 14.2 %collective-permute-start.9 = (bf16[384,768]{1,0:T(8,128)(2,1)S(1)}, bf16[384,768]{1,0:T(8,128)(2,1)S(1)}, u32[]{:S(2)}, u32[]{:S(2)}) collective-permute-start(bf16[384,768]{1,0:T(8,128)(2,1)S(1)} %collective-permute-done.8.refs_2_.refs_7_.refs_8_), channel_id=1, source_target_pairs={{0,1},{1,0},{2,3},{3,2},{4,5},{5,4},{6,7},{7,6},{8,9},{9,8},{10,11... | collective-permute-start | bytes 1769480 | tf_op jit(solution)/shard_map/ppermute | solution.py:261
  46.7 2.1 %collective-permute-start.14 = (bf16[384,768]{1,0:T(8,128)(2,1)S(1)}, bf16[384,768]{1,0:T(8,128)(2,1)S(1)}, u32[]{:S(2)}, u32[]{:S(2)}) collective-permute-start(bf16[384,768]{1,0:T(8,128)(2,1)S(1)} %collective-permute-done.10.refs_4_.refs_9_.refs_10_), channel_id=1, source_target_pairs={{0,1},{1,0},{2,3},{3,2},{4,5},{5,4},{6,7},{7,6},{8,9},{9,8},{10,11... | collective-permute-start | bytes 1769480 | tf_op jit(solution)/shard_map/ppermute | solution.py:261
  46.7 2.8 %collective-permute-start.15 = (bf16[384,768]{1,0:T(8,128)(2,1)S(1)}, bf16[384,768]{1,0:T(8,128)(2,1)S(1)}, u32[]{:S(2)}, u32[]{:S(2)}) collective-permute-start(bf16[384,768]{1,0:T(8,128)(2,1)S(1)} %collective-permute-done.11.refs_6_.refs_11_.refs_12_), channel_id=1, source_target_pairs={{0,1},{1,0},{2,3},{3,2},{4,5},{5,4},{6,7},{7,6},{8,9},{9,8},{10,11... | collective-permute-start | bytes 1769480 | tf_op jit(solution)/shard_map/ppermute | solution.py:261
  47.2 20.7 %collective-permute-start.19 = (bf16[256,768]{1,0:T(8,128)(2,1)S(1)}, bf16[256,768]{1,0:T(8,128)(2,1)S(1)}, u32[]{:S(2)}, u32[]{:S(2)}) collective-permute-start(bf16[256,768]{1,0:T(8,128)(2,1)S(1)} %collective-permute-done.13.refs_1_), channel_id=1, source_target_pairs={{8,0},{16,24},{9,1},{17,25},{10,2},{18,26},{11,3},{19,27},{12,4},{... | collective-permute-start | bytes 1179656 | tf_op jit(solution)/shard_map/ppermute | solution.py:274
  50.8 15.7 %collective-permute-start.16 = (bf16[64,768]{1,0:T(8,128)(2,1)S(1)}, bf16[64,768]{1,0:T(8,128)(2,1)S(1)}, u32[]{:S(2)}, u32[]{:S(2)}) collective-permute-start(bf16[64,768]{1,0:T(8,128)(2,1)S(1)} %get-tuple-element.57), channel_id=1, source_target_pairs={{0,8},{8,0},{16,24},{24,16},{1,9},{9,1},{17,25},{25,17},{2,10},{10... | collective-permute-start | bytes 294920 | tf_op jit(solution)/shard_map/ppermute | solution.py:261
  52.8 15.1 %collective-permute-start.17 = (bf16[64,768]{1,0:T(8,128)(2,1)S(1)}, bf16[64,768]{1,0:T(8,128)(2,1)S(1)}, u32[]{:S(2)}, u32[]{:S(2)}) collective-permute-start(bf16[64,768]{1,0:T(8,128)(2,1)S(1)} %get-tuple-element.59), channel_id=1, source_target_pairs={{0,16},{8,24},{16,0},{24,8},{1,17},{9,25},{17,1},{25,9},{2,18},{10... | collective-permute-start | bytes 294920 | tf_op jit(solution)/shard_map/ppermute | solution.py:261
  54.7 13.2 %collective-permute-start.18 = (bf16[64,768]{1,0:T(8,128)(2,1)S(1)}, bf16[64,768]{1,0:T(8,128)(2,1)S(1)}, u32[]{:S(2)}, u32[]{:S(2)}) collective-permute-start(bf16[64,768]{1,0:T(8,128)(2,1)S(1)} %get-tuple-element.58), channel_id=1, source_target_pairs={{0,24},{8,16},{16,8},{24,0},{1,25},{9,17},{17,9},{25,1},{2,26},{10... | collective-permute-start | bytes 294920 | tf_op jit(solution)/shard_map/ppermute | solution.py:261
  58.3 13.9 %collective-permute-start.21 = (f32[2,2,128]{2,1,0:T(2,128)S(1)}, f32[2,2,128]{2,1,0:T(2,128)S(1)}, u32[]{:S(2)}, u32[]{:S(2)}) collective-permute-start(f32[2,2,128]{2,1,0:T(2,128)S(1)} %score.5), channel_id=1, source_target_pairs={{0,8},{8,0},{16,24},{24,16},{1,9},{9,1},{17,25},{25,17},{2,10},{10... | collective-permute-start | bytes 6152 | tf_op jit(solution)/shard_map/ppermute | solution.py:261
  66.5 5.7 %collective-permute-start.22 = (f32[2,2,128]{2,1,0:T(2,128)S(1)}, f32[2,2,128]{2,1,0:T(2,128)S(1)}, u32[]{:S(2)}, u32[]{:S(2)}) collective-permute-start(f32[2,2,128]{2,1,0:T(2,128)S(1)} %score.6), channel_id=1, source_target_pairs={{0,16},{8,24},{16,0},{24,8},{1,17},{9,25},{17,1},{25,9},{2,18},{10... | collective-permute-start | bytes 6152 | tf_op jit(solution)/shard_map/ppermute | solution.py:261
  70.1 5.4 %collective-permute-start.23 = (f32[2,2,128]{2,1,0:T(2,128)S(1)}, f32[2,2,128]{2,1,0:T(2,128)S(1)}, u32[]{:S(2)}, u32[]{:S(2)}) collective-permute-start(f32[2,2,128]{2,1,0:T(2,128)S(1)} %score.7), channel_id=1, source_target_pairs={{0,24},{8,16},{16,8},{24,0},{1,25},{9,17},{17,9},{25,1},{2,26},{10... | collective-permute-start | bytes 6152 | tf_op jit(solution)/shard_map/ppermute | solution.py:261
  72.1 4.0 %collective-permute-start.20 = (bf16[192,768]{1,0:T(8,128)(2,1)S(1)}, bf16[192,768]{1,0:T(8,128)(2,1)S(1)}, u32[]{:S(2)}, u32[]{:S(2)}) collective-permute-start(bf16[192,768]{1,0:T(8,128)(2,1)S(1)} %pad_maximum_fusion.refs_1_), channel_id=1, source_target_pairs={{0,1},{1,0},{2,3},{3,2},{4,5},{5,4},{6,7},{7,6},{8,9},{9,8},{10,11... | collective-permute-start | bytes 884744 | tf_op jit(solution)/shard_map/ppermute | solution.py:261

commit v19 on v15

--- a/solution.py
+++ b/solution.py
@@ -87,7 +87,7 @@
 
 
 def meta_kernel(
-    place, ref_ids, neg, log_weight, ages, lw_out, row_out, code_out, target_out, own_out, ages_out,
+    place, ref_ids, neg, log_weight, lw_out, row_out, pack_out, apply_out, own_out, target_out,
     *, rows_dev, refresh_dev, cap, replicas
 ):
     outer, inner, core = place[0], place[1], place[2]
@@ -107,7 +107,6 @@
     row_out[:, :plane_rows] = jnp.where(refreshed, -1, table_ids).astype(jnp.float32)
     row_out[:, plane_rows:] = plane_ids.astype(jnp.float32)
     own_out[...] = refreshed[:, :rows_dev].astype(jnp.int32)
-    ages_out[...] = jnp.where(refreshed[:, :rows_dev], 0, ages[...])
     weights = jnp.where(refreshed, MASKED, log_weight[...])
     weights = jnp.concatenate([weights, jnp.zeros((1, plane_refresh), jnp.float32)], axis=1)
     for group in range(planes):
@@ -143,7 +142,9 @@
         for part in range(replicas):
             first = base + part * (planes - 1) * owners_plane * share
             target_out[:, first : first + share] = target[:, part * share : (part + 1) * share]
-    code_out[...] = jnp.concatenate(codes, axis=1)
+    pack_out[...] = one_hot(jnp.concatenate(codes, axis=1), pack_out.shape[0])
+    rows = lax.broadcasted_iota(jnp.int32, apply_out.shape, 0)
+    apply_out[...] = jnp.where(rows == target_out[...], 1.0, 0.0)
 
 
 def piece_offset(place, piece):
@@ -156,28 +157,27 @@
     return pl.multiple_of(column, size)
 
 
-def pack_kernel(place, code, *refs, pieces):
-    *buffers, out = refs
-    selects = [
-        one_hot(code[:, pl.ds(piece_offset(place, column), size)], out.shape[0]) for _, _, size, column in pieces
-    ]
-    values = [buffers[source][start : start + size, :] for source, start, size, _ in pieces]
-    select, values = jnp.concatenate(selects, axis=1), jnp.concatenate(values, axis=0)
-    out[...] = lax.dot_general(select, values, NN, preferred_element_type=jnp.float32).astype(jnp.bfloat16)
-
-
-def apply_kernel(target, refreshed, table, *refs):
-    *arrived, out = refs
-    values = jnp.concatenate([block[...] for block in arrived], axis=0)
-    rows = lax.broadcasted_iota(jnp.int32, (out.shape[0], values.shape[0]), 0)
-    chosen = jnp.where(rows == target[...], 1.0, 0.0).astype(jnp.bfloat16)
-    fresh = lax.dot_general(chosen, values, NN, preferred_element_type=jnp.float32)
-    for top in range(0, out.shape[0], LANES):
-        part = slice(top, top + LANES)
-        hit = to_lanes(refreshed[:, part].astype(jnp.float32)) > 0.5
-        for left in range(0, out.shape[1], LANES):
-            cols = slice(left, left + LANES)
-            out[part, cols] = jnp.where(hit, fresh[part, cols], table[part, cols].astype(jnp.float32)).astype(jnp.bfloat16)
+def pack_kernel(place, select, *refs, pieces):
+    out = refs[-1]
+    total = jnp.zeros(out.shape, jnp.float32)
+    for source, start, size, column in pieces:
+        columns = pl.ds(piece_offset(place, column), size)
+        total += lax.dot_general(
+            select[:, columns], refs[source][start : start + size, :], NN, preferred_element_type=jnp.float32
+        )
+    out[...] = total.astype(jnp.bfloat16)
+
+
+def apply_kernel(select, table, *refs):
+    out = refs[-1]
+    fresh = jnp.zeros(out.shape, jnp.float32)
+    first = 0
+    for arrived in refs[:-1]:
+        part = select[:, first : first + arrived.shape[0]].astype(jnp.bfloat16)
+        fresh += lax.dot_general(part, arrived[...], NN, preferred_element_type=jnp.float32)
+        first += arrived.shape[0]
+    hit = jnp.sum(select[...], axis=1, keepdims=True) > 0.5
+    out[...] = jnp.where(hit, fresh, table[...].astype(jnp.float32)).astype(jnp.bfloat16)
 
 
 def to_lanes(row):
@@ -288,7 +288,8 @@
     plane_rows = owners_plane * rows_dev
     plane_refresh = owners_plane * refresh_dev
     all_rows = plane_rows + plane_refresh
-    cap = max(2, (2 * refresh_dev + owners - 1) // owners)
+    cap_each = max(2, (2 * refresh_dev + owners - 1) // owners)
+    cap = owners_plane * cap_each
     share = cap // replicas
     table_half, fresh_half = rows_dev // replicas, refresh_dev // replicas
     bf16, f32 = jnp.bfloat16, jnp.float32
@@ -322,36 +323,33 @@
     neg_line = lines[:, plane_refresh : plane_refresh + list_size].astype(jnp.int32)
     positive = lines[:, plane_refresh + list_size :].reshape(planes, -1, LANES)
 
-    own_slots, part_slots = owners_plane * cap, owners_plane * share
-    lw, row_ids, code, target, own, new_ages = call(
+    lw, row_ids, pack, apply_to, own = call(
         meta_kernel,
         "meta",
         [
             jax.ShapeDtypeStruct((planes, all_rows), f32),
             jax.ShapeDtypeStruct((1, all_rows), f32),
-            jax.ShapeDtypeStruct((1, plane_refresh), jnp.int32),
-            jax.ShapeDtypeStruct((1, planes * own_slots), jnp.int32),
-            jax.ShapeDtypeStruct((1, rows_dev), jnp.int32),
+            jax.ShapeDtypeStruct((cap + (planes - 1) * share, plane_refresh), bf16),
+            jax.ShapeDtypeStruct((rows_dev, planes * cap), f32),
             jax.ShapeDtypeStruct((1, rows_dev), jnp.int32),
         ],
         place,
         ref_all,
         neg_line,
         log_weight_plane,
-        ages.reshape(1, -1),
         rows_dev=rows_dev,
+        scratch=[pltpu.VMEM((1, planes * cap), jnp.int32)],
         refresh_dev=refresh_dev,
-        cap=cap,
+        cap=cap_each,
         replicas=replicas,
     )
-    new_ages = new_ages.reshape(rows_dev)
+    new_ages = jnp.where(own.reshape(rows_dev) > 0, 0, ages)
 
     if replicas == 2 and owners_plane == 4:
         axes = ("inner", "query")
         first = [(2 * i + c, 2 * (i ^ (1 + c)) + c) for i in range(4) for c in range(2)]
         second = [(2 * i + c, 2 * (i ^ (2 - c)) + c) for i in range(4) for c in range(2)]
         near = lax.ppermute(rows_half, axes, first)
-        near, rows_half, _ = lax.optimization_barrier((near, rows_half, metas))
         side = lax.ppermute(rows_half, axes, second)
         far = lax.ppermute(near, axes, second)
         buffers = [table, fresh_rows]
@@ -378,21 +376,14 @@
         return [(a, b, c, (d[0] + columns, *d[1:])) for a, b, c, d in pieces]
 
     (packed,) = call(
-        pack_kernel,
-        "pack",
-        [jax.ShapeDtypeStruct((own_slots + (planes - 1) * part_slots, width), bf16)],
-        place,
-        code,
-        *buffers,
-        pieces=fresh_pieces,
+        pack_kernel, "pack", [jax.ShapeDtypeStruct((pack.shape[0], width), bf16)], place, pack, *buffers, pieces=fresh_pieces
     )
     parts = []
     for s in range(1, planes):
-        first = own_slots + (s - 1) * part_slots
-        parts.append(swap(packed[first : first + part_slots], "outer", s))
-    parts, *given = lax.optimization_barrier((jnp.concatenate(parts), *got_queries[-1]))
-    got_queries[-1] = tuple(given)
-    arrived = [packed[:own_slots], parts] + [swap(parts, "query", flip) for flip in range(1, replicas)]
+        first = cap + (s - 1) * share
+        parts.append(swap(packed[first : first + share], "outer", s))
+    parts = jnp.concatenate(parts)
+    arrived = [packed[:cap], parts] + [swap(parts, "query", flip) for flip in range(1, replicas)]
 
     pieces = table_pieces + shift(fresh_pieces, plane_rows)
     mine = None
@@ -416,7 +407,7 @@
             partial = swap(partial, "outer", s)
         mine = partial if mine is None else mine + partial
     (new_table,) = call(
-        apply_kernel, "apply", [jax.ShapeDtypeStruct(table.shape, bf16)], None, target, own, table, *arrived
+        apply_kernel, "apply", [jax.ShapeDtypeStruct(table.shape, bf16)], None, apply_to, table, *arrived
     )
     loss = (jnp.log2(mine[0]) - mine[1]) * math.log(2.0)
     return new_table, new_ages, loss.reshape(query_count)

time: 73.4 us -> 67.3 us (0.917)
  waiting for transfers between devices: 18.6 us -> 14.3 us
  starting transfers between devices: 33.5 us -> 29.6 us
  Pallas kernels: 16.4 us -> 17.8 us
    ppermute x17, starting transfers between devices: 24.3 us -> 20.4 us  [swap(): lax.ppermute(values, axis, [(i, i ^ flip) for i in range(lax.axis_size(ax...]
    ppermute x17, waiting for transfers between devices: 17.9 us -> 14.3 us  [swap(): lax.ppermute(values, axis, [(i, i ^ flip) for i in range(lax.axis_size(ax...]
    pallas_call x8, Pallas kernels: 16.4 us -> 17.8 us  [call(): pl.pallas_call(functools.partial(kernel, **options), out_shape=tuple(outs...]
    unnamed x16 -> x20, local copies, waits for them, and re-layouts: 2.84 us -> 2.86 us
  transfers between devices with their start and end apart: 24 -> 24, of which waited for: 9 -> 8; matrix products, arithmetic and copies ran while one was open for 1% -> 2% of each run, Pallas kernels for 19% -> 23%
where the time goes in v19:
time: 67.3 us; the launch traced here: 67 us
  starting transfers between devices  29.6 us (44%)
  Pallas kernels  17.8 us (26%)
  waiting for transfers between devices  14.3 us (21%)
  local copies, waits for them, and re-layouts  2.95 us (4%)
  other arithmetic  1.41 us (2%)
  between operations  0.94 us (1%)
    ppermute x17, starting transfers between devices, swap(): lax.ppermute(values, axis, [(i, i ^ flip) for i in range(lax.axis_size(ax...  20.4 us
    pallas_call x8, Pallas kernels, call(): pl.pallas_call(functools.partial(kernel, **options), out_shape=tuple(outs...  17.8 us
    ppermute x17, waiting for transfers between devices, swap(): lax.ppermute(values, axis, [(i, i ^ flip) for i in range(lax.axis_size(ax...  14.3 us
    ppermute x1, starting transfers between devices, on_device(): near = lax.ppermute(rows_half, axes, first)  3 us
    unnamed x20, local copies, waits for them, and re-layouts  2.86 us
    ppermute x1, starting transfers between devices, on_device(): far = lax.ppermute(near, axes, second)  1.52 us
    ppermute x1, starting transfers between devices, gather_line(): last = lax.ppermute(from_end, 'outer', outward)  1.47 us
  transfers between devices with their start and end apart: 24, of which 8 were waited for; matrix products, arithmetic and copies ran while one was open for 2% of the time, Pallas kernels for 23%

profile of v19, /device:TPU:0, one launch (start us, length us, event | category | flops | bytes accessed | tf_op | source)
XLA Modules:
  0.0 67.0 jit_solution(2668883794057911343)
XLA Ops:
  0.6 0.1 pad_add_fusion.place
  0.7 0.7 %copy-done.5 = s32[512]{0:T(512)S(1)} copy-done((s32[512]{0:T(512)S(1)}, s32[512]{0:T(512)}, u32[]{:S(2)}) %copy-start.5) | copy-done | bytes 2072
  1.4 0.0 copy-done.6
  1.4 1.1 %copy-done = bf16[512,768]{1,0:T(8,128)(2,1)S(1)} copy-done((bf16[512,768]{1,0:T(8,128)(2,1)S(1)}, bf16[512,768]{1,0:T(8,128)(2,1)}, u32[]{:S(2)}) %copy-start) | copy-done | bytes 786456
  2.6 1.0 %copy-done.2 = bf16[256,768]{1,0:T(8,128)(2,1)S(1)} copy-done((bf16[256,768]{1,0:T(8,128)(2,1)S(1)}, bf16[256,768]{1,0:T(8,128)(2,1)}, u32[]{:S(2)}) %copy-start.2) | copy-done | bytes 393240
  3.6 0.8 %prep.1 = (bf16[384,768]{1,0:T(8,128)(2,1)S(1)}, f32[12,128]{1,0:T(8,128)S(1)}) custom-call(s32[3]{0:T(128)S(1)} %pad_add_fusion.place, bf16[512,768]{1,0:T(8,128)(2,1)S(1)} %copy-done, bf16[256,768]{1,0:T(8,128)(2,1)S(1)} %copy-done.2, s32[4,128]{1,0:T(4,128)S(1)} %bitcast.23, s32[2,128]{1,0:T(2,128)S(1)} %bitcast.28), custom_call_target="tpu_custom_call" | custom-call | flops 1 | bytes 1 | tf_op jit(solution)/shard_map/prep/pallas_call | solution.py:248
  4.4 3.0 %collective-permute-start.8 = (bf16[384,768]{1,0:T(8,128)(2,1)S(1)}, bf16[384,768]{1,0:T(8,128)(2,1)S(1)}, u32[]{:S(2)}, u32[]{:S(2)}) collective-permute-start(bf16[384,768]{1,0:T(8,128)(2,1)S(1)} %get-tuple-element.17), channel_id=1, source_target_pairs={{0,2},{1,5},{2,0},{3,7},{4,6},{5,1},{6,4},{7,3},{8,10},{9,13},{10,... | collective-permute-start | bytes 1769480 | tf_op jit(solution)/shard_map/ppermute | solution.py:352
  7.4 0.0 copy-done.4
  7.4 1.6 %collective-permute-start = (bf16[256,768]{1,0:T(8,128)(2,1)S(1)}, bf16[256,768]{1,0:T(8,128)(2,1)S(1)}, u32[]{:S(2)}, u32[]{:S(2)}) collective-permute-start(bf16[256,768]{1,0:T(8,128)(2,1)S(1)} %copy-done.4), channel_id=1, source_target_pairs={{0,8},{8,0},{16,24},{24,16},{1,9},{9,1},{17,25},{25,17},{2,10},{10... | collective-permute-start | bytes 1179656 | tf_op jit(solution)/shard_map/ppermute | solution.py:261
  9.0 0.7 %collective-permute-start.1 = (bf16[256,768]{1,0:T(8,128)(2,1)S(1)}, bf16[256,768]{1,0:T(8,128)(2,1)S(1)}, u32[]{:S(2)}, u32[]{:S(2)}) collective-permute-start(bf16[256,768]{1,0:T(8,128)(2,1)S(1)} %copy-done.4), channel_id=1, source_target_pairs={{8,16},{16,8},{9,17},{17,9},{10,18},{18,10},{11,19},{19,11},{12,20... | collective-permute-start | bytes 1179656 | tf_op jit(solution)/shard_map/ppermute | solution.py:270
  9.7 0.6 collective-permute-start.2
  10.3 1.5 %collective-permute-start.3 = (f32[12,128]{1,0:T(8,128)S(1)}, f32[12,128]{1,0:T(8,128)S(1)}, u32[]{:S(2)}, u32[]{:S(2)}) collective-permute-start(f32[12,128]{1,0:T(8,128)S(1)} %get-tuple-element.13), channel_id=1, source_target_pairs={{0,4},{2,6},{4,0},{6,2},{1,5},{3,7},{5,1},{7,3},{8,12},{10,14},{12... | collective-permute-start | bytes 18440 | tf_op jit(solution)/shard_map/ppermute | solution.py:261
  11.8 3.7 %collective-permute-done.2 = f32[12,128]{1,0:T(8,128)S(1)} collective-permute-done((f32[12,128]{1,0:T(8,128)S(1)}, f32[12,128]{1,0:T(8,128)S(1)}, u32[]{:S(2)}, u32[]{:S(2)}) %collective-permute-start.2) | collective-permute-done | bytes 6176 | tf_op jit(solution)/shard_map/ppermute | solution.py:261
  15.5 3.0 %collective-permute-start.4 = (f32[12,128]{1,0:T(8,128)S(1)}, f32[12,128]{1,0:T(8,128)S(1)}, u32[]{:S(2)}, u32[]{:S(2)}) collective-permute-start(f32[12,128]{1,0:T(8,128)S(1)} %get-tuple-element.13), channel_id=1, source_target_pairs={{0,6},{2,4},{4,2},{6,0},{1,7},{3,5},{5,3},{7,1},{8,14},{10,12},{12... | collective-permute-start | bytes 18440 | tf_op jit(solution)/shard_map/ppermute | solution.py:261
  18.6 0.0 collective-permute-done.3
  18.6 0.6 collective-permute-start.10
  19.1 0.0 collective-permute-done.8.refs_2_.refs_7_.refs_8_
  19.1 1.5 %collective-permute-start.12 = (bf16[384,768]{1,0:T(8,128)(2,1)S(1)}, bf16[384,768]{1,0:T(8,128)(2,1)S(1)}, u32[]{:S(2)}, u32[]{:S(2)}) collective-permute-start(bf16[384,768]{1,0:T(8,128)(2,1)S(1)} %collective-permute-done.8.refs_2_.refs_7_.refs_8_), channel_id=1, source_target_pairs={{0,4},{1,3},{2,6},{3,1},{4,0},{5,7},{6,2},{7,5},{8,12},{9,11},{10,... | collective-permute-start | bytes 1769480 | tf_op jit(solution)/shard_map/ppermute | solution.py:354
  20.7 0.0 collective-permute-done.4
  20.7 0.0 collective-permute-done.refs_0_
  20.7 0.0 collective-permute-done.1.refs_1_
  20.7 1.9 %collective-permute-start.5 = (f32[3328]{0:T(1024)S(1)}, f32[3328]{0:T(1024)S(1)}, u32[]{:S(2)}, u32[]{:S(2)}) collective-permute-start(f32[3328]{0:T(1024)S(1)} %pad_maximum_fusion.3), channel_id=1, source_target_pairs={{0,8},{8,0},{16,24},{24,16},{1,9},{9,1},{17,25},{25,17},{2,10},{10... | collective-permute-start | bytes 39944 | tf_op jit(solution)/shard_map/ppermute | solution.py:261
  22.6 2.4 %collective-permute-start.6 = (f32[3328]{0:T(1024)S(1)}, f32[3328]{0:T(1024)S(1)}, u32[]{:S(2)}, u32[]{:S(2)}) collective-permute-start(f32[3328]{0:T(1024)S(1)} %pad_maximum_fusion.3), channel_id=1, source_target_pairs={{0,16},{8,24},{16,0},{24,8},{1,17},{9,25},{17,1},{25,9},{2,18},{10... | collective-permute-start | bytes 39944 | tf_op jit(solution)/shard_map/ppermute | solution.py:261
  25.0 0.2 collective-permute-start.7
  25.3 0.0 collective-permute-done.5
  25.3 0.7 %collective-permute-start.20 = (bf16[256,768]{1,0:T(8,128)(2,1)S(1)}, bf16[256,768]{1,0:T(8,128)(2,1)S(1)}, u32[]{:S(2)}, u32[]{:S(2)}) collective-permute-start(bf16[256,768]{1,0:T(8,128)(2,1)S(1)} %collective-permute-done.refs_0_), channel_id=1, source_target_pairs={{8,16},{16,8},{9,17},{17,9},{10,18},{18,10},{11,19},{19,11},{12,20... | collective-permute-start | bytes 1179656 | tf_op jit(solution)/shard_map/ppermute | solution.py:272
  26.0 1.3 %collective-permute-done.6 = f32[3328]{0:T(1024)S(1)} collective-permute-done((f32[3328]{0:T(1024)S(1)}, f32[3328]{0:T(1024)S(1)}, u32[]{:S(2)}, u32[]{:S(2)}) %collective-permute-start.6) | collective-permute-done | bytes 13344 | tf_op jit(solution)/shard_map/ppermute | solution.py:261
  27.3 1.3 %collective-permute-start.19 = (bf16[256,768]{1,0:T(8,128)(2,1)S(1)}, bf16[256,768]{1,0:T(8,128)(2,1)S(1)}, u32[]{:S(2)}, u32[]{:S(2)}) collective-permute-start(bf16[256,768]{1,0:T(8,128)(2,1)S(1)} %collective-permute-done.1.refs_1_), channel_id=1, source_target_pairs={{8,0},{16,24},{9,1},{17,25},{10,2},{18,26},{11,3},{19,27},{12,4},{... | collective-permute-start | bytes 1179656 | tf_op jit(solution)/shard_map/ppermute | solution.py:273
  28.6 2.1 %collective-permute-done.7 = f32[3328]{0:T(1024)S(1)} collective-permute-done((f32[3328]{0:T(1024)S(1)}, f32[3328]{0:T(1024)S(1)}, u32[]{:S(2)}, u32[]{:S(2)}) %collective-permute-start.7) | collective-permute-done | bytes 13344 | tf_op jit(solution)/shard_map/ppermute | solution.py:261
  30.8 4.4 %meta.1 = (f32[4,3072]{1,0:T(4,128)S(1)}, f32[1,3072]{1,0:T(1,128)S(1)}, bf16[320,1024]{1,0:T(8,128)(2,1)S(1)}, f32[512,512]{1,0:T(8,128)S(1)}, s32[1,512]{1,0:T(1,128)S(1)}) custom-call(s32[3]{0:T(128)S(1)} %pad_add_fusion.place, s32[4,1024]{1,0:T(4,128)S(1)} %maximum_convert_fusion.ref_ids, s32[4,2048]{1,0:T(4,128)S(1)} %fusion.neg, f32[1,2048]{1,0:T(1,128)S(1)} %bitcast.22), custom_call_target="tpu_custom_call" | custom-call | flops 1 | bytes 1 | tf_op jit(solution)/shard_map/meta/pallas_call | solution.py:248
  35.2 0.1 collective-permute-start.9
  35.3 0.0 collective-permute-done.10.refs_4_.refs_9_.refs_10_
  35.3 0.5 collective-permute-start.11
  35.8 0.0 collective-permute-done.12.refs_6_.refs_11_.refs_12_
  35.8 0.1 collective-permute-start.13
  36.0 0.0 collective-permute-done.20.refs_1_
  36.0 1.5 %collective-permute-start.22 = (bf16[256,768]{1,0:T(8,128)(2,1)S(1)}, bf16[256,768]{1,0:T(8,128)(2,1)S(1)}, u32[]{:S(2)}, u32[]{:S(2)}) collective-permute-start(bf16[256,768]{1,0:T(8,128)(2,1)S(1)} %collective-permute-done.20.refs_1_), channel_id=1, source_target_pairs={{8,0},{16,24},{9,1},{17,25},{10,2},{18,26},{11,3},{19,27},{12,4},{... | collective-permute-start | bytes 1179656 | tf_op jit(solution)/shard_map/ppermute | solution.py:274
  37.5 0.0 collective-permute-done.9.refs_3_.refs_8_.refs_9_
  37.5 0.7 collective-permute-done.11.refs_5_.refs_10_.refs_11_
  38.1 0.8 %collective-permute-done.13.refs_7_.refs_12_.refs_13_ = bf16[384,768]{1,0:T(8,128)(2,1)S(1)} collective-permute-done((bf16[384,768]{1,0:T(8,128)(2,1)S(1)}, bf16[384,768]{1,0:T(8,128)(2,1)S(1)}, u32[]{:S(2)}, u32[]{:S(2)}) %collective-permute-start.13) | collective-permute-done | bytes 589856 | tf_op jit(solution)/shard_map/ppermute | solution.py:261
  39.0 1.6 %pack.1 = bf16[320,768]{1,0:T(8,128)(2,1)S(1)} custom-call(s32[3]{0:T(128)S(1)} %pad_add_fusion.place, bf16[320,1024]{1,0:T(8,128)(2,1)S(1)} %get-tuple-element.16.select, bf16[512,768]{1,0:T(8,128)(2,1)S(1)} %copy-done.1, bf16[256,768]{1,0:T(8,128)(2,1)S(1)} %copy-done.3, bf16[384,768]{1,0:T(8,128)(2,1)S(1)} %collective-permute-done.8.refs_2_.refs_7_.refs_8_, ...), custom_call_target="tpu_custom_call" | custom-call | flops 1 | bytes 1 | tf_op jit(solution)/shard_map/pack/pallas_call | solution.py:248
  40.6 1.3 %collective-permute-start.14 = (bf16[64,768]{1,0:T(8,128)(2,1)S(1)}, bf16[64,768]{1,0:T(8,128)(2,1)S(1)}, u32[]{:S(2)}, u32[]{:S(2)}) collective-permute-start(bf16[64,768]{1,0:T(8,128)(2,1)S(1)} %get-tuple-element.25), channel_id=1, source_target_pairs={{0,8},{8,0},{16,24},{24,16},{1,9},{9,1},{17,25},{25,17},{2,10},{10... | collective-permute-start | bytes 294920 | tf_op jit(solution)/shard_map/ppermute | solution.py:261
  41.9 0.6 broadcast_select_fusion
  42.5 0.0 collective-permute-done.19.refs_0_
  42.5 2.3 %score.5 = f32[2,2,128]{2,1,0:T(2,128)S(1)} custom-call(s32[3]{0:T(128)S(1)} %pad_add_fusion.place, bf16[256,768]{1,0:T(8,128)(2,1)S(1)} %collective-permute-done.19.refs_0_, bf16[256,768]{1,0:T(8,128)(2,1)S(1)} %collective-permute-done.20.refs_1_, f32[2,128]{1,0:T(2,128)S(1)} %bitcast.27, f32[1,3072]{1,0:T(1,128)S(1)} %get-tuple-element.26.refs_3_, ...), custom_call_target="tpu_custom_call" | custom-call | flops 1 | bytes 1 | tf_op jit(solution)/shard_map/score/pallas_call | solution.py:248
  44.8 1.1 %collective-permute-start.21 = (f32[2,2,128]{2,1,0:T(2,128)S(1)}, f32[2,2,128]{2,1,0:T(2,128)S(1)}, u32[]{:S(2)}, u32[]{:S(2)}) collective-permute-start(f32[2,2,128]{2,1,0:T(2,128)S(1)} %score.5), channel_id=1, source_target_pairs={{0,16},{8,24},{16,0},{24,8},{1,17},{9,25},{17,1},{25,9},{2,18},{10... | collective-permute-start | bytes 6152 | tf_op jit(solution)/shard_map/ppermute | solution.py:261
  46.0 2.3 %score.4 = f32[2,2,128]{2,1,0:T(2,128)S(1)} custom-call(s32[3]{0:T(128)S(1)} %pad_add_fusion.place, bf16[256,768]{1,0:T(8,128)(2,1)S(1)} %collective-permute-done.refs_0_, f32[2,128]{1,0:T(2,128)S(1)} %bitcast.26, f32[1,3072]{1,0:T(1,128)S(1)} %get-tuple-element.29.refs_2_, f32[1,3072]{1,0:T(1,128)S(1)} %get-tuple-element.21.refs_3_.refs_4_, ...), custom_call_target="tpu_custom_call" | custom-call | flops 1 | bytes 1 | tf_op jit(solution)/shard_map/score/pallas_call | solution.py:248
  48.3 2.1 %collective-permute-start.18 = (f32[2,2,128]{2,1,0:T(2,128)S(1)}, f32[2,2,128]{2,1,0:T(2,128)S(1)}, u32[]{:S(2)}, u32[]{:S(2)}) collective-permute-start(f32[2,2,128]{2,1,0:T(2,128)S(1)} %score.4), channel_id=1, source_target_pairs={{0,8},{8,0},{16,24},{24,16},{1,9},{9,1},{17,25},{25,17},{2,10},{10... | collective-permute-start | bytes 6152 | tf_op jit(solution)/shard_map/ppermute | solution.py:261
  50.3 0.0 collective-permute-done.22.refs_0_
  50.3 2.3 %score.6 = f32[2,2,128]{2,1,0:T(2,128)S(1)} custom-call(s32[3]{0:T(128)S(1)} %pad_add_fusion.place, bf16[256,768]{1,0:T(8,128)(2,1)S(1)} %collective-permute-done.22.refs_0_, bf16[256,768]{1,0:T(8,128)(2,1)S(1)} %collective-permute-done.1.refs_1_, f32[2,128]{1,0:T(2,128)S(1)} %bitcast.25, f32[1,3072]{1,0:T(1,128)S(1)} %get-tuple-element.28.refs_3_, ...), custom_call_target="tpu_custom_call" | custom-call | flops 1 | bytes 1 | tf_op jit(solution)/shard_map/score/pallas_call | solution.py:248
  52.6 2.1 %collective-permute-start.23 = (f32[2,2,128]{2,1,0:T(2,128)S(1)}, f32[2,2,128]{2,1,0:T(2,128)S(1)}, u32[]{:S(2)}, u32[]{:S(2)}) collective-permute-start(f32[2,2,128]{2,1,0:T(2,128)S(1)} %score.6), channel_id=1, source_target_pairs={{0,24},{8,16},{16,8},{24,0},{1,25},{9,17},{17,9},{25,1},{2,26},{10... | collective-permute-start | bytes 6152 | tf_op jit(solution)/shard_map/ppermute | solution.py:261
  54.7 0.0 collective-permute-start.15
  54.7 2.3 %score.7 = f32[2,2,128]{2,1,0:T(2,128)S(1)} custom-call(s32[3]{0:T(128)S(1)} %pad_add_fusion.place, bf16[256,768]{1,0:T(8,128)(2,1)S(1)} %copy-done.4, f32[2,128]{1,0:T(2,128)S(1)} %bitcast.24, f32[1,3072]{1,0:T(1,128)S(1)} %get-tuple-element.27.refs_2_, f32[1,3072]{1,0:T(1,128)S(1)} %get-tuple-element.21.refs_3_.refs_4_, ...), custom_call_target="tpu_custom_call" | custom-call | flops 1 | bytes 1 | tf_op jit(solution)/shard_map/score/pallas_call | solution.py:248
  57.0 0.0 collective-permute-done.14
  57.1 1.9 %collective-permute-start.16 = (bf16[64,768]{1,0:T(8,128)(2,1)S(1)}, bf16[64,768]{1,0:T(8,128)(2,1)S(1)}, u32[]{:S(2)}, u32[]{:S(2)}) collective-permute-start(bf16[64,768]{1,0:T(8,128)(2,1)S(1)} %get-tuple-element.23), channel_id=1, source_target_pairs={{0,24},{8,16},{16,8},{24,0},{1,25},{9,17},{17,9},{25,1},{2,26},{10... | collective-permute-start | bytes 294920 | tf_op jit(solution)/shard_map/ppermute | solution.py:261
  58.9 3.3 %collective-permute-done.15 = bf16[64,768]{1,0:T(8,128)(2,1)S(1)} collective-permute-done((bf16[64,768]{1,0:T(8,128)(2,1)S(1)}, bf16[64,768]{1,0:T(8,128)(2,1)S(1)}, u32[]{:S(2)}, u32[]{:S(2)}) %collective-permute-start.15) | collective-permute-done | bytes 98336 | tf_op jit(solution)/shard_map/ppermute | solution.py:261
  62.2 1.4 %collective-permute-done.16 = bf16[64,768]{1,0:T(8,128)(2,1)S(1)} collective-permute-done((bf16[64,768]{1,0:T(8,128)(2,1)S(1)}, bf16[64,768]{1,0:T(8,128)(2,1)S(1)}, u32[]{:S(2)}, u32[]{:S(2)}) %collective-permute-start.16) | collective-permute-done | bytes 98336 | tf_op jit(solution)/shard_map/ppermute | solution.py:261
  63.7 0.1 collective-permute-start.17
  63.7 0.0 collective-permute-done.21
  63.7 0.0 collective-permute-done.18
  63.8 0.0 collective-permute-done.23
  63.8 0.6 fusion.2
  64.4 0.9 %collective-permute-done.17.refs_2_ = bf16[192,768]{1,0:T(8,128)(2,1)S(1)} collective-permute-done((bf16[192,768]{1,0:T(8,128)(2,1)S(1)}, bf16[192,768]{1,0:T(8,128)(2,1)S(1)}, u32[]{:S(2)}, u32[]{:S(2)}) %collective-permute-start.17) | collective-permute-done | bytes 294944 | tf_op jit(solution)/shard_map/ppermute | solution.py:261
  65.3 1.7 %apply.1 = bf16[512,768]{1,0:T(8,128)(2,1)} custom-call(f32[512,512]{1,0:T(8,128)S(1)} %get-tuple-element.15.select, bf16[512,768]{1,0:T(8,128)(2,1)S(1)} %copy-done.1, bf16[128,768]{1,0:T(8,128)(2,1)S(1)} %slice.93.refs_0_, bf16[192,768]{1,0:T(8,128)(2,1)S(1)} %constant_dynamic-update-slice_fusion.refs_1_, bf16[192,768]{1,0:T(8,128)(2,1)S(1)} %collective-permute-done.17.refs_2_), custom_call_target="tpu_custom_call" | custom-call | flops 1 | bytes 1 | tf_op jit(solution)/shard_map/apply/pallas_call | solution.py:248
  (36 shorter events, 0.3 us)
Async XLA Ops:
  0.6 17.9 %copy-start.7 = (s32[1,2048]{1,0:T(1,128)S(1)}, s32[1,2048]{1,0:T(1,128)}, u32[]{:S(2)}) copy-start(s32[1,2048]{1,0:T(1,128)} %param.11) | copy-start | bytes 24580
  0.7 0.7 %copy-start.5 = (s32[512]{0:T(512)S(1)}, s32[512]{0:T(512)}, u32[]{:S(2)}) copy-start(s32[512]{0:T(512)} %param.8) | copy-start | bytes 6148
  0.7 0.7 %copy-start.6 = (s32[256]{0:T(256)S(1)}, s32[256]{0:T(256)}, u32[]{:S(2)}) copy-start(s32[256]{0:T(256)} %param.9) | copy-start | bytes 3076
  1.4 1.1 %copy-start = (bf16[512,768]{1,0:T(8,128)(2,1)S(1)}, bf16[512,768]{1,0:T(8,128)(2,1)}, u32[]{:S(2)}) copy-start(bf16[512,768]{1,0:T(8,128)(2,1)} %refs_5_.3) | copy-start | bytes 2359300
  2.6 1.0 %copy-start.2 = (bf16[256,768]{1,0:T(8,128)(2,1)S(1)}, bf16[256,768]{1,0:T(8,128)(2,1)}, u32[]{:S(2)}) copy-start(bf16[256,768]{1,0:T(8,128)(2,1)} %refs_6_.7) | copy-start | bytes 1179652
  3.5 3.9 %copy-start.4 = (bf16[256,768]{1,0:T(8,128)(2,1)S(1)}, bf16[256,768]{1,0:T(8,128)(2,1)}, u32[]{:S(2)}) copy-start(bf16[256,768]{1,0:T(8,128)(2,1)} %refs_0_.3) | copy-start | bytes 1179652
  3.6 15.0 %copy-start.8 = (s32[256]{0:T(256)S(1)}, s32[256]{0:T(256)}, u32[]{:S(2)}) copy-start(s32[256]{0:T(256)} %param.13) | copy-start | bytes 3076
  3.6 35.4 %copy-start.1 = (bf16[512,768]{1,0:T(8,128)(2,1)S(1)}, bf16[512,768]{1,0:T(8,128)(2,1)}, u32[]{:S(2)}) copy-start(bf16[512,768]{1,0:T(8,128)(2,1)} %refs_5_.3) | copy-start | bytes 2359300
  4.4 34.6 %copy-start.3 = (bf16[256,768]{1,0:T(8,128)(2,1)S(1)}, bf16[256,768]{1,0:T(8,128)(2,1)}, u32[]{:S(2)}) copy-start(bf16[256,768]{1,0:T(8,128)(2,1)} %refs_6_.7) | copy-start | bytes 1179652
  4.4 14.7 %collective-permute-start.8 = (bf16[384,768]{1,0:T(8,128)(2,1)S(1)}, bf16[384,768]{1,0:T(8,128)(2,1)S(1)}, u32[]{:S(2)}, u32[]{:S(2)}) collective-permute-start(bf16[384,768]{1,0:T(8,128)(2,1)S(1)} %get-tuple-element.17), channel_id=1, source_target_pairs={{0,2},{1,5},{2,0},{3,7},{4,6},{5,1},{6,4},{7,3},{8,10},{9,13},{10,... | collective-permute-start | bytes 1769480 | tf_op jit(solution)/shard_map/ppermute | solution.py:352
  7.4 13.3 %collective-permute-start = (bf16[256,768]{1,0:T(8,128)(2,1)S(1)}, bf16[256,768]{1,0:T(8,128)(2,1)S(1)}, u32[]{:S(2)}, u32[]{:S(2)}) collective-permute-start(bf16[256,768]{1,0:T(8,128)(2,1)S(1)} %copy-done.4), channel_id=1, source_target_pairs={{0,8},{8,0},{16,24},{24,16},{1,9},{9,1},{17,25},{25,17},{2,10},{10... | collective-permute-start | bytes 1179656 | tf_op jit(solution)/shard_map/ppermute | solution.py:261
  9.0 11.7 %collective-permute-start.1 = (bf16[256,768]{1,0:T(8,128)(2,1)S(1)}, bf16[256,768]{1,0:T(8,128)(2,1)S(1)}, u32[]{:S(2)}, u32[]{:S(2)}) collective-permute-start(bf16[256,768]{1,0:T(8,128)(2,1)S(1)} %copy-done.4), channel_id=1, source_target_pairs={{8,16},{16,8},{9,17},{17,9},{10,18},{18,10},{11,19},{19,11},{12,20... | collective-permute-start | bytes 1179656 | tf_op jit(solution)/shard_map/ppermute | solution.py:270
  9.7 5.9 %collective-permute-start.2 = (f32[12,128]{1,0:T(8,128)S(1)}, f32[12,128]{1,0:T(8,128)S(1)}, u32[]{:S(2)}, u32[]{:S(2)}) collective-permute-start(f32[12,128]{1,0:T(8,128)S(1)} %get-tuple-element.13), channel_id=1, source_target_pairs={{0,2},{2,0},{4,6},{6,4},{1,3},{3,1},{5,7},{7,5},{8,10},{10,8},{12,... | collective-permute-start | bytes 18440 | tf_op jit(solution)/shard_map/ppermute | solution.py:261
  10.3 8.3 %collective-permute-start.3 = (f32[12,128]{1,0:T(8,128)S(1)}, f32[12,128]{1,0:T(8,128)S(1)}, u32[]{:S(2)}, u32[]{:S(2)}) collective-permute-start(f32[12,128]{1,0:T(8,128)S(1)} %get-tuple-element.13), channel_id=1, source_target_pairs={{0,4},{2,6},{4,0},{6,2},{1,5},{3,7},{5,1},{7,3},{8,12},{10,14},{12... | collective-permute-start | bytes 18440 | tf_op jit(solution)/shard_map/ppermute | solution.py:261
  15.5 5.1 %collective-permute-start.4 = (f32[12,128]{1,0:T(8,128)S(1)}, f32[12,128]{1,0:T(8,128)S(1)}, u32[]{:S(2)}, u32[]{:S(2)}) collective-permute-start(f32[12,128]{1,0:T(8,128)S(1)} %get-tuple-element.13), channel_id=1, source_target_pairs={{0,6},{2,4},{4,2},{6,0},{1,7},{3,5},{5,3},{7,1},{8,14},{10,12},{12... | collective-permute-start | bytes 18440 | tf_op jit(solution)/shard_map/ppermute | solution.py:261
  18.6 16.8 %collective-permute-start.10 = (bf16[384,768]{1,0:T(8,128)(2,1)S(1)}, bf16[384,768]{1,0:T(8,128)(2,1)S(1)}, u32[]{:S(2)}, u32[]{:S(2)}) collective-permute-start(bf16[384,768]{1,0:T(8,128)(2,1)S(1)} %get-tuple-element.17), channel_id=1, source_target_pairs={{0,4},{1,3},{2,6},{3,1},{4,0},{5,7},{6,2},{7,5},{8,12},{9,11},{10,... | collective-permute-start | bytes 1769480 | tf_op jit(solution)/shard_map/ppermute | solution.py:353
  19.1 16.7 %collective-permute-start.12 = (bf16[384,768]{1,0:T(8,128)(2,1)S(1)}, bf16[384,768]{1,0:T(8,128)(2,1)S(1)}, u32[]{:S(2)}, u32[]{:S(2)}) collective-permute-start(bf16[384,768]{1,0:T(8,128)(2,1)S(1)} %collective-permute-done.8.refs_2_.refs_7_.refs_8_), channel_id=1, source_target_pairs={{0,4},{1,3},{2,6},{3,1},{4,0},{5,7},{6,2},{7,5},{8,12},{9,11},{10,... | collective-permute-start | bytes 1769480 | tf_op jit(solution)/shard_map/ppermute | solution.py:354
  20.7 4.6 %collective-permute-start.5 = (f32[3328]{0:T(1024)S(1)}, f32[3328]{0:T(1024)S(1)}, u32[]{:S(2)}, u32[]{:S(2)}) collective-permute-start(f32[3328]{0:T(1024)S(1)} %pad_maximum_fusion.3), channel_id=1, source_target_pairs={{0,8},{8,0},{16,24},{24,16},{1,9},{9,1},{17,25},{25,17},{2,10},{10... | collective-permute-start | bytes 39944 | tf_op jit(solution)/shard_map/ppermute | solution.py:261
  22.6 4.7 %collective-permute-start.6 = (f32[3328]{0:T(1024)S(1)}, f32[3328]{0:T(1024)S(1)}, u32[]{:S(2)}, u32[]{:S(2)}) collective-permute-start(f32[3328]{0:T(1024)S(1)} %pad_maximum_fusion.3), channel_id=1, source_target_pairs={{0,16},{8,24},{16,0},{24,8},{1,17},{9,25},{17,1},{25,9},{2,18},{10... | collective-permute-start | bytes 39944 | tf_op jit(solution)/shard_map/ppermute | solution.py:261
  25.0 5.7 %collective-permute-start.7 = (f32[3328]{0:T(1024)S(1)}, f32[3328]{0:T(1024)S(1)}, u32[]{:S(2)}, u32[]{:S(2)}) collective-permute-start(f32[3328]{0:T(1024)S(1)} %pad_maximum_fusion.3), channel_id=1, source_target_pairs={{0,24},{8,16},{16,8},{24,0},{1,25},{9,17},{17,9},{25,1},{2,26},{10... | collective-permute-start | bytes 39944 | tf_op jit(solution)/shard_map/ppermute | solution.py:261
  25.3 10.7 %collective-permute-start.20 = (bf16[256,768]{1,0:T(8,128)(2,1)S(1)}, bf16[256,768]{1,0:T(8,128)(2,1)S(1)}, u32[]{:S(2)}, u32[]{:S(2)}) collective-permute-start(bf16[256,768]{1,0:T(8,128)(2,1)S(1)} %collective-permute-done.refs_0_), channel_id=1, source_target_pairs={{8,16},{16,8},{9,17},{17,9},{10,18},{18,10},{11,19},{19,11},{12,20... | collective-permute-start | bytes 1179656 | tf_op jit(solution)/shard_map/ppermute | solution.py:272
  27.3 15.1 %collective-permute-start.19 = (bf16[256,768]{1,0:T(8,128)(2,1)S(1)}, bf16[256,768]{1,0:T(8,128)(2,1)S(1)}, u32[]{:S(2)}, u32[]{:S(2)}) collective-permute-start(bf16[256,768]{1,0:T(8,128)(2,1)S(1)} %collective-permute-done.1.refs_1_), channel_id=1, source_target_pairs={{8,0},{16,24},{9,1},{17,25},{10,2},{18,26},{11,3},{19,27},{12,4},{... | collective-permute-start | bytes 1179656 | tf_op jit(solution)/shard_map/ppermute | solution.py:273
  35.2 2.2 %collective-permute-start.9 = (bf16[384,768]{1,0:T(8,128)(2,1)S(1)}, bf16[384,768]{1,0:T(8,128)(2,1)S(1)}, u32[]{:S(2)}, u32[]{:S(2)}) collective-permute-start(bf16[384,768]{1,0:T(8,128)(2,1)S(1)} %collective-permute-done.8.refs_2_.refs_7_.refs_8_), channel_id=1, source_target_pairs={{0,1},{1,0},{2,3},{3,2},{4,5},{5,4},{6,7},{7,6},{8,9},{9,8},{10,11... | collective-permute-start | bytes 1769480 | tf_op jit(solution)/shard_map/ppermute | solution.py:261
  35.3 2.8 %collective-permute-start.11 = (bf16[384,768]{1,0:T(8,128)(2,1)S(1)}, bf16[384,768]{1,0:T(8,128)(2,1)S(1)}, u32[]{:S(2)}, u32[]{:S(2)}) collective-permute-start(bf16[384,768]{1,0:T(8,128)(2,1)S(1)} %collective-permute-done.10.refs_4_.refs_9_.refs_10_), channel_id=1, source_target_pairs={{0,1},{1,0},{2,3},{3,2},{4,5},{5,4},{6,7},{7,6},{8,9},{9,8},{10,11... | collective-permute-start | bytes 1769480 | tf_op jit(solution)/shard_map/ppermute | solution.py:261
  35.8 3.2 %collective-permute-start.13 = (bf16[384,768]{1,0:T(8,128)(2,1)S(1)}, bf16[384,768]{1,0:T(8,128)(2,1)S(1)}, u32[]{:S(2)}, u32[]{:S(2)}) collective-permute-start(bf16[384,768]{1,0:T(8,128)(2,1)S(1)} %collective-permute-done.12.refs_6_.refs_11_.refs_12_), channel_id=1, source_target_pairs={{0,1},{1,0},{2,3},{3,2},{4,5},{5,4},{6,7},{7,6},{8,9},{9,8},{10,11... | collective-permute-start | bytes 1769480 | tf_op jit(solution)/shard_map/ppermute | solution.py:261
  36.0 14.3 %collective-permute-start.22 = (bf16[256,768]{1,0:T(8,128)(2,1)S(1)}, bf16[256,768]{1,0:T(8,128)(2,1)S(1)}, u32[]{:S(2)}, u32[]{:S(2)}) collective-permute-start(bf16[256,768]{1,0:T(8,128)(2,1)S(1)} %collective-permute-done.20.refs_1_), channel_id=1, source_target_pairs={{8,0},{16,24},{9,1},{17,25},{10,2},{18,26},{11,3},{19,27},{12,4},{... | collective-permute-start | bytes 1179656 | tf_op jit(solution)/shard_map/ppermute | solution.py:274
  40.6 16.4 %collective-permute-start.14 = (bf16[64,768]{1,0:T(8,128)(2,1)S(1)}, bf16[64,768]{1,0:T(8,128)(2,1)S(1)}, u32[]{:S(2)}, u32[]{:S(2)}) collective-permute-start(bf16[64,768]{1,0:T(8,128)(2,1)S(1)} %get-tuple-element.25), channel_id=1, source_target_pairs={{0,8},{8,0},{16,24},{24,16},{1,9},{9,1},{17,25},{25,17},{2,10},{10... | collective-permute-start | bytes 294920 | tf_op jit(solution)/shard_map/ppermute | solution.py:261
  44.8 18.9 %collective-permute-start.21 = (f32[2,2,128]{2,1,0:T(2,128)S(1)}, f32[2,2,128]{2,1,0:T(2,128)S(1)}, u32[]{:S(2)}, u32[]{:S(2)}) collective-permute-start(f32[2,2,128]{2,1,0:T(2,128)S(1)} %score.5), channel_id=1, source_target_pairs={{0,16},{8,24},{16,0},{24,8},{1,17},{9,25},{17,1},{25,9},{2,18},{10... | collective-permute-start | bytes 6152 | tf_op jit(solution)/shard_map/ppermute | solution.py:261
  48.3 15.5 %collective-permute-start.18 = (f32[2,2,128]{2,1,0:T(2,128)S(1)}, f32[2,2,128]{2,1,0:T(2,128)S(1)}, u32[]{:S(2)}, u32[]{:S(2)}) collective-permute-start(f32[2,2,128]{2,1,0:T(2,128)S(1)} %score.4), channel_id=1, source_target_pairs={{0,8},{8,0},{16,24},{24,16},{1,9},{9,1},{17,25},{25,17},{2,10},{10... | collective-permute-start | bytes 6152 | tf_op jit(solution)/shard_map/ppermute | solution.py:261
  52.6 11.1 %collective-permute-start.23 = (f32[2,2,128]{2,1,0:T(2,128)S(1)}, f32[2,2,128]{2,1,0:T(2,128)S(1)}, u32[]{:S(2)}, u32[]{:S(2)}) collective-permute-start(f32[2,2,128]{2,1,0:T(2,128)S(1)} %score.6), channel_id=1, source_target_pairs={{0,24},{8,16},{16,8},{24,0},{1,25},{9,17},{17,9},{25,1},{2,26},{10... | collective-permute-start | bytes 6152 | tf_op jit(solution)/shard_map/ppermute | solution.py:261
  54.7 7.5 %collective-permute-start.15 = (bf16[64,768]{1,0:T(8,128)(2,1)S(1)}, bf16[64,768]{1,0:T(8,128)(2,1)S(1)}, u32[]{:S(2)}, u32[]{:S(2)}) collective-permute-start(bf16[64,768]{1,0:T(8,128)(2,1)S(1)} %get-tuple-element.24), channel_id=1, source_target_pairs={{0,16},{8,24},{16,0},{24,8},{1,17},{9,25},{17,1},{25,9},{2,18},{10... | collective-permute-start | bytes 294920 | tf_op jit(solution)/shard_map/ppermute | solution.py:261
  57.1 6.6 %collective-permute-start.16 = (bf16[64,768]{1,0:T(8,128)(2,1)S(1)}, bf16[64,768]{1,0:T(8,128)(2,1)S(1)}, u32[]{:S(2)}, u32[]{:S(2)}) collective-permute-start(bf16[64,768]{1,0:T(8,128)(2,1)S(1)} %get-tuple-element.23), channel_id=1, source_target_pairs={{0,24},{8,16},{16,8},{24,0},{1,25},{9,17},{17,9},{25,1},{2,26},{10... | collective-permute-start | bytes 294920 | tf_op jit(solution)/shard_map/ppermute | solution.py:261
  63.7 1.6 %collective-permute-start.17 = (bf16[192,768]{1,0:T(8,128)(2,1)S(1)}, bf16[192,768]{1,0:T(8,128)(2,1)S(1)}, u32[]{:S(2)}, u32[]{:S(2)}) collective-permute-start(bf16[192,768]{1,0:T(8,128)(2,1)S(1)} %constant_dynamic-update-slice_fusion.refs_1_), channel_id=1, source_target_pairs={{0,1},{1,0},{2,3},{3,2},{4,5},{5,4},{6,7},{7,6},{8,9},{9,8},{10,11... | collective-permute-start | bytes 884744 | tf_op jit(solution)/shard_map/ppermute | solution.py:261

commit v20 on v19

--- a/solution.py
+++ b/solution.py
@@ -382,7 +382,8 @@
     for s in range(1, planes):
         first = cap + (s - 1) * share
         parts.append(swap(packed[first : first + share], "outer", s))
-    parts = jnp.concatenate(parts)
+    parts, own_queries = lax.optimization_barrier((jnp.concatenate(parts), queries))
+    got_queries[0] = (own_queries,)
     arrived = [packed[:cap], parts] + [swap(parts, "query", flip) for flip in range(1, replicas)]
 
     pieces = table_pieces + shift(fresh_pieces, plane_rows)

time: 67.3 us -> 64.4 us (0.957)
  waiting for transfers between devices: 14.3 us -> 11.4 us
    ppermute x17, waiting for transfers between devices: 14.3 us -> 9.05 us  [swap(): lax.ppermute(values, axis, [(i, i ^ flip) for i in range(lax.axis_size(ax...]
    ppermute x1, waiting for transfers between devices: 0.01 us -> 2.32 us  [gather_line(): last = lax.ppermute(from_end, 'outer', outward)]
    unnamed x20 -> x18, local copies, waits for them, and re-layouts: 2.86 us -> 2.84 us
  transfers between devices with their start and end apart: 24 -> 24, of which waited for: 8 -> 7; matrix products, arithmetic and copies ran while one was open for 2% -> 2% of each run, Pallas kernels for 23% -> 24%
where the time goes in v20:
time: 64.4 us; the launch traced here: 64.1 us
  starting transfers between devices  29.6 us (46%)
  Pallas kernels  17.8 us (28%)
  waiting for transfers between devices  11.4 us (18%)
  local copies, waits for them, and re-layouts  2.93 us (5%)
  other arithmetic  1.43 us (2%)
  between operations  0.93 us (1%)
    ppermute x17, starting transfers between devices, swap(): lax.ppermute(values, axis, [(i, i ^ flip) for i in range(lax.axis_size(ax...  20.4 us
    pallas_call x8, Pallas kernels, call(): pl.pallas_call(functools.partial(kernel, **options), out_shape=tuple(outs...  17.8 us
    ppermute x17, waiting for transfers between devices, swap(): lax.ppermute(values, axis, [(i, i ^ flip) for i in range(lax.axis_size(ax...  9.05 us
    ppermute x1, starting transfers between devices, on_device(): near = lax.ppermute(rows_half, axes, first)  3 us
    unnamed x18, local copies, waits for them, and re-layouts  2.84 us
    ppermute x1, waiting for transfers between devices, gather_line(): last = lax.ppermute(from_end, 'outer', outward)  2.32 us
    ppermute x1, starting transfers between devices, on_device(): far = lax.ppermute(near, axes, second)  1.52 us
    ppermute x1, starting transfers between devices, gather_line(): last = lax.ppermute(from_end, 'outer', outward)  1.47 us
  transfers between devices with their start and end apart: 24, of which 7 were waited for; matrix products, arithmetic and copies ran while one was open for 2% of the time, Pallas kernels for 24%

profile of v20, /device:TPU:0, one launch (start us, length us, event | category | flops | bytes accessed | tf_op | source)
XLA Modules:
  0.0 64.1 jit_solution(17217310960389592677)
XLA Ops:
  0.6 0.1 pad_add_fusion.place
  0.7 0.7 %copy-done.5 = s32[512]{0:T(512)S(1)} copy-done((s32[512]{0:T(512)S(1)}, s32[512]{0:T(512)}, u32[]{:S(2)}) %copy-start.5) | copy-done | bytes 2072
  1.4 0.0 copy-done.6
  1.4 1.1 %copy-done = bf16[512,768]{1,0:T(8,128)(2,1)S(1)} copy-done((bf16[512,768]{1,0:T(8,128)(2,1)S(1)}, bf16[512,768]{1,0:T(8,128)(2,1)}, u32[]{:S(2)}) %copy-start) | copy-done | bytes 786456
  2.6 1.0 %copy-done.2 = bf16[256,768]{1,0:T(8,128)(2,1)S(1)} copy-done((bf16[256,768]{1,0:T(8,128)(2,1)S(1)}, bf16[256,768]{1,0:T(8,128)(2,1)}, u32[]{:S(2)}) %copy-start.2) | copy-done | bytes 393240
  3.6 0.8 %prep.1 = (bf16[384,768]{1,0:T(8,128)(2,1)S(1)}, f32[12,128]{1,0:T(8,128)S(1)}) custom-call(s32[3]{0:T(128)S(1)} %pad_add_fusion.place, bf16[512,768]{1,0:T(8,128)(2,1)S(1)} %copy-done, bf16[256,768]{1,0:T(8,128)(2,1)S(1)} %copy-done.2, s32[4,128]{1,0:T(4,128)S(1)} %bitcast.23, s32[2,128]{1,0:T(2,128)S(1)} %bitcast.28), custom_call_target="tpu_custom_call" | custom-call | flops 1 | bytes 1 | tf_op jit(solution)/shard_map/prep/pallas_call | solution.py:248
  4.4 3.0 %collective-permute-start.8 = (bf16[384,768]{1,0:T(8,128)(2,1)S(1)}, bf16[384,768]{1,0:T(8,128)(2,1)S(1)}, u32[]{:S(2)}, u32[]{:S(2)}) collective-permute-start(bf16[384,768]{1,0:T(8,128)(2,1)S(1)} %get-tuple-element.19), channel_id=1, source_target_pairs={{0,2},{1,5},{2,0},{3,7},{4,6},{5,1},{6,4},{7,3},{8,10},{9,13},{10,... | collective-permute-start | bytes 1769480 | tf_op jit(solution)/shard_map/ppermute | solution.py:352
  7.4 0.0 copy-done.4
  7.4 1.6 %collective-permute-start = (bf16[256,768]{1,0:T(8,128)(2,1)S(1)}, bf16[256,768]{1,0:T(8,128)(2,1)S(1)}, u32[]{:S(2)}, u32[]{:S(2)}) collective-permute-start(bf16[256,768]{1,0:T(8,128)(2,1)S(1)} %copy-done.4), channel_id=1, source_target_pairs={{0,8},{8,0},{16,24},{24,16},{1,9},{9,1},{17,25},{25,17},{2,10},{10... | collective-permute-start | bytes 1179656 | tf_op jit(solution)/shard_map/ppermute | solution.py:261
  9.0 0.7 %collective-permute-start.1 = (bf16[256,768]{1,0:T(8,128)(2,1)S(1)}, bf16[256,768]{1,0:T(8,128)(2,1)S(1)}, u32[]{:S(2)}, u32[]{:S(2)}) collective-permute-start(bf16[256,768]{1,0:T(8,128)(2,1)S(1)} %copy-done.4), channel_id=1, source_target_pairs={{8,16},{16,8},{9,17},{17,9},{10,18},{18,10},{11,19},{19,11},{12,20... | collective-permute-start | bytes 1179656 | tf_op jit(solution)/shard_map/ppermute | solution.py:270
  9.7 0.6 collective-permute-start.2
  10.3 1.5 %collective-permute-start.3 = (f32[12,128]{1,0:T(8,128)S(1)}, f32[12,128]{1,0:T(8,128)S(1)}, u32[]{:S(2)}, u32[]{:S(2)}) collective-permute-start(f32[12,128]{1,0:T(8,128)S(1)} %get-tuple-element.15), channel_id=1, source_target_pairs={{0,4},{2,6},{4,0},{6,2},{1,5},{3,7},{5,1},{7,3},{8,12},{10,14},{12... | collective-permute-start | bytes 18440 | tf_op jit(solution)/shard_map/ppermute | solution.py:261
  11.8 3.7 %collective-permute-done.2 = f32[12,128]{1,0:T(8,128)S(1)} collective-permute-done((f32[12,128]{1,0:T(8,128)S(1)}, f32[12,128]{1,0:T(8,128)S(1)}, u32[]{:S(2)}, u32[]{:S(2)}) %collective-permute-start.2) | collective-permute-done | bytes 6176 | tf_op jit(solution)/shard_map/ppermute | solution.py:261
  15.5 3.0 %collective-permute-start.4 = (f32[12,128]{1,0:T(8,128)S(1)}, f32[12,128]{1,0:T(8,128)S(1)}, u32[]{:S(2)}, u32[]{:S(2)}) collective-permute-start(f32[12,128]{1,0:T(8,128)S(1)} %get-tuple-element.15), channel_id=1, source_target_pairs={{0,6},{2,4},{4,2},{6,0},{1,7},{3,5},{5,3},{7,1},{8,14},{10,12},{12... | collective-permute-start | bytes 18440 | tf_op jit(solution)/shard_map/ppermute | solution.py:261
  18.6 0.0 collective-permute-done.3
  18.6 0.6 collective-permute-start.10
  19.1 0.0 collective-permute-done.8.refs_2_.refs_7_.refs_8_
  19.1 1.5 %collective-permute-start.12 = (bf16[384,768]{1,0:T(8,128)(2,1)S(1)}, bf16[384,768]{1,0:T(8,128)(2,1)S(1)}, u32[]{:S(2)}, u32[]{:S(2)}) collective-permute-start(bf16[384,768]{1,0:T(8,128)(2,1)S(1)} %collective-permute-done.8.refs_2_.refs_7_.refs_8_), channel_id=1, source_target_pairs={{0,4},{1,3},{2,6},{3,1},{4,0},{5,7},{6,2},{7,5},{8,12},{9,11},{10,... | collective-permute-start | bytes 1769480 | tf_op jit(solution)/shard_map/ppermute | solution.py:354
  20.7 0.0 collective-permute-done.4
  20.7 0.0 collective-permute-done.refs_0_
  20.7 0.0 collective-permute-done.1.refs_1_
  20.7 1.9 %collective-permute-start.5 = (f32[3328]{0:T(1024)S(1)}, f32[3328]{0:T(1024)S(1)}, u32[]{:S(2)}, u32[]{:S(2)}) collective-permute-start(f32[3328]{0:T(1024)S(1)} %pad_maximum_fusion.4), channel_id=1, source_target_pairs={{0,8},{8,0},{16,24},{24,16},{1,9},{9,1},{17,25},{25,17},{2,10},{10... | collective-permute-start | bytes 39944 | tf_op jit(solution)/shard_map/ppermute | solution.py:261
  22.6 2.4 %collective-permute-start.6 = (f32[3328]{0:T(1024)S(1)}, f32[3328]{0:T(1024)S(1)}, u32[]{:S(2)}, u32[]{:S(2)}) collective-permute-start(f32[3328]{0:T(1024)S(1)} %pad_maximum_fusion.4), channel_id=1, source_target_pairs={{0,16},{8,24},{16,0},{24,8},{1,17},{9,25},{17,1},{25,9},{2,18},{10... | collective-permute-start | bytes 39944 | tf_op jit(solution)/shard_map/ppermute | solution.py:261
  25.0 0.2 collective-permute-start.7
  25.3 0.0 collective-permute-done.5
  25.3 0.7 %collective-permute-start.20 = (bf16[256,768]{1,0:T(8,128)(2,1)S(1)}, bf16[256,768]{1,0:T(8,128)(2,1)S(1)}, u32[]{:S(2)}, u32[]{:S(2)}) collective-permute-start(bf16[256,768]{1,0:T(8,128)(2,1)S(1)} %collective-permute-done.refs_0_), channel_id=1, source_target_pairs={{8,16},{16,8},{9,17},{17,9},{10,18},{18,10},{11,19},{19,11},{12,20... | collective-permute-start | bytes 1179656 | tf_op jit(solution)/shard_map/ppermute | solution.py:272
  26.0 1.3 %collective-permute-done.6 = f32[3328]{0:T(1024)S(1)} collective-permute-done((f32[3328]{0:T(1024)S(1)}, f32[3328]{0:T(1024)S(1)}, u32[]{:S(2)}, u32[]{:S(2)}) %collective-permute-start.6) | collective-permute-done | bytes 13344 | tf_op jit(solution)/shard_map/ppermute | solution.py:261
  27.3 1.3 %collective-permute-start.19 = (bf16[256,768]{1,0:T(8,128)(2,1)S(1)}, bf16[256,768]{1,0:T(8,128)(2,1)S(1)}, u32[]{:S(2)}, u32[]{:S(2)}) collective-permute-start(bf16[256,768]{1,0:T(8,128)(2,1)S(1)} %collective-permute-done.1.refs_1_), channel_id=1, source_target_pairs={{8,0},{16,24},{9,1},{17,25},{10,2},{18,26},{11,3},{19,27},{12,4},{... | collective-permute-start | bytes 1179656 | tf_op jit(solution)/shard_map/ppermute | solution.py:273
  28.6 2.1 %collective-permute-done.7 = f32[3328]{0:T(1024)S(1)} collective-permute-done((f32[3328]{0:T(1024)S(1)}, f32[3328]{0:T(1024)S(1)}, u32[]{:S(2)}, u32[]{:S(2)}) %collective-permute-start.7) | collective-permute-done | bytes 13344 | tf_op jit(solution)/shard_map/ppermute | solution.py:261
  30.8 4.4 %meta.1 = (f32[4,3072]{1,0:T(4,128)S(1)}, f32[1,3072]{1,0:T(1,128)S(1)}, bf16[320,1024]{1,0:T(8,128)(2,1)S(1)}, f32[512,512]{1,0:T(8,128)S(1)}, s32[1,512]{1,0:T(1,128)S(1)}) custom-call(s32[3]{0:T(128)S(1)} %pad_add_fusion.place, s32[4,1024]{1,0:T(4,128)S(1)} %maximum_convert_fusion.ref_ids, s32[4,2048]{1,0:T(4,128)S(1)} %fusion.neg, f32[1,2048]{1,0:T(1,128)S(1)} %bitcast.22), custom_call_target="tpu_custom_call" | custom-call | flops 1 | bytes 1 | tf_op jit(solution)/shard_map/meta/pallas_call | solution.py:248
  35.2 0.1 collective-permute-start.9
  35.3 0.0 collective-permute-done.10.refs_4_.refs_9_.refs_10_
  35.3 0.5 collective-permute-start.11
  35.8 0.0 collective-permute-done.12.refs_6_.refs_11_.refs_12_
  35.8 0.1 collective-permute-start.13
  36.0 0.0 collective-permute-done.20.refs_1_
  36.0 1.5 %collective-permute-start.22 = (bf16[256,768]{1,0:T(8,128)(2,1)S(1)}, bf16[256,768]{1,0:T(8,128)(2,1)S(1)}, u32[]{:S(2)}, u32[]{:S(2)}) collective-permute-start(bf16[256,768]{1,0:T(8,128)(2,1)S(1)} %collective-permute-done.20.refs_1_), channel_id=1, source_target_pairs={{8,0},{16,24},{9,1},{17,25},{10,2},{18,26},{11,3},{19,27},{12,4},{... | collective-permute-start | bytes 1179656 | tf_op jit(solution)/shard_map/ppermute | solution.py:274
  37.5 0.0 collective-permute-done.9.refs_3_.refs_8_.refs_9_
  37.5 0.7 %collective-permute-done.11.refs_5_.refs_10_.refs_11_ = bf16[384,768]{1,0:T(8,128)(2,1)S(1)} collective-permute-done((bf16[384,768]{1,0:T(8,128)(2,1)S(1)}, bf16[384,768]{1,0:T(8,128)(2,1)S(1)}, u32[]{:S(2)}, u32[]{:S(2)}) %collective-permute-start.11) | collective-permute-done | bytes 589856 | tf_op jit(solution)/shard_map/ppermute | solution.py:261
  38.1 0.8 %collective-permute-done.13.refs_7_.refs_12_.refs_13_ = bf16[384,768]{1,0:T(8,128)(2,1)S(1)} collective-permute-done((bf16[384,768]{1,0:T(8,128)(2,1)S(1)}, bf16[384,768]{1,0:T(8,128)(2,1)S(1)}, u32[]{:S(2)}, u32[]{:S(2)}) %collective-permute-start.13) | collective-permute-done | bytes 589856 | tf_op jit(solution)/shard_map/ppermute | solution.py:261
  39.0 1.6 %pack.1 = bf16[320,768]{1,0:T(8,128)(2,1)S(1)} custom-call(s32[3]{0:T(128)S(1)} %pad_add_fusion.place, bf16[320,1024]{1,0:T(8,128)(2,1)S(1)} %get-tuple-element.18.select, bf16[512,768]{1,0:T(8,128)(2,1)S(1)} %copy-done.1, bf16[256,768]{1,0:T(8,128)(2,1)S(1)} %copy-done.3, bf16[384,768]{1,0:T(8,128)(2,1)S(1)} %collective-permute-done.8.refs_2_.refs_7_.refs_8_, ...), custom_call_target="tpu_custom_call" | custom-call | flops 1 | bytes 1 | tf_op jit(solution)/shard_map/pack/pallas_call | solution.py:248
  40.6 1.3 %collective-permute-start.14 = (bf16[64,768]{1,0:T(8,128)(2,1)S(1)}, bf16[64,768]{1,0:T(8,128)(2,1)S(1)}, u32[]{:S(2)}, u32[]{:S(2)}) collective-permute-start(bf16[64,768]{1,0:T(8,128)(2,1)S(1)} %get-tuple-element.27), channel_id=1, source_target_pairs={{0,8},{8,0},{16,24},{24,16},{1,9},{9,1},{17,25},{25,17},{2,10},{10... | collective-permute-start | bytes 294920 | tf_op jit(solution)/shard_map/ppermute | solution.py:261
  41.9 1.1 %collective-permute-start.15 = (bf16[64,768]{1,0:T(8,128)(2,1)S(1)}, bf16[64,768]{1,0:T(8,128)(2,1)S(1)}, u32[]{:S(2)}, u32[]{:S(2)}) collective-permute-start(bf16[64,768]{1,0:T(8,128)(2,1)S(1)} %get-tuple-element.29), channel_id=1, source_target_pairs={{0,16},{8,24},{16,0},{24,8},{1,17},{9,25},{17,1},{25,9},{2,18},{10... | collective-permute-start | bytes 294920 | tf_op jit(solution)/shard_map/ppermute | solution.py:261
  43.0 2.0 %collective-permute-start.16 = (bf16[64,768]{1,0:T(8,128)(2,1)S(1)}, bf16[64,768]{1,0:T(8,128)(2,1)S(1)}, u32[]{:S(2)}, u32[]{:S(2)}) collective-permute-start(bf16[64,768]{1,0:T(8,128)(2,1)S(1)} %get-tuple-element.28), channel_id=1, source_target_pairs={{0,24},{8,16},{16,8},{24,0},{1,25},{9,17},{17,9},{25,1},{2,26},{10... | collective-permute-start | bytes 294920 | tf_op jit(solution)/shard_map/ppermute | solution.py:261
  45.1 0.6 broadcast_select_fusion
  45.6 0.0 collective-permute-done.19.refs_0_
  45.7 2.3 %score.5 = f32[2,2,128]{2,1,0:T(2,128)S(1)} custom-call(s32[3]{0:T(128)S(1)} %pad_add_fusion.place, bf16[256,768]{1,0:T(8,128)(2,1)S(1)} %collective-permute-done.19.refs_0_, bf16[256,768]{1,0:T(8,128)(2,1)S(1)} %collective-permute-done.20.refs_1_, f32[2,128]{1,0:T(2,128)S(1)} %bitcast.27, f32[1,3072]{1,0:T(1,128)S(1)} %get-tuple-element.30.refs_3_, ...), custom_call_target="tpu_custom_call" | custom-call | flops 1 | bytes 1 | tf_op jit(solution)/shard_map/score/pallas_call | solution.py:248
  48.0 1.4 %collective-permute-start.21 = (f32[2,2,128]{2,1,0:T(2,128)S(1)}, f32[2,2,128]{2,1,0:T(2,128)S(1)}, u32[]{:S(2)}, u32[]{:S(2)}) collective-permute-start(f32[2,2,128]{2,1,0:T(2,128)S(1)} %score.5), channel_id=1, source_target_pairs={{0,16},{8,24},{16,0},{24,8},{1,17},{9,25},{17,1},{25,9},{2,18},{10... | collective-permute-start | bytes 6152 | tf_op jit(solution)/shard_map/ppermute | solution.py:261
  49.4 2.3 %score.4 = f32[2,2,128]{2,1,0:T(2,128)S(1)} custom-call(s32[3]{0:T(128)S(1)} %pad_add_fusion.place, bf16[256,768]{1,0:T(8,128)(2,1)S(1)} %collective-permute-done.refs_0_, f32[2,128]{1,0:T(2,128)S(1)} %bitcast.26, f32[1,3072]{1,0:T(1,128)S(1)} %get-tuple-element.33.refs_2_, f32[1,3072]{1,0:T(1,128)S(1)} %get-tuple-element.24.refs_3_.refs_4_, ...), custom_call_target="tpu_custom_call" | custom-call | flops 1 | bytes 1 | tf_op jit(solution)/shard_map/score/pallas_call | solution.py:248
  51.7 2.3 %collective-permute-done.22.refs_0_ = bf16[256,768]{1,0:T(8,128)(2,1)S(1)} collective-permute-done((bf16[256,768]{1,0:T(8,128)(2,1)S(1)}, bf16[256,768]{1,0:T(8,128)(2,1)S(1)}, u32[]{:S(2)}, u32[]{:S(2)}) %collective-permute-start.22) | collective-permute-done | bytes 393248 | tf_op jit(solution)/shard_map/ppermute | solution.py:274
  54.1 0.0 collective-permute-start.18
  54.1 2.3 %score.6 = f32[2,2,128]{2,1,0:T(2,128)S(1)} custom-call(s32[3]{0:T(128)S(1)} %pad_add_fusion.place, bf16[256,768]{1,0:T(8,128)(2,1)S(1)} %collective-permute-done.22.refs_0_, bf16[256,768]{1,0:T(8,128)(2,1)S(1)} %collective-permute-done.1.refs_1_, f32[2,128]{1,0:T(2,128)S(1)} %bitcast.25, f32[1,3072]{1,0:T(1,128)S(1)} %get-tuple-element.32.refs_3_, ...), custom_call_target="tpu_custom_call" | custom-call | flops 1 | bytes 1 | tf_op jit(solution)/shard_map/score/pallas_call | solution.py:248
  56.4 0.0 collective-permute-done.14
  56.4 2.6 %collective-permute-start.23 = (f32[2,2,128]{2,1,0:T(2,128)S(1)}, f32[2,2,128]{2,1,0:T(2,128)S(1)}, u32[]{:S(2)}, u32[]{:S(2)}) collective-permute-start(f32[2,2,128]{2,1,0:T(2,128)S(1)} %score.6), channel_id=1, source_target_pairs={{0,24},{8,16},{16,8},{24,0},{1,25},{9,17},{17,9},{25,1},{2,26},{10... | collective-permute-start | bytes 6152 | tf_op jit(solution)/shard_map/ppermute | solution.py:261
  59.0 0.0 collective-permute-done.15
  59.0 0.0 collective-permute-done.16
  59.0 0.1 collective-permute-start.17
  59.1 2.3 %score.7 = f32[2,2,128]{2,1,0:T(2,128)S(1)} custom-call(s32[3]{0:T(128)S(1)} %pad_add_fusion.place, bf16[256,768]{1,0:T(8,128)(2,1)S(1)} %copy-done.4, f32[2,128]{1,0:T(2,128)S(1)} %bitcast.24, f32[1,3072]{1,0:T(1,128)S(1)} %get-tuple-element.31.refs_2_, f32[1,3072]{1,0:T(1,128)S(1)} %get-tuple-element.24.refs_3_.refs_4_, ...), custom_call_target="tpu_custom_call" | custom-call | flops 1 | bytes 1 | tf_op jit(solution)/shard_map/score/pallas_call | solution.py:248
  61.4 0.0 collective-permute-done.21
  61.4 0.0 collective-permute-done.18
  61.4 0.4 collective-permute-done.23
  61.8 0.6 fusion.2
  62.4 0.0 collective-permute-done.17.refs_2_
  62.4 1.7 %apply.1 = bf16[512,768]{1,0:T(8,128)(2,1)} custom-call(f32[512,512]{1,0:T(8,128)S(1)} %get-tuple-element.17.select, bf16[512,768]{1,0:T(8,128)(2,1)S(1)} %copy-done.1, bf16[128,768]{1,0:T(8,128)(2,1)S(1)} %slice.93.refs_0_, bf16[192,768]{1,0:T(8,128)(2,1)S(1)} %pad_maximum_fusion.refs_1_, bf16[192,768]{1,0:T(8,128)(2,1)S(1)} %collective-permute-done.17.refs_2_), custom_call_target="tpu_custom_call" | custom-call | flops 1 | bytes 1 | tf_op jit(solution)/shard_map/apply/pallas_call | solution.py:248
  (34 shorter events, 0.3 us)
Async XLA Ops:
  0.6 17.9 %copy-start.7 = (s32[1,2048]{1,0:T(1,128)S(1)}, s32[1,2048]{1,0:T(1,128)}, u32[]{:S(2)}) copy-start(s32[1,2048]{1,0:T(1,128)} %param.11) | copy-start | bytes 24580
  0.7 0.7 %copy-start.5 = (s32[512]{0:T(512)S(1)}, s32[512]{0:T(512)}, u32[]{:S(2)}) copy-start(s32[512]{0:T(512)} %param.8) | copy-start | bytes 6148
  0.7 0.7 %copy-start.6 = (s32[256]{0:T(256)S(1)}, s32[256]{0:T(256)}, u32[]{:S(2)}) copy-start(s32[256]{0:T(256)} %param.9) | copy-start | bytes 3076
  1.4 1.1 %copy-start = (bf16[512,768]{1,0:T(8,128)(2,1)S(1)}, bf16[512,768]{1,0:T(8,128)(2,1)}, u32[]{:S(2)}) copy-start(bf16[512,768]{1,0:T(8,128)(2,1)} %refs_5_.3) | copy-start | bytes 2359300
  2.6 1.0 %copy-start.2 = (bf16[256,768]{1,0:T(8,128)(2,1)S(1)}, bf16[256,768]{1,0:T(8,128)(2,1)}, u32[]{:S(2)}) copy-start(bf16[256,768]{1,0:T(8,128)(2,1)} %refs_6_.7) | copy-start | bytes 1179652
  3.5 3.9 %copy-start.4 = (bf16[256,768]{1,0:T(8,128)(2,1)S(1)}, bf16[256,768]{1,0:T(8,128)(2,1)}, u32[]{:S(2)}) copy-start(bf16[256,768]{1,0:T(8,128)(2,1)} %refs_0_.2) | copy-start | bytes 1179652
  3.6 15.0 %copy-start.8 = (s32[256]{0:T(256)S(1)}, s32[256]{0:T(256)}, u32[]{:S(2)}) copy-start(s32[256]{0:T(256)} %param.13) | copy-start | bytes 3076
  3.6 35.4 %copy-start.1 = (bf16[512,768]{1,0:T(8,128)(2,1)S(1)}, bf16[512,768]{1,0:T(8,128)(2,1)}, u32[]{:S(2)}) copy-start(bf16[512,768]{1,0:T(8,128)(2,1)} %refs_5_.3) | copy-start | bytes 2359300
  4.4 34.6 %copy-start.3 = (bf16[256,768]{1,0:T(8,128)(2,1)S(1)}, bf16[256,768]{1,0:T(8,128)(2,1)}, u32[]{:S(2)}) copy-start(bf16[256,768]{1,0:T(8,128)(2,1)} %refs_6_.7) | copy-start | bytes 1179652
  4.4 14.7 %collective-permute-start.8 = (bf16[384,768]{1,0:T(8,128)(2,1)S(1)}, bf16[384,768]{1,0:T(8,128)(2,1)S(1)}, u32[]{:S(2)}, u32[]{:S(2)}) collective-permute-start(bf16[384,768]{1,0:T(8,128)(2,1)S(1)} %get-tuple-element.19), channel_id=1, source_target_pairs={{0,2},{1,5},{2,0},{3,7},{4,6},{5,1},{6,4},{7,3},{8,10},{9,13},{10,... | collective-permute-start | bytes 1769480 | tf_op jit(solution)/shard_map/ppermute | solution.py:352
  7.4 13.3 %collective-permute-start = (bf16[256,768]{1,0:T(8,128)(2,1)S(1)}, bf16[256,768]{1,0:T(8,128)(2,1)S(1)}, u32[]{:S(2)}, u32[]{:S(2)}) collective-permute-start(bf16[256,768]{1,0:T(8,128)(2,1)S(1)} %copy-done.4), channel_id=1, source_target_pairs={{0,8},{8,0},{16,24},{24,16},{1,9},{9,1},{17,25},{25,17},{2,10},{10... | collective-permute-start | bytes 1179656 | tf_op jit(solution)/shard_map/ppermute | solution.py:261
  9.0 11.7 %collective-permute-start.1 = (bf16[256,768]{1,0:T(8,128)(2,1)S(1)}, bf16[256,768]{1,0:T(8,128)(2,1)S(1)}, u32[]{:S(2)}, u32[]{:S(2)}) collective-permute-start(bf16[256,768]{1,0:T(8,128)(2,1)S(1)} %copy-done.4), channel_id=1, source_target_pairs={{8,16},{16,8},{9,17},{17,9},{10,18},{18,10},{11,19},{19,11},{12,20... | collective-permute-start | bytes 1179656 | tf_op jit(solution)/shard_map/ppermute | solution.py:270
  9.7 5.9 %collective-permute-start.2 = (f32[12,128]{1,0:T(8,128)S(1)}, f32[12,128]{1,0:T(8,128)S(1)}, u32[]{:S(2)}, u32[]{:S(2)}) collective-permute-start(f32[12,128]{1,0:T(8,128)S(1)} %get-tuple-element.15), channel_id=1, source_target_pairs={{0,2},{2,0},{4,6},{6,4},{1,3},{3,1},{5,7},{7,5},{8,10},{10,8},{12,... | collective-permute-start | bytes 18440 | tf_op jit(solution)/shard_map/ppermute | solution.py:261
  10.3 8.3 %collective-permute-start.3 = (f32[12,128]{1,0:T(8,128)S(1)}, f32[12,128]{1,0:T(8,128)S(1)}, u32[]{:S(2)}, u32[]{:S(2)}) collective-permute-start(f32[12,128]{1,0:T(8,128)S(1)} %get-tuple-element.15), channel_id=1, source_target_pairs={{0,4},{2,6},{4,0},{6,2},{1,5},{3,7},{5,1},{7,3},{8,12},{10,14},{12... | collective-permute-start | bytes 18440 | tf_op jit(solution)/shard_map/ppermute | solution.py:261
  15.5 5.1 %collective-permute-start.4 = (f32[12,128]{1,0:T(8,128)S(1)}, f32[12,128]{1,0:T(8,128)S(1)}, u32[]{:S(2)}, u32[]{:S(2)}) collective-permute-start(f32[12,128]{1,0:T(8,128)S(1)} %get-tuple-element.15), channel_id=1, source_target_pairs={{0,6},{2,4},{4,2},{6,0},{1,7},{3,5},{5,3},{7,1},{8,14},{10,12},{12... | collective-permute-start | bytes 18440 | tf_op jit(solution)/shard_map/ppermute | solution.py:261
  18.6 16.8 %collective-permute-start.10 = (bf16[384,768]{1,0:T(8,128)(2,1)S(1)}, bf16[384,768]{1,0:T(8,128)(2,1)S(1)}, u32[]{:S(2)}, u32[]{:S(2)}) collective-permute-start(bf16[384,768]{1,0:T(8,128)(2,1)S(1)} %get-tuple-element.19), channel_id=1, source_target_pairs={{0,4},{1,3},{2,6},{3,1},{4,0},{5,7},{6,2},{7,5},{8,12},{9,11},{10,... | collective-permute-start | bytes 1769480 | tf_op jit(solution)/shard_map/ppermute | solution.py:353
  19.1 16.7 %collective-permute-start.12 = (bf16[384,768]{1,0:T(8,128)(2,1)S(1)}, bf16[384,768]{1,0:T(8,128)(2,1)S(1)}, u32[]{:S(2)}, u32[]{:S(2)}) collective-permute-start(bf16[384,768]{1,0:T(8,128)(2,1)S(1)} %collective-permute-done.8.refs_2_.refs_7_.refs_8_), channel_id=1, source_target_pairs={{0,4},{1,3},{2,6},{3,1},{4,0},{5,7},{6,2},{7,5},{8,12},{9,11},{10,... | collective-permute-start | bytes 1769480 | tf_op jit(solution)/shard_map/ppermute | solution.py:354
  20.7 4.6 %collective-permute-start.5 = (f32[3328]{0:T(1024)S(1)}, f32[3328]{0:T(1024)S(1)}, u32[]{:S(2)}, u32[]{:S(2)}) collective-permute-start(f32[3328]{0:T(1024)S(1)} %pad_maximum_fusion.4), channel_id=1, source_target_pairs={{0,8},{8,0},{16,24},{24,16},{1,9},{9,1},{17,25},{25,17},{2,10},{10... | collective-permute-start | bytes 39944 | tf_op jit(solution)/shard_map/ppermute | solution.py:261
  22.6 4.7 %collective-permute-start.6 = (f32[3328]{0:T(1024)S(1)}, f32[3328]{0:T(1024)S(1)}, u32[]{:S(2)}, u32[]{:S(2)}) collective-permute-start(f32[3328]{0:T(1024)S(1)} %pad_maximum_fusion.4), channel_id=1, source_target_pairs={{0,16},{8,24},{16,0},{24,8},{1,17},{9,25},{17,1},{25,9},{2,18},{10... | collective-permute-start | bytes 39944 | tf_op jit(solution)/shard_map/ppermute | solution.py:261
  25.0 5.7 %collective-permute-start.7 = (f32[3328]{0:T(1024)S(1)}, f32[3328]{0:T(1024)S(1)}, u32[]{:S(2)}, u32[]{:S(2)}) collective-permute-start(f32[3328]{0:T(1024)S(1)} %pad_maximum_fusion.4), channel_id=1, source_target_pairs={{0,24},{8,16},{16,8},{24,0},{1,25},{9,17},{17,9},{25,1},{2,26},{10... | collective-permute-start | bytes 39944 | tf_op jit(solution)/shard_map/ppermute | solution.py:261
  25.3 10.7 %collective-permute-start.20 = (bf16[256,768]{1,0:T(8,128)(2,1)S(1)}, bf16[256,768]{1,0:T(8,128)(2,1)S(1)}, u32[]{:S(2)}, u32[]{:S(2)}) collective-permute-start(bf16[256,768]{1,0:T(8,128)(2,1)S(1)} %collective-permute-done.refs_0_), channel_id=1, source_target_pairs={{8,16},{16,8},{9,17},{17,9},{10,18},{18,10},{11,19},{19,11},{12,20... | collective-permute-start | bytes 1179656 | tf_op jit(solution)/shard_map/ppermute | solution.py:272
  27.3 18.3 %collective-permute-start.19 = (bf16[256,768]{1,0:T(8,128)(2,1)S(1)}, bf16[256,768]{1,0:T(8,128)(2,1)S(1)}, u32[]{:S(2)}, u32[]{:S(2)}) collective-permute-start(bf16[256,768]{1,0:T(8,128)(2,1)S(1)} %collective-permute-done.1.refs_1_), channel_id=1, source_target_pairs={{8,0},{16,24},{9,1},{17,25},{10,2},{18,26},{11,3},{19,27},{12,4},{... | collective-permute-start | bytes 1179656 | tf_op jit(solution)/shard_map/ppermute | solution.py:273
  35.2 2.2 %collective-permute-start.9 = (bf16[384,768]{1,0:T(8,128)(2,1)S(1)}, bf16[384,768]{1,0:T(8,128)(2,1)S(1)}, u32[]{:S(2)}, u32[]{:S(2)}) collective-permute-start(bf16[384,768]{1,0:T(8,128)(2,1)S(1)} %collective-permute-done.8.refs_2_.refs_7_.refs_8_), channel_id=1, source_target_pairs={{0,1},{1,0},{2,3},{3,2},{4,5},{5,4},{6,7},{7,6},{8,9},{9,8},{10,11... | collective-permute-start | bytes 1769480 | tf_op jit(solution)/shard_map/ppermute | solution.py:261
  35.3 2.8 %collective-permute-start.11 = (bf16[384,768]{1,0:T(8,128)(2,1)S(1)}, bf16[384,768]{1,0:T(8,128)(2,1)S(1)}, u32[]{:S(2)}, u32[]{:S(2)}) collective-permute-start(bf16[384,768]{1,0:T(8,128)(2,1)S(1)} %collective-permute-done.10.refs_4_.refs_9_.refs_10_), channel_id=1, source_target_pairs={{0,1},{1,0},{2,3},{3,2},{4,5},{5,4},{6,7},{7,6},{8,9},{9,8},{10,11... | collective-permute-start | bytes 1769480 | tf_op jit(solution)/shard_map/ppermute | solution.py:261
  35.8 3.2 %collective-permute-start.13 = (bf16[384,768]{1,0:T(8,128)(2,1)S(1)}, bf16[384,768]{1,0:T(8,128)(2,1)S(1)}, u32[]{:S(2)}, u32[]{:S(2)}) collective-permute-start(bf16[384,768]{1,0:T(8,128)(2,1)S(1)} %collective-permute-done.12.refs_6_.refs_11_.refs_12_), channel_id=1, source_target_pairs={{0,1},{1,0},{2,3},{3,2},{4,5},{5,4},{6,7},{7,6},{8,9},{9,8},{10,11... | collective-permute-start | bytes 1769480 | tf_op jit(solution)/shard_map/ppermute | solution.py:261
  36.0 18.1 %collective-permute-start.22 = (bf16[256,768]{1,0:T(8,128)(2,1)S(1)}, bf16[256,768]{1,0:T(8,128)(2,1)S(1)}, u32[]{:S(2)}, u32[]{:S(2)}) collective-permute-start(bf16[256,768]{1,0:T(8,128)(2,1)S(1)} %collective-permute-done.20.refs_1_), channel_id=1, source_target_pairs={{8,0},{16,24},{9,1},{17,25},{10,2},{18,26},{11,3},{19,27},{12,4},{... | collective-permute-start | bytes 1179656 | tf_op jit(solution)/shard_map/ppermute | solution.py:274
  40.6 15.8 %collective-permute-start.14 = (bf16[64,768]{1,0:T(8,128)(2,1)S(1)}, bf16[64,768]{1,0:T(8,128)(2,1)S(1)}, u32[]{:S(2)}, u32[]{:S(2)}) collective-permute-start(bf16[64,768]{1,0:T(8,128)(2,1)S(1)} %get-tuple-element.27), channel_id=1, source_target_pairs={{0,8},{8,0},{16,24},{24,16},{1,9},{9,1},{17,25},{25,17},{2,10},{10... | collective-permute-start | bytes 294920 | tf_op jit(solution)/shard_map/ppermute | solution.py:261
  41.9 17.1 %collective-permute-start.15 = (bf16[64,768]{1,0:T(8,128)(2,1)S(1)}, bf16[64,768]{1,0:T(8,128)(2,1)S(1)}, u32[]{:S(2)}, u32[]{:S(2)}) collective-permute-start(bf16[64,768]{1,0:T(8,128)(2,1)S(1)} %get-tuple-element.29), channel_id=1, source_target_pairs={{0,16},{8,24},{16,0},{24,8},{1,17},{9,25},{17,1},{25,9},{2,18},{10... | collective-permute-start | bytes 294920 | tf_op jit(solution)/shard_map/ppermute | solution.py:261
  43.0 16.0 %collective-permute-start.16 = (bf16[64,768]{1,0:T(8,128)(2,1)S(1)}, bf16[64,768]{1,0:T(8,128)(2,1)S(1)}, u32[]{:S(2)}, u32[]{:S(2)}) collective-permute-start(bf16[64,768]{1,0:T(8,128)(2,1)S(1)} %get-tuple-element.28), channel_id=1, source_target_pairs={{0,24},{8,16},{16,8},{24,0},{1,25},{9,17},{17,9},{25,1},{2,26},{10... | collective-permute-start | bytes 294920 | tf_op jit(solution)/shard_map/ppermute | solution.py:261
  48.0 13.4 %collective-permute-start.21 = (f32[2,2,128]{2,1,0:T(2,128)S(1)}, f32[2,2,128]{2,1,0:T(2,128)S(1)}, u32[]{:S(2)}, u32[]{:S(2)}) collective-permute-start(f32[2,2,128]{2,1,0:T(2,128)S(1)} %score.5), channel_id=1, source_target_pairs={{0,16},{8,24},{16,0},{24,8},{1,17},{9,25},{17,1},{25,9},{2,18},{10... | collective-permute-start | bytes 6152 | tf_op jit(solution)/shard_map/ppermute | solution.py:261
  54.1 7.4 %collective-permute-start.18 = (f32[2,2,128]{2,1,0:T(2,128)S(1)}, f32[2,2,128]{2,1,0:T(2,128)S(1)}, u32[]{:S(2)}, u32[]{:S(2)}) collective-permute-start(f32[2,2,128]{2,1,0:T(2,128)S(1)} %score.4), channel_id=1, source_target_pairs={{0,8},{8,0},{16,24},{24,16},{1,9},{9,1},{17,25},{25,17},{2,10},{10... | collective-permute-start | bytes 6152 | tf_op jit(solution)/shard_map/ppermute | solution.py:261
  56.4 5.4 %collective-permute-start.23 = (f32[2,2,128]{2,1,0:T(2,128)S(1)}, f32[2,2,128]{2,1,0:T(2,128)S(1)}, u32[]{:S(2)}, u32[]{:S(2)}) collective-permute-start(f32[2,2,128]{2,1,0:T(2,128)S(1)} %score.6), channel_id=1, source_target_pairs={{0,24},{8,16},{16,8},{24,0},{1,25},{9,17},{17,9},{25,1},{2,26},{10... | collective-permute-start | bytes 6152 | tf_op jit(solution)/shard_map/ppermute | solution.py:261
  59.0 3.4 %collective-permute-start.17 = (bf16[192,768]{1,0:T(8,128)(2,1)S(1)}, bf16[192,768]{1,0:T(8,128)(2,1)S(1)}, u32[]{:S(2)}, u32[]{:S(2)}) collective-permute-start(bf16[192,768]{1,0:T(8,128)(2,1)S(1)} %pad_maximum_fusion.refs_1_), channel_id=1, source_target_pairs={{0,1},{1,0},{2,3},{3,2},{4,5},{5,4},{6,7},{7,6},{8,9},{9,8},{10,11... | collective-permute-start | bytes 884744 | tf_op jit(solution)/shard_map/ppermute | solution.py:261

commit v21 on v20

--- a/solution.py
+++ b/solution.py
@@ -158,24 +158,17 @@
 
 
 def pack_kernel(place, select, *refs, pieces):
-    out = refs[-1]
-    total = jnp.zeros(out.shape, jnp.float32)
-    for source, start, size, column in pieces:
-        columns = pl.ds(piece_offset(place, column), size)
-        total += lax.dot_general(
-            select[:, columns], refs[source][start : start + size, :], NN, preferred_element_type=jnp.float32
-        )
-    out[...] = total.astype(jnp.bfloat16)
+    *buffers, out = refs
+    selects = [select[:, pl.ds(piece_offset(place, column), size)] for _, _, size, column in pieces]
+    values = [buffers[source][start : start + size, :] for source, start, size, _ in pieces]
+    selects, values = jnp.concatenate(selects, axis=1), jnp.concatenate(values, axis=0)
+    out[...] = lax.dot_general(selects, values, NN, preferred_element_type=jnp.float32).astype(jnp.bfloat16)
 
 
 def apply_kernel(select, table, *refs):
-    out = refs[-1]
-    fresh = jnp.zeros(out.shape, jnp.float32)
-    first = 0
-    for arrived in refs[:-1]:
-        part = select[:, first : first + arrived.shape[0]].astype(jnp.bfloat16)
-        fresh += lax.dot_general(part, arrived[...], NN, preferred_element_type=jnp.float32)
-        first += arrived.shape[0]
+    *arrived, out = refs
+    values = jnp.concatenate([block[...] for block in arrived], axis=0)
+    fresh = lax.dot_general(select[...].astype(jnp.bfloat16), values, NN, preferred_element_type=jnp.float32)
     hit = jnp.sum(select[...], axis=1, keepdims=True) > 0.5
     out[...] = jnp.where(hit, fresh, table[...].astype(jnp.float32)).astype(jnp.bfloat16)
 

time: 64.4 us -> 64.2 us (level)
  transfers between devices with their start and end apart: 24 -> 24, of which waited for: 7 -> 7; matrix products, arithmetic and copies ran while one was open for 2% -> 2% of each run, Pallas kernels for 24% -> 23%
where the time goes in v21:
time: 64.2 us; the launch traced here: 63.9 us
  starting transfers between devices  29.6 us (46%)
  Pallas kernels  17.2 us (27%)
  waiting for transfers between devices  11.7 us (18%)
  local copies, waits for them, and re-layouts  2.93 us (5%)
  other arithmetic  1.43 us (2%)
  between operations  0.93 us (1%)
    ppermute x17, starting transfers between devices, swap(): lax.ppermute(values, axis, [(i, i ^ flip) for i in range(lax.axis_size(ax...  20.4 us
    pallas_call x8, Pallas kernels, call(): pl.pallas_call(functools.partial(kernel, **options), out_shape=tuple(outs...  17.2 us
    ppermute x17, waiting for transfers between devices, swap(): lax.ppermute(values, axis, [(i, i ^ flip) for i in range(lax.axis_size(ax...  9.05 us
    ppermute x1, starting transfers between devices, on_device(): near = lax.ppermute(rows_half, axes, first)  3 us
    unnamed x18, local copies, waits for them, and re-layouts  2.84 us
    ppermute x1, waiting for transfers between devices, gather_line(): last = lax.ppermute(from_end, 'outer', outward)  2.67 us
    ppermute x1, starting transfers between devices, on_device(): far = lax.ppermute(near, axes, second)  1.52 us
    ppermute x1, starting transfers between devices, gather_line(): last = lax.ppermute(from_end, 'outer', outward)  1.47 us
  transfers between devices with their start and end apart: 24, of which 7 were waited for; matrix products, arithmetic and copies ran while one was open for 2% of the time, Pallas kernels for 23%

profile of v21, /device:TPU:0, one launch (start us, length us, event | category | flops | bytes accessed | tf_op | source)
XLA Modules:
  0.0 63.9 jit_solution(8268400170447225503)
XLA Ops:
  0.6 0.1 pad_add_fusion.place
  0.7 0.7 %copy-done.5 = s32[512]{0:T(512)S(1)} copy-done((s32[512]{0:T(512)S(1)}, s32[512]{0:T(512)}, u32[]{:S(2)}) %copy-start.5) | copy-done | bytes 2072
  1.4 0.0 copy-done.6
  1.4 1.1 %copy-done = bf16[512,768]{1,0:T(8,128)(2,1)S(1)} copy-done((bf16[512,768]{1,0:T(8,128)(2,1)S(1)}, bf16[512,768]{1,0:T(8,128)(2,1)}, u32[]{:S(2)}) %copy-start) | copy-done | bytes 786456
  2.6 1.0 %copy-done.2 = bf16[256,768]{1,0:T(8,128)(2,1)S(1)} copy-done((bf16[256,768]{1,0:T(8,128)(2,1)S(1)}, bf16[256,768]{1,0:T(8,128)(2,1)}, u32[]{:S(2)}) %copy-start.2) | copy-done | bytes 393240
  3.6 0.8 %prep.1 = (bf16[384,768]{1,0:T(8,128)(2,1)S(1)}, f32[12,128]{1,0:T(8,128)S(1)}) custom-call(s32[3]{0:T(128)S(1)} %pad_add_fusion.place, bf16[512,768]{1,0:T(8,128)(2,1)S(1)} %copy-done, bf16[256,768]{1,0:T(8,128)(2,1)S(1)} %copy-done.2, s32[4,128]{1,0:T(4,128)S(1)} %bitcast.23, s32[2,128]{1,0:T(2,128)S(1)} %bitcast.28), custom_call_target="tpu_custom_call" | custom-call | flops 1 | bytes 1 | tf_op jit(solution)/shard_map/prep/pallas_call | solution.py:241
  4.4 3.0 %collective-permute-start.8 = (bf16[384,768]{1,0:T(8,128)(2,1)S(1)}, bf16[384,768]{1,0:T(8,128)(2,1)S(1)}, u32[]{:S(2)}, u32[]{:S(2)}) collective-permute-start(bf16[384,768]{1,0:T(8,128)(2,1)S(1)} %get-tuple-element.19), channel_id=1, source_target_pairs={{0,2},{1,5},{2,0},{3,7},{4,6},{5,1},{6,4},{7,3},{8,10},{9,13},{10,... | collective-permute-start | bytes 1769480 | tf_op jit(solution)/shard_map/ppermute | solution.py:345
  7.4 1.6 %collective-permute-start = (bf16[256,768]{1,0:T(8,128)(2,1)S(1)}, bf16[256,768]{1,0:T(8,128)(2,1)S(1)}, u32[]{:S(2)}, u32[]{:S(2)}) collective-permute-start(bf16[256,768]{1,0:T(8,128)(2,1)S(1)} %copy-done.4), channel_id=1, source_target_pairs={{0,8},{8,0},{16,24},{24,16},{1,9},{9,1},{17,25},{25,17},{2,10},{10... | collective-permute-start | bytes 1179656 | tf_op jit(solution)/shard_map/ppermute | solution.py:254
  9.0 0.7 %collective-permute-start.1 = (bf16[256,768]{1,0:T(8,128)(2,1)S(1)}, bf16[256,768]{1,0:T(8,128)(2,1)S(1)}, u32[]{:S(2)}, u32[]{:S(2)}) collective-permute-start(bf16[256,768]{1,0:T(8,128)(2,1)S(1)} %copy-done.4), channel_id=1, source_target_pairs={{8,16},{16,8},{9,17},{17,9},{10,18},{18,10},{11,19},{19,11},{12,20... | collective-permute-start | bytes 1179656 | tf_op jit(solution)/shard_map/ppermute | solution.py:263
  9.7 0.6 collective-permute-start.2
  10.3 1.5 %collective-permute-start.3 = (f32[12,128]{1,0:T(8,128)S(1)}, f32[12,128]{1,0:T(8,128)S(1)}, u32[]{:S(2)}, u32[]{:S(2)}) collective-permute-start(f32[12,128]{1,0:T(8,128)S(1)} %get-tuple-element.15), channel_id=1, source_target_pairs={{0,4},{2,6},{4,0},{6,2},{1,5},{3,7},{5,1},{7,3},{8,12},{10,14},{12... | collective-permute-start | bytes 18440 | tf_op jit(solution)/shard_map/ppermute | solution.py:254
  11.8 3.7 %collective-permute-done.2 = f32[12,128]{1,0:T(8,128)S(1)} collective-permute-done((f32[12,128]{1,0:T(8,128)S(1)}, f32[12,128]{1,0:T(8,128)S(1)}, u32[]{:S(2)}, u32[]{:S(2)}) %collective-permute-start.2) | collective-permute-done | bytes 6176 | tf_op jit(solution)/shard_map/ppermute | solution.py:254
  15.5 3.0 %collective-permute-start.4 = (f32[12,128]{1,0:T(8,128)S(1)}, f32[12,128]{1,0:T(8,128)S(1)}, u32[]{:S(2)}, u32[]{:S(2)}) collective-permute-start(f32[12,128]{1,0:T(8,128)S(1)} %get-tuple-element.15), channel_id=1, source_target_pairs={{0,6},{2,4},{4,2},{6,0},{1,7},{3,5},{5,3},{7,1},{8,14},{10,12},{12... | collective-permute-start | bytes 18440 | tf_op jit(solution)/shard_map/ppermute | solution.py:254
  18.5 0.0 copy-done.8
  18.6 0.0 collective-permute-done.3
  18.6 0.6 collective-permute-start.10
  19.1 0.0 collective-permute-done.8.refs_2_.refs_7_.refs_8_
  19.1 1.5 %collective-permute-start.12 = (bf16[384,768]{1,0:T(8,128)(2,1)S(1)}, bf16[384,768]{1,0:T(8,128)(2,1)S(1)}, u32[]{:S(2)}, u32[]{:S(2)}) collective-permute-start(bf16[384,768]{1,0:T(8,128)(2,1)S(1)} %collective-permute-done.8.refs_2_.refs_7_.refs_8_), channel_id=1, source_target_pairs={{0,4},{1,3},{2,6},{3,1},{4,0},{5,7},{6,2},{7,5},{8,12},{9,11},{10,... | collective-permute-start | bytes 1769480 | tf_op jit(solution)/shard_map/ppermute | solution.py:347
  20.7 0.0 collective-permute-done.4
  20.7 0.0 collective-permute-done.refs_0_
  20.7 0.0 collective-permute-done.1.refs_1_
  20.7 1.9 %collective-permute-start.5 = (f32[3328]{0:T(1024)S(1)}, f32[3328]{0:T(1024)S(1)}, u32[]{:S(2)}, u32[]{:S(2)}) collective-permute-start(f32[3328]{0:T(1024)S(1)} %pad_maximum_fusion.4), channel_id=1, source_target_pairs={{0,8},{8,0},{16,24},{24,16},{1,9},{9,1},{17,25},{25,17},{2,10},{10... | collective-permute-start | bytes 39944 | tf_op jit(solution)/shard_map/ppermute | solution.py:254
  22.6 2.4 %collective-permute-start.6 = (f32[3328]{0:T(1024)S(1)}, f32[3328]{0:T(1024)S(1)}, u32[]{:S(2)}, u32[]{:S(2)}) collective-permute-start(f32[3328]{0:T(1024)S(1)} %pad_maximum_fusion.4), channel_id=1, source_target_pairs={{0,16},{8,24},{16,0},{24,8},{1,17},{9,25},{17,1},{25,9},{2,18},{10... | collective-permute-start | bytes 39944 | tf_op jit(solution)/shard_map/ppermute | solution.py:254
  25.0 0.2 collective-permute-start.7
  25.3 0.0 collective-permute-done.5
  25.3 0.7 %collective-permute-start.20 = (bf16[256,768]{1,0:T(8,128)(2,1)S(1)}, bf16[256,768]{1,0:T(8,128)(2,1)S(1)}, u32[]{:S(2)}, u32[]{:S(2)}) collective-permute-start(bf16[256,768]{1,0:T(8,128)(2,1)S(1)} %collective-permute-done.refs_0_), channel_id=1, source_target_pairs={{8,16},{16,8},{9,17},{17,9},{10,18},{18,10},{11,19},{19,11},{12,20... | collective-permute-start | bytes 1179656 | tf_op jit(solution)/shard_map/ppermute | solution.py:265
  26.0 1.3 %collective-permute-done.6 = f32[3328]{0:T(1024)S(1)} collective-permute-done((f32[3328]{0:T(1024)S(1)}, f32[3328]{0:T(1024)S(1)}, u32[]{:S(2)}, u32[]{:S(2)}) %collective-permute-start.6) | collective-permute-done | bytes 13344 | tf_op jit(solution)/shard_map/ppermute | solution.py:254
  27.3 1.3 %collective-permute-start.19 = (bf16[256,768]{1,0:T(8,128)(2,1)S(1)}, bf16[256,768]{1,0:T(8,128)(2,1)S(1)}, u32[]{:S(2)}, u32[]{:S(2)}) collective-permute-start(bf16[256,768]{1,0:T(8,128)(2,1)S(1)} %collective-permute-done.1.refs_1_), channel_id=1, source_target_pairs={{8,0},{16,24},{9,1},{17,25},{10,2},{18,26},{11,3},{19,27},{12,4},{... | collective-permute-start | bytes 1179656 | tf_op jit(solution)/shard_map/ppermute | solution.py:266
  28.6 2.1 %collective-permute-done.7 = f32[3328]{0:T(1024)S(1)} collective-permute-done((f32[3328]{0:T(1024)S(1)}, f32[3328]{0:T(1024)S(1)}, u32[]{:S(2)}, u32[]{:S(2)}) %collective-permute-start.7) | collective-permute-done | bytes 13344 | tf_op jit(solution)/shard_map/ppermute | solution.py:254
  30.8 4.4 %meta.1 = (f32[4,3072]{1,0:T(4,128)S(1)}, f32[1,3072]{1,0:T(1,128)S(1)}, bf16[320,1024]{1,0:T(8,128)(2,1)S(1)}, f32[512,512]{1,0:T(8,128)S(1)}, s32[1,512]{1,0:T(1,128)S(1)}) custom-call(s32[3]{0:T(128)S(1)} %pad_add_fusion.place, s32[4,1024]{1,0:T(4,128)S(1)} %maximum_convert_fusion.ref_ids, s32[4,2048]{1,0:T(4,128)S(1)} %fusion.neg, f32[1,2048]{1,0:T(1,128)S(1)} %bitcast.22), custom_call_target="tpu_custom_call" | custom-call | flops 1 | bytes 1 | tf_op jit(solution)/shard_map/meta/pallas_call | solution.py:241
  35.2 0.1 collective-permute-start.9
  35.3 0.0 collective-permute-done.10.refs_4_.refs_9_.refs_10_
  35.3 0.5 collective-permute-start.11
  35.8 0.0 collective-permute-done.12.refs_6_.refs_11_.refs_12_
  35.8 0.1 collective-permute-start.13
  36.0 0.0 collective-permute-done.20.refs_1_
  36.0 1.5 %collective-permute-start.22 = (bf16[256,768]{1,0:T(8,128)(2,1)S(1)}, bf16[256,768]{1,0:T(8,128)(2,1)S(1)}, u32[]{:S(2)}, u32[]{:S(2)}) collective-permute-start(bf16[256,768]{1,0:T(8,128)(2,1)S(1)} %collective-permute-done.20.refs_1_), channel_id=1, source_target_pairs={{8,0},{16,24},{9,1},{17,25},{10,2},{18,26},{11,3},{19,27},{12,4},{... | collective-permute-start | bytes 1179656 | tf_op jit(solution)/shard_map/ppermute | solution.py:267
  37.5 0.0 collective-permute-done.9.refs_3_.refs_8_.refs_9_
  37.5 0.7 %collective-permute-done.11.refs_5_.refs_10_.refs_11_ = bf16[384,768]{1,0:T(8,128)(2,1)S(1)} collective-permute-done((bf16[384,768]{1,0:T(8,128)(2,1)S(1)}, bf16[384,768]{1,0:T(8,128)(2,1)S(1)}, u32[]{:S(2)}, u32[]{:S(2)}) %collective-permute-start.11) | collective-permute-done | bytes 589856 | tf_op jit(solution)/shard_map/ppermute | solution.py:254
  38.1 0.8 %collective-permute-done.13.refs_7_.refs_12_.refs_13_ = bf16[384,768]{1,0:T(8,128)(2,1)S(1)} collective-permute-done((bf16[384,768]{1,0:T(8,128)(2,1)S(1)}, bf16[384,768]{1,0:T(8,128)(2,1)S(1)}, u32[]{:S(2)}, u32[]{:S(2)}) %collective-permute-start.13) | collective-permute-done | bytes 589856 | tf_op jit(solution)/shard_map/ppermute | solution.py:254
  39.0 1.2 %pack.1 = bf16[320,768]{1,0:T(8,128)(2,1)S(1)} custom-call(s32[3]{0:T(128)S(1)} %pad_add_fusion.place, bf16[320,1024]{1,0:T(8,128)(2,1)S(1)} %get-tuple-element.18.select, bf16[512,768]{1,0:T(8,128)(2,1)S(1)} %copy-done.1, bf16[256,768]{1,0:T(8,128)(2,1)S(1)} %copy-done.3, bf16[384,768]{1,0:T(8,128)(2,1)S(1)} %collective-permute-done.8.refs_2_.refs_7_.refs_8_, ...), custom_call_target="tpu_custom_call" | custom-call | flops 1 | bytes 1 | tf_op jit(solution)/shard_map/pack/pallas_call | solution.py:241
  40.3 1.3 %collective-permute-start.14 = (bf16[64,768]{1,0:T(8,128)(2,1)S(1)}, bf16[64,768]{1,0:T(8,128)(2,1)S(1)}, u32[]{:S(2)}, u32[]{:S(2)}) collective-permute-start(bf16[64,768]{1,0:T(8,128)(2,1)S(1)} %get-tuple-element.27), channel_id=1, source_target_pairs={{0,8},{8,0},{16,24},{24,16},{1,9},{9,1},{17,25},{25,17},{2,10},{10... | collective-permute-start | bytes 294920 | tf_op jit(solution)/shard_map/ppermute | solution.py:254
  41.5 1.2 %collective-permute-start.15 = (bf16[64,768]{1,0:T(8,128)(2,1)S(1)}, bf16[64,768]{1,0:T(8,128)(2,1)S(1)}, u32[]{:S(2)}, u32[]{:S(2)}) collective-permute-start(bf16[64,768]{1,0:T(8,128)(2,1)S(1)} %get-tuple-element.29), channel_id=1, source_target_pairs={{0,16},{8,24},{16,0},{24,8},{1,17},{9,25},{17,1},{25,9},{2,18},{10... | collective-permute-start | bytes 294920 | tf_op jit(solution)/shard_map/ppermute | solution.py:254
  42.7 2.0 %collective-permute-start.16 = (bf16[64,768]{1,0:T(8,128)(2,1)S(1)}, bf16[64,768]{1,0:T(8,128)(2,1)S(1)}, u32[]{:S(2)}, u32[]{:S(2)}) collective-permute-start(bf16[64,768]{1,0:T(8,128)(2,1)S(1)} %get-tuple-element.28), channel_id=1, source_target_pairs={{0,24},{8,16},{16,8},{24,0},{1,25},{9,17},{17,9},{25,1},{2,26},{10... | collective-permute-start | bytes 294920 | tf_op jit(solution)/shard_map/ppermute | solution.py:254
  44.7 0.6 broadcast_select_fusion
  45.3 0.0 collective-permute-done.19.refs_0_
  45.3 2.3 %score.5 = f32[2,2,128]{2,1,0:T(2,128)S(1)} custom-call(s32[3]{0:T(128)S(1)} %pad_add_fusion.place, bf16[256,768]{1,0:T(8,128)(2,1)S(1)} %collective-permute-done.19.refs_0_, bf16[256,768]{1,0:T(8,128)(2,1)S(1)} %collective-permute-done.20.refs_1_, f32[2,128]{1,0:T(2,128)S(1)} %bitcast.27, f32[1,3072]{1,0:T(1,128)S(1)} %get-tuple-element.30.refs_3_, ...), custom_call_target="tpu_custom_call" | custom-call | flops 1 | bytes 1 | tf_op jit(solution)/shard_map/score/pallas_call | solution.py:241
  47.6 1.4 %collective-permute-start.21 = (f32[2,2,128]{2,1,0:T(2,128)S(1)}, f32[2,2,128]{2,1,0:T(2,128)S(1)}, u32[]{:S(2)}, u32[]{:S(2)}) collective-permute-start(f32[2,2,128]{2,1,0:T(2,128)S(1)} %score.5), channel_id=1, source_target_pairs={{0,16},{8,24},{16,0},{24,8},{1,17},{9,25},{17,1},{25,9},{2,18},{10... | collective-permute-start | bytes 6152 | tf_op jit(solution)/shard_map/ppermute | solution.py:254
  49.1 2.3 %score.4 = f32[2,2,128]{2,1,0:T(2,128)S(1)} custom-call(s32[3]{0:T(128)S(1)} %pad_add_fusion.place, bf16[256,768]{1,0:T(8,128)(2,1)S(1)} %collective-permute-done.refs_0_, f32[2,128]{1,0:T(2,128)S(1)} %bitcast.26, f32[1,3072]{1,0:T(1,128)S(1)} %get-tuple-element.33.refs_2_, f32[1,3072]{1,0:T(1,128)S(1)} %get-tuple-element.24.refs_3_.refs_4_, ...), custom_call_target="tpu_custom_call" | custom-call | flops 1 | bytes 1 | tf_op jit(solution)/shard_map/score/pallas_call | solution.py:241
  51.4 2.7 %collective-permute-done.22.refs_0_ = bf16[256,768]{1,0:T(8,128)(2,1)S(1)} collective-permute-done((bf16[256,768]{1,0:T(8,128)(2,1)S(1)}, bf16[256,768]{1,0:T(8,128)(2,1)S(1)}, u32[]{:S(2)}, u32[]{:S(2)}) %collective-permute-start.22) | collective-permute-done | bytes 393248 | tf_op jit(solution)/shard_map/ppermute | solution.py:267
  54.1 0.0 collective-permute-start.18
  54.1 2.3 %score.6 = f32[2,2,128]{2,1,0:T(2,128)S(1)} custom-call(s32[3]{0:T(128)S(1)} %pad_add_fusion.place, bf16[256,768]{1,0:T(8,128)(2,1)S(1)} %collective-permute-done.22.refs_0_, bf16[256,768]{1,0:T(8,128)(2,1)S(1)} %collective-permute-done.1.refs_1_, f32[2,128]{1,0:T(2,128)S(1)} %bitcast.25, f32[1,3072]{1,0:T(1,128)S(1)} %get-tuple-element.32.refs_3_, ...), custom_call_target="tpu_custom_call" | custom-call | flops 1 | bytes 1 | tf_op jit(solution)/shard_map/score/pallas_call | solution.py:241
  56.4 0.0 collective-permute-done.14
  56.4 2.6 %collective-permute-start.23 = (f32[2,2,128]{2,1,0:T(2,128)S(1)}, f32[2,2,128]{2,1,0:T(2,128)S(1)}, u32[]{:S(2)}, u32[]{:S(2)}) collective-permute-start(f32[2,2,128]{2,1,0:T(2,128)S(1)} %score.6), channel_id=1, source_target_pairs={{0,24},{8,16},{16,8},{24,0},{1,25},{9,17},{17,9},{25,1},{2,26},{10... | collective-permute-start | bytes 6152 | tf_op jit(solution)/shard_map/ppermute | solution.py:254
  59.0 0.0 collective-permute-done.15
  59.0 0.0 collective-permute-done.16
  59.0 0.1 collective-permute-start.17
  59.1 2.3 %score.7 = f32[2,2,128]{2,1,0:T(2,128)S(1)} custom-call(s32[3]{0:T(128)S(1)} %pad_add_fusion.place, bf16[256,768]{1,0:T(8,128)(2,1)S(1)} %copy-done.4, f32[2,128]{1,0:T(2,128)S(1)} %bitcast.24, f32[1,3072]{1,0:T(1,128)S(1)} %get-tuple-element.31.refs_2_, f32[1,3072]{1,0:T(1,128)S(1)} %get-tuple-element.24.refs_3_.refs_4_, ...), custom_call_target="tpu_custom_call" | custom-call | flops 1 | bytes 1 | tf_op jit(solution)/shard_map/score/pallas_call | solution.py:241
  61.4 0.0 collective-permute-done.21
  61.4 0.0 collective-permute-done.18
  61.4 0.4 collective-permute-done.23
  61.8 0.6 fusion.2
  62.4 0.0 collective-permute-done.17.refs_2_
  62.4 1.5 %apply.1 = bf16[512,768]{1,0:T(8,128)(2,1)} custom-call(f32[512,512]{1,0:T(8,128)S(1)} %get-tuple-element.17.select, bf16[512,768]{1,0:T(8,128)(2,1)S(1)} %copy-done.1, bf16[128,768]{1,0:T(8,128)(2,1)S(1)} %slice.93.refs_0_, bf16[192,768]{1,0:T(8,128)(2,1)S(1)} %pad_maximum_fusion.refs_1_, bf16[192,768]{1,0:T(8,128)(2,1)S(1)} %collective-permute-done.17.refs_2_), custom_call_target="tpu_custom_call" | custom-call | flops 1 | bytes 1 | tf_op jit(solution)/shard_map/apply/pallas_call | solution.py:241
  (34 shorter events, 0.3 us)
Async XLA Ops:
  0.6 17.9 %copy-start.7 = (s32[1,2048]{1,0:T(1,128)S(1)}, s32[1,2048]{1,0:T(1,128)}, u32[]{:S(2)}) copy-start(s32[1,2048]{1,0:T(1,128)} %param.11) | copy-start | bytes 24580
  0.7 0.7 %copy-start.5 = (s32[512]{0:T(512)S(1)}, s32[512]{0:T(512)}, u32[]{:S(2)}) copy-start(s32[512]{0:T(512)} %param.8) | copy-start | bytes 6148
  0.7 0.7 %copy-start.6 = (s32[256]{0:T(256)S(1)}, s32[256]{0:T(256)}, u32[]{:S(2)}) copy-start(s32[256]{0:T(256)} %param.9) | copy-start | bytes 3076
  1.4 1.1 %copy-start = (bf16[512,768]{1,0:T(8,128)(2,1)S(1)}, bf16[512,768]{1,0:T(8,128)(2,1)}, u32[]{:S(2)}) copy-start(bf16[512,768]{1,0:T(8,128)(2,1)} %refs_5_.3) | copy-start | bytes 2359300
  2.6 1.0 %copy-start.2 = (bf16[256,768]{1,0:T(8,128)(2,1)S(1)}, bf16[256,768]{1,0:T(8,128)(2,1)}, u32[]{:S(2)}) copy-start(bf16[256,768]{1,0:T(8,128)(2,1)} %refs_6_.7) | copy-start | bytes 1179652
  3.5 3.9 %copy-start.4 = (bf16[256,768]{1,0:T(8,128)(2,1)S(1)}, bf16[256,768]{1,0:T(8,128)(2,1)}, u32[]{:S(2)}) copy-start(bf16[256,768]{1,0:T(8,128)(2,1)} %refs_0_.2) | copy-start | bytes 1179652
  3.6 15.0 %copy-start.8 = (s32[256]{0:T(256)S(1)}, s32[256]{0:T(256)}, u32[]{:S(2)}) copy-start(s32[256]{0:T(256)} %param.13) | copy-start | bytes 3076
  3.6 35.4 %copy-start.1 = (bf16[512,768]{1,0:T(8,128)(2,1)S(1)}, bf16[512,768]{1,0:T(8,128)(2,1)}, u32[]{:S(2)}) copy-start(bf16[512,768]{1,0:T(8,128)(2,1)} %refs_5_.3) | copy-start | bytes 2359300
  4.4 34.6 %copy-start.3 = (bf16[256,768]{1,0:T(8,128)(2,1)S(1)}, bf16[256,768]{1,0:T(8,128)(2,1)}, u32[]{:S(2)}) copy-start(bf16[256,768]{1,0:T(8,128)(2,1)} %refs_6_.7) | copy-start | bytes 1179652
  4.4 14.7 %collective-permute-start.8 = (bf16[384,768]{1,0:T(8,128)(2,1)S(1)}, bf16[384,768]{1,0:T(8,128)(2,1)S(1)}, u32[]{:S(2)}, u32[]{:S(2)}) collective-permute-start(bf16[384,768]{1,0:T(8,128)(2,1)S(1)} %get-tuple-element.19), channel_id=1, source_target_pairs={{0,2},{1,5},{2,0},{3,7},{4,6},{5,1},{6,4},{7,3},{8,10},{9,13},{10,... | collective-permute-start | bytes 1769480 | tf_op jit(solution)/shard_map/ppermute | solution.py:345
  7.4 13.3 %collective-permute-start = (bf16[256,768]{1,0:T(8,128)(2,1)S(1)}, bf16[256,768]{1,0:T(8,128)(2,1)S(1)}, u32[]{:S(2)}, u32[]{:S(2)}) collective-permute-start(bf16[256,768]{1,0:T(8,128)(2,1)S(1)} %copy-done.4), channel_id=1, source_target_pairs={{0,8},{8,0},{16,24},{24,16},{1,9},{9,1},{17,25},{25,17},{2,10},{10... | collective-permute-start | bytes 1179656 | tf_op jit(solution)/shard_map/ppermute | solution.py:254
  9.0 11.7 %collective-permute-start.1 = (bf16[256,768]{1,0:T(8,128)(2,1)S(1)}, bf16[256,768]{1,0:T(8,128)(2,1)S(1)}, u32[]{:S(2)}, u32[]{:S(2)}) collective-permute-start(bf16[256,768]{1,0:T(8,128)(2,1)S(1)} %copy-done.4), channel_id=1, source_target_pairs={{8,16},{16,8},{9,17},{17,9},{10,18},{18,10},{11,19},{19,11},{12,20... | collective-permute-start | bytes 1179656 | tf_op jit(solution)/shard_map/ppermute | solution.py:263
  9.7 5.9 %collective-permute-start.2 = (f32[12,128]{1,0:T(8,128)S(1)}, f32[12,128]{1,0:T(8,128)S(1)}, u32[]{:S(2)}, u32[]{:S(2)}) collective-permute-start(f32[12,128]{1,0:T(8,128)S(1)} %get-tuple-element.15), channel_id=1, source_target_pairs={{0,2},{2,0},{4,6},{6,4},{1,3},{3,1},{5,7},{7,5},{8,10},{10,8},{12,... | collective-permute-start | bytes 18440 | tf_op jit(solution)/shard_map/ppermute | solution.py:254
  10.3 8.3 %collective-permute-start.3 = (f32[12,128]{1,0:T(8,128)S(1)}, f32[12,128]{1,0:T(8,128)S(1)}, u32[]{:S(2)}, u32[]{:S(2)}) collective-permute-start(f32[12,128]{1,0:T(8,128)S(1)} %get-tuple-element.15), channel_id=1, source_target_pairs={{0,4},{2,6},{4,0},{6,2},{1,5},{3,7},{5,1},{7,3},{8,12},{10,14},{12... | collective-permute-start | bytes 18440 | tf_op jit(solution)/shard_map/ppermute | solution.py:254
  15.5 5.1 %collective-permute-start.4 = (f32[12,128]{1,0:T(8,128)S(1)}, f32[12,128]{1,0:T(8,128)S(1)}, u32[]{:S(2)}, u32[]{:S(2)}) collective-permute-start(f32[12,128]{1,0:T(8,128)S(1)} %get-tuple-element.15), channel_id=1, source_target_pairs={{0,6},{2,4},{4,2},{6,0},{1,7},{3,5},{5,3},{7,1},{8,14},{10,12},{12... | collective-permute-start | bytes 18440 | tf_op jit(solution)/shard_map/ppermute | solution.py:254
  18.6 16.8 %collective-permute-start.10 = (bf16[384,768]{1,0:T(8,128)(2,1)S(1)}, bf16[384,768]{1,0:T(8,128)(2,1)S(1)}, u32[]{:S(2)}, u32[]{:S(2)}) collective-permute-start(bf16[384,768]{1,0:T(8,128)(2,1)S(1)} %get-tuple-element.19), channel_id=1, source_target_pairs={{0,4},{1,3},{2,6},{3,1},{4,0},{5,7},{6,2},{7,5},{8,12},{9,11},{10,... | collective-permute-start | bytes 1769480 | tf_op jit(solution)/shard_map/ppermute | solution.py:346
  19.1 16.7 %collective-permute-start.12 = (bf16[384,768]{1,0:T(8,128)(2,1)S(1)}, bf16[384,768]{1,0:T(8,128)(2,1)S(1)}, u32[]{:S(2)}, u32[]{:S(2)}) collective-permute-start(bf16[384,768]{1,0:T(8,128)(2,1)S(1)} %collective-permute-done.8.refs_2_.refs_7_.refs_8_), channel_id=1, source_target_pairs={{0,4},{1,3},{2,6},{3,1},{4,0},{5,7},{6,2},{7,5},{8,12},{9,11},{10,... | collective-permute-start | bytes 1769480 | tf_op jit(solution)/shard_map/ppermute | solution.py:347
  20.7 4.6 %collective-permute-start.5 = (f32[3328]{0:T(1024)S(1)}, f32[3328]{0:T(1024)S(1)}, u32[]{:S(2)}, u32[]{:S(2)}) collective-permute-start(f32[3328]{0:T(1024)S(1)} %pad_maximum_fusion.4), channel_id=1, source_target_pairs={{0,8},{8,0},{16,24},{24,16},{1,9},{9,1},{17,25},{25,17},{2,10},{10... | collective-permute-start | bytes 39944 | tf_op jit(solution)/shard_map/ppermute | solution.py:254
  22.6 4.7 %collective-permute-start.6 = (f32[3328]{0:T(1024)S(1)}, f32[3328]{0:T(1024)S(1)}, u32[]{:S(2)}, u32[]{:S(2)}) collective-permute-start(f32[3328]{0:T(1024)S(1)} %pad_maximum_fusion.4), channel_id=1, source_target_pairs={{0,16},{8,24},{16,0},{24,8},{1,17},{9,25},{17,1},{25,9},{2,18},{10... | collective-permute-start | bytes 39944 | tf_op jit(solution)/shard_map/ppermute | solution.py:254
  25.0 5.7 %collective-permute-start.7 = (f32[3328]{0:T(1024)S(1)}, f32[3328]{0:T(1024)S(1)}, u32[]{:S(2)}, u32[]{:S(2)}) collective-permute-start(f32[3328]{0:T(1024)S(1)} %pad_maximum_fusion.4), channel_id=1, source_target_pairs={{0,24},{8,16},{16,8},{24,0},{1,25},{9,17},{17,9},{25,1},{2,26},{10... | collective-permute-start | bytes 39944 | tf_op jit(solution)/shard_map/ppermute | solution.py:254
  25.3 10.7 %collective-permute-start.20 = (bf16[256,768]{1,0:T(8,128)(2,1)S(1)}, bf16[256,768]{1,0:T(8,128)(2,1)S(1)}, u32[]{:S(2)}, u32[]{:S(2)}) collective-permute-start(bf16[256,768]{1,0:T(8,128)(2,1)S(1)} %collective-permute-done.refs_0_), channel_id=1, source_target_pairs={{8,16},{16,8},{9,17},{17,9},{10,18},{18,10},{11,19},{19,11},{12,20... | collective-permute-start | bytes 1179656 | tf_op jit(solution)/shard_map/ppermute | solution.py:265
  27.3 18.0 %collective-permute-start.19 = (bf16[256,768]{1,0:T(8,128)(2,1)S(1)}, bf16[256,768]{1,0:T(8,128)(2,1)S(1)}, u32[]{:S(2)}, u32[]{:S(2)}) collective-permute-start(bf16[256,768]{1,0:T(8,128)(2,1)S(1)} %collective-permute-done.1.refs_1_), channel_id=1, source_target_pairs={{8,0},{16,24},{9,1},{17,25},{10,2},{18,26},{11,3},{19,27},{12,4},{... | collective-permute-start | bytes 1179656 | tf_op jit(solution)/shard_map/ppermute | solution.py:266
  35.2 2.2 %collective-permute-start.9 = (bf16[384,768]{1,0:T(8,128)(2,1)S(1)}, bf16[384,768]{1,0:T(8,128)(2,1)S(1)}, u32[]{:S(2)}, u32[]{:S(2)}) collective-permute-start(bf16[384,768]{1,0:T(8,128)(2,1)S(1)} %collective-permute-done.8.refs_2_.refs_7_.refs_8_), channel_id=1, source_target_pairs={{0,1},{1,0},{2,3},{3,2},{4,5},{5,4},{6,7},{7,6},{8,9},{9,8},{10,11... | collective-permute-start | bytes 1769480 | tf_op jit(solution)/shard_map/ppermute | solution.py:254
  35.3 2.8 %collective-permute-start.11 = (bf16[384,768]{1,0:T(8,128)(2,1)S(1)}, bf16[384,768]{1,0:T(8,128)(2,1)S(1)}, u32[]{:S(2)}, u32[]{:S(2)}) collective-permute-start(bf16[384,768]{1,0:T(8,128)(2,1)S(1)} %collective-permute-done.10.refs_4_.refs_9_.refs_10_), channel_id=1, source_target_pairs={{0,1},{1,0},{2,3},{3,2},{4,5},{5,4},{6,7},{7,6},{8,9},{9,8},{10,11... | collective-permute-start | bytes 1769480 | tf_op jit(solution)/shard_map/ppermute | solution.py:254
  35.8 3.2 %collective-permute-start.13 = (bf16[384,768]{1,0:T(8,128)(2,1)S(1)}, bf16[384,768]{1,0:T(8,128)(2,1)S(1)}, u32[]{:S(2)}, u32[]{:S(2)}) collective-permute-start(bf16[384,768]{1,0:T(8,128)(2,1)S(1)} %collective-permute-done.12.refs_6_.refs_11_.refs_12_), channel_id=1, source_target_pairs={{0,1},{1,0},{2,3},{3,2},{4,5},{5,4},{6,7},{7,6},{8,9},{9,8},{10,11... | collective-permute-start | bytes 1769480 | tf_op jit(solution)/shard_map/ppermute | solution.py:254
  36.0 18.1 %collective-permute-start.22 = (bf16[256,768]{1,0:T(8,128)(2,1)S(1)}, bf16[256,768]{1,0:T(8,128)(2,1)S(1)}, u32[]{:S(2)}, u32[]{:S(2)}) collective-permute-start(bf16[256,768]{1,0:T(8,128)(2,1)S(1)} %collective-permute-done.20.refs_1_), channel_id=1, source_target_pairs={{8,0},{16,24},{9,1},{17,25},{10,2},{18,26},{11,3},{19,27},{12,4},{... | collective-permute-start | bytes 1179656 | tf_op jit(solution)/shard_map/ppermute | solution.py:267
  40.3 16.1 %collective-permute-start.14 = (bf16[64,768]{1,0:T(8,128)(2,1)S(1)}, bf16[64,768]{1,0:T(8,128)(2,1)S(1)}, u32[]{:S(2)}, u32[]{:S(2)}) collective-permute-start(bf16[64,768]{1,0:T(8,128)(2,1)S(1)} %get-tuple-element.27), channel_id=1, source_target_pairs={{0,8},{8,0},{16,24},{24,16},{1,9},{9,1},{17,25},{25,17},{2,10},{10... | collective-permute-start | bytes 294920 | tf_op jit(solution)/shard_map/ppermute | solution.py:254
  41.5 17.5 %collective-permute-start.15 = (bf16[64,768]{1,0:T(8,128)(2,1)S(1)}, bf16[64,768]{1,0:T(8,128)(2,1)S(1)}, u32[]{:S(2)}, u32[]{:S(2)}) collective-permute-start(bf16[64,768]{1,0:T(8,128)(2,1)S(1)} %get-tuple-element.29), channel_id=1, source_target_pairs={{0,16},{8,24},{16,0},{24,8},{1,17},{9,25},{17,1},{25,9},{2,18},{10... | collective-permute-start | bytes 294920 | tf_op jit(solution)/shard_map/ppermute | solution.py:254
  42.7 16.3 %collective-permute-start.16 = (bf16[64,768]{1,0:T(8,128)(2,1)S(1)}, bf16[64,768]{1,0:T(8,128)(2,1)S(1)}, u32[]{:S(2)}, u32[]{:S(2)}) collective-permute-start(bf16[64,768]{1,0:T(8,128)(2,1)S(1)} %get-tuple-element.28), channel_id=1, source_target_pairs={{0,24},{8,16},{16,8},{24,0},{1,25},{9,17},{17,9},{25,1},{2,26},{10... | collective-permute-start | bytes 294920 | tf_op jit(solution)/shard_map/ppermute | solution.py:254
  47.6 13.8 %collective-permute-start.21 = (f32[2,2,128]{2,1,0:T(2,128)S(1)}, f32[2,2,128]{2,1,0:T(2,128)S(1)}, u32[]{:S(2)}, u32[]{:S(2)}) collective-permute-start(f32[2,2,128]{2,1,0:T(2,128)S(1)} %score.5), channel_id=1, source_target_pairs={{0,16},{8,24},{16,0},{24,8},{1,17},{9,25},{17,1},{25,9},{2,18},{10... | collective-permute-start | bytes 6152 | tf_op jit(solution)/shard_map/ppermute | solution.py:254
  54.1 7.4 %collective-permute-start.18 = (f32[2,2,128]{2,1,0:T(2,128)S(1)}, f32[2,2,128]{2,1,0:T(2,128)S(1)}, u32[]{:S(2)}, u32[]{:S(2)}) collective-permute-start(f32[2,2,128]{2,1,0:T(2,128)S(1)} %score.4), channel_id=1, source_target_pairs={{0,8},{8,0},{16,24},{24,16},{1,9},{9,1},{17,25},{25,17},{2,10},{10... | collective-permute-start | bytes 6152 | tf_op jit(solution)/shard_map/ppermute | solution.py:254
  56.4 5.4 %collective-permute-start.23 = (f32[2,2,128]{2,1,0:T(2,128)S(1)}, f32[2,2,128]{2,1,0:T(2,128)S(1)}, u32[]{:S(2)}, u32[]{:S(2)}) collective-permute-start(f32[2,2,128]{2,1,0:T(2,128)S(1)} %score.6), channel_id=1, source_target_pairs={{0,24},{8,16},{16,8},{24,0},{1,25},{9,17},{17,9},{25,1},{2,26},{10... | collective-permute-start | bytes 6152 | tf_op jit(solution)/shard_map/ppermute | solution.py:254
  59.0 3.4 %collective-permute-start.17 = (bf16[192,768]{1,0:T(8,128)(2,1)S(1)}, bf16[192,768]{1,0:T(8,128)(2,1)S(1)}, u32[]{:S(2)}, u32[]{:S(2)}) collective-permute-start(bf16[192,768]{1,0:T(8,128)(2,1)S(1)} %pad_maximum_fusion.refs_1_), channel_id=1, source_target_pairs={{0,1},{1,0},{2,3},{3,2},{4,5},{5,4},{6,7},{7,6},{8,9},{9,8},{10,11... | collective-permute-start | bytes 884744 | tf_op jit(solution)/shard_map/ppermute | solution.py:254
